TPU v7x, 32 devices: a whole 2x2x4 slice. The times are simulated.
32 devices in a mesh: parts: 2 (over x), center: 8 (over z, y), sub: 2 (over core).
Axes of the slice: x: 2, y: 2, z: 4, core: 2. Of those that a mesh axis runs over, the one named last changes fastest.
Arguments:
- centers: bfloat16 [24576, 3072], P(('parts', 'center', 'sub')), parts along dimension 0
- weights: float32 [24576, 1000], P(('parts', 'center', 'sub')), parts along dimension 0, may hold values from -0.2 to 0.2
- targets: float32 [512, 1000], P('parts'), parts along dimension 0, may hold values from -6 to 6
- batch_index: int32 [512], P('parts'), parts along dimension 0, may hold values from 0 to 12287
- nys_index: int32 [10240], P(('parts', 'center', 'sub')), parts along dimension 0, may hold values from 0 to 12287, as said below
- eigvec: float32 [10240, 160], P(('parts', 'center', 'sub')), parts along dimension 0, may hold values from -0.078125 to 0.078125
- eigval: float32 [320], P('parts'), parts along dimension 0, may hold values from 0.05 to 1
Outputs:
- new_weights: float32 [24576, 1000], P(('parts', 'center', 'sub')), parts along dimension 0
- predictions: float32 [512, 1000], P('parts'), parts along dimension 0
There are 2 independent parts, one for each index of `parts`. A program takes and returns all parts, laid end to end along the dimension named above; each array names one. Nothing has to cross between parts.
Inputs may be any that keep to these rules, and one draw needn't show every extreme that they name: `nys_index`: each Nystrom point of the k-th block of 320 entries lies in the k-th block of 768 centers.
All inputs are finite; a program needn't handle non-finite values.
Results may differ from a plain program's by a relative error of at most 0.0003.
Values may be sent and summed in bfloat16 or wider, within the bound.
No kernel may reach another device: no remote copies, remote signals or barrier semaphores. Data moves between devices by JAX's collectives and lax.ppermute only.
A program may use at most 64 MiB of HBM per device.

v0:
```python
import jax
import jax.numpy as jnp
from jax import lax
from jax.sharding import PartitionSpec as P


def kernel(left, right):
    cross = jnp.dot(left, right.T, preferred_element_type=jnp.float32)
    lf = left.astype(jnp.float32)
    rf = right.astype(jnp.float32)
    lnorm = jnp.sum(lf * lf, axis=1)
    rnorm = jnp.sum(rf * rf, axis=1)
    square = jnp.maximum(lnorm[:, None] + rnorm[None, :] - 2.0 * cross, 0.0)
    return jnp.exp(-jnp.sqrt(square) / jnp.sqrt(jnp.float32(left.shape[1])))


def on_device(centers, weights, targets, batch_index, nys_index, eigvec, eigval):
    rows_here = centers.shape[0]
    start = lax.axis_index(("center", "sub")) * rows_here
    slots = jnp.arange(rows_here, dtype=jnp.int32)
    pick_batch = slots[:, None] == (batch_index - start)[None, :]
    partial_rows = jnp.dot(
        pick_batch.astype(jnp.bfloat16).T, centers, preferred_element_type=jnp.float32
    )
    batch = lax.psum(partial_rows, ("center", "sub")).astype(jnp.bfloat16)
    local_nys = nys_index - start
    nystrom = jnp.take(centers, local_nys, axis=0)
    kb_local = kernel(batch, centers)
    ks_local = kernel(nystrom, batch)
    pred_part = jnp.dot(kb_local, weights, precision=lax.Precision.HIGHEST)
    predictions = lax.psum(pred_part, ("center", "sub"))
    residual = predictions - targets
    proj_part = jnp.dot(
        eigvec.T,
        jnp.dot(ks_local, residual, precision=lax.Precision.HIGHEST),
        precision=lax.Precision.HIGHEST,
    )
    proj = lax.psum(proj_part, ("center", "sub"))
    lowest = jnp.min(eigval)
    scaled = (1.0 - lowest / eigval) / eigval
    correct = jnp.dot(eigvec, scaled[:, None] * proj, precision=lax.Precision.HIGHEST)
    pick_nys = (slots[:, None] == local_nys[None, :]).astype(jnp.float32)
    step_batch = jnp.dot(pick_batch.astype(jnp.float32), residual, precision=lax.Precision.HIGHEST)
    step_nys = jnp.dot(pick_nys, correct, precision=lax.Precision.HIGHEST)
    new_weights = weights - 0.25 * step_batch + 0.25 * step_nys
    return (new_weights, predictions)


def solution(mesh):
    return jax.shard_map(
        on_device,
        mesh=mesh,
        in_specs=(
            P(("parts", "center", "sub"), None),
            P(("parts", "center", "sub"), None),
            P("parts", None),
            P("parts"),
            P(("parts", "center", "sub")),
            P(("parts", "center", "sub"), None),
            P("parts"),
        ),
        out_specs=(P(("parts", "center", "sub"), None), P("parts", None)),
        check_vma=False,
    )
```

profile of v0, /device:TPU:1, one launch (start us, length us, event | category | flops | bytes accessed | tf_op | source)
XLA Modules:
  0.0 310.5 jit_solution(8494638583011076017)
XLA Ops:
  7.2 0.0 copy-start
  7.2 0.0 copy-start.6
  7.2 0.0 all-reduce.4.cloned.1.call-start
  7.2 3.3 %multiply_reduce_fusion = f32[768]{0:T(1024)S(1)} fusion(bf16[768,3072]{1,0:T(8,128)(2,1)} %param.7), kind=kLoop, calls=%fused_computation.1 | loop fusion | flops 7077120 | bytes 4721664 | tf_op jit(solution)/shard_map/reduce_sum | solution.py:12
  10.6 0.0 copy-done.6
  10.6 5.5 %fusion.13 = f32[256,3072]{1,0:T(8,128)} fusion(bf16[768,3072]{1,0:T(8,128)(2,1)} %param.7, s32[256]{0:T(256)S(1)} %broadcast_subtract_fusion.1), kind=kOutput, calls=%fused_computation.24 | convolution fusion | flops 1208156160 | bytes 7865344 | tf_op jit(solution)/shard_map/dot_general | solution.py:22
  16.1 81.0 %all-reduce.7 = bf16[256,3072]{1,0:T(8,128)(2,1)S(1)} all-reduce(f32[256,3072]{1,0:T(8,128)} %fusion.13), channel_id=1, replica_groups=mesh['parts'=2,'center'=8,'sub'=2] {'center','sub'}, use_global_device_ids=true, to_apply=%region_0.0 | all-reduce | flops 786432 | bytes 4718592 | tf_op jit(solution)/shard_map/psum | solution.py:25
  97.0 0.0 copy-start.3
  97.0 1.1 copy-done.3
  98.2 0.4 multiply_reduce_fusion.2
  98.6 0.0 copy-start.1
  98.6 4.6 %fusion.5 = f32[256,768]{1,0:T(8,128)S(1)} fusion(bf16[768,3072]{1,0:T(8,128)(2,1)} %param.7, f32[768]{0:T(1024)S(1)} %multiply_reduce_fusion, f32[256]{0:T(256)S(1)} %multiply_reduce_fusion.2, bf16[256,3072]{1,0:T(8,128)(2,1)} %copy-done.3), kind=kOutput, calls=%fused_computation.13 | convolution fusion | flops 1209139200 | bytes 7081984 | tf_op jit(solution)/shard_map/dot_general | solution.py:8
  103.2 0.0 copy-done.1
  103.2 0.0 copy-start.5
  103.2 3.5 %fusion.26 = f32[256,1000]{0,1:T(8,128)} fusion(f32[256,768]{1,0:T(8,128)S(1)} %fusion.5, f32[768,1000]{0,1:T(8,128)S(1)} %copy-done.1), kind=kOutput, calls=%fused_computation.43 | convolution fusion | flops 2359296000 | bytes 4882432 | tf_op jit(solution)/shard_map/dot_general | solution.py:30
  106.8 0.0 all-reduce.4.cloned.1.call-update
  106.8 0.0 all-reduce.6.cloned.1.call-start
  106.9 0.0 copy-done.5
  106.9 0.0 copy-start.4
  106.9 9.6 %gather_fusion = bf16[320,3072]{1,0:T(8,128)(2,1)} fusion(bf16[768,3072]{1,0:T(8,128)(2,1)} %param.7, s32[1024]{0:T(1024)S(1)} %pad_clamp_fusion), kind=kCustom, calls=%fused_computation | custom fusion | bytes 3933440 | tf_op jit(solution)/shard_map/jit(_take)/gather | solution.py:27
  116.5 2.2 multiply_reduce_fusion.1
  118.8 0.0 copy-done.4
  118.8 0.7 reduce_min.9
  119.4 0.7 subtract_divide_fusion
  120.1 3.5 %fusion.11 = f32[320,256]{1,0:T(8,128)} fusion(bf16[320,3072]{1,0:T(8,128)(2,1)} %gather_fusion, pred[320]{0:T(512)(128)(4,1)S(1)} %get-tuple-element.2, f32[256]{0:T(256)S(1)} %multiply_reduce_fusion.2, f32[320]{0:T(512)S(1)} %multiply_reduce_fusion.1, bf16[256,3072]{1,0:T(8,128)(2,1)} %copy-done.3), kind=kOutput, calls=%fused_computation.20 | convolution fusion | flops 504791040 | bytes 3869248 | tf_op jit(solution)/shard_map/dot_general | solution.py:8
  123.7 73.5 %all-reduce.4.cloned.1.call-done = f32[256,1000]{0,1:T(8,128)} async-done(((f32[256,1000]{0,1:T(8,128)}), f32[256,1000]{0,1:T(8,128)}) %all-reduce.4.cloned.1.call-update) | async-done | bytes 1024016 | tf_op jit(solution)/shard_map/psum | solution.py:31
  197.2 2.9 fusion.17
  200.0 0.0 copy-done
  200.0 2.2 convolution_bitcast_fusion
  202.2 0.0 all-reduce.6.cloned.1.call-update
  202.2 4.7 %fusion.12 = f32[768,1000]{0,1:T(8,128)} fusion(f32[256,1000]{0,1:T(8,128)} %all-reduce.4.cloned.1.call-done, f32[256,1000]{0,1:T(8,128)} %param.9, s32[256]{0:T(256)S(1)} %broadcast_subtract_fusion.1), kind=kOutput, calls=%fused_computation.23 | convolution fusion | flops 2359748608 | bytes 5121024 | tf_op jit(solution)/shard_map/dot_general | solution.py:43
  206.9 86.3 %all-reduce.6.cloned.1.call-done = f32[160,1000]{1,0:T(8,128)} async-done(((f32[160,1000]{1,0:T(8,128)}), f32[160,1000]{1,0:T(8,128)}) %all-reduce.6.cloned.1.call-update) | async-done | bytes 640016 | tf_op jit(solution)/shard_map/psum | solution.py:38
  293.2 3.1 fusion.14
  296.3 0.0 copy-start.2
  296.3 6.4 %multiply_add_fusion = f32[768,1000]{0,1:T(8,128)} fusion(f32[768,1000]{0,1:T(8,128)S(1)} %copy-done.1, f32[768,1000]{0,1:T(8,128)} %fusion.12, f32[1000,320]{1,0:T(8,128)S(1)} %fusion.14, s32[320]{0:T(512)S(1)} %get-tuple-element.3), kind=kOutput, calls=%fused_computation.4 | convolution fusion | flops 2952437760 | bytes 10497280 | tf_op jit(solution)/shard_map/dot_general | solution.py:44
  302.7 0.0 copy-done.2
  302.7 1.0 copy.13
  (4 shorter events, 0.0 us)
Async XLA Ops:
  7.2 192.9 %copy-start = (f32[320,160]{0,1:T(8,128)S(1)}, f32[320,160]{0,1:T(8,128)}, u32[]{:S(2)}) copy-start(f32[320,160]{0,1:T(8,128)} %param.12) | copy-start | bytes 614404
  7.2 3.4 %copy-start.6 = (s32[256]{0:T(256)S(1)}, s32[256]{0:T(256)}, u32[]{:S(2)}) copy-start(s32[256]{0:T(256)} %param.10) | copy-start | bytes 3076
  7.2 190.0 %all-reduce.4.cloned.1.call-start = ((), (), s32[]{:S(2)}) async-start(), calls=%async_computation | async-start | bytes 2048000 | tf_op jit(solution)/shard_map/psum | solution.py:31
  97.0 1.2 copy-start.3
  98.6 4.6 %copy-start.1 = (f32[768,1000]{0,1:T(8,128)S(1)}, f32[768,1000]{0,1:T(8,128)}, u32[]{:S(2)}) copy-start(f32[768,1000]{0,1:T(8,128)} %param.8) | copy-start | bytes 9216004
  103.2 3.6 %copy-start.5 = (s32[320]{0:T(512)S(1)}, s32[320]{0:T(512)}, u32[]{:S(2)}) copy-start(s32[320]{0:T(512)} %param.11) | copy-start | bytes 3844
  106.8 186.4 %all-reduce.6.cloned.1.call-start = ((), (), s32[]{:S(2)}) async-start(), calls=%async_computation.1 | async-start | bytes 1310720 | tf_op jit(solution)/shard_map/psum | solution.py:38
  106.9 11.8 %copy-start.4 = (f32[160]{0:T(256)S(1)}, f32[160]{0:T(256)}, u32[]{:S(2)}) copy-start(f32[160]{0:T(256)} %param.13) | copy-start | bytes 1924
  296.3 6.4 %copy-start.2 = (f32[256,1000]{0,1:T(8,128)S(1)}, f32[256,1000]{0,1:T(8,128)}, u32[]{:S(2)}) copy-start(f32[256,1000]{0,1:T(8,128)} %all-reduce.4.cloned.1.call-done) | copy-start | bytes 3072004
Sparse Core Ops, SparseCore 0:
  106.9 90.1 all-reduce.3
  202.4 90.8 all-reduce.5
where the time goes:
time: 312 us; the launch traced here: 311 us
  waiting for transfers between devices  160 us (51%)
  blocking collectives  81 us (26%)
  matrix products  36.4 us (12%)
  between operations  14.2 us (5%)
  local copies, waits for them, and re-layouts  11.7 us (4%)
  other arithmetic  7.35 us (2%)
    psum x1, waiting for transfers between devices, on_device(): proj = lax.psum(proj_part, ('center', 'sub'))  86.3 us
    psum x1, blocking collectives, on_device(): batch = lax.psum(partial_rows, ('center', 'sub')).astype(jnp.bfloat16)  81 us
    psum x1, waiting for transfers between devices, on_device(): predictions = lax.psum(pred_part, ('center', 'sub'))  73.5 us
    gather x1, local copies, waits for them, and re-layouts, on_device(): nystrom = jnp.take(centers, local_nys, axis=0)  9.59 us
    dot_general x2, matrix products, kernel(): cross = jnp.dot(left, right.T, preferred_element_type=jnp.float32)  8.16 us
    dot_general x1, matrix products, on_device(): step_nys = jnp.dot(pick_nys, correct, precision=lax.Precision.HIGHEST)  6.41 us
  transfers between devices with their start and end apart: 2, of which 2 were waited for; matrix products, arithmetic and copies ran while one was open for 7% of the time, Pallas kernels for 0%

commit v1 on v0

v1 whole, which is shorter than its diff:
```python
import functools
import math

import jax
import jax.numpy as jnp
from jax import lax
from jax.experimental import pallas as pl
from jax.experimental.pallas import tpu as pltpu
from jax.sharding import PartitionSpec as P

F32 = jnp.float32
BF16 = jnp.bfloat16
AXES = ("center", "sub")
LEVELS = 4
CHUNKS = 1 << LEVELS
LANE = 128
NT = (((1,), (1,)), ((), ()))
NN = (((1,), (0,)), ((), ()))
TN = (((0,), (0,)), ((), ()))
VMEM_LIMIT = 56 * 1024 * 1024


def dot(a, b, dims):
    return lax.dot_general(a, b, dims, preferred_element_type=F32)


def position():
    return lax.axis_index("center") * 2 + lax.axis_index("sub")


def reversed_bits(value, bits):
    out = 0
    for bit in range(bits):
        out = out + ((value >> bit) & 1) * (1 << (bits - 1 - bit))
    return out


def column_of(row, width):
    return jnp.broadcast_to(row.astype(F32), (width, row.shape[1])).T


def two(x):
    high = x.astype(BF16)
    return high, (x - high.astype(F32)).astype(BF16)


def pick_rows(index_ref, columns, start, dtype, scale):
    column = column_of(index_ref[...] - start, LANE)
    lanes = lax.broadcasted_iota(jnp.int32, (1, LANE), 1).astype(F32)
    blocks = [
        jnp.where(column == lanes + float(LANE * k), scale, 0.0).astype(dtype)
        for k in range(columns // LANE)
    ]
    return jnp.concatenate(blocks, axis=1)


def pick_body(index_ref, centers_ref, keep_ref, send_ref, pick_ref):
    me = position()
    turn = reversed_bits(me, LEVELS)
    rows = index_ref.shape[1]
    size = rows // CHUNKS
    count = centers_ref.shape[0]

    @pl.when(pl.program_id(0) == 0)
    def _():
        pick = pick_rows(index_ref, count, me * count, F32, 1.0)
        for chunk in range(CHUNKS):
            to = pl.multiple_of((chunk ^ turn) * size, size)
            pick_ref[pl.ds(to, size), :] = pick[chunk * size : (chunk + 1) * size].astype(BF16)

    found = dot(pick_ref[...], centers_ref[...], NN).astype(BF16)
    keep_ref[...] = found[: rows // 2]
    send_ref[...] = found[rows // 2 :]


def pick_batch(batch_index, centers):
    rows = batch_index.shape[1]
    count, depth = centers.shape
    block = 1024
    half = jax.ShapeDtypeStruct((rows // 2, depth), BF16)
    return pl.pallas_call(
        pick_body,
        grid=(depth // block,),
        in_specs=[
            pl.BlockSpec((1, rows), lambda i: (0, 0)),
            pl.BlockSpec((count, block), lambda i: (0, i)),
        ],
        out_specs=[pl.BlockSpec((rows // 2, block), lambda i: (0, i))] * 2,
        out_shape=[half, half],
        scratch_shapes=[pltpu.VMEM((rows, count), BF16)],
        compiler_params=pltpu.CompilerParams(vmem_limit_bytes=VMEM_LIMIT),
        cost_estimate=pl.CostEstimate(
            flops=2 * rows * count * depth, bytes_accessed=2 * depth * (count + rows), transcendentals=0
        ),
        name="pick_batch",
    )(batch_index, centers)


def prepare_body(classes, index_ref, eigvec_ref, weights_ref, high_ref, low_ref, spread_ref, all_ref):
    me = position()
    turn = reversed_bits(me >> 1, LEVELS - 1)
    rank, points = eigvec_ref.shape
    count = weights_ref.shape[1]
    padded = high_ref.shape[0]
    size = padded // (CHUNKS // 2)
    local = index_ref[...] - me * count
    slots = lax.broadcasted_iota(jnp.int32, (count, points), 0)
    pick = jnp.where(slots == local, 1.0, 0.0).astype(BF16)
    vec = eigvec_ref[...]
    high = vec.astype(BF16)
    rest = vec - high.astype(F32)
    mid = rest.astype(BF16)
    low = (rest - mid.astype(F32)).astype(BF16)
    spread = dot(high, pick, NT) + dot(mid, pick, NT) + dot(low, pick, NT)
    spread_ref[...] = spread
    all_ref[:classes] = weights_ref[...]
    all_ref[classes : classes + rank] = spread
    all_ref[classes + rank :] = jnp.zeros((padded - classes - rank, count), F32)
    for chunk in range(CHUNKS // 2):
        to = pl.multiple_of((chunk ^ turn) * size, 8)
        high, low = two(all_ref[pl.ds(to, size), :])
        high_ref[chunk * size : (chunk + 1) * size] = high
        low_ref[chunk * size : (chunk + 1) * size] = low


def prepare(nys_index, eigvec, weights, padded):
    classes, count = weights.shape
    rank, points = eigvec.shape
    return pl.pallas_call(
        functools.partial(prepare_body, classes),
        out_shape=[
            jax.ShapeDtypeStruct((padded, count), BF16),
            jax.ShapeDtypeStruct((padded, count), BF16),
            jax.ShapeDtypeStruct((rank, count), F32),
        ],
        scratch_shapes=[pltpu.VMEM((padded, count), F32)],
        compiler_params=pltpu.CompilerParams(vmem_limit_bytes=VMEM_LIMIT),
        cost_estimate=pl.CostEstimate(
            flops=6 * rank * points * count, bytes_accessed=8 * padded * count, transcendentals=0
        ),
        name="prepare",
    )(nys_index, eigvec, weights)


def predict_body(mine_ref, other_ref, centers_ref, high_ref, low_ref, keep_ref, send_ref, batch_ref, norm_ref, total_ref):
    me = position()
    turn = reversed_bits(me, LEVELS)
    rows, depth = batch_ref.shape
    half = rows // 2
    size = rows // CHUNKS
    step = pl.program_id(0)

    @pl.when(step == 0)
    def _():
        for chunk in range(CHUNKS):
            ref = mine_ref if chunk < CHUNKS // 2 else other_ref
            at = chunk % (CHUNKS // 2) * size
            to = pl.multiple_of((chunk ^ turn) * size, size)
            batch_ref[pl.ds(to, size), :] = ref[at : at + size, :]
        batch = batch_ref[...].astype(F32)
        norm = jnp.sum(batch * batch, axis=1, keepdims=True)
        norm_ref[...] = jnp.broadcast_to(norm, (rows, LANE)).T[:8]
        total_ref[...] = jnp.zeros_like(total_ref)

    block = centers_ref[...]
    cross = dot(block, batch_ref[...], NT)
    wide = block.astype(F32)
    norm = jnp.sum(wide * wide, axis=1, keepdims=True)
    square = jnp.maximum(norm + norm_ref[0:1, :] - 2.0 * cross, 0.0)
    value = jnp.exp(jnp.sqrt(square) * (-1.0 / math.sqrt(depth)))
    value_high, value_low = two(value)
    high = high_ref[...]
    total_ref[...] += dot(high, value_high, NN) + (dot(high, value_low, NN) + dot(low_ref[...], value_high, NN))

    @pl.when(step == pl.num_programs(0) - 1)
    def _():
        first = total_ref[:, :half]
        second = total_ref[:, half:]
        lower = (me & 1) == 0
        keep_ref[...] = jnp.where(lower, first, second)
        send_ref[...] = jnp.where(lower, second, first)


def predict(mine, other, centers, high, low):
    half, depth = mine.shape
    rows = 2 * half
    count = centers.shape[0]
    padded = high.shape[0]
    block = 256
    out = jax.ShapeDtypeStruct((padded, half), F32)
    return pl.pallas_call(
        predict_body,
        grid=(count // block,),
        in_specs=[
            pl.BlockSpec((half, depth), lambda i: (0, 0)),
            pl.BlockSpec((half, depth), lambda i: (0, 0)),
            pl.BlockSpec((block, depth), lambda i: (i, 0)),
            pl.BlockSpec((padded, block), lambda i: (0, i)),
            pl.BlockSpec((padded, block), lambda i: (0, i)),
        ],
        out_specs=[pl.BlockSpec((padded, half), lambda i: (0, 0))] * 2,
        out_shape=[out, out],
        scratch_shapes=[
            pltpu.VMEM((rows, depth), BF16),
            pltpu.VMEM((8, rows), F32),
            pltpu.VMEM((padded, rows), F32),
        ],
        compiler_params=pltpu.CompilerParams(vmem_limit_bytes=VMEM_LIMIT),
        cost_estimate=pl.CostEstimate(
            flops=2 * rows * count * (depth + 3 * padded),
            bytes_accessed=2 * depth * (count + rows) + 4 * padded * (count + rows),
            transcendentals=2 * rows * count,
        ),
        name="predict",
    )(mine, other, centers, high, low)


def update_body(
    classes, mine_ref, other_ref, targets_ref, index_ref, eigval_ref, spread_ref, weights_ref,
    new_ref, out_ref, total_ref, high_ref, low_ref,
):
    me = position()
    step = pl.program_id(0)
    block = new_ref.shape[0]
    rank, count = spread_ref.shape
    half = mine_ref.shape[1]

    @pl.when(step == 0)
    def _():
        turn = reversed_bits(me >> 1, LEVELS - 1)
        size = mine_ref.shape[0] // (CHUNKS // 2)
        lower = (me & 1) == 0
        for chunk in range(CHUNKS // 2):
            to = pl.multiple_of((chunk ^ turn) * size, 8)
            mine = mine_ref[chunk * size : (chunk + 1) * size]
            other = other_ref[chunk * size : (chunk + 1) * size]
            total_ref[pl.ds(to, size), :half] = jnp.where(lower, mine, other)
            total_ref[pl.ds(to, size), half:] = jnp.where(lower, other, mine)
        value = eigval_ref[...]
        lowest = jnp.min(value, axis=1, keepdims=True)
        scaled = (1.0 - lowest / value) / value
        mixed_high, mixed_low = two(total_ref[classes : classes + rank].T * (0.25 * scaled))
        spread_high, spread_low = two(spread_ref[...])
        turned = dot(mixed_high, spread_high, NN) + (
            dot(mixed_high, spread_low, NN) + dot(mixed_low, spread_high, NN)
        )
        high, low = two(turned - pick_rows(index_ref, count, me * count, F32, 0.25))
        high_ref[...] = high
        low_ref[...] = low

    at = pl.multiple_of(step * block, 8)
    predictions = total_ref[pl.ds(at, block), :]
    out_ref[...] = predictions
    high, low = two(predictions - targets_ref[...])
    new_ref[...] = weights_ref[...] + (
        dot(high, high_ref[...], NN) + (dot(high, low_ref[...], NN) + dot(low, high_ref[...], NN))
    )


def update(mine, other, targets, batch_index, eigval, spread, weights):
    classes, count = weights.shape
    padded, half = mine.shape
    rows = 2 * half
    rank = spread.shape[0]
    block = 200
    whole = lambda shape: pl.BlockSpec(shape, lambda i: (0, 0))
    return pl.pallas_call(
        functools.partial(update_body, classes),
        grid=(classes // block,),
        in_specs=[
            whole((padded, half)),
            whole((padded, half)),
            pl.BlockSpec((block, rows), lambda i: (i, 0)),
            whole((1, rows)),
            whole((1, rank)),
            whole((rank, count)),
            pl.BlockSpec((block, count), lambda i: (i, 0)),
        ],
        out_specs=[
            pl.BlockSpec((block, count), lambda i: (i, 0)),
            pl.BlockSpec((block, rows), lambda i: (i, 0)),
        ],
        out_shape=[
            jax.ShapeDtypeStruct((classes, count), F32),
            jax.ShapeDtypeStruct((classes, rows), F32),
        ],
        scratch_shapes=[
            pltpu.VMEM((padded, rows), F32),
            pltpu.VMEM((rows, count), BF16),
            pltpu.VMEM((rows, count), BF16),
        ],
        compiler_params=pltpu.CompilerParams(vmem_limit_bytes=VMEM_LIMIT),
        cost_estimate=pl.CostEstimate(
            flops=6 * rows * count * (classes + rank),
            bytes_accessed=8 * classes * (count + rows),
            transcendentals=0,
        ),
        name="update",
    )(mine, other, targets, batch_index, eigval, spread, weights)


def swap(x, mask, devices):
    return lax.ppermute(x, AXES, [(i, i ^ mask) for i in range(devices)])


def total_of(keep, send, devices):
    for level in range(LEVELS):
        keep = keep + swap(send, 1 << level, devices)
        if level < LEVELS - 1:
            half = keep.shape[0] // 2
            keep, send = keep[:half], keep[half:]
    for level in range(LEVELS, int(math.log2(devices))):
        keep = keep + swap(keep, 1 << level, devices)
    for level in reversed(range(1, LEVELS)):
        keep = jnp.concatenate([keep, swap(keep, 1 << level, devices)])
    return keep, swap(keep, 1, devices)


def on_device(devices, centers, weights, targets, batch_index, nys_index, eigvec, eigval):
    rows = batch_index.shape[0]
    classes = weights.shape[1]
    rank = eigvec.shape[1]
    unit = 8 * CHUNKS // 2
    padded = -(-(classes + rank) // unit) * unit
    batch_index = batch_index.reshape(1, rows)
    mine, other = total_of(*pick_batch(batch_index, centers), devices)
    high, low, spread = prepare(nys_index.reshape(1, -1), eigvec.T, weights.T, padded)
    mine, other = total_of(*predict(mine, other, centers, high, low), devices)
    new_weights, predictions = update(
        mine, other, targets.T, batch_index, eigval.reshape(1, rank), spread, weights.T
    )
    return new_weights.T, predictions.T


def solution(mesh):
    devices = mesh.shape["center"] * mesh.shape["sub"]
    return jax.shard_map(
        functools.partial(on_device, devices),
        mesh=mesh,
        in_specs=(
            P(("parts", "center", "sub"), None),
            P(("parts", "center", "sub"), None),
            P("parts", None),
            P("parts"),
            P(("parts", "center", "sub")),
            P(("parts", "center", "sub"), None),
            P("parts"),
        ),
        out_specs=(P(("parts", "center", "sub"), None), P("parts", None)),
        check_vma=False,
    )
```

time: 312 us -> 127 us (0.41)
  waiting for transfers between devices: 160 us -> 62.2 us
  blocking collectives: 81 us -> 0 us
  matrix products: 36.4 us -> 0 us
  Pallas kernels: 0 us -> 29.1 us
  starting transfers between devices: 0.08 us -> 28.8 us
  between operations: 14.2 us -> 0.8 us
  local copies, waits for them, and re-layouts: 11.7 us -> 2.41 us
  other arithmetic: 7.35 us -> 2.79 us
    psum x2 -> x0, waiting for transfers between devices: 160 us -> none  [the longest x1 86.3 us: on_device(): proj = lax.psum(proj_part, ('center', 'sub'))]
    psum x1 -> x0, blocking collectives: 81 us -> none  [on_device(): batch = lax.psum(partial_rows, ('center', 'sub')).astype(jnp.bfloat16)]
    ppermute x0 -> x16, waiting for transfers between devices: none -> 62.2 us  [swap(): return lax.ppermute(x, AXES, [(i, i ^ mask) for i in range(devices)])]
    dot_general x9 -> x0, matrix products: 36.4 us -> none  [the longest x2 8.16 us: kernel(): cross = jnp.dot(left, right.T, preferred_element_type=jnp.float32)]
    pallas_call x0 -> x4, Pallas kernels: none -> 29.1 us  [the longest x1 10.5 us: predict(): pl.pallas_call(predict_body, grid=(count // block,), in_specs=[pl.BlockSp...]
    ppermute x0 -> x16, starting transfers between devices: none -> 28.8 us  [swap(): return lax.ppermute(x, AXES, [(i, i ^ mask) for i in range(devices)])]
    gather x1 -> x0, local copies, waits for them, and re-layouts: 9.59 us -> none  [on_device(): nystrom = jnp.take(centers, local_nys, axis=0)]
    reduce_sum x3 -> x0, other arithmetic: 5.95 us -> none  [the longest x1 3.32 us: kernel(): rnorm = jnp.sum(rf * rf, axis=1)]
  transfers between devices with their start and end apart: 2 -> 16, of which waited for: 2 -> 15; matrix products, arithmetic and copies ran while one was open for 7% -> 0% of each run, Pallas kernels for 0% -> 4%
where the time goes in v1:
time: 127 us; the launch traced here: 126 us
  waiting for transfers between devices  62.2 us (49%)
  Pallas kernels  29.1 us (23%)
  starting transfers between devices  28.8 us (23%)
  other arithmetic  2.79 us (2%)
  local copies, waits for them, and re-layouts  2.41 us (2%)
    ppermute x16, waiting for transfers between devices, swap(): return lax.ppermute(x, AXES, [(i, i ^ mask) for i in range(devices)])  62.2 us
    ppermute x16, starting transfers between devices, swap(): return lax.ppermute(x, AXES, [(i, i ^ mask) for i in range(devices)])  28.8 us
    pallas_call x1, Pallas kernels, predict(): pl.pallas_call(predict_body, grid=(count // block,), in_specs=[pl.BlockSp...  10.5 us
    pallas_call x1, Pallas kernels, update(): pl.pallas_call(functools.partial(update_body, classes), grid=(classes //...  7.95 us
    pallas_call x1, Pallas kernels, prepare(): pl.pallas_call(functools.partial(prepare_body, classes), out_shape=[jax.S...  5.48 us
    pallas_call x1, Pallas kernels, pick_batch(): pl.pallas_call(pick_body, grid=(depth // block,), in_specs=[pl.BlockSpec(...  5.21 us
    add x8, other arithmetic, total_of(): keep = keep + swap(send, 1 << level, devices)  2.62 us
  transfers between devices with their start and end apart: 16, of which 15 were waited for; matrix products, arithmetic and copies ran while one was open for 0% of the time, Pallas kernels for 4%

profile of v1, /device:TPU:1, one launch (start us, length us, event | category | flops | bytes accessed | tf_op | source)
XLA Modules:
  0.0 126.1 jit_solution(3109113502097890336)
XLA Ops:
  0.6 5.2 %pick_batch.1 = (bf16[128,3072]{1,0:T(8,128)(2,1)}, bf16[128,3072]{1,0:T(8,128)(2,1)}) custom-call(s32[1,256]{1,0:T(1,128)} %bitcast.11, bf16[768,3072]{1,0:T(8,128)(2,1)} %centers_ref.3), custom_call_target="tpu_custom_call" | custom-call | flops 1207959552 | bytes 6291456 | tf_op jit(solution)/shard_map/pick_batch/pallas_call | solution.py:81
  5.8 0.1 collective-permute-start
  5.9 2.4 %collective-permute-done = bf16[128,3072]{1,0:T(8,128)(2,1)S(1)} collective-permute-done((bf16[128,3072]{1,0:T(8,128)(2,1)}, bf16[128,3072]{1,0:T(8,128)(2,1)S(1)}, u32[]{:S(2)}, u32[]{:S(2)}) %collective-permute-start) | collective-permute-done | bytes 786464 | tf_op jit(solution)/shard_map/ppermute | solution.py:303
  8.3 1.3 %add.24 = bf16[128,3072]{1,0:T(8,128)(2,1)S(1)} add(bf16[128,3072]{1,0:T(8,128)(2,1)} %get-tuple-element.11, bf16[128,3072]{1,0:T(8,128)(2,1)S(1)} %collective-permute-done) | non-fusion elementwise | flops 393216 | bytes 2359296 | tf_op jit(solution)/shard_map/add | solution.py:308
  9.7 2.4 %collective-permute-start.1 = (bf16[64,3072]{1,0:T(8,128)(2,1)S(1)}, bf16[64,3072]{1,0:T(8,128)(2,1)S(1)}, u32[]{:S(2)}, u32[]{:S(2)}) collective-permute-start(bf16[64,3072]{1,0:T(8,128)(2,1)S(1)} %slice.49), channel_id=1, source_target_pairs={{0,2},{1,3},{2,0},{3,1},{4,6},{5,7},{6,4},{7,5},{8,10},{9,11},{10,... | collective-permute-start | bytes 1179656 | tf_op jit(solution)/shard_map/ppermute | solution.py:303
  12.1 9.2 %collective-permute-done.1 = bf16[64,3072]{1,0:T(8,128)(2,1)S(1)} collective-permute-done((bf16[64,3072]{1,0:T(8,128)(2,1)S(1)}, bf16[64,3072]{1,0:T(8,128)(2,1)S(1)}, u32[]{:S(2)}, u32[]{:S(2)}) %collective-permute-start.1) | collective-permute-done | bytes 393248 | tf_op jit(solution)/shard_map/ppermute | solution.py:303
  21.3 0.1 slice_add_fusion
  21.4 1.3 %collective-permute-start.2 = (bf16[32,3072]{1,0:T(8,128)(2,1)S(1)}, bf16[32,3072]{1,0:T(8,128)(2,1)S(1)}, u32[]{:S(2)}, u32[]{:S(2)}) collective-permute-start(bf16[32,3072]{1,0:T(8,128)(2,1)S(1)} %slice.51), channel_id=1, source_target_pairs={{0,4},{1,5},{2,6},{3,7},{4,0},{5,1},{6,2},{7,3},{8,12},{9,13},{10,... | collective-permute-start | bytes 589832 | tf_op jit(solution)/shard_map/ppermute | solution.py:303
  22.7 4.3 %collective-permute-done.2 = bf16[32,3072]{1,0:T(8,128)(2,1)S(1)} collective-permute-done((bf16[32,3072]{1,0:T(8,128)(2,1)S(1)}, bf16[32,3072]{1,0:T(8,128)(2,1)S(1)}, u32[]{:S(2)}, u32[]{:S(2)}) %collective-permute-start.2) | collective-permute-done | bytes 196640 | tf_op jit(solution)/shard_map/ppermute | solution.py:303
  27.0 0.0 copy-start.4
  27.1 1.9 %collective-permute-start.3 = (bf16[16,3072]{1,0:T(8,128)(2,1)S(1)}, bf16[16,3072]{1,0:T(8,128)(2,1)S(1)}, u32[]{:S(2)}, u32[]{:S(2)}) collective-permute-start(bf16[16,3072]{1,0:T(8,128)(2,1)S(1)} %slice.53), channel_id=1, source_target_pairs={{0,8},{1,9},{2,10},{3,11},{4,12},{5,13},{6,14},{7,15},{8,0},{9,1},... | collective-permute-start | bytes 294920 | tf_op jit(solution)/shard_map/ppermute | solution.py:303
  29.0 3.5 %collective-permute-done.3 = bf16[16,3072]{1,0:T(8,128)(2,1)S(1)} collective-permute-done((bf16[16,3072]{1,0:T(8,128)(2,1)S(1)}, bf16[16,3072]{1,0:T(8,128)(2,1)S(1)}, u32[]{:S(2)}, u32[]{:S(2)}) %collective-permute-start.3) | collective-permute-done | bytes 98336 | tf_op jit(solution)/shard_map/ppermute | solution.py:303
  32.6 1.0 collective-permute-start.4
  33.5 4.5 %collective-permute-done.4 = bf16[16,3072]{1,0:T(8,128)(2,1)S(1)} collective-permute-done((bf16[16,3072]{1,0:T(8,128)(2,1)S(1)}, bf16[16,3072]{1,0:T(8,128)(2,1)S(1)}, u32[]{:S(2)}, u32[]{:S(2)}) %collective-permute-start.4) | collective-permute-done | bytes 98336 | tf_op jit(solution)/shard_map/ppermute | solution.py:303
  38.1 0.1 collective-permute-start.5
  38.1 4.5 %collective-permute-done.5 = bf16[32,3072]{1,0:T(8,128)(2,1)S(1)} collective-permute-done((bf16[32,3072]{1,0:T(8,128)(2,1)S(1)}, bf16[32,3072]{1,0:T(8,128)(2,1)S(1)}, u32[]{:S(2)}, u32[]{:S(2)}) %collective-permute-start.5) | collective-permute-done | bytes 196640 | tf_op jit(solution)/shard_map/ppermute | solution.py:303
  42.7 0.1 collective-permute-start.6
  42.7 6.6 %collective-permute-done.6 = bf16[64,3072]{1,0:T(8,128)(2,1)S(1)} collective-permute-done((bf16[64,3072]{1,0:T(8,128)(2,1)S(1)}, bf16[64,3072]{1,0:T(8,128)(2,1)S(1)}, u32[]{:S(2)}, u32[]{:S(2)}) %collective-permute-start.6) | collective-permute-done | bytes 393248 | tf_op jit(solution)/shard_map/ppermute | solution.py:303
  49.4 0.1 pad_maximum_fusion.mine_ref
  49.4 0.0 copy-start
  49.4 6.3 %collective-permute-start.7 = (bf16[128,3072]{1,0:T(8,128)(2,1)S(1)}, bf16[128,3072]{1,0:T(8,128)(2,1)S(1)}, u32[]{:S(2)}, u32[]{:S(2)}) collective-permute-start(bf16[128,3072]{1,0:T(8,128)(2,1)S(1)} %pad_maximum_fusion.mine_ref), channel_id=1, source_target_pairs={{0,1},{1,0},{2,3},{3,2},{4,5},{5,4},{6,7},{7,6},{8,9},{9,8},{10,11... | collective-permute-start | bytes 2359304 | tf_op jit(solution)/shard_map/ppermute | solution.py:303
  55.8 0.0 copy-done.4
  55.8 0.6 reshape.14.index_ref
  56.4 5.5 %prepare.1 = (bf16[1216,768]{1,0:T(8,128)(2,1)}, bf16[1216,768]{1,0:T(8,128)(2,1)}, f32[160,768]{1,0:T(8,128)}) custom-call(s32[1,320]{1,0:T(1,128)} %reshape.14.index_ref, f32[160,320]{1,0:T(8,128)} %bitcast.10, f32[1000,768]{1,0:T(8,128)} %bitcast.7), custom_call_target="tpu_custom_call" | custom-call | flops 235929600 | bytes 7471104 | tf_op jit(solution)/shard_map/prepare/pallas_call | solution.py:129
  61.8 0.0 copy-done
  61.8 0.0 collective-permute-done.7.other_ref
  61.8 0.0 copy-start.2
  61.9 0.9 copy-done.2
  62.7 10.5 %predict.1 = (f32[1216,128]{1,0:T(8,128)}, f32[1216,128]{1,0:T(8,128)}) custom-call(bf16[128,3072]{1,0:T(8,128)(2,1)} %copy-done, bf16[128,3072]{1,0:T(8,128)(2,1)} %copy-done.2, bf16[768,3072]{1,0:T(8,128)(2,1)} %centers_ref.3, bf16[1216,768]{1,0:T(8,128)(2,1)} %get-tuple-element.13.high_ref, bf16[1216,768]{1,0:T(8,128)(2,1)} %get-tuple-element.14.low_ref), custom_call_target="tpu_custom_call" | custom-call | flops 2642411520 | bytes 11272192 | tf_op jit(solution)/shard_map/predict/pallas_call | solution.py:191
  73.2 0.2 collective-permute-start.8
  73.4 2.1 %collective-permute-done.8 = f32[1216,128]{1,0:T(8,128)S(1)} collective-permute-done((f32[1216,128]{1,0:T(8,128)}, f32[1216,128]{1,0:T(8,128)S(1)}, u32[]{:S(2)}, u32[]{:S(2)}) %collective-permute-start.8) | collective-permute-done | bytes 622624 | tf_op jit(solution)/shard_map/ppermute | solution.py:303
  75.5 1.1 add.28
  76.6 1.3 %collective-permute-start.9 = (f32[608,128]{1,0:T(8,128)S(1)}, f32[608,128]{1,0:T(8,128)S(1)}, u32[]{:S(2)}, u32[]{:S(2)}) collective-permute-start(f32[608,128]{1,0:T(8,128)S(1)} %slice.55), channel_id=1, source_target_pairs={{0,2},{1,3},{2,0},{3,1},{4,6},{5,7},{6,4},{7,5},{8,10},{9,11},{10,... | collective-permute-start | bytes 933896 | tf_op jit(solution)/shard_map/ppermute | solution.py:303
  78.0 7.6 %collective-permute-done.9 = f32[608,128]{1,0:T(8,128)S(1)} collective-permute-done((f32[608,128]{1,0:T(8,128)S(1)}, f32[608,128]{1,0:T(8,128)S(1)}, u32[]{:S(2)}, u32[]{:S(2)}) %collective-permute-start.9) | collective-permute-done | bytes 311328 | tf_op jit(solution)/shard_map/ppermute | solution.py:303
  85.6 1.8 %collective-permute-start.10 = (f32[304,128]{1,0:T(8,128)S(1)}, f32[304,128]{1,0:T(8,128)S(1)}, u32[]{:S(2)}, u32[]{:S(2)}) collective-permute-start(f32[304,128]{1,0:T(8,128)S(1)} %slice.57), channel_id=1, source_target_pairs={{0,4},{1,5},{2,6},{3,7},{4,0},{5,1},{6,2},{7,3},{8,12},{9,13},{10,... | collective-permute-start | bytes 466952 | tf_op jit(solution)/shard_map/ppermute | solution.py:303
  87.4 3.4 %collective-permute-done.10 = f32[304,128]{1,0:T(8,128)S(1)} collective-permute-done((f32[304,128]{1,0:T(8,128)S(1)}, f32[304,128]{1,0:T(8,128)S(1)}, u32[]{:S(2)}, u32[]{:S(2)}) %collective-permute-start.10) | collective-permute-done | bytes 155680 | tf_op jit(solution)/shard_map/ppermute | solution.py:303
  90.8 1.9 %collective-permute-start.11 = (f32[152,128]{1,0:T(8,128)S(1)}, f32[152,128]{1,0:T(8,128)S(1)}, u32[]{:S(2)}, u32[]{:S(2)}) collective-permute-start(f32[152,128]{1,0:T(8,128)S(1)} %slice.59), channel_id=1, source_target_pairs={{0,8},{1,9},{2,10},{3,11},{4,12},{5,13},{6,14},{7,15},{8,0},{9,1},... | collective-permute-start | bytes 233480 | tf_op jit(solution)/shard_map/ppermute | solution.py:303
  92.8 2.3 %collective-permute-done.11 = f32[152,128]{1,0:T(8,128)S(1)} collective-permute-done((f32[152,128]{1,0:T(8,128)S(1)}, f32[152,128]{1,0:T(8,128)S(1)}, u32[]{:S(2)}, u32[]{:S(2)}) %collective-permute-start.11) | collective-permute-done | bytes 77856 | tf_op jit(solution)/shard_map/ppermute | solution.py:303
  95.1 2.0 %collective-permute-start.12 = (f32[152,128]{1,0:T(8,128)S(1)}, f32[152,128]{1,0:T(8,128)S(1)}, u32[]{:S(2)}, u32[]{:S(2)}) collective-permute-start(f32[152,128]{1,0:T(8,128)S(1)} %slice_add_fusion.5), channel_id=1, source_target_pairs={{0,8},{1,9},{2,10},{3,11},{4,12},{5,13},{6,14},{7,15},{8,0},{9,1},... | collective-permute-start | bytes 233480 | tf_op jit(solution)/shard_map/ppermute | solution.py:303
  97.1 2.2 %collective-permute-done.12 = f32[152,128]{1,0:T(8,128)S(1)} collective-permute-done((f32[152,128]{1,0:T(8,128)S(1)}, f32[152,128]{1,0:T(8,128)S(1)}, u32[]{:S(2)}, u32[]{:S(2)}) %collective-permute-start.12) | collective-permute-done | bytes 77856 | tf_op jit(solution)/shard_map/ppermute | solution.py:303
  99.3 1.5 %collective-permute-start.13 = (f32[304,128]{1,0:T(8,128)S(1)}, f32[304,128]{1,0:T(8,128)S(1)}, u32[]{:S(2)}, u32[]{:S(2)}) collective-permute-start(f32[304,128]{1,0:T(8,128)S(1)} %pad_maximum_fusion.5), channel_id=1, source_target_pairs={{0,4},{1,5},{2,6},{3,7},{4,0},{5,1},{6,2},{7,3},{8,12},{9,13},{10,... | collective-permute-start | bytes 466952 | tf_op jit(solution)/shard_map/ppermute | solution.py:303
  100.8 3.3 %collective-permute-done.13 = f32[304,128]{1,0:T(8,128)S(1)} collective-permute-done((f32[304,128]{1,0:T(8,128)S(1)}, f32[304,128]{1,0:T(8,128)S(1)}, u32[]{:S(2)}, u32[]{:S(2)}) %collective-permute-start.13) | collective-permute-done | bytes 155680 | tf_op jit(solution)/shard_map/ppermute | solution.py:303
  104.2 1.3 %collective-permute-start.14 = (f32[608,128]{1,0:T(8,128)S(1)}, f32[608,128]{1,0:T(8,128)S(1)}, u32[]{:S(2)}, u32[]{:S(2)}) collective-permute-start(f32[608,128]{1,0:T(8,128)S(1)} %pad_maximum_fusion.3), channel_id=1, source_target_pairs={{0,2},{1,3},{2,0},{3,1},{4,6},{5,7},{6,4},{7,5},{8,10},{9,11},{10,... | collective-permute-start | bytes 933896 | tf_op jit(solution)/shard_map/ppermute | solution.py:303
  105.5 4.5 %collective-permute-done.14 = f32[608,128]{1,0:T(8,128)S(1)} collective-permute-done((f32[608,128]{1,0:T(8,128)S(1)}, f32[608,128]{1,0:T(8,128)S(1)}, u32[]{:S(2)}, u32[]{:S(2)}) %collective-permute-start.14) | collective-permute-done | bytes 311328 | tf_op jit(solution)/shard_map/ppermute | solution.py:303
  110.0 0.0 copy-start.1
  110.0 5.6 %collective-permute-start.15 = (f32[1216,128]{1,0:T(8,128)S(1)}, f32[1216,128]{1,0:T(8,128)S(1)}, u32[]{:S(2)}, u32[]{:S(2)}) collective-permute-start(f32[1216,128]{1,0:T(8,128)S(1)} %pad_maximum_fusion.1.mine_ref), channel_id=1, source_target_pairs={{0,1},{1,0},{2,3},{3,2},{4,5},{5,4},{6,7},{7,6},{8,9},{9,8},{10,11... | collective-permute-start | bytes 1867784 | tf_op jit(solution)/shard_map/ppermute | solution.py:303
  115.6 1.7 %collective-permute-done.15.other_ref = f32[1216,128]{1,0:T(8,128)S(1)} collective-permute-done((f32[1216,128]{1,0:T(8,128)S(1)}, f32[1216,128]{1,0:T(8,128)S(1)}, u32[]{:S(2)}, u32[]{:S(2)}) %collective-permute-start.15) | collective-permute-done | bytes 622624 | tf_op jit(solution)/shard_map/ppermute | solution.py:303
  117.3 0.0 copy-start.3
  117.3 0.0 copy-done.1
  117.3 0.8 copy-done.3
  118.2 7.9 %update.1 = (f32[1000,768]{1,0:T(8,128)}, f32[1000,256]{1,0:T(8,128)}) custom-call(f32[1216,128]{1,0:T(8,128)} %copy-done.1, f32[1216,128]{1,0:T(8,128)} %copy-done.3, f32[1000,256]{1,0:T(8,128)} %bitcast.9, s32[1,256]{1,0:T(1,128)} %bitcast.12, f32[1,160]{1,0:T(1,128)} %bitcast.13, f32[160,768]{1,0:T(8,128)} %get-tuple-element.17.spread_ref, ...), custom_call_target="tpu_custom_call" | custom-call | flops 1368391680 | bytes 8192000 | tf_op jit(solution)/shard_map/update/pallas_call | solution.py:267
  (16 shorter events, 0.3 us)
Async XLA Ops:
  5.8 2.5 %collective-permute-start = (bf16[128,3072]{1,0:T(8,128)(2,1)}, bf16[128,3072]{1,0:T(8,128)(2,1)S(1)}, u32[]{:S(2)}, u32[]{:S(2)}) collective-permute-start(bf16[128,3072]{1,0:T(8,128)(2,1)} %get-tuple-element.12), channel_id=1, source_target_pairs={{0,1},{1,0},{2,3},{3,2},{4,5},{5,4},{6,7},{7,6},{8,9},{9,8},{10,11... | collective-permute-start | bytes 2359304 | tf_op jit(solution)/shard_map/ppermute | solution.py:303
  9.7 11.6 %collective-permute-start.1 = (bf16[64,3072]{1,0:T(8,128)(2,1)S(1)}, bf16[64,3072]{1,0:T(8,128)(2,1)S(1)}, u32[]{:S(2)}, u32[]{:S(2)}) collective-permute-start(bf16[64,3072]{1,0:T(8,128)(2,1)S(1)} %slice.49), channel_id=1, source_target_pairs={{0,2},{1,3},{2,0},{3,1},{4,6},{5,7},{6,4},{7,5},{8,10},{9,11},{10,... | collective-permute-start | bytes 1179656 | tf_op jit(solution)/shard_map/ppermute | solution.py:303
  21.4 5.6 %collective-permute-start.2 = (bf16[32,3072]{1,0:T(8,128)(2,1)S(1)}, bf16[32,3072]{1,0:T(8,128)(2,1)S(1)}, u32[]{:S(2)}, u32[]{:S(2)}) collective-permute-start(bf16[32,3072]{1,0:T(8,128)(2,1)S(1)} %slice.51), channel_id=1, source_target_pairs={{0,4},{1,5},{2,6},{3,7},{4,0},{5,1},{6,2},{7,3},{8,12},{9,13},{10,... | collective-permute-start | bytes 589832 | tf_op jit(solution)/shard_map/ppermute | solution.py:303
  27.0 28.7 %copy-start.4 = (s32[320]{0:T(512)S(1)}, s32[320]{0:T(512)}, u32[]{:S(2)}) copy-start(s32[320]{0:T(512)} %param.11) | copy-start | bytes 3844
  27.1 5.5 %collective-permute-start.3 = (bf16[16,3072]{1,0:T(8,128)(2,1)S(1)}, bf16[16,3072]{1,0:T(8,128)(2,1)S(1)}, u32[]{:S(2)}, u32[]{:S(2)}) collective-permute-start(bf16[16,3072]{1,0:T(8,128)(2,1)S(1)} %slice.53), channel_id=1, source_target_pairs={{0,8},{1,9},{2,10},{3,11},{4,12},{5,13},{6,14},{7,15},{8,0},{9,1},... | collective-permute-start | bytes 294920 | tf_op jit(solution)/shard_map/ppermute | solution.py:303
  32.6 5.5 %collective-permute-start.4 = (bf16[16,3072]{1,0:T(8,128)(2,1)S(1)}, bf16[16,3072]{1,0:T(8,128)(2,1)S(1)}, u32[]{:S(2)}, u32[]{:S(2)}) collective-permute-start(bf16[16,3072]{1,0:T(8,128)(2,1)S(1)} %slice_add_fusion.4), channel_id=1, source_target_pairs={{0,8},{1,9},{2,10},{3,11},{4,12},{5,13},{6,14},{7,15},{8,0},{9,1},... | collective-permute-start | bytes 294920 | tf_op jit(solution)/shard_map/ppermute | solution.py:303
  38.1 4.6 %collective-permute-start.5 = (bf16[32,3072]{1,0:T(8,128)(2,1)S(1)}, bf16[32,3072]{1,0:T(8,128)(2,1)S(1)}, u32[]{:S(2)}, u32[]{:S(2)}) collective-permute-start(bf16[32,3072]{1,0:T(8,128)(2,1)S(1)} %pad_maximum_fusion.4), channel_id=1, source_target_pairs={{0,4},{1,5},{2,6},{3,7},{4,0},{5,1},{6,2},{7,3},{8,12},{9,13},{10,... | collective-permute-start | bytes 589832 | tf_op jit(solution)/shard_map/ppermute | solution.py:303
  42.7 6.7 %collective-permute-start.6 = (bf16[64,3072]{1,0:T(8,128)(2,1)S(1)}, bf16[64,3072]{1,0:T(8,128)(2,1)S(1)}, u32[]{:S(2)}, u32[]{:S(2)}) collective-permute-start(bf16[64,3072]{1,0:T(8,128)(2,1)S(1)} %pad_maximum_fusion.2), channel_id=1, source_target_pairs={{0,2},{1,3},{2,0},{3,1},{4,6},{5,7},{6,4},{7,5},{8,10},{9,11},{10,... | collective-permute-start | bytes 1179656 | tf_op jit(solution)/shard_map/ppermute | solution.py:303
  49.4 12.4 %copy-start = (bf16[128,3072]{1,0:T(8,128)(2,1)}, bf16[128,3072]{1,0:T(8,128)(2,1)S(1)}, u32[]{:S(2)}) copy-start(bf16[128,3072]{1,0:T(8,128)(2,1)S(1)} %pad_maximum_fusion.mine_ref) | copy-start | bytes 2359300
  49.4 12.4 %collective-permute-start.7 = (bf16[128,3072]{1,0:T(8,128)(2,1)S(1)}, bf16[128,3072]{1,0:T(8,128)(2,1)S(1)}, u32[]{:S(2)}, u32[]{:S(2)}) collective-permute-start(bf16[128,3072]{1,0:T(8,128)(2,1)S(1)} %pad_maximum_fusion.mine_ref), channel_id=1, source_target_pairs={{0,1},{1,0},{2,3},{3,2},{4,5},{5,4},{6,7},{7,6},{8,9},{9,8},{10,11... | collective-permute-start | bytes 2359304 | tf_op jit(solution)/shard_map/ppermute | solution.py:303
  61.8 0.9 copy-start.2
  73.2 2.3 %collective-permute-start.8 = (f32[1216,128]{1,0:T(8,128)}, f32[1216,128]{1,0:T(8,128)S(1)}, u32[]{:S(2)}, u32[]{:S(2)}) collective-permute-start(f32[1216,128]{1,0:T(8,128)} %get-tuple-element.16), channel_id=1, source_target_pairs={{0,1},{1,0},{2,3},{3,2},{4,5},{5,4},{6,7},{7,6},{8,9},{9,8},{10,11... | collective-permute-start | bytes 1867784 | tf_op jit(solution)/shard_map/ppermute | solution.py:303
  76.6 8.9 %collective-permute-start.9 = (f32[608,128]{1,0:T(8,128)S(1)}, f32[608,128]{1,0:T(8,128)S(1)}, u32[]{:S(2)}, u32[]{:S(2)}) collective-permute-start(f32[608,128]{1,0:T(8,128)S(1)} %slice.55), channel_id=1, source_target_pairs={{0,2},{1,3},{2,0},{3,1},{4,6},{5,7},{6,4},{7,5},{8,10},{9,11},{10,... | collective-permute-start | bytes 933896 | tf_op jit(solution)/shard_map/ppermute | solution.py:303
  85.6 5.2 %collective-permute-start.10 = (f32[304,128]{1,0:T(8,128)S(1)}, f32[304,128]{1,0:T(8,128)S(1)}, u32[]{:S(2)}, u32[]{:S(2)}) collective-permute-start(f32[304,128]{1,0:T(8,128)S(1)} %slice.57), channel_id=1, source_target_pairs={{0,4},{1,5},{2,6},{3,7},{4,0},{5,1},{6,2},{7,3},{8,12},{9,13},{10,... | collective-permute-start | bytes 466952 | tf_op jit(solution)/shard_map/ppermute | solution.py:303
  90.8 4.2 %collective-permute-start.11 = (f32[152,128]{1,0:T(8,128)S(1)}, f32[152,128]{1,0:T(8,128)S(1)}, u32[]{:S(2)}, u32[]{:S(2)}) collective-permute-start(f32[152,128]{1,0:T(8,128)S(1)} %slice.59), channel_id=1, source_target_pairs={{0,8},{1,9},{2,10},{3,11},{4,12},{5,13},{6,14},{7,15},{8,0},{9,1},... | collective-permute-start | bytes 233480 | tf_op jit(solution)/shard_map/ppermute | solution.py:303
  95.1 4.2 %collective-permute-start.12 = (f32[152,128]{1,0:T(8,128)S(1)}, f32[152,128]{1,0:T(8,128)S(1)}, u32[]{:S(2)}, u32[]{:S(2)}) collective-permute-start(f32[152,128]{1,0:T(8,128)S(1)} %slice_add_fusion.5), channel_id=1, source_target_pairs={{0,8},{1,9},{2,10},{3,11},{4,12},{5,13},{6,14},{7,15},{8,0},{9,1},... | collective-permute-start | bytes 233480 | tf_op jit(solution)/shard_map/ppermute | solution.py:303
  99.3 4.8 %collective-permute-start.13 = (f32[304,128]{1,0:T(8,128)S(1)}, f32[304,128]{1,0:T(8,128)S(1)}, u32[]{:S(2)}, u32[]{:S(2)}) collective-permute-start(f32[304,128]{1,0:T(8,128)S(1)} %pad_maximum_fusion.5), channel_id=1, source_target_pairs={{0,4},{1,5},{2,6},{3,7},{4,0},{5,1},{6,2},{7,3},{8,12},{9,13},{10,... | collective-permute-start | bytes 466952 | tf_op jit(solution)/shard_map/ppermute | solution.py:303
  104.2 5.8 %collective-permute-start.14 = (f32[608,128]{1,0:T(8,128)S(1)}, f32[608,128]{1,0:T(8,128)S(1)}, u32[]{:S(2)}, u32[]{:S(2)}) collective-permute-start(f32[608,128]{1,0:T(8,128)S(1)} %pad_maximum_fusion.3), channel_id=1, source_target_pairs={{0,2},{1,3},{2,0},{3,1},{4,6},{5,7},{6,4},{7,5},{8,10},{9,11},{10,... | collective-permute-start | bytes 933896 | tf_op jit(solution)/shard_map/ppermute | solution.py:303
  110.0 7.3 %copy-start.1 = (f32[1216,128]{1,0:T(8,128)}, f32[1216,128]{1,0:T(8,128)S(1)}, u32[]{:S(2)}) copy-start(f32[1216,128]{1,0:T(8,128)S(1)} %pad_maximum_fusion.1.mine_ref) | copy-start | bytes 1867780
  110.0 7.3 %collective-permute-start.15 = (f32[1216,128]{1,0:T(8,128)S(1)}, f32[1216,128]{1,0:T(8,128)S(1)}, u32[]{:S(2)}, u32[]{:S(2)}) collective-permute-start(f32[1216,128]{1,0:T(8,128)S(1)} %pad_maximum_fusion.1.mine_ref), channel_id=1, source_target_pairs={{0,1},{1,0},{2,3},{3,2},{4,5},{5,4},{6,7},{7,6},{8,9},{9,8},{10,11... | collective-permute-start | bytes 1867784 | tf_op jit(solution)/shard_map/ppermute | solution.py:303
  117.3 0.8 copy-start.3

commit v2 on v1

--- a/solution.py
+++ b/solution.py
@@ -10,9 +10,6 @@
 
 F32 = jnp.float32
 BF16 = jnp.bfloat16
-AXES = ("center", "sub")
-LEVELS = 4
-CHUNKS = 1 << LEVELS
 LANE = 128
 NT = (((1,), (1,)), ((), ()))
 NN = (((1,), (0,)), ((), ()))
@@ -26,13 +23,6 @@
 
 def position():
     return lax.axis_index("center") * 2 + lax.axis_index("sub")
-
-
-def reversed_bits(value, bits):
-    out = 0
-    for bit in range(bits):
-        out = out + ((value >> bit) & 1) * (1 << (bits - 1 - bit))
-    return out
 
 
 def column_of(row, width):
@@ -56,21 +46,20 @@
 
 def pick_body(index_ref, centers_ref, keep_ref, send_ref, pick_ref):
     me = position()
-    turn = reversed_bits(me, LEVELS)
     rows = index_ref.shape[1]
-    size = rows // CHUNKS
+    half = rows // 2
     count = centers_ref.shape[0]
 
     @pl.when(pl.program_id(0) == 0)
     def _():
         pick = pick_rows(index_ref, count, me * count, F32, 1.0)
-        for chunk in range(CHUNKS):
-            to = pl.multiple_of((chunk ^ turn) * size, size)
-            pick_ref[pl.ds(to, size), :] = pick[chunk * size : (chunk + 1) * size].astype(BF16)
+        mine = pl.multiple_of((me & 1) * half, half)
+        pick_ref[pl.ds(mine, half), :] = pick[:half].astype(BF16)
+        pick_ref[pl.ds(half - mine, half), :] = pick[half:].astype(BF16)
 
     found = dot(pick_ref[...], centers_ref[...], NN).astype(BF16)
-    keep_ref[...] = found[: rows // 2]
-    send_ref[...] = found[rows // 2 :]
+    keep_ref[...] = found[:half]
+    send_ref[...] = found[half:]
 
 
 def pick_batch(batch_index, centers):
@@ -96,13 +85,11 @@
     )(batch_index, centers)
 
 
-def prepare_body(classes, index_ref, eigvec_ref, weights_ref, high_ref, low_ref, spread_ref, all_ref):
+def prepare_body(classes, index_ref, eigvec_ref, weights_ref, high_ref, low_ref, spread_ref):
     me = position()
-    turn = reversed_bits(me >> 1, LEVELS - 1)
     rank, points = eigvec_ref.shape
     count = weights_ref.shape[1]
     padded = high_ref.shape[0]
-    size = padded // (CHUNKS // 2)
     local = index_ref[...] - me * count
     slots = lax.broadcasted_iota(jnp.int32, (count, points), 0)
     pick = jnp.where(slots == local, 1.0, 0.0).astype(BF16)
@@ -113,14 +100,9 @@
     low = (rest - mid.astype(F32)).astype(BF16)
     spread = dot(high, pick, NT) + dot(mid, pick, NT) + dot(low, pick, NT)
     spread_ref[...] = spread
-    all_ref[:classes] = weights_ref[...]
-    all_ref[classes : classes + rank] = spread
-    all_ref[classes + rank :] = jnp.zeros((padded - classes - rank, count), F32)
-    for chunk in range(CHUNKS // 2):
-        to = pl.multiple_of((chunk ^ turn) * size, 8)
-        high, low = two(all_ref[pl.ds(to, size), :])
-        high_ref[chunk * size : (chunk + 1) * size] = high
-        low_ref[chunk * size : (chunk + 1) * size] = low
+    blank = jnp.zeros((padded - classes - rank, count), F32)
+    stacked = jnp.concatenate([weights_ref[...], spread, blank])
+    high_ref[...], low_ref[...] = two(stacked)
 
 
 def prepare(nys_index, eigvec, weights, padded):
@@ -133,7 +115,6 @@
             jax.ShapeDtypeStruct((padded, count), BF16),
             jax.ShapeDtypeStruct((rank, count), F32),
         ],
-        scratch_shapes=[pltpu.VMEM((padded, count), F32)],
         compiler_params=pltpu.CompilerParams(vmem_limit_bytes=VMEM_LIMIT),
         cost_estimate=pl.CostEstimate(
             flops=6 * rank * points * count, bytes_accessed=8 * padded * count, transcendentals=0
@@ -144,19 +125,15 @@
 
 def predict_body(mine_ref, other_ref, centers_ref, high_ref, low_ref, keep_ref, send_ref, batch_ref, norm_ref, total_ref):
     me = position()
-    turn = reversed_bits(me, LEVELS)
     rows, depth = batch_ref.shape
     half = rows // 2
-    size = rows // CHUNKS
     step = pl.program_id(0)
 
     @pl.when(step == 0)
     def _():
-        for chunk in range(CHUNKS):
-            ref = mine_ref if chunk < CHUNKS // 2 else other_ref
-            at = chunk % (CHUNKS // 2) * size
-            to = pl.multiple_of((chunk ^ turn) * size, size)
-            batch_ref[pl.ds(to, size), :] = ref[at : at + size, :]
+        at = pl.multiple_of((me & 1) * half, half)
+        batch_ref[pl.ds(at, half), :] = mine_ref[...]
+        batch_ref[pl.ds(half - at, half), :] = other_ref[...]
         batch = batch_ref[...].astype(F32)
         norm = jnp.sum(batch * batch, axis=1, keepdims=True)
         norm_ref[...] = jnp.broadcast_to(norm, (rows, LANE)).T[:8]
@@ -227,15 +204,11 @@
 
     @pl.when(step == 0)
     def _():
-        turn = reversed_bits(me >> 1, LEVELS - 1)
-        size = mine_ref.shape[0] // (CHUNKS // 2)
         lower = (me & 1) == 0
-        for chunk in range(CHUNKS // 2):
-            to = pl.multiple_of((chunk ^ turn) * size, 8)
-            mine = mine_ref[chunk * size : (chunk + 1) * size]
-            other = other_ref[chunk * size : (chunk + 1) * size]
-            total_ref[pl.ds(to, size), :half] = jnp.where(lower, mine, other)
-            total_ref[pl.ds(to, size), half:] = jnp.where(lower, other, mine)
+        mine = mine_ref[...]
+        other = other_ref[...]
+        total_ref[:, :half] = jnp.where(lower, mine, other)
+        total_ref[:, half:] = jnp.where(lower, other, mine)
         value = eigval_ref[...]
         lowest = jnp.min(value, axis=1, keepdims=True)
         scaled = (1.0 - lowest / value) / value
@@ -299,33 +272,32 @@
     )(mine, other, targets, batch_index, eigval, spread, weights)
 
 
-def swap(x, mask, devices):
-    return lax.ppermute(x, AXES, [(i, i ^ mask) for i in range(devices)])
-
-
-def total_of(keep, send, devices):
-    for level in range(LEVELS):
-        keep = keep + swap(send, 1 << level, devices)
-        if level < LEVELS - 1:
-            half = keep.shape[0] // 2
-            keep, send = keep[:half], keep[half:]
-    for level in range(LEVELS, int(math.log2(devices))):
-        keep = keep + swap(keep, 1 << level, devices)
-    for level in reversed(range(1, LEVELS)):
-        keep = jnp.concatenate([keep, swap(keep, 1 << level, devices)])
-    return keep, swap(keep, 1, devices)
-
-
-def on_device(devices, centers, weights, targets, batch_index, nys_index, eigvec, eigval):
+def swap(x):
+    return lax.ppermute(x, "sub", [(0, 1), (1, 0)])
+
+
+def shuffle(x):
+    return lax.all_to_all(x, "center", 0, 0, tiled=True)
+
+
+def total_of(keep, send, chips):
+    rows, width = keep.shape
+    parts = shuffle(keep + swap(send)).reshape(chips, rows // chips, width)
+    part = jnp.sum(parts.astype(F32), axis=0).astype(keep.dtype)
+    whole = shuffle(jnp.broadcast_to(part, parts.shape).reshape(rows, width))
+    return whole, swap(whole)
+
+
+def on_device(chips, centers, weights, targets, batch_index, nys_index, eigvec, eigval):
     rows = batch_index.shape[0]
     classes = weights.shape[1]
     rank = eigvec.shape[1]
-    unit = 8 * CHUNKS // 2
+    unit = 8 * chips
     padded = -(-(classes + rank) // unit) * unit
     batch_index = batch_index.reshape(1, rows)
-    mine, other = total_of(*pick_batch(batch_index, centers), devices)
+    mine, other = total_of(*pick_batch(batch_index, centers), chips)
     high, low, spread = prepare(nys_index.reshape(1, -1), eigvec.T, weights.T, padded)
-    mine, other = total_of(*predict(mine, other, centers, high, low), devices)
+    mine, other = total_of(*predict(mine, other, centers, high, low), chips)
     new_weights, predictions = update(
         mine, other, targets.T, batch_index, eigval.reshape(1, rank), spread, weights.T
     )
@@ -333,9 +305,8 @@
 
 
 def solution(mesh):
-    devices = mesh.shape["center"] * mesh.shape["sub"]
     return jax.shard_map(
-        functools.partial(on_device, devices),
+        functools.partial(on_device, mesh.shape["center"]),
         mesh=mesh,
         in_specs=(
             P(("parts", "center", "sub"), None),

time: 127 us -> 134 us (1.055)
  blocking collectives: 0 us -> 88 us
  waiting for transfers between devices: 62.2 us -> 6.35 us
  starting transfers between devices: 28.8 us -> 3.97 us
    all_to_all x0 -> x4, blocking collectives: none -> 88 us  [shuffle(): return lax.all_to_all(x, 'center', 0, 0, tiled=True)]
    ppermute x16 -> x4, waiting for transfers between devices: 62.2 us -> 6.35 us  [swap(): return lax.ppermute(x, 'sub', [(0, 1), (1, 0)])]
    ppermute x16 -> x4, starting transfers between devices: 28.8 us -> 3.97 us  [swap(): return lax.ppermute(x, 'sub', [(0, 1), (1, 0)])]
  transfers between devices with their start and end apart: 16 -> 4, of which waited for: 15 -> 3; matrix products, arithmetic and copies ran while one was open for 0% -> 0% of each run, Pallas kernels for 4% -> 4%
where the time goes in v2:
time: 134 us; the launch traced here: 133 us
  blocking collectives  88 us (66%)
  Pallas kernels  29.4 us (22%)
  waiting for transfers between devices  6.35 us (5%)
  starting transfers between devices  3.97 us (3%)
  other arithmetic  2.62 us (2%)
  local copies, waits for them, and re-layouts  2.37 us (2%)
    all_to_all x4, blocking collectives, shuffle(): return lax.all_to_all(x, 'center', 0, 0, tiled=True)  88 us
    pallas_call x1, Pallas kernels, predict(): pl.pallas_call(predict_body, grid=(count // block,), in_specs=[pl.BlockSp...  10.9 us
    pallas_call x1, Pallas kernels, update(): pl.pallas_call(functools.partial(update_body, classes), grid=(classes //...  7.95 us
    ppermute x4, waiting for transfers between devices, swap(): return lax.ppermute(x, 'sub', [(0, 1), (1, 0)])  6.35 us
    pallas_call x1, Pallas kernels, prepare(): pl.pallas_call(functools.partial(prepare_body, classes), out_shape=[jax.S...  5.39 us
    pallas_call x1, Pallas kernels, pick_batch(): pl.pallas_call(pick_body, grid=(depth // block,), in_specs=[pl.BlockSpec(...  5.22 us
    ppermute x4, starting transfers between devices, swap(): return lax.ppermute(x, 'sub', [(0, 1), (1, 0)])  3.97 us
  transfers between devices with their start and end apart: 4, of which 3 were waited for; matrix products, arithmetic and copies ran while one was open for 0% of the time, Pallas kernels for 4%

profile of v2, /device:TPU:1, one launch (start us, length us, event | category | flops | bytes accessed | tf_op | source)
XLA Modules:
  0.0 133.4 jit_solution(18355032584168797172)
XLA Ops:
  0.6 5.2 %pick_batch.1 = (bf16[128,3072]{1,0:T(8,128)(2,1)}, bf16[128,3072]{1,0:T(8,128)(2,1)}) custom-call(s32[1,256]{1,0:T(1,128)} %bitcast.21, bf16[768,3072]{1,0:T(8,128)(2,1)} %centers_ref.3), custom_call_target="tpu_custom_call" | custom-call | flops 1207959552 | bytes 6291456 | tf_op jit(solution)/shard_map/pick_batch/pallas_call | solution.py:70
  5.8 0.1 collective-permute-start
  5.9 2.4 %collective-permute-done = bf16[128,3072]{1,0:T(8,128)(2,1)S(1)} collective-permute-done((bf16[128,3072]{1,0:T(8,128)(2,1)}, bf16[128,3072]{1,0:T(8,128)(2,1)S(1)}, u32[]{:S(2)}, u32[]{:S(2)}) %collective-permute-start) | collective-permute-done | bytes 786464 | tf_op jit(solution)/shard_map/ppermute | solution.py:276
  8.3 0.0 copy-start.4
  8.3 1.3 add.6
  9.7 25.7 %all_to_all.34 = bf16[8,16,3072]{2,1,0:T(8,128)(2,1)S(1)} all-to-all(bf16[8,16,3072]{2,1,0:T(8,128)(2,1)S(1)} %bitcast.15), channel_id=1, replica_groups=mesh['parts'=2,'center'=8,'sub'=2] {'center'}, dimensions={0} | all-to-all | bytes 1572864 | tf_op jit(solution)/shard_map/all_to_all | solution.py:280
  35.4 0.1 reduce_sum.21
  35.5 0.1 broadcast_in_dim.6
  35.6 23.2 %all_to_all.35 = bf16[8,16,3072]{2,1,0:T(8,128)(2,1)S(1)} all-to-all(bf16[8,16,3072]{2,1,0:T(8,128)(2,1)S(1)} %broadcast_in_dim.6), channel_id=1, replica_groups=mesh['parts'=2,'center'=8,'sub'=2] {'center'}, dimensions={0} | all-to-all | bytes 1572864 | tf_op jit(solution)/shard_map/all_to_all | solution.py:280
  58.8 0.0 copy-start
  58.8 1.8 %collective-permute-start.1 = (bf16[128,3072]{1,0:T(8,128)(2,1)S(1)}, bf16[128,3072]{1,0:T(8,128)(2,1)S(1)}, u32[]{:S(2)}, u32[]{:S(2)}) collective-permute-start(bf16[128,3072]{1,0:T(8,128)(2,1)S(1)} %bitcast.13), channel_id=1, source_target_pairs={{0,1},{1,0},{2,3},{3,2},{4,5},{5,4},{6,7},{7,6},{8,9},{9,8},{10,11... | collective-permute-start | bytes 2359304 | tf_op jit(solution)/shard_map/ppermute | solution.py:276
  60.7 0.0 copy-done.4
  60.7 0.5 reshape.30.index_ref
  61.2 5.4 %prepare.1 = (bf16[1216,768]{1,0:T(8,128)(2,1)}, bf16[1216,768]{1,0:T(8,128)(2,1)}, f32[160,768]{1,0:T(8,128)}) custom-call(s32[1,320]{1,0:T(1,128)} %reshape.30.index_ref, f32[160,320]{1,0:T(8,128)} %bitcast.20, f32[1000,768]{1,0:T(8,128)} %bitcast.11), custom_call_target="tpu_custom_call" | custom-call | flops 235929600 | bytes 7471104 | tf_op jit(solution)/shard_map/prepare/pallas_call | solution.py:111
  66.6 0.0 collective-permute-done.1.other_ref
  66.6 0.0 copy-start.2
  66.6 0.0 copy-done
  66.6 0.9 copy-done.2
  67.5 10.9 %predict.1 = (f32[1216,128]{1,0:T(8,128)}, f32[1216,128]{1,0:T(8,128)}) custom-call(bf16[128,3072]{1,0:T(8,128)(2,1)} %bitcast.14, bf16[128,3072]{1,0:T(8,128)(2,1)} %copy-done.2, bf16[768,3072]{1,0:T(8,128)(2,1)} %centers_ref.3, bf16[1216,768]{1,0:T(8,128)(2,1)} %get-tuple-element.13.high_ref, bf16[1216,768]{1,0:T(8,128)(2,1)} %get-tuple-element.14.low_ref), custom_call_target="tpu_custom_call" | custom-call | flops 2642411520 | bytes 11272192 | tf_op jit(solution)/shard_map/predict/pallas_call | solution.py:168
  78.4 0.0 collective-permute-start.2
  78.4 2.2 %collective-permute-done.2 = f32[1216,128]{1,0:T(8,128)S(1)} collective-permute-done((f32[1216,128]{1,0:T(8,128)}, f32[1216,128]{1,0:T(8,128)S(1)}, u32[]{:S(2)}, u32[]{:S(2)}) %collective-permute-start.2) | collective-permute-done | bytes 622624 | tf_op jit(solution)/shard_map/ppermute | solution.py:276
  80.6 1.1 add.7
  81.8 19.2 %all_to_all.36 = f32[8,152,128]{2,1,0:T(8,128)S(1)} all-to-all(f32[8,152,128]{2,1,0:T(8,128)S(1)} %bitcast.16), channel_id=1, replica_groups=mesh['parts'=2,'center'=8,'sub'=2] {'center'}, dimensions={0} | all-to-all | bytes 1245184 | tf_op jit(solution)/shard_map/all_to_all | solution.py:280
  101.1 19.9 %all_to_all.37 = f32[8,152,128]{2,1,0:T(8,128)S(1)} all-to-all(f32[8,152,128]{2,1,0:T(8,128)S(1)} %broadcast_in_dim.7), channel_id=1, replica_groups=mesh['parts'=2,'center'=8,'sub'=2] {'center'}, dimensions={0} | all-to-all | bytes 1245184 | tf_op jit(solution)/shard_map/all_to_all | solution.py:280
  120.9 0.0 copy-start.1
  120.9 2.1 %collective-permute-start.3 = (f32[1216,128]{1,0:T(8,128)S(1)}, f32[1216,128]{1,0:T(8,128)S(1)}, u32[]{:S(2)}, u32[]{:S(2)}) collective-permute-start(f32[1216,128]{1,0:T(8,128)S(1)} %bitcast.17), channel_id=1, source_target_pairs={{0,1},{1,0},{2,3},{3,2},{4,5},{5,4},{6,7},{7,6},{8,9},{9,8},{10,11... | collective-permute-start | bytes 1867784 | tf_op jit(solution)/shard_map/ppermute | solution.py:276
  123.0 1.7 %collective-permute-done.3.other_ref = f32[1216,128]{1,0:T(8,128)S(1)} collective-permute-done((f32[1216,128]{1,0:T(8,128)S(1)}, f32[1216,128]{1,0:T(8,128)S(1)}, u32[]{:S(2)}, u32[]{:S(2)}) %collective-permute-start.3) | collective-permute-done | bytes 622624 | tf_op jit(solution)/shard_map/ppermute | solution.py:276
  124.6 0.0 copy-start.3
  124.6 0.0 copy-done.1
  124.6 0.8 copy-done.3
  125.5 7.9 %update.1 = (f32[1000,768]{1,0:T(8,128)}, f32[1000,256]{1,0:T(8,128)}) custom-call(f32[1216,128]{1,0:T(8,128)} %bitcast.18, f32[1216,128]{1,0:T(8,128)} %copy-done.3, f32[1000,256]{1,0:T(8,128)} %bitcast.19, s32[1,256]{1,0:T(1,128)} %bitcast.22, f32[1,160]{1,0:T(1,128)} %bitcast.23, f32[160,768]{1,0:T(8,128)} %get-tuple-element.17.spread_ref, ...), custom_call_target="tpu_custom_call" | custom-call | flops 1368391680 | bytes 8192000 | tf_op jit(solution)/shard_map/update/pallas_call | solution.py:240
  (2 shorter events, 0.1 us)
Async XLA Ops:
  5.8 2.5 %collective-permute-start = (bf16[128,3072]{1,0:T(8,128)(2,1)}, bf16[128,3072]{1,0:T(8,128)(2,1)S(1)}, u32[]{:S(2)}, u32[]{:S(2)}) collective-permute-start(bf16[128,3072]{1,0:T(8,128)(2,1)} %get-tuple-element.12), channel_id=1, source_target_pairs={{0,1},{1,0},{2,3},{3,2},{4,5},{5,4},{6,7},{7,6},{8,9},{9,8},{10,11... | collective-permute-start | bytes 2359304 | tf_op jit(solution)/shard_map/ppermute | solution.py:276
  8.3 52.3 %copy-start.4 = (s32[320]{0:T(512)S(1)}, s32[320]{0:T(512)}, u32[]{:S(2)}) copy-start(s32[320]{0:T(512)} %param.11) | copy-start | bytes 3844
  58.8 7.8 %copy-start = (bf16[8,16,3072]{2,1,0:T(8,128)(2,1)}, bf16[8,16,3072]{2,1,0:T(8,128)(2,1)S(1)}, u32[]{:S(2)}) copy-start(bf16[8,16,3072]{2,1,0:T(8,128)(2,1)S(1)} %all_to_all.35) | copy-start | bytes 2359300
  58.8 7.8 %collective-permute-start.1 = (bf16[128,3072]{1,0:T(8,128)(2,1)S(1)}, bf16[128,3072]{1,0:T(8,128)(2,1)S(1)}, u32[]{:S(2)}, u32[]{:S(2)}) collective-permute-start(bf16[128,3072]{1,0:T(8,128)(2,1)S(1)} %bitcast.13), channel_id=1, source_target_pairs={{0,1},{1,0},{2,3},{3,2},{4,5},{5,4},{6,7},{7,6},{8,9},{9,8},{10,11... | collective-permute-start | bytes 2359304 | tf_op jit(solution)/shard_map/ppermute | solution.py:276
  66.6 0.9 copy-start.2
  78.4 2.3 %collective-permute-start.2 = (f32[1216,128]{1,0:T(8,128)}, f32[1216,128]{1,0:T(8,128)S(1)}, u32[]{:S(2)}, u32[]{:S(2)}) collective-permute-start(f32[1216,128]{1,0:T(8,128)} %get-tuple-element.16), channel_id=1, source_target_pairs={{0,1},{1,0},{2,3},{3,2},{4,5},{5,4},{6,7},{7,6},{8,9},{9,8},{10,11... | collective-permute-start | bytes 1867784 | tf_op jit(solution)/shard_map/ppermute | solution.py:276
  120.9 3.7 %copy-start.1 = (f32[8,152,128]{2,1,0:T(8,128)}, f32[8,152,128]{2,1,0:T(8,128)S(1)}, u32[]{:S(2)}) copy-start(f32[8,152,128]{2,1,0:T(8,128)S(1)} %all_to_all.37) | copy-start | bytes 1867780
  120.9 3.7 %collective-permute-start.3 = (f32[1216,128]{1,0:T(8,128)S(1)}, f32[1216,128]{1,0:T(8,128)S(1)}, u32[]{:S(2)}, u32[]{:S(2)}) collective-permute-start(f32[1216,128]{1,0:T(8,128)S(1)} %bitcast.17), channel_id=1, source_target_pairs={{0,1},{1,0},{2,3},{3,2},{4,5},{5,4},{6,7},{7,6},{8,9},{9,8},{10,11... | collective-permute-start | bytes 1867784 | tf_op jit(solution)/shard_map/ppermute | solution.py:276
  124.6 0.8 copy-start.3

commit v3 on v2

--- a/solution.py
+++ b/solution.py
@@ -284,7 +284,7 @@
     rows, width = keep.shape
     parts = shuffle(keep + swap(send)).reshape(chips, rows // chips, width)
     part = jnp.sum(parts.astype(F32), axis=0).astype(keep.dtype)
-    whole = shuffle(jnp.broadcast_to(part, parts.shape).reshape(rows, width))
+    whole = lax.all_gather(part, "center", tiled=True)
     return whole, swap(whole)
 
 

time: 134 us -> 155 us (1.16)
  starting transfers between devices: 3.97 us -> 15.6 us
  blocking collectives: 88 us -> 97.2 us
    all_gather x0 -> x2, blocking collectives: none -> 52.2 us  [total_of(): whole = lax.all_gather(part, 'center', tiled=True)]
    all_to_all x4 -> x2, blocking collectives: 88 us -> 45 us  [shuffle(): return lax.all_to_all(x, 'center', 0, 0, tiled=True)]
    ppermute x4, starting transfers between devices: 3.97 us -> 15.6 us  [swap(): return lax.ppermute(x, 'sub', [(0, 1), (1, 0)])]
  transfers between devices with their start and end apart: 4 -> 4, of which waited for: 3 -> 3; matrix products, arithmetic and copies ran while one was open for 0% -> 0% of each run, Pallas kernels for 4% -> 3%
where the time goes in v3:
time: 155 us; the launch traced here: 154 us
  blocking collectives  97.2 us (63%)
  Pallas kernels  29.4 us (19%)
  starting transfers between devices  15.6 us (10%)
  waiting for transfers between devices  6.34 us (4%)
  other arithmetic  2.6 us (2%)
  local copies, waits for them, and re-layouts  2.26 us (1%)
    all_gather x2, blocking collectives, total_of(): whole = lax.all_gather(part, 'center', tiled=True)  52.2 us
    all_to_all x2, blocking collectives, shuffle(): return lax.all_to_all(x, 'center', 0, 0, tiled=True)  45 us
    ppermute x4, starting transfers between devices, swap(): return lax.ppermute(x, 'sub', [(0, 1), (1, 0)])  15.6 us
    pallas_call x1, Pallas kernels, predict(): pl.pallas_call(predict_body, grid=(count // block,), in_specs=[pl.BlockSp...  10.9 us
    pallas_call x1, Pallas kernels, update(): pl.pallas_call(functools.partial(update_body, classes), grid=(classes //...  7.95 us
    ppermute x4, waiting for transfers between devices, swap(): return lax.ppermute(x, 'sub', [(0, 1), (1, 0)])  6.34 us
    pallas_call x1, Pallas kernels, prepare(): pl.pallas_call(functools.partial(prepare_body, classes), out_shape=[jax.S...  5.39 us
    pallas_call x1, Pallas kernels, pick_batch(): pl.pallas_call(pick_body, grid=(depth // block,), in_specs=[pl.BlockSpec(...  5.22 us
  transfers between devices with their start and end apart: 4, of which 3 were waited for; matrix products, arithmetic and copies ran while one was open for 0% of the time, Pallas kernels for 3%

profile of v3, /device:TPU:1, one launch (start us, length us, event | category | flops | bytes accessed | tf_op | source)
XLA Modules:
  0.0 154.1 jit_solution(6473002441030623523)
XLA Ops:
  0.6 5.2 %pick_batch.1 = (bf16[128,3072]{1,0:T(8,128)(2,1)}, bf16[128,3072]{1,0:T(8,128)(2,1)}) custom-call(s32[1,256]{1,0:T(1,128)} %bitcast.15, bf16[768,3072]{1,0:T(8,128)(2,1)} %centers_ref.3), custom_call_target="tpu_custom_call" | custom-call | flops 1207959552 | bytes 6291456 | tf_op jit(solution)/shard_map/pick_batch/pallas_call | solution.py:70
  5.8 0.0 copy-start.4
  5.9 0.1 collective-permute-start
  5.9 2.4 %collective-permute-done = bf16[128,3072]{1,0:T(8,128)(2,1)S(1)} collective-permute-done((bf16[128,3072]{1,0:T(8,128)(2,1)}, bf16[128,3072]{1,0:T(8,128)(2,1)S(1)}, u32[]{:S(2)}, u32[]{:S(2)}) %collective-permute-start) | collective-permute-done | bytes 786464 | tf_op jit(solution)/shard_map/ppermute | solution.py:276
  8.3 1.3 add.6
  9.7 25.7 %all_to_all.18 = bf16[8,16,3072]{2,1,0:T(8,128)(2,1)S(1)} all-to-all(bf16[8,16,3072]{2,1,0:T(8,128)(2,1)S(1)} %bitcast.11), channel_id=1, replica_groups=mesh['parts'=2,'center'=8,'sub'=2] {'center'}, dimensions={0} | all-to-all | bytes 1572864 | tf_op jit(solution)/shard_map/all_to_all | solution.py:280
  35.4 0.1 reduce_sum.21
  35.5 26.5 %all_gather.6.mine_ref = bf16[128,3072]{1,0:T(8,128)(2,1)S(1)} all-gather(bf16[16,3072]{1,0:T(8,128)(2,1)S(1)} %reduce_sum.21), channel_id=1, replica_groups=mesh['parts'=2,'center'=8,'sub'=2] {'center'}, dimensions={0}, use_global_device_ids=true | all-gather | bytes 884736 | tf_op jit(solution)/shard_map/all_gather | solution.py:287
  62.0 0.0 copy-start
  62.0 7.4 %collective-permute-start.1 = (bf16[128,3072]{1,0:T(8,128)(2,1)S(1)}, bf16[128,3072]{1,0:T(8,128)(2,1)S(1)}, u32[]{:S(2)}, u32[]{:S(2)}) collective-permute-start(bf16[128,3072]{1,0:T(8,128)(2,1)S(1)} %all_gather.6.mine_ref), channel_id=1, source_target_pairs={{0,1},{1,0},{2,3},{3,2},{4,5},{5,4},{6,7},{7,6},{8,9},{9,8},{10,11... | collective-permute-start | bytes 2359304 | tf_op jit(solution)/shard_map/ppermute | solution.py:276
  69.4 0.0 copy-done.4
  69.4 0.5 reshape.22.index_ref
  69.9 5.4 %prepare.1 = (bf16[1216,768]{1,0:T(8,128)(2,1)}, bf16[1216,768]{1,0:T(8,128)(2,1)}, f32[160,768]{1,0:T(8,128)}) custom-call(s32[1,320]{1,0:T(1,128)} %reshape.22.index_ref, f32[160,320]{1,0:T(8,128)} %bitcast.14, f32[1000,768]{1,0:T(8,128)} %bitcast.9), custom_call_target="tpu_custom_call" | custom-call | flops 235929600 | bytes 7471104 | tf_op jit(solution)/shard_map/prepare/pallas_call | solution.py:111
  75.3 0.0 collective-permute-done.1.other_ref
  75.3 0.0 copy-start.2
  75.3 0.0 copy-done
  75.3 0.9 copy-done.2
  76.2 10.9 %predict.1 = (f32[1216,128]{1,0:T(8,128)}, f32[1216,128]{1,0:T(8,128)}) custom-call(bf16[128,3072]{1,0:T(8,128)(2,1)} %copy-done, bf16[128,3072]{1,0:T(8,128)(2,1)} %copy-done.2, bf16[768,3072]{1,0:T(8,128)(2,1)} %centers_ref.3, bf16[1216,768]{1,0:T(8,128)(2,1)} %get-tuple-element.13.high_ref, bf16[1216,768]{1,0:T(8,128)(2,1)} %get-tuple-element.14.low_ref), custom_call_target="tpu_custom_call" | custom-call | flops 2642411520 | bytes 11272192 | tf_op jit(solution)/shard_map/predict/pallas_call | solution.py:168
  87.1 0.0 collective-permute-start.2
  87.1 2.2 %collective-permute-done.2 = f32[1216,128]{1,0:T(8,128)S(1)} collective-permute-done((f32[1216,128]{1,0:T(8,128)}, f32[1216,128]{1,0:T(8,128)S(1)}, u32[]{:S(2)}, u32[]{:S(2)}) %collective-permute-start.2) | collective-permute-done | bytes 622624 | tf_op jit(solution)/shard_map/ppermute | solution.py:276
  89.4 1.1 add.7
  90.5 19.3 %all_to_all.19 = f32[8,152,128]{2,1,0:T(8,128)S(1)} all-to-all(f32[8,152,128]{2,1,0:T(8,128)S(1)} %bitcast.12), channel_id=1, replica_groups=mesh['parts'=2,'center'=8,'sub'=2] {'center'}, dimensions={0} | all-to-all | bytes 1245184 | tf_op jit(solution)/shard_map/all_to_all | solution.py:280
  109.9 25.7 %all_gather.7.mine_ref = f32[1216,128]{1,0:T(8,128)S(1)} all-gather(f32[152,128]{1,0:T(8,128)S(1)} %reduce_sum.22), channel_id=1, replica_groups=mesh['parts'=2,'center'=8,'sub'=2] {'center'}, dimensions={0}, use_global_device_ids=true | all-gather | bytes 700416 | tf_op jit(solution)/shard_map/all_gather | solution.py:287
  135.6 0.0 copy-start.1
  135.6 8.1 %collective-permute-start.3 = (f32[1216,128]{1,0:T(8,128)S(1)}, f32[1216,128]{1,0:T(8,128)S(1)}, u32[]{:S(2)}, u32[]{:S(2)}) collective-permute-start(f32[1216,128]{1,0:T(8,128)S(1)} %all_gather.7.mine_ref), channel_id=1, source_target_pairs={{0,1},{1,0},{2,3},{3,2},{4,5},{5,4},{6,7},{7,6},{8,9},{9,8},{10,11... | collective-permute-start | bytes 1867784 | tf_op jit(solution)/shard_map/ppermute | solution.py:276
  143.7 1.7 %collective-permute-done.3.other_ref = f32[1216,128]{1,0:T(8,128)S(1)} collective-permute-done((f32[1216,128]{1,0:T(8,128)S(1)}, f32[1216,128]{1,0:T(8,128)S(1)}, u32[]{:S(2)}, u32[]{:S(2)}) %collective-permute-start.3) | collective-permute-done | bytes 622624 | tf_op jit(solution)/shard_map/ppermute | solution.py:276
  145.3 0.0 copy-start.3
  145.3 0.0 copy-done.1
  145.3 0.8 copy-done.3
  146.2 8.0 %update.1 = (f32[1000,768]{1,0:T(8,128)}, f32[1000,256]{1,0:T(8,128)}) custom-call(f32[1216,128]{1,0:T(8,128)} %copy-done.1, f32[1216,128]{1,0:T(8,128)} %copy-done.3, f32[1000,256]{1,0:T(8,128)} %bitcast.13, s32[1,256]{1,0:T(1,128)} %bitcast.16, f32[1,160]{1,0:T(1,128)} %bitcast.17, f32[160,768]{1,0:T(8,128)} %get-tuple-element.17.spread_ref, ...), custom_call_target="tpu_custom_call" | custom-call | flops 1368391680 | bytes 8192000 | tf_op jit(solution)/shard_map/update/pallas_call | solution.py:240
  (1 shorter events, 0.0 us)
Async XLA Ops:
  5.8 63.5 %copy-start.4 = (s32[320]{0:T(512)S(1)}, s32[320]{0:T(512)}, u32[]{:S(2)}) copy-start(s32[320]{0:T(512)} %param.11) | copy-start | bytes 3844
  5.9 2.5 %collective-permute-start = (bf16[128,3072]{1,0:T(8,128)(2,1)}, bf16[128,3072]{1,0:T(8,128)(2,1)S(1)}, u32[]{:S(2)}, u32[]{:S(2)}) collective-permute-start(bf16[128,3072]{1,0:T(8,128)(2,1)} %get-tuple-element.12), channel_id=1, source_target_pairs={{0,1},{1,0},{2,3},{3,2},{4,5},{5,4},{6,7},{7,6},{8,9},{9,8},{10,11... | collective-permute-start | bytes 2359304 | tf_op jit(solution)/shard_map/ppermute | solution.py:276
  62.0 13.3 %copy-start = (bf16[128,3072]{1,0:T(8,128)(2,1)}, bf16[128,3072]{1,0:T(8,128)(2,1)S(1)}, u32[]{:S(2)}) copy-start(bf16[128,3072]{1,0:T(8,128)(2,1)S(1)} %all_gather.6.mine_ref) | copy-start | bytes 2359300
  62.0 13.3 %collective-permute-start.1 = (bf16[128,3072]{1,0:T(8,128)(2,1)S(1)}, bf16[128,3072]{1,0:T(8,128)(2,1)S(1)}, u32[]{:S(2)}, u32[]{:S(2)}) collective-permute-start(bf16[128,3072]{1,0:T(8,128)(2,1)S(1)} %all_gather.6.mine_ref), channel_id=1, source_target_pairs={{0,1},{1,0},{2,3},{3,2},{4,5},{5,4},{6,7},{7,6},{8,9},{9,8},{10,11... | collective-permute-start | bytes 2359304 | tf_op jit(solution)/shard_map/ppermute | solution.py:276
  75.3 0.9 copy-start.2
  87.1 2.3 %collective-permute-start.2 = (f32[1216,128]{1,0:T(8,128)}, f32[1216,128]{1,0:T(8,128)S(1)}, u32[]{:S(2)}, u32[]{:S(2)}) collective-permute-start(f32[1216,128]{1,0:T(8,128)} %get-tuple-element.16), channel_id=1, source_target_pairs={{0,1},{1,0},{2,3},{3,2},{4,5},{5,4},{6,7},{7,6},{8,9},{9,8},{10,11... | collective-permute-start | bytes 1867784 | tf_op jit(solution)/shard_map/ppermute | solution.py:276
  135.6 9.8 %copy-start.1 = (f32[1216,128]{1,0:T(8,128)}, f32[1216,128]{1,0:T(8,128)S(1)}, u32[]{:S(2)}) copy-start(f32[1216,128]{1,0:T(8,128)S(1)} %all_gather.7.mine_ref) | copy-start | bytes 1867780
  135.6 9.8 %collective-permute-start.3 = (f32[1216,128]{1,0:T(8,128)S(1)}, f32[1216,128]{1,0:T(8,128)S(1)}, u32[]{:S(2)}, u32[]{:S(2)}) collective-permute-start(f32[1216,128]{1,0:T(8,128)S(1)} %all_gather.7.mine_ref), channel_id=1, source_target_pairs={{0,1},{1,0},{2,3},{3,2},{4,5},{5,4},{6,7},{7,6},{8,9},{9,8},{10,11... | collective-permute-start | bytes 1867784 | tf_op jit(solution)/shard_map/ppermute | solution.py:276
  145.3 0.8 copy-start.3

commit v4 on v1

v4 whole, which is shorter than its diff:
```python
import functools
import math

import jax
import jax.numpy as jnp
from jax import lax
from jax.experimental import pallas as pl
from jax.experimental.pallas import tpu as pltpu
from jax.sharding import PartitionSpec as P

F32 = jnp.float32
BF16 = jnp.bfloat16
AXES = ("center", "sub")
LEVELS = 4
CHUNKS = 1 << LEVELS
LANE = 128
PARTS = 2
NT = (((1,), (1,)), ((), ()))
NN = (((1,), (0,)), ((), ()))
VMEM_LIMIT = 24 * 1024 * 1024


def dot(a, b, dims):
    return lax.dot_general(a, b, dims, preferred_element_type=F32)


def position():
    return lax.axis_index("center") * 2 + lax.axis_index("sub")


def reversed_bits(value, bits):
    out = 0
    for bit in range(bits):
        out = out + ((value >> bit) & 1) * (1 << (bits - 1 - bit))
    return out


def column_of(row, width):
    return jnp.broadcast_to(row.astype(F32), (width, row.shape[1])).T


def two(x):
    high = x.astype(BF16)
    return high, (x - high.astype(F32)).astype(BF16)


def pick_rows(index_ref, columns, start, dtype, scale):
    column = column_of(index_ref[...] - start, LANE)
    lanes = lax.broadcasted_iota(jnp.int32, (1, LANE), 1).astype(F32)
    blocks = [
        jnp.where(column == lanes + float(LANE * k), scale, 0.0).astype(dtype)
        for k in range(columns // LANE)
    ]
    return jnp.concatenate(blocks, axis=1)


def params():
    return pltpu.CompilerParams(vmem_limit_bytes=VMEM_LIMIT)


def pick_body(index_ref, centers_ref, keep_ref, send_ref, pick_ref):
    me = position()
    turn = reversed_bits(me, LEVELS)
    rows = index_ref.shape[1]
    size = rows // CHUNKS
    count = centers_ref.shape[0]

    @pl.when(pl.program_id(0) == 0)
    def _():
        pick = pick_rows(index_ref, count, me * count, BF16, 1.0)
        for chunk in range(CHUNKS):
            to = pl.multiple_of((chunk ^ turn) * size, size)
            pick_ref[pl.ds(to, size), :] = pick[chunk * size : (chunk + 1) * size]

    found = dot(pick_ref[...], centers_ref[...], NN).astype(BF16)
    keep_ref[...] = found[: rows // 2]
    send_ref[...] = found[rows // 2 :]


def pick_batch(batch_index, centers, part):
    rows = batch_index.shape[1]
    count, depth = centers.shape
    block = depth // PARTS // 2
    half = jax.ShapeDtypeStruct((rows // 2, depth // PARTS), BF16)
    return pl.pallas_call(
        pick_body,
        grid=(2,),
        in_specs=[
            pl.BlockSpec((1, rows), lambda i: (0, 0)),
            pl.BlockSpec((count, block), lambda i: (0, 2 * part + i)),
        ],
        out_specs=[pl.BlockSpec((rows // 2, block), lambda i: (0, i))] * 2,
        out_shape=[half, half],
        scratch_shapes=[pltpu.VMEM((rows, count), BF16)],
        compiler_params=params(),
        cost_estimate=pl.CostEstimate(
            flops=2 * rows * count * depth // PARTS,
            bytes_accessed=2 * depth * (count + rows) // PARTS,
            transcendentals=0,
        ),
        name="pick_batch",
    )(batch_index, centers)


def spread_body(
    first, classes, index_ref, eigvec_ref, weights_ref,
    high1_ref, low1_ref, high2_ref, low2_ref, spread_ref, all_ref,
):
    me = position()
    turn = reversed_bits(me >> 1, LEVELS - 1)
    rank, points = eigvec_ref.shape
    count = weights_ref.shape[1]
    local = index_ref[...] - me * count
    slots = lax.broadcasted_iota(jnp.int32, (count, points), 0)
    pick = jnp.where(slots == local, 1.0, 0.0).astype(BF16)
    vec = eigvec_ref[...]
    high = vec.astype(BF16)
    rest = vec - high.astype(F32)
    mid = rest.astype(BF16)
    low = (rest - mid.astype(F32)).astype(BF16)
    spread = dot(high, pick, NT) + dot(mid, pick, NT) + dot(low, pick, NT)
    spread_ref[...] = spread
    all_ref[:rank] = spread
    all_ref[rank : rank + classes] = weights_ref[...]
    all_ref[rank + classes :] = jnp.zeros((all_ref.shape[0] - rank - classes, count), F32)
    for begin, high_ref, low_ref in ((0, high1_ref, low1_ref), (first, high2_ref, low2_ref)):
        size = high_ref.shape[0] // (CHUNKS // 2)
        for chunk in range(CHUNKS // 2):
            at = pl.multiple_of(begin + (chunk ^ turn) * size, 8)
            high, low = two(all_ref[pl.ds(at, size), :])
            high_ref[chunk * size : (chunk + 1) * size] = high
            low_ref[chunk * size : (chunk + 1) * size] = low


def spread_weights(nys_index, eigvec, weights, first, second):
    classes, count = weights.shape
    rank, points = eigvec.shape
    return pl.pallas_call(
        functools.partial(spread_body, first, classes),
        out_shape=[
            jax.ShapeDtypeStruct((first, count), BF16),
            jax.ShapeDtypeStruct((first, count), BF16),
            jax.ShapeDtypeStruct((second, count), BF16),
            jax.ShapeDtypeStruct((second, count), BF16),
            jax.ShapeDtypeStruct((rank, count), F32),
        ],
        scratch_shapes=[pltpu.VMEM((first + second, count), F32)],
        compiler_params=params(),
        cost_estimate=pl.CostEstimate(
            flops=6 * rank * points * count, bytes_accessed=8 * (first + second) * count, transcendentals=0
        ),
        name="spread_weights",
    )(nys_index, eigvec, weights)


def norms_body(centers_ref, norm_ref):
    wide = centers_ref[...].astype(F32)
    norm = jnp.sum(wide * wide, axis=1, keepdims=True)
    norm_ref[...] = jnp.broadcast_to(norm, norm_ref.shape)


def center_norms(centers):
    count, depth = centers.shape
    block = 256
    return pl.pallas_call(
        norms_body,
        grid=(count // block,),
        in_specs=[pl.BlockSpec((block, depth), lambda i: (i, 0))],
        out_specs=pl.BlockSpec((block, LANE), lambda i: (i, 0)),
        out_shape=jax.ShapeDtypeStruct((count, LANE), F32),
        compiler_params=params(),
        cost_estimate=pl.CostEstimate(flops=2 * count * depth, bytes_accessed=2 * count * depth, transcendentals=0),
        name="center_norms",
    )(centers)


def distance_step(mine_ref, other_ref, centers_ref, before, total_ref, batch_ref):
    step = pl.program_id(0)
    blocks, rows, block = batch_ref.shape
    size = rows // CHUNKS

    @pl.when(step == 0)
    def _():
        turn = reversed_bits(position(), LEVELS)
        for chunk in range(CHUNKS):
            ref = mine_ref if chunk < CHUNKS // 2 else other_ref
            at = chunk % (CHUNKS // 2) * size
            to = pl.multiple_of((chunk ^ turn) * size, size)
            for k in range(blocks):
                batch_ref[k, pl.ds(to, size), :] = ref[at : at + size, k * block : (k + 1) * block]
        norm = jnp.zeros((rows, 1), F32)
        for k in range(blocks):
            batch = batch_ref[k].astype(F32)
            norm = norm + jnp.sum(batch * batch, axis=1, keepdims=True)
        total_ref[...] = before() + jnp.broadcast_to(norm, (rows, LANE)).T[0:1]

    total_ref[...] -= 2.0 * dot(centers_ref[...], batch_ref[step], NT)


def product(me, high_ref, low_ref, value_high, value_low, keep_ref, send_ref):
    half = keep_ref.shape[1]
    high = high_ref[...]
    total = dot(high, value_high, NN) + (dot(high, value_low, NN) + dot(low_ref[...], value_high, NN))
    lower = (me & 1) == 0
    keep_ref[...] = jnp.where(lower, total[:, :half], total[:, half:])
    send_ref[...] = jnp.where(lower, total[:, half:], total[:, :half])


def distance_body(mine_ref, other_ref, centers_ref, norm_ref, total_ref, batch_ref):
    distance_step(mine_ref, other_ref, centers_ref, lambda: norm_ref[:, 0:1], total_ref, batch_ref)


def predict_body(
    depth, mine_ref, other_ref, centers_ref, before_ref, high_hbm, low_hbm,
    keep_ref, send_ref, value_high_ref, value_low_ref, total_ref, batch_ref, high_ref, low_ref, sems,
):
    copies = [
        pltpu.make_async_copy(high_hbm, high_ref, sems.at[0]),
        pltpu.make_async_copy(low_hbm, low_ref, sems.at[1]),
    ]

    @pl.when(pl.program_id(0) == 0)
    def _():
        for copy in copies:
            copy.start()

    distance_step(mine_ref, other_ref, centers_ref, lambda: before_ref[...], total_ref, batch_ref)

    @pl.when(pl.program_id(0) == pl.num_programs(0) - 1)
    def _():
        square = jnp.maximum(total_ref[...], 0.0)
        value_high, value_low = two(jnp.exp(jnp.sqrt(square) * (-1.0 / math.sqrt(depth))))
        value_high_ref[...] = value_high
        value_low_ref[...] = value_low
        for copy in copies:
            copy.wait()
        product(position(), high_ref, low_ref, value_high, value_low, keep_ref, send_ref)


def exchange_specs(half, depth, count, block, part):
    blocks = depth // block
    return [
        pl.BlockSpec((half, depth), lambda i: (0, 0)),
        pl.BlockSpec((half, depth), lambda i: (0, 0)),
        pl.BlockSpec((count, block), lambda i: (0, part * blocks + i)),
    ]


def distances(mine, other, centers, norms):
    half, depth = mine.shape
    rows = 2 * half
    count = centers.shape[0]
    block = 512
    return pl.pallas_call(
        distance_body,
        grid=(depth // block,),
        in_specs=exchange_specs(half, depth, count, block, 0) + [pl.BlockSpec((count, LANE), lambda i: (0, 0))],
        out_specs=pl.BlockSpec((count, rows), lambda i: (0, 0)),
        out_shape=jax.ShapeDtypeStruct((count, rows), F32),
        scratch_shapes=[pltpu.VMEM((depth // block, rows, block), BF16)],
        compiler_params=params(),
        cost_estimate=pl.CostEstimate(
            flops=2 * rows * count * depth, bytes_accessed=2 * depth * (count + rows), transcendentals=0
        ),
        name="distances",
    )(mine, other, centers, norms)


def predict(mine, other, centers, before, high, low):
    half, depth = mine.shape
    rows = 2 * half
    count = centers.shape[0]
    padded = high.shape[0]
    block = 512
    fixed = lambda shape: pl.BlockSpec(shape, lambda i: (0, 0))
    out = jax.ShapeDtypeStruct((padded, half), F32)
    value = jax.ShapeDtypeStruct((count, rows), BF16)
    return pl.pallas_call(
        functools.partial(predict_body, centers.shape[1]),
        grid=(depth // block,),
        in_specs=exchange_specs(half, depth, count, block, 1)
        + [fixed((count, rows)), pl.BlockSpec(memory_space=pl.ANY), pl.BlockSpec(memory_space=pl.ANY)],
        out_specs=[fixed((padded, half))] * 2 + [fixed((count, rows))] * 2,
        out_shape=[out, out, value, value],
        scratch_shapes=[
            pltpu.VMEM((count, rows), F32),
            pltpu.VMEM((depth // block, rows, block), BF16),
            pltpu.VMEM((padded, count), BF16),
            pltpu.VMEM((padded, count), BF16),
            pltpu.SemaphoreType.DMA((2,)),
        ],
        compiler_params=params(),
        cost_estimate=pl.CostEstimate(
            flops=2 * rows * count * (depth + 3 * padded),
            bytes_accessed=2 * depth * (count + rows) + 4 * padded * (count + rows),
            transcendentals=2 * rows * count,
        ),
        name="predict",
    )(mine, other, centers, before, high, low)


def more_body(high_ref, low_ref, value_high_ref, value_low_ref, keep_ref, send_ref):
    product(position(), high_ref, low_ref, value_high_ref[...], value_low_ref[...], keep_ref, send_ref)


def predict_more(high, low, value_high, value_low):
    padded = high.shape[0]
    count, rows = value_high.shape
    out = jax.ShapeDtypeStruct((padded, rows // 2), F32)
    return pl.pallas_call(
        more_body,
        out_shape=[out, out],
        compiler_params=params(),
        cost_estimate=pl.CostEstimate(
            flops=6 * rows * count * padded, bytes_accessed=4 * padded * (count + rows), transcendentals=0
        ),
        name="predict_more",
    )(high, low, value_high, value_low)


def gather_total(mine_ref, other_ref, total_ref):
    me = position()
    turn = reversed_bits(me >> 1, LEVELS - 1)
    half = mine_ref.shape[1]
    size = mine_ref.shape[0] // (CHUNKS // 2)
    lower = (me & 1) == 0
    for chunk in range(CHUNKS // 2):
        to = pl.multiple_of((chunk ^ turn) * size, 8)
        mine = mine_ref[chunk * size : (chunk + 1) * size]
        other = other_ref[chunk * size : (chunk + 1) * size]
        total_ref[pl.ds(to, size), :half] = jnp.where(lower, mine, other)
        total_ref[pl.ds(to, size), half:] = jnp.where(lower, other, mine)


def write_rows(begin, skip, total_ref, targets_ref, weights_ref, high_ref, low_ref, new_hbm, out_hbm, new_ref, sems):
    rows = new_ref.shape[0]
    blocks = sems.shape[0] - 1
    size = rows // blocks
    high_right = high_ref[...]
    low_right = low_ref[...]
    copies = [
        pltpu.make_async_copy(
            total_ref.at[pl.ds(skip, rows)], out_hbm.at[pl.ds(begin, rows)], sems.at[blocks]
        )
    ]
    copies[0].start()
    for k in range(blocks):
        at = slice(k * size, (k + 1) * size)
        from_ = slice(begin + k * size, begin + (k + 1) * size)
        high, low = two(total_ref[skip + k * size : skip + (k + 1) * size] - targets_ref[from_])
        new_ref[at] = weights_ref[from_] + (
            dot(high, high_right, NN) + (dot(high, low_right, NN) + dot(low, high_right, NN))
        )
        copy = pltpu.make_async_copy(
            new_ref.at[pl.ds(k * size, size)], new_hbm.at[pl.ds(begin + k * size, size)], sems.at[k]
        )
        copy.start()
        copies.append(copy)
    for copy in copies:
        copy.wait()


def update_body(
    mine_ref, other_ref, targets_ref, index_ref, eigval_ref, spread_ref, weights_ref,
    new_hbm, out_hbm, high_ref, low_ref, total_ref, new_ref, sems,
):
    me = position()
    rank, count = spread_ref.shape
    gather_total(mine_ref, other_ref, total_ref)
    value = eigval_ref[...]
    lowest = jnp.min(value, axis=1, keepdims=True)
    scaled = (1.0 - lowest / value) / value
    mixed_high, mixed_low = two(total_ref[:rank].T * (0.25 * scaled))
    spread_high, spread_low = two(spread_ref[...])
    turned = dot(mixed_high, spread_high, NN) + (
        dot(mixed_high, spread_low, NN) + dot(mixed_low, spread_high, NN)
    )
    high_ref[...], low_ref[...] = two(turned - pick_rows(index_ref, count, me * count, F32, 0.25))
    write_rows(0, rank, total_ref, targets_ref, weights_ref, high_ref, low_ref, new_hbm, out_hbm, new_ref, sems)


def update(mine, other, targets, batch_index, eigval, spread, weights):
    classes, count = weights.shape
    padded, half = mine.shape
    rows = 2 * half
    rank = spread.shape[0]
    here = padded - rank
    vmem = pl.BlockSpec(memory_space=pltpu.VMEM)
    hbm = pl.BlockSpec(memory_space=pl.ANY)
    right = jax.ShapeDtypeStruct((rows, count), BF16)
    return pl.pallas_call(
        update_body,
        in_specs=[vmem] * 7,
        out_specs=[hbm, hbm, vmem, vmem],
        out_shape=[
            jax.ShapeDtypeStruct((classes, count), F32),
            jax.ShapeDtypeStruct((classes, rows), F32),
            right,
            right,
        ],
        scratch_shapes=[
            pltpu.VMEM((padded, rows), F32),
            pltpu.VMEM((here, count), F32),
            pltpu.SemaphoreType.DMA((4,)),
        ],
        compiler_params=params(),
        cost_estimate=pl.CostEstimate(
            flops=6 * rows * count * (here + rank), bytes_accessed=8 * here * (count + rows), transcendentals=0
        ),
        name="update",
    )(mine, other, targets, batch_index, eigval, spread, weights)


def update_more_body(
    begin, mine_ref, other_ref, targets_ref, weights_ref, high_ref, low_ref, new_in, out_in,
    new_hbm, out_hbm, total_ref, new_ref, sems,
):
    gather_total(mine_ref, other_ref, total_ref)
    write_rows(begin, 0, total_ref, targets_ref, weights_ref, high_ref, low_ref, new_hbm, out_hbm, new_ref, sems)


def update_more(mine, other, targets, weights, high, low, new, out, begin):
    classes, count = weights.shape
    padded, half = mine.shape
    rows = 2 * half
    here = classes - begin
    vmem = pl.BlockSpec(memory_space=pltpu.VMEM)
    hbm = pl.BlockSpec(memory_space=pl.ANY)
    return pl.pallas_call(
        functools.partial(update_more_body, begin),
        in_specs=[vmem] * 6 + [hbm] * 2,
        out_specs=[hbm, hbm],
        out_shape=[
            jax.ShapeDtypeStruct((classes, count), F32),
            jax.ShapeDtypeStruct((classes, rows), F32),
        ],
        input_output_aliases={6: 0, 7: 1},
        scratch_shapes=[
            pltpu.VMEM((padded, rows), F32),
            pltpu.VMEM((here, count), F32),
            pltpu.SemaphoreType.DMA((6,)),
        ],
        compiler_params=params(),
        cost_estimate=pl.CostEstimate(
            flops=6 * rows * count * here, bytes_accessed=8 * here * (count + rows), transcendentals=0
        ),
        name="update_more",
    )(mine, other, targets, weights, high, low, new, out)


def swap(x, mask, devices):
    return lax.ppermute(x, AXES, [(i, i ^ mask) for i in range(devices)])


def total_of(keep, send, devices):
    for level in range(LEVELS):
        keep = keep + swap(send, 1 << level, devices)
        if level < LEVELS - 1:
            half = keep.shape[0] // 2
            keep, send = keep[:half], keep[half:]
    for level in range(LEVELS, int(math.log2(devices))):
        keep = keep + swap(keep, 1 << level, devices)
    for level in reversed(range(1, LEVELS)):
        keep = jnp.concatenate([keep, swap(keep, 1 << level, devices)])
    return keep, swap(keep, 1, devices)


def on_device(devices, centers, weights, targets, batch_index, nys_index, eigvec, eigval):
    rows = batch_index.shape[0]
    classes = weights.shape[1]
    rank = eigvec.shape[1]
    unit = 8 * CHUNKS // 2
    units = -(-(classes + rank) // unit)
    first = (units + 1) // 2 * unit
    second = units * unit - first
    begin = first - rank
    batch_index = batch_index.reshape(1, rows)
    weights = weights.T
    targets = targets.T
    halves = [total_of(*pick_batch(batch_index, centers, part), devices) for part in range(PARTS)]
    high1, low1, high2, low2, spread = spread_weights(nys_index.reshape(1, -1), eigvec.T, weights, first, second)
    before = distances(*halves[0], centers, center_norms(centers))
    keep, send, value_high, value_low = predict(*halves[1], centers, before, high1, low1)
    one = total_of(keep, send, devices)
    another = total_of(*predict_more(high2, low2, value_high, value_low), devices)
    new, out, high, low = update(*one, targets, batch_index, eigval.reshape(1, rank), spread, weights)
    new, out = update_more(*another, targets, weights, high, low, new, out, begin)
    return new.T, out.T


def solution(mesh):
    devices = mesh.shape["center"] * mesh.shape["sub"]
    return jax.shard_map(
        functools.partial(on_device, devices),
        mesh=mesh,
        in_specs=(
            P(("parts", "center", "sub"), None),
            P(("parts", "center", "sub"), None),
            P("parts", None),
            P("parts"),
            P(("parts", "center", "sub")),
            P(("parts", "center", "sub"), None),
            P("parts"),
        ),
        out_specs=(P(("parts", "center", "sub"), None), P("parts", None)),
        check_vma=False,
    )
```

time: 127 us -> 97.1 us (0.76)
  waiting for transfers between devices: 62.2 us -> 22.4 us
  starting transfers between devices: 28.8 us -> 52.5 us
  Pallas kernels: 29.1 us -> 17 us
  other arithmetic: 2.79 us -> 0.58 us
    ppermute x16 -> x32, waiting for transfers between devices: 62.2 us -> 22.4 us  [swap(): return lax.ppermute(x, AXES, [(i, i ^ mask) for i in range(devices)])]
    ppermute x16 -> x32, starting transfers between devices: 28.8 us -> 52.5 us  [swap(): return lax.ppermute(x, AXES, [(i, i ^ mask) for i in range(devices)])]
    pallas_call x4 -> x9, Pallas kernels: 29.1 us -> 17 us  [the longest x1 4.09 us: predict(): pl.pallas_call(functools.partial(predict_body, centers.shape[1]), grid=(d...]
    add x8 -> x16, other arithmetic: 2.62 us -> 0.4 us  [total_of(): keep = keep + swap(send, 1 << level, devices)]
    unnamed x10 -> x20, local copies, waits for them, and re-layouts: 1.73 us -> 3.06 us
  transfers between devices with their start and end apart: 16 -> 32, of which waited for: 15 -> 16; matrix products, arithmetic and copies ran while one was open for 0% -> 1% of each run, Pallas kernels for 4% -> 10%
where the time goes in v4:
time: 97.1 us; the launch traced here: 96.9 us
  starting transfers between devices  52.5 us (54%)
  waiting for transfers between devices  22.4 us (23%)
  Pallas kernels  17 us (18%)
  local copies, waits for them, and re-layouts  3.17 us (3%)
  between operations  1.18 us (1%)
    ppermute x32, starting transfers between devices, swap(): return lax.ppermute(x, AXES, [(i, i ^ mask) for i in range(devices)])  52.5 us
    ppermute x32, waiting for transfers between devices, swap(): return lax.ppermute(x, AXES, [(i, i ^ mask) for i in range(devices)])  22.4 us
    pallas_call x1, Pallas kernels, predict(): pl.pallas_call(functools.partial(predict_body, centers.shape[1]), grid=(d...  4.09 us
    unnamed x20, local copies, waits for them, and re-layouts  3.06 us
    pallas_call x2, Pallas kernels, pick_batch(): pl.pallas_call(pick_body, grid=(2,), in_specs=[pl.BlockSpec((1, rows), la...  2.75 us
    pallas_call x1, Pallas kernels, update(): pl.pallas_call(update_body, in_specs=[vmem] * 7, out_specs=[hbm, hbm, vme...  2.48 us
    pallas_call x1, Pallas kernels, distances(): pl.pallas_call(distance_body, grid=(depth // block,), in_specs=exchange_s...  2.03 us
    pallas_call x1, Pallas kernels, update_more(): pl.pallas_call(functools.partial(update_more_body, begin), in_specs=[vmem...  1.98 us
  transfers between devices with their start and end apart: 32, of which 16 were waited for; matrix products, arithmetic and copies ran while one was open for 1% of the time, Pallas kernels for 10%

profile of v4, /device:TPU:1, one launch (start us, length us, event | category | flops | bytes accessed | tf_op | source)
XLA Modules:
  0.0 96.9 jit_solution(15949737331403419780)
XLA Ops:
  0.6 0.0 copy-start
  0.6 2.3 %copy-done = bf16[768,3072]{1,0:T(8,128)(2,1)S(1)} copy-done((bf16[768,3072]{1,0:T(8,128)(2,1)S(1)}, bf16[768,3072]{1,0:T(8,128)(2,1)}, u32[]{:S(2)}) %copy-start) | copy-done | bytes 4718616
  3.0 0.7 copy-done.4
  3.7 1.4 %pick_batch.3 = (bf16[128,1536]{1,0:T(8,128)(2,1)S(1)}, bf16[128,1536]{1,0:T(8,128)(2,1)S(1)}) custom-call(s32[1,256]{1,0:T(1,128)S(1)} %bitcast.15, bf16[768,3072]{1,0:T(8,128)(2,1)S(1)} %copy-done), custom_call_target="tpu_custom_call" | custom-call | flops 603979776 | bytes 3145728 | tf_op jit(solution)/shard_map/pick_batch/pallas_call | solution.py:85
  5.0 0.0 slice-start.1
  5.0 0.1 collective-permute-start.8
  5.2 1.4 %pick_batch.2 = (bf16[128,1536]{1,0:T(8,128)(2,1)S(1)}, bf16[128,1536]{1,0:T(8,128)(2,1)S(1)}) custom-call(s32[1,256]{1,0:T(1,128)S(1)} %bitcast.16, bf16[768,3072]{1,0:T(8,128)(2,1)S(1)} %copy-done), custom_call_target="tpu_custom_call" | custom-call | flops 603979776 | bytes 3145728 | tf_op jit(solution)/shard_map/pick_batch/pallas_call | solution.py:85
  6.6 0.5 collective-permute-start
  7.1 0.1 add.52
  7.2 2.3 %collective-permute-start.9 = (bf16[64,1536]{1,0:T(8,128)(2,1)S(1)}, bf16[64,1536]{1,0:T(8,128)(2,1)S(1)}, u32[]{:S(2)}, u32[]{:S(2)}) collective-permute-start(bf16[64,1536]{1,0:T(8,128)(2,1)S(1)} %slice.103), channel_id=1, source_target_pairs={{0,2},{1,3},{2,0},{3,1},{4,6},{5,7},{6,4},{7,5},{8,10},{9,11},{10,... | collective-permute-start | bytes 589832 | tf_op jit(solution)/shard_map/ppermute | solution.py:452
  9.5 0.1 add.48
  9.6 0.0 copy-start.7
  9.7 1.6 %collective-permute-start.1 = (bf16[64,1536]{1,0:T(8,128)(2,1)S(1)}, bf16[64,1536]{1,0:T(8,128)(2,1)S(1)}, u32[]{:S(2)}, u32[]{:S(2)}) collective-permute-start(bf16[64,1536]{1,0:T(8,128)(2,1)S(1)} %slice.97), channel_id=1, source_target_pairs={{0,2},{1,3},{2,0},{3,1},{4,6},{5,7},{6,4},{7,5},{8,10},{9,11},{10,... | collective-permute-start | bytes 589832 | tf_op jit(solution)/shard_map/ppermute | solution.py:452
  11.2 3.1 %collective-permute-done.9 = bf16[64,1536]{1,0:T(8,128)(2,1)S(1)} collective-permute-done((bf16[64,1536]{1,0:T(8,128)(2,1)S(1)}, bf16[64,1536]{1,0:T(8,128)(2,1)S(1)}, u32[]{:S(2)}, u32[]{:S(2)}) %collective-permute-start.9) | collective-permute-done | bytes 196640 | tf_op jit(solution)/shard_map/ppermute | solution.py:452
  14.4 1.3 %collective-permute-start.10 = (bf16[32,1536]{1,0:T(8,128)(2,1)S(1)}, bf16[32,1536]{1,0:T(8,128)(2,1)S(1)}, u32[]{:S(2)}, u32[]{:S(2)}) collective-permute-start(bf16[32,1536]{1,0:T(8,128)(2,1)S(1)} %slice.105), channel_id=1, source_target_pairs={{0,4},{1,5},{2,6},{3,7},{4,0},{5,1},{6,2},{7,3},{8,12},{9,13},{10,... | collective-permute-start | bytes 294920 | tf_op jit(solution)/shard_map/ppermute | solution.py:452
  15.7 2.9 %collective-permute-done.1 = bf16[64,1536]{1,0:T(8,128)(2,1)S(1)} collective-permute-done((bf16[64,1536]{1,0:T(8,128)(2,1)S(1)}, bf16[64,1536]{1,0:T(8,128)(2,1)S(1)}, u32[]{:S(2)}, u32[]{:S(2)}) %collective-permute-start.1) | collective-permute-done | bytes 196640 | tf_op jit(solution)/shard_map/ppermute | solution.py:452
  18.6 1.3 %collective-permute-start.2 = (bf16[32,1536]{1,0:T(8,128)(2,1)S(1)}, bf16[32,1536]{1,0:T(8,128)(2,1)S(1)}, u32[]{:S(2)}, u32[]{:S(2)}) collective-permute-start(bf16[32,1536]{1,0:T(8,128)(2,1)S(1)} %slice.99), channel_id=1, source_target_pairs={{0,4},{1,5},{2,6},{3,7},{4,0},{5,1},{6,2},{7,3},{8,12},{9,13},{10,... | collective-permute-start | bytes 294920 | tf_op jit(solution)/shard_map/ppermute | solution.py:452
  19.9 2.4 %collective-permute-start.11 = (bf16[16,1536]{1,0:T(8,128)(2,1)S(1)}, bf16[16,1536]{1,0:T(8,128)(2,1)S(1)}, u32[]{:S(2)}, u32[]{:S(2)}) collective-permute-start(bf16[16,1536]{1,0:T(8,128)(2,1)S(1)} %slice.107), channel_id=1, source_target_pairs={{0,8},{1,9},{2,10},{3,11},{4,12},{5,13},{6,14},{7,15},{8,0},{9,1},... | collective-permute-start | bytes 147464 | tf_op jit(solution)/shard_map/ppermute | solution.py:452
  22.3 2.1 %collective-permute-start.3 = (bf16[16,1536]{1,0:T(8,128)(2,1)S(1)}, bf16[16,1536]{1,0:T(8,128)(2,1)S(1)}, u32[]{:S(2)}, u32[]{:S(2)}) collective-permute-start(bf16[16,1536]{1,0:T(8,128)(2,1)S(1)} %slice.101), channel_id=1, source_target_pairs={{0,8},{1,9},{2,10},{3,11},{4,12},{5,13},{6,14},{7,15},{8,0},{9,1},... | collective-permute-start | bytes 147464 | tf_op jit(solution)/shard_map/ppermute | solution.py:452
  24.5 2.2 %collective-permute-start.12 = (bf16[16,1536]{1,0:T(8,128)(2,1)S(1)}, bf16[16,1536]{1,0:T(8,128)(2,1)S(1)}, u32[]{:S(2)}, u32[]{:S(2)}) collective-permute-start(bf16[16,1536]{1,0:T(8,128)(2,1)S(1)} %slice_add_fusion.8), channel_id=1, source_target_pairs={{0,8},{1,9},{2,10},{3,11},{4,12},{5,13},{6,14},{7,15},{8,0},{9,1},... | collective-permute-start | bytes 147464 | tf_op jit(solution)/shard_map/ppermute | solution.py:452
  26.6 0.8 collective-permute-done.3
  27.5 1.5 %collective-permute-start.4 = (bf16[16,1536]{1,0:T(8,128)(2,1)S(1)}, bf16[16,1536]{1,0:T(8,128)(2,1)S(1)}, u32[]{:S(2)}, u32[]{:S(2)}) collective-permute-start(bf16[16,1536]{1,0:T(8,128)(2,1)S(1)} %slice_add_fusion.9), channel_id=1, source_target_pairs={{0,8},{1,9},{2,10},{3,11},{4,12},{5,13},{6,14},{7,15},{8,0},{9,1},... | collective-permute-start | bytes 147464 | tf_op jit(solution)/shard_map/ppermute | solution.py:452
  29.0 2.0 %collective-permute-start.13 = (bf16[32,1536]{1,0:T(8,128)(2,1)S(1)}, bf16[32,1536]{1,0:T(8,128)(2,1)S(1)}, u32[]{:S(2)}, u32[]{:S(2)}) collective-permute-start(bf16[32,1536]{1,0:T(8,128)(2,1)S(1)} %pad_maximum_fusion.9), channel_id=1, source_target_pairs={{0,4},{1,5},{2,6},{3,7},{4,0},{5,1},{6,2},{7,3},{8,12},{9,13},{10,... | collective-permute-start | bytes 294920 | tf_op jit(solution)/shard_map/ppermute | solution.py:452
  31.0 1.0 collective-permute-done.4
  32.0 0.6 collective-permute-start.5
  32.6 0.6 collective-permute-done.13
  33.3 1.3 %collective-permute-start.14 = (bf16[64,1536]{1,0:T(8,128)(2,1)S(1)}, bf16[64,1536]{1,0:T(8,128)(2,1)S(1)}, u32[]{:S(2)}, u32[]{:S(2)}) collective-permute-start(bf16[64,1536]{1,0:T(8,128)(2,1)S(1)} %pad_maximum_fusion.5), channel_id=1, source_target_pairs={{0,2},{1,3},{2,0},{3,1},{4,6},{5,7},{6,4},{7,5},{8,10},{9,11},{10,... | collective-permute-start | bytes 589832 | tf_op jit(solution)/shard_map/ppermute | solution.py:452
  34.6 1.3 %collective-permute-done.5 = bf16[32,1536]{1,0:T(8,128)(2,1)S(1)} collective-permute-done((bf16[32,1536]{1,0:T(8,128)(2,1)S(1)}, bf16[32,1536]{1,0:T(8,128)(2,1)S(1)}, u32[]{:S(2)}, u32[]{:S(2)}) %collective-permute-start.5) | collective-permute-done | bytes 98336 | tf_op jit(solution)/shard_map/ppermute | solution.py:452
  35.9 1.5 %collective-permute-start.6 = (bf16[64,1536]{1,0:T(8,128)(2,1)S(1)}, bf16[64,1536]{1,0:T(8,128)(2,1)S(1)}, u32[]{:S(2)}, u32[]{:S(2)}) collective-permute-start(bf16[64,1536]{1,0:T(8,128)(2,1)S(1)} %pad_maximum_fusion.4), channel_id=1, source_target_pairs={{0,2},{1,3},{2,0},{3,1},{4,6},{5,7},{6,4},{7,5},{8,10},{9,11},{10,... | collective-permute-start | bytes 589832 | tf_op jit(solution)/shard_map/ppermute | solution.py:452
  37.4 0.7 collective-permute-done.14
  38.1 6.2 %collective-permute-start.15 = (bf16[128,1536]{1,0:T(8,128)(2,1)S(1)}, bf16[128,1536]{1,0:T(8,128)(2,1)S(1)}, u32[]{:S(2)}, u32[]{:S(2)}) collective-permute-start(bf16[128,1536]{1,0:T(8,128)(2,1)S(1)} %pad_maximum_fusion.1.mine_ref), channel_id=1, source_target_pairs={{0,1},{1,0},{2,3},{3,2},{4,5},{5,4},{6,7},{7,6},{8,9},{9,8},{10,11... | collective-permute-start | bytes 1179656 | tf_op jit(solution)/shard_map/ppermute | solution.py:452
  44.4 2.0 %collective-permute-start.7 = (bf16[128,1536]{1,0:T(8,128)(2,1)S(1)}, bf16[128,1536]{1,0:T(8,128)(2,1)S(1)}, u32[]{:S(2)}, u32[]{:S(2)}) collective-permute-start(bf16[128,1536]{1,0:T(8,128)(2,1)S(1)} %pad_maximum_fusion.mine_ref), channel_id=1, source_target_pairs={{0,1},{1,0},{2,3},{3,2},{4,5},{5,4},{6,7},{7,6},{8,9},{9,8},{10,11... | collective-permute-start | bytes 1179656 | tf_op jit(solution)/shard_map/ppermute | solution.py:452
  46.4 1.2 %center_norms.1.norm_ref = f32[768,128]{1,0:T(8,128)S(1)} custom-call(bf16[768,3072]{1,0:T(8,128)(2,1)S(1)} %bitcast.8), custom_call_target="tpu_custom_call" | custom-call | flops 4718592 | bytes 4718592 | tf_op jit(solution)/shard_map/center_norms/pallas_call | solution.py:165
  47.6 1.7 %spread_weights.1 = (bf16[640,768]{1,0:T(8,128)(2,1)S(1)}, bf16[640,768]{1,0:T(8,128)(2,1)S(1)}, bf16[576,768]{1,0:T(8,128)(2,1)S(1)}, bf16[576,768]{1,0:T(8,128)(2,1)S(1)}, f32[160,768]{1,0:T(8,128)S(1)}) custom-call(s32[1,320]{1,0:T(1,128)S(1)} %reshape.13.index_ref, f32[160,320]{1,0:T(8,128)S(1)} %bitcast.14, f32[1000,768]{1,0:T(8,128)S(1)} %bitcast.9), custom_call_target="tpu_custom_call" | custom-call | flops 235929600 | bytes 7471104 | tf_op jit(solution)/shard_map/spread_weights/pallas_call | solution.py:138
  49.3 2.0 %distances.1.before_ref = f32[768,256]{1,0:T(8,128)S(1)} custom-call(bf16[128,1536]{1,0:T(8,128)(2,1)S(1)} %pad_maximum_fusion.1.mine_ref, bf16[128,1536]{1,0:T(8,128)(2,1)S(1)} %collective-permute-done.15.other_ref, bf16[768,3072]{1,0:T(8,128)(2,1)S(1)} %bitcast.8, f32[768,128]{1,0:T(8,128)S(1)} %center_norms.1.norm_ref), custom_call_target="tpu_custom_call" | custom-call | flops 603979776 | bytes 3145728 | tf_op jit(solution)/shard_map/distances/pallas_call | solution.py:254
  51.4 4.1 %predict.1 = (f32[640,128]{1,0:T(8,128)S(1)}, f32[640,128]{1,0:T(8,128)S(1)}, bf16[768,256]{1,0:T(8,128)(2,1)S(1)}, bf16[768,256]{1,0:T(8,128)(2,1)S(1)}) custom-call(bf16[128,1536]{1,0:T(8,128)(2,1)S(1)} %pad_maximum_fusion.mine_ref, bf16[128,1536]{1,0:T(8,128)(2,1)S(1)} %collective-permute-done.7.other_ref, bf16[768,3072]{1,0:T(8,128)(2,1)S(1)} %bitcast.8, ...), custom_call_target="tpu_custom_call" | custom-call | flops 1358954496 | bytes 5767168 | tf_op jit(solution)/shard_map/predict/pallas_call | solution.py:278
  55.5 0.1 collective-permute-start.24
  55.6 0.9 predict_more.1
  56.4 0.5 collective-permute-start.16
  57.0 0.2 collective-permute-done.24
  57.3 1.3 %collective-permute-start.25 = (f32[320,128]{1,0:T(8,128)S(1)}, f32[320,128]{1,0:T(8,128)S(1)}, u32[]{:S(2)}, u32[]{:S(2)}) collective-permute-start(f32[320,128]{1,0:T(8,128)S(1)} %slice.115), channel_id=1, source_target_pairs={{0,2},{1,3},{2,0},{3,1},{4,6},{5,7},{6,4},{7,5},{8,10},{9,11},{10,... | collective-permute-start | bytes 491528 | tf_op jit(solution)/shard_map/ppermute | solution.py:452
  58.6 0.9 collective-permute-start.17
  59.6 3.4 %collective-permute-done.25 = f32[320,128]{1,0:T(8,128)S(1)} collective-permute-done((f32[320,128]{1,0:T(8,128)S(1)}, f32[320,128]{1,0:T(8,128)S(1)}, u32[]{:S(2)}, u32[]{:S(2)}) %collective-permute-start.25) | collective-permute-done | bytes 163872 | tf_op jit(solution)/shard_map/ppermute | solution.py:452
  63.0 0.9 collective-permute-start.26
  63.9 2.2 %collective-permute-done.17 = f32[288,128]{1,0:T(8,128)S(1)} collective-permute-done((f32[288,128]{1,0:T(8,128)S(1)}, f32[288,128]{1,0:T(8,128)S(1)}, u32[]{:S(2)}, u32[]{:S(2)}) %collective-permute-start.17) | collective-permute-done | bytes 147488 | tf_op jit(solution)/shard_map/ppermute | solution.py:452
  66.2 0.9 collective-permute-start.18
  67.1 2.3 %collective-permute-start.27 = (f32[80,128]{1,0:T(8,128)S(1)}, f32[80,128]{1,0:T(8,128)S(1)}, u32[]{:S(2)}, u32[]{:S(2)}) collective-permute-start(f32[80,128]{1,0:T(8,128)S(1)} %slice.119), channel_id=1, source_target_pairs={{0,8},{1,9},{2,10},{3,11},{4,12},{5,13},{6,14},{7,15},{8,0},{9,1},... | collective-permute-start | bytes 122888 | tf_op jit(solution)/shard_map/ppermute | solution.py:452
  69.4 0.1 collective-permute-done.18
  69.5 1.6 %collective-permute-start.19 = (f32[72,128]{1,0:T(8,128)S(1)}, f32[72,128]{1,0:T(8,128)S(1)}, u32[]{:S(2)}, u32[]{:S(2)}) collective-permute-start(f32[72,128]{1,0:T(8,128)S(1)} %slice.113), channel_id=1, source_target_pairs={{0,8},{1,9},{2,10},{3,11},{4,12},{5,13},{6,14},{7,15},{8,0},{9,1},... | collective-permute-start | bytes 110600 | tf_op jit(solution)/shard_map/ppermute | solution.py:452
  71.1 2.0 %collective-permute-start.28 = (f32[80,128]{1,0:T(8,128)S(1)}, f32[80,128]{1,0:T(8,128)S(1)}, u32[]{:S(2)}, u32[]{:S(2)}) collective-permute-start(f32[80,128]{1,0:T(8,128)S(1)} %slice_add_fusion.10), channel_id=1, source_target_pairs={{0,8},{1,9},{2,10},{3,11},{4,12},{5,13},{6,14},{7,15},{8,0},{9,1},... | collective-permute-start | bytes 122888 | tf_op jit(solution)/shard_map/ppermute | solution.py:452
  73.1 1.6 %collective-permute-done.19 = f32[72,128]{1,0:T(8,128)S(1)} collective-permute-done((f32[72,128]{1,0:T(8,128)S(1)}, f32[72,128]{1,0:T(8,128)S(1)}, u32[]{:S(2)}, u32[]{:S(2)}) %collective-permute-start.19) | collective-permute-done | bytes 36896 | tf_op jit(solution)/shard_map/ppermute | solution.py:452
  74.7 0.8 collective-permute-start.20
  75.5 2.1 %collective-permute-start.29 = (f32[160,128]{1,0:T(8,128)S(1)}, f32[160,128]{1,0:T(8,128)S(1)}, u32[]{:S(2)}, u32[]{:S(2)}) collective-permute-start(f32[160,128]{1,0:T(8,128)S(1)} %pad_maximum_fusion.10), channel_id=1, source_target_pairs={{0,4},{1,5},{2,6},{3,7},{4,0},{5,1},{6,2},{7,3},{8,12},{9,13},{10,... | collective-permute-start | bytes 245768 | tf_op jit(solution)/shard_map/ppermute | solution.py:452
  77.6 1.3 %collective-permute-done.20 = f32[72,128]{1,0:T(8,128)S(1)} collective-permute-done((f32[72,128]{1,0:T(8,128)S(1)}, f32[72,128]{1,0:T(8,128)S(1)}, u32[]{:S(2)}, u32[]{:S(2)}) %collective-permute-start.20) | collective-permute-done | bytes 36896 | tf_op jit(solution)/shard_map/ppermute | solution.py:452
  78.9 0.0 collective-permute-start.21
  79.0 1.2 %collective-permute-done.29 = f32[160,128]{1,0:T(8,128)S(1)} collective-permute-done((f32[160,128]{1,0:T(8,128)S(1)}, f32[160,128]{1,0:T(8,128)S(1)}, u32[]{:S(2)}, u32[]{:S(2)}) %collective-permute-start.29) | collective-permute-done | bytes 81952 | tf_op jit(solution)/shard_map/ppermute | solution.py:452
  80.1 1.3 %collective-permute-start.30 = (f32[320,128]{1,0:T(8,128)S(1)}, f32[320,128]{1,0:T(8,128)S(1)}, u32[]{:S(2)}, u32[]{:S(2)}) collective-permute-start(f32[320,128]{1,0:T(8,128)S(1)} %pad_maximum_fusion.6), channel_id=1, source_target_pairs={{0,2},{1,3},{2,0},{3,1},{4,6},{5,7},{6,4},{7,5},{8,10},{9,11},{10,... | collective-permute-start | bytes 491528 | tf_op jit(solution)/shard_map/ppermute | solution.py:452
  81.4 1.1 %collective-permute-done.21 = f32[144,128]{1,0:T(8,128)S(1)} collective-permute-done((f32[144,128]{1,0:T(8,128)S(1)}, f32[144,128]{1,0:T(8,128)S(1)}, u32[]{:S(2)}, u32[]{:S(2)}) %collective-permute-start.21) | collective-permute-done | bytes 73760 | tf_op jit(solution)/shard_map/ppermute | solution.py:452
  82.6 1.3 %collective-permute-start.22 = (f32[288,128]{1,0:T(8,128)S(1)}, f32[288,128]{1,0:T(8,128)S(1)}, u32[]{:S(2)}, u32[]{:S(2)}) collective-permute-start(f32[288,128]{1,0:T(8,128)S(1)} %pad_maximum_fusion.7), channel_id=1, source_target_pairs={{0,2},{1,3},{2,0},{3,1},{4,6},{5,7},{6,4},{7,5},{8,10},{9,11},{10,... | collective-permute-start | bytes 442376 | tf_op jit(solution)/shard_map/ppermute | solution.py:452
  83.9 0.7 collective-permute-done.30
  84.6 5.9 %collective-permute-start.31 = (f32[640,128]{1,0:T(8,128)S(1)}, f32[640,128]{1,0:T(8,128)S(1)}, u32[]{:S(2)}, u32[]{:S(2)}) collective-permute-start(f32[640,128]{1,0:T(8,128)S(1)} %pad_maximum_fusion.2.mine_ref), channel_id=1, source_target_pairs={{0,1},{1,0},{2,3},{3,2},{4,5},{5,4},{6,7},{7,6},{8,9},{9,8},{10,11... | collective-permute-start | bytes 983048 | tf_op jit(solution)/shard_map/ppermute | solution.py:452
  90.5 1.7 %collective-permute-start.23 = (f32[576,128]{1,0:T(8,128)S(1)}, f32[576,128]{1,0:T(8,128)S(1)}, u32[]{:S(2)}, u32[]{:S(2)}) collective-permute-start(f32[576,128]{1,0:T(8,128)S(1)} %pad_maximum_fusion.3.mine_ref), channel_id=1, source_target_pairs={{0,1},{1,0},{2,3},{3,2},{4,5},{5,4},{6,7},{7,6},{8,9},{9,8},{10,11... | collective-permute-start | bytes 884744 | tf_op jit(solution)/shard_map/ppermute | solution.py:452
  92.3 2.5 %update.1 = (f32[1000,768]{1,0:T(8,128)}, f32[1000,256]{1,0:T(8,128)}, bf16[256,768]{1,0:T(8,128)(2,1)S(1)}, bf16[256,768]{1,0:T(8,128)(2,1)S(1)}) custom-call(f32[640,128]{1,0:T(8,128)S(1)} %pad_maximum_fusion.2.mine_ref, f32[640,128]{1,0:T(8,128)S(1)} %collective-permute-done.31.other_ref, f32[1000,256]{1,0:T(8,128)S(1)} %bitcast.12, ...), custom_call_target="tpu_custom_call" | custom-call | flops 754974720 | bytes 3932160 | tf_op jit(solution)/shard_map/update/pallas_call | solution.py:391
  94.8 2.0 %update_more.1 = (f32[1000,768]{1,0:T(8,128)}, f32[1000,256]{1,0:T(8,128)}) custom-call(f32[576,128]{1,0:T(8,128)S(1)} %pad_maximum_fusion.3.mine_ref, f32[576,128]{1,0:T(8,128)S(1)} %collective-permute-done.23.other_ref, f32[1000,256]{1,0:T(8,128)S(1)} %bitcast.13, f32[1000,768]{1,0:T(8,128)S(1)} %bitcast.11, ...), custom_call_target="tpu_custom_call", output_to_operand_aliasing={{0}: (6, {}), {1}: (7, {})} | custom-call | flops 613416960 | bytes 4259840 | tf_op jit(solution)/shard_map/update_more/pallas_call | solution.py:429
  (71 shorter events, 0.6 us)
Async XLA Ops:
  0.6 2.3 %copy-start = (bf16[768,3072]{1,0:T(8,128)(2,1)S(1)}, bf16[768,3072]{1,0:T(8,128)(2,1)}, u32[]{:S(2)}) copy-start(bf16[768,3072]{1,0:T(8,128)(2,1)} %centers_ref.9) | copy-start | bytes 14155780
  3.0 0.7 copy-start.4
  3.6 42.8 %slice-start = ((s8[4718592]{0:T(1024)(128)(4,1)}), s8[4194304]{0:T(1024)(128)(4,1)S(1)}, s32[]{:S(2)}) async-start(s8[4718592]{0:T(1024)(128)(4,1)} %bitcast.7), calls=%async_computation | async-start | bytes 8388608
  5.0 41.4 %slice-start.1 = ((s8[4718592]{0:T(1024)(128)(4,1)}), s8[524288]{0:T(1024)(128)(4,1)S(1)}, s32[]{:S(2)}) async-start(s8[4718592]{0:T(1024)(128)(4,1)} %bitcast.7), calls=%async_computation.1 | async-start | bytes 1048576
  5.0 2.0 %collective-permute-start.8 = (bf16[128,1536]{1,0:T(8,128)(2,1)S(1)}, bf16[128,1536]{1,0:T(8,128)(2,1)S(1)}, u32[]{:S(2)}, u32[]{:S(2)}) collective-permute-start(bf16[128,1536]{1,0:T(8,128)(2,1)S(1)} %get-tuple-element.28), channel_id=1, source_target_pairs={{0,1},{1,0},{2,3},{3,2},{4,5},{5,4},{6,7},{7,6},{8,9},{9,8},{10,11... | collective-permute-start | bytes 1179656 | tf_op jit(solution)/shard_map/ppermute | solution.py:452
  6.6 3.0 %collective-permute-start = (bf16[128,1536]{1,0:T(8,128)(2,1)S(1)}, bf16[128,1536]{1,0:T(8,128)(2,1)S(1)}, u32[]{:S(2)}, u32[]{:S(2)}) collective-permute-start(bf16[128,1536]{1,0:T(8,128)(2,1)S(1)} %get-tuple-element.26), channel_id=1, source_target_pairs={{0,1},{1,0},{2,3},{3,2},{4,5},{5,4},{6,7},{7,6},{8,9},{9,8},{10,11... | collective-permute-start | bytes 1179656 | tf_op jit(solution)/shard_map/ppermute | solution.py:452
  7.2 7.2 %collective-permute-start.9 = (bf16[64,1536]{1,0:T(8,128)(2,1)S(1)}, bf16[64,1536]{1,0:T(8,128)(2,1)S(1)}, u32[]{:S(2)}, u32[]{:S(2)}) collective-permute-start(bf16[64,1536]{1,0:T(8,128)(2,1)S(1)} %slice.103), channel_id=1, source_target_pairs={{0,2},{1,3},{2,0},{3,1},{4,6},{5,7},{6,4},{7,5},{8,10},{9,11},{10,... | collective-permute-start | bytes 589832 | tf_op jit(solution)/shard_map/ppermute | solution.py:452
  9.6 36.8 %copy-start.7 = (s32[320]{0:T(512)S(1)}, s32[320]{0:T(512)}, u32[]{:S(2)}) copy-start(s32[320]{0:T(512)} %param.11) | copy-start | bytes 3844
  9.7 8.9 %collective-permute-start.1 = (bf16[64,1536]{1,0:T(8,128)(2,1)S(1)}, bf16[64,1536]{1,0:T(8,128)(2,1)S(1)}, u32[]{:S(2)}, u32[]{:S(2)}) collective-permute-start(bf16[64,1536]{1,0:T(8,128)(2,1)S(1)} %slice.97), channel_id=1, source_target_pairs={{0,2},{1,3},{2,0},{3,1},{4,6},{5,7},{6,4},{7,5},{8,10},{9,11},{10,... | collective-permute-start | bytes 589832 | tf_op jit(solution)/shard_map/ppermute | solution.py:452
  14.4 5.5 %collective-permute-start.10 = (bf16[32,1536]{1,0:T(8,128)(2,1)S(1)}, bf16[32,1536]{1,0:T(8,128)(2,1)S(1)}, u32[]{:S(2)}, u32[]{:S(2)}) collective-permute-start(bf16[32,1536]{1,0:T(8,128)(2,1)S(1)} %slice.105), channel_id=1, source_target_pairs={{0,4},{1,5},{2,6},{3,7},{4,0},{5,1},{6,2},{7,3},{8,12},{9,13},{10,... | collective-permute-start | bytes 294920 | tf_op jit(solution)/shard_map/ppermute | solution.py:452
  18.6 3.7 %collective-permute-start.2 = (bf16[32,1536]{1,0:T(8,128)(2,1)S(1)}, bf16[32,1536]{1,0:T(8,128)(2,1)S(1)}, u32[]{:S(2)}, u32[]{:S(2)}) collective-permute-start(bf16[32,1536]{1,0:T(8,128)(2,1)S(1)} %slice.99), channel_id=1, source_target_pairs={{0,4},{1,5},{2,6},{3,7},{4,0},{5,1},{6,2},{7,3},{8,12},{9,13},{10,... | collective-permute-start | bytes 294920 | tf_op jit(solution)/shard_map/ppermute | solution.py:452
  19.9 4.5 %collective-permute-start.11 = (bf16[16,1536]{1,0:T(8,128)(2,1)S(1)}, bf16[16,1536]{1,0:T(8,128)(2,1)S(1)}, u32[]{:S(2)}, u32[]{:S(2)}) collective-permute-start(bf16[16,1536]{1,0:T(8,128)(2,1)S(1)} %slice.107), channel_id=1, source_target_pairs={{0,8},{1,9},{2,10},{3,11},{4,12},{5,13},{6,14},{7,15},{8,0},{9,1},... | collective-permute-start | bytes 147464 | tf_op jit(solution)/shard_map/ppermute | solution.py:452
  22.3 5.1 %collective-permute-start.3 = (bf16[16,1536]{1,0:T(8,128)(2,1)S(1)}, bf16[16,1536]{1,0:T(8,128)(2,1)S(1)}, u32[]{:S(2)}, u32[]{:S(2)}) collective-permute-start(bf16[16,1536]{1,0:T(8,128)(2,1)S(1)} %slice.101), channel_id=1, source_target_pairs={{0,8},{1,9},{2,10},{3,11},{4,12},{5,13},{6,14},{7,15},{8,0},{9,1},... | collective-permute-start | bytes 147464 | tf_op jit(solution)/shard_map/ppermute | solution.py:452
  24.5 4.5 %collective-permute-start.12 = (bf16[16,1536]{1,0:T(8,128)(2,1)S(1)}, bf16[16,1536]{1,0:T(8,128)(2,1)S(1)}, u32[]{:S(2)}, u32[]{:S(2)}) collective-permute-start(bf16[16,1536]{1,0:T(8,128)(2,1)S(1)} %slice_add_fusion.8), channel_id=1, source_target_pairs={{0,8},{1,9},{2,10},{3,11},{4,12},{5,13},{6,14},{7,15},{8,0},{9,1},... | collective-permute-start | bytes 147464 | tf_op jit(solution)/shard_map/ppermute | solution.py:452
  27.5 4.5 %collective-permute-start.4 = (bf16[16,1536]{1,0:T(8,128)(2,1)S(1)}, bf16[16,1536]{1,0:T(8,128)(2,1)S(1)}, u32[]{:S(2)}, u32[]{:S(2)}) collective-permute-start(bf16[16,1536]{1,0:T(8,128)(2,1)S(1)} %slice_add_fusion.9), channel_id=1, source_target_pairs={{0,8},{1,9},{2,10},{3,11},{4,12},{5,13},{6,14},{7,15},{8,0},{9,1},... | collective-permute-start | bytes 147464 | tf_op jit(solution)/shard_map/ppermute | solution.py:452
  29.0 4.3 %collective-permute-start.13 = (bf16[32,1536]{1,0:T(8,128)(2,1)S(1)}, bf16[32,1536]{1,0:T(8,128)(2,1)S(1)}, u32[]{:S(2)}, u32[]{:S(2)}) collective-permute-start(bf16[32,1536]{1,0:T(8,128)(2,1)S(1)} %pad_maximum_fusion.9), channel_id=1, source_target_pairs={{0,4},{1,5},{2,6},{3,7},{4,0},{5,1},{6,2},{7,3},{8,12},{9,13},{10,... | collective-permute-start | bytes 294920 | tf_op jit(solution)/shard_map/ppermute | solution.py:452
  32.0 3.9 %collective-permute-start.5 = (bf16[32,1536]{1,0:T(8,128)(2,1)S(1)}, bf16[32,1536]{1,0:T(8,128)(2,1)S(1)}, u32[]{:S(2)}, u32[]{:S(2)}) collective-permute-start(bf16[32,1536]{1,0:T(8,128)(2,1)S(1)} %pad_maximum_fusion.8), channel_id=1, source_target_pairs={{0,4},{1,5},{2,6},{3,7},{4,0},{5,1},{6,2},{7,3},{8,12},{9,13},{10,... | collective-permute-start | bytes 294920 | tf_op jit(solution)/shard_map/ppermute | solution.py:452
  33.3 4.8 %collective-permute-start.14 = (bf16[64,1536]{1,0:T(8,128)(2,1)S(1)}, bf16[64,1536]{1,0:T(8,128)(2,1)S(1)}, u32[]{:S(2)}, u32[]{:S(2)}) collective-permute-start(bf16[64,1536]{1,0:T(8,128)(2,1)S(1)} %pad_maximum_fusion.5), channel_id=1, source_target_pairs={{0,2},{1,3},{2,0},{3,1},{4,6},{5,7},{6,4},{7,5},{8,10},{9,11},{10,... | collective-permute-start | bytes 589832 | tf_op jit(solution)/shard_map/ppermute | solution.py:452
  35.9 8.4 %collective-permute-start.6 = (bf16[64,1536]{1,0:T(8,128)(2,1)S(1)}, bf16[64,1536]{1,0:T(8,128)(2,1)S(1)}, u32[]{:S(2)}, u32[]{:S(2)}) collective-permute-start(bf16[64,1536]{1,0:T(8,128)(2,1)S(1)} %pad_maximum_fusion.4), channel_id=1, source_target_pairs={{0,2},{1,3},{2,0},{3,1},{4,6},{5,7},{6,4},{7,5},{8,10},{9,11},{10,... | collective-permute-start | bytes 589832 | tf_op jit(solution)/shard_map/ppermute | solution.py:452
  38.1 9.5 %copy-start.1 = (f32[768,1000]{0,1:T(8,128)S(1)}, f32[768,1000]{0,1:T(8,128)}, u32[]{:S(2)}) copy-start(f32[768,1000]{0,1:T(8,128)} %param.8) | copy-start | bytes 9216004
  38.1 9.5 %copy-start.3 = (f32[320,160]{0,1:T(8,128)S(1)}, f32[320,160]{0,1:T(8,128)}, u32[]{:S(2)}) copy-start(f32[320,160]{0,1:T(8,128)} %param.12) | copy-start | bytes 614404
  38.1 11.2 %collective-permute-start.15 = (bf16[128,1536]{1,0:T(8,128)(2,1)S(1)}, bf16[128,1536]{1,0:T(8,128)(2,1)S(1)}, u32[]{:S(2)}, u32[]{:S(2)}) collective-permute-start(bf16[128,1536]{1,0:T(8,128)(2,1)S(1)} %pad_maximum_fusion.1.mine_ref), channel_id=1, source_target_pairs={{0,1},{1,0},{2,3},{3,2},{4,5},{5,4},{6,7},{7,6},{8,9},{9,8},{10,11... | collective-permute-start | bytes 1179656 | tf_op jit(solution)/shard_map/ppermute | solution.py:452
  44.4 7.0 %collective-permute-start.7 = (bf16[128,1536]{1,0:T(8,128)(2,1)S(1)}, bf16[128,1536]{1,0:T(8,128)(2,1)S(1)}, u32[]{:S(2)}, u32[]{:S(2)}) collective-permute-start(bf16[128,1536]{1,0:T(8,128)(2,1)S(1)} %pad_maximum_fusion.mine_ref), channel_id=1, source_target_pairs={{0,1},{1,0},{2,3},{3,2},{4,5},{5,4},{6,7},{7,6},{8,9},{9,8},{10,11... | collective-permute-start | bytes 1179656 | tf_op jit(solution)/shard_map/ppermute | solution.py:452
  55.5 1.7 %collective-permute-start.24 = (f32[640,128]{1,0:T(8,128)S(1)}, f32[640,128]{1,0:T(8,128)S(1)}, u32[]{:S(2)}, u32[]{:S(2)}) collective-permute-start(f32[640,128]{1,0:T(8,128)S(1)} %get-tuple-element.36), channel_id=1, source_target_pairs={{0,1},{1,0},{2,3},{3,2},{4,5},{5,4},{6,7},{7,6},{8,9},{9,8},{10,11... | collective-permute-start | bytes 983048 | tf_op jit(solution)/shard_map/ppermute | solution.py:452
  56.4 2.1 %collective-permute-start.16 = (f32[576,128]{1,0:T(8,128)S(1)}, f32[576,128]{1,0:T(8,128)S(1)}, u32[]{:S(2)}, u32[]{:S(2)}) collective-permute-start(f32[576,128]{1,0:T(8,128)S(1)} %get-tuple-element.34), channel_id=1, source_target_pairs={{0,1},{1,0},{2,3},{3,2},{4,5},{5,4},{6,7},{7,6},{8,9},{9,8},{10,11... | collective-permute-start | bytes 884744 | tf_op jit(solution)/shard_map/ppermute | solution.py:452
  57.2 35.0 %copy-start.2 = (f32[256,1000]{0,1:T(8,128)S(1)}, f32[256,1000]{0,1:T(8,128)}, u32[]{:S(2)}) copy-start(f32[256,1000]{0,1:T(8,128)} %param.9) | copy-start | bytes 3072004
  57.2 35.0 %copy-start.5 = (s32[256]{0:T(256)S(1)}, s32[256]{0:T(256)}, u32[]{:S(2)}) copy-start(s32[256]{0:T(256)} %param.10) | copy-start | bytes 3076
  57.2 35.0 %copy-start.6 = (f32[160]{0:T(256)S(1)}, f32[160]{0:T(256)}, u32[]{:S(2)}) copy-start(f32[160]{0:T(256)} %param.13) | copy-start | bytes 1924
  57.3 5.7 %collective-permute-start.25 = (f32[320,128]{1,0:T(8,128)S(1)}, f32[320,128]{1,0:T(8,128)S(1)}, u32[]{:S(2)}, u32[]{:S(2)}) collective-permute-start(f32[320,128]{1,0:T(8,128)S(1)} %slice.115), channel_id=1, source_target_pairs={{0,2},{1,3},{2,0},{3,1},{4,6},{5,7},{6,4},{7,5},{8,10},{9,11},{10,... | collective-permute-start | bytes 491528 | tf_op jit(solution)/shard_map/ppermute | solution.py:452
  58.6 7.5 %collective-permute-start.17 = (f32[288,128]{1,0:T(8,128)S(1)}, f32[288,128]{1,0:T(8,128)S(1)}, u32[]{:S(2)}, u32[]{:S(2)}) collective-permute-start(f32[288,128]{1,0:T(8,128)S(1)} %slice.109), channel_id=1, source_target_pairs={{0,2},{1,3},{2,0},{3,1},{4,6},{5,7},{6,4},{7,5},{8,10},{9,11},{10,... | collective-permute-start | bytes 442376 | tf_op jit(solution)/shard_map/ppermute | solution.py:452
  63.0 4.0 %collective-permute-start.26 = (f32[160,128]{1,0:T(8,128)S(1)}, f32[160,128]{1,0:T(8,128)S(1)}, u32[]{:S(2)}, u32[]{:S(2)}) collective-permute-start(f32[160,128]{1,0:T(8,128)S(1)} %slice.117), channel_id=1, source_target_pairs={{0,4},{1,5},{2,6},{3,7},{4,0},{5,1},{6,2},{7,3},{8,12},{9,13},{10,... | collective-permute-start | bytes 245768 | tf_op jit(solution)/shard_map/ppermute | solution.py:452
  66.2 3.3 %collective-permute-start.18 = (f32[144,128]{1,0:T(8,128)S(1)}, f32[144,128]{1,0:T(8,128)S(1)}, u32[]{:S(2)}, u32[]{:S(2)}) collective-permute-start(f32[144,128]{1,0:T(8,128)S(1)} %slice.111), channel_id=1, source_target_pairs={{0,4},{1,5},{2,6},{3,7},{4,0},{5,1},{6,2},{7,3},{8,12},{9,13},{10,... | collective-permute-start | bytes 221192 | tf_op jit(solution)/shard_map/ppermute | solution.py:452
  67.1 4.0 %collective-permute-start.27 = (f32[80,128]{1,0:T(8,128)S(1)}, f32[80,128]{1,0:T(8,128)S(1)}, u32[]{:S(2)}, u32[]{:S(2)}) collective-permute-start(f32[80,128]{1,0:T(8,128)S(1)} %slice.119), channel_id=1, source_target_pairs={{0,8},{1,9},{2,10},{3,11},{4,12},{5,13},{6,14},{7,15},{8,0},{9,1},... | collective-permute-start | bytes 122888 | tf_op jit(solution)/shard_map/ppermute | solution.py:452
  69.5 5.2 %collective-permute-start.19 = (f32[72,128]{1,0:T(8,128)S(1)}, f32[72,128]{1,0:T(8,128)S(1)}, u32[]{:S(2)}, u32[]{:S(2)}) collective-permute-start(f32[72,128]{1,0:T(8,128)S(1)} %slice.113), channel_id=1, source_target_pairs={{0,8},{1,9},{2,10},{3,11},{4,12},{5,13},{6,14},{7,15},{8,0},{9,1},... | collective-permute-start | bytes 110600 | tf_op jit(solution)/shard_map/ppermute | solution.py:452
  71.1 4.4 %collective-permute-start.28 = (f32[80,128]{1,0:T(8,128)S(1)}, f32[80,128]{1,0:T(8,128)S(1)}, u32[]{:S(2)}, u32[]{:S(2)}) collective-permute-start(f32[80,128]{1,0:T(8,128)S(1)} %slice_add_fusion.10), channel_id=1, source_target_pairs={{0,8},{1,9},{2,10},{3,11},{4,12},{5,13},{6,14},{7,15},{8,0},{9,1},... | collective-permute-start | bytes 122888 | tf_op jit(solution)/shard_map/ppermute | solution.py:452
  74.7 4.2 %collective-permute-start.20 = (f32[72,128]{1,0:T(8,128)S(1)}, f32[72,128]{1,0:T(8,128)S(1)}, u32[]{:S(2)}, u32[]{:S(2)}) collective-permute-start(f32[72,128]{1,0:T(8,128)S(1)} %slice_add_fusion.11), channel_id=1, source_target_pairs={{0,8},{1,9},{2,10},{3,11},{4,12},{5,13},{6,14},{7,15},{8,0},{9,1},... | collective-permute-start | bytes 110600 | tf_op jit(solution)/shard_map/ppermute | solution.py:452
  75.5 4.6 %collective-permute-start.29 = (f32[160,128]{1,0:T(8,128)S(1)}, f32[160,128]{1,0:T(8,128)S(1)}, u32[]{:S(2)}, u32[]{:S(2)}) collective-permute-start(f32[160,128]{1,0:T(8,128)S(1)} %pad_maximum_fusion.10), channel_id=1, source_target_pairs={{0,4},{1,5},{2,6},{3,7},{4,0},{5,1},{6,2},{7,3},{8,12},{9,13},{10,... | collective-permute-start | bytes 245768 | tf_op jit(solution)/shard_map/ppermute | solution.py:452
  78.9 3.6 %collective-permute-start.21 = (f32[144,128]{1,0:T(8,128)S(1)}, f32[144,128]{1,0:T(8,128)S(1)}, u32[]{:S(2)}, u32[]{:S(2)}) collective-permute-start(f32[144,128]{1,0:T(8,128)S(1)} %pad_maximum_fusion.11), channel_id=1, source_target_pairs={{0,4},{1,5},{2,6},{3,7},{4,0},{5,1},{6,2},{7,3},{8,12},{9,13},{10,... | collective-permute-start | bytes 221192 | tf_op jit(solution)/shard_map/ppermute | solution.py:452
  80.1 4.5 %collective-permute-start.30 = (f32[320,128]{1,0:T(8,128)S(1)}, f32[320,128]{1,0:T(8,128)S(1)}, u32[]{:S(2)}, u32[]{:S(2)}) collective-permute-start(f32[320,128]{1,0:T(8,128)S(1)} %pad_maximum_fusion.6), channel_id=1, source_target_pairs={{0,2},{1,3},{2,0},{3,1},{4,6},{5,7},{6,4},{7,5},{8,10},{9,11},{10,... | collective-permute-start | bytes 491528 | tf_op jit(solution)/shard_map/ppermute | solution.py:452
  82.6 7.9 %collective-permute-start.22 = (f32[288,128]{1,0:T(8,128)S(1)}, f32[288,128]{1,0:T(8,128)S(1)}, u32[]{:S(2)}, u32[]{:S(2)}) collective-permute-start(f32[288,128]{1,0:T(8,128)S(1)} %pad_maximum_fusion.7), channel_id=1, source_target_pairs={{0,2},{1,3},{2,0},{3,1},{4,6},{5,7},{6,4},{7,5},{8,10},{9,11},{10,... | collective-permute-start | bytes 442376 | tf_op jit(solution)/shard_map/ppermute | solution.py:452
  84.6 7.6 %collective-permute-start.31 = (f32[640,128]{1,0:T(8,128)S(1)}, f32[640,128]{1,0:T(8,128)S(1)}, u32[]{:S(2)}, u32[]{:S(2)}) collective-permute-start(f32[640,128]{1,0:T(8,128)S(1)} %pad_maximum_fusion.2.mine_ref), channel_id=1, source_target_pairs={{0,1},{1,0},{2,3},{3,2},{4,5},{5,4},{6,7},{7,6},{8,9},{9,8},{10,11... | collective-permute-start | bytes 983048 | tf_op jit(solution)/shard_map/ppermute | solution.py:452
  90.5 4.2 %collective-permute-start.23 = (f32[576,128]{1,0:T(8,128)S(1)}, f32[576,128]{1,0:T(8,128)S(1)}, u32[]{:S(2)}, u32[]{:S(2)}) collective-permute-start(f32[576,128]{1,0:T(8,128)S(1)} %pad_maximum_fusion.3.mine_ref), channel_id=1, source_target_pairs={{0,1},{1,0},{2,3},{3,2},{4,5},{5,4},{6,7},{7,6},{8,9},{9,8},{10,11... | collective-permute-start | bytes 884744 | tf_op jit(solution)/shard_map/ppermute | solution.py:452

commit v5 on v4

v5 whole, which is shorter than its diff:
```python
import functools
import math

import jax
import jax.numpy as jnp
from jax import lax
from jax.experimental import pallas as pl
from jax.experimental.pallas import tpu as pltpu
from jax.sharding import PartitionSpec as P

F32 = jnp.float32
BF16 = jnp.bfloat16
AXES = ("center", "sub")
HALVINGS = 2
CHUNKS = 1 << HALVINGS
LANE = 128
PARTS = 2
NT = (((1,), (1,)), ((), ()))
NN = (((1,), (0,)), ((), ()))
VMEM_LIMIT = 24 * 1024 * 1024


def dot(a, b, dims):
    return lax.dot_general(a, b, dims, preferred_element_type=F32)


def walk(sub, bits):
    order = list(range(bits))
    return order if sub == 0 else order[1:3] + order[:1] + order[3:]


def turns():
    center = lax.axis_index("center")
    return [
        sum(((center >> bit) & 1) << (HALVINGS - 1 - k) for k, bit in enumerate(walk(sub, HALVINGS + 1)[:HALVINGS]))
        for sub in range(2)
    ]


def column_of(row, width):
    return jnp.broadcast_to(row.astype(F32), (width, row.shape[1])).T


def two(x):
    high = x.astype(BF16)
    return high, (x - high.astype(F32)).astype(BF16)


def pick_rows(index_ref, columns, start, dtype, scale):
    column = column_of(index_ref[...] - start, LANE)
    lanes = lax.broadcasted_iota(jnp.int32, (1, LANE), 1).astype(F32)
    blocks = [
        jnp.where(column == lanes + float(LANE * k), scale, 0.0).astype(dtype)
        for k in range(columns // LANE)
    ]
    return jnp.concatenate(blocks, axis=1)


def params():
    return pltpu.CompilerParams(vmem_limit_bytes=VMEM_LIMIT)


def pick_body(first, index_hbm, centers_hbm, keep_ref, send_ref, pick_ref, index_ref, centers_ref, sems):
    sub = lax.axis_index("sub")
    blocks, count, block = centers_ref.shape
    rows = index_ref.shape[1]
    half = rows // 2
    size = half // CHUNKS
    copies = [pltpu.make_async_copy(index_hbm, index_ref, sems.at[blocks])] + [
        pltpu.make_async_copy(
            centers_hbm.at[:, pl.ds(first + k * block, block)], centers_ref.at[k], sems.at[k]
        )
        for k in range(blocks)
    ]
    for copy in copies:
        copy.start()
    copies[0].wait()
    start = (lax.axis_index("center") * 2 + sub) * count
    pick = pick_rows(index_ref, count, start, BF16, 1.0)
    for part, turn in enumerate(turns()):
        begin = jnp.where(sub == part, 0, half)
        for chunk in range(CHUNKS):
            to = pl.multiple_of(begin + (chunk ^ turn) * size, size)
            at = part * half + chunk * size
            pick_ref[pl.ds(to, size), :] = pick[at : at + size]
    for k in range(blocks):
        copies[k + 1].wait()
        found = dot(pick_ref[...], centers_ref[k], NN).astype(BF16)
        keep_ref[:, k * block : (k + 1) * block] = found[:half]
        send_ref[:, k * block : (k + 1) * block] = found[half:]


def pick_batch(batch_index, centers, part):
    rows = batch_index.shape[1]
    count, depth = centers.shape
    depth = depth // PARTS
    block = 512
    half = jax.ShapeDtypeStruct((rows // 2, depth), BF16)
    hbm = pl.BlockSpec(memory_space=pltpu.HBM)
    vmem = pl.BlockSpec(memory_space=pltpu.VMEM)
    return pl.pallas_call(
        functools.partial(pick_body, part * depth),
        in_specs=[hbm, hbm],
        out_specs=[vmem, vmem],
        out_shape=[half, half],
        scratch_shapes=[
            pltpu.VMEM((rows, count), BF16),
            pltpu.VMEM((1, rows), jnp.int32),
            pltpu.VMEM((depth // block, count, block), BF16),
            pltpu.SemaphoreType.DMA((depth // block + 1,)),
        ],
        compiler_params=params(),
        cost_estimate=pl.CostEstimate(
            flops=2 * rows * count * depth, bytes_accessed=2 * depth * (count + rows), transcendentals=0
        ),
        name="pick_batch",
    )(batch_index, centers)


def spread_body(
    first, classes, index_ref, eigvec_ref, weights_ref,
    high1_ref, low1_ref, high2_ref, low2_ref, spread_ref, all_ref,
):
    rank, points = eigvec_ref.shape
    count = weights_ref.shape[1]
    local = index_ref[...] - (lax.axis_index("center") * 2 + lax.axis_index("sub")) * count
    slots = lax.broadcasted_iota(jnp.int32, (count, points), 0)
    pick = jnp.where(slots == local, 1.0, 0.0).astype(BF16)
    vec = eigvec_ref[...]
    high = vec.astype(BF16)
    rest = vec - high.astype(F32)
    mid = rest.astype(BF16)
    low = (rest - mid.astype(F32)).astype(BF16)
    spread = dot(high, pick, NT) + dot(mid, pick, NT) + dot(low, pick, NT)
    spread_ref[...] = spread
    all_ref[:rank] = spread
    all_ref[rank : rank + classes] = weights_ref[...]
    all_ref[rank + classes :] = jnp.zeros((all_ref.shape[0] - rank - classes, count), F32)
    for begin, high_ref, low_ref in ((0, high1_ref, low1_ref), (first, high2_ref, low2_ref)):
        high_ref[...], low_ref[...] = two(all_ref[begin : begin + high_ref.shape[0]])


def spread_weights(nys_index, eigvec, weights, first, second):
    classes, count = weights.shape
    rank, points = eigvec.shape
    return pl.pallas_call(
        functools.partial(spread_body, first, classes),
        out_shape=[
            jax.ShapeDtypeStruct((first, count), BF16),
            jax.ShapeDtypeStruct((first, count), BF16),
            jax.ShapeDtypeStruct((second, count), BF16),
            jax.ShapeDtypeStruct((second, count), BF16),
            jax.ShapeDtypeStruct((rank, count), F32),
        ],
        scratch_shapes=[pltpu.VMEM((first + second, count), F32)],
        compiler_params=params(),
        cost_estimate=pl.CostEstimate(
            flops=6 * rank * points * count, bytes_accessed=8 * (first + second) * count, transcendentals=0
        ),
        name="spread_weights",
    )(nys_index, eigvec, weights)


def norms_body(centers_ref, norm_ref):
    wide = centers_ref[...].astype(F32)
    norm = jnp.sum(wide * wide, axis=1, keepdims=True)
    norm_ref[...] = jnp.broadcast_to(norm, norm_ref.shape)


def center_norms(centers):
    count, depth = centers.shape
    block = 256
    return pl.pallas_call(
        norms_body,
        grid=(count // block,),
        in_specs=[pl.BlockSpec((block, depth), lambda i: (i, 0))],
        out_specs=pl.BlockSpec((block, LANE), lambda i: (i, 0)),
        out_shape=jax.ShapeDtypeStruct((count, LANE), F32),
        compiler_params=params(),
        cost_estimate=pl.CostEstimate(flops=2 * count * depth, bytes_accessed=2 * count * depth, transcendentals=0),
        name="center_norms",
    )(centers)


def gather_batch(mine_ref, other_ref, batch_ref):
    lower = lax.axis_index("sub") == 0
    half = mine_ref.shape[0]
    size = half // CHUNKS
    for part, turn in enumerate(turns()):
        for chunk in range(CHUNKS):
            at = slice(chunk * size, (chunk + 1) * size)
            same = lower if part == 0 else jnp.logical_not(lower)
            to = pl.multiple_of(part * half + (chunk ^ turn) * size, size)
            batch_ref[pl.ds(to, size), :] = jnp.where(same, mine_ref[at], other_ref[at])


def nearer(first, centers_ref, batch_ref):
    rows, depth = batch_ref.shape
    batch = batch_ref[...].astype(F32)
    norm = jnp.sum(batch * batch, axis=1, keepdims=True)
    cross = dot(centers_ref[:, first : first + depth], batch_ref[...], NT)
    return jnp.broadcast_to(norm, (rows, LANE)).T[0:1] - 2.0 * cross


def product(high_ref, low_ref, value_high, value_low, total_ref, keep_ref, send_ref):
    half = keep_ref.shape[1]
    high = high_ref[...]
    total_ref[...] = dot(high, value_high, NN) + (dot(high, value_low, NN) + dot(low_ref[...], value_high, NN))
    lower = lax.axis_index("sub") == 0
    size = keep_ref.shape[0] // CHUNKS
    for chunk in range(CHUNKS):
        at = slice(chunk * size, (chunk + 1) * size)
        first, second = [
            total_ref[pl.ds(pl.multiple_of((chunk ^ turn) * size, 8), size), part * half : (part + 1) * half]
            for part, turn in enumerate(turns())
        ]
        keep_ref[at] = jnp.where(lower, first, second)
        send_ref[at] = jnp.where(lower, second, first)


def distance_body(mine_ref, other_ref, centers_ref, norm_ref, total_ref, batch_ref):
    gather_batch(mine_ref, other_ref, batch_ref)
    total_ref[...] = norm_ref[:, 0:1] + nearer(0, centers_ref, batch_ref)


def predict_body(
    mine_ref, other_ref, centers_ref, before_ref, high_ref, low_ref,
    keep_ref, send_ref, value_high_ref, value_low_ref, batch_ref, total_ref,
):
    depth = centers_ref.shape[1]
    gather_batch(mine_ref, other_ref, batch_ref)
    square = jnp.maximum(before_ref[...] + nearer(depth - batch_ref.shape[1], centers_ref, batch_ref), 0.0)
    value_high, value_low = two(jnp.exp(jnp.sqrt(square) * (-1.0 / math.sqrt(depth))))
    value_high_ref[...] = value_high
    value_low_ref[...] = value_low
    product(high_ref, low_ref, value_high, value_low, total_ref, keep_ref, send_ref)


def distances(mine, other, centers, norms):
    half, depth = mine.shape
    rows = 2 * half
    count = centers.shape[0]
    vmem = pl.BlockSpec(memory_space=pltpu.VMEM)
    return pl.pallas_call(
        distance_body,
        in_specs=[vmem] * 4,
        out_specs=vmem,
        out_shape=jax.ShapeDtypeStruct((count, rows), F32),
        scratch_shapes=[pltpu.VMEM((rows, depth), BF16)],
        compiler_params=params(),
        cost_estimate=pl.CostEstimate(
            flops=2 * rows * count * depth, bytes_accessed=2 * depth * (count + rows), transcendentals=0
        ),
        name="distances",
    )(mine, other, centers, norms)


def predict(mine, other, centers, before, high, low):
    half, depth = mine.shape
    rows = 2 * half
    count = centers.shape[0]
    padded = high.shape[0]
    out = jax.ShapeDtypeStruct((padded, half), F32)
    value = jax.ShapeDtypeStruct((count, rows), BF16)
    vmem = pl.BlockSpec(memory_space=pltpu.VMEM)
    return pl.pallas_call(
        predict_body,
        in_specs=[vmem] * 6,
        out_specs=[vmem] * 4,
        out_shape=[out, out, value, value],
        scratch_shapes=[pltpu.VMEM((rows, depth), BF16), pltpu.VMEM((padded, rows), F32)],
        compiler_params=params(),
        cost_estimate=pl.CostEstimate(
            flops=2 * rows * count * (depth + 3 * padded),
            bytes_accessed=2 * depth * (count + rows) + 4 * padded * (count + rows),
            transcendentals=2 * rows * count,
        ),
        name="predict",
    )(mine, other, centers, before, high, low)


def more_body(high_ref, low_ref, value_high_ref, value_low_ref, keep_ref, send_ref, total_ref):
    product(high_ref, low_ref, value_high_ref[...], value_low_ref[...], total_ref, keep_ref, send_ref)


def predict_more(high, low, value_high, value_low):
    padded = high.shape[0]
    count, rows = value_high.shape
    out = jax.ShapeDtypeStruct((padded, rows // 2), F32)
    return pl.pallas_call(
        more_body,
        out_shape=[out, out],
        scratch_shapes=[pltpu.VMEM((padded, rows), F32)],
        compiler_params=params(),
        cost_estimate=pl.CostEstimate(
            flops=6 * rows * count * padded, bytes_accessed=4 * padded * (count + rows), transcendentals=0
        ),
        name="predict_more",
    )(high, low, value_high, value_low)


def gather_total(mine_ref, other_ref, total_ref):
    lower = lax.axis_index("sub") == 0
    half = mine_ref.shape[1]
    size = mine_ref.shape[0] // CHUNKS
    for part, turn in enumerate(turns()):
        for chunk in range(CHUNKS):
            at = slice(chunk * size, (chunk + 1) * size)
            same = lower if part == 0 else jnp.logical_not(lower)
            to = pl.multiple_of((chunk ^ turn) * size, 8)
            total_ref[pl.ds(to, size), part * half : (part + 1) * half] = jnp.where(
                same, mine_ref[at], other_ref[at]
            )


def write_rows(begin, skip, total_ref, targets_ref, weights_ref, high_ref, low_ref, new_hbm, out_hbm, new_ref, sems):
    rows = new_ref.shape[0]
    blocks = sems.shape[0] - 1
    bounds = [8 * (rows // 8 * k // blocks) for k in range(blocks)] + [rows]
    high_right = high_ref[...]
    low_right = low_ref[...]
    copies = [
        pltpu.make_async_copy(
            total_ref.at[pl.ds(skip, rows)], out_hbm.at[pl.ds(begin, rows)], sems.at[blocks]
        )
    ]
    copies[0].start()
    for k in range(blocks):
        low_end, high_end = bounds[k : k + 2]
        here = slice(begin + low_end, begin + high_end)
        high, low = two(total_ref[skip + low_end : skip + high_end] - targets_ref[here])
        new_ref[low_end:high_end] = weights_ref[here] + (
            dot(high, high_right, NN) + (dot(high, low_right, NN) + dot(low, high_right, NN))
        )
        copy = pltpu.make_async_copy(
            new_ref.at[pl.ds(low_end, high_end - low_end)],
            new_hbm.at[pl.ds(begin + low_end, high_end - low_end)],
            sems.at[k],
        )
        copy.start()
        copies.append(copy)
    for copy in copies:
        copy.wait()


def update_body(
    mine_ref, other_ref, targets_ref, index_ref, eigval_ref, spread_ref, weights_ref,
    new_hbm, out_hbm, high_ref, low_ref, total_ref, new_ref, sems,
):
    start = (lax.axis_index("center") * 2 + lax.axis_index("sub")) * spread_ref.shape[1]
    rank, count = spread_ref.shape
    gather_total(mine_ref, other_ref, total_ref)
    value = eigval_ref[...]
    lowest = jnp.min(value, axis=1, keepdims=True)
    scaled = (1.0 - lowest / value) / value
    mixed_high, mixed_low = two(total_ref[:rank].T * (0.25 * scaled))
    spread_high, spread_low = two(spread_ref[...])
    turned = dot(mixed_high, spread_high, NN) + (
        dot(mixed_high, spread_low, NN) + dot(mixed_low, spread_high, NN)
    )
    high_ref[...], low_ref[...] = two(turned - pick_rows(index_ref, count, start, F32, 0.25))
    write_rows(0, rank, total_ref, targets_ref, weights_ref, high_ref, low_ref, new_hbm, out_hbm, new_ref, sems)


def update(mine, other, targets, batch_index, eigval, spread, weights):
    classes, count = weights.shape
    padded, half = mine.shape
    rows = 2 * half
    rank = spread.shape[0]
    here = padded - rank
    vmem = pl.BlockSpec(memory_space=pltpu.VMEM)
    hbm = pl.BlockSpec(memory_space=pl.ANY)
    right = jax.ShapeDtypeStruct((rows, count), BF16)
    return pl.pallas_call(
        update_body,
        in_specs=[vmem] * 7,
        out_specs=[hbm, hbm, vmem, vmem],
        out_shape=[
            jax.ShapeDtypeStruct((classes, count), F32),
            jax.ShapeDtypeStruct((classes, rows), F32),
            right,
            right,
        ],
        scratch_shapes=[
            pltpu.VMEM((padded, rows), F32),
            pltpu.VMEM((here, count), F32),
            pltpu.SemaphoreType.DMA((4,)),
        ],
        compiler_params=params(),
        cost_estimate=pl.CostEstimate(
            flops=6 * rows * count * (here + rank), bytes_accessed=8 * here * (count + rows), transcendentals=0
        ),
        name="update",
    )(mine, other, targets, batch_index, eigval, spread, weights)


def update_more_body(
    begin, mine_ref, other_ref, targets_ref, weights_ref, high_ref, low_ref, new_in, out_in,
    new_hbm, out_hbm, total_ref, new_ref, sems,
):
    gather_total(mine_ref, other_ref, total_ref)
    write_rows(begin, 0, total_ref, targets_ref, weights_ref, high_ref, low_ref, new_hbm, out_hbm, new_ref, sems)


def update_more(mine, other, targets, weights, high, low, new, out, begin):
    classes, count = weights.shape
    padded, half = mine.shape
    rows = 2 * half
    here = classes - begin
    vmem = pl.BlockSpec(memory_space=pltpu.VMEM)
    hbm = pl.BlockSpec(memory_space=pl.ANY)
    return pl.pallas_call(
        functools.partial(update_more_body, begin),
        in_specs=[vmem] * 6 + [hbm] * 2,
        out_specs=[hbm, hbm],
        out_shape=[
            jax.ShapeDtypeStruct((classes, count), F32),
            jax.ShapeDtypeStruct((classes, rows), F32),
        ],
        input_output_aliases={6: 0, 7: 1},
        scratch_shapes=[
            pltpu.VMEM((padded, rows), F32),
            pltpu.VMEM((here, count), F32),
            pltpu.SemaphoreType.DMA((6,)),
        ],
        compiler_params=params(),
        cost_estimate=pl.CostEstimate(
            flops=6 * rows * count * here, bytes_accessed=8 * here * (count + rows), transcendentals=0
        ),
        name="update_more",
    )(mine, other, targets, weights, high, low, new, out)


def swap(x, chips, level):
    bits = chips.bit_length() - 1
    flip = [1, 1] if level < 0 else [2 << walk(sub, bits)[level] for sub in range(2)]
    return lax.ppermute(x, AXES, [(i, i ^ flip[i & 1]) for i in range(2 * chips)])


def total_of(keep, send, chips, tied=()):
    keep = keep + swap(send, chips, -1)
    for level in range(chips.bit_length() - 1):
        if level >= HALVINGS:
            keep = keep + swap(keep, chips, level)
            continue
        half = keep.shape[0] // 2
        keep, send = keep[:half], keep[half:]
        if level == 1 and tied:
            send, *tied = lax.optimization_barrier((send, *tied))
        keep = keep + swap(send, chips, level)
    for level in reversed(range(HALVINGS)):
        keep = jnp.concatenate([keep, swap(keep, chips, level)])
    return [keep, swap(keep, chips, -1), *tied]


def on_device(chips, centers, weights, targets, batch_index, nys_index, eigvec, eigval):
    rows = batch_index.shape[0]
    classes = weights.shape[1]
    rank = eigvec.shape[1]
    unit = 8 * CHUNKS
    units = -(-(classes + rank) // unit)
    first = (units + 1) // 2 * unit
    second = units * unit - first
    begin = first - rank
    batch_index = batch_index.reshape(1, rows)
    weights = weights.T
    targets = targets.T
    picked = [pick_batch(batch_index, centers, part) for part in range(PARTS)]
    ready = [
        center_norms(centers),
        *spread_weights(nys_index.reshape(1, -1), eigvec.T, weights, first, second),
    ]
    mine, other, norms, high1, low1, high2, low2, spread = total_of(*picked[0], chips, ready)
    before = distances(mine, other, centers, norms)
    keep, send, value_high, value_low = predict(*total_of(*picked[1], chips), centers, before, high1, low1)
    one = total_of(keep, send, chips)
    another = total_of(*predict_more(high2, low2, value_high, value_low), chips)
    new, out, high, low = update(*one, targets, batch_index, eigval.reshape(1, rank), spread, weights)
    new, out = update_more(*another, targets, weights, high, low, new, out, begin)
    return new.T, out.T


def solution(mesh):
    return jax.shard_map(
        functools.partial(on_device, mesh.shape["center"]),
        mesh=mesh,
        in_specs=(
            P(("parts", "center", "sub"), None),
            P(("parts", "center", "sub"), None),
            P("parts", None),
            P("parts"),
            P(("parts", "center", "sub")),
            P(("parts", "center", "sub"), None),
            P("parts"),
        ),
        out_specs=(P(("parts", "center", "sub"), None), P("parts", None)),
        check_vma=False,
    )
```

time: 97.1 us -> 92.9 us (0.957)
  starting transfers between devices: 52.5 us -> 34.2 us
  waiting for transfers between devices: 22.4 us -> 38 us
  Pallas kernels: 17 us -> 15.5 us
    ppermute x32 -> x28, starting transfers between devices: 52.5 us -> 34.2 us  [swap(): lax.ppermute(x, AXES, [(i, i ^ flip[i & 1]) for i in range(2 * chips)])]
    ppermute x32 -> x28, waiting for transfers between devices: 22.4 us -> 38 us  [swap(): lax.ppermute(x, AXES, [(i, i ^ flip[i & 1]) for i in range(2 * chips)])]
    pallas_call x5, Pallas kernels: 9.72 us -> 8.17 us  [the longest x2 3.23 us: pick_batch(): pl.pallas_call(functools.partial(pick_body, part * depth), in_specs=[hbm,...]
    unnamed x20 -> x18, local copies, waits for them, and re-layouts: 3.06 us -> 3.05 us
  transfers between devices with their start and end apart: 32 -> 28, of which waited for: 16 -> 17; matrix products, arithmetic and copies ran while one was open for 1% -> 1% of each run, Pallas kernels for 10% -> 10%
where the time goes in v5:
time: 92.9 us; the launch traced here: 92.7 us
  waiting for transfers between devices  38 us (41%)
  starting transfers between devices  34.2 us (37%)
  Pallas kernels  15.5 us (17%)
  local copies, waits for them, and re-layouts  3.14 us (3%)
  between operations  1.17 us (1%)
    ppermute x28, waiting for transfers between devices, swap(): lax.ppermute(x, AXES, [(i, i ^ flip[i & 1]) for i in range(2 * chips)])  38 us
    ppermute x28, starting transfers between devices, swap(): lax.ppermute(x, AXES, [(i, i ^ flip[i & 1]) for i in range(2 * chips)])  34.2 us
    pallas_call x2, Pallas kernels, pick_batch(): pl.pallas_call(functools.partial(pick_body, part * depth), in_specs=[hbm,...  3.23 us
    pallas_call x1, Pallas kernels, predict(): pl.pallas_call(predict_body, in_specs=[vmem] * 6, out_specs=[vmem] * 4, o...  3.05 us
    unnamed x18, local copies, waits for them, and re-layouts  3.05 us
    pallas_call x1, Pallas kernels, update(): pl.pallas_call(update_body, in_specs=[vmem] * 7, out_specs=[hbm, hbm, vme...  2.45 us
    pallas_call x1, Pallas kernels, update_more(): pl.pallas_call(functools.partial(update_more_body, begin), in_specs=[vmem...  2 us
  transfers between devices with their start and end apart: 28, of which 17 were waited for; matrix products, arithmetic and copies ran while one was open for 1% of the time, Pallas kernels for 10%

profile of v5, /device:TPU:1, one launch (start us, length us, event | category | flops | bytes accessed | tf_op | source)
XLA Modules:
  0.0 92.7 jit_solution(10752005864474617804)
XLA Ops:
  0.6 0.0 copy-start
  0.6 2.3 %copy-done = bf16[768,3072]{1,0:T(8,128)(2,1)S(1)} copy-done((bf16[768,3072]{1,0:T(8,128)(2,1)S(1)}, bf16[768,3072]{1,0:T(8,128)(2,1)}, u32[]{:S(2)}) %copy-start) | copy-done | bytes 4718616
  3.0 0.7 copy-done.5
  3.6 1.6 %pick_batch.2 = (bf16[128,1536]{1,0:T(8,128)(2,1)S(1)}, bf16[128,1536]{1,0:T(8,128)(2,1)S(1)}) custom-call(s32[1,256]{1,0:T(1,128)S(1)} %bitcast.13, bf16[768,3072]{1,0:T(8,128)(2,1)S(1)} %copy-done), custom_call_target="tpu_custom_call" | custom-call | flops 603979776 | bytes 3145728 | tf_op jit(solution)/shard_map/pick_batch/pallas_call | solution.py:101
  5.3 0.0 copy-start.8
  5.3 0.0 copy-start.1
  5.3 0.1 collective-permute-start
  5.4 1.6 %pick_batch.3 = (bf16[128,1536]{1,0:T(8,128)(2,1)S(1)}, bf16[128,1536]{1,0:T(8,128)(2,1)S(1)}) custom-call(s32[1,256]{1,0:T(1,128)S(1)} %bitcast.14, bf16[768,3072]{1,0:T(8,128)(2,1)S(1)} %copy-done), custom_call_target="tpu_custom_call" | custom-call | flops 603979776 | bytes 3145728 | tf_op jit(solution)/shard_map/pick_batch/pallas_call | solution.py:101
  7.0 0.5 collective-permute-start.2
  7.6 0.1 add.48
  7.7 2.4 %collective-permute-start.1 = (bf16[64,1536]{1,0:T(8,128)(2,1)S(1)}, bf16[64,1536]{1,0:T(8,128)(2,1)S(1)}, u32[]{:S(2)}, u32[]{:S(2)}) collective-permute-start(bf16[64,1536]{1,0:T(8,128)(2,1)S(1)} %slice.65), channel_id=1, source_target_pairs={{0,2},{1,5},{2,0},{3,7},{4,6},{5,1},{6,4},{7,3},{8,10},{9,13},{10,... | collective-permute-start | bytes 589832 | tf_op jit(solution)/shard_map/ppermute | solution.py:437
  10.1 1.3 %center_norms.1.norm_ref = f32[768,128]{1,0:T(8,128)S(1)} custom-call(bf16[768,3072]{1,0:T(8,128)(2,1)S(1)} %copy-done.1), custom_call_target="tpu_custom_call" | custom-call | flops 4718592 | bytes 4718592 | tf_op jit(solution)/shard_map/center_norms/pallas_call | solution.py:173
  11.4 1.6 %spread_weights.1 = (bf16[608,768]{1,0:T(8,128)(2,1)S(1)}, bf16[608,768]{1,0:T(8,128)(2,1)S(1)}, bf16[576,768]{1,0:T(8,128)(2,1)S(1)}, bf16[576,768]{1,0:T(8,128)(2,1)S(1)}, f32[160,768]{1,0:T(8,128)S(1)}) custom-call(s32[1,320]{1,0:T(1,128)S(1)} %reshape.14.index_ref, f32[160,320]{1,0:T(8,128)S(1)} %bitcast.12, f32[1000,768]{1,0:T(8,128)S(1)} %bitcast.7), custom_call_target="tpu_custom_call" | custom-call | flops 235929600 | bytes 7274496 | tf_op jit(solution)/shard_map/spread_weights/pallas_call | solution.py:146
  13.0 0.1 add.50
  13.2 0.4 collective-permute-start.3
  13.6 2.4 %collective-permute-start.9 = (bf16[32,1536]{1,0:T(8,128)(2,1)S(1)}, bf16[32,1536]{1,0:T(8,128)(2,1)S(1)}, u32[]{:S(2)}, u32[]{:S(2)}) collective-permute-start(bf16[32,1536]{1,0:T(8,128)(2,1)S(1)} %slice.66), channel_id=1, source_target_pairs={{0,4},{1,9},{2,6},{3,11},{4,0},{5,13},{6,2},{7,15},{8,12},{9,1},{1... | collective-permute-start | bytes 294920 | tf_op jit(solution)/shard_map/ppermute | solution.py:437
  16.0 3.7 %collective-permute-done.3 = bf16[64,1536]{1,0:T(8,128)(2,1)S(1)} collective-permute-done((bf16[64,1536]{1,0:T(8,128)(2,1)S(1)}, bf16[64,1536]{1,0:T(8,128)(2,1)S(1)}, u32[]{:S(2)}, u32[]{:S(2)}) %collective-permute-start.3) | collective-permute-done | bytes 196640 | tf_op jit(solution)/shard_map/ppermute | solution.py:437
  19.7 0.7 collective-permute-start.4
  20.5 1.3 %collective-permute-start.10 = (bf16[32,1536]{1,0:T(8,128)(2,1)S(1)}, bf16[32,1536]{1,0:T(8,128)(2,1)S(1)}, u32[]{:S(2)}, u32[]{:S(2)}) collective-permute-start(bf16[32,1536]{1,0:T(8,128)(2,1)S(1)} %slice_add_fusion.4), channel_id=1, source_target_pairs={{0,8},{1,3},{2,10},{3,1},{4,12},{5,7},{6,14},{7,5},{8,0},{9,11},{1... | collective-permute-start | bytes 294920 | tf_op jit(solution)/shard_map/ppermute | solution.py:437
  21.8 2.5 %collective-permute-done.4 = bf16[32,1536]{1,0:T(8,128)(2,1)S(1)} collective-permute-done((bf16[32,1536]{1,0:T(8,128)(2,1)S(1)}, bf16[32,1536]{1,0:T(8,128)(2,1)S(1)}, u32[]{:S(2)}, u32[]{:S(2)}) %collective-permute-start.4) | collective-permute-done | bytes 98336 | tf_op jit(solution)/shard_map/ppermute | solution.py:437
  24.3 1.2 %collective-permute-start.5 = (bf16[32,1536]{1,0:T(8,128)(2,1)S(1)}, bf16[32,1536]{1,0:T(8,128)(2,1)S(1)}, u32[]{:S(2)}, u32[]{:S(2)}) collective-permute-start(bf16[32,1536]{1,0:T(8,128)(2,1)S(1)} %slice_add_fusion.5), channel_id=1, source_target_pairs={{0,8},{1,3},{2,10},{3,1},{4,12},{5,7},{6,14},{7,5},{8,0},{9,11},{1... | collective-permute-start | bytes 294920 | tf_op jit(solution)/shard_map/ppermute | solution.py:437
  25.5 1.8 %collective-permute-start.11 = (bf16[32,1536]{1,0:T(8,128)(2,1)S(1)}, bf16[32,1536]{1,0:T(8,128)(2,1)S(1)}, u32[]{:S(2)}, u32[]{:S(2)}) collective-permute-start(bf16[32,1536]{1,0:T(8,128)(2,1)S(1)} %add.55), channel_id=1, source_target_pairs={{0,4},{1,9},{2,6},{3,11},{4,0},{5,13},{6,2},{7,15},{8,12},{9,1},{1... | collective-permute-start | bytes 294920 | tf_op jit(solution)/shard_map/ppermute | solution.py:437
  27.3 0.6 collective-permute-done.5
  27.9 1.4 %collective-permute-start.6 = (bf16[32,1536]{1,0:T(8,128)(2,1)S(1)}, bf16[32,1536]{1,0:T(8,128)(2,1)S(1)}, u32[]{:S(2)}, u32[]{:S(2)}) collective-permute-start(bf16[32,1536]{1,0:T(8,128)(2,1)S(1)} %add.53), channel_id=1, source_target_pairs={{0,4},{1,9},{2,6},{3,11},{4,0},{5,13},{6,2},{7,15},{8,12},{9,1},{1... | collective-permute-start | bytes 294920 | tf_op jit(solution)/shard_map/ppermute | solution.py:437
  29.3 4.9 %collective-permute-done.11 = bf16[32,1536]{1,0:T(8,128)(2,1)S(1)} collective-permute-done((bf16[32,1536]{1,0:T(8,128)(2,1)S(1)}, bf16[32,1536]{1,0:T(8,128)(2,1)S(1)}, u32[]{:S(2)}, u32[]{:S(2)}) %collective-permute-start.11) | collective-permute-done | bytes 98336 | tf_op jit(solution)/shard_map/ppermute | solution.py:437
  34.2 0.1 collective-permute-start.12
  34.3 0.7 collective-permute-done.6
  35.0 0.8 collective-permute-start.7
  35.8 4.3 %collective-permute-done.12 = bf16[64,1536]{1,0:T(8,128)(2,1)S(1)} collective-permute-done((bf16[64,1536]{1,0:T(8,128)(2,1)S(1)}, bf16[64,1536]{1,0:T(8,128)(2,1)S(1)}, u32[]{:S(2)}, u32[]{:S(2)}) %collective-permute-start.12) | collective-permute-done | bytes 196640 | tf_op jit(solution)/shard_map/ppermute | solution.py:437
  40.2 0.5 collective-permute-start.13
  40.7 1.2 %collective-permute-done.7 = bf16[64,1536]{1,0:T(8,128)(2,1)S(1)} collective-permute-done((bf16[64,1536]{1,0:T(8,128)(2,1)S(1)}, bf16[64,1536]{1,0:T(8,128)(2,1)S(1)}, u32[]{:S(2)}, u32[]{:S(2)}) %collective-permute-start.7) | collective-permute-done | bytes 196640 | tf_op jit(solution)/shard_map/ppermute | solution.py:437
  42.0 4.3 %collective-permute-start.8 = (bf16[128,1536]{1,0:T(8,128)(2,1)S(1)}, bf16[128,1536]{1,0:T(8,128)(2,1)S(1)}, u32[]{:S(2)}, u32[]{:S(2)}) collective-permute-start(bf16[128,1536]{1,0:T(8,128)(2,1)S(1)} %pad_maximum_fusion.mine_ref), channel_id=1, source_target_pairs={{0,1},{1,0},{2,3},{3,2},{4,5},{5,4},{6,7},{7,6},{8,9},{9,8},{10,11... | collective-permute-start | bytes 1179656 | tf_op jit(solution)/shard_map/ppermute | solution.py:437
  46.3 1.0 %distances.1.before_ref = f32[768,256]{1,0:T(8,128)S(1)} custom-call(bf16[128,1536]{1,0:T(8,128)(2,1)S(1)} %pad_maximum_fusion.1.mine_ref, bf16[128,1536]{1,0:T(8,128)(2,1)S(1)} %collective-permute-done.13.other_ref, bf16[768,3072]{1,0:T(8,128)(2,1)S(1)} %copy-done.1, f32[768,128]{1,0:T(8,128)S(1)} %center_norms.1.norm_ref), custom_call_target="tpu_custom_call" | custom-call | flops 603979776 | bytes 3145728 | tf_op jit(solution)/shard_map/distances/pallas_call | solution.py:244
  47.3 0.4 collective-permute-done.8.other_ref
  47.6 3.1 %predict.1 = (f32[608,128]{1,0:T(8,128)S(1)}, f32[608,128]{1,0:T(8,128)S(1)}, bf16[768,256]{1,0:T(8,128)(2,1)S(1)}, bf16[768,256]{1,0:T(8,128)(2,1)S(1)}) custom-call(bf16[128,1536]{1,0:T(8,128)(2,1)S(1)} %pad_maximum_fusion.mine_ref, bf16[128,1536]{1,0:T(8,128)(2,1)S(1)} %collective-permute-done.8.other_ref, bf16[768,3072]{1,0:T(8,128)(2,1)S(1)} %copy-done.1, ...), custom_call_target="tpu_custom_call" | custom-call | flops 1321205760 | bytes 5636096 | tf_op jit(solution)/shard_map/predict/pallas_call | solution.py:266
  50.7 0.4 collective-permute-start.21
  51.1 1.2 %collective-permute-done.21 = f32[608,128]{1,0:T(8,128)S(1)} collective-permute-done((f32[608,128]{1,0:T(8,128)S(1)}, f32[608,128]{1,0:T(8,128)S(1)}, u32[]{:S(2)}, u32[]{:S(2)}) %collective-permute-start.21) | collective-permute-done | bytes 311328 | tf_op jit(solution)/shard_map/ppermute | solution.py:437
  52.4 0.1 collective-permute-start.22
  52.5 0.9 predict_more.1
  53.4 0.0 copy-start.3
  53.4 0.0 copy-start.6
  53.4 0.0 copy-start.7
  53.4 0.4 collective-permute-start.14
  53.9 3.0 %collective-permute-done.22 = f32[304,128]{1,0:T(8,128)S(1)} collective-permute-done((f32[304,128]{1,0:T(8,128)S(1)}, f32[304,128]{1,0:T(8,128)S(1)}, u32[]{:S(2)}, u32[]{:S(2)}) %collective-permute-start.22) | collective-permute-done | bytes 155680 | tf_op jit(solution)/shard_map/ppermute | solution.py:437
  56.9 1.6 %collective-permute-start.23 = (f32[152,128]{1,0:T(8,128)S(1)}, f32[152,128]{1,0:T(8,128)S(1)}, u32[]{:S(2)}, u32[]{:S(2)}) collective-permute-start(f32[152,128]{1,0:T(8,128)S(1)} %slice.79), channel_id=1, source_target_pairs={{0,4},{1,9},{2,6},{3,11},{4,0},{5,13},{6,2},{7,15},{8,12},{9,1},{1... | collective-permute-start | bytes 233480 | tf_op jit(solution)/shard_map/ppermute | solution.py:437
  58.6 1.5 %collective-permute-start.15 = (f32[288,128]{1,0:T(8,128)S(1)}, f32[288,128]{1,0:T(8,128)S(1)}, u32[]{:S(2)}, u32[]{:S(2)}) collective-permute-start(f32[288,128]{1,0:T(8,128)S(1)} %slice.73), channel_id=1, source_target_pairs={{0,2},{1,5},{2,0},{3,7},{4,6},{5,1},{6,4},{7,3},{8,10},{9,13},{10,... | collective-permute-start | bytes 442376 | tf_op jit(solution)/shard_map/ppermute | solution.py:437
  60.1 2.0 %collective-permute-done.23 = f32[152,128]{1,0:T(8,128)S(1)} collective-permute-done((f32[152,128]{1,0:T(8,128)S(1)}, f32[152,128]{1,0:T(8,128)S(1)}, u32[]{:S(2)}, u32[]{:S(2)}) %collective-permute-start.23) | collective-permute-done | bytes 77856 | tf_op jit(solution)/shard_map/ppermute | solution.py:437
  62.1 0.1 collective-permute-start.24
  62.1 1.7 %collective-permute-done.15 = f32[288,128]{1,0:T(8,128)S(1)} collective-permute-done((f32[288,128]{1,0:T(8,128)S(1)}, f32[288,128]{1,0:T(8,128)S(1)}, u32[]{:S(2)}, u32[]{:S(2)}) %collective-permute-start.15) | collective-permute-done | bytes 147488 | tf_op jit(solution)/shard_map/ppermute | solution.py:437
  63.9 0.5 collective-permute-start.16
  64.4 1.0 %collective-permute-done.24 = f32[152,128]{1,0:T(8,128)S(1)} collective-permute-done((f32[152,128]{1,0:T(8,128)S(1)}, f32[152,128]{1,0:T(8,128)S(1)}, u32[]{:S(2)}, u32[]{:S(2)}) %collective-permute-start.24) | collective-permute-done | bytes 77856 | tf_op jit(solution)/shard_map/ppermute | solution.py:437
  65.4 1.6 %collective-permute-start.25 = (f32[152,128]{1,0:T(8,128)S(1)}, f32[152,128]{1,0:T(8,128)S(1)}, u32[]{:S(2)}, u32[]{:S(2)}) collective-permute-start(f32[152,128]{1,0:T(8,128)S(1)} %add.63), channel_id=1, source_target_pairs={{0,4},{1,9},{2,6},{3,11},{4,0},{5,13},{6,2},{7,15},{8,12},{9,1},{1... | collective-permute-start | bytes 233480 | tf_op jit(solution)/shard_map/ppermute | solution.py:437
  67.0 4.3 %collective-permute-done.16 = f32[144,128]{1,0:T(8,128)S(1)} collective-permute-done((f32[144,128]{1,0:T(8,128)S(1)}, f32[144,128]{1,0:T(8,128)S(1)}, u32[]{:S(2)}, u32[]{:S(2)}) %collective-permute-start.16) | collective-permute-done | bytes 73760 | tf_op jit(solution)/shard_map/ppermute | solution.py:437
  71.3 0.1 collective-permute-start.17
  71.4 3.2 %collective-permute-done.17 = f32[144,128]{1,0:T(8,128)S(1)} collective-permute-done((f32[144,128]{1,0:T(8,128)S(1)}, f32[144,128]{1,0:T(8,128)S(1)}, u32[]{:S(2)}, u32[]{:S(2)}) %collective-permute-start.17) | collective-permute-done | bytes 73760 | tf_op jit(solution)/shard_map/ppermute | solution.py:437
  74.6 0.1 collective-permute-start.18
  74.7 1.8 %collective-permute-start.26 = (f32[304,128]{1,0:T(8,128)S(1)}, f32[304,128]{1,0:T(8,128)S(1)}, u32[]{:S(2)}, u32[]{:S(2)}) collective-permute-start(f32[304,128]{1,0:T(8,128)S(1)} %pad_maximum_fusion.6), channel_id=1, source_target_pairs={{0,2},{1,5},{2,0},{3,7},{4,6},{5,1},{6,4},{7,3},{8,10},{9,13},{10,... | collective-permute-start | bytes 466952 | tf_op jit(solution)/shard_map/ppermute | solution.py:437
  76.6 3.1 %collective-permute-done.18 = f32[144,128]{1,0:T(8,128)S(1)} collective-permute-done((f32[144,128]{1,0:T(8,128)S(1)}, f32[144,128]{1,0:T(8,128)S(1)}, u32[]{:S(2)}, u32[]{:S(2)}) %collective-permute-start.18) | collective-permute-done | bytes 73760 | tf_op jit(solution)/shard_map/ppermute | solution.py:437
  79.6 0.1 collective-permute-start.19
  79.7 0.3 collective-permute-done.26
  80.0 5.5 %collective-permute-start.27 = (f32[608,128]{1,0:T(8,128)S(1)}, f32[608,128]{1,0:T(8,128)S(1)}, u32[]{:S(2)}, u32[]{:S(2)}) collective-permute-start(f32[608,128]{1,0:T(8,128)S(1)} %pad_maximum_fusion.2.mine_ref), channel_id=1, source_target_pairs={{0,1},{1,0},{2,3},{3,2},{4,5},{5,4},{6,7},{7,6},{8,9},{9,8},{10,11... | collective-permute-start | bytes 933896 | tf_op jit(solution)/shard_map/ppermute | solution.py:437
  85.6 2.5 %collective-permute-start.20 = (f32[576,128]{1,0:T(8,128)S(1)}, f32[576,128]{1,0:T(8,128)S(1)}, u32[]{:S(2)}, u32[]{:S(2)}) collective-permute-start(f32[576,128]{1,0:T(8,128)S(1)} %pad_maximum_fusion.3.mine_ref), channel_id=1, source_target_pairs={{0,1},{1,0},{2,3},{3,2},{4,5},{5,4},{6,7},{7,6},{8,9},{9,8},{10,11... | collective-permute-start | bytes 884744 | tf_op jit(solution)/shard_map/ppermute | solution.py:437
  88.1 2.4 %update.1 = (f32[1000,768]{1,0:T(8,128)}, f32[1000,256]{1,0:T(8,128)}, bf16[256,768]{1,0:T(8,128)(2,1)S(1)}, bf16[256,768]{1,0:T(8,128)(2,1)S(1)}) custom-call(f32[608,128]{1,0:T(8,128)S(1)} %pad_maximum_fusion.2.mine_ref, f32[608,128]{1,0:T(8,128)S(1)} %collective-permute-done.27.other_ref, f32[1000,256]{1,0:T(8,128)S(1)} %bitcast.10, ...), custom_call_target="tpu_custom_call" | custom-call | flops 717225984 | bytes 3670016 | tf_op jit(solution)/shard_map/update/pallas_call | solution.py:374
  90.5 2.0 %update_more.1 = (f32[1000,768]{1,0:T(8,128)}, f32[1000,256]{1,0:T(8,128)}) custom-call(f32[576,128]{1,0:T(8,128)S(1)} %pad_maximum_fusion.3.mine_ref, f32[576,128]{1,0:T(8,128)S(1)} %collective-permute-done.20.other_ref, f32[1000,256]{1,0:T(8,128)S(1)} %bitcast.11, f32[1000,768]{1,0:T(8,128)S(1)} %bitcast.9, ...), custom_call_target="tpu_custom_call", output_to_operand_aliasing={{0}: (6, {}), {1}: (7, {})} | custom-call | flops 651165696 | bytes 4521984 | tf_op jit(solution)/shard_map/update_more/pallas_call | solution.py:412
  (52 shorter events, 0.6 us)
Async XLA Ops:
  0.6 2.3 %copy-start = (bf16[768,3072]{1,0:T(8,128)(2,1)S(1)}, bf16[768,3072]{1,0:T(8,128)(2,1)}, u32[]{:S(2)}) copy-start(bf16[768,3072]{1,0:T(8,128)(2,1)} %centers_ref.5) | copy-start | bytes 14155780
  3.0 0.7 copy-start.5
  5.3 4.8 %copy-start.8 = (s32[320]{0:T(512)S(1)}, s32[320]{0:T(512)}, u32[]{:S(2)}) copy-start(s32[320]{0:T(512)} %param.11) | copy-start | bytes 3844
  5.3 4.8 %copy-start.1 = (bf16[768,3072]{1,0:T(8,128)(2,1)S(1)}, bf16[768,3072]{1,0:T(8,128)(2,1)}, u32[]{:S(2)}) copy-start(bf16[768,3072]{1,0:T(8,128)(2,1)} %centers_ref.5) | copy-start | bytes 14155780
  5.3 2.3 %collective-permute-start = (bf16[128,1536]{1,0:T(8,128)(2,1)S(1)}, bf16[128,1536]{1,0:T(8,128)(2,1)S(1)}, u32[]{:S(2)}, u32[]{:S(2)}) collective-permute-start(bf16[128,1536]{1,0:T(8,128)(2,1)S(1)} %get-tuple-element.31), channel_id=1, source_target_pairs={{0,1},{1,0},{2,3},{3,2},{4,5},{5,4},{6,7},{7,6},{8,9},{9,8},{10,11... | collective-permute-start | bytes 1179656 | tf_op jit(solution)/shard_map/ppermute | solution.py:437
  7.0 6.0 %collective-permute-start.2 = (bf16[128,1536]{1,0:T(8,128)(2,1)S(1)}, bf16[128,1536]{1,0:T(8,128)(2,1)S(1)}, u32[]{:S(2)}, u32[]{:S(2)}) collective-permute-start(bf16[128,1536]{1,0:T(8,128)(2,1)S(1)} %get-tuple-element.40), channel_id=1, source_target_pairs={{0,1},{1,0},{2,3},{3,2},{4,5},{5,4},{6,7},{7,6},{8,9},{9,8},{10,11... | collective-permute-start | bytes 1179656 | tf_op jit(solution)/shard_map/ppermute | solution.py:437
  7.6 3.8 %copy-start.2 = (f32[768,1000]{0,1:T(8,128)S(1)}, f32[768,1000]{0,1:T(8,128)}, u32[]{:S(2)}) copy-start(f32[768,1000]{0,1:T(8,128)} %param.8) | copy-start | bytes 9216004
  7.6 3.8 %copy-start.4 = (f32[320,160]{0,1:T(8,128)S(1)}, f32[320,160]{0,1:T(8,128)}, u32[]{:S(2)}) copy-start(f32[320,160]{0,1:T(8,128)} %param.12) | copy-start | bytes 614404
  7.7 5.9 %collective-permute-start.1 = (bf16[64,1536]{1,0:T(8,128)(2,1)S(1)}, bf16[64,1536]{1,0:T(8,128)(2,1)S(1)}, u32[]{:S(2)}, u32[]{:S(2)}) collective-permute-start(bf16[64,1536]{1,0:T(8,128)(2,1)S(1)} %slice.65), channel_id=1, source_target_pairs={{0,2},{1,5},{2,0},{3,7},{4,6},{5,1},{6,4},{7,3},{8,10},{9,13},{10,... | collective-permute-start | bytes 589832 | tf_op jit(solution)/shard_map/ppermute | solution.py:437
  13.2 6.5 %collective-permute-start.3 = (bf16[64,1536]{1,0:T(8,128)(2,1)S(1)}, bf16[64,1536]{1,0:T(8,128)(2,1)S(1)}, u32[]{:S(2)}, u32[]{:S(2)}) collective-permute-start(bf16[64,1536]{1,0:T(8,128)(2,1)S(1)} %slice.68), channel_id=1, source_target_pairs={{0,2},{1,5},{2,0},{3,7},{4,6},{5,1},{6,4},{7,3},{8,10},{9,13},{10,... | collective-permute-start | bytes 589832 | tf_op jit(solution)/shard_map/ppermute | solution.py:437
  13.6 6.9 %collective-permute-start.9 = (bf16[32,1536]{1,0:T(8,128)(2,1)S(1)}, bf16[32,1536]{1,0:T(8,128)(2,1)S(1)}, u32[]{:S(2)}, u32[]{:S(2)}) collective-permute-start(bf16[32,1536]{1,0:T(8,128)(2,1)S(1)} %slice.66), channel_id=1, source_target_pairs={{0,4},{1,9},{2,6},{3,11},{4,0},{5,13},{6,2},{7,15},{8,12},{9,1},{1... | collective-permute-start | bytes 294920 | tf_op jit(solution)/shard_map/ppermute | solution.py:437
  19.7 4.6 %collective-permute-start.4 = (bf16[32,1536]{1,0:T(8,128)(2,1)S(1)}, bf16[32,1536]{1,0:T(8,128)(2,1)S(1)}, u32[]{:S(2)}, u32[]{:S(2)}) collective-permute-start(bf16[32,1536]{1,0:T(8,128)(2,1)S(1)} %slice.70), channel_id=1, source_target_pairs={{0,4},{1,9},{2,6},{3,11},{4,0},{5,13},{6,2},{7,15},{8,12},{9,1},{1... | collective-permute-start | bytes 294920 | tf_op jit(solution)/shard_map/ppermute | solution.py:437
  20.5 5.0 %collective-permute-start.10 = (bf16[32,1536]{1,0:T(8,128)(2,1)S(1)}, bf16[32,1536]{1,0:T(8,128)(2,1)S(1)}, u32[]{:S(2)}, u32[]{:S(2)}) collective-permute-start(bf16[32,1536]{1,0:T(8,128)(2,1)S(1)} %slice_add_fusion.4), channel_id=1, source_target_pairs={{0,8},{1,3},{2,10},{3,1},{4,12},{5,7},{6,14},{7,5},{8,0},{9,11},{1... | collective-permute-start | bytes 294920 | tf_op jit(solution)/shard_map/ppermute | solution.py:437
  24.3 3.5 %collective-permute-start.5 = (bf16[32,1536]{1,0:T(8,128)(2,1)S(1)}, bf16[32,1536]{1,0:T(8,128)(2,1)S(1)}, u32[]{:S(2)}, u32[]{:S(2)}) collective-permute-start(bf16[32,1536]{1,0:T(8,128)(2,1)S(1)} %slice_add_fusion.5), channel_id=1, source_target_pairs={{0,8},{1,3},{2,10},{3,1},{4,12},{5,7},{6,14},{7,5},{8,0},{9,11},{1... | collective-permute-start | bytes 294920 | tf_op jit(solution)/shard_map/ppermute | solution.py:437
  25.5 8.7 %collective-permute-start.11 = (bf16[32,1536]{1,0:T(8,128)(2,1)S(1)}, bf16[32,1536]{1,0:T(8,128)(2,1)S(1)}, u32[]{:S(2)}, u32[]{:S(2)}) collective-permute-start(bf16[32,1536]{1,0:T(8,128)(2,1)S(1)} %add.55), channel_id=1, source_target_pairs={{0,4},{1,9},{2,6},{3,11},{4,0},{5,13},{6,2},{7,15},{8,12},{9,1},{1... | collective-permute-start | bytes 294920 | tf_op jit(solution)/shard_map/ppermute | solution.py:437
  27.9 7.1 %collective-permute-start.6 = (bf16[32,1536]{1,0:T(8,128)(2,1)S(1)}, bf16[32,1536]{1,0:T(8,128)(2,1)S(1)}, u32[]{:S(2)}, u32[]{:S(2)}) collective-permute-start(bf16[32,1536]{1,0:T(8,128)(2,1)S(1)} %add.53), channel_id=1, source_target_pairs={{0,4},{1,9},{2,6},{3,11},{4,0},{5,13},{6,2},{7,15},{8,12},{9,1},{1... | collective-permute-start | bytes 294920 | tf_op jit(solution)/shard_map/ppermute | solution.py:437
  34.2 5.9 %collective-permute-start.12 = (bf16[64,1536]{1,0:T(8,128)(2,1)S(1)}, bf16[64,1536]{1,0:T(8,128)(2,1)S(1)}, u32[]{:S(2)}, u32[]{:S(2)}) collective-permute-start(bf16[64,1536]{1,0:T(8,128)(2,1)S(1)} %pad_maximum_fusion.5), channel_id=1, source_target_pairs={{0,2},{1,5},{2,0},{3,7},{4,6},{5,1},{6,4},{7,3},{8,10},{9,13},{10,... | collective-permute-start | bytes 589832 | tf_op jit(solution)/shard_map/ppermute | solution.py:437
  35.0 6.9 %collective-permute-start.7 = (bf16[64,1536]{1,0:T(8,128)(2,1)S(1)}, bf16[64,1536]{1,0:T(8,128)(2,1)S(1)}, u32[]{:S(2)}, u32[]{:S(2)}) collective-permute-start(bf16[64,1536]{1,0:T(8,128)(2,1)S(1)} %pad_maximum_fusion.4), channel_id=1, source_target_pairs={{0,2},{1,5},{2,0},{3,7},{4,6},{5,1},{6,4},{7,3},{8,10},{9,13},{10,... | collective-permute-start | bytes 589832 | tf_op jit(solution)/shard_map/ppermute | solution.py:437
  40.2 6.1 %collective-permute-start.13 = (bf16[128,1536]{1,0:T(8,128)(2,1)S(1)}, bf16[128,1536]{1,0:T(8,128)(2,1)S(1)}, u32[]{:S(2)}, u32[]{:S(2)}) collective-permute-start(bf16[128,1536]{1,0:T(8,128)(2,1)S(1)} %pad_maximum_fusion.1.mine_ref), channel_id=1, source_target_pairs={{0,1},{1,0},{2,3},{3,2},{4,5},{5,4},{6,7},{7,6},{8,9},{9,8},{10,11... | collective-permute-start | bytes 1179656 | tf_op jit(solution)/shard_map/ppermute | solution.py:437
  42.0 5.7 %collective-permute-start.8 = (bf16[128,1536]{1,0:T(8,128)(2,1)S(1)}, bf16[128,1536]{1,0:T(8,128)(2,1)S(1)}, u32[]{:S(2)}, u32[]{:S(2)}) collective-permute-start(bf16[128,1536]{1,0:T(8,128)(2,1)S(1)} %pad_maximum_fusion.mine_ref), channel_id=1, source_target_pairs={{0,1},{1,0},{2,3},{3,2},{4,5},{5,4},{6,7},{7,6},{8,9},{9,8},{10,11... | collective-permute-start | bytes 1179656 | tf_op jit(solution)/shard_map/ppermute | solution.py:437
  50.7 1.7 %collective-permute-start.21 = (f32[608,128]{1,0:T(8,128)S(1)}, f32[608,128]{1,0:T(8,128)S(1)}, u32[]{:S(2)}, u32[]{:S(2)}) collective-permute-start(f32[608,128]{1,0:T(8,128)S(1)} %get-tuple-element.50), channel_id=1, source_target_pairs={{0,1},{1,0},{2,3},{3,2},{4,5},{5,4},{6,7},{7,6},{8,9},{9,8},{10,11... | collective-permute-start | bytes 933896 | tf_op jit(solution)/shard_map/ppermute | solution.py:437
  52.4 4.4 %collective-permute-start.22 = (f32[304,128]{1,0:T(8,128)S(1)}, f32[304,128]{1,0:T(8,128)S(1)}, u32[]{:S(2)}, u32[]{:S(2)}) collective-permute-start(f32[304,128]{1,0:T(8,128)S(1)} %slice.77), channel_id=1, source_target_pairs={{0,2},{1,5},{2,0},{3,7},{4,6},{5,1},{6,4},{7,3},{8,10},{9,13},{10,... | collective-permute-start | bytes 466952 | tf_op jit(solution)/shard_map/ppermute | solution.py:437
  53.4 34.6 %copy-start.3 = (f32[256,1000]{0,1:T(8,128)S(1)}, f32[256,1000]{0,1:T(8,128)}, u32[]{:S(2)}) copy-start(f32[256,1000]{0,1:T(8,128)} %param.9) | copy-start | bytes 3072004
  53.4 34.6 %copy-start.6 = (s32[256]{0:T(256)S(1)}, s32[256]{0:T(256)}, u32[]{:S(2)}) copy-start(s32[256]{0:T(256)} %param.10) | copy-start | bytes 3076
  53.4 34.6 %copy-start.7 = (f32[160]{0:T(256)S(1)}, f32[160]{0:T(256)}, u32[]{:S(2)}) copy-start(f32[160]{0:T(256)} %param.13) | copy-start | bytes 1924
  53.4 5.1 %collective-permute-start.14 = (f32[576,128]{1,0:T(8,128)S(1)}, f32[576,128]{1,0:T(8,128)S(1)}, u32[]{:S(2)}, u32[]{:S(2)}) collective-permute-start(f32[576,128]{1,0:T(8,128)S(1)} %get-tuple-element.48), channel_id=1, source_target_pairs={{0,1},{1,0},{2,3},{3,2},{4,5},{5,4},{6,7},{7,6},{8,9},{9,8},{10,11... | collective-permute-start | bytes 884744 | tf_op jit(solution)/shard_map/ppermute | solution.py:437
  56.9 5.2 %collective-permute-start.23 = (f32[152,128]{1,0:T(8,128)S(1)}, f32[152,128]{1,0:T(8,128)S(1)}, u32[]{:S(2)}, u32[]{:S(2)}) collective-permute-start(f32[152,128]{1,0:T(8,128)S(1)} %slice.79), channel_id=1, source_target_pairs={{0,4},{1,9},{2,6},{3,11},{4,0},{5,13},{6,2},{7,15},{8,12},{9,1},{1... | collective-permute-start | bytes 233480 | tf_op jit(solution)/shard_map/ppermute | solution.py:437
  58.6 5.3 %collective-permute-start.15 = (f32[288,128]{1,0:T(8,128)S(1)}, f32[288,128]{1,0:T(8,128)S(1)}, u32[]{:S(2)}, u32[]{:S(2)}) collective-permute-start(f32[288,128]{1,0:T(8,128)S(1)} %slice.73), channel_id=1, source_target_pairs={{0,2},{1,5},{2,0},{3,7},{4,6},{5,1},{6,4},{7,3},{8,10},{9,13},{10,... | collective-permute-start | bytes 442376 | tf_op jit(solution)/shard_map/ppermute | solution.py:437
  62.1 3.3 %collective-permute-start.24 = (f32[152,128]{1,0:T(8,128)S(1)}, f32[152,128]{1,0:T(8,128)S(1)}, u32[]{:S(2)}, u32[]{:S(2)}) collective-permute-start(f32[152,128]{1,0:T(8,128)S(1)} %slice_add_fusion.6), channel_id=1, source_target_pairs={{0,8},{1,3},{2,10},{3,1},{4,12},{5,7},{6,14},{7,5},{8,0},{9,11},{1... | collective-permute-start | bytes 233480 | tf_op jit(solution)/shard_map/ppermute | solution.py:437
  63.9 7.5 %collective-permute-start.16 = (f32[144,128]{1,0:T(8,128)S(1)}, f32[144,128]{1,0:T(8,128)S(1)}, u32[]{:S(2)}, u32[]{:S(2)}) collective-permute-start(f32[144,128]{1,0:T(8,128)S(1)} %slice.75), channel_id=1, source_target_pairs={{0,4},{1,9},{2,6},{3,11},{4,0},{5,13},{6,2},{7,15},{8,12},{9,1},{1... | collective-permute-start | bytes 221192 | tf_op jit(solution)/shard_map/ppermute | solution.py:437
  65.4 9.3 %collective-permute-start.25 = (f32[152,128]{1,0:T(8,128)S(1)}, f32[152,128]{1,0:T(8,128)S(1)}, u32[]{:S(2)}, u32[]{:S(2)}) collective-permute-start(f32[152,128]{1,0:T(8,128)S(1)} %add.63), channel_id=1, source_target_pairs={{0,4},{1,9},{2,6},{3,11},{4,0},{5,13},{6,2},{7,15},{8,12},{9,1},{1... | collective-permute-start | bytes 233480 | tf_op jit(solution)/shard_map/ppermute | solution.py:437
  71.3 3.3 %collective-permute-start.17 = (f32[144,128]{1,0:T(8,128)S(1)}, f32[144,128]{1,0:T(8,128)S(1)}, u32[]{:S(2)}, u32[]{:S(2)}) collective-permute-start(f32[144,128]{1,0:T(8,128)S(1)} %slice_add_fusion.7), channel_id=1, source_target_pairs={{0,8},{1,3},{2,10},{3,1},{4,12},{5,7},{6,14},{7,5},{8,0},{9,11},{1... | collective-permute-start | bytes 221192 | tf_op jit(solution)/shard_map/ppermute | solution.py:437
  74.6 5.0 %collective-permute-start.18 = (f32[144,128]{1,0:T(8,128)S(1)}, f32[144,128]{1,0:T(8,128)S(1)}, u32[]{:S(2)}, u32[]{:S(2)}) collective-permute-start(f32[144,128]{1,0:T(8,128)S(1)} %add.59), channel_id=1, source_target_pairs={{0,4},{1,9},{2,6},{3,11},{4,0},{5,13},{6,2},{7,15},{8,12},{9,1},{1... | collective-permute-start | bytes 221192 | tf_op jit(solution)/shard_map/ppermute | solution.py:437
  74.7 5.2 %collective-permute-start.26 = (f32[304,128]{1,0:T(8,128)S(1)}, f32[304,128]{1,0:T(8,128)S(1)}, u32[]{:S(2)}, u32[]{:S(2)}) collective-permute-start(f32[304,128]{1,0:T(8,128)S(1)} %pad_maximum_fusion.6), channel_id=1, source_target_pairs={{0,2},{1,5},{2,0},{3,7},{4,6},{5,1},{6,4},{7,3},{8,10},{9,13},{10,... | collective-permute-start | bytes 466952 | tf_op jit(solution)/shard_map/ppermute | solution.py:437
  79.6 5.9 %collective-permute-start.19 = (f32[288,128]{1,0:T(8,128)S(1)}, f32[288,128]{1,0:T(8,128)S(1)}, u32[]{:S(2)}, u32[]{:S(2)}) collective-permute-start(f32[288,128]{1,0:T(8,128)S(1)} %pad_maximum_fusion.7), channel_id=1, source_target_pairs={{0,2},{1,5},{2,0},{3,7},{4,6},{5,1},{6,4},{7,3},{8,10},{9,13},{10,... | collective-permute-start | bytes 442376 | tf_op jit(solution)/shard_map/ppermute | solution.py:437
  80.0 8.1 %collective-permute-start.27 = (f32[608,128]{1,0:T(8,128)S(1)}, f32[608,128]{1,0:T(8,128)S(1)}, u32[]{:S(2)}, u32[]{:S(2)}) collective-permute-start(f32[608,128]{1,0:T(8,128)S(1)} %pad_maximum_fusion.2.mine_ref), channel_id=1, source_target_pairs={{0,1},{1,0},{2,3},{3,2},{4,5},{5,4},{6,7},{7,6},{8,9},{9,8},{10,11... | collective-permute-start | bytes 933896 | tf_op jit(solution)/shard_map/ppermute | solution.py:437
  85.6 5.0 %collective-permute-start.20 = (f32[576,128]{1,0:T(8,128)S(1)}, f32[576,128]{1,0:T(8,128)S(1)}, u32[]{:S(2)}, u32[]{:S(2)}) collective-permute-start(f32[576,128]{1,0:T(8,128)S(1)} %pad_maximum_fusion.3.mine_ref), channel_id=1, source_target_pairs={{0,1},{1,0},{2,3},{3,2},{4,5},{5,4},{6,7},{7,6},{8,9},{9,8},{10,11... | collective-permute-start | bytes 884744 | tf_op jit(solution)/shard_map/ppermute | solution.py:437

commit v6 on v5

--- a/solution.py
+++ b/solution.py
@@ -26,7 +26,7 @@
 
 def walk(sub, bits):
     order = list(range(bits))
-    return order if sub == 0 else order[1:3] + order[:1] + order[3:]
+    return order if sub == 0 else order[1::-1] + order[2:]
 
 
 def turns():
@@ -465,7 +465,8 @@
     batch_index = batch_index.reshape(1, rows)
     weights = weights.T
     targets = targets.T
-    picked = [pick_batch(batch_index, centers, part) for part in range(PARTS)]
+    far = [pltpu.with_memory_space_constraint(x, pltpu.HBM) for x in (batch_index, centers)]
+    picked = [pick_batch(*far, part) for part in range(PARTS)]
     ready = [
         center_norms(centers),
         *spread_weights(nys_index.reshape(1, -1), eigvec.T, weights, first, second),

time: 92.9 us -> 86.7 us (0.933)
  waiting for transfers between devices: 38 us -> 27.7 us
  starting transfers between devices: 34.2 us -> 40.3 us
  local copies, waits for them, and re-layouts: 3.14 us -> 0.13 us
  Pallas kernels: 15.5 us -> 16.9 us
    ppermute x28, waiting for transfers between devices: 38 us -> 27.7 us  [swap(): lax.ppermute(x, AXES, [(i, i ^ flip[i & 1]) for i in range(2 * chips)])]
    ppermute x28, starting transfers between devices: 34.2 us -> 40.3 us  [swap(): lax.ppermute(x, AXES, [(i, i ^ flip[i & 1]) for i in range(2 * chips)])]
    unnamed x18 -> x14, local copies, waits for them, and re-layouts: 3.05 us -> 0.04 us
    pallas_call x2, Pallas kernels: 3.23 us -> 4.74 us  [pick_batch(): pl.pallas_call(functools.partial(pick_body, part * depth), in_specs=[hbm,...]
  transfers between devices with their start and end apart: 28 -> 28, of which waited for: 17 -> 15; matrix products, arithmetic and copies ran while one was open for 1% -> 1% of each run, Pallas kernels for 10% -> 11%
where the time goes in v6:
time: 86.7 us; the launch traced here: 86.5 us
  starting transfers between devices  40.3 us (46%)
  waiting for transfers between devices  27.7 us (32%)
  Pallas kernels  16.9 us (19%)
  between operations  0.96 us (1%)
    ppermute x28, starting transfers between devices, swap(): lax.ppermute(x, AXES, [(i, i ^ flip[i & 1]) for i in range(2 * chips)])  40.3 us
    ppermute x28, waiting for transfers between devices, swap(): lax.ppermute(x, AXES, [(i, i ^ flip[i & 1]) for i in range(2 * chips)])  27.7 us
    pallas_call x2, Pallas kernels, pick_batch(): pl.pallas_call(functools.partial(pick_body, part * depth), in_specs=[hbm,...  4.74 us
    pallas_call x1, Pallas kernels, predict(): pl.pallas_call(predict_body, in_specs=[vmem] * 6, out_specs=[vmem] * 4, o...  3.06 us
    pallas_call x1, Pallas kernels, update(): pl.pallas_call(update_body, in_specs=[vmem] * 7, out_specs=[hbm, hbm, vme...  2.44 us
    pallas_call x1, Pallas kernels, update_more(): pl.pallas_call(functools.partial(update_more_body, begin), in_specs=[vmem...  2 us
  transfers between devices with their start and end apart: 28, of which 15 were waited for; matrix products, arithmetic and copies ran while one was open for 1% of the time, Pallas kernels for 11%

profile of v6, /device:TPU:1, one launch (start us, length us, event | category | flops | bytes accessed | tf_op | source)
XLA Modules:
  0.0 86.5 jit_solution(15575748033264495205)
XLA Ops:
  0.6 2.3 %pick_batch.2 = (bf16[128,1536]{1,0:T(8,128)(2,1)S(1)}, bf16[128,1536]{1,0:T(8,128)(2,1)S(1)}) custom-call(s32[1,256]{1,0:T(1,128)} %bitcast.13, bf16[768,3072]{1,0:T(8,128)(2,1)} %centers_ref.5), custom_call_target="tpu_custom_call" | custom-call | flops 603979776 | bytes 3145728 | tf_op jit(solution)/shard_map/pick_batch/pallas_call | solution.py:101
  2.9 0.0 copy-start.6
  2.9 0.0 copy-start
  3.0 0.1 collective-permute-start
  3.1 2.4 %pick_batch.3 = (bf16[128,1536]{1,0:T(8,128)(2,1)S(1)}, bf16[128,1536]{1,0:T(8,128)(2,1)S(1)}) custom-call(s32[1,256]{1,0:T(1,128)} %bitcast.14, bf16[768,3072]{1,0:T(8,128)(2,1)} %centers_ref.5), custom_call_target="tpu_custom_call" | custom-call | flops 603979776 | bytes 3145728 | tf_op jit(solution)/shard_map/pick_batch/pallas_call | solution.py:101
  5.5 0.6 collective-permute-start.2
  6.2 0.0 collective-permute-done
  6.2 0.1 add.48
  6.3 2.5 %collective-permute-start.1 = (bf16[64,1536]{1,0:T(8,128)(2,1)S(1)}, bf16[64,1536]{1,0:T(8,128)(2,1)S(1)}, u32[]{:S(2)}, u32[]{:S(2)}) collective-permute-start(bf16[64,1536]{1,0:T(8,128)(2,1)S(1)} %slice.65), channel_id=1, source_target_pairs={{0,2},{1,5},{2,0},{3,7},{4,6},{5,1},{6,4},{7,3},{8,10},{9,13},{10,... | collective-permute-start | bytes 589832 | tf_op jit(solution)/shard_map/ppermute | solution.py:437
  8.8 1.2 %center_norms.1.norm_ref = f32[768,128]{1,0:T(8,128)S(1)} custom-call(bf16[768,3072]{1,0:T(8,128)(2,1)S(1)} %copy-done), custom_call_target="tpu_custom_call" | custom-call | flops 4718592 | bytes 4718592 | tf_op jit(solution)/shard_map/center_norms/pallas_call | solution.py:173
  10.0 1.6 %spread_weights.1 = (bf16[608,768]{1,0:T(8,128)(2,1)S(1)}, bf16[608,768]{1,0:T(8,128)(2,1)S(1)}, bf16[576,768]{1,0:T(8,128)(2,1)S(1)}, bf16[576,768]{1,0:T(8,128)(2,1)S(1)}, f32[160,768]{1,0:T(8,128)S(1)}) custom-call(s32[1,320]{1,0:T(1,128)S(1)} %reshape.14.index_ref, f32[160,320]{1,0:T(8,128)S(1)} %bitcast.12, f32[1000,768]{1,0:T(8,128)S(1)} %bitcast.7), custom_call_target="tpu_custom_call" | custom-call | flops 235929600 | bytes 7274496 | tf_op jit(solution)/shard_map/spread_weights/pallas_call | solution.py:146
  11.6 0.1 add.50
  11.7 0.5 collective-permute-start.3
  12.3 0.0 collective-permute-done.1
  12.3 1.4 %collective-permute-start.9 = (bf16[32,1536]{1,0:T(8,128)(2,1)S(1)}, bf16[32,1536]{1,0:T(8,128)(2,1)S(1)}, u32[]{:S(2)}, u32[]{:S(2)}) collective-permute-start(bf16[32,1536]{1,0:T(8,128)(2,1)S(1)} %slice.66), channel_id=1, source_target_pairs={{0,4},{1,3},{2,6},{3,1},{4,0},{5,7},{6,2},{7,5},{8,12},{9,11},{10,... | collective-permute-start | bytes 294920 | tf_op jit(solution)/shard_map/ppermute | solution.py:437
  13.7 3.0 %collective-permute-done.3 = bf16[64,1536]{1,0:T(8,128)(2,1)S(1)} collective-permute-done((bf16[64,1536]{1,0:T(8,128)(2,1)S(1)}, bf16[64,1536]{1,0:T(8,128)(2,1)S(1)}, u32[]{:S(2)}, u32[]{:S(2)}) %collective-permute-start.3) | collective-permute-done | bytes 196640 | tf_op jit(solution)/shard_map/ppermute | solution.py:437
  16.7 1.2 %collective-permute-start.4 = (bf16[32,1536]{1,0:T(8,128)(2,1)S(1)}, bf16[32,1536]{1,0:T(8,128)(2,1)S(1)}, u32[]{:S(2)}, u32[]{:S(2)}) collective-permute-start(bf16[32,1536]{1,0:T(8,128)(2,1)S(1)} %slice.70), channel_id=1, source_target_pairs={{0,4},{1,3},{2,6},{3,1},{4,0},{5,7},{6,2},{7,5},{8,12},{9,11},{10,... | collective-permute-start | bytes 294920 | tf_op jit(solution)/shard_map/ppermute | solution.py:437
  18.0 2.4 %collective-permute-start.10 = (bf16[32,1536]{1,0:T(8,128)(2,1)S(1)}, bf16[32,1536]{1,0:T(8,128)(2,1)S(1)}, u32[]{:S(2)}, u32[]{:S(2)}) collective-permute-start(bf16[32,1536]{1,0:T(8,128)(2,1)S(1)} %slice_add_fusion.4), channel_id=1, source_target_pairs={{0,8},{1,9},{2,10},{3,11},{4,12},{5,13},{6,14},{7,15},{8,0},{9,1},... | collective-permute-start | bytes 294920 | tf_op jit(solution)/shard_map/ppermute | solution.py:437
  20.4 2.2 %collective-permute-start.5 = (bf16[32,1536]{1,0:T(8,128)(2,1)S(1)}, bf16[32,1536]{1,0:T(8,128)(2,1)S(1)}, u32[]{:S(2)}, u32[]{:S(2)}) collective-permute-start(bf16[32,1536]{1,0:T(8,128)(2,1)S(1)} %slice_add_fusion.5), channel_id=1, source_target_pairs={{0,8},{1,9},{2,10},{3,11},{4,12},{5,13},{6,14},{7,15},{8,0},{9,1},... | collective-permute-start | bytes 294920 | tf_op jit(solution)/shard_map/ppermute | solution.py:437
  22.6 0.9 %collective-permute-done.10 = bf16[32,1536]{1,0:T(8,128)(2,1)S(1)} collective-permute-done((bf16[32,1536]{1,0:T(8,128)(2,1)S(1)}, bf16[32,1536]{1,0:T(8,128)(2,1)S(1)}, u32[]{:S(2)}, u32[]{:S(2)}) %collective-permute-start.10) | collective-permute-done | bytes 98336 | tf_op jit(solution)/shard_map/ppermute | solution.py:437
  23.5 0.4 collective-permute-start.11
  23.9 4.1 %collective-permute-done.5 = bf16[32,1536]{1,0:T(8,128)(2,1)S(1)} collective-permute-done((bf16[32,1536]{1,0:T(8,128)(2,1)S(1)}, bf16[32,1536]{1,0:T(8,128)(2,1)S(1)}, u32[]{:S(2)}, u32[]{:S(2)}) %collective-permute-start.5) | collective-permute-done | bytes 98336 | tf_op jit(solution)/shard_map/ppermute | solution.py:437
  28.0 1.3 %collective-permute-start.6 = (bf16[32,1536]{1,0:T(8,128)(2,1)S(1)}, bf16[32,1536]{1,0:T(8,128)(2,1)S(1)}, u32[]{:S(2)}, u32[]{:S(2)}) collective-permute-start(bf16[32,1536]{1,0:T(8,128)(2,1)S(1)} %add.53), channel_id=1, source_target_pairs={{0,4},{1,3},{2,6},{3,1},{4,0},{5,7},{6,2},{7,5},{8,12},{9,11},{10,... | collective-permute-start | bytes 294920 | tf_op jit(solution)/shard_map/ppermute | solution.py:437
  29.3 0.1 collective-permute-start.12
  29.4 2.2 %collective-permute-done.6 = bf16[32,1536]{1,0:T(8,128)(2,1)S(1)} collective-permute-done((bf16[32,1536]{1,0:T(8,128)(2,1)S(1)}, bf16[32,1536]{1,0:T(8,128)(2,1)S(1)}, u32[]{:S(2)}, u32[]{:S(2)}) %collective-permute-start.6) | collective-permute-done | bytes 98336 | tf_op jit(solution)/shard_map/ppermute | solution.py:437
  31.5 0.1 collective-permute-start.7
  31.6 4.3 %collective-permute-done.12 = bf16[64,1536]{1,0:T(8,128)(2,1)S(1)} collective-permute-done((bf16[64,1536]{1,0:T(8,128)(2,1)S(1)}, bf16[64,1536]{1,0:T(8,128)(2,1)S(1)}, u32[]{:S(2)}, u32[]{:S(2)}) %collective-permute-start.12) | collective-permute-done | bytes 196640 | tf_op jit(solution)/shard_map/ppermute | solution.py:437
  36.0 4.1 %collective-permute-start.13 = (bf16[128,1536]{1,0:T(8,128)(2,1)S(1)}, bf16[128,1536]{1,0:T(8,128)(2,1)S(1)}, u32[]{:S(2)}, u32[]{:S(2)}) collective-permute-start(bf16[128,1536]{1,0:T(8,128)(2,1)S(1)} %pad_maximum_fusion.1.mine_ref), channel_id=1, source_target_pairs={{0,1},{1,0},{2,3},{3,2},{4,5},{5,4},{6,7},{7,6},{8,9},{9,8},{10,11... | collective-permute-start | bytes 1179656 | tf_op jit(solution)/shard_map/ppermute | solution.py:437
  40.1 0.0 collective-permute-done.7
  40.1 2.1 %collective-permute-start.8 = (bf16[128,1536]{1,0:T(8,128)(2,1)S(1)}, bf16[128,1536]{1,0:T(8,128)(2,1)S(1)}, u32[]{:S(2)}, u32[]{:S(2)}) collective-permute-start(bf16[128,1536]{1,0:T(8,128)(2,1)S(1)} %pad_maximum_fusion.mine_ref), channel_id=1, source_target_pairs={{0,1},{1,0},{2,3},{3,2},{4,5},{5,4},{6,7},{7,6},{8,9},{9,8},{10,11... | collective-permute-start | bytes 1179656 | tf_op jit(solution)/shard_map/ppermute | solution.py:437
  42.2 1.0 %distances.1.before_ref = f32[768,256]{1,0:T(8,128)S(1)} custom-call(bf16[128,1536]{1,0:T(8,128)(2,1)S(1)} %pad_maximum_fusion.1.mine_ref, bf16[128,1536]{1,0:T(8,128)(2,1)S(1)} %collective-permute-done.13.other_ref, bf16[768,3072]{1,0:T(8,128)(2,1)S(1)} %copy-done, f32[768,128]{1,0:T(8,128)S(1)} %center_norms.1.norm_ref), custom_call_target="tpu_custom_call" | custom-call | flops 603979776 | bytes 3145728 | tf_op jit(solution)/shard_map/distances/pallas_call | solution.py:244
  43.2 0.4 collective-permute-done.8.other_ref
  43.6 3.1 %predict.1 = (f32[608,128]{1,0:T(8,128)S(1)}, f32[608,128]{1,0:T(8,128)S(1)}, bf16[768,256]{1,0:T(8,128)(2,1)S(1)}, bf16[768,256]{1,0:T(8,128)(2,1)S(1)}) custom-call(bf16[128,1536]{1,0:T(8,128)(2,1)S(1)} %pad_maximum_fusion.mine_ref, bf16[128,1536]{1,0:T(8,128)(2,1)S(1)} %collective-permute-done.8.other_ref, bf16[768,3072]{1,0:T(8,128)(2,1)S(1)} %copy-done, ...), custom_call_target="tpu_custom_call" | custom-call | flops 1321205760 | bytes 5636096 | tf_op jit(solution)/shard_map/predict/pallas_call | solution.py:266
  46.6 0.4 collective-permute-start.21
  47.1 1.2 %collective-permute-done.21 = f32[608,128]{1,0:T(8,128)S(1)} collective-permute-done((f32[608,128]{1,0:T(8,128)S(1)}, f32[608,128]{1,0:T(8,128)S(1)}, u32[]{:S(2)}, u32[]{:S(2)}) %collective-permute-start.21) | collective-permute-done | bytes 311328 | tf_op jit(solution)/shard_map/ppermute | solution.py:437
  48.3 0.7 collective-permute-start.22
  49.0 0.9 %predict_more.1 = (f32[576,128]{1,0:T(8,128)S(1)}, f32[576,128]{1,0:T(8,128)S(1)}) custom-call(bf16[576,768]{1,0:T(8,128)(2,1)S(1)} %get-tuple-element.37.high_ref, bf16[576,768]{1,0:T(8,128)(2,1)S(1)} %get-tuple-element.38.low_ref, bf16[768,256]{1,0:T(8,128)(2,1)S(1)} %get-tuple-element.45.value_high_ref, bf16[768,256]{1,0:T(8,128)(2,1)S(1)} %get-tuple-element.46.value_low_ref), custom_call_target="tpu_custom_call" | custom-call | flops 679477248 | bytes 2359296 | tf_op jit(solution)/shard_map/predict_more/pallas_call | solution.py:290
  49.9 0.0 copy-start.2
  50.0 0.0 copy-start.4
  50.0 0.0 copy-start.5
  50.0 1.3 %collective-permute-start.14 = (f32[576,128]{1,0:T(8,128)S(1)}, f32[576,128]{1,0:T(8,128)S(1)}, u32[]{:S(2)}, u32[]{:S(2)}) collective-permute-start(f32[576,128]{1,0:T(8,128)S(1)} %get-tuple-element.48), channel_id=1, source_target_pairs={{0,1},{1,0},{2,3},{3,2},{4,5},{5,4},{6,7},{7,6},{8,9},{9,8},{10,11... | collective-permute-start | bytes 884744 | tf_op jit(solution)/shard_map/ppermute | solution.py:437
  51.3 1.5 %collective-permute-done.22 = f32[304,128]{1,0:T(8,128)S(1)} collective-permute-done((f32[304,128]{1,0:T(8,128)S(1)}, f32[304,128]{1,0:T(8,128)S(1)}, u32[]{:S(2)}, u32[]{:S(2)}) %collective-permute-start.22) | collective-permute-done | bytes 155680 | tf_op jit(solution)/shard_map/ppermute | solution.py:437
  52.8 1.3 %collective-permute-start.23 = (f32[152,128]{1,0:T(8,128)S(1)}, f32[152,128]{1,0:T(8,128)S(1)}, u32[]{:S(2)}, u32[]{:S(2)}) collective-permute-start(f32[152,128]{1,0:T(8,128)S(1)} %slice.79), channel_id=1, source_target_pairs={{0,4},{1,3},{2,6},{3,1},{4,0},{5,7},{6,2},{7,5},{8,12},{9,11},{10,... | collective-permute-start | bytes 233480 | tf_op jit(solution)/shard_map/ppermute | solution.py:437
  54.1 0.0 collective-permute-done.14
  54.1 0.9 collective-permute-start.15
  55.0 1.1 %collective-permute-done.23 = f32[152,128]{1,0:T(8,128)S(1)} collective-permute-done((f32[152,128]{1,0:T(8,128)S(1)}, f32[152,128]{1,0:T(8,128)S(1)}, u32[]{:S(2)}, u32[]{:S(2)}) %collective-permute-start.23) | collective-permute-done | bytes 77856 | tf_op jit(solution)/shard_map/ppermute | solution.py:437
  56.2 2.2 %collective-permute-start.24 = (f32[152,128]{1,0:T(8,128)S(1)}, f32[152,128]{1,0:T(8,128)S(1)}, u32[]{:S(2)}, u32[]{:S(2)}) collective-permute-start(f32[152,128]{1,0:T(8,128)S(1)} %slice_add_fusion.6), channel_id=1, source_target_pairs={{0,8},{1,9},{2,10},{3,11},{4,12},{5,13},{6,14},{7,15},{8,0},{9,1},... | collective-permute-start | bytes 233480 | tf_op jit(solution)/shard_map/ppermute | solution.py:437
  58.3 1.0 %collective-permute-done.15 = f32[288,128]{1,0:T(8,128)S(1)} collective-permute-done((f32[288,128]{1,0:T(8,128)S(1)}, f32[288,128]{1,0:T(8,128)S(1)}, u32[]{:S(2)}, u32[]{:S(2)}) %collective-permute-start.15) | collective-permute-done | bytes 147488 | tf_op jit(solution)/shard_map/ppermute | solution.py:437
  59.4 0.2 collective-permute-start.16
  59.6 0.8 collective-permute-done.24
  60.4 1.3 %collective-permute-start.25 = (f32[152,128]{1,0:T(8,128)S(1)}, f32[152,128]{1,0:T(8,128)S(1)}, u32[]{:S(2)}, u32[]{:S(2)}) collective-permute-start(f32[152,128]{1,0:T(8,128)S(1)} %add.63), channel_id=1, source_target_pairs={{0,4},{1,3},{2,6},{3,1},{4,0},{5,7},{6,2},{7,5},{8,12},{9,11},{10,... | collective-permute-start | bytes 233480 | tf_op jit(solution)/shard_map/ppermute | solution.py:437
  61.6 1.0 %collective-permute-done.16 = f32[144,128]{1,0:T(8,128)S(1)} collective-permute-done((f32[144,128]{1,0:T(8,128)S(1)}, f32[144,128]{1,0:T(8,128)S(1)}, u32[]{:S(2)}, u32[]{:S(2)}) %collective-permute-start.16) | collective-permute-done | bytes 73760 | tf_op jit(solution)/shard_map/ppermute | solution.py:437
  62.6 2.1 %collective-permute-start.17 = (f32[144,128]{1,0:T(8,128)S(1)}, f32[144,128]{1,0:T(8,128)S(1)}, u32[]{:S(2)}, u32[]{:S(2)}) collective-permute-start(f32[144,128]{1,0:T(8,128)S(1)} %slice_add_fusion.7), channel_id=1, source_target_pairs={{0,8},{1,9},{2,10},{3,11},{4,12},{5,13},{6,14},{7,15},{8,0},{9,1},... | collective-permute-start | bytes 221192 | tf_op jit(solution)/shard_map/ppermute | solution.py:437
  64.8 2.8 %collective-permute-done.17 = f32[144,128]{1,0:T(8,128)S(1)} collective-permute-done((f32[144,128]{1,0:T(8,128)S(1)}, f32[144,128]{1,0:T(8,128)S(1)}, u32[]{:S(2)}, u32[]{:S(2)}) %collective-permute-start.17) | collective-permute-done | bytes 73760 | tf_op jit(solution)/shard_map/ppermute | solution.py:437
  67.6 0.1 collective-permute-start.18
  67.7 1.4 %collective-permute-start.26 = (f32[304,128]{1,0:T(8,128)S(1)}, f32[304,128]{1,0:T(8,128)S(1)}, u32[]{:S(2)}, u32[]{:S(2)}) collective-permute-start(f32[304,128]{1,0:T(8,128)S(1)} %pad_maximum_fusion.6), channel_id=1, source_target_pairs={{0,2},{1,5},{2,0},{3,7},{4,6},{5,1},{6,4},{7,3},{8,10},{9,13},{10,... | collective-permute-start | bytes 466952 | tf_op jit(solution)/shard_map/ppermute | solution.py:437
  69.1 2.1 %collective-permute-done.18 = f32[144,128]{1,0:T(8,128)S(1)} collective-permute-done((f32[144,128]{1,0:T(8,128)S(1)}, f32[144,128]{1,0:T(8,128)S(1)}, u32[]{:S(2)}, u32[]{:S(2)}) %collective-permute-start.18) | collective-permute-done | bytes 73760 | tf_op jit(solution)/shard_map/ppermute | solution.py:437
  71.2 0.2 collective-permute-start.19
  71.4 1.2 %collective-permute-done.26 = f32[304,128]{1,0:T(8,128)S(1)} collective-permute-done((f32[304,128]{1,0:T(8,128)S(1)}, f32[304,128]{1,0:T(8,128)S(1)}, u32[]{:S(2)}, u32[]{:S(2)}) %collective-permute-start.26) | collective-permute-done | bytes 155680 | tf_op jit(solution)/shard_map/ppermute | solution.py:437
  72.6 6.4 %collective-permute-start.27 = (f32[608,128]{1,0:T(8,128)S(1)}, f32[608,128]{1,0:T(8,128)S(1)}, u32[]{:S(2)}, u32[]{:S(2)}) collective-permute-start(f32[608,128]{1,0:T(8,128)S(1)} %pad_maximum_fusion.2.mine_ref), channel_id=1, source_target_pairs={{0,1},{1,0},{2,3},{3,2},{4,5},{5,4},{6,7},{7,6},{8,9},{9,8},{10,11... | collective-permute-start | bytes 933896 | tf_op jit(solution)/shard_map/ppermute | solution.py:437
  79.0 3.0 %collective-permute-start.20 = (f32[576,128]{1,0:T(8,128)S(1)}, f32[576,128]{1,0:T(8,128)S(1)}, u32[]{:S(2)}, u32[]{:S(2)}) collective-permute-start(f32[576,128]{1,0:T(8,128)S(1)} %pad_maximum_fusion.3.mine_ref), channel_id=1, source_target_pairs={{0,1},{1,0},{2,3},{3,2},{4,5},{5,4},{6,7},{7,6},{8,9},{9,8},{10,11... | collective-permute-start | bytes 884744 | tf_op jit(solution)/shard_map/ppermute | solution.py:437
  82.0 0.0 collective-permute-done.27.other_ref
  82.1 2.4 %update.1 = (f32[1000,768]{1,0:T(8,128)}, f32[1000,256]{1,0:T(8,128)}, bf16[256,768]{1,0:T(8,128)(2,1)S(1)}, bf16[256,768]{1,0:T(8,128)(2,1)S(1)}) custom-call(f32[608,128]{1,0:T(8,128)S(1)} %pad_maximum_fusion.2.mine_ref, f32[608,128]{1,0:T(8,128)S(1)} %collective-permute-done.27.other_ref, f32[1000,256]{1,0:T(8,128)S(1)} %bitcast.10, ...), custom_call_target="tpu_custom_call" | custom-call | flops 717225984 | bytes 3670016 | tf_op jit(solution)/shard_map/update/pallas_call | solution.py:374
  84.5 2.0 %update_more.1 = (f32[1000,768]{1,0:T(8,128)}, f32[1000,256]{1,0:T(8,128)}) custom-call(f32[576,128]{1,0:T(8,128)S(1)} %pad_maximum_fusion.3.mine_ref, f32[576,128]{1,0:T(8,128)S(1)} %collective-permute-done.20.other_ref, f32[1000,256]{1,0:T(8,128)S(1)} %bitcast.11, f32[1000,768]{1,0:T(8,128)S(1)} %bitcast.9, ...), custom_call_target="tpu_custom_call", output_to_operand_aliasing={{0}: (6, {}), {1}: (7, {})} | custom-call | flops 651165696 | bytes 4521984 | tf_op jit(solution)/shard_map/update_more/pallas_call | solution.py:412
  (48 shorter events, 0.6 us)
Async XLA Ops:
  2.9 5.9 %copy-start.6 = (s32[320]{0:T(512)S(1)}, s32[320]{0:T(512)}, u32[]{:S(2)}) copy-start(s32[320]{0:T(512)} %param.11) | copy-start | bytes 3844
  2.9 5.9 %copy-start = (bf16[768,3072]{1,0:T(8,128)(2,1)S(1)}, bf16[768,3072]{1,0:T(8,128)(2,1)}, u32[]{:S(2)}) copy-start(bf16[768,3072]{1,0:T(8,128)(2,1)} %centers_ref.5) | copy-start | bytes 14155780
  3.0 3.2 %collective-permute-start = (bf16[128,1536]{1,0:T(8,128)(2,1)S(1)}, bf16[128,1536]{1,0:T(8,128)(2,1)S(1)}, u32[]{:S(2)}, u32[]{:S(2)}) collective-permute-start(bf16[128,1536]{1,0:T(8,128)(2,1)S(1)} %get-tuple-element.31), channel_id=1, source_target_pairs={{0,1},{1,0},{2,3},{3,2},{4,5},{5,4},{6,7},{7,6},{8,9},{9,8},{10,11... | collective-permute-start | bytes 1179656 | tf_op jit(solution)/shard_map/ppermute | solution.py:437
  5.5 6.1 %collective-permute-start.2 = (bf16[128,1536]{1,0:T(8,128)(2,1)S(1)}, bf16[128,1536]{1,0:T(8,128)(2,1)S(1)}, u32[]{:S(2)}, u32[]{:S(2)}) collective-permute-start(bf16[128,1536]{1,0:T(8,128)(2,1)S(1)} %get-tuple-element.40), channel_id=1, source_target_pairs={{0,1},{1,0},{2,3},{3,2},{4,5},{5,4},{6,7},{7,6},{8,9},{9,8},{10,11... | collective-permute-start | bytes 1179656 | tf_op jit(solution)/shard_map/ppermute | solution.py:437
  6.2 3.8 %copy-start.1 = (f32[768,1000]{0,1:T(8,128)S(1)}, f32[768,1000]{0,1:T(8,128)}, u32[]{:S(2)}) copy-start(f32[768,1000]{0,1:T(8,128)} %param.8) | copy-start | bytes 9216004
  6.2 3.8 %copy-start.3 = (f32[320,160]{0,1:T(8,128)S(1)}, f32[320,160]{0,1:T(8,128)}, u32[]{:S(2)}) copy-start(f32[320,160]{0,1:T(8,128)} %param.12) | copy-start | bytes 614404
  6.3 6.0 %collective-permute-start.1 = (bf16[64,1536]{1,0:T(8,128)(2,1)S(1)}, bf16[64,1536]{1,0:T(8,128)(2,1)S(1)}, u32[]{:S(2)}, u32[]{:S(2)}) collective-permute-start(bf16[64,1536]{1,0:T(8,128)(2,1)S(1)} %slice.65), channel_id=1, source_target_pairs={{0,2},{1,5},{2,0},{3,7},{4,6},{5,1},{6,4},{7,3},{8,10},{9,13},{10,... | collective-permute-start | bytes 589832 | tf_op jit(solution)/shard_map/ppermute | solution.py:437
  11.7 4.9 %collective-permute-start.3 = (bf16[64,1536]{1,0:T(8,128)(2,1)S(1)}, bf16[64,1536]{1,0:T(8,128)(2,1)S(1)}, u32[]{:S(2)}, u32[]{:S(2)}) collective-permute-start(bf16[64,1536]{1,0:T(8,128)(2,1)S(1)} %slice.68), channel_id=1, source_target_pairs={{0,2},{1,5},{2,0},{3,7},{4,6},{5,1},{6,4},{7,3},{8,10},{9,13},{10,... | collective-permute-start | bytes 589832 | tf_op jit(solution)/shard_map/ppermute | solution.py:437
  12.3 5.6 %collective-permute-start.9 = (bf16[32,1536]{1,0:T(8,128)(2,1)S(1)}, bf16[32,1536]{1,0:T(8,128)(2,1)S(1)}, u32[]{:S(2)}, u32[]{:S(2)}) collective-permute-start(bf16[32,1536]{1,0:T(8,128)(2,1)S(1)} %slice.66), channel_id=1, source_target_pairs={{0,4},{1,3},{2,6},{3,1},{4,0},{5,7},{6,2},{7,5},{8,12},{9,11},{10,... | collective-permute-start | bytes 294920 | tf_op jit(solution)/shard_map/ppermute | solution.py:437
  16.7 3.6 %collective-permute-start.4 = (bf16[32,1536]{1,0:T(8,128)(2,1)S(1)}, bf16[32,1536]{1,0:T(8,128)(2,1)S(1)}, u32[]{:S(2)}, u32[]{:S(2)}) collective-permute-start(bf16[32,1536]{1,0:T(8,128)(2,1)S(1)} %slice.70), channel_id=1, source_target_pairs={{0,4},{1,3},{2,6},{3,1},{4,0},{5,7},{6,2},{7,5},{8,12},{9,11},{10,... | collective-permute-start | bytes 294920 | tf_op jit(solution)/shard_map/ppermute | solution.py:437
  18.0 5.5 %collective-permute-start.10 = (bf16[32,1536]{1,0:T(8,128)(2,1)S(1)}, bf16[32,1536]{1,0:T(8,128)(2,1)S(1)}, u32[]{:S(2)}, u32[]{:S(2)}) collective-permute-start(bf16[32,1536]{1,0:T(8,128)(2,1)S(1)} %slice_add_fusion.4), channel_id=1, source_target_pairs={{0,8},{1,9},{2,10},{3,11},{4,12},{5,13},{6,14},{7,15},{8,0},{9,1},... | collective-permute-start | bytes 294920 | tf_op jit(solution)/shard_map/ppermute | solution.py:437
  20.4 7.6 %collective-permute-start.5 = (bf16[32,1536]{1,0:T(8,128)(2,1)S(1)}, bf16[32,1536]{1,0:T(8,128)(2,1)S(1)}, u32[]{:S(2)}, u32[]{:S(2)}) collective-permute-start(bf16[32,1536]{1,0:T(8,128)(2,1)S(1)} %slice_add_fusion.5), channel_id=1, source_target_pairs={{0,8},{1,9},{2,10},{3,11},{4,12},{5,13},{6,14},{7,15},{8,0},{9,1},... | collective-permute-start | bytes 294920 | tf_op jit(solution)/shard_map/ppermute | solution.py:437
  23.5 5.8 %collective-permute-start.11 = (bf16[32,1536]{1,0:T(8,128)(2,1)S(1)}, bf16[32,1536]{1,0:T(8,128)(2,1)S(1)}, u32[]{:S(2)}, u32[]{:S(2)}) collective-permute-start(bf16[32,1536]{1,0:T(8,128)(2,1)S(1)} %add.55), channel_id=1, source_target_pairs={{0,4},{1,3},{2,6},{3,1},{4,0},{5,7},{6,2},{7,5},{8,12},{9,11},{10,... | collective-permute-start | bytes 294920 | tf_op jit(solution)/shard_map/ppermute | solution.py:437
  28.0 3.5 %collective-permute-start.6 = (bf16[32,1536]{1,0:T(8,128)(2,1)S(1)}, bf16[32,1536]{1,0:T(8,128)(2,1)S(1)}, u32[]{:S(2)}, u32[]{:S(2)}) collective-permute-start(bf16[32,1536]{1,0:T(8,128)(2,1)S(1)} %add.53), channel_id=1, source_target_pairs={{0,4},{1,3},{2,6},{3,1},{4,0},{5,7},{6,2},{7,5},{8,12},{9,11},{10,... | collective-permute-start | bytes 294920 | tf_op jit(solution)/shard_map/ppermute | solution.py:437
  29.3 6.7 %collective-permute-start.12 = (bf16[64,1536]{1,0:T(8,128)(2,1)S(1)}, bf16[64,1536]{1,0:T(8,128)(2,1)S(1)}, u32[]{:S(2)}, u32[]{:S(2)}) collective-permute-start(bf16[64,1536]{1,0:T(8,128)(2,1)S(1)} %pad_maximum_fusion.5), channel_id=1, source_target_pairs={{0,2},{1,5},{2,0},{3,7},{4,6},{5,1},{6,4},{7,3},{8,10},{9,13},{10,... | collective-permute-start | bytes 589832 | tf_op jit(solution)/shard_map/ppermute | solution.py:437
  31.5 8.6 %collective-permute-start.7 = (bf16[64,1536]{1,0:T(8,128)(2,1)S(1)}, bf16[64,1536]{1,0:T(8,128)(2,1)S(1)}, u32[]{:S(2)}, u32[]{:S(2)}) collective-permute-start(bf16[64,1536]{1,0:T(8,128)(2,1)S(1)} %pad_maximum_fusion.4), channel_id=1, source_target_pairs={{0,2},{1,5},{2,0},{3,7},{4,6},{5,1},{6,4},{7,3},{8,10},{9,13},{10,... | collective-permute-start | bytes 589832 | tf_op jit(solution)/shard_map/ppermute | solution.py:437
  36.0 6.2 %collective-permute-start.13 = (bf16[128,1536]{1,0:T(8,128)(2,1)S(1)}, bf16[128,1536]{1,0:T(8,128)(2,1)S(1)}, u32[]{:S(2)}, u32[]{:S(2)}) collective-permute-start(bf16[128,1536]{1,0:T(8,128)(2,1)S(1)} %pad_maximum_fusion.1.mine_ref), channel_id=1, source_target_pairs={{0,1},{1,0},{2,3},{3,2},{4,5},{5,4},{6,7},{7,6},{8,9},{9,8},{10,11... | collective-permute-start | bytes 1179656 | tf_op jit(solution)/shard_map/ppermute | solution.py:437
  40.1 3.4 %collective-permute-start.8 = (bf16[128,1536]{1,0:T(8,128)(2,1)S(1)}, bf16[128,1536]{1,0:T(8,128)(2,1)S(1)}, u32[]{:S(2)}, u32[]{:S(2)}) collective-permute-start(bf16[128,1536]{1,0:T(8,128)(2,1)S(1)} %pad_maximum_fusion.mine_ref), channel_id=1, source_target_pairs={{0,1},{1,0},{2,3},{3,2},{4,5},{5,4},{6,7},{7,6},{8,9},{9,8},{10,11... | collective-permute-start | bytes 1179656 | tf_op jit(solution)/shard_map/ppermute | solution.py:437
  46.6 1.7 %collective-permute-start.21 = (f32[608,128]{1,0:T(8,128)S(1)}, f32[608,128]{1,0:T(8,128)S(1)}, u32[]{:S(2)}, u32[]{:S(2)}) collective-permute-start(f32[608,128]{1,0:T(8,128)S(1)} %get-tuple-element.50), channel_id=1, source_target_pairs={{0,1},{1,0},{2,3},{3,2},{4,5},{5,4},{6,7},{7,6},{8,9},{9,8},{10,11... | collective-permute-start | bytes 933896 | tf_op jit(solution)/shard_map/ppermute | solution.py:437
  48.3 4.4 %collective-permute-start.22 = (f32[304,128]{1,0:T(8,128)S(1)}, f32[304,128]{1,0:T(8,128)S(1)}, u32[]{:S(2)}, u32[]{:S(2)}) collective-permute-start(f32[304,128]{1,0:T(8,128)S(1)} %slice.77), channel_id=1, source_target_pairs={{0,2},{1,5},{2,0},{3,7},{4,6},{5,1},{6,4},{7,3},{8,10},{9,13},{10,... | collective-permute-start | bytes 466952 | tf_op jit(solution)/shard_map/ppermute | solution.py:437
  49.9 32.1 %copy-start.2 = (f32[256,1000]{0,1:T(8,128)S(1)}, f32[256,1000]{0,1:T(8,128)}, u32[]{:S(2)}) copy-start(f32[256,1000]{0,1:T(8,128)} %param.9) | copy-start | bytes 3072004
  50.0 32.1 %copy-start.4 = (s32[256]{0:T(256)S(1)}, s32[256]{0:T(256)}, u32[]{:S(2)}) copy-start(s32[256]{0:T(256)} %param.10) | copy-start | bytes 3076
  50.0 32.1 %copy-start.5 = (f32[160]{0:T(256)S(1)}, f32[160]{0:T(256)}, u32[]{:S(2)}) copy-start(f32[160]{0:T(256)} %param.13) | copy-start | bytes 1924
  50.0 4.1 %collective-permute-start.14 = (f32[576,128]{1,0:T(8,128)S(1)}, f32[576,128]{1,0:T(8,128)S(1)}, u32[]{:S(2)}, u32[]{:S(2)}) collective-permute-start(f32[576,128]{1,0:T(8,128)S(1)} %get-tuple-element.48), channel_id=1, source_target_pairs={{0,1},{1,0},{2,3},{3,2},{4,5},{5,4},{6,7},{7,6},{8,9},{9,8},{10,11... | collective-permute-start | bytes 884744 | tf_op jit(solution)/shard_map/ppermute | solution.py:437
  52.8 3.3 %collective-permute-start.23 = (f32[152,128]{1,0:T(8,128)S(1)}, f32[152,128]{1,0:T(8,128)S(1)}, u32[]{:S(2)}, u32[]{:S(2)}) collective-permute-start(f32[152,128]{1,0:T(8,128)S(1)} %slice.79), channel_id=1, source_target_pairs={{0,4},{1,3},{2,6},{3,1},{4,0},{5,7},{6,2},{7,5},{8,12},{9,11},{10,... | collective-permute-start | bytes 233480 | tf_op jit(solution)/shard_map/ppermute | solution.py:437
  54.1 5.2 %collective-permute-start.15 = (f32[288,128]{1,0:T(8,128)S(1)}, f32[288,128]{1,0:T(8,128)S(1)}, u32[]{:S(2)}, u32[]{:S(2)}) collective-permute-start(f32[288,128]{1,0:T(8,128)S(1)} %slice.73), channel_id=1, source_target_pairs={{0,2},{1,5},{2,0},{3,7},{4,6},{5,1},{6,4},{7,3},{8,10},{9,13},{10,... | collective-permute-start | bytes 442376 | tf_op jit(solution)/shard_map/ppermute | solution.py:437
  56.2 4.2 %collective-permute-start.24 = (f32[152,128]{1,0:T(8,128)S(1)}, f32[152,128]{1,0:T(8,128)S(1)}, u32[]{:S(2)}, u32[]{:S(2)}) collective-permute-start(f32[152,128]{1,0:T(8,128)S(1)} %slice_add_fusion.6), channel_id=1, source_target_pairs={{0,8},{1,9},{2,10},{3,11},{4,12},{5,13},{6,14},{7,15},{8,0},{9,1},... | collective-permute-start | bytes 233480 | tf_op jit(solution)/shard_map/ppermute | solution.py:437
  59.4 3.3 %collective-permute-start.16 = (f32[144,128]{1,0:T(8,128)S(1)}, f32[144,128]{1,0:T(8,128)S(1)}, u32[]{:S(2)}, u32[]{:S(2)}) collective-permute-start(f32[144,128]{1,0:T(8,128)S(1)} %slice.75), channel_id=1, source_target_pairs={{0,4},{1,3},{2,6},{3,1},{4,0},{5,7},{6,2},{7,5},{8,12},{9,11},{10,... | collective-permute-start | bytes 221192 | tf_op jit(solution)/shard_map/ppermute | solution.py:437
  60.4 7.3 %collective-permute-start.25 = (f32[152,128]{1,0:T(8,128)S(1)}, f32[152,128]{1,0:T(8,128)S(1)}, u32[]{:S(2)}, u32[]{:S(2)}) collective-permute-start(f32[152,128]{1,0:T(8,128)S(1)} %add.63), channel_id=1, source_target_pairs={{0,4},{1,3},{2,6},{3,1},{4,0},{5,7},{6,2},{7,5},{8,12},{9,11},{10,... | collective-permute-start | bytes 233480 | tf_op jit(solution)/shard_map/ppermute | solution.py:437
  62.6 5.0 %collective-permute-start.17 = (f32[144,128]{1,0:T(8,128)S(1)}, f32[144,128]{1,0:T(8,128)S(1)}, u32[]{:S(2)}, u32[]{:S(2)}) collective-permute-start(f32[144,128]{1,0:T(8,128)S(1)} %slice_add_fusion.7), channel_id=1, source_target_pairs={{0,8},{1,9},{2,10},{3,11},{4,12},{5,13},{6,14},{7,15},{8,0},{9,1},... | collective-permute-start | bytes 221192 | tf_op jit(solution)/shard_map/ppermute | solution.py:437
  67.6 3.6 %collective-permute-start.18 = (f32[144,128]{1,0:T(8,128)S(1)}, f32[144,128]{1,0:T(8,128)S(1)}, u32[]{:S(2)}, u32[]{:S(2)}) collective-permute-start(f32[144,128]{1,0:T(8,128)S(1)} %add.59), channel_id=1, source_target_pairs={{0,4},{1,3},{2,6},{3,1},{4,0},{5,7},{6,2},{7,5},{8,12},{9,11},{10,... | collective-permute-start | bytes 221192 | tf_op jit(solution)/shard_map/ppermute | solution.py:437
  67.7 4.9 %collective-permute-start.26 = (f32[304,128]{1,0:T(8,128)S(1)}, f32[304,128]{1,0:T(8,128)S(1)}, u32[]{:S(2)}, u32[]{:S(2)}) collective-permute-start(f32[304,128]{1,0:T(8,128)S(1)} %pad_maximum_fusion.6), channel_id=1, source_target_pairs={{0,2},{1,5},{2,0},{3,7},{4,6},{5,1},{6,4},{7,3},{8,10},{9,13},{10,... | collective-permute-start | bytes 466952 | tf_op jit(solution)/shard_map/ppermute | solution.py:437
  71.2 7.8 %collective-permute-start.19 = (f32[288,128]{1,0:T(8,128)S(1)}, f32[288,128]{1,0:T(8,128)S(1)}, u32[]{:S(2)}, u32[]{:S(2)}) collective-permute-start(f32[288,128]{1,0:T(8,128)S(1)} %pad_maximum_fusion.7), channel_id=1, source_target_pairs={{0,2},{1,5},{2,0},{3,7},{4,6},{5,1},{6,4},{7,3},{8,10},{9,13},{10,... | collective-permute-start | bytes 442376 | tf_op jit(solution)/shard_map/ppermute | solution.py:437
  72.6 9.4 %collective-permute-start.27 = (f32[608,128]{1,0:T(8,128)S(1)}, f32[608,128]{1,0:T(8,128)S(1)}, u32[]{:S(2)}, u32[]{:S(2)}) collective-permute-start(f32[608,128]{1,0:T(8,128)S(1)} %pad_maximum_fusion.2.mine_ref), channel_id=1, source_target_pairs={{0,1},{1,0},{2,3},{3,2},{4,5},{5,4},{6,7},{7,6},{8,9},{9,8},{10,11... | collective-permute-start | bytes 933896 | tf_op jit(solution)/shard_map/ppermute | solution.py:437
  79.0 5.5 %collective-permute-start.20 = (f32[576,128]{1,0:T(8,128)S(1)}, f32[576,128]{1,0:T(8,128)S(1)}, u32[]{:S(2)}, u32[]{:S(2)}) collective-permute-start(f32[576,128]{1,0:T(8,128)S(1)} %pad_maximum_fusion.3.mine_ref), channel_id=1, source_target_pairs={{0,1},{1,0},{2,3},{3,2},{4,5},{5,4},{6,7},{7,6},{8,9},{9,8},{10,11... | collective-permute-start | bytes 884744 | tf_op jit(solution)/shard_map/ppermute | solution.py:437

commit v7 on v6

--- a/solution.py
+++ b/solution.py
@@ -15,6 +15,7 @@
 CHUNKS = 1 << HALVINGS
 LANE = 128
 PARTS = 2
+UPDATES = 5
 NT = (((1,), (1,)), ((), ()))
 NN = (((1,), (0,)), ((), ()))
 VMEM_LIMIT = 24 * 1024 * 1024
@@ -117,45 +118,37 @@
     )(batch_index, centers)
 
 
-def spread_body(
-    first, classes, index_ref, eigvec_ref, weights_ref,
-    high1_ref, low1_ref, high2_ref, low2_ref, spread_ref, all_ref,
-):
+def spread_body(classes, index_ref, eigvec_ref, weights_ref, high_ref, low_ref, spread_ref):
     rank, points = eigvec_ref.shape
     count = weights_ref.shape[1]
     local = index_ref[...] - (lax.axis_index("center") * 2 + lax.axis_index("sub")) * count
     slots = lax.broadcasted_iota(jnp.int32, (count, points), 0)
     pick = jnp.where(slots == local, 1.0, 0.0).astype(BF16)
     vec = eigvec_ref[...]
-    high = vec.astype(BF16)
-    rest = vec - high.astype(F32)
-    mid = rest.astype(BF16)
-    low = (rest - mid.astype(F32)).astype(BF16)
-    spread = dot(high, pick, NT) + dot(mid, pick, NT) + dot(low, pick, NT)
+    vec_high = vec.astype(BF16)
+    rest = vec - vec_high.astype(F32)
+    vec_mid = rest.astype(BF16)
+    vec_low = (rest - vec_mid.astype(F32)).astype(BF16)
+    spread = dot(vec_high, pick, NT) + dot(vec_mid, pick, NT) + dot(vec_low, pick, NT)
     spread_ref[...] = spread
-    all_ref[:rank] = spread
-    all_ref[rank : rank + classes] = weights_ref[...]
-    all_ref[rank + classes :] = jnp.zeros((all_ref.shape[0] - rank - classes, count), F32)
-    for begin, high_ref, low_ref in ((0, high1_ref, low1_ref), (first, high2_ref, low2_ref)):
-        high_ref[...], low_ref[...] = two(all_ref[begin : begin + high_ref.shape[0]])
-
-
-def spread_weights(nys_index, eigvec, weights, first, second):
+    blank = jnp.zeros((high_ref.shape[0] - rank - classes, count), F32)
+    for at, rows in ((0, spread), (rank, weights_ref[...]), (rank + classes, blank)):
+        high_ref[at : at + rows.shape[0]], low_ref[at : at + rows.shape[0]] = two(rows)
+
+
+def spread_weights(nys_index, eigvec, weights, padded):
     classes, count = weights.shape
     rank, points = eigvec.shape
     return pl.pallas_call(
-        functools.partial(spread_body, first, classes),
+        functools.partial(spread_body, classes),
         out_shape=[
-            jax.ShapeDtypeStruct((first, count), BF16),
-            jax.ShapeDtypeStruct((first, count), BF16),
-            jax.ShapeDtypeStruct((second, count), BF16),
-            jax.ShapeDtypeStruct((second, count), BF16),
+            jax.ShapeDtypeStruct((padded, count), BF16),
+            jax.ShapeDtypeStruct((padded, count), BF16),
             jax.ShapeDtypeStruct((rank, count), F32),
         ],
-        scratch_shapes=[pltpu.VMEM((first + second, count), F32)],
         compiler_params=params(),
         cost_estimate=pl.CostEstimate(
-            flops=6 * rank * points * count, bytes_accessed=8 * (first + second) * count, transcendentals=0
+            flops=6 * rank * points * count, bytes_accessed=8 * padded * count, transcendentals=0
         ),
         name="spread_weights",
     )(nys_index, eigvec, weights)
@@ -225,14 +218,12 @@
 
 def predict_body(
     mine_ref, other_ref, centers_ref, before_ref, high_ref, low_ref,
-    keep_ref, send_ref, value_high_ref, value_low_ref, batch_ref, total_ref,
+    keep_ref, send_ref, batch_ref, total_ref,
 ):
     depth = centers_ref.shape[1]
     gather_batch(mine_ref, other_ref, batch_ref)
     square = jnp.maximum(before_ref[...] + nearer(depth - batch_ref.shape[1], centers_ref, batch_ref), 0.0)
     value_high, value_low = two(jnp.exp(jnp.sqrt(square) * (-1.0 / math.sqrt(depth))))
-    value_high_ref[...] = value_high
-    value_low_ref[...] = value_low
     product(high_ref, low_ref, value_high, value_low, total_ref, keep_ref, send_ref)
 
 
@@ -261,13 +252,12 @@
     count = centers.shape[0]
     padded = high.shape[0]
     out = jax.ShapeDtypeStruct((padded, half), F32)
-    value = jax.ShapeDtypeStruct((count, rows), BF16)
     vmem = pl.BlockSpec(memory_space=pltpu.VMEM)
     return pl.pallas_call(
         predict_body,
         in_specs=[vmem] * 6,
-        out_specs=[vmem] * 4,
-        out_shape=[out, out, value, value],
+        out_specs=[vmem] * 2,
+        out_shape=[out, out],
         scratch_shapes=[pltpu.VMEM((rows, depth), BF16), pltpu.VMEM((padded, rows), F32)],
         compiler_params=params(),
         cost_estimate=pl.CostEstimate(
@@ -277,26 +267,6 @@
         ),
         name="predict",
     )(mine, other, centers, before, high, low)
-
-
-def more_body(high_ref, low_ref, value_high_ref, value_low_ref, keep_ref, send_ref, total_ref):
-    product(high_ref, low_ref, value_high_ref[...], value_low_ref[...], total_ref, keep_ref, send_ref)
-
-
-def predict_more(high, low, value_high, value_low):
-    padded = high.shape[0]
-    count, rows = value_high.shape
-    out = jax.ShapeDtypeStruct((padded, rows // 2), F32)
-    return pl.pallas_call(
-        more_body,
-        out_shape=[out, out],
-        scratch_shapes=[pltpu.VMEM((padded, rows), F32)],
-        compiler_params=params(),
-        cost_estimate=pl.CostEstimate(
-            flops=6 * rows * count * padded, bytes_accessed=4 * padded * (count + rows), transcendentals=0
-        ),
-        name="predict_more",
-    )(high, low, value_high, value_low)
 
 
 def gather_total(mine_ref, other_ref, total_ref):
@@ -313,43 +283,16 @@
             )
 
 
-def write_rows(begin, skip, total_ref, targets_ref, weights_ref, high_ref, low_ref, new_hbm, out_hbm, new_ref, sems):
-    rows = new_ref.shape[0]
-    blocks = sems.shape[0] - 1
-    bounds = [8 * (rows // 8 * k // blocks) for k in range(blocks)] + [rows]
-    high_right = high_ref[...]
-    low_right = low_ref[...]
-    copies = [
-        pltpu.make_async_copy(
-            total_ref.at[pl.ds(skip, rows)], out_hbm.at[pl.ds(begin, rows)], sems.at[blocks]
-        )
-    ]
-    copies[0].start()
-    for k in range(blocks):
-        low_end, high_end = bounds[k : k + 2]
-        here = slice(begin + low_end, begin + high_end)
-        high, low = two(total_ref[skip + low_end : skip + high_end] - targets_ref[here])
-        new_ref[low_end:high_end] = weights_ref[here] + (
-            dot(high, high_right, NN) + (dot(high, low_right, NN) + dot(low, high_right, NN))
-        )
-        copy = pltpu.make_async_copy(
-            new_ref.at[pl.ds(low_end, high_end - low_end)],
-            new_hbm.at[pl.ds(begin + low_end, high_end - low_end)],
-            sems.at[k],
-        )
-        copy.start()
-        copies.append(copy)
-    for copy in copies:
-        copy.wait()
-
-
 def update_body(
     mine_ref, other_ref, targets_ref, index_ref, eigval_ref, spread_ref, weights_ref,
-    new_hbm, out_hbm, high_ref, low_ref, total_ref, new_ref, sems,
+    new_hbm, out_hbm, total_ref, new_ref, sems,
 ):
-    start = (lax.axis_index("center") * 2 + lax.axis_index("sub")) * spread_ref.shape[1]
     rank, count = spread_ref.shape
+    classes = new_ref.shape[0]
+    start = (lax.axis_index("center") * 2 + lax.axis_index("sub")) * count
     gather_total(mine_ref, other_ref, total_ref)
+    copies = [pltpu.make_async_copy(total_ref.at[pl.ds(rank, classes)], out_hbm, sems.at[UPDATES])]
+    copies[0].start()
     value = eigval_ref[...]
     lowest = jnp.min(value, axis=1, keepdims=True)
     scaled = (1.0 - lowest / value) / value
@@ -358,8 +301,19 @@
     turned = dot(mixed_high, spread_high, NN) + (
         dot(mixed_high, spread_low, NN) + dot(mixed_low, spread_high, NN)
     )
-    high_ref[...], low_ref[...] = two(turned - pick_rows(index_ref, count, start, F32, 0.25))
-    write_rows(0, rank, total_ref, targets_ref, weights_ref, high_ref, low_ref, new_hbm, out_hbm, new_ref, sems)
+    right_high, right_low = two(turned - pick_rows(index_ref, count, start, F32, 0.25))
+    size = classes // UPDATES
+    for k in range(UPDATES):
+        at = slice(k * size, (k + 1) * size)
+        high, low = two(total_ref[rank + k * size : rank + (k + 1) * size] - targets_ref[at])
+        new_ref[at] = weights_ref[at] + (
+            dot(high, right_high, NN) + (dot(high, right_low, NN) + dot(low, right_high, NN))
+        )
+        rows = pl.ds(k * size, size)
+        copies.append(pltpu.make_async_copy(new_ref.at[rows], new_hbm.at[rows], sems.at[k]))
+        copies[-1].start()
+    for copy in copies:
+        copy.wait()
 
 
 def update(mine, other, targets, batch_index, eigval, spread, weights):
@@ -367,68 +321,27 @@
     padded, half = mine.shape
     rows = 2 * half
     rank = spread.shape[0]
-    here = padded - rank
     vmem = pl.BlockSpec(memory_space=pltpu.VMEM)
     hbm = pl.BlockSpec(memory_space=pl.ANY)
-    right = jax.ShapeDtypeStruct((rows, count), BF16)
     return pl.pallas_call(
         update_body,
         in_specs=[vmem] * 7,
-        out_specs=[hbm, hbm, vmem, vmem],
-        out_shape=[
-            jax.ShapeDtypeStruct((classes, count), F32),
-            jax.ShapeDtypeStruct((classes, rows), F32),
-            right,
-            right,
-        ],
-        scratch_shapes=[
-            pltpu.VMEM((padded, rows), F32),
-            pltpu.VMEM((here, count), F32),
-            pltpu.SemaphoreType.DMA((4,)),
-        ],
-        compiler_params=params(),
-        cost_estimate=pl.CostEstimate(
-            flops=6 * rows * count * (here + rank), bytes_accessed=8 * here * (count + rows), transcendentals=0
-        ),
-        name="update",
-    )(mine, other, targets, batch_index, eigval, spread, weights)
-
-
-def update_more_body(
-    begin, mine_ref, other_ref, targets_ref, weights_ref, high_ref, low_ref, new_in, out_in,
-    new_hbm, out_hbm, total_ref, new_ref, sems,
-):
-    gather_total(mine_ref, other_ref, total_ref)
-    write_rows(begin, 0, total_ref, targets_ref, weights_ref, high_ref, low_ref, new_hbm, out_hbm, new_ref, sems)
-
-
-def update_more(mine, other, targets, weights, high, low, new, out, begin):
-    classes, count = weights.shape
-    padded, half = mine.shape
-    rows = 2 * half
-    here = classes - begin
-    vmem = pl.BlockSpec(memory_space=pltpu.VMEM)
-    hbm = pl.BlockSpec(memory_space=pl.ANY)
-    return pl.pallas_call(
-        functools.partial(update_more_body, begin),
-        in_specs=[vmem] * 6 + [hbm] * 2,
         out_specs=[hbm, hbm],
         out_shape=[
             jax.ShapeDtypeStruct((classes, count), F32),
             jax.ShapeDtypeStruct((classes, rows), F32),
         ],
-        input_output_aliases={6: 0, 7: 1},
         scratch_shapes=[
             pltpu.VMEM((padded, rows), F32),
-            pltpu.VMEM((here, count), F32),
-            pltpu.SemaphoreType.DMA((6,)),
+            pltpu.VMEM((classes, count), F32),
+            pltpu.SemaphoreType.DMA((UPDATES + 1,)),
         ],
         compiler_params=params(),
         cost_estimate=pl.CostEstimate(
-            flops=6 * rows * count * here, bytes_accessed=8 * here * (count + rows), transcendentals=0
-        ),
-        name="update_more",
-    )(mine, other, targets, weights, high, low, new, out)
+            flops=6 * rows * count * (classes + rank), bytes_accessed=8 * classes * (count + rows), transcendentals=0
+        ),
+        name="update",
+    )(mine, other, targets, batch_index, eigval, spread, weights)
 
 
 def swap(x, chips, level):
@@ -458,10 +371,7 @@
     classes = weights.shape[1]
     rank = eigvec.shape[1]
     unit = 8 * CHUNKS
-    units = -(-(classes + rank) // unit)
-    first = (units + 1) // 2 * unit
-    second = units * unit - first
-    begin = first - rank
+    padded = -(-(classes + rank) // unit) * unit
     batch_index = batch_index.reshape(1, rows)
     weights = weights.T
     targets = targets.T
@@ -469,15 +379,12 @@
     picked = [pick_batch(*far, part) for part in range(PARTS)]
     ready = [
         center_norms(centers),
-        *spread_weights(nys_index.reshape(1, -1), eigvec.T, weights, first, second),
+        *spread_weights(nys_index.reshape(1, -1), eigvec.T, weights, padded),
     ]
-    mine, other, norms, high1, low1, high2, low2, spread = total_of(*picked[0], chips, ready)
+    mine, other, norms, high, low, spread = total_of(*picked[0], chips, ready)
     before = distances(mine, other, centers, norms)
-    keep, send, value_high, value_low = predict(*total_of(*picked[1], chips), centers, before, high1, low1)
-    one = total_of(keep, send, chips)
-    another = total_of(*predict_more(high2, low2, value_high, value_low), chips)
-    new, out, high, low = update(*one, targets, batch_index, eigval.reshape(1, rank), spread, weights)
-    new, out = update_more(*another, targets, weights, high, low, new, out, begin)
+    parts = predict(*total_of(*picked[1], chips), centers, before, high, low)
+    new, out = update(*total_of(*parts, chips), targets, batch_index, eigval.reshape(1, rank), spread, weights)
     return new.T, out.T
 
 

time: 86.7 us -> 88.7 us (1.023)
  waiting for transfers between devices: 27.7 us -> 41.6 us
  starting transfers between devices: 40.3 us -> 29.3 us
  Pallas kernels: 16.9 us -> 15.8 us
    ppermute x28 -> x21, waiting for transfers between devices: 27.7 us -> 41.6 us  [swap(): lax.ppermute(x, AXES, [(i, i ^ flip[i & 1]) for i in range(2 * chips)])]
    ppermute x28 -> x21, starting transfers between devices: 40.3 us -> 29.3 us  [swap(): lax.ppermute(x, AXES, [(i, i ^ flip[i & 1]) for i in range(2 * chips)])]
    pallas_call x5 -> x3, Pallas kernels: 9.99 us -> 8.93 us  [the longest x1 3.93 us: predict(): pl.pallas_call(predict_body, in_specs=[vmem] * 6, out_specs=[vmem] * 2, o...]
  transfers between devices with their start and end apart: 28 -> 21, of which waited for: 15 -> 13; matrix products, arithmetic and copies ran while one was open for 1% -> 0% of each run, Pallas kernels for 11% -> 7%
where the time goes in v7:
time: 88.7 us; the launch traced here: 88.3 us
  waiting for transfers between devices  41.6 us (47%)
  starting transfers between devices  29.3 us (33%)
  Pallas kernels  15.8 us (18%)
    ppermute x21, waiting for transfers between devices, swap(): lax.ppermute(x, AXES, [(i, i ^ flip[i & 1]) for i in range(2 * chips)])  41.6 us
    ppermute x21, starting transfers between devices, swap(): lax.ppermute(x, AXES, [(i, i ^ flip[i & 1]) for i in range(2 * chips)])  29.3 us
    pallas_call x2, Pallas kernels, pick_batch(): pl.pallas_call(functools.partial(pick_body, part * depth), in_specs=[hbm,...  4.74 us
    pallas_call x1, Pallas kernels, predict(): pl.pallas_call(predict_body, in_specs=[vmem] * 6, out_specs=[vmem] * 2, o...  3.93 us
    pallas_call x1, Pallas kernels, update(): pl.pallas_call(update_body, in_specs=[vmem] * 7, out_specs=[hbm, hbm], ou...  3.46 us
  transfers between devices with their start and end apart: 21, of which 13 were waited for; matrix products, arithmetic and copies ran while one was open for 0% of the time, Pallas kernels for 7%

profile of v7, /device:TPU:1, one launch (start us, length us, event | category | flops | bytes accessed | tf_op | source)
XLA Modules:
  0.0 88.3 jit_solution(14843499043276201592)
XLA Ops:
  0.6 2.3 %pick_batch.3 = (bf16[128,1536]{1,0:T(8,128)(2,1)S(1)}, bf16[128,1536]{1,0:T(8,128)(2,1)S(1)}) custom-call(s32[1,256]{1,0:T(1,128)} %bitcast.11, bf16[768,3072]{1,0:T(8,128)(2,1)} %centers_ref.5), custom_call_target="tpu_custom_call" | custom-call | flops 603979776 | bytes 3145728 | tf_op jit(solution)/shard_map/pick_batch/pallas_call | solution.py:102
  2.9 0.0 copy-start.6
  2.9 0.0 copy-start
  3.0 0.1 collective-permute-start.7
  3.1 2.4 %pick_batch.2 = (bf16[128,1536]{1,0:T(8,128)(2,1)S(1)}, bf16[128,1536]{1,0:T(8,128)(2,1)S(1)}) custom-call(s32[1,256]{1,0:T(1,128)} %bitcast.12, bf16[768,3072]{1,0:T(8,128)(2,1)} %centers_ref.5), custom_call_target="tpu_custom_call" | custom-call | flops 603979776 | bytes 3145728 | tf_op jit(solution)/shard_map/pick_batch/pallas_call | solution.py:102
  5.5 0.6 collective-permute-start
  6.2 0.0 collective-permute-done.7
  6.2 0.0 copy-start.1
  6.2 0.0 copy-start.3
  6.2 0.1 add.40
  6.3 2.5 %collective-permute-start.8 = (bf16[64,1536]{1,0:T(8,128)(2,1)S(1)}, bf16[64,1536]{1,0:T(8,128)(2,1)S(1)}, u32[]{:S(2)}, u32[]{:S(2)}) collective-permute-start(bf16[64,1536]{1,0:T(8,128)(2,1)S(1)} %slice.53), channel_id=1, source_target_pairs={{0,2},{1,5},{2,0},{3,7},{4,6},{5,1},{6,4},{7,3},{8,10},{9,13},{10,... | collective-permute-start | bytes 589832 | tf_op jit(solution)/shard_map/ppermute | solution.py:350
  8.8 0.0 copy-done.6
  8.8 0.0 copy-done
  8.8 1.2 %center_norms.1.norm_ref = f32[768,128]{1,0:T(8,128)S(1)} custom-call(bf16[768,3072]{1,0:T(8,128)(2,1)S(1)} %copy-done), custom_call_target="tpu_custom_call" | custom-call | flops 4718592 | bytes 4718592 | tf_op jit(solution)/shard_map/center_norms/pallas_call | solution.py:166
  10.0 0.0 copy-done.1
  10.0 0.0 copy-done.3
  10.0 1.5 %spread_weights.1 = (bf16[1184,768]{1,0:T(8,128)(2,1)S(1)}, bf16[1184,768]{1,0:T(8,128)(2,1)S(1)}, f32[160,768]{1,0:T(8,128)S(1)}) custom-call(s32[1,320]{1,0:T(1,128)S(1)} %reshape.14.index_ref, f32[160,320]{1,0:T(8,128)S(1)} %bitcast.10, f32[1000,768]{1,0:T(8,128)S(1)} %bitcast.7), custom_call_target="tpu_custom_call" | custom-call | flops 235929600 | bytes 7274496 | tf_op jit(solution)/shard_map/spread_weights/pallas_call | solution.py:142
  11.5 0.0 collective-permute-done
  11.5 0.1 add.36
  11.7 0.5 collective-permute-start.1
  12.2 0.0 collective-permute-done.8
  12.2 1.4 %collective-permute-start.9 = (bf16[32,1536]{1,0:T(8,128)(2,1)S(1)}, bf16[32,1536]{1,0:T(8,128)(2,1)S(1)}, u32[]{:S(2)}, u32[]{:S(2)}) collective-permute-start(bf16[32,1536]{1,0:T(8,128)(2,1)S(1)} %slice.55), channel_id=1, source_target_pairs={{0,4},{1,3},{2,6},{3,1},{4,0},{5,7},{6,2},{7,5},{8,12},{9,11},{10,... | collective-permute-start | bytes 294920 | tf_op jit(solution)/shard_map/ppermute | solution.py:350
  13.7 2.9 %collective-permute-done.1 = bf16[64,1536]{1,0:T(8,128)(2,1)S(1)} collective-permute-done((bf16[64,1536]{1,0:T(8,128)(2,1)S(1)}, bf16[64,1536]{1,0:T(8,128)(2,1)S(1)}, u32[]{:S(2)}, u32[]{:S(2)}) %collective-permute-start.1) | collective-permute-done | bytes 196640 | tf_op jit(solution)/shard_map/ppermute | solution.py:350
  16.6 1.3 %collective-permute-start.2 = (bf16[32,1536]{1,0:T(8,128)(2,1)S(1)}, bf16[32,1536]{1,0:T(8,128)(2,1)S(1)}, u32[]{:S(2)}, u32[]{:S(2)}) collective-permute-start(bf16[32,1536]{1,0:T(8,128)(2,1)S(1)} %slice.51), channel_id=1, source_target_pairs={{0,4},{1,3},{2,6},{3,1},{4,0},{5,7},{6,2},{7,5},{8,12},{9,11},{10,... | collective-permute-start | bytes 294920 | tf_op jit(solution)/shard_map/ppermute | solution.py:350
  17.9 0.0 collective-permute-done.9
  17.9 2.4 %collective-permute-start.10 = (bf16[32,1536]{1,0:T(8,128)(2,1)S(1)}, bf16[32,1536]{1,0:T(8,128)(2,1)S(1)}, u32[]{:S(2)}, u32[]{:S(2)}) collective-permute-start(bf16[32,1536]{1,0:T(8,128)(2,1)S(1)} %slice_add_fusion.4), channel_id=1, source_target_pairs={{0,8},{1,9},{2,10},{3,11},{4,12},{5,13},{6,14},{7,15},{8,0},{9,1},... | collective-permute-start | bytes 294920 | tf_op jit(solution)/shard_map/ppermute | solution.py:350
  20.3 0.0 collective-permute-done.2
  20.3 2.2 %collective-permute-start.3 = (bf16[32,1536]{1,0:T(8,128)(2,1)S(1)}, bf16[32,1536]{1,0:T(8,128)(2,1)S(1)}, u32[]{:S(2)}, u32[]{:S(2)}) collective-permute-start(bf16[32,1536]{1,0:T(8,128)(2,1)S(1)} %slice_add_fusion.5), channel_id=1, source_target_pairs={{0,8},{1,9},{2,10},{3,11},{4,12},{5,13},{6,14},{7,15},{8,0},{9,1},... | collective-permute-start | bytes 294920 | tf_op jit(solution)/shard_map/ppermute | solution.py:350
  22.5 0.9 %collective-permute-done.10 = bf16[32,1536]{1,0:T(8,128)(2,1)S(1)} collective-permute-done((bf16[32,1536]{1,0:T(8,128)(2,1)S(1)}, bf16[32,1536]{1,0:T(8,128)(2,1)S(1)}, u32[]{:S(2)}, u32[]{:S(2)}) %collective-permute-start.10) | collective-permute-done | bytes 98336 | tf_op jit(solution)/shard_map/ppermute | solution.py:350
  23.4 0.4 collective-permute-start.11
  23.8 4.1 %collective-permute-done.3 = bf16[32,1536]{1,0:T(8,128)(2,1)S(1)} collective-permute-done((bf16[32,1536]{1,0:T(8,128)(2,1)S(1)}, bf16[32,1536]{1,0:T(8,128)(2,1)S(1)}, u32[]{:S(2)}, u32[]{:S(2)}) %collective-permute-start.3) | collective-permute-done | bytes 98336 | tf_op jit(solution)/shard_map/ppermute | solution.py:350
  27.9 1.3 %collective-permute-start.4 = (bf16[32,1536]{1,0:T(8,128)(2,1)S(1)}, bf16[32,1536]{1,0:T(8,128)(2,1)S(1)}, u32[]{:S(2)}, u32[]{:S(2)}) collective-permute-start(bf16[32,1536]{1,0:T(8,128)(2,1)S(1)} %add.39), channel_id=1, source_target_pairs={{0,4},{1,3},{2,6},{3,1},{4,0},{5,7},{6,2},{7,5},{8,12},{9,11},{10,... | collective-permute-start | bytes 294920 | tf_op jit(solution)/shard_map/ppermute | solution.py:350
  29.2 0.0 collective-permute-done.11
  29.2 0.1 collective-permute-start.12
  29.3 2.2 %collective-permute-done.4 = bf16[32,1536]{1,0:T(8,128)(2,1)S(1)} collective-permute-done((bf16[32,1536]{1,0:T(8,128)(2,1)S(1)}, bf16[32,1536]{1,0:T(8,128)(2,1)S(1)}, u32[]{:S(2)}, u32[]{:S(2)}) %collective-permute-start.4) | collective-permute-done | bytes 98336 | tf_op jit(solution)/shard_map/ppermute | solution.py:350
  31.5 0.1 collective-permute-start.5
  31.6 4.4 %collective-permute-done.12 = bf16[64,1536]{1,0:T(8,128)(2,1)S(1)} collective-permute-done((bf16[64,1536]{1,0:T(8,128)(2,1)S(1)}, bf16[64,1536]{1,0:T(8,128)(2,1)S(1)}, u32[]{:S(2)}, u32[]{:S(2)}) %collective-permute-start.12) | collective-permute-done | bytes 196640 | tf_op jit(solution)/shard_map/ppermute | solution.py:350
  36.0 4.1 %collective-permute-start.13 = (bf16[128,1536]{1,0:T(8,128)(2,1)S(1)}, bf16[128,1536]{1,0:T(8,128)(2,1)S(1)}, u32[]{:S(2)}, u32[]{:S(2)}) collective-permute-start(bf16[128,1536]{1,0:T(8,128)(2,1)S(1)} %pad_maximum_fusion.2.mine_ref), channel_id=1, source_target_pairs={{0,1},{1,0},{2,3},{3,2},{4,5},{5,4},{6,7},{7,6},{8,9},{9,8},{10,11... | collective-permute-start | bytes 1179656 | tf_op jit(solution)/shard_map/ppermute | solution.py:350
  40.1 0.0 collective-permute-done.5
  40.1 2.1 %collective-permute-start.6 = (bf16[128,1536]{1,0:T(8,128)(2,1)S(1)}, bf16[128,1536]{1,0:T(8,128)(2,1)S(1)}, u32[]{:S(2)}, u32[]{:S(2)}) collective-permute-start(bf16[128,1536]{1,0:T(8,128)(2,1)S(1)} %pad_maximum_fusion.1.mine_ref), channel_id=1, source_target_pairs={{0,1},{1,0},{2,3},{3,2},{4,5},{5,4},{6,7},{7,6},{8,9},{9,8},{10,11... | collective-permute-start | bytes 1179656 | tf_op jit(solution)/shard_map/ppermute | solution.py:350
  42.2 0.0 collective-permute-done.13.other_ref
  42.2 1.0 %distances.1.before_ref = f32[768,256]{1,0:T(8,128)S(1)} custom-call(bf16[128,1536]{1,0:T(8,128)(2,1)S(1)} %pad_maximum_fusion.2.mine_ref, bf16[128,1536]{1,0:T(8,128)(2,1)S(1)} %collective-permute-done.13.other_ref, bf16[768,3072]{1,0:T(8,128)(2,1)S(1)} %copy-done, f32[768,128]{1,0:T(8,128)S(1)} %center_norms.1.norm_ref), custom_call_target="tpu_custom_call" | custom-call | flops 603979776 | bytes 3145728 | tf_op jit(solution)/shard_map/distances/pallas_call | solution.py:235
  43.2 0.4 collective-permute-done.6.other_ref
  43.5 3.9 %predict.1 = (f32[1184,128]{1,0:T(8,128)S(1)}, f32[1184,128]{1,0:T(8,128)S(1)}) custom-call(bf16[128,1536]{1,0:T(8,128)(2,1)S(1)} %pad_maximum_fusion.1.mine_ref, bf16[128,1536]{1,0:T(8,128)(2,1)S(1)} %collective-permute-done.6.other_ref, bf16[768,3072]{1,0:T(8,128)(2,1)S(1)} %copy-done, f32[768,256]{1,0:T(8,128)S(1)} %distances.1.before_ref, ...), custom_call_target="tpu_custom_call" | custom-call | flops 2000683008 | bytes 7995392 | tf_op jit(solution)/shard_map/predict/pallas_call | solution.py:256
  47.5 0.4 collective-permute-start.14
  47.9 1.7 %collective-permute-done.14 = f32[1184,128]{1,0:T(8,128)S(1)} collective-permute-done((f32[1184,128]{1,0:T(8,128)S(1)}, f32[1184,128]{1,0:T(8,128)S(1)}, u32[]{:S(2)}, u32[]{:S(2)}) %collective-permute-start.14) | collective-permute-done | bytes 606240 | tf_op jit(solution)/shard_map/ppermute | solution.py:350
  49.6 0.0 copy-start.2
  49.6 0.1 add.44
  49.7 0.9 %collective-permute-start.15 = (f32[592,128]{1,0:T(8,128)S(1)}, f32[592,128]{1,0:T(8,128)S(1)}, u32[]{:S(2)}, u32[]{:S(2)}) collective-permute-start(f32[592,128]{1,0:T(8,128)S(1)} %slice.57), channel_id=1, source_target_pairs={{0,2},{1,5},{2,0},{3,7},{4,6},{5,1},{6,4},{7,3},{8,10},{9,13},{10,... | collective-permute-start | bytes 909320 | tf_op jit(solution)/shard_map/ppermute | solution.py:350
  50.6 5.1 %collective-permute-done.15 = f32[592,128]{1,0:T(8,128)S(1)} collective-permute-done((f32[592,128]{1,0:T(8,128)S(1)}, f32[592,128]{1,0:T(8,128)S(1)}, u32[]{:S(2)}, u32[]{:S(2)}) %collective-permute-start.15) | collective-permute-done | bytes 303136 | tf_op jit(solution)/shard_map/ppermute | solution.py:350
  55.8 1.2 %collective-permute-start.16 = (f32[296,128]{1,0:T(8,128)S(1)}, f32[296,128]{1,0:T(8,128)S(1)}, u32[]{:S(2)}, u32[]{:S(2)}) collective-permute-start(f32[296,128]{1,0:T(8,128)S(1)} %slice.59), channel_id=1, source_target_pairs={{0,4},{1,3},{2,6},{3,1},{4,0},{5,7},{6,2},{7,5},{8,12},{9,11},{10,... | collective-permute-start | bytes 454664 | tf_op jit(solution)/shard_map/ppermute | solution.py:350
  57.0 2.9 %collective-permute-done.16 = f32[296,128]{1,0:T(8,128)S(1)} collective-permute-done((f32[296,128]{1,0:T(8,128)S(1)}, f32[296,128]{1,0:T(8,128)S(1)}, u32[]{:S(2)}, u32[]{:S(2)}) %collective-permute-start.16) | collective-permute-done | bytes 151584 | tf_op jit(solution)/shard_map/ppermute | solution.py:350
  59.9 2.8 %collective-permute-start.17 = (f32[296,128]{1,0:T(8,128)S(1)}, f32[296,128]{1,0:T(8,128)S(1)}, u32[]{:S(2)}, u32[]{:S(2)}) collective-permute-start(f32[296,128]{1,0:T(8,128)S(1)} %slice_add_fusion.3), channel_id=1, source_target_pairs={{0,8},{1,9},{2,10},{3,11},{4,12},{5,13},{6,14},{7,15},{8,0},{9,1},... | collective-permute-start | bytes 454664 | tf_op jit(solution)/shard_map/ppermute | solution.py:350
  62.7 6.7 %collective-permute-done.17 = f32[296,128]{1,0:T(8,128)S(1)} collective-permute-done((f32[296,128]{1,0:T(8,128)S(1)}, f32[296,128]{1,0:T(8,128)S(1)}, u32[]{:S(2)}, u32[]{:S(2)}) %collective-permute-start.17) | collective-permute-done | bytes 151584 | tf_op jit(solution)/shard_map/ppermute | solution.py:350
  69.4 0.6 collective-permute-start.18
  70.0 3.5 %collective-permute-done.18 = f32[296,128]{1,0:T(8,128)S(1)} collective-permute-done((f32[296,128]{1,0:T(8,128)S(1)}, f32[296,128]{1,0:T(8,128)S(1)}, u32[]{:S(2)}, u32[]{:S(2)}) %collective-permute-start.18) | collective-permute-done | bytes 151584 | tf_op jit(solution)/shard_map/ppermute | solution.py:350
  73.6 0.7 collective-permute-start.19
  74.3 5.3 %collective-permute-done.19 = f32[592,128]{1,0:T(8,128)S(1)} collective-permute-done((f32[592,128]{1,0:T(8,128)S(1)}, f32[592,128]{1,0:T(8,128)S(1)}, u32[]{:S(2)}, u32[]{:S(2)}) %collective-permute-start.19) | collective-permute-done | bytes 303136 | tf_op jit(solution)/shard_map/ppermute | solution.py:350
  79.6 3.5 %collective-permute-start.20 = (f32[1184,128]{1,0:T(8,128)S(1)}, f32[1184,128]{1,0:T(8,128)S(1)}, u32[]{:S(2)}, u32[]{:S(2)}) collective-permute-start(f32[1184,128]{1,0:T(8,128)S(1)} %pad_maximum_fusion.mine_ref), channel_id=1, source_target_pairs={{0,1},{1,0},{2,3},{3,2},{4,5},{5,4},{6,7},{7,6},{8,9},{9,8},{10,11... | collective-permute-start | bytes 1818632 | tf_op jit(solution)/shard_map/ppermute | solution.py:350
  83.1 1.7 %collective-permute-done.20.other_ref = f32[1184,128]{1,0:T(8,128)S(1)} collective-permute-done((f32[1184,128]{1,0:T(8,128)S(1)}, f32[1184,128]{1,0:T(8,128)S(1)}, u32[]{:S(2)}, u32[]{:S(2)}) %collective-permute-start.20) | collective-permute-done | bytes 606240 | tf_op jit(solution)/shard_map/ppermute | solution.py:350
  84.8 0.0 copy-done.2
  84.8 0.0 copy-done.4
  84.8 0.0 copy-done.5
  84.8 3.5 %update.1 = (f32[1000,768]{1,0:T(8,128)}, f32[1000,256]{1,0:T(8,128)}) custom-call(f32[1184,128]{1,0:T(8,128)S(1)} %pad_maximum_fusion.mine_ref, f32[1184,128]{1,0:T(8,128)S(1)} %collective-permute-done.20.other_ref, f32[1000,256]{1,0:T(8,128)S(1)} %bitcast.9, s32[1,256]{1,0:T(1,128)S(1)} %bitcast.13, f32[1,160]{1,0:T(1,128)S(1)} %bitcast.14, ...), custom_call_target="tpu_custom_call" | custom-call | flops 1368391680 | bytes 8192000 | tf_op jit(solution)/shard_map/update/pallas_call | solution.py:326
  (24 shorter events, 0.4 us)
Async XLA Ops:
  2.9 5.9 %copy-start.6 = (s32[320]{0:T(512)S(1)}, s32[320]{0:T(512)}, u32[]{:S(2)}) copy-start(s32[320]{0:T(512)} %param.11) | copy-start | bytes 3844
  2.9 5.9 %copy-start = (bf16[768,3072]{1,0:T(8,128)(2,1)S(1)}, bf16[768,3072]{1,0:T(8,128)(2,1)}, u32[]{:S(2)}) copy-start(bf16[768,3072]{1,0:T(8,128)(2,1)} %centers_ref.5) | copy-start | bytes 14155780
  3.0 3.2 %collective-permute-start.7 = (bf16[128,1536]{1,0:T(8,128)(2,1)S(1)}, bf16[128,1536]{1,0:T(8,128)(2,1)S(1)}, u32[]{:S(2)}, u32[]{:S(2)}) collective-permute-start(bf16[128,1536]{1,0:T(8,128)(2,1)S(1)} %get-tuple-element.21), channel_id=1, source_target_pairs={{0,1},{1,0},{2,3},{3,2},{4,5},{5,4},{6,7},{7,6},{8,9},{9,8},{10,11... | collective-permute-start | bytes 1179656 | tf_op jit(solution)/shard_map/ppermute | solution.py:350
  5.5 6.0 %collective-permute-start = (bf16[128,1536]{1,0:T(8,128)(2,1)S(1)}, bf16[128,1536]{1,0:T(8,128)(2,1)S(1)}, u32[]{:S(2)}, u32[]{:S(2)}) collective-permute-start(bf16[128,1536]{1,0:T(8,128)(2,1)S(1)} %get-tuple-element.19), channel_id=1, source_target_pairs={{0,1},{1,0},{2,3},{3,2},{4,5},{5,4},{6,7},{7,6},{8,9},{9,8},{10,11... | collective-permute-start | bytes 1179656 | tf_op jit(solution)/shard_map/ppermute | solution.py:350
  6.2 3.8 %copy-start.1 = (f32[768,1000]{0,1:T(8,128)S(1)}, f32[768,1000]{0,1:T(8,128)}, u32[]{:S(2)}) copy-start(f32[768,1000]{0,1:T(8,128)} %param.8) | copy-start | bytes 9216004
  6.2 3.8 %copy-start.3 = (f32[320,160]{0,1:T(8,128)S(1)}, f32[320,160]{0,1:T(8,128)}, u32[]{:S(2)}) copy-start(f32[320,160]{0,1:T(8,128)} %param.12) | copy-start | bytes 614404
  6.3 5.9 %collective-permute-start.8 = (bf16[64,1536]{1,0:T(8,128)(2,1)S(1)}, bf16[64,1536]{1,0:T(8,128)(2,1)S(1)}, u32[]{:S(2)}, u32[]{:S(2)}) collective-permute-start(bf16[64,1536]{1,0:T(8,128)(2,1)S(1)} %slice.53), channel_id=1, source_target_pairs={{0,2},{1,5},{2,0},{3,7},{4,6},{5,1},{6,4},{7,3},{8,10},{9,13},{10,... | collective-permute-start | bytes 589832 | tf_op jit(solution)/shard_map/ppermute | solution.py:350
  11.7 4.9 %collective-permute-start.1 = (bf16[64,1536]{1,0:T(8,128)(2,1)S(1)}, bf16[64,1536]{1,0:T(8,128)(2,1)S(1)}, u32[]{:S(2)}, u32[]{:S(2)}) collective-permute-start(bf16[64,1536]{1,0:T(8,128)(2,1)S(1)} %slice.49), channel_id=1, source_target_pairs={{0,2},{1,5},{2,0},{3,7},{4,6},{5,1},{6,4},{7,3},{8,10},{9,13},{10,... | collective-permute-start | bytes 589832 | tf_op jit(solution)/shard_map/ppermute | solution.py:350
  12.2 5.6 %collective-permute-start.9 = (bf16[32,1536]{1,0:T(8,128)(2,1)S(1)}, bf16[32,1536]{1,0:T(8,128)(2,1)S(1)}, u32[]{:S(2)}, u32[]{:S(2)}) collective-permute-start(bf16[32,1536]{1,0:T(8,128)(2,1)S(1)} %slice.55), channel_id=1, source_target_pairs={{0,4},{1,3},{2,6},{3,1},{4,0},{5,7},{6,2},{7,5},{8,12},{9,11},{10,... | collective-permute-start | bytes 294920 | tf_op jit(solution)/shard_map/ppermute | solution.py:350
  16.6 3.7 %collective-permute-start.2 = (bf16[32,1536]{1,0:T(8,128)(2,1)S(1)}, bf16[32,1536]{1,0:T(8,128)(2,1)S(1)}, u32[]{:S(2)}, u32[]{:S(2)}) collective-permute-start(bf16[32,1536]{1,0:T(8,128)(2,1)S(1)} %slice.51), channel_id=1, source_target_pairs={{0,4},{1,3},{2,6},{3,1},{4,0},{5,7},{6,2},{7,5},{8,12},{9,11},{10,... | collective-permute-start | bytes 294920 | tf_op jit(solution)/shard_map/ppermute | solution.py:350
  17.9 5.5 %collective-permute-start.10 = (bf16[32,1536]{1,0:T(8,128)(2,1)S(1)}, bf16[32,1536]{1,0:T(8,128)(2,1)S(1)}, u32[]{:S(2)}, u32[]{:S(2)}) collective-permute-start(bf16[32,1536]{1,0:T(8,128)(2,1)S(1)} %slice_add_fusion.4), channel_id=1, source_target_pairs={{0,8},{1,9},{2,10},{3,11},{4,12},{5,13},{6,14},{7,15},{8,0},{9,1},... | collective-permute-start | bytes 294920 | tf_op jit(solution)/shard_map/ppermute | solution.py:350
  20.3 7.6 %collective-permute-start.3 = (bf16[32,1536]{1,0:T(8,128)(2,1)S(1)}, bf16[32,1536]{1,0:T(8,128)(2,1)S(1)}, u32[]{:S(2)}, u32[]{:S(2)}) collective-permute-start(bf16[32,1536]{1,0:T(8,128)(2,1)S(1)} %slice_add_fusion.5), channel_id=1, source_target_pairs={{0,8},{1,9},{2,10},{3,11},{4,12},{5,13},{6,14},{7,15},{8,0},{9,1},... | collective-permute-start | bytes 294920 | tf_op jit(solution)/shard_map/ppermute | solution.py:350
  23.4 5.8 %collective-permute-start.11 = (bf16[32,1536]{1,0:T(8,128)(2,1)S(1)}, bf16[32,1536]{1,0:T(8,128)(2,1)S(1)}, u32[]{:S(2)}, u32[]{:S(2)}) collective-permute-start(bf16[32,1536]{1,0:T(8,128)(2,1)S(1)} %add.43), channel_id=1, source_target_pairs={{0,4},{1,3},{2,6},{3,1},{4,0},{5,7},{6,2},{7,5},{8,12},{9,11},{10,... | collective-permute-start | bytes 294920 | tf_op jit(solution)/shard_map/ppermute | solution.py:350
  27.9 3.5 %collective-permute-start.4 = (bf16[32,1536]{1,0:T(8,128)(2,1)S(1)}, bf16[32,1536]{1,0:T(8,128)(2,1)S(1)}, u32[]{:S(2)}, u32[]{:S(2)}) collective-permute-start(bf16[32,1536]{1,0:T(8,128)(2,1)S(1)} %add.39), channel_id=1, source_target_pairs={{0,4},{1,3},{2,6},{3,1},{4,0},{5,7},{6,2},{7,5},{8,12},{9,11},{10,... | collective-permute-start | bytes 294920 | tf_op jit(solution)/shard_map/ppermute | solution.py:350
  29.2 6.7 %collective-permute-start.12 = (bf16[64,1536]{1,0:T(8,128)(2,1)S(1)}, bf16[64,1536]{1,0:T(8,128)(2,1)S(1)}, u32[]{:S(2)}, u32[]{:S(2)}) collective-permute-start(bf16[64,1536]{1,0:T(8,128)(2,1)S(1)} %pad_maximum_fusion.5), channel_id=1, source_target_pairs={{0,2},{1,5},{2,0},{3,7},{4,6},{5,1},{6,4},{7,3},{8,10},{9,13},{10,... | collective-permute-start | bytes 589832 | tf_op jit(solution)/shard_map/ppermute | solution.py:350
  31.5 8.6 %collective-permute-start.5 = (bf16[64,1536]{1,0:T(8,128)(2,1)S(1)}, bf16[64,1536]{1,0:T(8,128)(2,1)S(1)}, u32[]{:S(2)}, u32[]{:S(2)}) collective-permute-start(bf16[64,1536]{1,0:T(8,128)(2,1)S(1)} %pad_maximum_fusion.4), channel_id=1, source_target_pairs={{0,2},{1,5},{2,0},{3,7},{4,6},{5,1},{6,4},{7,3},{8,10},{9,13},{10,... | collective-permute-start | bytes 589832 | tf_op jit(solution)/shard_map/ppermute | solution.py:350
  36.0 6.2 %collective-permute-start.13 = (bf16[128,1536]{1,0:T(8,128)(2,1)S(1)}, bf16[128,1536]{1,0:T(8,128)(2,1)S(1)}, u32[]{:S(2)}, u32[]{:S(2)}) collective-permute-start(bf16[128,1536]{1,0:T(8,128)(2,1)S(1)} %pad_maximum_fusion.2.mine_ref), channel_id=1, source_target_pairs={{0,1},{1,0},{2,3},{3,2},{4,5},{5,4},{6,7},{7,6},{8,9},{9,8},{10,11... | collective-permute-start | bytes 1179656 | tf_op jit(solution)/shard_map/ppermute | solution.py:350
  40.1 3.4 %collective-permute-start.6 = (bf16[128,1536]{1,0:T(8,128)(2,1)S(1)}, bf16[128,1536]{1,0:T(8,128)(2,1)S(1)}, u32[]{:S(2)}, u32[]{:S(2)}) collective-permute-start(bf16[128,1536]{1,0:T(8,128)(2,1)S(1)} %pad_maximum_fusion.1.mine_ref), channel_id=1, source_target_pairs={{0,1},{1,0},{2,3},{3,2},{4,5},{5,4},{6,7},{7,6},{8,9},{9,8},{10,11... | collective-permute-start | bytes 1179656 | tf_op jit(solution)/shard_map/ppermute | solution.py:350
  47.5 2.1 %collective-permute-start.14 = (f32[1184,128]{1,0:T(8,128)S(1)}, f32[1184,128]{1,0:T(8,128)S(1)}, u32[]{:S(2)}, u32[]{:S(2)}) collective-permute-start(f32[1184,128]{1,0:T(8,128)S(1)} %get-tuple-element.30), channel_id=1, source_target_pairs={{0,1},{1,0},{2,3},{3,2},{4,5},{5,4},{6,7},{7,6},{8,9},{9,8},{10,11... | collective-permute-start | bytes 1818632 | tf_op jit(solution)/shard_map/ppermute | solution.py:350
  49.6 35.2 %copy-start.2 = (f32[256,1000]{0,1:T(8,128)S(1)}, f32[256,1000]{0,1:T(8,128)}, u32[]{:S(2)}) copy-start(f32[256,1000]{0,1:T(8,128)} %param.9) | copy-start | bytes 3072004
  49.6 35.2 %copy-start.4 = (s32[256]{0:T(256)S(1)}, s32[256]{0:T(256)}, u32[]{:S(2)}) copy-start(s32[256]{0:T(256)} %param.10) | copy-start | bytes 3076
  49.6 35.2 %copy-start.5 = (f32[160]{0:T(256)S(1)}, f32[160]{0:T(256)}, u32[]{:S(2)}) copy-start(f32[160]{0:T(256)} %param.13) | copy-start | bytes 1924
  49.7 6.0 %collective-permute-start.15 = (f32[592,128]{1,0:T(8,128)S(1)}, f32[592,128]{1,0:T(8,128)S(1)}, u32[]{:S(2)}, u32[]{:S(2)}) collective-permute-start(f32[592,128]{1,0:T(8,128)S(1)} %slice.57), channel_id=1, source_target_pairs={{0,2},{1,5},{2,0},{3,7},{4,6},{5,1},{6,4},{7,3},{8,10},{9,13},{10,... | collective-permute-start | bytes 909320 | tf_op jit(solution)/shard_map/ppermute | solution.py:350
  55.8 4.1 %collective-permute-start.16 = (f32[296,128]{1,0:T(8,128)S(1)}, f32[296,128]{1,0:T(8,128)S(1)}, u32[]{:S(2)}, u32[]{:S(2)}) collective-permute-start(f32[296,128]{1,0:T(8,128)S(1)} %slice.59), channel_id=1, source_target_pairs={{0,4},{1,3},{2,6},{3,1},{4,0},{5,7},{6,2},{7,5},{8,12},{9,11},{10,... | collective-permute-start | bytes 454664 | tf_op jit(solution)/shard_map/ppermute | solution.py:350
  59.9 9.5 %collective-permute-start.17 = (f32[296,128]{1,0:T(8,128)S(1)}, f32[296,128]{1,0:T(8,128)S(1)}, u32[]{:S(2)}, u32[]{:S(2)}) collective-permute-start(f32[296,128]{1,0:T(8,128)S(1)} %slice_add_fusion.3), channel_id=1, source_target_pairs={{0,8},{1,9},{2,10},{3,11},{4,12},{5,13},{6,14},{7,15},{8,0},{9,1},... | collective-permute-start | bytes 454664 | tf_op jit(solution)/shard_map/ppermute | solution.py:350
  69.4 4.1 %collective-permute-start.18 = (f32[296,128]{1,0:T(8,128)S(1)}, f32[296,128]{1,0:T(8,128)S(1)}, u32[]{:S(2)}, u32[]{:S(2)}) collective-permute-start(f32[296,128]{1,0:T(8,128)S(1)} %add.47), channel_id=1, source_target_pairs={{0,4},{1,3},{2,6},{3,1},{4,0},{5,7},{6,2},{7,5},{8,12},{9,11},{10,... | collective-permute-start | bytes 454664 | tf_op jit(solution)/shard_map/ppermute | solution.py:350
  73.6 6.0 %collective-permute-start.19 = (f32[592,128]{1,0:T(8,128)S(1)}, f32[592,128]{1,0:T(8,128)S(1)}, u32[]{:S(2)}, u32[]{:S(2)}) collective-permute-start(f32[592,128]{1,0:T(8,128)S(1)} %pad_maximum_fusion.3), channel_id=1, source_target_pairs={{0,2},{1,5},{2,0},{3,7},{4,6},{5,1},{6,4},{7,3},{8,10},{9,13},{10,... | collective-permute-start | bytes 909320 | tf_op jit(solution)/shard_map/ppermute | solution.py:350
  79.6 5.2 %collective-permute-start.20 = (f32[1184,128]{1,0:T(8,128)S(1)}, f32[1184,128]{1,0:T(8,128)S(1)}, u32[]{:S(2)}, u32[]{:S(2)}) collective-permute-start(f32[1184,128]{1,0:T(8,128)S(1)} %pad_maximum_fusion.mine_ref), channel_id=1, source_target_pairs={{0,1},{1,0},{2,3},{3,2},{4,5},{5,4},{6,7},{7,6},{8,9},{9,8},{10,11... | collective-permute-start | bytes 1818632 | tf_op jit(solution)/shard_map/ppermute | solution.py:350

commit v8 on v6

--- a/solution.py
+++ b/solution.py
@@ -15,6 +15,7 @@
 CHUNKS = 1 << HALVINGS
 LANE = 128
 PARTS = 2
+SLOTS = 32
 NT = (((1,), (1,)), ((), ()))
 NN = (((1,), (0,)), ((), ()))
 VMEM_LIMIT = 24 * 1024 * 1024
@@ -27,6 +28,11 @@
 def walk(sub, bits):
     order = list(range(bits))
     return order if sub == 0 else order[1::-1] + order[2:]
+
+
+def far_first(sub, bits):
+    order = list(range(bits))[::-1]
+    return order if sub == 0 else order[:-2] + order[:-3:-1]
 
 
 def turns():
@@ -117,6 +123,58 @@
     )(batch_index, centers)
 
 
+def pack_body(first, index_hbm, rank_hbm, centers_hbm, out_ref, index_ref, rank_ref, centers_ref, sems):
+    blocks, count, block = centers_ref.shape
+    rows = index_ref.shape[1]
+    copies = [
+        pltpu.make_async_copy(index_hbm, index_ref, sems.at[blocks]),
+        pltpu.make_async_copy(rank_hbm, rank_ref, sems.at[blocks + 1]),
+    ] + [
+        pltpu.make_async_copy(
+            centers_hbm.at[:, pl.ds(first + k * block, block)], centers_ref.at[k], sems.at[k]
+        )
+        for k in range(blocks)
+    ]
+    for copy in copies:
+        copy.start()
+    copies[0].wait()
+    copies[1].wait()
+    start = (lax.axis_index("center") * 2 + lax.axis_index("sub")) * count
+    local = index_ref[...] - start
+    rank = jnp.where((local >= 0) & (local < count), rank_ref[...], -1)
+    slots = lax.broadcasted_iota(jnp.int32, (SLOTS, rows), 0)
+    to_slot = jnp.where(slots == rank, 1.0, 0.0).astype(BF16)
+    pick = dot(to_slot, pick_rows(index_ref, count, start, BF16, 1.0), NN).astype(BF16)
+    for k in range(blocks):
+        copies[k + 2].wait()
+        out_ref[:, k * block : (k + 1) * block] = dot(pick, centers_ref[k], NN).astype(BF16)
+
+
+def pack_rows(batch_index, rank, centers, part):
+    rows = batch_index.shape[1]
+    count, depth = centers.shape
+    depth = depth // PARTS
+    block = 512
+    hbm = pl.BlockSpec(memory_space=pltpu.HBM)
+    return pl.pallas_call(
+        functools.partial(pack_body, part * depth),
+        in_specs=[hbm, hbm, hbm],
+        out_specs=pl.BlockSpec(memory_space=pltpu.VMEM),
+        out_shape=jax.ShapeDtypeStruct((SLOTS, depth), BF16),
+        scratch_shapes=[
+            pltpu.VMEM((1, rows), jnp.int32),
+            pltpu.VMEM((1, rows), jnp.int32),
+            pltpu.VMEM((depth // block, count, block), BF16),
+            pltpu.SemaphoreType.DMA((depth // block + 2,)),
+        ],
+        compiler_params=params(),
+        cost_estimate=pl.CostEstimate(
+            flops=2 * SLOTS * count * depth, bytes_accessed=2 * depth * (count + SLOTS), transcendentals=0
+        ),
+        name="pack_rows",
+    )(batch_index, rank, centers)
+
+
 def spread_body(
     first, classes, index_ref, eigvec_ref, weights_ref,
     high1_ref, low1_ref, high2_ref, low2_ref, spread_ref, all_ref,
@@ -182,16 +240,10 @@
     )(centers)
 
 
-def gather_batch(mine_ref, other_ref, batch_ref):
-    lower = lax.axis_index("sub") == 0
+def gather_batch(mine_ref, other_ref, select_ref, batch_ref):
     half = mine_ref.shape[0]
-    size = half // CHUNKS
-    for part, turn in enumerate(turns()):
-        for chunk in range(CHUNKS):
-            at = slice(chunk * size, (chunk + 1) * size)
-            same = lower if part == 0 else jnp.logical_not(lower)
-            to = pl.multiple_of(part * half + (chunk ^ turn) * size, size)
-            batch_ref[pl.ds(to, size), :] = jnp.where(same, mine_ref[at], other_ref[at])
+    found = dot(select_ref[:, :half], mine_ref[...], NN) + dot(select_ref[:, half:], other_ref[...], NN)
+    batch_ref[...] = found.astype(BF16)
 
 
 def nearer(first, centers_ref, batch_ref):
@@ -218,17 +270,17 @@
         send_ref[at] = jnp.where(lower, second, first)
 
 
-def distance_body(mine_ref, other_ref, centers_ref, norm_ref, total_ref, batch_ref):
-    gather_batch(mine_ref, other_ref, batch_ref)
+def distance_body(mine_ref, other_ref, select_ref, centers_ref, norm_ref, total_ref, batch_ref):
+    gather_batch(mine_ref, other_ref, select_ref, batch_ref)
     total_ref[...] = norm_ref[:, 0:1] + nearer(0, centers_ref, batch_ref)
 
 
 def predict_body(
-    mine_ref, other_ref, centers_ref, before_ref, high_ref, low_ref,
+    mine_ref, other_ref, select_ref, centers_ref, before_ref, high_ref, low_ref,
     keep_ref, send_ref, value_high_ref, value_low_ref, batch_ref, total_ref,
 ):
     depth = centers_ref.shape[1]
-    gather_batch(mine_ref, other_ref, batch_ref)
+    gather_batch(mine_ref, other_ref, select_ref, batch_ref)
     square = jnp.maximum(before_ref[...] + nearer(depth - batch_ref.shape[1], centers_ref, batch_ref), 0.0)
     value_high, value_low = two(jnp.exp(jnp.sqrt(square) * (-1.0 / math.sqrt(depth))))
     value_high_ref[...] = value_high
@@ -236,14 +288,14 @@
     product(high_ref, low_ref, value_high, value_low, total_ref, keep_ref, send_ref)
 
 
-def distances(mine, other, centers, norms):
-    half, depth = mine.shape
-    rows = 2 * half
+def distances(mine, other, select, centers, norms):
+    depth = mine.shape[1]
+    rows = select.shape[0]
     count = centers.shape[0]
     vmem = pl.BlockSpec(memory_space=pltpu.VMEM)
     return pl.pallas_call(
         distance_body,
-        in_specs=[vmem] * 4,
+        in_specs=[vmem] * 5,
         out_specs=vmem,
         out_shape=jax.ShapeDtypeStruct((count, rows), F32),
         scratch_shapes=[pltpu.VMEM((rows, depth), BF16)],
@@ -252,12 +304,13 @@
             flops=2 * rows * count * depth, bytes_accessed=2 * depth * (count + rows), transcendentals=0
         ),
         name="distances",
-    )(mine, other, centers, norms)
-
-
-def predict(mine, other, centers, before, high, low):
-    half, depth = mine.shape
-    rows = 2 * half
+    )(mine, other, select, centers, norms)
+
+
+def predict(mine, other, select, centers, before, high, low):
+    depth = mine.shape[1]
+    rows = select.shape[0]
+    half = rows // 2
     count = centers.shape[0]
     padded = high.shape[0]
     out = jax.ShapeDtypeStruct((padded, half), F32)
@@ -265,7 +318,7 @@
     vmem = pl.BlockSpec(memory_space=pltpu.VMEM)
     return pl.pallas_call(
         predict_body,
-        in_specs=[vmem] * 6,
+        in_specs=[vmem] * 7,
         out_specs=[vmem] * 4,
         out_shape=[out, out, value, value],
         scratch_shapes=[pltpu.VMEM((rows, depth), BF16), pltpu.VMEM((padded, rows), F32)],
@@ -276,7 +329,7 @@
             transcendentals=2 * rows * count,
         ),
         name="predict",
-    )(mine, other, centers, before, high, low)
+    )(mine, other, select, centers, before, high, low)
 
 
 def more_body(high_ref, low_ref, value_high_ref, value_low_ref, keep_ref, send_ref, total_ref):
@@ -431,53 +484,113 @@
     )(mine, other, targets, weights, high, low, new, out)
 
 
-def swap(x, chips, level):
-    bits = chips.bit_length() - 1
-    flip = [1, 1] if level < 0 else [2 << walk(sub, bits)[level] for sub in range(2)]
+def swap(x, chips, order=None, level=0):
+    flip = [2 << order(sub, chips.bit_length() - 1)[level] if order else 1 for sub in range(2)]
     return lax.ppermute(x, AXES, [(i, i ^ flip[i & 1]) for i in range(2 * chips)])
 
 
+def tie(x, tied):
+    x, *tied = lax.optimization_barrier((x, *tied))
+    return x, tied
+
+
 def total_of(keep, send, chips, tied=()):
-    keep = keep + swap(send, chips, -1)
+    keep = keep + swap(send, chips)
     for level in range(chips.bit_length() - 1):
         if level >= HALVINGS:
-            keep = keep + swap(keep, chips, level)
+            keep = keep + swap(keep, chips, walk, level)
             continue
         half = keep.shape[0] // 2
         keep, send = keep[:half], keep[half:]
         if level == 1 and tied:
-            send, *tied = lax.optimization_barrier((send, *tied))
-        keep = keep + swap(send, chips, level)
+            send, tied = tie(send, tied)
+        keep = keep + swap(send, chips, walk, level)
     for level in reversed(range(HALVINGS)):
-        keep = jnp.concatenate([keep, swap(keep, chips, level)])
-    return [keep, swap(keep, chips, -1), *tied]
-
-
-def on_device(chips, centers, weights, targets, batch_index, nys_index, eigvec, eigval):
-    rows = batch_index.shape[0]
-    classes = weights.shape[1]
-    rank = eigvec.shape[1]
+        keep = jnp.concatenate([keep, swap(keep, chips, walk, level)])
+    return [keep, swap(keep, chips), *tied]
+
+
+def all_of(keep, chips, tied=()):
+    for level in range(chips.bit_length() - 1):
+        if level == 1 and tied:
+            keep, tied = tie(keep, tied)
+        keep = jnp.concatenate([keep, swap(keep, chips, far_first, level)])
+    return [keep, swap(keep, chips), *tied]
+
+
+def one_hot(slot, slots):
+    return (slot[:, None] == jnp.arange(slots, dtype=jnp.int32)[None, :]).astype(BF16)
+
+
+def select_summed(rows):
+    row = jnp.arange(rows, dtype=jnp.int32)
+    half = rows // 2
+    size = half // CHUNKS
+    turn = jnp.stack(turns())[row // half]
+    chunk = (row % half // size) ^ turn
+    far = jnp.where(row // half == lax.axis_index("sub"), 0, half)
+    return one_hot(far + chunk * size + row % size, rows)
+
+
+def select_packed(owner, rank, chips):
+    away = (owner >> 1) ^ lax.axis_index("center")
+    places = [
+        sum(((away >> bit) & 1) << k for k, bit in enumerate(far_first(sub, chips.bit_length() - 1)))
+        for sub in range(2)
+    ]
+    place = jnp.where(owner & 1 == 0, *places)
+    far = jnp.where(owner & 1 == lax.axis_index("sub"), 0, chips * SLOTS)
+    return one_hot(far + place * SLOTS + rank, 2 * chips * SLOTS)
+
+
+def step(packed, chips, owner, rank, centers, weights, targets, batch_index, nys_index, eigvec, eigval):
+    rows = batch_index.shape[1]
+    classes, count = weights.shape
+    depth = eigvec.shape[0]
     unit = 8 * CHUNKS
-    units = -(-(classes + rank) // unit)
+    units = -(-(classes + depth) // unit)
     first = (units + 1) // 2 * unit
     second = units * unit - first
-    begin = first - rank
-    batch_index = batch_index.reshape(1, rows)
-    weights = weights.T
-    targets = targets.T
     far = [pltpu.with_memory_space_constraint(x, pltpu.HBM) for x in (batch_index, centers)]
-    picked = [pick_batch(*far, part) for part in range(PARTS)]
-    ready = [
-        center_norms(centers),
-        *spread_weights(nys_index.reshape(1, -1), eigvec.T, weights, first, second),
-    ]
-    mine, other, norms, high1, low1, high2, low2, spread = total_of(*picked[0], chips, ready)
-    before = distances(mine, other, centers, norms)
-    keep, send, value_high, value_low = predict(*total_of(*picked[1], chips), centers, before, high1, low1)
+    ready = [center_norms(centers), *spread_weights(nys_index, eigvec, weights, first, second)]
+    if packed:
+        rank_row = rank.reshape(1, rows)
+        ready.append(select_packed(owner, rank, chips))
+        slots = [pack_rows(far[0], rank_row, far[1], part) for part in range(PARTS)]
+        mine, other, norms, high1, low1, high2, low2, spread, select = all_of(slots[0], chips, ready)
+        late = all_of(slots[1], chips)
+    else:
+        ready.append(select_summed(rows))
+        picked = [pick_batch(*far, part) for part in range(PARTS)]
+        mine, other, norms, high1, low1, high2, low2, spread, select = total_of(*picked[0], chips, ready)
+        late = total_of(*picked[1], chips)
+    before = distances(mine, other, select, centers, norms)
+    keep, send, value_high, value_low = predict(*late, select, centers, before, high1, low1)
     one = total_of(keep, send, chips)
     another = total_of(*predict_more(high2, low2, value_high, value_low), chips)
-    new, out, high, low = update(*one, targets, batch_index, eigval.reshape(1, rank), spread, weights)
-    new, out = update_more(*another, targets, weights, high, low, new, out, begin)
+    new, out, high, low = update(*one, targets, batch_index, eigval, spread, weights)
+    return update_more(*another, targets, weights, high, low, new, out, first - depth)
+
+
+def on_device(chips, centers, weights, targets, batch_index, nys_index, eigvec, eigval):
+    row = jnp.arange(batch_index.shape[0], dtype=jnp.int32)
+    owner = batch_index // centers.shape[0]
+    earlier = (owner[None, :] == owner[:, None]) & (row[None, :] < row[:, None])
+    rank = jnp.sum(earlier.astype(jnp.int32), axis=1)
+    new, out = lax.cond(
+        jnp.max(rank) < SLOTS,
+        functools.partial(step, True, chips),
+        functools.partial(step, False, chips),
+        owner,
+        rank,
+        centers,
+        weights.T,
+        targets.T,
+        batch_index.reshape(1, -1),
+        nys_index.reshape(1, -1),
+        eigvec.T,
+        eigval.reshape(1, -1),
+    )
     return new.T, out.T
 
 

time: 86.7 us -> 87.1 us (level)
  waiting for transfers between devices: 27.7 us -> 21.4 us
  other arithmetic: 0.61 us -> 5.56 us
  Pallas kernels: 16.9 us -> 19.9 us
  starting transfers between devices: 40.3 us -> 37.4 us
    ppermute x28 -> x22, waiting for transfers between devices: 27.7 us -> 21.4 us  [swap(): lax.ppermute(x, AXES, [(i, i ^ flip[i & 1]) for i in range(2 * chips)])]
    concatenate x8 -> x9, other arithmetic: 0.15 us -> 3.77 us  [the longest x5 3.7 us: all_of(): keep = jnp.concatenate([keep, swap(keep, chips, far_first, level)])]
    pallas_call x1, Pallas kernels: 1.17 us -> 4.52 us  [center_norms(): pl.pallas_call(norms_body, grid=(count // block,), in_specs=[pl.BlockSpec...]
    ppermute x28 -> x22, starting transfers between devices: 40.3 us -> 37.4 us  [swap(): lax.ppermute(x, AXES, [(i, i ^ flip[i & 1]) for i in range(2 * chips)])]
  transfers between devices with their start and end apart: 28 -> 22, of which waited for: 15 -> 12; matrix products, arithmetic and copies ran while one was open for 1% -> 5% of each run, Pallas kernels for 11% -> 15%
where the time goes in v8:
time: 87.1 us; the launch traced here: 86.7 us
  starting transfers between devices  37.4 us (43%)
  waiting for transfers between devices  21.4 us (25%)
  Pallas kernels  19.9 us (23%)
  other arithmetic  5.56 us (6%)
  between operations  1.44 us (2%)
    ppermute x22, starting transfers between devices, swap(): lax.ppermute(x, AXES, [(i, i ^ flip[i & 1]) for i in range(2 * chips)])  37.4 us
    ppermute x22, waiting for transfers between devices, swap(): lax.ppermute(x, AXES, [(i, i ^ flip[i & 1]) for i in range(2 * chips)])  21.4 us
    pallas_call x1, Pallas kernels, center_norms(): pl.pallas_call(norms_body, grid=(count // block,), in_specs=[pl.BlockSpec...  4.52 us
    pallas_call x2, Pallas kernels, pack_rows(): pl.pallas_call(functools.partial(pack_body, part * depth), in_specs=[hbm,...  3.91 us
    concatenate x5, other arithmetic, all_of(): keep = jnp.concatenate([keep, swap(keep, chips, far_first, level)])  3.7 us
    pallas_call x1, Pallas kernels, predict(): pl.pallas_call(predict_body, in_specs=[vmem] * 7, out_specs=[vmem] * 4, o...  3.34 us
    pallas_call x1, Pallas kernels, update(): pl.pallas_call(update_body, in_specs=[vmem] * 7, out_specs=[hbm, hbm, vme...  2.42 us
    pallas_call x1, Pallas kernels, update_more(): pl.pallas_call(functools.partial(update_more_body, begin), in_specs=[vmem...  1.96 us
  transfers between devices with their start and end apart: 22, of which 12 were waited for; matrix products, arithmetic and copies ran while one was open for 5% of the time, Pallas kernels for 15%

profile of v8, /device:TPU:1, one launch (start us, length us, event | category | flops | bytes accessed | tf_op | source)
XLA Modules:
  0.0 86.7 jit_solution(13432280617136673340)
XLA Ops:
  0.6 0.7 and_select_fusion.5
  1.3 0.2 convert_reduce_fusion
  1.5 0.6 reduce_max.9
  2.8 0.7 reshape.102
  3.5 83.1 %conditional.1 = ((f32[1000,768]{1,0:T(8,128)}, f32[1000,256]{1,0:T(8,128)})) conditional(s32[]{:T(128)} %convert_element_type.13, (s32[1,256]{1,0:T(1,128)}, bf16[768,3072]{1,0:T(8,128)(2,1)}, s32[1,320]{1,0:T(1,128)S(1)}, f32[160,320]{1,0:T(8,128)}, f32[1000,768]{1,0:T(8,128)}, /*index=5*/f32[1000,256]{1,0:T(8,128)}, f32[1,160]{1,0:T(1,128)}) %tuple.31, ...), branch_computations={%region_2.3_spmd, %region_3.4_spmd} | conditional | flops 5426420736 | bytes 104632288 | solution.py:580
  3.5 2.0 %pack_rows.2 = bf16[32,1536]{1,0:T(8,128)(2,1)S(1)} custom-call(s32[1,256]{1,0:T(1,128)} %get-tuple-element.66.index_hbm.index_ref, s32[1,256]{1,0:T(1,128)S(1)} %bitcast.21, bf16[768,3072]{1,0:T(8,128)(2,1)} %get-tuple-element.68.centers_hbm.centers_ref), custom_call_target="tpu_custom_call" | custom-call | flops 75497472 | bytes 2457600 | tf_op jit(solution)/shard_map/cond/branch_1_fun/pack_rows/pallas_call | solution.py:159
  5.4 3.2 %collective-permute-start.28 = (bf16[32,1536]{1,0:T(8,128)(2,1)S(1)}, bf16[32,1536]{1,0:T(8,128)(2,1)}, u32[]{:S(2)}, u32[]{:S(2)}) collective-permute-start(bf16[32,1536]{1,0:T(8,128)(2,1)S(1)} %pack_rows.2), channel_id=1, source_target_pairs={{0,8},{1,9},{2,10},{3,11},{4,12},{5,13},{6,14},{7,15},{8,0},{9,1},... | collective-permute-start | bytes 294920 | tf_op jit(solution)/shard_map/cond/branch_1_fun/ppermute | solution.py:489
  8.7 2.0 %pack_rows.3 = bf16[32,1536]{1,0:T(8,128)(2,1)S(1)} custom-call(s32[1,256]{1,0:T(1,128)} %get-tuple-element.66.index_hbm.index_ref, s32[1,256]{1,0:T(1,128)S(1)} %bitcast.22, bf16[768,3072]{1,0:T(8,128)(2,1)} %get-tuple-element.68.centers_hbm.centers_ref), custom_call_target="tpu_custom_call" | custom-call | flops 75497472 | bytes 2457600 | tf_op jit(solution)/shard_map/cond/branch_1_fun/pack_rows/pallas_call | solution.py:159
  10.6 0.0 copy-start.1
  10.6 0.0 copy-start.5
  10.6 0.1 collective-permute-start.29
  10.7 0.1 fusion.5.select_ref
  10.9 0.0 slice-start.2
  10.9 4.5 %center_norms.3.norm_ref = f32[768,128]{1,0:T(8,128)S(1)} custom-call(bf16[768,3072]{1,0:T(8,128)(2,1)} %get-tuple-element.68.centers_hbm.centers_ref), custom_call_target="tpu_custom_call" | custom-call | flops 4718592 | bytes 4718592 | tf_op jit(solution)/shard_map/cond/branch_1_fun/center_norms/pallas_call | solution.py:231
  15.4 1.6 %spread_weights.3 = (bf16[608,768]{1,0:T(8,128)(2,1)S(1)}, bf16[608,768]{1,0:T(8,128)(2,1)S(1)}, bf16[576,768]{1,0:T(8,128)(2,1)S(1)}, bf16[576,768]{1,0:T(8,128)(2,1)S(1)}, f32[160,768]{1,0:T(8,128)S(1)}) custom-call(s32[1,320]{1,0:T(1,128)S(1)} %get-tuple-element.69.index_ref, f32[160,320]{1,0:T(8,128)S(1)} %copy-done.5, f32[1000,768]{1,0:T(8,128)S(1)} %copy-done.1), custom_call_target="tpu_custom_call" | custom-call | flops 235929600 | bytes 7274496 | tf_op jit(solution)/shard_map/cond/branch_1_fun/spread_weights/pallas_call | solution.py:204
  17.0 0.0 collective-permute-done.29
  17.0 0.9 %pad_maximum_fusion.14 = bf16[64,1536]{1,0:T(8,128)(2,1)S(1)} fusion(bf16[32,1536]{1,0:T(8,128)(2,1)} %collective-permute-done.29, bf16[32,1536]{1,0:T(8,128)(2,1)S(1)} %pack_rows.3), kind=kLoop, calls=%fused_computation.47 | loop fusion | flops 393216 | bytes 393216 | tf_op jit(solution)/shard_map/cond/branch_1_fun/concatenate | solution.py:517
  17.9 1.3 %collective-permute-start.30 = (bf16[64,1536]{1,0:T(8,128)(2,1)S(1)}, bf16[64,1536]{1,0:T(8,128)(2,1)S(1)}, u32[]{:S(2)}, u32[]{:S(2)}) collective-permute-start(bf16[64,1536]{1,0:T(8,128)(2,1)S(1)} %pad_maximum_fusion.14), channel_id=1, source_target_pairs={{0,4},{1,3},{2,6},{3,1},{4,0},{5,7},{6,2},{7,5},{8,12},{9,11},{10,... | collective-permute-start | bytes 589832 | tf_op jit(solution)/shard_map/cond/branch_1_fun/ppermute | solution.py:489
  19.3 0.9 %pad_maximum_fusion.13 = bf16[64,1536]{1,0:T(8,128)(2,1)S(1)} fusion(bf16[32,1536]{1,0:T(8,128)(2,1)} %collective-permute-done.28, bf16[32,1536]{1,0:T(8,128)(2,1)S(1)} %pack_rows.2), kind=kLoop, calls=%fused_computation.46 | loop fusion | flops 393216 | bytes 393216 | tf_op jit(solution)/shard_map/cond/branch_1_fun/concatenate | solution.py:517
  20.2 0.3 collective-permute-start.33
  20.4 4.6 %collective-permute-done.33 = bf16[64,1536]{1,0:T(8,128)(2,1)S(1)} collective-permute-done((bf16[64,1536]{1,0:T(8,128)(2,1)S(1)}, bf16[64,1536]{1,0:T(8,128)(2,1)S(1)}, u32[]{:S(2)}, u32[]{:S(2)}) %collective-permute-start.33) | collective-permute-done | bytes 196640 | tf_op jit(solution)/shard_map/cond/branch_1_fun/ppermute | solution.py:489
  25.1 1.7 %collective-permute-start.34 = (bf16[128,1536]{1,0:T(8,128)(2,1)S(1)}, bf16[128,1536]{1,0:T(8,128)(2,1)S(1)}, u32[]{:S(2)}, u32[]{:S(2)}) collective-permute-start(bf16[128,1536]{1,0:T(8,128)(2,1)S(1)} %pad_maximum_fusion.10), channel_id=1, source_target_pairs={{0,2},{1,5},{2,0},{3,7},{4,6},{5,1},{6,4},{7,3},{8,10},{9,13},{10,... | collective-permute-start | bytes 1179656 | tf_op jit(solution)/shard_map/cond/branch_1_fun/ppermute | solution.py:489
  26.8 0.0 collective-permute-done.30
  26.8 0.9 %pad_maximum_fusion.9 = bf16[128,1536]{1,0:T(8,128)(2,1)S(1)} fusion(bf16[64,1536]{1,0:T(8,128)(2,1)S(1)} %collective-permute-done.30, bf16[32,1536]{1,0:T(8,128)(2,1)} %collective-permute-done.29, bf16[32,1536]{1,0:T(8,128)(2,1)S(1)} %pack_rows.3), kind=kLoop, calls=%fused_computation.42 | loop fusion | flops 1179648 | bytes 786432 | tf_op jit(solution)/shard_map/cond/branch_1_fun/concatenate | solution.py:517
  27.7 0.1 collective-permute-start.31
  27.8 4.4 %collective-permute-done.34 = bf16[128,1536]{1,0:T(8,128)(2,1)S(1)} collective-permute-done((bf16[128,1536]{1,0:T(8,128)(2,1)S(1)}, bf16[128,1536]{1,0:T(8,128)(2,1)S(1)}, u32[]{:S(2)}, u32[]{:S(2)}) %collective-permute-start.34) | collective-permute-done | bytes 393248 | tf_op jit(solution)/shard_map/cond/branch_1_fun/ppermute | solution.py:489
  32.3 3.5 %collective-permute-start.35 = (bf16[256,1536]{1,0:T(8,128)(2,1)S(1)}, bf16[256,1536]{1,0:T(8,128)(2,1)S(1)}, u32[]{:S(2)}, u32[]{:S(2)}) collective-permute-start(bf16[256,1536]{1,0:T(8,128)(2,1)S(1)} %constant_dynamic-update-slice_fusion.mine_ref), channel_id=1, source_target_pairs={{0,1},{1,0},{2,3},{3,2},{4,5},{5,4},{6,7},{7,6},{8,9},{9,8},{10,11... | collective-permute-start | bytes 2359304 | tf_op jit(solution)/shard_map/cond/branch_1_fun/ppermute | solution.py:489
  35.7 0.7 collective-permute-done.31
  36.5 0.9 %pad_maximum_fusion.8.mine_ref = bf16[256,1536]{1,0:T(8,128)(2,1)S(1)} fusion(bf16[128,1536]{1,0:T(8,128)(2,1)S(1)} %collective-permute-done.31, bf16[64,1536]{1,0:T(8,128)(2,1)S(1)} %collective-permute-done.30, bf16[32,1536]{1,0:T(8,128)(2,1)} %collective-permute-done.29, bf16[32,1536]{1,0:T(8,128)(2,1)S(1)} %pack_rows.3), kind=kLoop, calls=%fused_computation.39 | loop fusion | flops 3145728 | bytes 1572864 | tf_op jit(solution)/shard_map/cond/branch_1_fun/concatenate | solution.py:517
  37.4 3.5 %collective-permute-start.32 = (bf16[256,1536]{1,0:T(8,128)(2,1)S(1)}, bf16[256,1536]{1,0:T(8,128)(2,1)S(1)}, u32[]{:S(2)}, u32[]{:S(2)}) collective-permute-start(bf16[256,1536]{1,0:T(8,128)(2,1)S(1)} %pad_maximum_fusion.8.mine_ref), channel_id=1, source_target_pairs={{0,1},{1,0},{2,3},{3,2},{4,5},{5,4},{6,7},{7,6},{8,9},{9,8},{10,11... | collective-permute-start | bytes 2359304 | tf_op jit(solution)/shard_map/cond/branch_1_fun/ppermute | solution.py:489
  40.9 0.0 collective-permute-done.35.other_ref
  40.9 1.3 %distances.3.before_ref = f32[768,256]{1,0:T(8,128)S(1)} custom-call(bf16[256,1536]{1,0:T(8,128)(2,1)S(1)} %constant_dynamic-update-slice_fusion.mine_ref, bf16[256,1536]{1,0:T(8,128)(2,1)S(1)} %collective-permute-done.35.other_ref, bf16[256,512]{1,0:T(8,128)(2,1)S(1)} %fusion.5.select_ref, bf16[768,3072]{1,0:T(8,128)(2,1)S(1)} %bitcast.12, ...), custom_call_target="tpu_custom_call" | custom-call | flops 603979776 | bytes 3145728 | tf_op jit(solution)/shard_map/cond/branch_1_fun/distances/pallas_call | solution.py:296
  42.2 0.6 collective-permute-done.32.other_ref
  42.8 3.3 %predict.3 = (f32[608,128]{1,0:T(8,128)S(1)}, f32[608,128]{1,0:T(8,128)S(1)}, bf16[768,256]{1,0:T(8,128)(2,1)S(1)}, bf16[768,256]{1,0:T(8,128)(2,1)S(1)}) custom-call(bf16[256,1536]{1,0:T(8,128)(2,1)S(1)} %pad_maximum_fusion.8.mine_ref, bf16[256,1536]{1,0:T(8,128)(2,1)S(1)} %collective-permute-done.32.other_ref, bf16[256,512]{1,0:T(8,128)(2,1)S(1)} %fusion.5.select_ref, ...), custom_call_target="tpu_custom_call" | custom-call | flops 1321205760 | bytes 5636096 | tf_op jit(solution)/shard_map/cond/branch_1_fun/predict/pallas_call | solution.py:319
  46.1 0.4 collective-permute-start.43
  46.6 1.2 %collective-permute-done.43 = f32[608,128]{1,0:T(8,128)S(1)} collective-permute-done((f32[608,128]{1,0:T(8,128)S(1)}, f32[608,128]{1,0:T(8,128)S(1)}, u32[]{:S(2)}, u32[]{:S(2)}) %collective-permute-start.43) | collective-permute-done | bytes 311328 | tf_op jit(solution)/shard_map/cond/branch_1_fun/ppermute | solution.py:489
  47.9 0.7 collective-permute-start.44
  48.6 0.9 %predict_more.3 = (f32[576,128]{1,0:T(8,128)S(1)}, f32[576,128]{1,0:T(8,128)S(1)}) custom-call(bf16[576,768]{1,0:T(8,128)(2,1)S(1)} %get-tuple-element.78.high_ref, bf16[576,768]{1,0:T(8,128)(2,1)S(1)} %get-tuple-element.79.low_ref, bf16[768,256]{1,0:T(8,128)(2,1)S(1)} %get-tuple-element.85.value_high_ref, bf16[768,256]{1,0:T(8,128)(2,1)S(1)} %get-tuple-element.86.value_low_ref), custom_call_target="tpu_custom_call" | custom-call | flops 679477248 | bytes 2359296 | tf_op jit(solution)/shard_map/cond/branch_1_fun/predict_more/pallas_call | solution.py:343
  49.5 0.0 copy-start.3
  49.5 0.0 copy-start.7
  49.5 0.0 copy-start.9
  49.5 1.3 %collective-permute-start.36 = (f32[576,128]{1,0:T(8,128)S(1)}, f32[576,128]{1,0:T(8,128)S(1)}, u32[]{:S(2)}, u32[]{:S(2)}) collective-permute-start(f32[576,128]{1,0:T(8,128)S(1)} %get-tuple-element.88), channel_id=1, source_target_pairs={{0,1},{1,0},{2,3},{3,2},{4,5},{5,4},{6,7},{7,6},{8,9},{9,8},{10,11... | collective-permute-start | bytes 884744 | tf_op jit(solution)/shard_map/cond/branch_1_fun/ppermute | solution.py:489
  50.8 1.5 %collective-permute-done.44 = f32[304,128]{1,0:T(8,128)S(1)} collective-permute-done((f32[304,128]{1,0:T(8,128)S(1)}, f32[304,128]{1,0:T(8,128)S(1)}, u32[]{:S(2)}, u32[]{:S(2)}) %collective-permute-start.44) | collective-permute-done | bytes 155680 | tf_op jit(solution)/shard_map/cond/branch_1_fun/ppermute | solution.py:489
  52.3 1.3 %collective-permute-start.45 = (f32[152,128]{1,0:T(8,128)S(1)}, f32[152,128]{1,0:T(8,128)S(1)}, u32[]{:S(2)}, u32[]{:S(2)}) collective-permute-start(f32[152,128]{1,0:T(8,128)S(1)} %slice.98), channel_id=1, source_target_pairs={{0,4},{1,3},{2,6},{3,1},{4,0},{5,7},{6,2},{7,5},{8,12},{9,11},{10,... | collective-permute-start | bytes 233480 | tf_op jit(solution)/shard_map/cond/branch_1_fun/ppermute | solution.py:489
  53.7 0.0 collective-permute-done.36
  53.7 0.7 collective-permute-start.37
  54.4 1.2 %collective-permute-done.45 = f32[152,128]{1,0:T(8,128)S(1)} collective-permute-done((f32[152,128]{1,0:T(8,128)S(1)}, f32[152,128]{1,0:T(8,128)S(1)}, u32[]{:S(2)}, u32[]{:S(2)}) %collective-permute-start.45) | collective-permute-done | bytes 77856 | tf_op jit(solution)/shard_map/cond/branch_1_fun/ppermute | solution.py:489
  55.7 2.6 %collective-permute-start.46 = (f32[152,128]{1,0:T(8,128)S(1)}, f32[152,128]{1,0:T(8,128)S(1)}, u32[]{:S(2)}, u32[]{:S(2)}) collective-permute-start(f32[152,128]{1,0:T(8,128)S(1)} %slice_add_fusion.10), channel_id=1, source_target_pairs={{0,8},{1,9},{2,10},{3,11},{4,12},{5,13},{6,14},{7,15},{8,0},{9,1},... | collective-permute-start | bytes 233480 | tf_op jit(solution)/shard_map/cond/branch_1_fun/ppermute | solution.py:489
  58.2 0.7 collective-permute-done.37
  58.9 0.6 collective-permute-start.38
  59.6 0.4 collective-permute-done.46
  60.0 2.1 %collective-permute-start.47 = (f32[152,128]{1,0:T(8,128)S(1)}, f32[152,128]{1,0:T(8,128)S(1)}, u32[]{:S(2)}, u32[]{:S(2)}) collective-permute-start(f32[152,128]{1,0:T(8,128)S(1)} %add.154), channel_id=1, source_target_pairs={{0,4},{1,3},{2,6},{3,1},{4,0},{5,7},{6,2},{7,5},{8,12},{9,11},{10,... | collective-permute-start | bytes 233480 | tf_op jit(solution)/shard_map/cond/branch_1_fun/ppermute | solution.py:489
  62.2 0.0 collective-permute-done.38
  62.2 2.6 %collective-permute-start.39 = (f32[144,128]{1,0:T(8,128)S(1)}, f32[144,128]{1,0:T(8,128)S(1)}, u32[]{:S(2)}, u32[]{:S(2)}) collective-permute-start(f32[144,128]{1,0:T(8,128)S(1)} %slice_add_fusion.11), channel_id=1, source_target_pairs={{0,8},{1,9},{2,10},{3,11},{4,12},{5,13},{6,14},{7,15},{8,0},{9,1},... | collective-permute-start | bytes 221192 | tf_op jit(solution)/shard_map/cond/branch_1_fun/ppermute | solution.py:489
  64.8 2.5 %collective-permute-done.39 = f32[144,128]{1,0:T(8,128)S(1)} collective-permute-done((f32[144,128]{1,0:T(8,128)S(1)}, f32[144,128]{1,0:T(8,128)S(1)}, u32[]{:S(2)}, u32[]{:S(2)}) %collective-permute-start.39) | collective-permute-done | bytes 73760 | tf_op jit(solution)/shard_map/cond/branch_1_fun/ppermute | solution.py:489
  67.3 0.1 collective-permute-start.40
  67.4 1.1 %collective-permute-start.48 = (f32[304,128]{1,0:T(8,128)S(1)}, f32[304,128]{1,0:T(8,128)S(1)}, u32[]{:S(2)}, u32[]{:S(2)}) collective-permute-start(f32[304,128]{1,0:T(8,128)S(1)} %pad_maximum_fusion.15), channel_id=1, source_target_pairs={{0,2},{1,5},{2,0},{3,7},{4,6},{5,1},{6,4},{7,3},{8,10},{9,13},{10,... | collective-permute-start | bytes 466952 | tf_op jit(solution)/shard_map/cond/branch_1_fun/ppermute | solution.py:489
  68.5 2.4 %collective-permute-done.40 = f32[144,128]{1,0:T(8,128)S(1)} collective-permute-done((f32[144,128]{1,0:T(8,128)S(1)}, f32[144,128]{1,0:T(8,128)S(1)}, u32[]{:S(2)}, u32[]{:S(2)}) %collective-permute-start.40) | collective-permute-done | bytes 73760 | tf_op jit(solution)/shard_map/cond/branch_1_fun/ppermute | solution.py:489
  70.9 0.5 collective-permute-start.41
  71.4 1.0 %collective-permute-done.48 = f32[304,128]{1,0:T(8,128)S(1)} collective-permute-done((f32[304,128]{1,0:T(8,128)S(1)}, f32[304,128]{1,0:T(8,128)S(1)}, u32[]{:S(2)}, u32[]{:S(2)}) %collective-permute-start.48) | collective-permute-done | bytes 155680 | tf_op jit(solution)/shard_map/cond/branch_1_fun/ppermute | solution.py:489
  72.4 5.8 %collective-permute-start.49 = (f32[608,128]{1,0:T(8,128)S(1)}, f32[608,128]{1,0:T(8,128)S(1)}, u32[]{:S(2)}, u32[]{:S(2)}) collective-permute-start(f32[608,128]{1,0:T(8,128)S(1)} %pad_maximum_fusion.11.mine_ref), channel_id=1, source_target_pairs={{0,1},{1,0},{2,3},{3,2},{4,5},{5,4},{6,7},{7,6},{8,9},{9,8},{10,11... | collective-permute-start | bytes 933896 | tf_op jit(solution)/shard_map/cond/branch_1_fun/ppermute | solution.py:489
  78.3 3.9 %collective-permute-start.42 = (f32[576,128]{1,0:T(8,128)S(1)}, f32[576,128]{1,0:T(8,128)S(1)}, u32[]{:S(2)}, u32[]{:S(2)}) collective-permute-start(f32[576,128]{1,0:T(8,128)S(1)} %pad_maximum_fusion.12.mine_ref), channel_id=1, source_target_pairs={{0,1},{1,0},{2,3},{3,2},{4,5},{5,4},{6,7},{7,6},{8,9},{9,8},{10,11... | collective-permute-start | bytes 884744 | tf_op jit(solution)/shard_map/cond/branch_1_fun/ppermute | solution.py:489
  82.2 2.4 %update.3 = (f32[1000,768]{1,0:T(8,128)}, f32[1000,256]{1,0:T(8,128)}, bf16[256,768]{1,0:T(8,128)(2,1)S(1)}, bf16[256,768]{1,0:T(8,128)(2,1)S(1)}) custom-call(f32[608,128]{1,0:T(8,128)S(1)} %pad_maximum_fusion.11.mine_ref, f32[608,128]{1,0:T(8,128)S(1)} %collective-permute-done.49.other_ref, f32[1000,256]{1,0:T(8,128)S(1)} %copy-done.3, ...), custom_call_target="tpu_custom_call" | custom-call | flops 717225984 | bytes 3670016 | tf_op jit(solution)/shard_map/cond/branch_1_fun/update/pallas_call | solution.py:427
  84.6 2.0 %update_more.3 = (f32[1000,768]{1,0:T(8,128)}, f32[1000,256]{1,0:T(8,128)}) custom-call(f32[576,128]{1,0:T(8,128)S(1)} %pad_maximum_fusion.12.mine_ref, f32[576,128]{1,0:T(8,128)S(1)} %collective-permute-done.42.other_ref, f32[1000,256]{1,0:T(8,128)S(1)} %copy-done.3, f32[1000,768]{1,0:T(8,128)S(1)} %copy-done.1, ...), custom_call_target="tpu_custom_call", output_to_operand_aliasing={{0}: (6, {}), {1}: (7, {})} | custom-call | flops 651165696 | bytes 4521984 | tf_op jit(solution)/shard_map/cond/branch_1_fun/update_more/pallas_call | solution.py:465
  (35 shorter events, 0.4 us)
Async XLA Ops:
  5.4 13.8 %collective-permute-start.28 = (bf16[32,1536]{1,0:T(8,128)(2,1)S(1)}, bf16[32,1536]{1,0:T(8,128)(2,1)}, u32[]{:S(2)}, u32[]{:S(2)}) collective-permute-start(bf16[32,1536]{1,0:T(8,128)(2,1)S(1)} %pack_rows.2), channel_id=1, source_target_pairs={{0,8},{1,9},{2,10},{3,11},{4,12},{5,13},{6,14},{7,15},{8,0},{9,1},... | collective-permute-start | bytes 294920 | tf_op jit(solution)/shard_map/cond/branch_1_fun/ppermute | solution.py:489
  10.6 4.8 %copy-start.1 = (f32[1000,768]{1,0:T(8,128)S(1)}, f32[1000,768]{1,0:T(8,128)}, u32[]{:S(2)}) copy-start(f32[1000,768]{1,0:T(8,128)} %get-tuple-element.71.weights_ref) | copy-start | bytes 9216004 | tf_op jit(solution)/shard_map/cond
  10.6 4.8 %copy-start.5 = (f32[160,320]{1,0:T(8,128)S(1)}, f32[160,320]{1,0:T(8,128)}, u32[]{:S(2)}) copy-start(f32[160,320]{1,0:T(8,128)} %get-tuple-element.70.eigvec_ref) | copy-start | bytes 614404 | tf_op jit(solution)/shard_map/cond
  10.6 6.4 %collective-permute-start.29 = (bf16[32,1536]{1,0:T(8,128)(2,1)S(1)}, bf16[32,1536]{1,0:T(8,128)(2,1)}, u32[]{:S(2)}, u32[]{:S(2)}) collective-permute-start(bf16[32,1536]{1,0:T(8,128)(2,1)S(1)} %pack_rows.3), channel_id=1, source_target_pairs={{0,8},{1,9},{2,10},{3,11},{4,12},{5,13},{6,14},{7,15},{8,0},{9,1},... | collective-permute-start | bytes 294920 | tf_op jit(solution)/shard_map/cond/branch_1_fun/ppermute | solution.py:489
  10.9 30.0 %slice-start.2 = ((s8[4718592]{0:T(1024)(128)(4,1)}), s8[4194304]{0:T(1024)(128)(4,1)S(1)}, s32[]{:S(2)}) async-start(s8[4718592]{0:T(1024)(128)(4,1)} %bitcast.11), calls=%async_computation.2 | async-start | bytes 8388608 | tf_op jit(solution)/shard_map/cond
  15.4 25.5 %slice-start.3 = ((s8[4718592]{0:T(1024)(128)(4,1)}), s8[524288]{0:T(1024)(128)(4,1)S(1)}, s32[]{:S(2)}) async-start(s8[4718592]{0:T(1024)(128)(4,1)} %bitcast.11), calls=%async_computation.3 | async-start | bytes 1048576 | tf_op jit(solution)/shard_map/cond
  17.9 8.9 %collective-permute-start.30 = (bf16[64,1536]{1,0:T(8,128)(2,1)S(1)}, bf16[64,1536]{1,0:T(8,128)(2,1)S(1)}, u32[]{:S(2)}, u32[]{:S(2)}) collective-permute-start(bf16[64,1536]{1,0:T(8,128)(2,1)S(1)} %pad_maximum_fusion.14), channel_id=1, source_target_pairs={{0,4},{1,3},{2,6},{3,1},{4,0},{5,7},{6,2},{7,5},{8,12},{9,11},{10,... | collective-permute-start | bytes 589832 | tf_op jit(solution)/shard_map/cond/branch_1_fun/ppermute | solution.py:489
  20.2 4.9 %collective-permute-start.33 = (bf16[64,1536]{1,0:T(8,128)(2,1)S(1)}, bf16[64,1536]{1,0:T(8,128)(2,1)S(1)}, u32[]{:S(2)}, u32[]{:S(2)}) collective-permute-start(bf16[64,1536]{1,0:T(8,128)(2,1)S(1)} %pad_maximum_fusion.13), channel_id=1, source_target_pairs={{0,4},{1,3},{2,6},{3,1},{4,0},{5,7},{6,2},{7,5},{8,12},{9,11},{10,... | collective-permute-start | bytes 589832 | tf_op jit(solution)/shard_map/cond/branch_1_fun/ppermute | solution.py:489
  25.1 7.2 %collective-permute-start.34 = (bf16[128,1536]{1,0:T(8,128)(2,1)S(1)}, bf16[128,1536]{1,0:T(8,128)(2,1)S(1)}, u32[]{:S(2)}, u32[]{:S(2)}) collective-permute-start(bf16[128,1536]{1,0:T(8,128)(2,1)S(1)} %pad_maximum_fusion.10), channel_id=1, source_target_pairs={{0,2},{1,5},{2,0},{3,7},{4,6},{5,1},{6,4},{7,3},{8,10},{9,13},{10,... | collective-permute-start | bytes 1179656 | tf_op jit(solution)/shard_map/cond/branch_1_fun/ppermute | solution.py:489
  27.7 8.7 %collective-permute-start.31 = (bf16[128,1536]{1,0:T(8,128)(2,1)S(1)}, bf16[128,1536]{1,0:T(8,128)(2,1)S(1)}, u32[]{:S(2)}, u32[]{:S(2)}) collective-permute-start(bf16[128,1536]{1,0:T(8,128)(2,1)S(1)} %pad_maximum_fusion.9), channel_id=1, source_target_pairs={{0,2},{1,5},{2,0},{3,7},{4,6},{5,1},{6,4},{7,3},{8,10},{9,13},{10,... | collective-permute-start | bytes 1179656 | tf_op jit(solution)/shard_map/cond/branch_1_fun/ppermute | solution.py:489
  32.3 8.6 %collective-permute-start.35 = (bf16[256,1536]{1,0:T(8,128)(2,1)S(1)}, bf16[256,1536]{1,0:T(8,128)(2,1)S(1)}, u32[]{:S(2)}, u32[]{:S(2)}) collective-permute-start(bf16[256,1536]{1,0:T(8,128)(2,1)S(1)} %constant_dynamic-update-slice_fusion.mine_ref), channel_id=1, source_target_pairs={{0,1},{1,0},{2,3},{3,2},{4,5},{5,4},{6,7},{7,6},{8,9},{9,8},{10,11... | collective-permute-start | bytes 2359304 | tf_op jit(solution)/shard_map/cond/branch_1_fun/ppermute | solution.py:489
  37.4 5.4 %collective-permute-start.32 = (bf16[256,1536]{1,0:T(8,128)(2,1)S(1)}, bf16[256,1536]{1,0:T(8,128)(2,1)S(1)}, u32[]{:S(2)}, u32[]{:S(2)}) collective-permute-start(bf16[256,1536]{1,0:T(8,128)(2,1)S(1)} %pad_maximum_fusion.8.mine_ref), channel_id=1, source_target_pairs={{0,1},{1,0},{2,3},{3,2},{4,5},{5,4},{6,7},{7,6},{8,9},{9,8},{10,11... | collective-permute-start | bytes 2359304 | tf_op jit(solution)/shard_map/cond/branch_1_fun/ppermute | solution.py:489
  46.1 1.7 %collective-permute-start.43 = (f32[608,128]{1,0:T(8,128)S(1)}, f32[608,128]{1,0:T(8,128)S(1)}, u32[]{:S(2)}, u32[]{:S(2)}) collective-permute-start(f32[608,128]{1,0:T(8,128)S(1)} %get-tuple-element.91), channel_id=1, source_target_pairs={{0,1},{1,0},{2,3},{3,2},{4,5},{5,4},{6,7},{7,6},{8,9},{9,8},{10,11... | collective-permute-start | bytes 933896 | tf_op jit(solution)/shard_map/cond/branch_1_fun/ppermute | solution.py:489
  47.9 4.4 %collective-permute-start.44 = (f32[304,128]{1,0:T(8,128)S(1)}, f32[304,128]{1,0:T(8,128)S(1)}, u32[]{:S(2)}, u32[]{:S(2)}) collective-permute-start(f32[304,128]{1,0:T(8,128)S(1)} %slice.96), channel_id=1, source_target_pairs={{0,2},{1,5},{2,0},{3,7},{4,6},{5,1},{6,4},{7,3},{8,10},{9,13},{10,... | collective-permute-start | bytes 466952 | tf_op jit(solution)/shard_map/cond/branch_1_fun/ppermute | solution.py:489
  49.5 32.7 %copy-start.3 = (f32[1000,256]{1,0:T(8,128)S(1)}, f32[1000,256]{1,0:T(8,128)}, u32[]{:S(2)}) copy-start(f32[1000,256]{1,0:T(8,128)} %get-tuple-element.89.targets_ref) | copy-start | bytes 3072004 | tf_op jit(solution)/shard_map/cond
  49.5 32.7 %copy-start.7 = (s32[1,256]{1,0:T(1,128)S(1)}, s32[1,256]{1,0:T(1,128)}, u32[]{:S(2)}) copy-start(s32[1,256]{1,0:T(1,128)} %get-tuple-element.66.index_hbm.index_ref) | copy-start | bytes 3076 | tf_op jit(solution)/shard_map/cond
  49.5 32.7 %copy-start.9 = (f32[1,160]{1,0:T(1,128)S(1)}, f32[1,160]{1,0:T(1,128)}, u32[]{:S(2)}) copy-start(f32[1,160]{1,0:T(1,128)} %get-tuple-element.92.eigval_ref) | copy-start | bytes 1924 | tf_op jit(solution)/shard_map/cond
  49.5 4.2 %collective-permute-start.36 = (f32[576,128]{1,0:T(8,128)S(1)}, f32[576,128]{1,0:T(8,128)S(1)}, u32[]{:S(2)}, u32[]{:S(2)}) collective-permute-start(f32[576,128]{1,0:T(8,128)S(1)} %get-tuple-element.88), channel_id=1, source_target_pairs={{0,1},{1,0},{2,3},{3,2},{4,5},{5,4},{6,7},{7,6},{8,9},{9,8},{10,11... | collective-permute-start | bytes 884744 | tf_op jit(solution)/shard_map/cond/branch_1_fun/ppermute | solution.py:489
  52.3 3.3 %collective-permute-start.45 = (f32[152,128]{1,0:T(8,128)S(1)}, f32[152,128]{1,0:T(8,128)S(1)}, u32[]{:S(2)}, u32[]{:S(2)}) collective-permute-start(f32[152,128]{1,0:T(8,128)S(1)} %slice.98), channel_id=1, source_target_pairs={{0,4},{1,3},{2,6},{3,1},{4,0},{5,7},{6,2},{7,5},{8,12},{9,11},{10,... | collective-permute-start | bytes 233480 | tf_op jit(solution)/shard_map/cond/branch_1_fun/ppermute | solution.py:489
  53.7 5.2 %collective-permute-start.37 = (f32[288,128]{1,0:T(8,128)S(1)}, f32[288,128]{1,0:T(8,128)S(1)}, u32[]{:S(2)}, u32[]{:S(2)}) collective-permute-start(f32[288,128]{1,0:T(8,128)S(1)} %slice.92), channel_id=1, source_target_pairs={{0,2},{1,5},{2,0},{3,7},{4,6},{5,1},{6,4},{7,3},{8,10},{9,13},{10,... | collective-permute-start | bytes 442376 | tf_op jit(solution)/shard_map/cond/branch_1_fun/ppermute | solution.py:489
  55.7 4.3 %collective-permute-start.46 = (f32[152,128]{1,0:T(8,128)S(1)}, f32[152,128]{1,0:T(8,128)S(1)}, u32[]{:S(2)}, u32[]{:S(2)}) collective-permute-start(f32[152,128]{1,0:T(8,128)S(1)} %slice_add_fusion.10), channel_id=1, source_target_pairs={{0,8},{1,9},{2,10},{3,11},{4,12},{5,13},{6,14},{7,15},{8,0},{9,1},... | collective-permute-start | bytes 233480 | tf_op jit(solution)/shard_map/cond/branch_1_fun/ppermute | solution.py:489
  58.9 3.3 %collective-permute-start.38 = (f32[144,128]{1,0:T(8,128)S(1)}, f32[144,128]{1,0:T(8,128)S(1)}, u32[]{:S(2)}, u32[]{:S(2)}) collective-permute-start(f32[144,128]{1,0:T(8,128)S(1)} %slice.94), channel_id=1, source_target_pairs={{0,4},{1,3},{2,6},{3,1},{4,0},{5,7},{6,2},{7,5},{8,12},{9,11},{10,... | collective-permute-start | bytes 221192 | tf_op jit(solution)/shard_map/cond/branch_1_fun/ppermute | solution.py:489
  60.0 7.4 %collective-permute-start.47 = (f32[152,128]{1,0:T(8,128)S(1)}, f32[152,128]{1,0:T(8,128)S(1)}, u32[]{:S(2)}, u32[]{:S(2)}) collective-permute-start(f32[152,128]{1,0:T(8,128)S(1)} %add.154), channel_id=1, source_target_pairs={{0,4},{1,3},{2,6},{3,1},{4,0},{5,7},{6,2},{7,5},{8,12},{9,11},{10,... | collective-permute-start | bytes 233480 | tf_op jit(solution)/shard_map/cond/branch_1_fun/ppermute | solution.py:489
  62.2 5.1 %collective-permute-start.39 = (f32[144,128]{1,0:T(8,128)S(1)}, f32[144,128]{1,0:T(8,128)S(1)}, u32[]{:S(2)}, u32[]{:S(2)}) collective-permute-start(f32[144,128]{1,0:T(8,128)S(1)} %slice_add_fusion.11), channel_id=1, source_target_pairs={{0,8},{1,9},{2,10},{3,11},{4,12},{5,13},{6,14},{7,15},{8,0},{9,1},... | collective-permute-start | bytes 221192 | tf_op jit(solution)/shard_map/cond/branch_1_fun/ppermute | solution.py:489
  67.3 3.6 %collective-permute-start.40 = (f32[144,128]{1,0:T(8,128)S(1)}, f32[144,128]{1,0:T(8,128)S(1)}, u32[]{:S(2)}, u32[]{:S(2)}) collective-permute-start(f32[144,128]{1,0:T(8,128)S(1)} %add.150), channel_id=1, source_target_pairs={{0,4},{1,3},{2,6},{3,1},{4,0},{5,7},{6,2},{7,5},{8,12},{9,11},{10,... | collective-permute-start | bytes 221192 | tf_op jit(solution)/shard_map/cond/branch_1_fun/ppermute | solution.py:489
  67.4 4.9 %collective-permute-start.48 = (f32[304,128]{1,0:T(8,128)S(1)}, f32[304,128]{1,0:T(8,128)S(1)}, u32[]{:S(2)}, u32[]{:S(2)}) collective-permute-start(f32[304,128]{1,0:T(8,128)S(1)} %pad_maximum_fusion.15), channel_id=1, source_target_pairs={{0,2},{1,5},{2,0},{3,7},{4,6},{5,1},{6,4},{7,3},{8,10},{9,13},{10,... | collective-permute-start | bytes 466952 | tf_op jit(solution)/shard_map/cond/branch_1_fun/ppermute | solution.py:489
  70.9 7.3 %collective-permute-start.41 = (f32[288,128]{1,0:T(8,128)S(1)}, f32[288,128]{1,0:T(8,128)S(1)}, u32[]{:S(2)}, u32[]{:S(2)}) collective-permute-start(f32[288,128]{1,0:T(8,128)S(1)} %pad_maximum_fusion.16), channel_id=1, source_target_pairs={{0,2},{1,5},{2,0},{3,7},{4,6},{5,1},{6,4},{7,3},{8,10},{9,13},{10,... | collective-permute-start | bytes 442376 | tf_op jit(solution)/shard_map/cond/branch_1_fun/ppermute | solution.py:489
  72.4 9.8 %collective-permute-start.49 = (f32[608,128]{1,0:T(8,128)S(1)}, f32[608,128]{1,0:T(8,128)S(1)}, u32[]{:S(2)}, u32[]{:S(2)}) collective-permute-start(f32[608,128]{1,0:T(8,128)S(1)} %pad_maximum_fusion.11.mine_ref), channel_id=1, source_target_pairs={{0,1},{1,0},{2,3},{3,2},{4,5},{5,4},{6,7},{7,6},{8,9},{9,8},{10,11... | collective-permute-start | bytes 933896 | tf_op jit(solution)/shard_map/cond/branch_1_fun/ppermute | solution.py:489
  78.3 6.4 %collective-permute-start.42 = (f32[576,128]{1,0:T(8,128)S(1)}, f32[576,128]{1,0:T(8,128)S(1)}, u32[]{:S(2)}, u32[]{:S(2)}) collective-permute-start(f32[576,128]{1,0:T(8,128)S(1)} %pad_maximum_fusion.12.mine_ref), channel_id=1, source_target_pairs={{0,1},{1,0},{2,3},{3,2},{4,5},{5,4},{6,7},{7,6},{8,9},{9,8},{10,11... | collective-permute-start | bytes 884744 | tf_op jit(solution)/shard_map/cond/branch_1_fun/ppermute | solution.py:489

commit v9 on v6

--- a/solution.py
+++ b/solution.py
@@ -15,6 +15,8 @@
 CHUNKS = 1 << HALVINGS
 LANE = 128
 PARTS = 2
+SLOTS = 32
+TIED = 2
 NT = (((1,), (1,)), ((), ()))
 NN = (((1,), (0,)), ((), ()))
 VMEM_LIMIT = 24 * 1024 * 1024
@@ -27,6 +29,11 @@
 def walk(sub, bits):
     order = list(range(bits))
     return order if sub == 0 else order[1::-1] + order[2:]
+
+
+def far_first(sub, bits):
+    order = list(range(bits))[::-1]
+    return order if sub == 0 else order[:-2] + order[:-3:-1]
 
 
 def turns():
@@ -60,12 +67,9 @@
     return pltpu.CompilerParams(vmem_limit_bytes=VMEM_LIMIT)
 
 
-def pick_body(first, index_hbm, centers_hbm, keep_ref, send_ref, pick_ref, index_ref, centers_ref, sems):
-    sub = lax.axis_index("sub")
+def pack_body(first, offset_ref, index_hbm, centers_hbm, out_ref, index_ref, centers_ref, sems):
     blocks, count, block = centers_ref.shape
     rows = index_ref.shape[1]
-    half = rows // 2
-    size = half // CHUNKS
     copies = [pltpu.make_async_copy(index_hbm, index_ref, sems.at[blocks])] + [
         pltpu.make_async_copy(
             centers_hbm.at[:, pl.ds(first + k * block, block)], centers_ref.at[k], sems.at[k]
@@ -75,46 +79,41 @@
     for copy in copies:
         copy.start()
     copies[0].wait()
-    start = (lax.axis_index("center") * 2 + sub) * count
-    pick = pick_rows(index_ref, count, start, BF16, 1.0)
-    for part, turn in enumerate(turns()):
-        begin = jnp.where(sub == part, 0, half)
-        for chunk in range(CHUNKS):
-            to = pl.multiple_of(begin + (chunk ^ turn) * size, size)
-            at = part * half + chunk * size
-            pick_ref[pl.ds(to, size), :] = pick[at : at + size]
+    start = (lax.axis_index("center") * 2 + lax.axis_index("sub")) * count
+    local = index_ref[...] - start
+    here = jnp.where((local >= 0) & (local < count), 1.0, 0.0)
+    earlier = lax.broadcasted_iota(jnp.int32, (rows, rows), 0) < lax.broadcasted_iota(jnp.int32, (rows, rows), 1)
+    rank = dot(jnp.broadcast_to(here, (8, rows)).astype(BF16), jnp.where(earlier, 1.0, 0.0).astype(BF16), NN)[0:1]
+    slots = (lax.broadcasted_iota(jnp.int32, (SLOTS, 1), 0) + offset_ref[0]).astype(F32)
+    to_slot = jnp.where(slots == rank, here, 0.0).astype(BF16)
+    pick = dot(to_slot, pick_rows(index_ref, count, start, BF16, 1.0), NN).astype(BF16)
     for k in range(blocks):
         copies[k + 1].wait()
-        found = dot(pick_ref[...], centers_ref[k], NN).astype(BF16)
-        keep_ref[:, k * block : (k + 1) * block] = found[:half]
-        send_ref[:, k * block : (k + 1) * block] = found[half:]
-
-
-def pick_batch(batch_index, centers, part):
+        out_ref[:, k * block : (k + 1) * block] = dot(pick, centers_ref[k], NN).astype(BF16)
+
+
+def pack_rows(offset, batch_index, centers, part):
     rows = batch_index.shape[1]
     count, depth = centers.shape
     depth = depth // PARTS
     block = 512
-    half = jax.ShapeDtypeStruct((rows // 2, depth), BF16)
     hbm = pl.BlockSpec(memory_space=pltpu.HBM)
-    vmem = pl.BlockSpec(memory_space=pltpu.VMEM)
-    return pl.pallas_call(
-        functools.partial(pick_body, part * depth),
-        in_specs=[hbm, hbm],
-        out_specs=[vmem, vmem],
-        out_shape=[half, half],
+    return pl.pallas_call(
+        functools.partial(pack_body, part * depth),
+        in_specs=[pl.BlockSpec(memory_space=pltpu.SMEM), hbm, hbm],
+        out_specs=pl.BlockSpec(memory_space=pltpu.VMEM),
+        out_shape=jax.ShapeDtypeStruct((SLOTS, depth), BF16),
         scratch_shapes=[
-            pltpu.VMEM((rows, count), BF16),
             pltpu.VMEM((1, rows), jnp.int32),
             pltpu.VMEM((depth // block, count, block), BF16),
             pltpu.SemaphoreType.DMA((depth // block + 1,)),
         ],
         compiler_params=params(),
         cost_estimate=pl.CostEstimate(
-            flops=2 * rows * count * depth, bytes_accessed=2 * depth * (count + rows), transcendentals=0
-        ),
-        name="pick_batch",
-    )(batch_index, centers)
+            flops=2 * SLOTS * count * depth, bytes_accessed=2 * depth * (count + SLOTS), transcendentals=0
+        ),
+        name="pack_rows",
+    )(offset, batch_index, centers)
 
 
 def spread_body(
@@ -182,16 +181,10 @@
     )(centers)
 
 
-def gather_batch(mine_ref, other_ref, batch_ref):
-    lower = lax.axis_index("sub") == 0
+def gather_batch(mine_ref, other_ref, select_ref, more_ref, batch_ref):
     half = mine_ref.shape[0]
-    size = half // CHUNKS
-    for part, turn in enumerate(turns()):
-        for chunk in range(CHUNKS):
-            at = slice(chunk * size, (chunk + 1) * size)
-            same = lower if part == 0 else jnp.logical_not(lower)
-            to = pl.multiple_of(part * half + (chunk ^ turn) * size, size)
-            batch_ref[pl.ds(to, size), :] = jnp.where(same, mine_ref[at], other_ref[at])
+    found = dot(select_ref[:, :half], mine_ref[...], NN) + dot(select_ref[:, half:], other_ref[...], NN)
+    batch_ref[...] = (found + more_ref[...].astype(F32)).astype(BF16)
 
 
 def nearer(first, centers_ref, batch_ref):
@@ -218,17 +211,17 @@
         send_ref[at] = jnp.where(lower, second, first)
 
 
-def distance_body(mine_ref, other_ref, centers_ref, norm_ref, total_ref, batch_ref):
-    gather_batch(mine_ref, other_ref, batch_ref)
+def distance_body(mine_ref, other_ref, select_ref, more_ref, centers_ref, norm_ref, total_ref, batch_ref):
+    gather_batch(mine_ref, other_ref, select_ref, more_ref, batch_ref)
     total_ref[...] = norm_ref[:, 0:1] + nearer(0, centers_ref, batch_ref)
 
 
 def predict_body(
-    mine_ref, other_ref, centers_ref, before_ref, high_ref, low_ref,
+    mine_ref, other_ref, select_ref, more_ref, centers_ref, before_ref, high_ref, low_ref,
     keep_ref, send_ref, value_high_ref, value_low_ref, batch_ref, total_ref,
 ):
     depth = centers_ref.shape[1]
-    gather_batch(mine_ref, other_ref, batch_ref)
+    gather_batch(mine_ref, other_ref, select_ref, more_ref, batch_ref)
     square = jnp.maximum(before_ref[...] + nearer(depth - batch_ref.shape[1], centers_ref, batch_ref), 0.0)
     value_high, value_low = two(jnp.exp(jnp.sqrt(square) * (-1.0 / math.sqrt(depth))))
     value_high_ref[...] = value_high
@@ -236,14 +229,14 @@
     product(high_ref, low_ref, value_high, value_low, total_ref, keep_ref, send_ref)
 
 
-def distances(mine, other, centers, norms):
-    half, depth = mine.shape
-    rows = 2 * half
+def distances(mine, other, select, more, centers, norms):
+    depth = mine.shape[1]
+    rows = select.shape[0]
     count = centers.shape[0]
     vmem = pl.BlockSpec(memory_space=pltpu.VMEM)
     return pl.pallas_call(
         distance_body,
-        in_specs=[vmem] * 4,
+        in_specs=[vmem] * 6,
         out_specs=vmem,
         out_shape=jax.ShapeDtypeStruct((count, rows), F32),
         scratch_shapes=[pltpu.VMEM((rows, depth), BF16)],
@@ -252,12 +245,13 @@
             flops=2 * rows * count * depth, bytes_accessed=2 * depth * (count + rows), transcendentals=0
         ),
         name="distances",
-    )(mine, other, centers, norms)
-
-
-def predict(mine, other, centers, before, high, low):
-    half, depth = mine.shape
-    rows = 2 * half
+    )(mine, other, select, more, centers, norms)
+
+
+def predict(mine, other, select, more, centers, before, high, low):
+    depth = mine.shape[1]
+    rows = select.shape[0]
+    half = rows // 2
     count = centers.shape[0]
     padded = high.shape[0]
     out = jax.ShapeDtypeStruct((padded, half), F32)
@@ -265,7 +259,7 @@
     vmem = pl.BlockSpec(memory_space=pltpu.VMEM)
     return pl.pallas_call(
         predict_body,
-        in_specs=[vmem] * 6,
+        in_specs=[vmem] * 8,
         out_specs=[vmem] * 4,
         out_shape=[out, out, value, value],
         scratch_shapes=[pltpu.VMEM((rows, depth), BF16), pltpu.VMEM((padded, rows), F32)],
@@ -276,7 +270,7 @@
             transcendentals=2 * rows * count,
         ),
         name="predict",
-    )(mine, other, centers, before, high, low)
+    )(mine, other, select, more, centers, before, high, low)
 
 
 def more_body(high_ref, low_ref, value_high_ref, value_low_ref, keep_ref, send_ref, total_ref):
@@ -431,53 +425,94 @@
     )(mine, other, targets, weights, high, low, new, out)
 
 
-def swap(x, chips, level):
-    bits = chips.bit_length() - 1
-    flip = [1, 1] if level < 0 else [2 << walk(sub, bits)[level] for sub in range(2)]
+def swap(x, chips, order=None, level=0):
+    flip = [2 << order(sub, chips.bit_length() - 1)[level] if order else 1 for sub in range(2)]
     return lax.ppermute(x, AXES, [(i, i ^ flip[i & 1]) for i in range(2 * chips)])
 
 
-def total_of(keep, send, chips, tied=()):
-    keep = keep + swap(send, chips, -1)
+def total_of(keep, send, chips):
+    keep = keep + swap(send, chips)
     for level in range(chips.bit_length() - 1):
         if level >= HALVINGS:
-            keep = keep + swap(keep, chips, level)
+            keep = keep + swap(keep, chips, walk, level)
             continue
         half = keep.shape[0] // 2
-        keep, send = keep[:half], keep[half:]
-        if level == 1 and tied:
-            send, *tied = lax.optimization_barrier((send, *tied))
-        keep = keep + swap(send, chips, level)
+        keep = keep[:half] + swap(keep[half:], chips, walk, level)
     for level in reversed(range(HALVINGS)):
-        keep = jnp.concatenate([keep, swap(keep, chips, level)])
-    return [keep, swap(keep, chips, -1), *tied]
+        keep = jnp.concatenate([keep, swap(keep, chips, walk, level)])
+    return keep, swap(keep, chips)
+
+
+def all_of(keep, chips, tied=()):
+    for level in range(chips.bit_length() - 1):
+        if level == TIED and tied:
+            keep, *tied = lax.optimization_barrier((keep, *tied))
+        keep = jnp.concatenate([keep, swap(keep, chips, far_first, level)])
+    return [keep, swap(keep, chips), *tied]
+
+
+def select_rows(owner, rank, offset, chips):
+    away = (owner >> 1) ^ lax.axis_index("center")
+    places = [
+        sum(((away >> bit) & 1) << k for k, bit in enumerate(far_first(sub, chips.bit_length() - 1)))
+        for sub in range(2)
+    ]
+    place = jnp.where(owner & 1 == 0, *places)
+    far = jnp.where(owner & 1 == lax.axis_index("sub"), 0, chips * SLOTS)
+    within = rank - offset
+    slot = jnp.where((within >= 0) & (within < SLOTS), far + place * SLOTS + within, -1)
+    return (slot[:, None] == jnp.arange(2 * chips * SLOTS, dtype=jnp.int32)[None, :]).astype(BF16)
+
+
+def more_rows(owner, rank, batch_index, centers, chips):
+    most = jnp.max(rank) + 1
+    shape = (batch_index.shape[1], centers.shape[1] // PARTS)
+
+    def one_pass(state):
+        offset, *found = state
+        select = select_rows(owner, rank, offset, chips)
+        for part in range(PARTS):
+            rows = pack_rows(offset.reshape(1), batch_index, centers, part)
+            slots = jnp.concatenate(all_of(rows, chips))
+            here = jnp.dot(select, slots, preferred_element_type=F32)
+            found[part] = (found[part].astype(F32) + here).astype(BF16)
+        return (offset + SLOTS, *found)
+
+    blank = jnp.zeros(shape, BF16)
+    return lax.while_loop(lambda state: state[0] < most, one_pass, (jnp.int32(SLOTS), blank, blank))[1:]
 
 
 def on_device(chips, centers, weights, targets, batch_index, nys_index, eigvec, eigval):
     rows = batch_index.shape[0]
     classes = weights.shape[1]
-    rank = eigvec.shape[1]
+    depth = eigvec.shape[1]
     unit = 8 * CHUNKS
-    units = -(-(classes + rank) // unit)
+    units = -(-(classes + depth) // unit)
     first = (units + 1) // 2 * unit
     second = units * unit - first
-    begin = first - rank
+    row = jnp.arange(rows, dtype=jnp.int32)
+    owner = batch_index // centers.shape[0]
+    earlier = (owner[None, :] == owner[:, None]) & (row[None, :] < row[:, None])
+    rank = jnp.sum(earlier.astype(jnp.int32), axis=1)
     batch_index = batch_index.reshape(1, rows)
     weights = weights.T
     targets = targets.T
     far = [pltpu.with_memory_space_constraint(x, pltpu.HBM) for x in (batch_index, centers)]
-    picked = [pick_batch(*far, part) for part in range(PARTS)]
+    packed = [pack_rows(jnp.zeros(1, jnp.int32), *far, part) for part in range(PARTS)]
+    more = more_rows(owner, rank, *far, chips)
     ready = [
         center_norms(centers),
         *spread_weights(nys_index.reshape(1, -1), eigvec.T, weights, first, second),
+        select_rows(owner, rank, 0, chips),
     ]
-    mine, other, norms, high1, low1, high2, low2, spread = total_of(*picked[0], chips, ready)
-    before = distances(mine, other, centers, norms)
-    keep, send, value_high, value_low = predict(*total_of(*picked[1], chips), centers, before, high1, low1)
+    mine, other, norms, high1, low1, high2, low2, spread, select = all_of(packed[0], chips, ready)
+    before = distances(mine, other, select, more[0], centers, norms)
+    late = all_of(packed[1], chips)
+    keep, send, value_high, value_low = predict(*late, select, more[1], centers, before, high1, low1)
     one = total_of(keep, send, chips)
     another = total_of(*predict_more(high2, low2, value_high, value_low), chips)
-    new, out, high, low = update(*one, targets, batch_index, eigval.reshape(1, rank), spread, weights)
-    new, out = update_more(*another, targets, weights, high, low, new, out, begin)
+    new, out, high, low = update(*one, targets, batch_index, eigval.reshape(1, depth), spread, weights)
+    new, out = update_more(*another, targets, weights, high, low, new, out, first - depth)
     return new.T, out.T
 
 

time: 86.7 us -> 93 us (1.073)
  waiting for transfers between devices: 27.7 us -> 15 us
  local copies, waits for them, and re-layouts: 0.13 us -> 7.59 us
  Pallas kernels: 16.9 us -> 24 us
  other arithmetic: 0.61 us -> 6.78 us
  starting transfers between devices: 40.3 us -> 37.5 us
    ppermute x28 -> x22, waiting for transfers between devices: 27.7 us -> 15 us  [swap(): lax.ppermute(x, AXES, [(i, i ^ flip[i & 1]) for i in range(2 * chips)])]
    concatenate x8 -> x9, other arithmetic: 0.15 us -> 5.69 us  [the longest x5 5.63 us: all_of(): keep = jnp.concatenate([keep, swap(keep, chips, far_first, level)])]
    unnamed x14 -> x41, local copies, waits for them, and re-layouts: 0.04 us -> 4.84 us
    pallas_call x4, Pallas kernels: 8.76 us -> 13.4 us  [the longest x1 4.97 us: predict(): pl.pallas_call(predict_body, in_specs=[vmem] * 8, out_specs=[vmem] * 4, o...]
    ppermute x28 -> x22, starting transfers between devices: 40.3 us -> 37.5 us  [swap(): lax.ppermute(x, AXES, [(i, i ^ flip[i & 1]) for i in range(2 * chips)])]
    pallas_call x1, Pallas kernels: 1.17 us -> 3.76 us  [center_norms(): pl.pallas_call(norms_body, grid=(count // block,), in_specs=[pl.BlockSpec...]
    broadcast_in_dim x0 -> x2, local copies, waits for them, and re-layouts: none -> 1.93 us  [more_rows(): blank = jnp.zeros(shape, BF16)]
  transfers between devices with their start and end apart: 28 -> 22, of which waited for: 15 -> 13; matrix products, arithmetic and copies ran while one was open for 1% -> 11% of each run, Pallas kernels for 11% -> 16%
where the time goes in v9:
time: 93 us; the launch traced here: 92.6 us
  starting transfers between devices  37.5 us (40%)
  Pallas kernels  24 us (26%)
  waiting for transfers between devices  15 us (16%)
  local copies, waits for them, and re-layouts  7.59 us (8%)
  other arithmetic  6.78 us (7%)
  between operations  1.76 us (2%)
    ppermute x22, starting transfers between devices, swap(): lax.ppermute(x, AXES, [(i, i ^ flip[i & 1]) for i in range(2 * chips)])  37.5 us
    ppermute x22, waiting for transfers between devices, swap(): lax.ppermute(x, AXES, [(i, i ^ flip[i & 1]) for i in range(2 * chips)])  15 us
    concatenate x5, other arithmetic, all_of(): keep = jnp.concatenate([keep, swap(keep, chips, far_first, level)])  5.63 us
    pallas_call x1, Pallas kernels, predict(): pl.pallas_call(predict_body, in_specs=[vmem] * 8, out_specs=[vmem] * 4, o...  4.97 us
    unnamed x41, local copies, waits for them, and re-layouts  4.84 us
    pallas_call x1, Pallas kernels, distances(): pl.pallas_call(distance_body, in_specs=[vmem] * 6, out_specs=vmem, out_sh...  4.55 us
    pallas_call x2, Pallas kernels, pack_rows(): pl.pallas_call(functools.partial(pack_body, part * depth), in_specs=[pl.B...  3.84 us
    pallas_call x1, Pallas kernels, center_norms(): pl.pallas_call(norms_body, grid=(count // block,), in_specs=[pl.BlockSpec...  3.76 us
  transfers between devices with their start and end apart: 22, of which 13 were waited for; matrix products, arithmetic and copies ran while one was open for 11% of the time, Pallas kernels for 16%

profile of v9, /device:TPU:1, one launch (start us, length us, event | category | flops | bytes accessed | tf_op | source)
XLA Modules:
  0.0 92.6 jit_solution(18390789942510502787)
XLA Ops:
  0.6 1.9 %pack_rows.4 = bf16[32,1536]{1,0:T(8,128)(2,1)S(1)} custom-call(s32[1]{0:T(128)} %constant.28.clone.1.offset_ref, s32[1,256]{1,0:T(1,128)} %bitcast.25, bf16[768,3072]{1,0:T(8,128)(2,1)} %centers_ref.5), custom_call_target="tpu_custom_call" | custom-call | flops 75497472 | bytes 2457600 | tf_op jit(solution)/shard_map/pack_rows/pallas_call | solution.py:101
  2.6 0.0 copy-start.24
  2.6 0.0 copy-start.26
  2.6 3.2 %collective-permute-start.8 = (bf16[32,1536]{1,0:T(8,128)(2,1)S(1)}, bf16[32,1536]{1,0:T(8,128)(2,1)}, u32[]{:S(2)}, u32[]{:S(2)}) collective-permute-start(bf16[32,1536]{1,0:T(8,128)(2,1)S(1)} %pack_rows.4), channel_id=1, source_target_pairs={{0,8},{1,9},{2,10},{3,11},{4,12},{5,13},{6,14},{7,15},{8,0},{9,1},... | collective-permute-start | bytes 294920 | tf_op jit(solution)/shard_map/ppermute | solution.py:430
  5.8 1.9 %pack_rows.5 = bf16[32,1536]{1,0:T(8,128)(2,1)S(1)} custom-call(s32[1]{0:T(128)} %constant.28.clone.1.offset_ref, s32[1,256]{1,0:T(1,128)} %bitcast.26, bf16[768,3072]{1,0:T(8,128)(2,1)} %centers_ref.5), custom_call_target="tpu_custom_call" | custom-call | flops 75497472 | bytes 2457600 | tf_op jit(solution)/shard_map/pack_rows/pallas_call | solution.py:101
  7.7 0.1 collective-permute-start.10
  7.8 0.2 convert_reduce_fusion
  8.0 0.6 fusion.12
  8.6 0.1 fusion.7.select_ref
  9.5 3.8 %center_norms.1.norm_ref = f32[768,128]{1,0:T(8,128)S(1)} custom-call(bf16[768,3072]{1,0:T(8,128)(2,1)} %centers_ref.5), custom_call_target="tpu_custom_call" | custom-call | flops 4718592 | bytes 4718592 | tf_op jit(solution)/shard_map/center_norms/pallas_call | solution.py:172
  13.2 0.8 copy-done.2
  14.0 1.6 %spread_weights.1 = (bf16[608,768]{1,0:T(8,128)(2,1)S(1)}, bf16[608,768]{1,0:T(8,128)(2,1)S(1)}, bf16[576,768]{1,0:T(8,128)(2,1)S(1)}, bf16[576,768]{1,0:T(8,128)(2,1)S(1)}, f32[160,768]{1,0:T(8,128)S(1)}) custom-call(s32[1,320]{1,0:T(1,128)S(1)} %reshape.55.index_ref, f32[160,320]{1,0:T(8,128)S(1)} %bitcast.21, f32[1000,768]{1,0:T(8,128)S(1)} %bitcast.16), custom_call_target="tpu_custom_call" | custom-call | flops 235929600 | bytes 7274496 | tf_op jit(solution)/shard_map/spread_weights/pallas_call | solution.py:145
  15.6 0.9 %copy-done.10 = bf16[576,768]{1,0:T(8,128)(2,1)} copy-done((bf16[576,768]{1,0:T(8,128)(2,1)}, bf16[576,768]{1,0:T(8,128)(2,1)S(1)}, u32[]{:S(2)}) %copy-start.10) | copy-done | bytes 884760
  16.5 0.8 copy-done.12
  17.3 1.0 %pad_maximum_fusion.12 = bf16[64,1536]{1,0:T(8,128)(2,1)S(1)} fusion(bf16[32,1536]{1,0:T(8,128)(2,1)} %collective-permute-done.10, bf16[32,1536]{1,0:T(8,128)(2,1)S(1)} %pack_rows.5), kind=kLoop, calls=%fused_computation.40 | loop fusion | flops 393216 | bytes 393216 | tf_op jit(solution)/shard_map/concatenate | solution.py:450
  18.3 1.3 %collective-permute-start.11 = (bf16[64,1536]{1,0:T(8,128)(2,1)S(1)}, bf16[64,1536]{1,0:T(8,128)(2,1)S(1)}, u32[]{:S(2)}, u32[]{:S(2)}) collective-permute-start(bf16[64,1536]{1,0:T(8,128)(2,1)S(1)} %pad_maximum_fusion.12), channel_id=1, source_target_pairs={{0,4},{1,3},{2,6},{3,1},{4,0},{5,7},{6,2},{7,5},{8,12},{9,11},{10,... | collective-permute-start | bytes 589832 | tf_op jit(solution)/shard_map/ppermute | solution.py:430
  19.7 0.9 pad_maximum_fusion.11
  20.6 0.3 collective-permute-start.9
  20.8 2.4 %collective-permute-done.11 = bf16[64,1536]{1,0:T(8,128)(2,1)S(1)} collective-permute-done((bf16[64,1536]{1,0:T(8,128)(2,1)S(1)}, bf16[64,1536]{1,0:T(8,128)(2,1)S(1)}, u32[]{:S(2)}, u32[]{:S(2)}) %collective-permute-start.11) | collective-permute-done | bytes 196640 | tf_op jit(solution)/shard_map/ppermute | solution.py:430
  23.2 0.9 pad_maximum_fusion.8
  24.1 1.4 %collective-permute-start.12 = (bf16[128,1536]{1,0:T(8,128)(2,1)S(1)}, bf16[128,1536]{1,0:T(8,128)(2,1)S(1)}, u32[]{:S(2)}, u32[]{:S(2)}) collective-permute-start(bf16[128,1536]{1,0:T(8,128)(2,1)S(1)} %pad_maximum_fusion.8), channel_id=1, source_target_pairs={{0,2},{1,5},{2,0},{3,7},{4,6},{5,1},{6,4},{7,3},{8,10},{9,13},{10,... | collective-permute-start | bytes 1179656 | tf_op jit(solution)/shard_map/ppermute | solution.py:430
  25.5 0.9 pad_maximum_fusion.7
  26.5 1.3 %collective-permute-start.14 = (bf16[128,1536]{1,0:T(8,128)(2,1)S(1)}, bf16[128,1536]{1,0:T(8,128)(2,1)S(1)}, u32[]{:S(2)}, u32[]{:S(2)}) collective-permute-start(bf16[128,1536]{1,0:T(8,128)(2,1)S(1)} %pad_maximum_fusion.7), channel_id=1, source_target_pairs={{0,2},{1,5},{2,0},{3,7},{4,6},{5,1},{6,4},{7,3},{8,10},{9,13},{10,... | collective-permute-start | bytes 1179656 | tf_op jit(solution)/shard_map/ppermute | solution.py:430
  27.8 0.8 constant_dynamic-update-slice_fusion.11
  28.6 3.1 %collective-permute-done.12 = bf16[128,1536]{1,0:T(8,128)(2,1)S(1)} collective-permute-done((bf16[128,1536]{1,0:T(8,128)(2,1)S(1)}, bf16[128,1536]{1,0:T(8,128)(2,1)S(1)}, u32[]{:S(2)}, u32[]{:S(2)}) %collective-permute-start.12) | collective-permute-done | bytes 393248 | tf_op jit(solution)/shard_map/ppermute | solution.py:430
  31.7 1.9 %pad_maximum_fusion.6.mine_ref = bf16[256,1536]{1,0:T(8,128)(2,1)} fusion(bf16[128,1536]{1,0:T(8,128)(2,1)S(1)} %collective-permute-done.12, bf16[64,1536]{1,0:T(8,128)(2,1)S(1)} %collective-permute-done.11, bf16[32,1536]{1,0:T(8,128)(2,1)} %collective-permute-done.10, bf16[32,1536]{1,0:T(8,128)(2,1)S(1)} %pack_rows.5), kind=kLoop, calls=%fused_computation.29 | loop fusion | flops 3145728 | bytes 1572864 | tf_op jit(solution)/shard_map/concatenate | solution.py:450
  33.6 2.1 %collective-permute-start.13 = (bf16[256,1536]{1,0:T(8,128)(2,1)}, bf16[256,1536]{1,0:T(8,128)(2,1)}, u32[]{:S(2)}, u32[]{:S(2)}) collective-permute-start(bf16[256,1536]{1,0:T(8,128)(2,1)} %pad_maximum_fusion.6.mine_ref), channel_id=1, source_target_pairs={{0,1},{1,0},{2,3},{3,2},{4,5},{5,4},{6,7},{7,6},{8,9},{9,8},{10,11... | collective-permute-start | bytes 2359304 | tf_op jit(solution)/shard_map/ppermute | solution.py:430
  35.7 0.3 collective-permute-done.14
  35.9 0.8 constant_dynamic-update-slice_fusion.10.mine_ref
  36.7 2.1 %collective-permute-start.15 = (bf16[256,1536]{1,0:T(8,128)(2,1)}, bf16[256,1536]{1,0:T(8,128)(2,1)}, u32[]{:S(2)}, u32[]{:S(2)}) collective-permute-start(bf16[256,1536]{1,0:T(8,128)(2,1)} %constant_dynamic-update-slice_fusion.10.mine_ref), channel_id=1, source_target_pairs={{0,1},{1,0},{2,3},{3,2},{4,5},{5,4},{6,7},{7,6},{8,9},{9,8},{10,11... | collective-permute-start | bytes 2359304 | tf_op jit(solution)/shard_map/ppermute | solution.py:430
  38.8 1.0 %broadcast_in_dim.30.clone = bf16[256,1536]{1,0:T(8,128)(2,1)} broadcast(bf16[]{:T(256)} %constant.17.clone.1), dimensions={} | broadcast | bytes 786434 | tf_op jit(solution)/shard_map/broadcast_in_dim | solution.py:481
  39.8 0.9 %broadcast_in_dim.30 = bf16[256,1536]{1,0:T(8,128)(2,1)} broadcast(bf16[]{:T(256)} %constant.17.clone.1), dimensions={} | broadcast | bytes 786434 | tf_op jit(solution)/shard_map/broadcast_in_dim | solution.py:481
  40.7 0.3 collective-permute-done.15.other_ref
  41.1 1.0 %copy-done.3 = f32[768,128]{1,0:T(8,128)S(1)} copy-done((f32[768,128]{1,0:T(8,128)S(1)}, f32[768,128]{1,0:T(8,128)}, u32[]{:S(2)}) %copy-start.3) | copy-done | bytes 393240
  42.1 4.6 %distances.1.before_ref = f32[768,256]{1,0:T(8,128)S(1)} custom-call(bf16[256,1536]{1,0:T(8,128)(2,1)} %constant_dynamic-update-slice_fusion.10.mine_ref, bf16[256,1536]{1,0:T(8,128)(2,1)} %collective-permute-done.15.other_ref, bf16[256,512]{1,0:T(8,128)(2,1)S(1)} %fusion.7.select_ref, bf16[256,1536]{1,0:T(8,128)(2,1)} %get-tuple-element.236, ...), custom_call_target="tpu_custom_call" | custom-call | flops 603979776 | bytes 3145728 | tf_op jit(solution)/shard_map/distances/pallas_call | solution.py:237
  46.6 0.4 copy-done.16
  47.0 0.1 copy-done.21
  47.1 5.0 %predict.1 = (f32[608,128]{1,0:T(8,128)S(1)}, f32[608,128]{1,0:T(8,128)S(1)}, bf16[768,256]{1,0:T(8,128)(2,1)S(1)}, bf16[768,256]{1,0:T(8,128)(2,1)S(1)}) custom-call(bf16[256,1536]{1,0:T(8,128)(2,1)} %pad_maximum_fusion.6.mine_ref, bf16[256,1536]{1,0:T(8,128)(2,1)} %collective-permute-done.13.other_ref, bf16[256,512]{1,0:T(8,128)(2,1)S(1)} %fusion.7.select_ref, ...), custom_call_target="tpu_custom_call" | custom-call | flops 1321205760 | bytes 5636096 | tf_op jit(solution)/shard_map/predict/pallas_call | solution.py:260
  52.1 0.4 collective-permute-start.23
  52.6 1.2 %collective-permute-done.23 = f32[608,128]{1,0:T(8,128)S(1)} collective-permute-done((f32[608,128]{1,0:T(8,128)S(1)}, f32[608,128]{1,0:T(8,128)S(1)}, u32[]{:S(2)}, u32[]{:S(2)}) %collective-permute-start.23) | collective-permute-done | bytes 311328 | tf_op jit(solution)/shard_map/ppermute | solution.py:430
  53.9 1.7 %collective-permute-start.24 = (f32[304,128]{1,0:T(8,128)S(1)}, f32[304,128]{1,0:T(8,128)S(1)}, u32[]{:S(2)}, u32[]{:S(2)}) collective-permute-start(f32[304,128]{1,0:T(8,128)S(1)} %slice.37), channel_id=1, source_target_pairs={{0,2},{1,5},{2,0},{3,7},{4,6},{5,1},{6,4},{7,3},{8,10},{9,13},{10,... | collective-permute-start | bytes 466952 | tf_op jit(solution)/shard_map/ppermute | solution.py:430
  55.5 0.9 predict_more.1
  56.4 0.7 collective-permute-start.16
  57.1 1.3 %collective-permute-done.24 = f32[304,128]{1,0:T(8,128)S(1)} collective-permute-done((f32[304,128]{1,0:T(8,128)S(1)}, f32[304,128]{1,0:T(8,128)S(1)}, u32[]{:S(2)}, u32[]{:S(2)}) %collective-permute-start.24) | collective-permute-done | bytes 155680 | tf_op jit(solution)/shard_map/ppermute | solution.py:430
  58.5 1.5 %collective-permute-start.25 = (f32[152,128]{1,0:T(8,128)S(1)}, f32[152,128]{1,0:T(8,128)S(1)}, u32[]{:S(2)}, u32[]{:S(2)}) collective-permute-start(f32[152,128]{1,0:T(8,128)S(1)} %slice.39), channel_id=1, source_target_pairs={{0,4},{1,3},{2,6},{3,1},{4,0},{5,7},{6,2},{7,5},{8,12},{9,11},{10,... | collective-permute-start | bytes 233480 | tf_op jit(solution)/shard_map/ppermute | solution.py:430
  60.0 1.4 %collective-permute-start.17 = (f32[288,128]{1,0:T(8,128)S(1)}, f32[288,128]{1,0:T(8,128)S(1)}, u32[]{:S(2)}, u32[]{:S(2)}) collective-permute-start(f32[288,128]{1,0:T(8,128)S(1)} %slice.33), channel_id=1, source_target_pairs={{0,2},{1,5},{2,0},{3,7},{4,6},{5,1},{6,4},{7,3},{8,10},{9,13},{10,... | collective-permute-start | bytes 442376 | tf_op jit(solution)/shard_map/ppermute | solution.py:430
  61.4 0.4 collective-permute-done.25
  61.8 2.5 %collective-permute-start.26 = (f32[152,128]{1,0:T(8,128)S(1)}, f32[152,128]{1,0:T(8,128)S(1)}, u32[]{:S(2)}, u32[]{:S(2)}) collective-permute-start(f32[152,128]{1,0:T(8,128)S(1)} %slice_add_fusion.2), channel_id=1, source_target_pairs={{0,8},{1,9},{2,10},{3,11},{4,12},{5,13},{6,14},{7,15},{8,0},{9,1},... | collective-permute-start | bytes 233480 | tf_op jit(solution)/shard_map/ppermute | solution.py:430
  64.4 0.8 collective-permute-done.17
  65.2 0.5 collective-permute-start.18
  65.7 0.4 collective-permute-done.26
  66.2 1.3 %collective-permute-start.27 = (f32[152,128]{1,0:T(8,128)S(1)}, f32[152,128]{1,0:T(8,128)S(1)}, u32[]{:S(2)}, u32[]{:S(2)}) collective-permute-start(f32[152,128]{1,0:T(8,128)S(1)} %add.111), channel_id=1, source_target_pairs={{0,4},{1,3},{2,6},{3,1},{4,0},{5,7},{6,2},{7,5},{8,12},{9,11},{10,... | collective-permute-start | bytes 233480 | tf_op jit(solution)/shard_map/ppermute | solution.py:430
  67.5 1.0 %collective-permute-done.18 = f32[144,128]{1,0:T(8,128)S(1)} collective-permute-done((f32[144,128]{1,0:T(8,128)S(1)}, f32[144,128]{1,0:T(8,128)S(1)}, u32[]{:S(2)}, u32[]{:S(2)}) %collective-permute-start.18) | collective-permute-done | bytes 73760 | tf_op jit(solution)/shard_map/ppermute | solution.py:430
  68.5 2.4 %collective-permute-start.19 = (f32[144,128]{1,0:T(8,128)S(1)}, f32[144,128]{1,0:T(8,128)S(1)}, u32[]{:S(2)}, u32[]{:S(2)}) collective-permute-start(f32[144,128]{1,0:T(8,128)S(1)} %slice_add_fusion.3), channel_id=1, source_target_pairs={{0,8},{1,9},{2,10},{3,11},{4,12},{5,13},{6,14},{7,15},{8,0},{9,1},... | collective-permute-start | bytes 221192 | tf_op jit(solution)/shard_map/ppermute | solution.py:430
  70.9 1.8 %collective-permute-done.19 = f32[144,128]{1,0:T(8,128)S(1)} collective-permute-done((f32[144,128]{1,0:T(8,128)S(1)}, f32[144,128]{1,0:T(8,128)S(1)}, u32[]{:S(2)}, u32[]{:S(2)}) %collective-permute-start.19) | collective-permute-done | bytes 73760 | tf_op jit(solution)/shard_map/ppermute | solution.py:430
  72.7 0.5 collective-permute-start.20
  73.2 1.9 %collective-permute-start.28 = (f32[304,128]{1,0:T(8,128)S(1)}, f32[304,128]{1,0:T(8,128)S(1)}, u32[]{:S(2)}, u32[]{:S(2)}) collective-permute-start(f32[304,128]{1,0:T(8,128)S(1)} %pad_maximum_fusion.13), channel_id=1, source_target_pairs={{0,2},{1,5},{2,0},{3,7},{4,6},{5,1},{6,4},{7,3},{8,10},{9,13},{10,... | collective-permute-start | bytes 466952 | tf_op jit(solution)/shard_map/ppermute | solution.py:430
  75.1 0.9 collective-permute-done.20
  76.0 1.5 %collective-permute-start.21 = (f32[288,128]{1,0:T(8,128)S(1)}, f32[288,128]{1,0:T(8,128)S(1)}, u32[]{:S(2)}, u32[]{:S(2)}) collective-permute-start(f32[288,128]{1,0:T(8,128)S(1)} %pad_maximum_fusion.14), channel_id=1, source_target_pairs={{0,2},{1,5},{2,0},{3,7},{4,6},{5,1},{6,4},{7,3},{8,10},{9,13},{10,... | collective-permute-start | bytes 442376 | tf_op jit(solution)/shard_map/ppermute | solution.py:430
  77.5 1.0 %collective-permute-done.28 = f32[304,128]{1,0:T(8,128)S(1)} collective-permute-done((f32[304,128]{1,0:T(8,128)S(1)}, f32[304,128]{1,0:T(8,128)S(1)}, u32[]{:S(2)}, u32[]{:S(2)}) %collective-permute-start.28) | collective-permute-done | bytes 155680 | tf_op jit(solution)/shard_map/ppermute | solution.py:430
  78.5 6.4 %collective-permute-start.29 = (f32[608,128]{1,0:T(8,128)S(1)}, f32[608,128]{1,0:T(8,128)S(1)}, u32[]{:S(2)}, u32[]{:S(2)}) collective-permute-start(f32[608,128]{1,0:T(8,128)S(1)} %pad_maximum_fusion.9.mine_ref), channel_id=1, source_target_pairs={{0,1},{1,0},{2,3},{3,2},{4,5},{5,4},{6,7},{7,6},{8,9},{9,8},{10,11... | collective-permute-start | bytes 933896 | tf_op jit(solution)/shard_map/ppermute | solution.py:430
  84.9 3.0 %collective-permute-start.22 = (f32[576,128]{1,0:T(8,128)S(1)}, f32[576,128]{1,0:T(8,128)S(1)}, u32[]{:S(2)}, u32[]{:S(2)}) collective-permute-start(f32[576,128]{1,0:T(8,128)S(1)} %pad_maximum_fusion.10.mine_ref), channel_id=1, source_target_pairs={{0,1},{1,0},{2,3},{3,2},{4,5},{5,4},{6,7},{7,6},{8,9},{9,8},{10,11... | collective-permute-start | bytes 884744 | tf_op jit(solution)/shard_map/ppermute | solution.py:430
  88.0 2.4 %update.1 = (f32[1000,768]{1,0:T(8,128)}, f32[1000,256]{1,0:T(8,128)}, bf16[256,768]{1,0:T(8,128)(2,1)S(1)}, bf16[256,768]{1,0:T(8,128)(2,1)S(1)}) custom-call(f32[608,128]{1,0:T(8,128)S(1)} %pad_maximum_fusion.9.mine_ref, f32[608,128]{1,0:T(8,128)S(1)} %collective-permute-done.29.other_ref, f32[1000,256]{1,0:T(8,128)S(1)} %bitcast.19, ...), custom_call_target="tpu_custom_call" | custom-call | flops 717225984 | bytes 3670016 | tf_op jit(solution)/shard_map/update/pallas_call | solution.py:368
  90.4 2.0 %update_more.1 = (f32[1000,768]{1,0:T(8,128)}, f32[1000,256]{1,0:T(8,128)}) custom-call(f32[576,128]{1,0:T(8,128)S(1)} %pad_maximum_fusion.10.mine_ref, f32[576,128]{1,0:T(8,128)S(1)} %collective-permute-done.22.other_ref, f32[1000,256]{1,0:T(8,128)S(1)} %bitcast.20, f32[1000,768]{1,0:T(8,128)S(1)} %bitcast.18, ...), custom_call_target="tpu_custom_call", output_to_operand_aliasing={{0}: (6, {}), {1}: (7, {})} | custom-call | flops 651165696 | bytes 4521984 | tf_op jit(solution)/shard_map/update_more/pallas_call | solution.py:406
  (60 shorter events, 0.4 us)
Async XLA Ops:
  2.6 5.2 %copy-start.24 = (s32[256]{0:T(256)S(1)}, s32[256]{0:T(256)}, u32[]{:S(2)}) copy-start(s32[256]{0:T(256)} %param.12) | copy-start | bytes 3076
  2.6 6.2 %copy-start.26 = (s32[320]{0:T(512)S(1)}, s32[320]{0:T(512)}, u32[]{:S(2)}) copy-start(s32[320]{0:T(512)} %param.13) | copy-start | bytes 3844
  2.6 17.1 %collective-permute-start.8 = (bf16[32,1536]{1,0:T(8,128)(2,1)S(1)}, bf16[32,1536]{1,0:T(8,128)(2,1)}, u32[]{:S(2)}, u32[]{:S(2)}) collective-permute-start(bf16[32,1536]{1,0:T(8,128)(2,1)S(1)} %pack_rows.4), channel_id=1, source_target_pairs={{0,8},{1,9},{2,10},{3,11},{4,12},{5,13},{6,14},{7,15},{8,0},{9,1},... | collective-permute-start | bytes 294920 | tf_op jit(solution)/shard_map/ppermute | solution.py:430
  7.7 9.6 %collective-permute-start.10 = (bf16[32,1536]{1,0:T(8,128)(2,1)S(1)}, bf16[32,1536]{1,0:T(8,128)(2,1)}, u32[]{:S(2)}, u32[]{:S(2)}) collective-permute-start(bf16[32,1536]{1,0:T(8,128)(2,1)S(1)} %pack_rows.5), channel_id=1, source_target_pairs={{0,8},{1,9},{2,10},{3,11},{4,12},{5,13},{6,14},{7,15},{8,0},{9,1},... | collective-permute-start | bytes 294920 | tf_op jit(solution)/shard_map/ppermute | solution.py:430
  9.4 4.6 %copy-start = (f32[768,1000]{0,1:T(8,128)S(1)}, f32[768,1000]{0,1:T(8,128)}, u32[]{:S(2)}) copy-start(f32[768,1000]{0,1:T(8,128)} %param.10) | copy-start | bytes 9216004
  9.4 4.6 %copy-start.14 = (f32[320,160]{0,1:T(8,128)S(1)}, f32[320,160]{0,1:T(8,128)}, u32[]{:S(2)}) copy-start(f32[320,160]{0,1:T(8,128)} %param.14) | copy-start | bytes 614404
  13.2 0.8 copy-start.2
  15.6 0.9 %copy-start.10 = (bf16[576,768]{1,0:T(8,128)(2,1)}, bf16[576,768]{1,0:T(8,128)(2,1)S(1)}, u32[]{:S(2)}) copy-start(bf16[576,768]{1,0:T(8,128)(2,1)S(1)} %get-tuple-element.77.low_ref) | copy-start | bytes 2654212
  16.5 0.8 copy-start.12
  17.3 11.3 %copy-start.4 = (bf16[608,768]{1,0:T(8,128)(2,1)}, bf16[608,768]{1,0:T(8,128)(2,1)S(1)}, u32[]{:S(2)}) copy-start(bf16[608,768]{1,0:T(8,128)(2,1)S(1)} %get-tuple-element.83.high_ref) | copy-start | bytes 2801668
  17.3 11.3 %copy-start.6 = (bf16[608,768]{1,0:T(8,128)(2,1)}, bf16[608,768]{1,0:T(8,128)(2,1)S(1)}, u32[]{:S(2)}) copy-start(bf16[608,768]{1,0:T(8,128)(2,1)S(1)} %get-tuple-element.84.low_ref) | copy-start | bytes 2801668
  17.3 11.3 %copy-start.8 = (bf16[576,768]{1,0:T(8,128)(2,1)}, bf16[576,768]{1,0:T(8,128)(2,1)S(1)}, u32[]{:S(2)}) copy-start(bf16[576,768]{1,0:T(8,128)(2,1)S(1)} %get-tuple-element.76.high_ref) | copy-start | bytes 2654212
  18.3 4.9 %collective-permute-start.11 = (bf16[64,1536]{1,0:T(8,128)(2,1)S(1)}, bf16[64,1536]{1,0:T(8,128)(2,1)S(1)}, u32[]{:S(2)}, u32[]{:S(2)}) collective-permute-start(bf16[64,1536]{1,0:T(8,128)(2,1)S(1)} %pad_maximum_fusion.12), channel_id=1, source_target_pairs={{0,4},{1,3},{2,6},{3,1},{4,0},{5,7},{6,2},{7,5},{8,12},{9,11},{10,... | collective-permute-start | bytes 589832 | tf_op jit(solution)/shard_map/ppermute | solution.py:430
  20.6 5.0 %collective-permute-start.9 = (bf16[64,1536]{1,0:T(8,128)(2,1)S(1)}, bf16[64,1536]{1,0:T(8,128)(2,1)S(1)}, u32[]{:S(2)}, u32[]{:S(2)}) collective-permute-start(bf16[64,1536]{1,0:T(8,128)(2,1)S(1)} %pad_maximum_fusion.11), channel_id=1, source_target_pairs={{0,4},{1,3},{2,6},{3,1},{4,0},{5,7},{6,2},{7,5},{8,12},{9,11},{10,... | collective-permute-start | bytes 589832 | tf_op jit(solution)/shard_map/ppermute | solution.py:430
  24.1 7.6 %collective-permute-start.12 = (bf16[128,1536]{1,0:T(8,128)(2,1)S(1)}, bf16[128,1536]{1,0:T(8,128)(2,1)S(1)}, u32[]{:S(2)}, u32[]{:S(2)}) collective-permute-start(bf16[128,1536]{1,0:T(8,128)(2,1)S(1)} %pad_maximum_fusion.8), channel_id=1, source_target_pairs={{0,2},{1,5},{2,0},{3,7},{4,6},{5,1},{6,4},{7,3},{8,10},{9,13},{10,... | collective-permute-start | bytes 1179656 | tf_op jit(solution)/shard_map/ppermute | solution.py:430
  26.5 9.5 %collective-permute-start.14 = (bf16[128,1536]{1,0:T(8,128)(2,1)S(1)}, bf16[128,1536]{1,0:T(8,128)(2,1)S(1)}, u32[]{:S(2)}, u32[]{:S(2)}) collective-permute-start(bf16[128,1536]{1,0:T(8,128)(2,1)S(1)} %pad_maximum_fusion.7), channel_id=1, source_target_pairs={{0,2},{1,5},{2,0},{3,7},{4,6},{5,1},{6,4},{7,3},{8,10},{9,13},{10,... | collective-permute-start | bytes 1179656 | tf_op jit(solution)/shard_map/ppermute | solution.py:430
  33.6 13.1 %collective-permute-start.13 = (bf16[256,1536]{1,0:T(8,128)(2,1)}, bf16[256,1536]{1,0:T(8,128)(2,1)}, u32[]{:S(2)}, u32[]{:S(2)}) collective-permute-start(bf16[256,1536]{1,0:T(8,128)(2,1)} %pad_maximum_fusion.6.mine_ref), channel_id=1, source_target_pairs={{0,1},{1,0},{2,3},{3,2},{4,5},{5,4},{6,7},{7,6},{8,9},{9,8},{10,11... | collective-permute-start | bytes 2359304 | tf_op jit(solution)/shard_map/ppermute | solution.py:430
  36.7 4.3 %collective-permute-start.15 = (bf16[256,1536]{1,0:T(8,128)(2,1)}, bf16[256,1536]{1,0:T(8,128)(2,1)}, u32[]{:S(2)}, u32[]{:S(2)}) collective-permute-start(bf16[256,1536]{1,0:T(8,128)(2,1)} %constant_dynamic-update-slice_fusion.10.mine_ref), channel_id=1, source_target_pairs={{0,1},{1,0},{2,3},{3,2},{4,5},{5,4},{6,7},{7,6},{8,9},{9,8},{10,11... | collective-permute-start | bytes 2359304 | tf_op jit(solution)/shard_map/ppermute | solution.py:430
  41.1 1.0 %copy-start.3 = (f32[768,128]{1,0:T(8,128)S(1)}, f32[768,128]{1,0:T(8,128)}, u32[]{:S(2)}) copy-start(f32[768,128]{1,0:T(8,128)} %copy-done.2) | copy-start | bytes 1179652
  42.0 4.6 %copy-start.5 = (bf16[608,768]{1,0:T(8,128)(2,1)S(1)}, bf16[608,768]{1,0:T(8,128)(2,1)}, u32[]{:S(2)}) copy-start(bf16[608,768]{1,0:T(8,128)(2,1)} %copy-done.4) | copy-start | bytes 2801668
  42.0 4.6 %copy-start.7 = (bf16[608,768]{1,0:T(8,128)(2,1)S(1)}, bf16[608,768]{1,0:T(8,128)(2,1)}, u32[]{:S(2)}) copy-start(bf16[608,768]{1,0:T(8,128)(2,1)} %copy-done.6) | copy-start | bytes 2801668
  42.1 5.0 %copy-start.16 = (bf16[768,3072]{1,0:T(8,128)(2,1)S(1)}, bf16[768,3072]{1,0:T(8,128)(2,1)}, u32[]{:S(2)}) copy-start(bf16[768,3072]{1,0:T(8,128)(2,1)} %get-tuple-element.242) | copy-start | bytes 14155780
  42.1 5.1 %copy-start.21 = (bf16[256,1536]{1,0:T(8,128)(2,1)S(1)}, bf16[256,1536]{1,0:T(8,128)(2,1)}, u32[]{:S(2)}) copy-start(bf16[256,1536]{1,0:T(8,128)(2,1)} %get-tuple-element.237) | copy-start | bytes 2359300
  47.1 8.4 %copy-start.9 = (bf16[576,768]{1,0:T(8,128)(2,1)S(1)}, bf16[576,768]{1,0:T(8,128)(2,1)}, u32[]{:S(2)}) copy-start(bf16[576,768]{1,0:T(8,128)(2,1)} %copy-done.8) | copy-start | bytes 2654212
  47.1 8.4 %copy-start.11 = (bf16[576,768]{1,0:T(8,128)(2,1)S(1)}, bf16[576,768]{1,0:T(8,128)(2,1)}, u32[]{:S(2)}) copy-start(bf16[576,768]{1,0:T(8,128)(2,1)} %copy-done.10) | copy-start | bytes 2654212
  52.1 1.7 %collective-permute-start.23 = (f32[608,128]{1,0:T(8,128)S(1)}, f32[608,128]{1,0:T(8,128)S(1)}, u32[]{:S(2)}, u32[]{:S(2)}) collective-permute-start(f32[608,128]{1,0:T(8,128)S(1)} %get-tuple-element.90), channel_id=1, source_target_pairs={{0,1},{1,0},{2,3},{3,2},{4,5},{5,4},{6,7},{7,6},{8,9},{9,8},{10,11... | collective-permute-start | bytes 933896 | tf_op jit(solution)/shard_map/ppermute | solution.py:430
  53.9 4.6 %collective-permute-start.24 = (f32[304,128]{1,0:T(8,128)S(1)}, f32[304,128]{1,0:T(8,128)S(1)}, u32[]{:S(2)}, u32[]{:S(2)}) collective-permute-start(f32[304,128]{1,0:T(8,128)S(1)} %slice.37), channel_id=1, source_target_pairs={{0,2},{1,5},{2,0},{3,7},{4,6},{5,1},{6,4},{7,3},{8,10},{9,13},{10,... | collective-permute-start | bytes 466952 | tf_op jit(solution)/shard_map/ppermute | solution.py:430
  56.4 3.5 %collective-permute-start.16 = (f32[576,128]{1,0:T(8,128)S(1)}, f32[576,128]{1,0:T(8,128)S(1)}, u32[]{:S(2)}, u32[]{:S(2)}) collective-permute-start(f32[576,128]{1,0:T(8,128)S(1)} %get-tuple-element.88), channel_id=1, source_target_pairs={{0,1},{1,0},{2,3},{3,2},{4,5},{5,4},{6,7},{7,6},{8,9},{9,8},{10,11... | collective-permute-start | bytes 884744 | tf_op jit(solution)/shard_map/ppermute | solution.py:430
  58.5 3.3 %collective-permute-start.25 = (f32[152,128]{1,0:T(8,128)S(1)}, f32[152,128]{1,0:T(8,128)S(1)}, u32[]{:S(2)}, u32[]{:S(2)}) collective-permute-start(f32[152,128]{1,0:T(8,128)S(1)} %slice.39), channel_id=1, source_target_pairs={{0,4},{1,3},{2,6},{3,1},{4,0},{5,7},{6,2},{7,5},{8,12},{9,11},{10,... | collective-permute-start | bytes 233480 | tf_op jit(solution)/shard_map/ppermute | solution.py:430
  60.0 5.2 %collective-permute-start.17 = (f32[288,128]{1,0:T(8,128)S(1)}, f32[288,128]{1,0:T(8,128)S(1)}, u32[]{:S(2)}, u32[]{:S(2)}) collective-permute-start(f32[288,128]{1,0:T(8,128)S(1)} %slice.33), channel_id=1, source_target_pairs={{0,2},{1,5},{2,0},{3,7},{4,6},{5,1},{6,4},{7,3},{8,10},{9,13},{10,... | collective-permute-start | bytes 442376 | tf_op jit(solution)/shard_map/ppermute | solution.py:430
  61.8 26.2 %copy-start.1 = (f32[256,1000]{0,1:T(8,128)S(1)}, f32[256,1000]{0,1:T(8,128)}, u32[]{:S(2)}) copy-start(f32[256,1000]{0,1:T(8,128)} %param.11) | copy-start | bytes 3072004
  61.8 26.2 %copy-start.13 = (f32[160,768]{1,0:T(8,128)S(1)}, f32[160,768]{1,0:T(8,128)}, u32[]{:S(2)}) copy-start(f32[160,768]{1,0:T(8,128)} %copy-done.12) | copy-start | bytes 1474564
  61.8 26.2 %copy-start.15 = (f32[160]{0:T(256)S(1)}, f32[160]{0:T(256)}, u32[]{:S(2)}) copy-start(f32[160]{0:T(256)} %param.15) | copy-start | bytes 1924
  61.8 4.3 %collective-permute-start.26 = (f32[152,128]{1,0:T(8,128)S(1)}, f32[152,128]{1,0:T(8,128)S(1)}, u32[]{:S(2)}, u32[]{:S(2)}) collective-permute-start(f32[152,128]{1,0:T(8,128)S(1)} %slice_add_fusion.2), channel_id=1, source_target_pairs={{0,8},{1,9},{2,10},{3,11},{4,12},{5,13},{6,14},{7,15},{8,0},{9,1},... | collective-permute-start | bytes 233480 | tf_op jit(solution)/shard_map/ppermute | solution.py:430
  65.2 3.3 %collective-permute-start.18 = (f32[144,128]{1,0:T(8,128)S(1)}, f32[144,128]{1,0:T(8,128)S(1)}, u32[]{:S(2)}, u32[]{:S(2)}) collective-permute-start(f32[144,128]{1,0:T(8,128)S(1)} %slice.35), channel_id=1, source_target_pairs={{0,4},{1,3},{2,6},{3,1},{4,0},{5,7},{6,2},{7,5},{8,12},{9,11},{10,... | collective-permute-start | bytes 221192 | tf_op jit(solution)/shard_map/ppermute | solution.py:430
  66.2 7.0 %collective-permute-start.27 = (f32[152,128]{1,0:T(8,128)S(1)}, f32[152,128]{1,0:T(8,128)S(1)}, u32[]{:S(2)}, u32[]{:S(2)}) collective-permute-start(f32[152,128]{1,0:T(8,128)S(1)} %add.111), channel_id=1, source_target_pairs={{0,4},{1,3},{2,6},{3,1},{4,0},{5,7},{6,2},{7,5},{8,12},{9,11},{10,... | collective-permute-start | bytes 233480 | tf_op jit(solution)/shard_map/ppermute | solution.py:430
  68.5 4.2 %collective-permute-start.19 = (f32[144,128]{1,0:T(8,128)S(1)}, f32[144,128]{1,0:T(8,128)S(1)}, u32[]{:S(2)}, u32[]{:S(2)}) collective-permute-start(f32[144,128]{1,0:T(8,128)S(1)} %slice_add_fusion.3), channel_id=1, source_target_pairs={{0,8},{1,9},{2,10},{3,11},{4,12},{5,13},{6,14},{7,15},{8,0},{9,1},... | collective-permute-start | bytes 221192 | tf_op jit(solution)/shard_map/ppermute | solution.py:430
  72.7 3.3 %collective-permute-start.20 = (f32[144,128]{1,0:T(8,128)S(1)}, f32[144,128]{1,0:T(8,128)S(1)}, u32[]{:S(2)}, u32[]{:S(2)}) collective-permute-start(f32[144,128]{1,0:T(8,128)S(1)} %add.107), channel_id=1, source_target_pairs={{0,4},{1,3},{2,6},{3,1},{4,0},{5,7},{6,2},{7,5},{8,12},{9,11},{10,... | collective-permute-start | bytes 221192 | tf_op jit(solution)/shard_map/ppermute | solution.py:430
  73.2 5.3 %collective-permute-start.28 = (f32[304,128]{1,0:T(8,128)S(1)}, f32[304,128]{1,0:T(8,128)S(1)}, u32[]{:S(2)}, u32[]{:S(2)}) collective-permute-start(f32[304,128]{1,0:T(8,128)S(1)} %pad_maximum_fusion.13), channel_id=1, source_target_pairs={{0,2},{1,5},{2,0},{3,7},{4,6},{5,1},{6,4},{7,3},{8,10},{9,13},{10,... | collective-permute-start | bytes 466952 | tf_op jit(solution)/shard_map/ppermute | solution.py:430
  76.0 8.9 %collective-permute-start.21 = (f32[288,128]{1,0:T(8,128)S(1)}, f32[288,128]{1,0:T(8,128)S(1)}, u32[]{:S(2)}, u32[]{:S(2)}) collective-permute-start(f32[288,128]{1,0:T(8,128)S(1)} %pad_maximum_fusion.14), channel_id=1, source_target_pairs={{0,2},{1,5},{2,0},{3,7},{4,6},{5,1},{6,4},{7,3},{8,10},{9,13},{10,... | collective-permute-start | bytes 442376 | tf_op jit(solution)/shard_map/ppermute | solution.py:430
  78.5 9.5 %collective-permute-start.29 = (f32[608,128]{1,0:T(8,128)S(1)}, f32[608,128]{1,0:T(8,128)S(1)}, u32[]{:S(2)}, u32[]{:S(2)}) collective-permute-start(f32[608,128]{1,0:T(8,128)S(1)} %pad_maximum_fusion.9.mine_ref), channel_id=1, source_target_pairs={{0,1},{1,0},{2,3},{3,2},{4,5},{5,4},{6,7},{7,6},{8,9},{9,8},{10,11... | collective-permute-start | bytes 933896 | tf_op jit(solution)/shard_map/ppermute | solution.py:430
  84.9 5.5 %collective-permute-start.22 = (f32[576,128]{1,0:T(8,128)S(1)}, f32[576,128]{1,0:T(8,128)S(1)}, u32[]{:S(2)}, u32[]{:S(2)}) collective-permute-start(f32[576,128]{1,0:T(8,128)S(1)} %pad_maximum_fusion.10.mine_ref), channel_id=1, source_target_pairs={{0,1},{1,0},{2,3},{3,2},{4,5},{5,4},{6,7},{7,6},{8,9},{9,8},{10,11... | collective-permute-start | bytes 884744 | tf_op jit(solution)/shard_map/ppermute | solution.py:430

commit v10 on v8

--- a/solution.py
+++ b/solution.py
@@ -123,13 +123,33 @@
     )(batch_index, centers)
 
 
-def pack_body(first, index_hbm, rank_hbm, centers_hbm, out_ref, index_ref, rank_ref, centers_ref, sems):
+def fits_body(count, index_hbm, fits_ref, index_ref, sem):
+    copy = pltpu.make_async_copy(index_hbm, index_ref, sem)
+    copy.start()
+    copy.wait()
+    devices = 2 * lax.axis_size("center")
+    starts = lax.broadcasted_iota(jnp.int32, (devices, 1), 0) * count
+    local = index_ref[...] - starts
+    held = jnp.sum(jnp.where((local >= 0) & (local < count), 1.0, 0.0), axis=1, keepdims=True)
+    fits_ref[0] = (jnp.max(held) <= SLOTS).astype(jnp.int32)
+
+
+def rows_fit(batch_index, count):
+    return pl.pallas_call(
+        functools.partial(fits_body, count),
+        in_specs=[pl.BlockSpec(memory_space=pltpu.HBM)],
+        out_specs=pl.BlockSpec(memory_space=pltpu.SMEM),
+        out_shape=jax.ShapeDtypeStruct((1,), jnp.int32),
+        scratch_shapes=[pltpu.VMEM(batch_index.shape, jnp.int32), pltpu.SemaphoreType.DMA],
+        compiler_params=params(),
+        name="rows_fit",
+    )(batch_index)[0]
+
+
+def pack_body(first, index_hbm, centers_hbm, out_ref, index_ref, centers_ref, sems):
     blocks, count, block = centers_ref.shape
     rows = index_ref.shape[1]
-    copies = [
-        pltpu.make_async_copy(index_hbm, index_ref, sems.at[blocks]),
-        pltpu.make_async_copy(rank_hbm, rank_ref, sems.at[blocks + 1]),
-    ] + [
+    copies = [pltpu.make_async_copy(index_hbm, index_ref, sems.at[blocks])] + [
         pltpu.make_async_copy(
             centers_hbm.at[:, pl.ds(first + k * block, block)], centers_ref.at[k], sems.at[k]
         )
@@ -138,19 +158,20 @@
     for copy in copies:
         copy.start()
     copies[0].wait()
-    copies[1].wait()
     start = (lax.axis_index("center") * 2 + lax.axis_index("sub")) * count
     local = index_ref[...] - start
-    rank = jnp.where((local >= 0) & (local < count), rank_ref[...], -1)
-    slots = lax.broadcasted_iota(jnp.int32, (SLOTS, rows), 0)
-    to_slot = jnp.where(slots == rank, 1.0, 0.0).astype(BF16)
+    here = jnp.where((local >= 0) & (local < count), 1.0, 0.0)
+    earlier = lax.broadcasted_iota(jnp.int32, (rows, rows), 0) < lax.broadcasted_iota(jnp.int32, (rows, rows), 1)
+    rank = dot(jnp.broadcast_to(here, (8, rows)).astype(BF16), jnp.where(earlier, 1.0, 0.0).astype(BF16), NN)[0:1]
+    slots = lax.broadcasted_iota(jnp.int32, (SLOTS, 1), 0).astype(F32)
+    to_slot = jnp.where(slots == rank, here, 0.0).astype(BF16)
     pick = dot(to_slot, pick_rows(index_ref, count, start, BF16, 1.0), NN).astype(BF16)
     for k in range(blocks):
-        copies[k + 2].wait()
+        copies[k + 1].wait()
         out_ref[:, k * block : (k + 1) * block] = dot(pick, centers_ref[k], NN).astype(BF16)
 
 
-def pack_rows(batch_index, rank, centers, part):
+def pack_rows(batch_index, centers, part):
     rows = batch_index.shape[1]
     count, depth = centers.shape
     depth = depth // PARTS
@@ -158,21 +179,54 @@
     hbm = pl.BlockSpec(memory_space=pltpu.HBM)
     return pl.pallas_call(
         functools.partial(pack_body, part * depth),
-        in_specs=[hbm, hbm, hbm],
+        in_specs=[hbm, hbm],
         out_specs=pl.BlockSpec(memory_space=pltpu.VMEM),
         out_shape=jax.ShapeDtypeStruct((SLOTS, depth), BF16),
         scratch_shapes=[
             pltpu.VMEM((1, rows), jnp.int32),
-            pltpu.VMEM((1, rows), jnp.int32),
             pltpu.VMEM((depth // block, count, block), BF16),
-            pltpu.SemaphoreType.DMA((depth // block + 2,)),
+            pltpu.SemaphoreType.DMA((depth // block + 1,)),
         ],
         compiler_params=params(),
         cost_estimate=pl.CostEstimate(
             flops=2 * SLOTS * count * depth, bytes_accessed=2 * depth * (count + SLOTS), transcendentals=0
         ),
         name="pack_rows",
-    )(batch_index, rank, centers)
+    )(batch_index, centers)
+
+
+def select_body(count, index_ref, select_ref):
+    rows, slots = select_ref.shape
+    chips = slots // (2 * SLOTS)
+    index = index_ref[...]
+    owner = jnp.zeros_like(index)
+    for device in range(1, 2 * chips):
+        owner = owner + jnp.where(index >= device * count, 1, 0)
+    column = column_of(owner, LANE)
+    same = jnp.concatenate([column] * (rows // LANE), axis=1) == owner.astype(F32)
+    earlier = lax.broadcasted_iota(jnp.int32, (rows, rows), 0) < lax.broadcasted_iota(jnp.int32, (rows, rows), 1)
+    rank = jnp.sum(jnp.where(same & earlier, 1.0, 0.0), axis=0, keepdims=True)
+    away = (owner >> 1) ^ lax.axis_index("center")
+    places = [
+        sum(((away >> bit) & 1) << k for k, bit in enumerate(far_first(sub, chips.bit_length() - 1)))
+        for sub in range(2)
+    ]
+    place = jnp.where((owner & 1) == 0, *places)
+    far = jnp.where((owner & 1) == lax.axis_index("sub"), 0, chips * SLOTS)
+    slot = column_of((far + place * SLOTS).astype(F32) + rank, LANE)
+    lanes = lax.broadcasted_iota(jnp.int32, (1, LANE), 1).astype(F32)
+    for k in range(slots // LANE):
+        select_ref[:, k * LANE : (k + 1) * LANE] = jnp.where(slot == lanes + float(LANE * k), 1.0, 0.0).astype(BF16)
+
+
+def select_packed(batch_index, count, chips):
+    rows = batch_index.shape[1]
+    return pl.pallas_call(
+        functools.partial(select_body, count),
+        out_shape=jax.ShapeDtypeStruct((rows, 2 * chips * SLOTS), BF16),
+        compiler_params=params(),
+        name="select_packed",
+    )(batch_index)
 
 
 def spread_body(
@@ -532,18 +586,7 @@
     return one_hot(far + chunk * size + row % size, rows)
 
 
-def select_packed(owner, rank, chips):
-    away = (owner >> 1) ^ lax.axis_index("center")
-    places = [
-        sum(((away >> bit) & 1) << k for k, bit in enumerate(far_first(sub, chips.bit_length() - 1)))
-        for sub in range(2)
-    ]
-    place = jnp.where(owner & 1 == 0, *places)
-    far = jnp.where(owner & 1 == lax.axis_index("sub"), 0, chips * SLOTS)
-    return one_hot(far + place * SLOTS + rank, 2 * chips * SLOTS)
-
-
-def step(packed, chips, owner, rank, centers, weights, targets, batch_index, nys_index, eigvec, eigval):
+def step(packed, chips, centers, weights, targets, batch_index, nys_index, eigvec, eigval):
     rows = batch_index.shape[1]
     classes, count = weights.shape
     depth = eigvec.shape[0]
@@ -552,11 +595,10 @@
     first = (units + 1) // 2 * unit
     second = units * unit - first
     far = [pltpu.with_memory_space_constraint(x, pltpu.HBM) for x in (batch_index, centers)]
-    ready = [center_norms(centers), *spread_weights(nys_index, eigvec, weights, first, second)]
+    ready = [center_norms(centers), *spread_weights(nys_index.reshape(1, -1), eigvec, weights, first, second)]
     if packed:
-        rank_row = rank.reshape(1, rows)
-        ready.append(select_packed(owner, rank, chips))
-        slots = [pack_rows(far[0], rank_row, far[1], part) for part in range(PARTS)]
+        ready.append(select_packed(batch_index, count, chips))
+        slots = [pack_rows(*far, part) for part in range(PARTS)]
         mine, other, norms, high1, low1, high2, low2, spread, select = all_of(slots[0], chips, ready)
         late = all_of(slots[1], chips)
     else:
@@ -573,21 +615,16 @@
 
 
 def on_device(chips, centers, weights, targets, batch_index, nys_index, eigvec, eigval):
-    row = jnp.arange(batch_index.shape[0], dtype=jnp.int32)
-    owner = batch_index // centers.shape[0]
-    earlier = (owner[None, :] == owner[:, None]) & (row[None, :] < row[:, None])
-    rank = jnp.sum(earlier.astype(jnp.int32), axis=1)
+    batch_index = batch_index.reshape(1, -1)
     new, out = lax.cond(
-        jnp.max(rank) < SLOTS,
+        rows_fit(pltpu.with_memory_space_constraint(batch_index, pltpu.HBM), centers.shape[0]) > 0,
         functools.partial(step, True, chips),
         functools.partial(step, False, chips),
-        owner,
-        rank,
         centers,
         weights.T,
         targets.T,
-        batch_index.reshape(1, -1),
-        nys_index.reshape(1, -1),
+        batch_index,
+        nys_index,
         eigvec.T,
         eigval.reshape(1, -1),
     )

time: 87.1 us -> 81.7 us (0.938)
  other arithmetic: 5.56 us -> 0.36 us
  waiting for transfers between devices: 21.4 us -> 24.2 us
  Pallas kernels: 19.9 us -> 18.2 us
    concatenate x5, other arithmetic: 3.7 us -> 0.14 us  [all_of(): keep = jnp.concatenate([keep, swap(keep, chips, far_first, level)])]
    pallas_call x1, Pallas kernels: 4.52 us -> 1.17 us  [center_norms(): pl.pallas_call(norms_body, grid=(count // block,), in_specs=[pl.BlockSpec...]
    ppermute x22, waiting for transfers between devices: 21.4 us -> 24.2 us  [swap(): lax.ppermute(x, AXES, [(i, i ^ flip[i & 1]) for i in range(2 * chips)])]
    pallas_call x0 -> x2, Pallas kernels: none -> 1.6 us  [the longest x1 1.33 us: rows_fit(): pl.pallas_call(functools.partial(fits_body, count), in_specs=[pl.BlockSpe...]
  transfers between devices with their start and end apart: 22 -> 22, of which waited for: 12 -> 13; matrix products, arithmetic and copies ran while one was open for 5% -> 0% of each run, Pallas kernels for 15% -> 12%
where the time goes in v10:
time: 81.7 us; the launch traced here: 81.5 us
  starting transfers between devices  36.6 us (45%)
  waiting for transfers between devices  24.2 us (30%)
  Pallas kernels  18.2 us (22%)
  between operations  1.45 us (2%)
    ppermute x22, starting transfers between devices, swap(): lax.ppermute(x, AXES, [(i, i ^ flip[i & 1]) for i in range(2 * chips)])  36.6 us
    ppermute x22, waiting for transfers between devices, swap(): lax.ppermute(x, AXES, [(i, i ^ flip[i & 1]) for i in range(2 * chips)])  24.2 us
    pallas_call x2, Pallas kernels, pack_rows(): pl.pallas_call(functools.partial(pack_body, part * depth), in_specs=[hbm,...  3.84 us
    pallas_call x1, Pallas kernels, predict(): pl.pallas_call(predict_body, in_specs=[vmem] * 7, out_specs=[vmem] * 4, o...  3.37 us
    pallas_call x1, Pallas kernels, update(): pl.pallas_call(update_body, in_specs=[vmem] * 7, out_specs=[hbm, hbm, vme...  2.46 us
    pallas_call x1, Pallas kernels, update_more(): pl.pallas_call(functools.partial(update_more_body, begin), in_specs=[vmem...  2.02 us
  transfers between devices with their start and end apart: 22, of which 13 were waited for; matrix products, arithmetic and copies ran while one was open for 0% of the time, Pallas kernels for 12%

profile of v10, /device:TPU:1, one launch (start us, length us, event | category | flops | bytes accessed | tf_op | source)
XLA Modules:
  0.0 81.5 jit_solution(5159358443293643488)
XLA Ops:
  0.6 1.3 %rows_fit.1 = s32[1]{0:T(128)} custom-call(s32[1,256]{1,0:T(1,128)} %bitcast.17), custom_call_target="tpu_custom_call" | custom-call | tf_op jit(solution)/shard_map/rows_fit/pallas_call | solution.py:138
  2.6 78.7 %conditional.1 = ((f32[1000,768]{1,0:T(8,128)}, f32[1000,256]{1,0:T(8,128)})) conditional(s32[]{:T(128)} %bitcast.2, (s32[1,256]{1,0:T(1,128)}, bf16[768,3072]{1,0:T(8,128)(2,1)}, s32[320]{0:T(512)}, f32[160,320]{1,0:T(8,128)}, f32[1000,768]{1,0:T(8,128)}, /*index=5*/f32[1000,256]{1,0:T(8,128)}, f32[1,160]{1,0:T(1,128)}) %tuple.30, ...), branch_computations={%region_0.1_spmd, %region_1.2_spmd} | conditional | flops 5426420736 | bytes 105094208 | solution.py:619
  2.8 1.9 %pack_rows.3 = bf16[32,1536]{1,0:T(8,128)(2,1)S(1)} custom-call(s32[1,256]{1,0:T(1,128)} %get-tuple-element.62.index_hbm.index_ref, bf16[768,3072]{1,0:T(8,128)(2,1)} %get-tuple-element.63.centers_hbm.centers_ref), custom_call_target="tpu_custom_call" | custom-call | flops 75497472 | bytes 2457600 | tf_op jit(solution)/shard_map/cond/branch_1_fun/pack_rows/pallas_call | solution.py:180
  4.7 0.0 copy-start.8
  4.8 0.0 copy-start.10
  4.8 0.0 copy-start
  4.8 3.2 %collective-permute-start.29 = (bf16[32,1536]{1,0:T(8,128)(2,1)S(1)}, bf16[32,1536]{1,0:T(8,128)(2,1)S(1)}, u32[]{:S(2)}, u32[]{:S(2)}) collective-permute-start(bf16[32,1536]{1,0:T(8,128)(2,1)S(1)} %pack_rows.3), channel_id=1, source_target_pairs={{0,8},{1,9},{2,10},{3,11},{4,12},{5,13},{6,14},{7,15},{8,0},{9,1},... | collective-permute-start | bytes 294920 | tf_op jit(solution)/shard_map/cond/branch_1_fun/ppermute | solution.py:543
  8.0 1.9 %pack_rows.2 = bf16[32,1536]{1,0:T(8,128)(2,1)S(1)} custom-call(s32[1,256]{1,0:T(1,128)} %get-tuple-element.62.index_hbm.index_ref, bf16[768,3072]{1,0:T(8,128)(2,1)} %get-tuple-element.63.centers_hbm.centers_ref), custom_call_target="tpu_custom_call" | custom-call | flops 75497472 | bytes 2457600 | tf_op jit(solution)/shard_map/cond/branch_1_fun/pack_rows/pallas_call | solution.py:180
  9.9 0.0 copy-start.2
  9.9 0.0 copy-start.6
  9.9 0.2 collective-permute-start.28
  10.2 0.3 select_packed.1.select_ref
  10.5 1.2 %center_norms.3.norm_ref = f32[768,128]{1,0:T(8,128)S(1)} custom-call(bf16[768,3072]{1,0:T(8,128)(2,1)S(1)} %copy-done), custom_call_target="tpu_custom_call" | custom-call | flops 4718592 | bytes 4718592 | tf_op jit(solution)/shard_map/cond/branch_1_fun/center_norms/pallas_call | solution.py:285
  11.6 0.1 copy-done.2
  11.8 1.6 %spread_weights.3 = (bf16[608,768]{1,0:T(8,128)(2,1)S(1)}, bf16[608,768]{1,0:T(8,128)(2,1)S(1)}, bf16[576,768]{1,0:T(8,128)(2,1)S(1)}, bf16[576,768]{1,0:T(8,128)(2,1)S(1)}, f32[160,768]{1,0:T(8,128)S(1)}) custom-call(s32[1,320]{1,0:T(1,128)S(1)} %reshape.99.index_ref, f32[160,320]{1,0:T(8,128)S(1)} %copy-done.6, f32[1000,768]{1,0:T(8,128)S(1)} %copy-done.2), custom_call_target="tpu_custom_call" | custom-call | flops 235929600 | bytes 7274496 | tf_op jit(solution)/shard_map/cond/branch_1_fun/spread_weights/pallas_call | solution.py:258
  13.4 0.0 collective-permute-done.29
  13.4 1.3 %collective-permute-start.30 = (bf16[64,1536]{1,0:T(8,128)(2,1)S(1)}, bf16[64,1536]{1,0:T(8,128)(2,1)S(1)}, u32[]{:S(2)}, u32[]{:S(2)}) collective-permute-start(bf16[64,1536]{1,0:T(8,128)(2,1)S(1)} %pad_maximum_fusion.14), channel_id=1, source_target_pairs={{0,4},{1,3},{2,6},{3,1},{4,0},{5,7},{6,2},{7,5},{8,12},{9,11},{10,... | collective-permute-start | bytes 589832 | tf_op jit(solution)/shard_map/cond/branch_1_fun/ppermute | solution.py:543
  14.7 0.0 collective-permute-done.28
  14.7 1.0 %collective-permute-start.33 = (bf16[64,1536]{1,0:T(8,128)(2,1)S(1)}, bf16[64,1536]{1,0:T(8,128)(2,1)S(1)}, u32[]{:S(2)}, u32[]{:S(2)}) collective-permute-start(bf16[64,1536]{1,0:T(8,128)(2,1)S(1)} %pad_maximum_fusion.13), channel_id=1, source_target_pairs={{0,4},{1,3},{2,6},{3,1},{4,0},{5,7},{6,2},{7,5},{8,12},{9,11},{10,... | collective-permute-start | bytes 589832 | tf_op jit(solution)/shard_map/cond/branch_1_fun/ppermute | solution.py:543
  15.7 4.4 %collective-permute-done.33 = bf16[64,1536]{1,0:T(8,128)(2,1)S(1)} collective-permute-done((bf16[64,1536]{1,0:T(8,128)(2,1)S(1)}, bf16[64,1536]{1,0:T(8,128)(2,1)S(1)}, u32[]{:S(2)}, u32[]{:S(2)}) %collective-permute-start.33) | collective-permute-done | bytes 196640 | tf_op jit(solution)/shard_map/cond/branch_1_fun/ppermute | solution.py:543
  20.1 2.9 %collective-permute-start.34 = (bf16[128,1536]{1,0:T(8,128)(2,1)S(1)}, bf16[128,1536]{1,0:T(8,128)(2,1)S(1)}, u32[]{:S(2)}, u32[]{:S(2)}) collective-permute-start(bf16[128,1536]{1,0:T(8,128)(2,1)S(1)} %pad_maximum_fusion.10), channel_id=1, source_target_pairs={{0,2},{1,5},{2,0},{3,7},{4,6},{5,1},{6,4},{7,3},{8,10},{9,13},{10,... | collective-permute-start | bytes 1179656 | tf_op jit(solution)/shard_map/cond/branch_1_fun/ppermute | solution.py:543
  23.0 0.0 collective-permute-done.30
  23.0 0.1 collective-permute-start.31
  23.1 5.3 %collective-permute-done.34 = bf16[128,1536]{1,0:T(8,128)(2,1)S(1)} collective-permute-done((bf16[128,1536]{1,0:T(8,128)(2,1)S(1)}, bf16[128,1536]{1,0:T(8,128)(2,1)S(1)}, u32[]{:S(2)}, u32[]{:S(2)}) %collective-permute-start.34) | collective-permute-done | bytes 393248 | tf_op jit(solution)/shard_map/cond/branch_1_fun/ppermute | solution.py:543
  28.5 3.4 %collective-permute-start.35 = (bf16[256,1536]{1,0:T(8,128)(2,1)S(1)}, bf16[256,1536]{1,0:T(8,128)(2,1)S(1)}, u32[]{:S(2)}, u32[]{:S(2)}) collective-permute-start(bf16[256,1536]{1,0:T(8,128)(2,1)S(1)} %constant_dynamic-update-slice_fusion.mine_ref), channel_id=1, source_target_pairs={{0,1},{1,0},{2,3},{3,2},{4,5},{5,4},{6,7},{7,6},{8,9},{9,8},{10,11... | collective-permute-start | bytes 2359304 | tf_op jit(solution)/shard_map/cond/branch_1_fun/ppermute | solution.py:543
  31.9 0.7 collective-permute-done.31
  32.7 0.1 pad_maximum_fusion.8.mine_ref
  32.7 3.4 %collective-permute-start.32 = (bf16[256,1536]{1,0:T(8,128)(2,1)S(1)}, bf16[256,1536]{1,0:T(8,128)(2,1)S(1)}, u32[]{:S(2)}, u32[]{:S(2)}) collective-permute-start(bf16[256,1536]{1,0:T(8,128)(2,1)S(1)} %pad_maximum_fusion.8.mine_ref), channel_id=1, source_target_pairs={{0,1},{1,0},{2,3},{3,2},{4,5},{5,4},{6,7},{7,6},{8,9},{9,8},{10,11... | collective-permute-start | bytes 2359304 | tf_op jit(solution)/shard_map/cond/branch_1_fun/ppermute | solution.py:543
  36.2 0.0 collective-permute-done.35.other_ref
  36.2 1.3 %distances.3.before_ref = f32[768,256]{1,0:T(8,128)S(1)} custom-call(bf16[256,1536]{1,0:T(8,128)(2,1)S(1)} %constant_dynamic-update-slice_fusion.mine_ref, bf16[256,1536]{1,0:T(8,128)(2,1)S(1)} %collective-permute-done.35.other_ref, bf16[256,512]{1,0:T(8,128)(2,1)S(1)} %select_packed.1.select_ref, bf16[768,3072]{1,0:T(8,128)(2,1)S(1)} %copy-done, ...), custom_call_target="tpu_custom_call" | custom-call | flops 603979776 | bytes 3145728 | tf_op jit(solution)/shard_map/cond/branch_1_fun/distances/pallas_call | solution.py:350
  37.5 0.6 collective-permute-done.32.other_ref
  38.1 3.4 %predict.3 = (f32[608,128]{1,0:T(8,128)S(1)}, f32[608,128]{1,0:T(8,128)S(1)}, bf16[768,256]{1,0:T(8,128)(2,1)S(1)}, bf16[768,256]{1,0:T(8,128)(2,1)S(1)}) custom-call(bf16[256,1536]{1,0:T(8,128)(2,1)S(1)} %pad_maximum_fusion.8.mine_ref, bf16[256,1536]{1,0:T(8,128)(2,1)S(1)} %collective-permute-done.32.other_ref, ...), custom_call_target="tpu_custom_call" | custom-call | flops 1321205760 | bytes 5636096 | tf_op jit(solution)/shard_map/cond/branch_1_fun/predict/pallas_call | solution.py:373
  41.5 0.4 collective-permute-start.43
  41.9 1.2 %collective-permute-done.43 = f32[608,128]{1,0:T(8,128)S(1)} collective-permute-done((f32[608,128]{1,0:T(8,128)S(1)}, f32[608,128]{1,0:T(8,128)S(1)}, u32[]{:S(2)}, u32[]{:S(2)}) %collective-permute-start.43) | collective-permute-done | bytes 311328 | tf_op jit(solution)/shard_map/cond/branch_1_fun/ppermute | solution.py:543
  43.2 0.4 collective-permute-start.44
  43.6 0.9 %predict_more.3 = (f32[576,128]{1,0:T(8,128)S(1)}, f32[576,128]{1,0:T(8,128)S(1)}) custom-call(bf16[576,768]{1,0:T(8,128)(2,1)S(1)} %get-tuple-element.72.high_ref, bf16[576,768]{1,0:T(8,128)(2,1)S(1)} %get-tuple-element.73.low_ref, bf16[768,256]{1,0:T(8,128)(2,1)S(1)} %get-tuple-element.79.value_high_ref, bf16[768,256]{1,0:T(8,128)(2,1)S(1)} %get-tuple-element.80.value_low_ref), custom_call_target="tpu_custom_call" | custom-call | flops 679477248 | bytes 2359296 | tf_op jit(solution)/shard_map/cond/branch_1_fun/predict_more/pallas_call | solution.py:397
  44.5 0.0 copy-start.4
  44.6 0.0 copy-start.12
  44.6 1.6 %collective-permute-start.36 = (f32[576,128]{1,0:T(8,128)S(1)}, f32[576,128]{1,0:T(8,128)S(1)}, u32[]{:S(2)}, u32[]{:S(2)}) collective-permute-start(f32[576,128]{1,0:T(8,128)S(1)} %get-tuple-element.82), channel_id=1, source_target_pairs={{0,1},{1,0},{2,3},{3,2},{4,5},{5,4},{6,7},{7,6},{8,9},{9,8},{10,11... | collective-permute-start | bytes 884744 | tf_op jit(solution)/shard_map/cond/branch_1_fun/ppermute | solution.py:543
  46.2 1.5 %collective-permute-done.44 = f32[304,128]{1,0:T(8,128)S(1)} collective-permute-done((f32[304,128]{1,0:T(8,128)S(1)}, f32[304,128]{1,0:T(8,128)S(1)}, u32[]{:S(2)}, u32[]{:S(2)}) %collective-permute-start.44) | collective-permute-done | bytes 155680 | tf_op jit(solution)/shard_map/cond/branch_1_fun/ppermute | solution.py:543
  47.7 1.3 %collective-permute-start.45 = (f32[152,128]{1,0:T(8,128)S(1)}, f32[152,128]{1,0:T(8,128)S(1)}, u32[]{:S(2)}, u32[]{:S(2)}) collective-permute-start(f32[152,128]{1,0:T(8,128)S(1)} %slice.98), channel_id=1, source_target_pairs={{0,4},{1,3},{2,6},{3,1},{4,0},{5,7},{6,2},{7,5},{8,12},{9,11},{10,... | collective-permute-start | bytes 233480 | tf_op jit(solution)/shard_map/cond/branch_1_fun/ppermute | solution.py:543
  49.0 0.0 collective-permute-done.36
  49.0 0.5 collective-permute-start.37
  49.5 1.5 %collective-permute-done.45 = f32[152,128]{1,0:T(8,128)S(1)} collective-permute-done((f32[152,128]{1,0:T(8,128)S(1)}, f32[152,128]{1,0:T(8,128)S(1)}, u32[]{:S(2)}, u32[]{:S(2)}) %collective-permute-start.45) | collective-permute-done | bytes 77856 | tf_op jit(solution)/shard_map/cond/branch_1_fun/ppermute | solution.py:543
  51.0 2.1 %collective-permute-start.46 = (f32[152,128]{1,0:T(8,128)S(1)}, f32[152,128]{1,0:T(8,128)S(1)}, u32[]{:S(2)}, u32[]{:S(2)}) collective-permute-start(f32[152,128]{1,0:T(8,128)S(1)} %slice_add_fusion.10), channel_id=1, source_target_pairs={{0,8},{1,9},{2,10},{3,11},{4,12},{5,13},{6,14},{7,15},{8,0},{9,1},... | collective-permute-start | bytes 233480 | tf_op jit(solution)/shard_map/cond/branch_1_fun/ppermute | solution.py:543
  53.1 1.1 %collective-permute-done.37 = f32[288,128]{1,0:T(8,128)S(1)} collective-permute-done((f32[288,128]{1,0:T(8,128)S(1)}, f32[288,128]{1,0:T(8,128)S(1)}, u32[]{:S(2)}, u32[]{:S(2)}) %collective-permute-start.37) | collective-permute-done | bytes 147488 | tf_op jit(solution)/shard_map/cond/branch_1_fun/ppermute | solution.py:543
  54.3 0.2 collective-permute-start.38
  54.4 0.8 collective-permute-done.46
  55.2 1.3 %collective-permute-start.47 = (f32[152,128]{1,0:T(8,128)S(1)}, f32[152,128]{1,0:T(8,128)S(1)}, u32[]{:S(2)}, u32[]{:S(2)}) collective-permute-start(f32[152,128]{1,0:T(8,128)S(1)} %add.135), channel_id=1, source_target_pairs={{0,4},{1,3},{2,6},{3,1},{4,0},{5,7},{6,2},{7,5},{8,12},{9,11},{10,... | collective-permute-start | bytes 233480 | tf_op jit(solution)/shard_map/cond/branch_1_fun/ppermute | solution.py:543
  56.5 1.0 %collective-permute-done.38 = f32[144,128]{1,0:T(8,128)S(1)} collective-permute-done((f32[144,128]{1,0:T(8,128)S(1)}, f32[144,128]{1,0:T(8,128)S(1)}, u32[]{:S(2)}, u32[]{:S(2)}) %collective-permute-start.38) | collective-permute-done | bytes 73760 | tf_op jit(solution)/shard_map/cond/branch_1_fun/ppermute | solution.py:543
  57.5 2.1 %collective-permute-start.39 = (f32[144,128]{1,0:T(8,128)S(1)}, f32[144,128]{1,0:T(8,128)S(1)}, u32[]{:S(2)}, u32[]{:S(2)}) collective-permute-start(f32[144,128]{1,0:T(8,128)S(1)} %slice_add_fusion.11), channel_id=1, source_target_pairs={{0,8},{1,9},{2,10},{3,11},{4,12},{5,13},{6,14},{7,15},{8,0},{9,1},... | collective-permute-start | bytes 221192 | tf_op jit(solution)/shard_map/cond/branch_1_fun/ppermute | solution.py:543
  59.7 2.9 %collective-permute-done.39 = f32[144,128]{1,0:T(8,128)S(1)} collective-permute-done((f32[144,128]{1,0:T(8,128)S(1)}, f32[144,128]{1,0:T(8,128)S(1)}, u32[]{:S(2)}, u32[]{:S(2)}) %collective-permute-start.39) | collective-permute-done | bytes 73760 | tf_op jit(solution)/shard_map/cond/branch_1_fun/ppermute | solution.py:543
  62.5 0.1 collective-permute-start.40
  62.6 1.3 %collective-permute-start.48 = (f32[304,128]{1,0:T(8,128)S(1)}, f32[304,128]{1,0:T(8,128)S(1)}, u32[]{:S(2)}, u32[]{:S(2)}) collective-permute-start(f32[304,128]{1,0:T(8,128)S(1)} %pad_maximum_fusion.15), channel_id=1, source_target_pairs={{0,2},{1,5},{2,0},{3,7},{4,6},{5,1},{6,4},{7,3},{8,10},{9,13},{10,... | collective-permute-start | bytes 466952 | tf_op jit(solution)/shard_map/cond/branch_1_fun/ppermute | solution.py:543
  64.0 2.0 %collective-permute-done.40 = f32[144,128]{1,0:T(8,128)S(1)} collective-permute-done((f32[144,128]{1,0:T(8,128)S(1)}, f32[144,128]{1,0:T(8,128)S(1)}, u32[]{:S(2)}, u32[]{:S(2)}) %collective-permute-start.40) | collective-permute-done | bytes 73760 | tf_op jit(solution)/shard_map/cond/branch_1_fun/ppermute | solution.py:543
  66.0 0.3 collective-permute-start.41
  66.3 1.1 %collective-permute-done.48 = f32[304,128]{1,0:T(8,128)S(1)} collective-permute-done((f32[304,128]{1,0:T(8,128)S(1)}, f32[304,128]{1,0:T(8,128)S(1)}, u32[]{:S(2)}, u32[]{:S(2)}) %collective-permute-start.48) | collective-permute-done | bytes 155680 | tf_op jit(solution)/shard_map/cond/branch_1_fun/ppermute | solution.py:543
  67.4 6.5 %collective-permute-start.49 = (f32[608,128]{1,0:T(8,128)S(1)}, f32[608,128]{1,0:T(8,128)S(1)}, u32[]{:S(2)}, u32[]{:S(2)}) collective-permute-start(f32[608,128]{1,0:T(8,128)S(1)} %pad_maximum_fusion.11.mine_ref), channel_id=1, source_target_pairs={{0,1},{1,0},{2,3},{3,2},{4,5},{5,4},{6,7},{7,6},{8,9},{9,8},{10,11... | collective-permute-start | bytes 933896 | tf_op jit(solution)/shard_map/cond/branch_1_fun/ppermute | solution.py:543
  73.9 0.0 collective-permute-done.41
  74.0 2.9 %collective-permute-start.42 = (f32[576,128]{1,0:T(8,128)S(1)}, f32[576,128]{1,0:T(8,128)S(1)}, u32[]{:S(2)}, u32[]{:S(2)}) collective-permute-start(f32[576,128]{1,0:T(8,128)S(1)} %pad_maximum_fusion.12.mine_ref), channel_id=1, source_target_pairs={{0,1},{1,0},{2,3},{3,2},{4,5},{5,4},{6,7},{7,6},{8,9},{9,8},{10,11... | collective-permute-start | bytes 884744 | tf_op jit(solution)/shard_map/cond/branch_1_fun/ppermute | solution.py:543
  76.9 0.0 collective-permute-done.49.other_ref
  76.9 2.5 %update.3 = (f32[1000,768]{1,0:T(8,128)}, f32[1000,256]{1,0:T(8,128)}, bf16[256,768]{1,0:T(8,128)(2,1)S(1)}, bf16[256,768]{1,0:T(8,128)(2,1)S(1)}) custom-call(f32[608,128]{1,0:T(8,128)S(1)} %pad_maximum_fusion.11.mine_ref, f32[608,128]{1,0:T(8,128)S(1)} %collective-permute-done.49.other_ref, f32[1000,256]{1,0:T(8,128)S(1)} %copy-done.4, ...), custom_call_target="tpu_custom_call" | custom-call | flops 717225984 | bytes 3670016 | tf_op jit(solution)/shard_map/cond/branch_1_fun/update/pallas_call | solution.py:481
  79.3 0.0 collective-permute-done.42.other_ref
  79.3 2.0 %update_more.3 = (f32[1000,768]{1,0:T(8,128)}, f32[1000,256]{1,0:T(8,128)}) custom-call(f32[576,128]{1,0:T(8,128)S(1)} %pad_maximum_fusion.12.mine_ref, f32[576,128]{1,0:T(8,128)S(1)} %collective-permute-done.42.other_ref, f32[1000,256]{1,0:T(8,128)S(1)} %copy-done.4, f32[1000,768]{1,0:T(8,128)S(1)} %copy-done.2, ...), custom_call_target="tpu_custom_call", output_to_operand_aliasing={{0}: (6, {}), {1}: (7, {})} | custom-call | flops 651165696 | bytes 4521984 | tf_op jit(solution)/shard_map/cond/branch_1_fun/update_more/pallas_call | solution.py:519
  (31 shorter events, 0.4 us)
Async XLA Ops:
  4.7 5.4 %copy-start.8 = (s32[1,256]{1,0:T(1,128)S(1)}, s32[1,256]{1,0:T(1,128)}, u32[]{:S(2)}) copy-start(s32[1,256]{1,0:T(1,128)} %get-tuple-element.62.index_hbm.index_ref) | copy-start | bytes 3076 | tf_op jit(solution)/shard_map/cond
  4.8 5.7 %copy-start.10 = (s32[320]{0:T(512)S(1)}, s32[320]{0:T(512)}, u32[]{:S(2)}) copy-start(s32[320]{0:T(512)} %get-tuple-element.64) | copy-start | bytes 3844 | tf_op jit(solution)/shard_map/cond
  4.8 5.7 %copy-start = (bf16[768,3072]{1,0:T(8,128)(2,1)S(1)}, bf16[768,3072]{1,0:T(8,128)(2,1)}, u32[]{:S(2)}) copy-start(bf16[768,3072]{1,0:T(8,128)(2,1)} %get-tuple-element.63.centers_hbm.centers_ref) | copy-start | bytes 14155780 | tf_op jit(solution)/shard_map/cond
  4.8 8.6 %collective-permute-start.29 = (bf16[32,1536]{1,0:T(8,128)(2,1)S(1)}, bf16[32,1536]{1,0:T(8,128)(2,1)S(1)}, u32[]{:S(2)}, u32[]{:S(2)}) collective-permute-start(bf16[32,1536]{1,0:T(8,128)(2,1)S(1)} %pack_rows.3), channel_id=1, source_target_pairs={{0,8},{1,9},{2,10},{3,11},{4,12},{5,13},{6,14},{7,15},{8,0},{9,1},... | collective-permute-start | bytes 294920 | tf_op jit(solution)/shard_map/cond/branch_1_fun/ppermute | solution.py:543
  9.9 1.9 %copy-start.2 = (f32[1000,768]{1,0:T(8,128)S(1)}, f32[1000,768]{1,0:T(8,128)}, u32[]{:S(2)}) copy-start(f32[1000,768]{1,0:T(8,128)} %get-tuple-element.66.weights_ref) | copy-start | bytes 9216004 | tf_op jit(solution)/shard_map/cond
  9.9 1.9 %copy-start.6 = (f32[160,320]{1,0:T(8,128)S(1)}, f32[160,320]{1,0:T(8,128)}, u32[]{:S(2)}) copy-start(f32[160,320]{1,0:T(8,128)} %get-tuple-element.65.eigvec_ref) | copy-start | bytes 614404 | tf_op jit(solution)/shard_map/cond
  9.9 4.8 %collective-permute-start.28 = (bf16[32,1536]{1,0:T(8,128)(2,1)S(1)}, bf16[32,1536]{1,0:T(8,128)(2,1)S(1)}, u32[]{:S(2)}, u32[]{:S(2)}) collective-permute-start(bf16[32,1536]{1,0:T(8,128)(2,1)S(1)} %pack_rows.2), channel_id=1, source_target_pairs={{0,8},{1,9},{2,10},{3,11},{4,12},{5,13},{6,14},{7,15},{8,0},{9,1},... | collective-permute-start | bytes 294920 | tf_op jit(solution)/shard_map/cond/branch_1_fun/ppermute | solution.py:543
  13.4 9.6 %collective-permute-start.30 = (bf16[64,1536]{1,0:T(8,128)(2,1)S(1)}, bf16[64,1536]{1,0:T(8,128)(2,1)S(1)}, u32[]{:S(2)}, u32[]{:S(2)}) collective-permute-start(bf16[64,1536]{1,0:T(8,128)(2,1)S(1)} %pad_maximum_fusion.14), channel_id=1, source_target_pairs={{0,4},{1,3},{2,6},{3,1},{4,0},{5,7},{6,2},{7,5},{8,12},{9,11},{10,... | collective-permute-start | bytes 589832 | tf_op jit(solution)/shard_map/cond/branch_1_fun/ppermute | solution.py:543
  14.7 5.4 %collective-permute-start.33 = (bf16[64,1536]{1,0:T(8,128)(2,1)S(1)}, bf16[64,1536]{1,0:T(8,128)(2,1)S(1)}, u32[]{:S(2)}, u32[]{:S(2)}) collective-permute-start(bf16[64,1536]{1,0:T(8,128)(2,1)S(1)} %pad_maximum_fusion.13), channel_id=1, source_target_pairs={{0,4},{1,3},{2,6},{3,1},{4,0},{5,7},{6,2},{7,5},{8,12},{9,11},{10,... | collective-permute-start | bytes 589832 | tf_op jit(solution)/shard_map/cond/branch_1_fun/ppermute | solution.py:543
  20.1 8.3 %collective-permute-start.34 = (bf16[128,1536]{1,0:T(8,128)(2,1)S(1)}, bf16[128,1536]{1,0:T(8,128)(2,1)S(1)}, u32[]{:S(2)}, u32[]{:S(2)}) collective-permute-start(bf16[128,1536]{1,0:T(8,128)(2,1)S(1)} %pad_maximum_fusion.10), channel_id=1, source_target_pairs={{0,2},{1,5},{2,0},{3,7},{4,6},{5,1},{6,4},{7,3},{8,10},{9,13},{10,... | collective-permute-start | bytes 1179656 | tf_op jit(solution)/shard_map/cond/branch_1_fun/ppermute | solution.py:543
  23.0 9.6 %collective-permute-start.31 = (bf16[128,1536]{1,0:T(8,128)(2,1)S(1)}, bf16[128,1536]{1,0:T(8,128)(2,1)S(1)}, u32[]{:S(2)}, u32[]{:S(2)}) collective-permute-start(bf16[128,1536]{1,0:T(8,128)(2,1)S(1)} %pad_maximum_fusion.9), channel_id=1, source_target_pairs={{0,2},{1,5},{2,0},{3,7},{4,6},{5,1},{6,4},{7,3},{8,10},{9,13},{10,... | collective-permute-start | bytes 1179656 | tf_op jit(solution)/shard_map/cond/branch_1_fun/ppermute | solution.py:543
  28.5 7.7 %collective-permute-start.35 = (bf16[256,1536]{1,0:T(8,128)(2,1)S(1)}, bf16[256,1536]{1,0:T(8,128)(2,1)S(1)}, u32[]{:S(2)}, u32[]{:S(2)}) collective-permute-start(bf16[256,1536]{1,0:T(8,128)(2,1)S(1)} %constant_dynamic-update-slice_fusion.mine_ref), channel_id=1, source_target_pairs={{0,1},{1,0},{2,3},{3,2},{4,5},{5,4},{6,7},{7,6},{8,9},{9,8},{10,11... | collective-permute-start | bytes 2359304 | tf_op jit(solution)/shard_map/cond/branch_1_fun/ppermute | solution.py:543
  32.7 5.4 %collective-permute-start.32 = (bf16[256,1536]{1,0:T(8,128)(2,1)S(1)}, bf16[256,1536]{1,0:T(8,128)(2,1)S(1)}, u32[]{:S(2)}, u32[]{:S(2)}) collective-permute-start(bf16[256,1536]{1,0:T(8,128)(2,1)S(1)} %pad_maximum_fusion.8.mine_ref), channel_id=1, source_target_pairs={{0,1},{1,0},{2,3},{3,2},{4,5},{5,4},{6,7},{7,6},{8,9},{9,8},{10,11... | collective-permute-start | bytes 2359304 | tf_op jit(solution)/shard_map/cond/branch_1_fun/ppermute | solution.py:543
  41.5 1.7 %collective-permute-start.43 = (f32[608,128]{1,0:T(8,128)S(1)}, f32[608,128]{1,0:T(8,128)S(1)}, u32[]{:S(2)}, u32[]{:S(2)}) collective-permute-start(f32[608,128]{1,0:T(8,128)S(1)} %get-tuple-element.85), channel_id=1, source_target_pairs={{0,1},{1,0},{2,3},{3,2},{4,5},{5,4},{6,7},{7,6},{8,9},{9,8},{10,11... | collective-permute-start | bytes 933896 | tf_op jit(solution)/shard_map/cond/branch_1_fun/ppermute | solution.py:543
  43.2 4.4 %collective-permute-start.44 = (f32[304,128]{1,0:T(8,128)S(1)}, f32[304,128]{1,0:T(8,128)S(1)}, u32[]{:S(2)}, u32[]{:S(2)}) collective-permute-start(f32[304,128]{1,0:T(8,128)S(1)} %slice.96), channel_id=1, source_target_pairs={{0,2},{1,5},{2,0},{3,7},{4,6},{5,1},{6,4},{7,3},{8,10},{9,13},{10,... | collective-permute-start | bytes 466952 | tf_op jit(solution)/shard_map/cond/branch_1_fun/ppermute | solution.py:543
  44.5 32.3 %copy-start.4 = (f32[1000,256]{1,0:T(8,128)S(1)}, f32[1000,256]{1,0:T(8,128)}, u32[]{:S(2)}) copy-start(f32[1000,256]{1,0:T(8,128)} %get-tuple-element.83.targets_ref) | copy-start | bytes 3072004 | tf_op jit(solution)/shard_map/cond
  44.6 32.3 %copy-start.12 = (f32[1,160]{1,0:T(1,128)S(1)}, f32[1,160]{1,0:T(1,128)}, u32[]{:S(2)}) copy-start(f32[1,160]{1,0:T(1,128)} %get-tuple-element.86.eigval_ref) | copy-start | bytes 1924 | tf_op jit(solution)/shard_map/cond
  44.6 4.4 %collective-permute-start.36 = (f32[576,128]{1,0:T(8,128)S(1)}, f32[576,128]{1,0:T(8,128)S(1)}, u32[]{:S(2)}, u32[]{:S(2)}) collective-permute-start(f32[576,128]{1,0:T(8,128)S(1)} %get-tuple-element.82), channel_id=1, source_target_pairs={{0,1},{1,0},{2,3},{3,2},{4,5},{5,4},{6,7},{7,6},{8,9},{9,8},{10,11... | collective-permute-start | bytes 884744 | tf_op jit(solution)/shard_map/cond/branch_1_fun/ppermute | solution.py:543
  47.7 3.3 %collective-permute-start.45 = (f32[152,128]{1,0:T(8,128)S(1)}, f32[152,128]{1,0:T(8,128)S(1)}, u32[]{:S(2)}, u32[]{:S(2)}) collective-permute-start(f32[152,128]{1,0:T(8,128)S(1)} %slice.98), channel_id=1, source_target_pairs={{0,4},{1,3},{2,6},{3,1},{4,0},{5,7},{6,2},{7,5},{8,12},{9,11},{10,... | collective-permute-start | bytes 233480 | tf_op jit(solution)/shard_map/cond/branch_1_fun/ppermute | solution.py:543
  49.0 5.2 %collective-permute-start.37 = (f32[288,128]{1,0:T(8,128)S(1)}, f32[288,128]{1,0:T(8,128)S(1)}, u32[]{:S(2)}, u32[]{:S(2)}) collective-permute-start(f32[288,128]{1,0:T(8,128)S(1)} %slice.92), channel_id=1, source_target_pairs={{0,2},{1,5},{2,0},{3,7},{4,6},{5,1},{6,4},{7,3},{8,10},{9,13},{10,... | collective-permute-start | bytes 442376 | tf_op jit(solution)/shard_map/cond/branch_1_fun/ppermute | solution.py:543
  51.0 4.2 %collective-permute-start.46 = (f32[152,128]{1,0:T(8,128)S(1)}, f32[152,128]{1,0:T(8,128)S(1)}, u32[]{:S(2)}, u32[]{:S(2)}) collective-permute-start(f32[152,128]{1,0:T(8,128)S(1)} %slice_add_fusion.10), channel_id=1, source_target_pairs={{0,8},{1,9},{2,10},{3,11},{4,12},{5,13},{6,14},{7,15},{8,0},{9,1},... | collective-permute-start | bytes 233480 | tf_op jit(solution)/shard_map/cond/branch_1_fun/ppermute | solution.py:543
  54.3 3.3 %collective-permute-start.38 = (f32[144,128]{1,0:T(8,128)S(1)}, f32[144,128]{1,0:T(8,128)S(1)}, u32[]{:S(2)}, u32[]{:S(2)}) collective-permute-start(f32[144,128]{1,0:T(8,128)S(1)} %slice.94), channel_id=1, source_target_pairs={{0,4},{1,3},{2,6},{3,1},{4,0},{5,7},{6,2},{7,5},{8,12},{9,11},{10,... | collective-permute-start | bytes 221192 | tf_op jit(solution)/shard_map/cond/branch_1_fun/ppermute | solution.py:543
  55.2 7.4 %collective-permute-start.47 = (f32[152,128]{1,0:T(8,128)S(1)}, f32[152,128]{1,0:T(8,128)S(1)}, u32[]{:S(2)}, u32[]{:S(2)}) collective-permute-start(f32[152,128]{1,0:T(8,128)S(1)} %add.135), channel_id=1, source_target_pairs={{0,4},{1,3},{2,6},{3,1},{4,0},{5,7},{6,2},{7,5},{8,12},{9,11},{10,... | collective-permute-start | bytes 233480 | tf_op jit(solution)/shard_map/cond/branch_1_fun/ppermute | solution.py:543
  57.5 5.0 %collective-permute-start.39 = (f32[144,128]{1,0:T(8,128)S(1)}, f32[144,128]{1,0:T(8,128)S(1)}, u32[]{:S(2)}, u32[]{:S(2)}) collective-permute-start(f32[144,128]{1,0:T(8,128)S(1)} %slice_add_fusion.11), channel_id=1, source_target_pairs={{0,8},{1,9},{2,10},{3,11},{4,12},{5,13},{6,14},{7,15},{8,0},{9,1},... | collective-permute-start | bytes 221192 | tf_op jit(solution)/shard_map/cond/branch_1_fun/ppermute | solution.py:543
  62.5 3.5 %collective-permute-start.40 = (f32[144,128]{1,0:T(8,128)S(1)}, f32[144,128]{1,0:T(8,128)S(1)}, u32[]{:S(2)}, u32[]{:S(2)}) collective-permute-start(f32[144,128]{1,0:T(8,128)S(1)} %add.131), channel_id=1, source_target_pairs={{0,4},{1,3},{2,6},{3,1},{4,0},{5,7},{6,2},{7,5},{8,12},{9,11},{10,... | collective-permute-start | bytes 221192 | tf_op jit(solution)/shard_map/cond/branch_1_fun/ppermute | solution.py:543
  62.6 4.7 %collective-permute-start.48 = (f32[304,128]{1,0:T(8,128)S(1)}, f32[304,128]{1,0:T(8,128)S(1)}, u32[]{:S(2)}, u32[]{:S(2)}) collective-permute-start(f32[304,128]{1,0:T(8,128)S(1)} %pad_maximum_fusion.15), channel_id=1, source_target_pairs={{0,2},{1,5},{2,0},{3,7},{4,6},{5,1},{6,4},{7,3},{8,10},{9,13},{10,... | collective-permute-start | bytes 466952 | tf_op jit(solution)/shard_map/cond/branch_1_fun/ppermute | solution.py:543
  66.0 7.9 %collective-permute-start.41 = (f32[288,128]{1,0:T(8,128)S(1)}, f32[288,128]{1,0:T(8,128)S(1)}, u32[]{:S(2)}, u32[]{:S(2)}) collective-permute-start(f32[288,128]{1,0:T(8,128)S(1)} %pad_maximum_fusion.16), channel_id=1, source_target_pairs={{0,2},{1,5},{2,0},{3,7},{4,6},{5,1},{6,4},{7,3},{8,10},{9,13},{10,... | collective-permute-start | bytes 442376 | tf_op jit(solution)/shard_map/cond/branch_1_fun/ppermute | solution.py:543
  67.4 9.5 %collective-permute-start.49 = (f32[608,128]{1,0:T(8,128)S(1)}, f32[608,128]{1,0:T(8,128)S(1)}, u32[]{:S(2)}, u32[]{:S(2)}) collective-permute-start(f32[608,128]{1,0:T(8,128)S(1)} %pad_maximum_fusion.11.mine_ref), channel_id=1, source_target_pairs={{0,1},{1,0},{2,3},{3,2},{4,5},{5,4},{6,7},{7,6},{8,9},{9,8},{10,11... | collective-permute-start | bytes 933896 | tf_op jit(solution)/shard_map/cond/branch_1_fun/ppermute | solution.py:543
  74.0 5.4 %collective-permute-start.42 = (f32[576,128]{1,0:T(8,128)S(1)}, f32[576,128]{1,0:T(8,128)S(1)}, u32[]{:S(2)}, u32[]{:S(2)}) collective-permute-start(f32[576,128]{1,0:T(8,128)S(1)} %pad_maximum_fusion.12.mine_ref), channel_id=1, source_target_pairs={{0,1},{1,0},{2,3},{3,2},{4,5},{5,4},{6,7},{7,6},{8,9},{9,8},{10,11... | collective-permute-start | bytes 884744 | tf_op jit(solution)/shard_map/cond/branch_1_fun/ppermute | solution.py:543

commit v11 on v10

--- a/solution.py
+++ b/solution.py
@@ -123,30 +123,7 @@
     )(batch_index, centers)
 
 
-def fits_body(count, index_hbm, fits_ref, index_ref, sem):
-    copy = pltpu.make_async_copy(index_hbm, index_ref, sem)
-    copy.start()
-    copy.wait()
-    devices = 2 * lax.axis_size("center")
-    starts = lax.broadcasted_iota(jnp.int32, (devices, 1), 0) * count
-    local = index_ref[...] - starts
-    held = jnp.sum(jnp.where((local >= 0) & (local < count), 1.0, 0.0), axis=1, keepdims=True)
-    fits_ref[0] = (jnp.max(held) <= SLOTS).astype(jnp.int32)
-
-
-def rows_fit(batch_index, count):
-    return pl.pallas_call(
-        functools.partial(fits_body, count),
-        in_specs=[pl.BlockSpec(memory_space=pltpu.HBM)],
-        out_specs=pl.BlockSpec(memory_space=pltpu.SMEM),
-        out_shape=jax.ShapeDtypeStruct((1,), jnp.int32),
-        scratch_shapes=[pltpu.VMEM(batch_index.shape, jnp.int32), pltpu.SemaphoreType.DMA],
-        compiler_params=params(),
-        name="rows_fit",
-    )(batch_index)[0]
-
-
-def pack_body(first, index_hbm, centers_hbm, out_ref, index_ref, centers_ref, sems):
+def pack_body(first, index_hbm, centers_hbm, out_ref, fits_ref, index_ref, centers_ref, sems):
     blocks, count, block = centers_ref.shape
     rows = index_ref.shape[1]
     copies = [pltpu.make_async_copy(index_hbm, index_ref, sems.at[blocks])] + [
@@ -158,6 +135,10 @@
     for copy in copies:
         copy.start()
     copies[0].wait()
+    starts = lax.broadcasted_iota(jnp.int32, (2 * lax.axis_size("center"), 1), 0) * count
+    every = index_ref[...] - starts
+    held = jnp.sum(jnp.where((every >= 0) & (every < count), 1.0, 0.0), axis=1, keepdims=True)
+    fits_ref[0] = (jnp.max(held) <= SLOTS).astype(jnp.int32)
     start = (lax.axis_index("center") * 2 + lax.axis_index("sub")) * count
     local = index_ref[...] - start
     here = jnp.where((local >= 0) & (local < count), 1.0, 0.0)
@@ -180,8 +161,8 @@
     return pl.pallas_call(
         functools.partial(pack_body, part * depth),
         in_specs=[hbm, hbm],
-        out_specs=pl.BlockSpec(memory_space=pltpu.VMEM),
-        out_shape=jax.ShapeDtypeStruct((SLOTS, depth), BF16),
+        out_specs=[pl.BlockSpec(memory_space=pltpu.VMEM), pl.BlockSpec(memory_space=pltpu.SMEM)],
+        out_shape=[jax.ShapeDtypeStruct((SLOTS, depth), BF16), jax.ShapeDtypeStruct((1,), jnp.int32)],
         scratch_shapes=[
             pltpu.VMEM((1, rows), jnp.int32),
             pltpu.VMEM((depth // block, count, block), BF16),
@@ -294,9 +275,11 @@
     )(centers)
 
 
-def gather_batch(mine_ref, other_ref, select_ref, batch_ref):
-    half = mine_ref.shape[0]
-    found = dot(select_ref[:, :half], mine_ref[...], NN) + dot(select_ref[:, half:], other_ref[...], NN)
+def gather_batch(piece_refs, select_ref, batch_ref):
+    found = 0.0
+    for k, ref in enumerate(piece_refs):
+        size = ref.shape[0]
+        found = found + dot(select_ref[:, k * size : (k + 1) * size], ref[...], NN)
     batch_ref[...] = found.astype(BF16)
 
 
@@ -324,17 +307,17 @@
         send_ref[at] = jnp.where(lower, second, first)
 
 
-def distance_body(mine_ref, other_ref, select_ref, centers_ref, norm_ref, total_ref, batch_ref):
-    gather_batch(mine_ref, other_ref, select_ref, batch_ref)
+def distance_body(*refs):
+    *piece_refs, select_ref, centers_ref, norm_ref, total_ref, batch_ref = refs
+    gather_batch(piece_refs, select_ref, batch_ref)
     total_ref[...] = norm_ref[:, 0:1] + nearer(0, centers_ref, batch_ref)
 
 
-def predict_body(
-    mine_ref, other_ref, select_ref, centers_ref, before_ref, high_ref, low_ref,
-    keep_ref, send_ref, value_high_ref, value_low_ref, batch_ref, total_ref,
-):
+def predict_body(*refs):
+    *piece_refs, select_ref, centers_ref, before_ref, high_ref, low_ref = refs[:-6]
+    keep_ref, send_ref, value_high_ref, value_low_ref, batch_ref, total_ref = refs[-6:]
     depth = centers_ref.shape[1]
-    gather_batch(mine_ref, other_ref, select_ref, batch_ref)
+    gather_batch(piece_refs, select_ref, batch_ref)
     square = jnp.maximum(before_ref[...] + nearer(depth - batch_ref.shape[1], centers_ref, batch_ref), 0.0)
     value_high, value_low = two(jnp.exp(jnp.sqrt(square) * (-1.0 / math.sqrt(depth))))
     value_high_ref[...] = value_high
@@ -342,14 +325,14 @@
     product(high_ref, low_ref, value_high, value_low, total_ref, keep_ref, send_ref)
 
 
-def distances(mine, other, select, centers, norms):
-    depth = mine.shape[1]
+def distances(pieces, select, centers, norms):
+    depth = pieces[0].shape[1]
     rows = select.shape[0]
     count = centers.shape[0]
     vmem = pl.BlockSpec(memory_space=pltpu.VMEM)
     return pl.pallas_call(
         distance_body,
-        in_specs=[vmem] * 5,
+        in_specs=[vmem] * (len(pieces) + 3),
         out_specs=vmem,
         out_shape=jax.ShapeDtypeStruct((count, rows), F32),
         scratch_shapes=[pltpu.VMEM((rows, depth), BF16)],
@@ -358,11 +341,11 @@
             flops=2 * rows * count * depth, bytes_accessed=2 * depth * (count + rows), transcendentals=0
         ),
         name="distances",
-    )(mine, other, select, centers, norms)
-
-
-def predict(mine, other, select, centers, before, high, low):
-    depth = mine.shape[1]
+    )(*pieces, select, centers, norms)
+
+
+def predict(pieces, select, centers, before, high, low):
+    depth = pieces[0].shape[1]
     rows = select.shape[0]
     half = rows // 2
     count = centers.shape[0]
@@ -372,7 +355,7 @@
     vmem = pl.BlockSpec(memory_space=pltpu.VMEM)
     return pl.pallas_call(
         predict_body,
-        in_specs=[vmem] * 7,
+        in_specs=[vmem] * (len(pieces) + 5),
         out_specs=[vmem] * 4,
         out_shape=[out, out, value, value],
         scratch_shapes=[pltpu.VMEM((rows, depth), BF16), pltpu.VMEM((padded, rows), F32)],
@@ -383,7 +366,7 @@
             transcendentals=2 * rows * count,
         ),
         name="predict",
-    )(mine, other, select, centers, before, high, low)
+    )(*pieces, select, centers, before, high, low)
 
 
 def more_body(high_ref, low_ref, value_high_ref, value_low_ref, keep_ref, send_ref, total_ref):
@@ -406,18 +389,17 @@
     )(high, low, value_high, value_low)
 
 
-def gather_total(mine_ref, other_ref, total_ref):
+def gather_total(piece_refs, total_ref):
     lower = lax.axis_index("sub") == 0
-    half = mine_ref.shape[1]
-    size = mine_ref.shape[0] // CHUNKS
+    rows, half = piece_refs[0].shape
+    size = 2 * rows // CHUNKS
     for part, turn in enumerate(turns()):
         for chunk in range(CHUNKS):
-            at = slice(chunk * size, (chunk + 1) * size)
+            second, at = divmod(chunk * size, rows)
+            mine, other = [ref[at : at + size] for ref in (piece_refs[second], piece_refs[2 + second])]
             same = lower if part == 0 else jnp.logical_not(lower)
             to = pl.multiple_of((chunk ^ turn) * size, 8)
-            total_ref[pl.ds(to, size), part * half : (part + 1) * half] = jnp.where(
-                same, mine_ref[at], other_ref[at]
-            )
+            total_ref[pl.ds(to, size), part * half : (part + 1) * half] = jnp.where(same, mine, other)
 
 
 def write_rows(begin, skip, total_ref, targets_ref, weights_ref, high_ref, low_ref, new_hbm, out_hbm, new_ref, sems):
@@ -451,12 +433,12 @@
 
 
 def update_body(
-    mine_ref, other_ref, targets_ref, index_ref, eigval_ref, spread_ref, weights_ref,
+    keep_ref, got_ref, near_ref, far_ref, targets_ref, index_ref, eigval_ref, spread_ref, weights_ref,
     new_hbm, out_hbm, high_ref, low_ref, total_ref, new_ref, sems,
 ):
     start = (lax.axis_index("center") * 2 + lax.axis_index("sub")) * spread_ref.shape[1]
     rank, count = spread_ref.shape
-    gather_total(mine_ref, other_ref, total_ref)
+    gather_total((keep_ref, got_ref, near_ref, far_ref), total_ref)
     value = eigval_ref[...]
     lowest = jnp.min(value, axis=1, keepdims=True)
     scaled = (1.0 - lowest / value) / value
@@ -469,10 +451,9 @@
     write_rows(0, rank, total_ref, targets_ref, weights_ref, high_ref, low_ref, new_hbm, out_hbm, new_ref, sems)
 
 
-def update(mine, other, targets, batch_index, eigval, spread, weights):
+def update(pieces, targets, batch_index, eigval, spread, weights):
     classes, count = weights.shape
-    padded, half = mine.shape
-    rows = 2 * half
+    padded, rows = 2 * pieces[0].shape[0], 2 * pieces[0].shape[1]
     rank = spread.shape[0]
     here = padded - rank
     vmem = pl.BlockSpec(memory_space=pltpu.VMEM)
@@ -480,7 +461,7 @@
     right = jax.ShapeDtypeStruct((rows, count), BF16)
     return pl.pallas_call(
         update_body,
-        in_specs=[vmem] * 7,
+        in_specs=[vmem] * 9,
         out_specs=[hbm, hbm, vmem, vmem],
         out_shape=[
             jax.ShapeDtypeStruct((classes, count), F32),
@@ -498,33 +479,32 @@
             flops=6 * rows * count * (here + rank), bytes_accessed=8 * here * (count + rows), transcendentals=0
         ),
         name="update",
-    )(mine, other, targets, batch_index, eigval, spread, weights)
+    )(*pieces, targets, batch_index, eigval, spread, weights)
 
 
 def update_more_body(
-    begin, mine_ref, other_ref, targets_ref, weights_ref, high_ref, low_ref, new_in, out_in,
+    begin, keep_ref, got_ref, near_ref, far_ref, targets_ref, weights_ref, high_ref, low_ref, new_in, out_in,
     new_hbm, out_hbm, total_ref, new_ref, sems,
 ):
-    gather_total(mine_ref, other_ref, total_ref)
+    gather_total((keep_ref, got_ref, near_ref, far_ref), total_ref)
     write_rows(begin, 0, total_ref, targets_ref, weights_ref, high_ref, low_ref, new_hbm, out_hbm, new_ref, sems)
 
 
-def update_more(mine, other, targets, weights, high, low, new, out, begin):
+def update_more(pieces, targets, weights, high, low, new, out, begin):
     classes, count = weights.shape
-    padded, half = mine.shape
-    rows = 2 * half
+    padded, rows = 2 * pieces[0].shape[0], 2 * pieces[0].shape[1]
     here = classes - begin
     vmem = pl.BlockSpec(memory_space=pltpu.VMEM)
     hbm = pl.BlockSpec(memory_space=pl.ANY)
     return pl.pallas_call(
         functools.partial(update_more_body, begin),
-        in_specs=[vmem] * 6 + [hbm] * 2,
+        in_specs=[vmem] * 8 + [hbm] * 2,
         out_specs=[hbm, hbm],
         out_shape=[
             jax.ShapeDtypeStruct((classes, count), F32),
             jax.ShapeDtypeStruct((classes, rows), F32),
         ],
-        input_output_aliases={6: 0, 7: 1},
+        input_output_aliases={8: 0, 9: 1},
         scratch_shapes=[
             pltpu.VMEM((padded, rows), F32),
             pltpu.VMEM((here, count), F32),
@@ -535,7 +515,7 @@
             flops=6 * rows * count * here, bytes_accessed=8 * here * (count + rows), transcendentals=0
         ),
         name="update_more",
-    )(mine, other, targets, weights, high, low, new, out)
+    )(*pieces, targets, weights, high, low, new, out)
 
 
 def swap(x, chips, order=None, level=0):
@@ -543,33 +523,56 @@
     return lax.ppermute(x, AXES, [(i, i ^ flip[i & 1]) for i in range(2 * chips)])
 
 
-def tie(x, tied):
-    x, *tied = lax.optimization_barrier((x, *tied))
-    return x, tied
-
-
-def total_of(keep, send, chips, tied=()):
-    keep = keep + swap(send, chips)
+def tie(x, *others):
+    return lax.optimization_barrier((x, *others))
+
+
+def settle(keeps, gots, combine):
+    first = combine(keeps[0], gots[0])
+    got, _ = tie(gots[1], first)
+    return [first, combine(keeps[1], got)]
+
+
+def stack(keep, got):
+    return jnp.concatenate([keep, got])
+
+
+def add(keep, got):
+    return keep + got
+
+
+def pieces_of(keeps, gots, chips):
+    return [(keep, got, swap(keep, chips), swap(got, chips)) for keep, got in zip(keeps, gots)]
+
+
+def totals(parts, chips):
+    keeps = [keep for keep, _ in parts]
+    gots = [swap(send, chips) for _, send in parts]
+    gots[0], keeps[1] = tie(gots[0], keeps[1])
+    keeps = settle(keeps, gots, add)
     for level in range(chips.bit_length() - 1):
-        if level >= HALVINGS:
-            keep = keep + swap(keep, chips, walk, level)
-            continue
-        half = keep.shape[0] // 2
-        keep, send = keep[:half], keep[half:]
-        if level == 1 and tied:
-            send, tied = tie(send, tied)
-        keep = keep + swap(send, chips, walk, level)
+        sends = keeps
+        if level < HALVINGS:
+            half = [keep.shape[0] // 2 for keep in keeps]
+            sends = [keep[at:] for keep, at in zip(keeps, half)]
+            keeps = [keep[:at] for keep, at in zip(keeps, half)]
+        keeps = settle(keeps, [swap(send, chips, walk, level) for send in sends], add)
     for level in reversed(range(HALVINGS)):
-        keep = jnp.concatenate([keep, swap(keep, chips, walk, level)])
-    return [keep, swap(keep, chips), *tied]
-
-
-def all_of(keep, chips, tied=()):
-    for level in range(chips.bit_length() - 1):
-        if level == 1 and tied:
-            keep, tied = tie(keep, tied)
-        keep = jnp.concatenate([keep, swap(keep, chips, far_first, level)])
-    return [keep, swap(keep, chips), *tied]
+        gots = [swap(keep, chips, walk, level) for keep in keeps]
+        if level:
+            keeps = settle(keeps, gots, stack)
+    return pieces_of(keeps, gots, chips)
+
+
+def gathered(keeps, chips, tied):
+    bits = chips.bit_length() - 1
+    for level in range(bits):
+        if level == 1:
+            keeps[0], *tied = tie(keeps[0], *tied)
+        gots = [swap(keep, chips, far_first, level) for keep in keeps]
+        if level < bits - 1:
+            keeps = settle(keeps, gots, stack)
+    return pieces_of(keeps, gots, chips), tied
 
 
 def one_hot(slot, slots):
@@ -586,7 +589,7 @@
     return one_hot(far + chunk * size + row % size, rows)
 
 
-def step(packed, chips, centers, weights, targets, batch_index, nys_index, eigvec, eigval):
+def step(packed, chips, slots, centers, weights, targets, batch_index, nys_index, eigvec, eigval):
     rows = batch_index.shape[1]
     classes, count = weights.shape
     depth = eigvec.shape[0]
@@ -598,28 +601,27 @@
     ready = [center_norms(centers), *spread_weights(nys_index.reshape(1, -1), eigvec, weights, first, second)]
     if packed:
         ready.append(select_packed(batch_index, count, chips))
-        slots = [pack_rows(*far, part) for part in range(PARTS)]
-        mine, other, norms, high1, low1, high2, low2, spread, select = all_of(slots[0], chips, ready)
-        late = all_of(slots[1], chips)
+        halves, ready = gathered([slots, pack_rows(*far, 1)[0]], chips, ready)
     else:
         ready.append(select_summed(rows))
-        picked = [pick_batch(*far, part) for part in range(PARTS)]
-        mine, other, norms, high1, low1, high2, low2, spread, select = total_of(*picked[0], chips, ready)
-        late = total_of(*picked[1], chips)
-    before = distances(mine, other, select, centers, norms)
-    keep, send, value_high, value_low = predict(*late, select, centers, before, high1, low1)
-    one = total_of(keep, send, chips)
-    another = total_of(*predict_more(high2, low2, value_high, value_low), chips)
-    new, out, high, low = update(*one, targets, batch_index, eigval, spread, weights)
-    return update_more(*another, targets, weights, high, low, new, out, first - depth)
+        halves = totals([pick_batch(*far, part) for part in range(PARTS)], chips)
+    norms, high1, low1, high2, low2, spread, select = ready
+    before = distances(halves[0], select, centers, norms)
+    keep, send, value_high, value_low = predict(halves[1], select, centers, before, high1, low1)
+    one, another = totals([(keep, send), predict_more(high2, low2, value_high, value_low)], chips)
+    new, out, high, low = update(one, targets, batch_index, eigval, spread, weights)
+    return update_more(another, targets, weights, high, low, new, out, first - depth)
 
 
 def on_device(chips, centers, weights, targets, batch_index, nys_index, eigvec, eigval):
     batch_index = batch_index.reshape(1, -1)
+    far = [pltpu.with_memory_space_constraint(x, pltpu.HBM) for x in (batch_index, centers)]
+    slots, fits = pack_rows(*far, 0)
     new, out = lax.cond(
-        rows_fit(pltpu.with_memory_space_constraint(batch_index, pltpu.HBM), centers.shape[0]) > 0,
+        fits[0] > 0,
         functools.partial(step, True, chips),
         functools.partial(step, False, chips),
+        slots,
         centers,
         weights.T,
         targets.T,

time: 81.7 us -> 83.8 us (1.026)
  starting transfers between devices: 36.6 us -> 38 us
    ppermute x22 -> x26, starting transfers between devices: 36.6 us -> 38 us  [swap(): lax.ppermute(x, AXES, [(i, i ^ flip[i & 1]) for i in range(2 * chips)])]
    ppermute x22 -> x26, waiting for transfers between devices: 24.2 us -> 24.9 us  [swap(): lax.ppermute(x, AXES, [(i, i ^ flip[i & 1]) for i in range(2 * chips)])]
    pallas_call x4 -> x3, Pallas kernels: 8.42 us -> 7.86 us  [the longest x1 3.75 us: predict(): pl.pallas_call(predict_body, in_specs=[vmem] * (len(pieces) + 5), out_spe...]
  transfers between devices with their start and end apart: 22 -> 26, of which waited for: 13 -> 13; matrix products, arithmetic and copies ran while one was open for 0% -> 0% of each run, Pallas kernels for 12% -> 10%
where the time goes in v11:
time: 83.8 us; the launch traced here: 83.6 us
  starting transfers between devices  38 us (45%)
  waiting for transfers between devices  24.9 us (30%)
  Pallas kernels  18.5 us (22%)
  between operations  1.51 us (2%)
    ppermute x26, starting transfers between devices, swap(): lax.ppermute(x, AXES, [(i, i ^ flip[i & 1]) for i in range(2 * chips)])  38 us
    ppermute x26, waiting for transfers between devices, swap(): lax.ppermute(x, AXES, [(i, i ^ flip[i & 1]) for i in range(2 * chips)])  24.9 us
    pallas_call x2, Pallas kernels, pack_rows(): pl.pallas_call(functools.partial(pack_body, part * depth), in_specs=[hbm,...  4.66 us
    pallas_call x1, Pallas kernels, predict(): pl.pallas_call(predict_body, in_specs=[vmem] * (len(pieces) + 5), out_spe...  3.75 us
    pallas_call x1, Pallas kernels, update(): pl.pallas_call(update_body, in_specs=[vmem] * 9, out_specs=[hbm, hbm, vme...  2.46 us
    pallas_call x1, Pallas kernels, update_more(): pl.pallas_call(functools.partial(update_more_body, begin), in_specs=[vmem...  2.03 us
  transfers between devices with their start and end apart: 26, of which 13 were waited for; matrix products, arithmetic and copies ran while one was open for 0% of the time, Pallas kernels for 10%

profile of v11, /device:TPU:1, one launch (start us, length us, event | category | flops | bytes accessed | tf_op | source)
XLA Modules:
  0.0 83.6 jit_solution(9208240348845363808)
XLA Ops:
  0.7 2.3 %pack_rows.3 = (bf16[32,1536]{1,0:T(8,128)(2,1)S(1)}, s32[1]{0:T(128)}) custom-call(s32[1,256]{1,0:T(1,128)} %bitcast.17, bf16[768,3072]{1,0:T(8,128)(2,1)} %centers_hbm.1), custom_call_target="tpu_custom_call" | custom-call | flops 75497472 | bytes 2457600 | tf_op jit(solution)/shard_map/pack_rows/pallas_call | solution.py:161
  3.7 79.8 %conditional.1 = ((f32[1000,768]{1,0:T(8,128)}, f32[1000,256]{1,0:T(8,128)})) conditional(s32[]{:T(128)} %bitcast.2, (s32[1,256]{1,0:T(1,128)}, bf16[768,3072]{1,0:T(8,128)(2,1)}, s32[320]{0:T(512)S(1)}, f32[160,320]{1,0:T(8,128)S(1)}, f32[1000,768]{1,0:T(8,128)}, /*index=5*/f32[1000,256]{1,0:T(8,128)S(1)}, f32[1,160]{1,0:T(1,128)S(1)}) %tuple.52, ...), branch_computations={%region_0.1_spmd, %region_1.2_spmd} | conditional | flops 5423758336 | bytes 96931888 | solution.py:620
  3.9 0.0 copy-start.6
  3.9 0.0 copy-start
  3.9 2.4 %pack_rows.2 = (bf16[32,1536]{1,0:T(8,128)(2,1)S(1)}, s32[1]{0:T(128)}) custom-call(s32[1,256]{1,0:T(1,128)} %get-tuple-element.70.index_hbm.index_ref, bf16[768,3072]{1,0:T(8,128)(2,1)} %get-tuple-element.71.centers_hbm.centers_ref.refs_5_), custom_call_target="tpu_custom_call" | custom-call | flops 75497472 | bytes 2457600 | tf_op jit(solution)/shard_map/cond/branch_1_fun/pack_rows/pallas_call | solution.py:161
  6.3 0.0 copy-start.2
  6.3 3.2 %collective-permute-start.32 = (bf16[32,1536]{1,0:T(8,128)(2,1)S(1)}, bf16[32,1536]{1,0:T(8,128)(2,1)S(1)}, u32[]{:S(2)}, u32[]{:S(2)}) collective-permute-start(bf16[32,1536]{1,0:T(8,128)(2,1)S(1)} %get-tuple-element.72), channel_id=1, source_target_pairs={{0,8},{1,9},{2,10},{3,11},{4,12},{5,13},{6,14},{7,15},{8,0},{9,1},... | collective-permute-start | bytes 294920 | tf_op jit(solution)/shard_map/cond/branch_1_fun/ppermute | solution.py:523
  9.5 0.1 collective-permute-start.33
  9.6 0.3 select_packed.1.refs_4_
  9.9 1.2 %center_norms.3.refs_6_ = f32[768,128]{1,0:T(8,128)S(1)} custom-call(bf16[768,3072]{1,0:T(8,128)(2,1)S(1)} %copy-done), custom_call_target="tpu_custom_call" | custom-call | flops 4718592 | bytes 4718592 | tf_op jit(solution)/shard_map/cond/branch_1_fun/center_norms/pallas_call | solution.py:266
  11.1 1.6 %spread_weights.3 = (bf16[608,768]{1,0:T(8,128)(2,1)S(1)}, bf16[608,768]{1,0:T(8,128)(2,1)S(1)}, bf16[576,768]{1,0:T(8,128)(2,1)S(1)}, bf16[576,768]{1,0:T(8,128)(2,1)S(1)}, f32[160,768]{1,0:T(8,128)S(1)}) custom-call(s32[1,320]{1,0:T(1,128)S(1)} %reshape.99.index_ref, f32[160,320]{1,0:T(8,128)S(1)} %get-tuple-element.76.eigvec_ref, f32[1000,768]{1,0:T(8,128)S(1)} %copy-done.2), custom_call_target="tpu_custom_call" | custom-call | flops 235929600 | bytes 7274496 | tf_op jit(solution)/shard_map/cond/branch_1_fun/spread_weights/pallas_call | solution.py:239
  12.7 5.7 %collective-permute-done.33 = bf16[32,1536]{1,0:T(8,128)(2,1)S(1)} collective-permute-done((bf16[32,1536]{1,0:T(8,128)(2,1)S(1)}, bf16[32,1536]{1,0:T(8,128)(2,1)S(1)}, u32[]{:S(2)}, u32[]{:S(2)}) %collective-permute-start.33) | collective-permute-done | bytes 98336 | tf_op jit(solution)/shard_map/cond/branch_1_fun/ppermute | solution.py:523
  18.3 1.2 %collective-permute-start.35 = (bf16[64,1536]{1,0:T(8,128)(2,1)S(1)}, bf16[64,1536]{1,0:T(8,128)(2,1)S(1)}, u32[]{:S(2)}, u32[]{:S(2)}) collective-permute-start(bf16[64,1536]{1,0:T(8,128)(2,1)S(1)} %constant_dynamic-update-slice_fusion), channel_id=1, source_target_pairs={{0,4},{1,3},{2,6},{3,1},{4,0},{5,7},{6,2},{7,5},{8,12},{9,11},{10,... | collective-permute-start | bytes 589832 | tf_op jit(solution)/shard_map/cond/branch_1_fun/ppermute | solution.py:523
  19.5 0.0 collective-permute-done.32
  19.6 0.4 collective-permute-start.34
  20.0 3.2 %collective-permute-done.35 = bf16[64,1536]{1,0:T(8,128)(2,1)S(1)} collective-permute-done((bf16[64,1536]{1,0:T(8,128)(2,1)S(1)}, bf16[64,1536]{1,0:T(8,128)(2,1)S(1)}, u32[]{:S(2)}, u32[]{:S(2)}) %collective-permute-start.35) | collective-permute-done | bytes 196640 | tf_op jit(solution)/shard_map/cond/branch_1_fun/ppermute | solution.py:523
  23.2 1.2 %collective-permute-start.39 = (bf16[128,1536]{1,0:T(8,128)(2,1)S(1)}, bf16[128,1536]{1,0:T(8,128)(2,1)S(1)}, u32[]{:S(2)}, u32[]{:S(2)}) collective-permute-start(bf16[128,1536]{1,0:T(8,128)(2,1)S(1)} %constant_dynamic-update-slice_fusion.2.refs_0_), channel_id=1, source_target_pairs={{0,2},{1,5},{2,0},{3,7},{4,6},{5,1},{6,4},{7,3},{8,10},{9,13},{10,... | collective-permute-start | bytes 1179656 | tf_op jit(solution)/shard_map/cond/branch_1_fun/ppermute | solution.py:523
  24.4 0.9 %collective-permute-done.34 = bf16[64,1536]{1,0:T(8,128)(2,1)S(1)} collective-permute-done((bf16[64,1536]{1,0:T(8,128)(2,1)S(1)}, bf16[64,1536]{1,0:T(8,128)(2,1)S(1)}, u32[]{:S(2)}, u32[]{:S(2)}) %collective-permute-start.34) | collective-permute-done | bytes 196640 | tf_op jit(solution)/shard_map/cond/branch_1_fun/ppermute | solution.py:523
  25.3 1.2 %collective-permute-start.36 = (bf16[128,1536]{1,0:T(8,128)(2,1)S(1)}, bf16[128,1536]{1,0:T(8,128)(2,1)S(1)}, u32[]{:S(2)}, u32[]{:S(2)}) collective-permute-start(bf16[128,1536]{1,0:T(8,128)(2,1)S(1)} %constant_dynamic-update-slice_fusion.4.refs_0_), channel_id=1, source_target_pairs={{0,2},{1,5},{2,0},{3,7},{4,6},{5,1},{6,4},{7,3},{8,10},{9,13},{10,... | collective-permute-start | bytes 1179656 | tf_op jit(solution)/shard_map/cond/branch_1_fun/ppermute | solution.py:523
  26.5 3.6 %collective-permute-start.40 = (bf16[128,1536]{1,0:T(8,128)(2,1)S(1)}, bf16[128,1536]{1,0:T(8,128)(2,1)S(1)}, u32[]{:S(2)}, u32[]{:S(2)}) collective-permute-start(bf16[128,1536]{1,0:T(8,128)(2,1)S(1)} %constant_dynamic-update-slice_fusion.2.refs_0_), channel_id=1, source_target_pairs={{0,1},{1,0},{2,3},{3,2},{4,5},{5,4},{6,7},{7,6},{8,9},{9,8},{10,11... | collective-permute-start | bytes 1179656 | tf_op jit(solution)/shard_map/cond/branch_1_fun/ppermute | solution.py:523
  30.1 1.1 %collective-permute-done.39.refs_1_ = bf16[128,1536]{1,0:T(8,128)(2,1)S(1)} collective-permute-done((bf16[128,1536]{1,0:T(8,128)(2,1)S(1)}, bf16[128,1536]{1,0:T(8,128)(2,1)S(1)}, u32[]{:S(2)}, u32[]{:S(2)}) %collective-permute-start.39) | collective-permute-done | bytes 393248 | tf_op jit(solution)/shard_map/cond/branch_1_fun/ppermute | solution.py:523
  31.2 1.9 %collective-permute-start.41 = (bf16[128,1536]{1,0:T(8,128)(2,1)S(1)}, bf16[128,1536]{1,0:T(8,128)(2,1)S(1)}, u32[]{:S(2)}, u32[]{:S(2)}) collective-permute-start(bf16[128,1536]{1,0:T(8,128)(2,1)S(1)} %collective-permute-done.39.refs_1_), channel_id=1, source_target_pairs={{0,1},{1,0},{2,3},{3,2},{4,5},{5,4},{6,7},{7,6},{8,9},{9,8},{10,11... | collective-permute-start | bytes 1179656 | tf_op jit(solution)/shard_map/cond/branch_1_fun/ppermute | solution.py:523
  33.2 0.0 collective-permute-start.37
  33.2 2.3 %collective-permute-done.36.refs_1_ = bf16[128,1536]{1,0:T(8,128)(2,1)S(1)} collective-permute-done((bf16[128,1536]{1,0:T(8,128)(2,1)S(1)}, bf16[128,1536]{1,0:T(8,128)(2,1)S(1)}, u32[]{:S(2)}, u32[]{:S(2)}) %collective-permute-start.36) | collective-permute-done | bytes 393248 | tf_op jit(solution)/shard_map/cond/branch_1_fun/ppermute | solution.py:523
  35.4 1.9 %collective-permute-start.38 = (bf16[128,1536]{1,0:T(8,128)(2,1)S(1)}, bf16[128,1536]{1,0:T(8,128)(2,1)S(1)}, u32[]{:S(2)}, u32[]{:S(2)}) collective-permute-start(bf16[128,1536]{1,0:T(8,128)(2,1)S(1)} %collective-permute-done.36.refs_1_), channel_id=1, source_target_pairs={{0,1},{1,0},{2,3},{3,2},{4,5},{5,4},{6,7},{7,6},{8,9},{9,8},{10,11... | collective-permute-start | bytes 1179656 | tf_op jit(solution)/shard_map/cond/branch_1_fun/ppermute | solution.py:523
  37.4 0.0 collective-permute-done.40.refs_2_
  37.4 0.0 collective-permute-done.41.refs_3_
  37.4 1.7 %distances.3.refs_6_ = f32[768,256]{1,0:T(8,128)S(1)} custom-call(bf16[128,1536]{1,0:T(8,128)(2,1)S(1)} %constant_dynamic-update-slice_fusion.2.refs_0_, bf16[128,1536]{1,0:T(8,128)(2,1)S(1)} %collective-permute-done.39.refs_1_, bf16[128,1536]{1,0:T(8,128)(2,1)S(1)} %collective-permute-done.40.refs_2_, ...), custom_call_target="tpu_custom_call" | custom-call | flops 603979776 | bytes 3145728 | tf_op jit(solution)/shard_map/cond/branch_1_fun/distances/pallas_call | solution.py:333
  39.0 0.0 collective-permute-done.37.refs_2_
  39.0 0.0 collective-permute-done.38.refs_3_
  39.1 3.8 %predict.3 = (f32[608,128]{1,0:T(8,128)S(1)}, f32[608,128]{1,0:T(8,128)S(1)}, bf16[768,256]{1,0:T(8,128)(2,1)S(1)}, bf16[768,256]{1,0:T(8,128)(2,1)S(1)}) custom-call(bf16[128,1536]{1,0:T(8,128)(2,1)S(1)} %constant_dynamic-update-slice_fusion.4.refs_0_, bf16[128,1536]{1,0:T(8,128)(2,1)S(1)} %collective-permute-done.36.refs_1_, ...), custom_call_target="tpu_custom_call" | custom-call | flops 1321205760 | bytes 5636096 | tf_op jit(solution)/shard_map/cond/branch_1_fun/predict/pallas_call | solution.py:356
  42.8 0.1 collective-permute-start.42
  42.9 0.9 %predict_more.3 = (f32[576,128]{1,0:T(8,128)S(1)}, f32[576,128]{1,0:T(8,128)S(1)}) custom-call(bf16[576,768]{1,0:T(8,128)(2,1)S(1)} %get-tuple-element.90.high_ref, bf16[576,768]{1,0:T(8,128)(2,1)S(1)} %get-tuple-element.91.low_ref, bf16[768,256]{1,0:T(8,128)(2,1)S(1)} %get-tuple-element.92.value_high_ref, bf16[768,256]{1,0:T(8,128)(2,1)S(1)} %get-tuple-element.93.value_low_ref), custom_call_target="tpu_custom_call" | custom-call | flops 679477248 | bytes 2359296 | tf_op jit(solution)/shard_map/cond/branch_1_fun/predict_more/pallas_call | solution.py:380
  43.8 0.5 collective-permute-start.43
  44.4 0.1 collective-permute-done.42
  44.5 0.4 collective-permute-start.45
  45.0 0.6 collective-permute-done.43
  45.6 0.6 collective-permute-start.44
  46.2 2.8 %collective-permute-done.45 = f32[304,128]{1,0:T(8,128)S(1)} collective-permute-done((f32[304,128]{1,0:T(8,128)S(1)}, f32[304,128]{1,0:T(8,128)S(1)}, u32[]{:S(2)}, u32[]{:S(2)}) %collective-permute-start.45) | collective-permute-done | bytes 155680 | tf_op jit(solution)/shard_map/cond/branch_1_fun/ppermute | solution.py:523
  49.0 1.4 %collective-permute-start.47 = (f32[152,128]{1,0:T(8,128)S(1)}, f32[152,128]{1,0:T(8,128)S(1)}, u32[]{:S(2)}, u32[]{:S(2)}) collective-permute-start(f32[152,128]{1,0:T(8,128)S(1)} %slice.98), channel_id=1, source_target_pairs={{0,4},{1,3},{2,6},{3,1},{4,0},{5,7},{6,2},{7,5},{8,12},{9,11},{10,... | collective-permute-start | bytes 233480 | tf_op jit(solution)/shard_map/cond/branch_1_fun/ppermute | solution.py:523
  50.4 0.2 collective-permute-done.44
  50.6 1.8 %collective-permute-done.47 = f32[152,128]{1,0:T(8,128)S(1)} collective-permute-done((f32[152,128]{1,0:T(8,128)S(1)}, f32[152,128]{1,0:T(8,128)S(1)}, u32[]{:S(2)}, u32[]{:S(2)}) %collective-permute-start.47) | collective-permute-done | bytes 77856 | tf_op jit(solution)/shard_map/cond/branch_1_fun/ppermute | solution.py:523
  52.4 2.1 %collective-permute-start.49 = (f32[152,128]{1,0:T(8,128)S(1)}, f32[152,128]{1,0:T(8,128)S(1)}, u32[]{:S(2)}, u32[]{:S(2)}) collective-permute-start(f32[152,128]{1,0:T(8,128)S(1)} %slice_add_fusion.10), channel_id=1, source_target_pairs={{0,8},{1,9},{2,10},{3,11},{4,12},{5,13},{6,14},{7,15},{8,0},{9,1},... | collective-permute-start | bytes 233480 | tf_op jit(solution)/shard_map/cond/branch_1_fun/ppermute | solution.py:523
  54.5 1.3 %collective-permute-start.46 = (f32[144,128]{1,0:T(8,128)S(1)}, f32[144,128]{1,0:T(8,128)S(1)}, u32[]{:S(2)}, u32[]{:S(2)}) collective-permute-start(f32[144,128]{1,0:T(8,128)S(1)} %slice.96), channel_id=1, source_target_pairs={{0,4},{1,3},{2,6},{3,1},{4,0},{5,7},{6,2},{7,5},{8,12},{9,11},{10,... | collective-permute-start | bytes 221192 | tf_op jit(solution)/shard_map/cond/branch_1_fun/ppermute | solution.py:523
  55.9 1.9 %collective-permute-done.46 = f32[144,128]{1,0:T(8,128)S(1)} collective-permute-done((f32[144,128]{1,0:T(8,128)S(1)}, f32[144,128]{1,0:T(8,128)S(1)}, u32[]{:S(2)}, u32[]{:S(2)}) %collective-permute-start.46) | collective-permute-done | bytes 73760 | tf_op jit(solution)/shard_map/cond/branch_1_fun/ppermute | solution.py:523
  57.8 0.0 collective-permute-done.49
  57.8 1.3 %collective-permute-start.51 = (f32[152,128]{1,0:T(8,128)S(1)}, f32[152,128]{1,0:T(8,128)S(1)}, u32[]{:S(2)}, u32[]{:S(2)}) collective-permute-start(f32[152,128]{1,0:T(8,128)S(1)} %add.134), channel_id=1, source_target_pairs={{0,4},{1,3},{2,6},{3,1},{4,0},{5,7},{6,2},{7,5},{8,12},{9,11},{10,... | collective-permute-start | bytes 233480 | tf_op jit(solution)/shard_map/cond/branch_1_fun/ppermute | solution.py:523
  59.2 1.0 %collective-permute-start.48 = (f32[144,128]{1,0:T(8,128)S(1)}, f32[144,128]{1,0:T(8,128)S(1)}, u32[]{:S(2)}, u32[]{:S(2)}) collective-permute-start(f32[144,128]{1,0:T(8,128)S(1)} %slice_add_fusion.11), channel_id=1, source_target_pairs={{0,8},{1,9},{2,10},{3,11},{4,12},{5,13},{6,14},{7,15},{8,0},{9,1},... | collective-permute-start | bytes 221192 | tf_op jit(solution)/shard_map/cond/branch_1_fun/ppermute | solution.py:523
  60.1 3.2 %collective-permute-done.48 = f32[144,128]{1,0:T(8,128)S(1)} collective-permute-done((f32[144,128]{1,0:T(8,128)S(1)}, f32[144,128]{1,0:T(8,128)S(1)}, u32[]{:S(2)}, u32[]{:S(2)}) %collective-permute-start.48) | collective-permute-done | bytes 73760 | tf_op jit(solution)/shard_map/cond/branch_1_fun/ppermute | solution.py:523
  63.3 0.3 collective-permute-start.50
  63.6 1.9 %collective-permute-start.55 = (f32[304,128]{1,0:T(8,128)S(1)}, f32[304,128]{1,0:T(8,128)S(1)}, u32[]{:S(2)}, u32[]{:S(2)}) collective-permute-start(f32[304,128]{1,0:T(8,128)S(1)} %pad_maximum_fusion.5.keep_ref), channel_id=1, source_target_pairs={{0,2},{1,5},{2,0},{3,7},{4,6},{5,1},{6,4},{7,3},{8,10},{9,13},{10,... | collective-permute-start | bytes 466952 | tf_op jit(solution)/shard_map/cond/branch_1_fun/ppermute | solution.py:523
  65.5 1.1 %collective-permute-done.50 = f32[144,128]{1,0:T(8,128)S(1)} collective-permute-done((f32[144,128]{1,0:T(8,128)S(1)}, f32[144,128]{1,0:T(8,128)S(1)}, u32[]{:S(2)}, u32[]{:S(2)}) %collective-permute-start.50) | collective-permute-done | bytes 73760 | tf_op jit(solution)/shard_map/cond/branch_1_fun/ppermute | solution.py:523
  66.6 2.1 %collective-permute-start.52 = (f32[288,128]{1,0:T(8,128)S(1)}, f32[288,128]{1,0:T(8,128)S(1)}, u32[]{:S(2)}, u32[]{:S(2)}) collective-permute-start(f32[288,128]{1,0:T(8,128)S(1)} %pad_maximum_fusion.6.keep_ref), channel_id=1, source_target_pairs={{0,2},{1,5},{2,0},{3,7},{4,6},{5,1},{6,4},{7,3},{8,10},{9,13},{10,... | collective-permute-start | bytes 442376 | tf_op jit(solution)/shard_map/cond/branch_1_fun/ppermute | solution.py:523
  68.7 7.1 %collective-permute-start.56 = (f32[304,128]{1,0:T(8,128)S(1)}, f32[304,128]{1,0:T(8,128)S(1)}, u32[]{:S(2)}, u32[]{:S(2)}) collective-permute-start(f32[304,128]{1,0:T(8,128)S(1)} %pad_maximum_fusion.5.keep_ref), channel_id=1, source_target_pairs={{0,1},{1,0},{2,3},{3,2},{4,5},{5,4},{6,7},{7,6},{8,9},{9,8},{10,11... | collective-permute-start | bytes 466952 | tf_op jit(solution)/shard_map/cond/branch_1_fun/ppermute | solution.py:523
  75.8 0.0 collective-permute-done.55.got_ref
  75.8 0.0 collective-permute-start.57
  75.8 0.5 collective-permute-start.53
  76.3 0.0 collective-permute-done.52.got_ref
  76.3 2.6 %collective-permute-start.54 = (f32[288,128]{1,0:T(8,128)S(1)}, f32[288,128]{1,0:T(8,128)S(1)}, u32[]{:S(2)}, u32[]{:S(2)}) collective-permute-start(f32[288,128]{1,0:T(8,128)S(1)} %collective-permute-done.52.got_ref), channel_id=1, source_target_pairs={{0,1},{1,0},{2,3},{3,2},{4,5},{5,4},{6,7},{7,6},{8,9},{9,8},{10,11... | collective-permute-start | bytes 442376 | tf_op jit(solution)/shard_map/cond/branch_1_fun/ppermute | solution.py:523
  78.9 0.0 collective-permute-done.56.near_ref
  79.0 0.0 collective-permute-done.57.far_ref
  79.0 2.5 %update.3 = (f32[1000,768]{1,0:T(8,128)}, f32[1000,256]{1,0:T(8,128)}, bf16[256,768]{1,0:T(8,128)(2,1)S(1)}, bf16[256,768]{1,0:T(8,128)(2,1)S(1)}) custom-call(f32[304,128]{1,0:T(8,128)S(1)} %pad_maximum_fusion.5.keep_ref, f32[304,128]{1,0:T(8,128)S(1)} %collective-permute-done.55.got_ref, f32[304,128]{1,0:T(8,128)S(1)} %collective-permute-done.56.near_ref, ...), custom_call_target="tpu_custom_call" | custom-call | flops 717225984 | bytes 3670016 | tf_op jit(solution)/shard_map/cond/branch_1_fun/update/pallas_call | solution.py:462
  81.4 0.0 collective-permute-done.53.near_ref
  81.4 2.0 %update_more.3 = (f32[1000,768]{1,0:T(8,128)}, f32[1000,256]{1,0:T(8,128)}) custom-call(f32[288,128]{1,0:T(8,128)S(1)} %pad_maximum_fusion.6.keep_ref, f32[288,128]{1,0:T(8,128)S(1)} %collective-permute-done.52.got_ref, f32[288,128]{1,0:T(8,128)S(1)} %collective-permute-done.53.near_ref, ...), custom_call_target="tpu_custom_call", output_to_operand_aliasing={{0}: (8, {}), {1}: (9, {})} | custom-call | flops 651165696 | bytes 4521984 | tf_op jit(solution)/shard_map/cond/branch_1_fun/update_more/pallas_call | solution.py:499
  (36 shorter events, 0.3 us)
Async XLA Ops:
  0.6 3.0 %copy-start.7 = (s32[320]{0:T(512)S(1)}, s32[320]{0:T(512)}, u32[]{:S(2)}) copy-start(s32[320]{0:T(512)} %param.13) | copy-start | bytes 3844
  0.6 3.0 %copy-start.8 = (f32[160]{0:T(256)S(1)}, f32[160]{0:T(256)}, u32[]{:S(2)}) copy-start(f32[160]{0:T(256)} %param.15) | copy-start | bytes 1924
  0.7 3.0 %copy-start.4 = (f32[320,160]{0,1:T(8,128)S(1)}, f32[320,160]{0,1:T(8,128)}, u32[]{:S(2)}) copy-start(f32[320,160]{0,1:T(8,128)} %param.14) | copy-start | bytes 614404
  0.7 3.0 %copy-start.3 = (f32[256,1000]{0,1:T(8,128)S(1)}, f32[256,1000]{0,1:T(8,128)}, u32[]{:S(2)}) copy-start(f32[256,1000]{0,1:T(8,128)} %param.11) | copy-start | bytes 3072004
  3.9 5.7 %copy-start.6 = (s32[1,256]{1,0:T(1,128)S(1)}, s32[1,256]{1,0:T(1,128)}, u32[]{:S(2)}) copy-start(s32[1,256]{1,0:T(1,128)} %get-tuple-element.70.index_hbm.index_ref) | copy-start | bytes 3076 | tf_op jit(solution)/shard_map/cond
  3.9 6.0 %copy-start = (bf16[768,3072]{1,0:T(8,128)(2,1)S(1)}, bf16[768,3072]{1,0:T(8,128)(2,1)}, u32[]{:S(2)}) copy-start(bf16[768,3072]{1,0:T(8,128)(2,1)} %get-tuple-element.71.centers_hbm.centers_ref.refs_5_) | copy-start | bytes 14155780 | tf_op jit(solution)/shard_map/cond
  6.3 4.8 %copy-start.2 = (f32[1000,768]{1,0:T(8,128)S(1)}, f32[1000,768]{1,0:T(8,128)}, u32[]{:S(2)}) copy-start(f32[1000,768]{1,0:T(8,128)} %get-tuple-element.77.weights_ref) | copy-start | bytes 9216004 | tf_op jit(solution)/shard_map/cond
  6.3 13.3 %collective-permute-start.32 = (bf16[32,1536]{1,0:T(8,128)(2,1)S(1)}, bf16[32,1536]{1,0:T(8,128)(2,1)S(1)}, u32[]{:S(2)}, u32[]{:S(2)}) collective-permute-start(bf16[32,1536]{1,0:T(8,128)(2,1)S(1)} %get-tuple-element.72), channel_id=1, source_target_pairs={{0,8},{1,9},{2,10},{3,11},{4,12},{5,13},{6,14},{7,15},{8,0},{9,1},... | collective-permute-start | bytes 294920 | tf_op jit(solution)/shard_map/cond/branch_1_fun/ppermute | solution.py:523
  9.5 8.8 %collective-permute-start.33 = (bf16[32,1536]{1,0:T(8,128)(2,1)S(1)}, bf16[32,1536]{1,0:T(8,128)(2,1)S(1)}, u32[]{:S(2)}, u32[]{:S(2)}) collective-permute-start(bf16[32,1536]{1,0:T(8,128)(2,1)S(1)} %get-tuple-element.73), channel_id=1, source_target_pairs={{0,8},{1,9},{2,10},{3,11},{4,12},{5,13},{6,14},{7,15},{8,0},{9,1},... | collective-permute-start | bytes 294920 | tf_op jit(solution)/shard_map/cond/branch_1_fun/ppermute | solution.py:523
  18.3 4.9 %collective-permute-start.35 = (bf16[64,1536]{1,0:T(8,128)(2,1)S(1)}, bf16[64,1536]{1,0:T(8,128)(2,1)S(1)}, u32[]{:S(2)}, u32[]{:S(2)}) collective-permute-start(bf16[64,1536]{1,0:T(8,128)(2,1)S(1)} %constant_dynamic-update-slice_fusion), channel_id=1, source_target_pairs={{0,4},{1,3},{2,6},{3,1},{4,0},{5,7},{6,2},{7,5},{8,12},{9,11},{10,... | collective-permute-start | bytes 589832 | tf_op jit(solution)/shard_map/cond/branch_1_fun/ppermute | solution.py:523
  19.6 5.7 %collective-permute-start.34 = (bf16[64,1536]{1,0:T(8,128)(2,1)S(1)}, bf16[64,1536]{1,0:T(8,128)(2,1)S(1)}, u32[]{:S(2)}, u32[]{:S(2)}) collective-permute-start(bf16[64,1536]{1,0:T(8,128)(2,1)S(1)} %pad_maximum_fusion.4), channel_id=1, source_target_pairs={{0,4},{1,3},{2,6},{3,1},{4,0},{5,7},{6,2},{7,5},{8,12},{9,11},{10,... | collective-permute-start | bytes 589832 | tf_op jit(solution)/shard_map/cond/branch_1_fun/ppermute | solution.py:523
  23.2 8.0 %collective-permute-start.39 = (bf16[128,1536]{1,0:T(8,128)(2,1)S(1)}, bf16[128,1536]{1,0:T(8,128)(2,1)S(1)}, u32[]{:S(2)}, u32[]{:S(2)}) collective-permute-start(bf16[128,1536]{1,0:T(8,128)(2,1)S(1)} %constant_dynamic-update-slice_fusion.2.refs_0_), channel_id=1, source_target_pairs={{0,2},{1,5},{2,0},{3,7},{4,6},{5,1},{6,4},{7,3},{8,10},{9,13},{10,... | collective-permute-start | bytes 1179656 | tf_op jit(solution)/shard_map/cond/branch_1_fun/ppermute | solution.py:523
  25.3 10.1 %collective-permute-start.36 = (bf16[128,1536]{1,0:T(8,128)(2,1)S(1)}, bf16[128,1536]{1,0:T(8,128)(2,1)S(1)}, u32[]{:S(2)}, u32[]{:S(2)}) collective-permute-start(bf16[128,1536]{1,0:T(8,128)(2,1)S(1)} %constant_dynamic-update-slice_fusion.4.refs_0_), channel_id=1, source_target_pairs={{0,2},{1,5},{2,0},{3,7},{4,6},{5,1},{6,4},{7,3},{8,10},{9,13},{10,... | collective-permute-start | bytes 1179656 | tf_op jit(solution)/shard_map/cond/branch_1_fun/ppermute | solution.py:523
  26.5 10.9 %collective-permute-start.40 = (bf16[128,1536]{1,0:T(8,128)(2,1)S(1)}, bf16[128,1536]{1,0:T(8,128)(2,1)S(1)}, u32[]{:S(2)}, u32[]{:S(2)}) collective-permute-start(bf16[128,1536]{1,0:T(8,128)(2,1)S(1)} %constant_dynamic-update-slice_fusion.2.refs_0_), channel_id=1, source_target_pairs={{0,1},{1,0},{2,3},{3,2},{4,5},{5,4},{6,7},{7,6},{8,9},{9,8},{10,11... | collective-permute-start | bytes 1179656 | tf_op jit(solution)/shard_map/cond/branch_1_fun/ppermute | solution.py:523
  31.2 6.2 %collective-permute-start.41 = (bf16[128,1536]{1,0:T(8,128)(2,1)S(1)}, bf16[128,1536]{1,0:T(8,128)(2,1)S(1)}, u32[]{:S(2)}, u32[]{:S(2)}) collective-permute-start(bf16[128,1536]{1,0:T(8,128)(2,1)S(1)} %collective-permute-done.39.refs_1_), channel_id=1, source_target_pairs={{0,1},{1,0},{2,3},{3,2},{4,5},{5,4},{6,7},{7,6},{8,9},{9,8},{10,11... | collective-permute-start | bytes 1179656 | tf_op jit(solution)/shard_map/cond/branch_1_fun/ppermute | solution.py:523
  33.2 5.9 %collective-permute-start.37 = (bf16[128,1536]{1,0:T(8,128)(2,1)S(1)}, bf16[128,1536]{1,0:T(8,128)(2,1)S(1)}, u32[]{:S(2)}, u32[]{:S(2)}) collective-permute-start(bf16[128,1536]{1,0:T(8,128)(2,1)S(1)} %constant_dynamic-update-slice_fusion.4.refs_0_), channel_id=1, source_target_pairs={{0,1},{1,0},{2,3},{3,2},{4,5},{5,4},{6,7},{7,6},{8,9},{9,8},{10,11... | collective-permute-start | bytes 1179656 | tf_op jit(solution)/shard_map/cond/branch_1_fun/ppermute | solution.py:523
  35.4 3.6 %collective-permute-start.38 = (bf16[128,1536]{1,0:T(8,128)(2,1)S(1)}, bf16[128,1536]{1,0:T(8,128)(2,1)S(1)}, u32[]{:S(2)}, u32[]{:S(2)}) collective-permute-start(bf16[128,1536]{1,0:T(8,128)(2,1)S(1)} %collective-permute-done.36.refs_1_), channel_id=1, source_target_pairs={{0,1},{1,0},{2,3},{3,2},{4,5},{5,4},{6,7},{7,6},{8,9},{9,8},{10,11... | collective-permute-start | bytes 1179656 | tf_op jit(solution)/shard_map/cond/branch_1_fun/ppermute | solution.py:523
  42.8 1.7 %collective-permute-start.42 = (f32[608,128]{1,0:T(8,128)S(1)}, f32[608,128]{1,0:T(8,128)S(1)}, u32[]{:S(2)}, u32[]{:S(2)}) collective-permute-start(f32[608,128]{1,0:T(8,128)S(1)} %get-tuple-element.89), channel_id=1, source_target_pairs={{0,1},{1,0},{2,3},{3,2},{4,5},{5,4},{6,7},{7,6},{8,9},{9,8},{10,11... | collective-permute-start | bytes 933896 | tf_op jit(solution)/shard_map/cond/branch_1_fun/ppermute | solution.py:523
  43.8 1.8 %collective-permute-start.43 = (f32[576,128]{1,0:T(8,128)S(1)}, f32[576,128]{1,0:T(8,128)S(1)}, u32[]{:S(2)}, u32[]{:S(2)}) collective-permute-start(f32[576,128]{1,0:T(8,128)S(1)} %get-tuple-element.96), channel_id=1, source_target_pairs={{0,1},{1,0},{2,3},{3,2},{4,5},{5,4},{6,7},{7,6},{8,9},{9,8},{10,11... | collective-permute-start | bytes 884744 | tf_op jit(solution)/shard_map/cond/branch_1_fun/ppermute | solution.py:523
  44.5 4.4 %collective-permute-start.45 = (f32[304,128]{1,0:T(8,128)S(1)}, f32[304,128]{1,0:T(8,128)S(1)}, u32[]{:S(2)}, u32[]{:S(2)}) collective-permute-start(f32[304,128]{1,0:T(8,128)S(1)} %slice.94), channel_id=1, source_target_pairs={{0,2},{1,5},{2,0},{3,7},{4,6},{5,1},{6,4},{7,3},{8,10},{9,13},{10,... | collective-permute-start | bytes 466952 | tf_op jit(solution)/shard_map/cond/branch_1_fun/ppermute | solution.py:523
  45.6 4.9 %collective-permute-start.44 = (f32[288,128]{1,0:T(8,128)S(1)}, f32[288,128]{1,0:T(8,128)S(1)}, u32[]{:S(2)}, u32[]{:S(2)}) collective-permute-start(f32[288,128]{1,0:T(8,128)S(1)} %slice.92), channel_id=1, source_target_pairs={{0,2},{1,5},{2,0},{3,7},{4,6},{5,1},{6,4},{7,3},{8,10},{9,13},{10,... | collective-permute-start | bytes 442376 | tf_op jit(solution)/shard_map/cond/branch_1_fun/ppermute | solution.py:523
  49.0 3.3 %collective-permute-start.47 = (f32[152,128]{1,0:T(8,128)S(1)}, f32[152,128]{1,0:T(8,128)S(1)}, u32[]{:S(2)}, u32[]{:S(2)}) collective-permute-start(f32[152,128]{1,0:T(8,128)S(1)} %slice.98), channel_id=1, source_target_pairs={{0,4},{1,3},{2,6},{3,1},{4,0},{5,7},{6,2},{7,5},{8,12},{9,11},{10,... | collective-permute-start | bytes 233480 | tf_op jit(solution)/shard_map/cond/branch_1_fun/ppermute | solution.py:523
  52.4 5.5 %collective-permute-start.49 = (f32[152,128]{1,0:T(8,128)S(1)}, f32[152,128]{1,0:T(8,128)S(1)}, u32[]{:S(2)}, u32[]{:S(2)}) collective-permute-start(f32[152,128]{1,0:T(8,128)S(1)} %slice_add_fusion.10), channel_id=1, source_target_pairs={{0,8},{1,9},{2,10},{3,11},{4,12},{5,13},{6,14},{7,15},{8,0},{9,1},... | collective-permute-start | bytes 233480 | tf_op jit(solution)/shard_map/cond/branch_1_fun/ppermute | solution.py:523
  54.5 3.3 %collective-permute-start.46 = (f32[144,128]{1,0:T(8,128)S(1)}, f32[144,128]{1,0:T(8,128)S(1)}, u32[]{:S(2)}, u32[]{:S(2)}) collective-permute-start(f32[144,128]{1,0:T(8,128)S(1)} %slice.96), channel_id=1, source_target_pairs={{0,4},{1,3},{2,6},{3,1},{4,0},{5,7},{6,2},{7,5},{8,12},{9,11},{10,... | collective-permute-start | bytes 221192 | tf_op jit(solution)/shard_map/cond/branch_1_fun/ppermute | solution.py:523
  57.8 5.8 %collective-permute-start.51 = (f32[152,128]{1,0:T(8,128)S(1)}, f32[152,128]{1,0:T(8,128)S(1)}, u32[]{:S(2)}, u32[]{:S(2)}) collective-permute-start(f32[152,128]{1,0:T(8,128)S(1)} %add.134), channel_id=1, source_target_pairs={{0,4},{1,3},{2,6},{3,1},{4,0},{5,7},{6,2},{7,5},{8,12},{9,11},{10,... | collective-permute-start | bytes 233480 | tf_op jit(solution)/shard_map/cond/branch_1_fun/ppermute | solution.py:523
  59.2 4.2 %collective-permute-start.48 = (f32[144,128]{1,0:T(8,128)S(1)}, f32[144,128]{1,0:T(8,128)S(1)}, u32[]{:S(2)}, u32[]{:S(2)}) collective-permute-start(f32[144,128]{1,0:T(8,128)S(1)} %slice_add_fusion.11), channel_id=1, source_target_pairs={{0,8},{1,9},{2,10},{3,11},{4,12},{5,13},{6,14},{7,15},{8,0},{9,1},... | collective-permute-start | bytes 221192 | tf_op jit(solution)/shard_map/cond/branch_1_fun/ppermute | solution.py:523
  63.3 3.3 %collective-permute-start.50 = (f32[144,128]{1,0:T(8,128)S(1)}, f32[144,128]{1,0:T(8,128)S(1)}, u32[]{:S(2)}, u32[]{:S(2)}) collective-permute-start(f32[144,128]{1,0:T(8,128)S(1)} %add.135), channel_id=1, source_target_pairs={{0,4},{1,3},{2,6},{3,1},{4,0},{5,7},{6,2},{7,5},{8,12},{9,11},{10,... | collective-permute-start | bytes 221192 | tf_op jit(solution)/shard_map/cond/branch_1_fun/ppermute | solution.py:523
  63.6 12.2 %collective-permute-start.55 = (f32[304,128]{1,0:T(8,128)S(1)}, f32[304,128]{1,0:T(8,128)S(1)}, u32[]{:S(2)}, u32[]{:S(2)}) collective-permute-start(f32[304,128]{1,0:T(8,128)S(1)} %pad_maximum_fusion.5.keep_ref), channel_id=1, source_target_pairs={{0,2},{1,5},{2,0},{3,7},{4,6},{5,1},{6,4},{7,3},{8,10},{9,13},{10,... | collective-permute-start | bytes 466952 | tf_op jit(solution)/shard_map/cond/branch_1_fun/ppermute | solution.py:523
  66.6 9.7 %collective-permute-start.52 = (f32[288,128]{1,0:T(8,128)S(1)}, f32[288,128]{1,0:T(8,128)S(1)}, u32[]{:S(2)}, u32[]{:S(2)}) collective-permute-start(f32[288,128]{1,0:T(8,128)S(1)} %pad_maximum_fusion.6.keep_ref), channel_id=1, source_target_pairs={{0,2},{1,5},{2,0},{3,7},{4,6},{5,1},{6,4},{7,3},{8,10},{9,13},{10,... | collective-permute-start | bytes 442376 | tf_op jit(solution)/shard_map/cond/branch_1_fun/ppermute | solution.py:523
  68.7 10.3 %collective-permute-start.56 = (f32[304,128]{1,0:T(8,128)S(1)}, f32[304,128]{1,0:T(8,128)S(1)}, u32[]{:S(2)}, u32[]{:S(2)}) collective-permute-start(f32[304,128]{1,0:T(8,128)S(1)} %pad_maximum_fusion.5.keep_ref), channel_id=1, source_target_pairs={{0,1},{1,0},{2,3},{3,2},{4,5},{5,4},{6,7},{7,6},{8,9},{9,8},{10,11... | collective-permute-start | bytes 466952 | tf_op jit(solution)/shard_map/cond/branch_1_fun/ppermute | solution.py:523
  75.8 3.1 %collective-permute-start.57 = (f32[304,128]{1,0:T(8,128)S(1)}, f32[304,128]{1,0:T(8,128)S(1)}, u32[]{:S(2)}, u32[]{:S(2)}) collective-permute-start(f32[304,128]{1,0:T(8,128)S(1)} %collective-permute-done.55.got_ref), channel_id=1, source_target_pairs={{0,1},{1,0},{2,3},{3,2},{4,5},{5,4},{6,7},{7,6},{8,9},{9,8},{10,11... | collective-permute-start | bytes 466952 | tf_op jit(solution)/shard_map/cond/branch_1_fun/ppermute | solution.py:523
  75.8 5.6 %collective-permute-start.53 = (f32[288,128]{1,0:T(8,128)S(1)}, f32[288,128]{1,0:T(8,128)S(1)}, u32[]{:S(2)}, u32[]{:S(2)}) collective-permute-start(f32[288,128]{1,0:T(8,128)S(1)} %pad_maximum_fusion.6.keep_ref), channel_id=1, source_target_pairs={{0,1},{1,0},{2,3},{3,2},{4,5},{5,4},{6,7},{7,6},{8,9},{9,8},{10,11... | collective-permute-start | bytes 442376 | tf_op jit(solution)/shard_map/cond/branch_1_fun/ppermute | solution.py:523
  76.3 5.1 %collective-permute-start.54 = (f32[288,128]{1,0:T(8,128)S(1)}, f32[288,128]{1,0:T(8,128)S(1)}, u32[]{:S(2)}, u32[]{:S(2)}) collective-permute-start(f32[288,128]{1,0:T(8,128)S(1)} %collective-permute-done.52.got_ref), channel_id=1, source_target_pairs={{0,1},{1,0},{2,3},{3,2},{4,5},{5,4},{6,7},{7,6},{8,9},{9,8},{10,11... | collective-permute-start | bytes 442376 | tf_op jit(solution)/shard_map/cond/branch_1_fun/ppermute | solution.py:523

commit v12 on v10

--- a/solution.py
+++ b/solution.py
@@ -400,7 +400,7 @@
         scratch_shapes=[pltpu.VMEM((padded, rows), F32)],
         compiler_params=params(),
         cost_estimate=pl.CostEstimate(
-            flops=6 * rows * count * padded, bytes_accessed=4 * padded * (count + rows), transcendentals=0
+            flops=int(1.0 * 6) * rows * count * padded, bytes_accessed=4 * padded * (count + rows), transcendentals=0
         ),
         name="predict_more",
     )(high, low, value_high, value_low)
@@ -532,7 +532,7 @@
         ],
         compiler_params=params(),
         cost_estimate=pl.CostEstimate(
-            flops=6 * rows * count * here, bytes_accessed=8 * here * (count + rows), transcendentals=0
+            flops=int(1.0 * 6) * rows * count * here, bytes_accessed=8 * here * (count + rows), transcendentals=0
         ),
         name="update_more",
     )(mine, other, targets, weights, high, low, new, out)
@@ -593,14 +593,14 @@
     unit = 8 * CHUNKS
     units = -(-(classes + depth) // unit)
     first = (units + 1) // 2 * unit
-    second = units * unit - first
+    second = first
     far = [pltpu.with_memory_space_constraint(x, pltpu.HBM) for x in (batch_index, centers)]
     ready = [center_norms(centers), *spread_weights(nys_index.reshape(1, -1), eigvec, weights, first, second)]
     if packed:
         ready.append(select_packed(batch_index, count, chips))
         slots = [pack_rows(*far, part) for part in range(PARTS)]
-        mine, other, norms, high1, low1, high2, low2, spread, select = all_of(slots[0], chips, ready)
-        late = all_of(slots[1], chips)
+        mine, other = all_of(slots[0], chips)
+        *late, norms, high1, low1, high2, low2, spread, select = all_of(slots[1], chips, ready)
     else:
         ready.append(select_summed(rows))
         picked = [pick_batch(*far, part) for part in range(PARTS)]

time: 81.7 us -> 75.6 us (0.925)
  starting transfers between devices: 36.6 us -> 30.9 us
    ppermute x22, starting transfers between devices: 36.6 us -> 30.9 us  [swap(): lax.ppermute(x, AXES, [(i, i ^ flip[i & 1]) for i in range(2 * chips)])]
  transfers between devices with their start and end apart: 22 -> 22, of which waited for: 13 -> 13; matrix products, arithmetic and copies ran while one was open for 0% -> 1% of each run, Pallas kernels for 12% -> 13%
where the time goes in v12:
time: 75.6 us; the launch traced here: 75.4 us
  starting transfers between devices  30.9 us (41%)
  waiting for transfers between devices  23.7 us (31%)
  Pallas kernels  18.3 us (24%)
  between operations  1.45 us (2%)
    ppermute x22, starting transfers between devices, swap(): lax.ppermute(x, AXES, [(i, i ^ flip[i & 1]) for i in range(2 * chips)])  30.9 us
    ppermute x22, waiting for transfers between devices, swap(): lax.ppermute(x, AXES, [(i, i ^ flip[i & 1]) for i in range(2 * chips)])  23.7 us
    pallas_call x2, Pallas kernels, pack_rows(): pl.pallas_call(functools.partial(pack_body, part * depth), in_specs=[hbm,...  3.83 us
    pallas_call x1, Pallas kernels, predict(): pl.pallas_call(predict_body, in_specs=[vmem] * 7, out_specs=[vmem] * 4, o...  3.37 us
    pallas_call x1, Pallas kernels, update(): pl.pallas_call(update_body, in_specs=[vmem] * 7, out_specs=[hbm, hbm, vme...  2.46 us
    pallas_call x1, Pallas kernels, update_more(): pl.pallas_call(functools.partial(update_more_body, begin), in_specs=[vmem...  2.02 us
    pallas_call x1, Pallas kernels, spread_weights(): pl.pallas_call(functools.partial(spread_body, first, classes), out_shape=...  1.59 us
  transfers between devices with their start and end apart: 22, of which 13 were waited for; matrix products, arithmetic and copies ran while one was open for 1% of the time, Pallas kernels for 13%

profile of v12, /device:TPU:1, one launch (start us, length us, event | category | flops | bytes accessed | tf_op | source)
XLA Modules:
  0.0 75.4 jit_solution(10408997305480269436)
XLA Ops:
  0.6 1.3 %rows_fit.1 = s32[1]{0:T(128)} custom-call(s32[1,256]{1,0:T(1,128)} %bitcast.17), custom_call_target="tpu_custom_call" | custom-call | tf_op jit(solution)/shard_map/rows_fit/pallas_call | solution.py:138
  2.6 72.6 %conditional.1 = ((f32[1000,768]{1,0:T(8,128)}, f32[1000,256]{1,0:T(8,128)})) conditional(s32[]{:T(128)} %bitcast.2, (s32[1,256]{1,0:T(1,128)}, bf16[768,3072]{1,0:T(8,128)(2,1)}, s32[320]{0:T(512)}, f32[160,320]{1,0:T(8,128)}, f32[1000,768]{1,0:T(8,128)}, /*index=5*/f32[1000,256]{1,0:T(8,128)}, f32[1,160]{1,0:T(1,128)}) %tuple.30, ...), branch_computations={%region_0.1_spmd, %region_1.2_spmd} | conditional | flops 5464187904 | bytes 105839680 | solution.py:619
  2.8 1.9 %pack_rows.3 = bf16[32,1536]{1,0:T(8,128)(2,1)S(1)} custom-call(s32[1,256]{1,0:T(1,128)} %get-tuple-element.62.index_hbm.index_ref, bf16[768,3072]{1,0:T(8,128)(2,1)} %get-tuple-element.63.centers_hbm.centers_ref), custom_call_target="tpu_custom_call" | custom-call | flops 75497472 | bytes 2457600 | tf_op jit(solution)/shard_map/cond/branch_1_fun/pack_rows/pallas_call | solution.py:180
  4.7 0.0 copy-start.8
  4.8 0.0 copy-start.10
  4.8 0.0 copy-start
  4.8 3.2 %collective-permute-start.32 = (bf16[32,1536]{1,0:T(8,128)(2,1)S(1)}, bf16[32,1536]{1,0:T(8,128)(2,1)S(1)}, u32[]{:S(2)}, u32[]{:S(2)}) collective-permute-start(bf16[32,1536]{1,0:T(8,128)(2,1)S(1)} %pack_rows.3), channel_id=1, source_target_pairs={{0,8},{1,9},{2,10},{3,11},{4,12},{5,13},{6,14},{7,15},{8,0},{9,1},... | collective-permute-start | bytes 294920 | tf_op jit(solution)/shard_map/cond/branch_1_fun/ppermute | solution.py:543
  8.0 1.9 %pack_rows.2 = bf16[32,1536]{1,0:T(8,128)(2,1)S(1)} custom-call(s32[1,256]{1,0:T(1,128)} %get-tuple-element.62.index_hbm.index_ref, bf16[768,3072]{1,0:T(8,128)(2,1)} %get-tuple-element.63.centers_hbm.centers_ref), custom_call_target="tpu_custom_call" | custom-call | flops 75497472 | bytes 2457600 | tf_op jit(solution)/shard_map/cond/branch_1_fun/pack_rows/pallas_call | solution.py:180
  9.9 0.0 copy-start.2
  9.9 0.0 copy-start.6
  9.9 0.2 collective-permute-start.28
  10.2 0.0 copy-done.8
  10.2 0.3 select_packed.1.select_ref
  10.5 1.2 %center_norms.3.norm_ref = f32[768,128]{1,0:T(8,128)S(1)} custom-call(bf16[768,3072]{1,0:T(8,128)(2,1)S(1)} %copy-done), custom_call_target="tpu_custom_call" | custom-call | flops 4718592 | bytes 4718592 | tf_op jit(solution)/shard_map/cond/branch_1_fun/center_norms/pallas_call | solution.py:285
  11.6 0.1 copy-done.2
  11.8 1.6 %spread_weights.3 = (bf16[608,768]{1,0:T(8,128)(2,1)S(1)}, bf16[608,768]{1,0:T(8,128)(2,1)S(1)}, bf16[608,768]{1,0:T(8,128)(2,1)S(1)}, bf16[608,768]{1,0:T(8,128)(2,1)S(1)}, f32[160,768]{1,0:T(8,128)S(1)}) custom-call(s32[1,320]{1,0:T(1,128)S(1)} %reshape.99.index_ref, f32[160,320]{1,0:T(8,128)S(1)} %copy-done.6, f32[1000,768]{1,0:T(8,128)S(1)} %copy-done.2), custom_call_target="tpu_custom_call" | custom-call | flops 235929600 | bytes 7471104 | tf_op jit(solution)/shard_map/cond/branch_1_fun/spread_weights/pallas_call | solution.py:258
  13.4 0.0 collective-permute-done.32
  13.4 1.3 %collective-permute-start.33 = (bf16[64,1536]{1,0:T(8,128)(2,1)S(1)}, bf16[64,1536]{1,0:T(8,128)(2,1)S(1)}, u32[]{:S(2)}, u32[]{:S(2)}) collective-permute-start(bf16[64,1536]{1,0:T(8,128)(2,1)S(1)} %pad_maximum_fusion.14), channel_id=1, source_target_pairs={{0,4},{1,3},{2,6},{3,1},{4,0},{5,7},{6,2},{7,5},{8,12},{9,11},{10,... | collective-permute-start | bytes 589832 | tf_op jit(solution)/shard_map/cond/branch_1_fun/ppermute | solution.py:543
  14.7 0.0 collective-permute-done.28
  14.7 1.0 %collective-permute-start.29 = (bf16[64,1536]{1,0:T(8,128)(2,1)S(1)}, bf16[64,1536]{1,0:T(8,128)(2,1)S(1)}, u32[]{:S(2)}, u32[]{:S(2)}) collective-permute-start(bf16[64,1536]{1,0:T(8,128)(2,1)S(1)} %pad_maximum_fusion.13), channel_id=1, source_target_pairs={{0,4},{1,3},{2,6},{3,1},{4,0},{5,7},{6,2},{7,5},{8,12},{9,11},{10,... | collective-permute-start | bytes 589832 | tf_op jit(solution)/shard_map/cond/branch_1_fun/ppermute | solution.py:543
  15.7 2.6 %collective-permute-done.33 = bf16[64,1536]{1,0:T(8,128)(2,1)S(1)} collective-permute-done((bf16[64,1536]{1,0:T(8,128)(2,1)S(1)}, bf16[64,1536]{1,0:T(8,128)(2,1)S(1)}, u32[]{:S(2)}, u32[]{:S(2)}) %collective-permute-start.33) | collective-permute-done | bytes 196640 | tf_op jit(solution)/shard_map/cond/branch_1_fun/ppermute | solution.py:543
  18.3 2.6 %collective-permute-start.34 = (bf16[128,1536]{1,0:T(8,128)(2,1)S(1)}, bf16[128,1536]{1,0:T(8,128)(2,1)S(1)}, u32[]{:S(2)}, u32[]{:S(2)}) collective-permute-start(bf16[128,1536]{1,0:T(8,128)(2,1)S(1)} %pad_maximum_fusion.10), channel_id=1, source_target_pairs={{0,2},{1,5},{2,0},{3,7},{4,6},{5,1},{6,4},{7,3},{8,10},{9,13},{10,... | collective-permute-start | bytes 1179656 | tf_op jit(solution)/shard_map/cond/branch_1_fun/ppermute | solution.py:543
  20.9 0.0 collective-permute-done.29
  20.9 2.1 %collective-permute-start.30 = (bf16[128,1536]{1,0:T(8,128)(2,1)S(1)}, bf16[128,1536]{1,0:T(8,128)(2,1)S(1)}, u32[]{:S(2)}, u32[]{:S(2)}) collective-permute-start(bf16[128,1536]{1,0:T(8,128)(2,1)S(1)} %pad_maximum_fusion.9), channel_id=1, source_target_pairs={{0,2},{1,5},{2,0},{3,7},{4,6},{5,1},{6,4},{7,3},{8,10},{9,13},{10,... | collective-permute-start | bytes 1179656 | tf_op jit(solution)/shard_map/cond/branch_1_fun/ppermute | solution.py:543
  23.0 4.8 %collective-permute-done.34 = bf16[128,1536]{1,0:T(8,128)(2,1)S(1)} collective-permute-done((bf16[128,1536]{1,0:T(8,128)(2,1)S(1)}, bf16[128,1536]{1,0:T(8,128)(2,1)S(1)}, u32[]{:S(2)}, u32[]{:S(2)}) %collective-permute-start.34) | collective-permute-done | bytes 393248 | tf_op jit(solution)/shard_map/cond/branch_1_fun/ppermute | solution.py:543
  27.8 0.1 pad_maximum_fusion.8.mine_ref
  27.8 0.6 collective-permute-start.35
  28.5 3.5 %collective-permute-done.30 = bf16[128,1536]{1,0:T(8,128)(2,1)S(1)} collective-permute-done((bf16[128,1536]{1,0:T(8,128)(2,1)S(1)}, bf16[128,1536]{1,0:T(8,128)(2,1)S(1)}, u32[]{:S(2)}, u32[]{:S(2)}) %collective-permute-start.30) | collective-permute-done | bytes 393248 | tf_op jit(solution)/shard_map/cond/branch_1_fun/ppermute | solution.py:543
  32.0 1.4 %collective-permute-start.31 = (bf16[256,1536]{1,0:T(8,128)(2,1)S(1)}, bf16[256,1536]{1,0:T(8,128)(2,1)S(1)}, u32[]{:S(2)}, u32[]{:S(2)}) collective-permute-start(bf16[256,1536]{1,0:T(8,128)(2,1)S(1)} %constant_dynamic-update-slice_fusion.mine_ref), channel_id=1, source_target_pairs={{0,1},{1,0},{2,3},{3,2},{4,5},{5,4},{6,7},{7,6},{8,9},{9,8},{10,11... | collective-permute-start | bytes 2359304 | tf_op jit(solution)/shard_map/cond/branch_1_fun/ppermute | solution.py:543
  33.4 0.0 collective-permute-done.35.other_ref
  33.4 1.3 %distances.3.before_ref = f32[768,256]{1,0:T(8,128)S(1)} custom-call(bf16[256,1536]{1,0:T(8,128)(2,1)S(1)} %pad_maximum_fusion.8.mine_ref, bf16[256,1536]{1,0:T(8,128)(2,1)S(1)} %collective-permute-done.35.other_ref, bf16[256,512]{1,0:T(8,128)(2,1)S(1)} %select_packed.1.select_ref, bf16[768,3072]{1,0:T(8,128)(2,1)S(1)} %copy-done, ...), custom_call_target="tpu_custom_call" | custom-call | flops 603979776 | bytes 3145728 | tf_op jit(solution)/shard_map/cond/branch_1_fun/distances/pallas_call | solution.py:350
  34.7 0.6 collective-permute-done.31.other_ref
  35.3 3.4 %predict.3 = (f32[608,128]{1,0:T(8,128)S(1)}, f32[608,128]{1,0:T(8,128)S(1)}, bf16[768,256]{1,0:T(8,128)(2,1)S(1)}, bf16[768,256]{1,0:T(8,128)(2,1)S(1)}) custom-call(bf16[256,1536]{1,0:T(8,128)(2,1)S(1)} %constant_dynamic-update-slice_fusion.mine_ref, bf16[256,1536]{1,0:T(8,128)(2,1)S(1)} %collective-permute-done.31.other_ref, ...), custom_call_target="tpu_custom_call" | custom-call | flops 1321205760 | bytes 5636096 | tf_op jit(solution)/shard_map/cond/branch_1_fun/predict/pallas_call | solution.py:373
  38.7 0.4 collective-permute-start.43
  39.1 0.9 %predict_more.3 = (f32[608,128]{1,0:T(8,128)S(1)}, f32[608,128]{1,0:T(8,128)S(1)}) custom-call(bf16[608,768]{1,0:T(8,128)(2,1)S(1)} %get-tuple-element.72.high_ref, bf16[608,768]{1,0:T(8,128)(2,1)S(1)} %get-tuple-element.73.low_ref, bf16[768,256]{1,0:T(8,128)(2,1)S(1)} %get-tuple-element.79.value_high_ref, bf16[768,256]{1,0:T(8,128)(2,1)S(1)} %get-tuple-element.80.value_low_ref), custom_call_target="tpu_custom_call" | custom-call | flops 717225984 | bytes 2490368 | tf_op jit(solution)/shard_map/cond/branch_1_fun/predict_more/pallas_call | solution.py:397
  40.1 0.2 collective-permute-start.36
  40.3 0.1 collective-permute-done.43
  40.4 1.1 %collective-permute-start.44 = (f32[304,128]{1,0:T(8,128)S(1)}, f32[304,128]{1,0:T(8,128)S(1)}, u32[]{:S(2)}, u32[]{:S(2)}) collective-permute-start(f32[304,128]{1,0:T(8,128)S(1)} %slice.96), channel_id=1, source_target_pairs={{0,2},{1,5},{2,0},{3,7},{4,6},{5,1},{6,4},{7,3},{8,10},{9,13},{10,... | collective-permute-start | bytes 466952 | tf_op jit(solution)/shard_map/cond/branch_1_fun/ppermute | solution.py:543
  41.5 0.3 collective-permute-done.36
  41.8 1.1 %collective-permute-start.37 = (f32[304,128]{1,0:T(8,128)S(1)}, f32[304,128]{1,0:T(8,128)S(1)}, u32[]{:S(2)}, u32[]{:S(2)}) collective-permute-start(f32[304,128]{1,0:T(8,128)S(1)} %slice.92), channel_id=1, source_target_pairs={{0,2},{1,5},{2,0},{3,7},{4,6},{5,1},{6,4},{7,3},{8,10},{9,13},{10,... | collective-permute-start | bytes 466952 | tf_op jit(solution)/shard_map/cond/branch_1_fun/ppermute | solution.py:543
  42.9 2.0 %collective-permute-done.44 = f32[304,128]{1,0:T(8,128)S(1)} collective-permute-done((f32[304,128]{1,0:T(8,128)S(1)}, f32[304,128]{1,0:T(8,128)S(1)}, u32[]{:S(2)}, u32[]{:S(2)}) %collective-permute-start.44) | collective-permute-done | bytes 155680 | tf_op jit(solution)/shard_map/cond/branch_1_fun/ppermute | solution.py:543
  44.9 1.3 %collective-permute-start.45 = (f32[152,128]{1,0:T(8,128)S(1)}, f32[152,128]{1,0:T(8,128)S(1)}, u32[]{:S(2)}, u32[]{:S(2)}) collective-permute-start(f32[152,128]{1,0:T(8,128)S(1)} %slice.98), channel_id=1, source_target_pairs={{0,4},{1,3},{2,6},{3,1},{4,0},{5,7},{6,2},{7,5},{8,12},{9,11},{10,... | collective-permute-start | bytes 233480 | tf_op jit(solution)/shard_map/cond/branch_1_fun/ppermute | solution.py:543
  46.2 0.3 collective-permute-done.37
  46.6 1.3 %collective-permute-start.38 = (f32[152,128]{1,0:T(8,128)S(1)}, f32[152,128]{1,0:T(8,128)S(1)}, u32[]{:S(2)}, u32[]{:S(2)}) collective-permute-start(f32[152,128]{1,0:T(8,128)S(1)} %slice.94), channel_id=1, source_target_pairs={{0,4},{1,3},{2,6},{3,1},{4,0},{5,7},{6,2},{7,5},{8,12},{9,11},{10,... | collective-permute-start | bytes 233480 | tf_op jit(solution)/shard_map/cond/branch_1_fun/ppermute | solution.py:543
  47.9 0.3 collective-permute-done.45
  48.2 2.7 %collective-permute-start.46 = (f32[152,128]{1,0:T(8,128)S(1)}, f32[152,128]{1,0:T(8,128)S(1)}, u32[]{:S(2)}, u32[]{:S(2)}) collective-permute-start(f32[152,128]{1,0:T(8,128)S(1)} %slice_add_fusion.10), channel_id=1, source_target_pairs={{0,8},{1,9},{2,10},{3,11},{4,12},{5,13},{6,14},{7,15},{8,0},{9,1},... | collective-permute-start | bytes 233480 | tf_op jit(solution)/shard_map/cond/branch_1_fun/ppermute | solution.py:543
  51.0 0.0 collective-permute-done.38
  51.0 1.7 %collective-permute-start.39 = (f32[152,128]{1,0:T(8,128)S(1)}, f32[152,128]{1,0:T(8,128)S(1)}, u32[]{:S(2)}, u32[]{:S(2)}) collective-permute-start(f32[152,128]{1,0:T(8,128)S(1)} %slice_add_fusion.11), channel_id=1, source_target_pairs={{0,8},{1,9},{2,10},{3,11},{4,12},{5,13},{6,14},{7,15},{8,0},{9,1},... | collective-permute-start | bytes 233480 | tf_op jit(solution)/shard_map/cond/branch_1_fun/ppermute | solution.py:543
  52.7 0.1 collective-permute-done.46
  52.8 1.3 %collective-permute-start.47 = (f32[152,128]{1,0:T(8,128)S(1)}, f32[152,128]{1,0:T(8,128)S(1)}, u32[]{:S(2)}, u32[]{:S(2)}) collective-permute-start(f32[152,128]{1,0:T(8,128)S(1)} %add.135), channel_id=1, source_target_pairs={{0,4},{1,3},{2,6},{3,1},{4,0},{5,7},{6,2},{7,5},{8,12},{9,11},{10,... | collective-permute-start | bytes 233480 | tf_op jit(solution)/shard_map/cond/branch_1_fun/ppermute | solution.py:543
  54.1 3.9 %collective-permute-done.39 = f32[152,128]{1,0:T(8,128)S(1)} collective-permute-done((f32[152,128]{1,0:T(8,128)S(1)}, f32[152,128]{1,0:T(8,128)S(1)}, u32[]{:S(2)}, u32[]{:S(2)}) %collective-permute-start.39) | collective-permute-done | bytes 77856 | tf_op jit(solution)/shard_map/cond/branch_1_fun/ppermute | solution.py:543
  58.0 1.3 %collective-permute-start.40 = (f32[152,128]{1,0:T(8,128)S(1)}, f32[152,128]{1,0:T(8,128)S(1)}, u32[]{:S(2)}, u32[]{:S(2)}) collective-permute-start(f32[152,128]{1,0:T(8,128)S(1)} %add.131), channel_id=1, source_target_pairs={{0,4},{1,3},{2,6},{3,1},{4,0},{5,7},{6,2},{7,5},{8,12},{9,11},{10,... | collective-permute-start | bytes 233480 | tf_op jit(solution)/shard_map/cond/branch_1_fun/ppermute | solution.py:543
  59.4 0.0 collective-permute-done.47
  59.4 0.1 collective-permute-start.48
  59.5 1.9 %collective-permute-done.40 = f32[152,128]{1,0:T(8,128)S(1)} collective-permute-done((f32[152,128]{1,0:T(8,128)S(1)}, f32[152,128]{1,0:T(8,128)S(1)}, u32[]{:S(2)}, u32[]{:S(2)}) %collective-permute-start.40) | collective-permute-done | bytes 77856 | tf_op jit(solution)/shard_map/cond/branch_1_fun/ppermute | solution.py:543
  61.4 0.1 collective-permute-start.41
  61.4 3.3 %collective-permute-done.48 = f32[304,128]{1,0:T(8,128)S(1)} collective-permute-done((f32[304,128]{1,0:T(8,128)S(1)}, f32[304,128]{1,0:T(8,128)S(1)}, u32[]{:S(2)}, u32[]{:S(2)}) %collective-permute-start.48) | collective-permute-done | bytes 155680 | tf_op jit(solution)/shard_map/cond/branch_1_fun/ppermute | solution.py:543
  64.8 4.0 %collective-permute-start.49 = (f32[608,128]{1,0:T(8,128)S(1)}, f32[608,128]{1,0:T(8,128)S(1)}, u32[]{:S(2)}, u32[]{:S(2)}) collective-permute-start(f32[608,128]{1,0:T(8,128)S(1)} %pad_maximum_fusion.12.mine_ref), channel_id=1, source_target_pairs={{0,1},{1,0},{2,3},{3,2},{4,5},{5,4},{6,7},{7,6},{8,9},{9,8},{10,11... | collective-permute-start | bytes 933896 | tf_op jit(solution)/shard_map/cond/branch_1_fun/ppermute | solution.py:543
  68.8 0.0 collective-permute-done.41
  68.9 1.9 %collective-permute-start.42 = (f32[608,128]{1,0:T(8,128)S(1)}, f32[608,128]{1,0:T(8,128)S(1)}, u32[]{:S(2)}, u32[]{:S(2)}) collective-permute-start(f32[608,128]{1,0:T(8,128)S(1)} %pad_maximum_fusion.11.mine_ref), channel_id=1, source_target_pairs={{0,1},{1,0},{2,3},{3,2},{4,5},{5,4},{6,7},{7,6},{8,9},{9,8},{10,11... | collective-permute-start | bytes 933896 | tf_op jit(solution)/shard_map/cond/branch_1_fun/ppermute | solution.py:543
  70.8 0.0 collective-permute-done.49.other_ref
  70.8 2.5 %update.3 = (f32[1000,768]{1,0:T(8,128)}, f32[1000,256]{1,0:T(8,128)}, bf16[256,768]{1,0:T(8,128)(2,1)S(1)}, bf16[256,768]{1,0:T(8,128)(2,1)S(1)}) custom-call(f32[608,128]{1,0:T(8,128)S(1)} %pad_maximum_fusion.12.mine_ref, f32[608,128]{1,0:T(8,128)S(1)} %collective-permute-done.49.other_ref, f32[1000,256]{1,0:T(8,128)S(1)} %copy-done.4, ...), custom_call_target="tpu_custom_call" | custom-call | flops 717225984 | bytes 3670016 | tf_op jit(solution)/shard_map/cond/branch_1_fun/update/pallas_call | solution.py:481
  73.2 0.0 collective-permute-done.42.other_ref
  73.2 2.0 %update_more.3 = (f32[1000,768]{1,0:T(8,128)}, f32[1000,256]{1,0:T(8,128)}) custom-call(f32[608,128]{1,0:T(8,128)S(1)} %pad_maximum_fusion.11.mine_ref, f32[608,128]{1,0:T(8,128)S(1)} %collective-permute-done.42.other_ref, f32[1000,256]{1,0:T(8,128)S(1)} %copy-done.4, f32[1000,768]{1,0:T(8,128)S(1)} %copy-done.2, ...), custom_call_target="tpu_custom_call", output_to_operand_aliasing={{0}: (6, {}), {1}: (7, {})} | custom-call | flops 651165696 | bytes 4521984 | tf_op jit(solution)/shard_map/cond/branch_1_fun/update_more/pallas_call | solution.py:519
  (31 shorter events, 0.4 us)
Async XLA Ops:
  4.7 5.4 %copy-start.8 = (s32[1,256]{1,0:T(1,128)S(1)}, s32[1,256]{1,0:T(1,128)}, u32[]{:S(2)}) copy-start(s32[1,256]{1,0:T(1,128)} %get-tuple-element.62.index_hbm.index_ref) | copy-start | bytes 3076 | tf_op jit(solution)/shard_map/cond
  4.8 5.7 %copy-start.10 = (s32[320]{0:T(512)S(1)}, s32[320]{0:T(512)}, u32[]{:S(2)}) copy-start(s32[320]{0:T(512)} %get-tuple-element.64) | copy-start | bytes 3844 | tf_op jit(solution)/shard_map/cond
  4.8 5.7 %copy-start = (bf16[768,3072]{1,0:T(8,128)(2,1)S(1)}, bf16[768,3072]{1,0:T(8,128)(2,1)}, u32[]{:S(2)}) copy-start(bf16[768,3072]{1,0:T(8,128)(2,1)} %get-tuple-element.63.centers_hbm.centers_ref) | copy-start | bytes 14155780 | tf_op jit(solution)/shard_map/cond
  4.8 8.6 %collective-permute-start.32 = (bf16[32,1536]{1,0:T(8,128)(2,1)S(1)}, bf16[32,1536]{1,0:T(8,128)(2,1)S(1)}, u32[]{:S(2)}, u32[]{:S(2)}) collective-permute-start(bf16[32,1536]{1,0:T(8,128)(2,1)S(1)} %pack_rows.3), channel_id=1, source_target_pairs={{0,8},{1,9},{2,10},{3,11},{4,12},{5,13},{6,14},{7,15},{8,0},{9,1},... | collective-permute-start | bytes 294920 | tf_op jit(solution)/shard_map/cond/branch_1_fun/ppermute | solution.py:543
  9.9 1.9 %copy-start.2 = (f32[1000,768]{1,0:T(8,128)S(1)}, f32[1000,768]{1,0:T(8,128)}, u32[]{:S(2)}) copy-start(f32[1000,768]{1,0:T(8,128)} %get-tuple-element.66.weights_ref) | copy-start | bytes 9216004 | tf_op jit(solution)/shard_map/cond
  9.9 1.9 %copy-start.6 = (f32[160,320]{1,0:T(8,128)S(1)}, f32[160,320]{1,0:T(8,128)}, u32[]{:S(2)}) copy-start(f32[160,320]{1,0:T(8,128)} %get-tuple-element.65.eigvec_ref) | copy-start | bytes 614404 | tf_op jit(solution)/shard_map/cond
  9.9 4.8 %collective-permute-start.28 = (bf16[32,1536]{1,0:T(8,128)(2,1)S(1)}, bf16[32,1536]{1,0:T(8,128)(2,1)S(1)}, u32[]{:S(2)}, u32[]{:S(2)}) collective-permute-start(bf16[32,1536]{1,0:T(8,128)(2,1)S(1)} %pack_rows.2), channel_id=1, source_target_pairs={{0,8},{1,9},{2,10},{3,11},{4,12},{5,13},{6,14},{7,15},{8,0},{9,1},... | collective-permute-start | bytes 294920 | tf_op jit(solution)/shard_map/cond/branch_1_fun/ppermute | solution.py:543
  13.4 4.9 %collective-permute-start.33 = (bf16[64,1536]{1,0:T(8,128)(2,1)S(1)}, bf16[64,1536]{1,0:T(8,128)(2,1)S(1)}, u32[]{:S(2)}, u32[]{:S(2)}) collective-permute-start(bf16[64,1536]{1,0:T(8,128)(2,1)S(1)} %pad_maximum_fusion.14), channel_id=1, source_target_pairs={{0,4},{1,3},{2,6},{3,1},{4,0},{5,7},{6,2},{7,5},{8,12},{9,11},{10,... | collective-permute-start | bytes 589832 | tf_op jit(solution)/shard_map/cond/branch_1_fun/ppermute | solution.py:543
  14.7 6.1 %collective-permute-start.29 = (bf16[64,1536]{1,0:T(8,128)(2,1)S(1)}, bf16[64,1536]{1,0:T(8,128)(2,1)S(1)}, u32[]{:S(2)}, u32[]{:S(2)}) collective-permute-start(bf16[64,1536]{1,0:T(8,128)(2,1)S(1)} %pad_maximum_fusion.13), channel_id=1, source_target_pairs={{0,4},{1,3},{2,6},{3,1},{4,0},{5,7},{6,2},{7,5},{8,12},{9,11},{10,... | collective-permute-start | bytes 589832 | tf_op jit(solution)/shard_map/cond/branch_1_fun/ppermute | solution.py:543
  18.3 9.5 %collective-permute-start.34 = (bf16[128,1536]{1,0:T(8,128)(2,1)S(1)}, bf16[128,1536]{1,0:T(8,128)(2,1)S(1)}, u32[]{:S(2)}, u32[]{:S(2)}) collective-permute-start(bf16[128,1536]{1,0:T(8,128)(2,1)S(1)} %pad_maximum_fusion.10), channel_id=1, source_target_pairs={{0,2},{1,5},{2,0},{3,7},{4,6},{5,1},{6,4},{7,3},{8,10},{9,13},{10,... | collective-permute-start | bytes 1179656 | tf_op jit(solution)/shard_map/cond/branch_1_fun/ppermute | solution.py:543
  20.9 11.1 %collective-permute-start.30 = (bf16[128,1536]{1,0:T(8,128)(2,1)S(1)}, bf16[128,1536]{1,0:T(8,128)(2,1)S(1)}, u32[]{:S(2)}, u32[]{:S(2)}) collective-permute-start(bf16[128,1536]{1,0:T(8,128)(2,1)S(1)} %pad_maximum_fusion.9), channel_id=1, source_target_pairs={{0,2},{1,5},{2,0},{3,7},{4,6},{5,1},{6,4},{7,3},{8,10},{9,13},{10,... | collective-permute-start | bytes 1179656 | tf_op jit(solution)/shard_map/cond/branch_1_fun/ppermute | solution.py:543
  27.8 5.6 %collective-permute-start.35 = (bf16[256,1536]{1,0:T(8,128)(2,1)S(1)}, bf16[256,1536]{1,0:T(8,128)(2,1)S(1)}, u32[]{:S(2)}, u32[]{:S(2)}) collective-permute-start(bf16[256,1536]{1,0:T(8,128)(2,1)S(1)} %pad_maximum_fusion.8.mine_ref), channel_id=1, source_target_pairs={{0,1},{1,0},{2,3},{3,2},{4,5},{5,4},{6,7},{7,6},{8,9},{9,8},{10,11... | collective-permute-start | bytes 2359304 | tf_op jit(solution)/shard_map/cond/branch_1_fun/ppermute | solution.py:543
  32.0 3.3 %collective-permute-start.31 = (bf16[256,1536]{1,0:T(8,128)(2,1)S(1)}, bf16[256,1536]{1,0:T(8,128)(2,1)S(1)}, u32[]{:S(2)}, u32[]{:S(2)}) collective-permute-start(bf16[256,1536]{1,0:T(8,128)(2,1)S(1)} %constant_dynamic-update-slice_fusion.mine_ref), channel_id=1, source_target_pairs={{0,1},{1,0},{2,3},{3,2},{4,5},{5,4},{6,7},{7,6},{8,9},{9,8},{10,11... | collective-permute-start | bytes 2359304 | tf_op jit(solution)/shard_map/cond/branch_1_fun/ppermute | solution.py:543
  38.7 1.7 %collective-permute-start.43 = (f32[608,128]{1,0:T(8,128)S(1)}, f32[608,128]{1,0:T(8,128)S(1)}, u32[]{:S(2)}, u32[]{:S(2)}) collective-permute-start(f32[608,128]{1,0:T(8,128)S(1)} %get-tuple-element.85), channel_id=1, source_target_pairs={{0,1},{1,0},{2,3},{3,2},{4,5},{5,4},{6,7},{7,6},{8,9},{9,8},{10,11... | collective-permute-start | bytes 933896 | tf_op jit(solution)/shard_map/cond/branch_1_fun/ppermute | solution.py:543
  40.1 1.7 %collective-permute-start.36 = (f32[608,128]{1,0:T(8,128)S(1)}, f32[608,128]{1,0:T(8,128)S(1)}, u32[]{:S(2)}, u32[]{:S(2)}) collective-permute-start(f32[608,128]{1,0:T(8,128)S(1)} %get-tuple-element.82), channel_id=1, source_target_pairs={{0,1},{1,0},{2,3},{3,2},{4,5},{5,4},{6,7},{7,6},{8,9},{9,8},{10,11... | collective-permute-start | bytes 933896 | tf_op jit(solution)/shard_map/cond/branch_1_fun/ppermute | solution.py:543
  40.4 30.4 %copy-start.4 = (f32[1000,256]{1,0:T(8,128)S(1)}, f32[1000,256]{1,0:T(8,128)}, u32[]{:S(2)}) copy-start(f32[1000,256]{1,0:T(8,128)} %get-tuple-element.83.targets_ref) | copy-start | bytes 3072004 | tf_op jit(solution)/shard_map/cond
  40.4 30.4 %copy-start.12 = (f32[1,160]{1,0:T(1,128)S(1)}, f32[1,160]{1,0:T(1,128)}, u32[]{:S(2)}) copy-start(f32[1,160]{1,0:T(1,128)} %get-tuple-element.86.eigval_ref) | copy-start | bytes 1924 | tf_op jit(solution)/shard_map/cond
  40.4 4.4 %collective-permute-start.44 = (f32[304,128]{1,0:T(8,128)S(1)}, f32[304,128]{1,0:T(8,128)S(1)}, u32[]{:S(2)}, u32[]{:S(2)}) collective-permute-start(f32[304,128]{1,0:T(8,128)S(1)} %slice.96), channel_id=1, source_target_pairs={{0,2},{1,5},{2,0},{3,7},{4,6},{5,1},{6,4},{7,3},{8,10},{9,13},{10,... | collective-permute-start | bytes 466952 | tf_op jit(solution)/shard_map/cond/branch_1_fun/ppermute | solution.py:543
  41.8 4.7 %collective-permute-start.37 = (f32[304,128]{1,0:T(8,128)S(1)}, f32[304,128]{1,0:T(8,128)S(1)}, u32[]{:S(2)}, u32[]{:S(2)}) collective-permute-start(f32[304,128]{1,0:T(8,128)S(1)} %slice.92), channel_id=1, source_target_pairs={{0,2},{1,5},{2,0},{3,7},{4,6},{5,1},{6,4},{7,3},{8,10},{9,13},{10,... | collective-permute-start | bytes 466952 | tf_op jit(solution)/shard_map/cond/branch_1_fun/ppermute | solution.py:543
  44.9 3.3 %collective-permute-start.45 = (f32[152,128]{1,0:T(8,128)S(1)}, f32[152,128]{1,0:T(8,128)S(1)}, u32[]{:S(2)}, u32[]{:S(2)}) collective-permute-start(f32[152,128]{1,0:T(8,128)S(1)} %slice.98), channel_id=1, source_target_pairs={{0,4},{1,3},{2,6},{3,1},{4,0},{5,7},{6,2},{7,5},{8,12},{9,11},{10,... | collective-permute-start | bytes 233480 | tf_op jit(solution)/shard_map/cond/branch_1_fun/ppermute | solution.py:543
  46.6 4.4 %collective-permute-start.38 = (f32[152,128]{1,0:T(8,128)S(1)}, f32[152,128]{1,0:T(8,128)S(1)}, u32[]{:S(2)}, u32[]{:S(2)}) collective-permute-start(f32[152,128]{1,0:T(8,128)S(1)} %slice.94), channel_id=1, source_target_pairs={{0,4},{1,3},{2,6},{3,1},{4,0},{5,7},{6,2},{7,5},{8,12},{9,11},{10,... | collective-permute-start | bytes 233480 | tf_op jit(solution)/shard_map/cond/branch_1_fun/ppermute | solution.py:543
  48.2 4.5 %collective-permute-start.46 = (f32[152,128]{1,0:T(8,128)S(1)}, f32[152,128]{1,0:T(8,128)S(1)}, u32[]{:S(2)}, u32[]{:S(2)}) collective-permute-start(f32[152,128]{1,0:T(8,128)S(1)} %slice_add_fusion.10), channel_id=1, source_target_pairs={{0,8},{1,9},{2,10},{3,11},{4,12},{5,13},{6,14},{7,15},{8,0},{9,1},... | collective-permute-start | bytes 233480 | tf_op jit(solution)/shard_map/cond/branch_1_fun/ppermute | solution.py:543
  51.0 7.0 %collective-permute-start.39 = (f32[152,128]{1,0:T(8,128)S(1)}, f32[152,128]{1,0:T(8,128)S(1)}, u32[]{:S(2)}, u32[]{:S(2)}) collective-permute-start(f32[152,128]{1,0:T(8,128)S(1)} %slice_add_fusion.11), channel_id=1, source_target_pairs={{0,8},{1,9},{2,10},{3,11},{4,12},{5,13},{6,14},{7,15},{8,0},{9,1},... | collective-permute-start | bytes 233480 | tf_op jit(solution)/shard_map/cond/branch_1_fun/ppermute | solution.py:543
  52.8 6.6 %collective-permute-start.47 = (f32[152,128]{1,0:T(8,128)S(1)}, f32[152,128]{1,0:T(8,128)S(1)}, u32[]{:S(2)}, u32[]{:S(2)}) collective-permute-start(f32[152,128]{1,0:T(8,128)S(1)} %add.135), channel_id=1, source_target_pairs={{0,4},{1,3},{2,6},{3,1},{4,0},{5,7},{6,2},{7,5},{8,12},{9,11},{10,... | collective-permute-start | bytes 233480 | tf_op jit(solution)/shard_map/cond/branch_1_fun/ppermute | solution.py:543
  58.0 3.3 %collective-permute-start.40 = (f32[152,128]{1,0:T(8,128)S(1)}, f32[152,128]{1,0:T(8,128)S(1)}, u32[]{:S(2)}, u32[]{:S(2)}) collective-permute-start(f32[152,128]{1,0:T(8,128)S(1)} %add.131), channel_id=1, source_target_pairs={{0,4},{1,3},{2,6},{3,1},{4,0},{5,7},{6,2},{7,5},{8,12},{9,11},{10,... | collective-permute-start | bytes 233480 | tf_op jit(solution)/shard_map/cond/branch_1_fun/ppermute | solution.py:543
  59.4 5.4 %collective-permute-start.48 = (f32[304,128]{1,0:T(8,128)S(1)}, f32[304,128]{1,0:T(8,128)S(1)}, u32[]{:S(2)}, u32[]{:S(2)}) collective-permute-start(f32[304,128]{1,0:T(8,128)S(1)} %pad_maximum_fusion.16), channel_id=1, source_target_pairs={{0,2},{1,5},{2,0},{3,7},{4,6},{5,1},{6,4},{7,3},{8,10},{9,13},{10,... | collective-permute-start | bytes 466952 | tf_op jit(solution)/shard_map/cond/branch_1_fun/ppermute | solution.py:543
  61.4 7.5 %collective-permute-start.41 = (f32[304,128]{1,0:T(8,128)S(1)}, f32[304,128]{1,0:T(8,128)S(1)}, u32[]{:S(2)}, u32[]{:S(2)}) collective-permute-start(f32[304,128]{1,0:T(8,128)S(1)} %pad_maximum_fusion.15), channel_id=1, source_target_pairs={{0,2},{1,5},{2,0},{3,7},{4,6},{5,1},{6,4},{7,3},{8,10},{9,13},{10,... | collective-permute-start | bytes 466952 | tf_op jit(solution)/shard_map/cond/branch_1_fun/ppermute | solution.py:543
  64.8 6.0 %collective-permute-start.49 = (f32[608,128]{1,0:T(8,128)S(1)}, f32[608,128]{1,0:T(8,128)S(1)}, u32[]{:S(2)}, u32[]{:S(2)}) collective-permute-start(f32[608,128]{1,0:T(8,128)S(1)} %pad_maximum_fusion.12.mine_ref), channel_id=1, source_target_pairs={{0,1},{1,0},{2,3},{3,2},{4,5},{5,4},{6,7},{7,6},{8,9},{9,8},{10,11... | collective-permute-start | bytes 933896 | tf_op jit(solution)/shard_map/cond/branch_1_fun/ppermute | solution.py:543
  68.9 4.4 %collective-permute-start.42 = (f32[608,128]{1,0:T(8,128)S(1)}, f32[608,128]{1,0:T(8,128)S(1)}, u32[]{:S(2)}, u32[]{:S(2)}) collective-permute-start(f32[608,128]{1,0:T(8,128)S(1)} %pad_maximum_fusion.11.mine_ref), channel_id=1, source_target_pairs={{0,1},{1,0},{2,3},{3,2},{4,5},{5,4},{6,7},{7,6},{8,9},{9,8},{10,11... | collective-permute-start | bytes 933896 | tf_op jit(solution)/shard_map/cond/branch_1_fun/ppermute | solution.py:543

commit v13 on v12

--- a/solution.py
+++ b/solution.py
@@ -16,6 +16,7 @@
 LANE = 128
 PARTS = 2
 SLOTS = 32
+BLOCKS = 2
 NT = (((1,), (1,)), ((), ()))
 NN = (((1,), (0,)), ((), ()))
 VMEM_LIMIT = 24 * 1024 * 1024
@@ -231,7 +232,7 @@
 
 def spread_body(
     first, classes, index_ref, eigvec_ref, weights_ref,
-    high1_ref, low1_ref, high2_ref, low2_ref, spread_ref, all_ref,
+    left1_ref, left2_ref, spread_ref, all_ref,
 ):
     rank, points = eigvec_ref.shape
     count = weights_ref.shape[1]
@@ -248,8 +249,13 @@
     all_ref[:rank] = spread
     all_ref[rank : rank + classes] = weights_ref[...]
     all_ref[rank + classes :] = jnp.zeros((all_ref.shape[0] - rank - classes, count), F32)
-    for begin, high_ref, low_ref in ((0, high1_ref, low1_ref), (first, high2_ref, low2_ref)):
-        high_ref[...], low_ref[...] = two(all_ref[begin : begin + high_ref.shape[0]])
+    size = count // BLOCKS
+    for begin, left_ref in ((0, left1_ref), (first, left2_ref)):
+        for block in range(BLOCKS):
+            high, low = two(all_ref[begin : begin + left_ref.shape[0], block * size : (block + 1) * size])
+            for k, term in enumerate((high, high, low)):
+                at = (3 * block + k) * size
+                left_ref[:, at : at + size] = term
 
 
 def spread_weights(nys_index, eigvec, weights, first, second):
@@ -258,10 +264,8 @@
     return pl.pallas_call(
         functools.partial(spread_body, first, classes),
         out_shape=[
-            jax.ShapeDtypeStruct((first, count), BF16),
-            jax.ShapeDtypeStruct((first, count), BF16),
-            jax.ShapeDtypeStruct((second, count), BF16),
-            jax.ShapeDtypeStruct((second, count), BF16),
+            jax.ShapeDtypeStruct((first, 3 * count), BF16),
+            jax.ShapeDtypeStruct((second, 3 * count), BF16),
             jax.ShapeDtypeStruct((rank, count), F32),
         ],
         scratch_shapes=[pltpu.VMEM((first + second, count), F32)],
@@ -294,24 +298,20 @@
     )(centers)
 
 
-def gather_batch(mine_ref, other_ref, select_ref, batch_ref):
-    half = mine_ref.shape[0]
-    found = dot(select_ref[:, :half], mine_ref[...], NN) + dot(select_ref[:, half:], other_ref[...], NN)
-    batch_ref[...] = found.astype(BF16)
-
-
-def nearer(first, centers_ref, batch_ref):
-    rows, depth = batch_ref.shape
+def row_norms(batch_ref):
+    rows = batch_ref.shape[0]
     batch = batch_ref[...].astype(F32)
-    norm = jnp.sum(batch * batch, axis=1, keepdims=True)
-    cross = dot(centers_ref[:, first : first + depth], batch_ref[...], NT)
-    return jnp.broadcast_to(norm, (rows, LANE)).T[0:1] - 2.0 * cross
-
-
-def product(high_ref, low_ref, value_high, value_low, total_ref, keep_ref, send_ref):
+    return jnp.broadcast_to(jnp.sum(batch * batch, axis=1, keepdims=True), (rows, LANE)).T[0:1]
+
+
+def product(left_ref, right_ref, total_ref, keep_ref, send_ref):
     half = keep_ref.shape[1]
-    high = high_ref[...]
-    total_ref[...] = dot(high, value_high, NN) + (dot(high, value_low, NN) + dot(low_ref[...], value_high, NN))
+    size = left_ref.shape[1] // BLOCKS
+    total = 0.0
+    for block in range(BLOCKS):
+        at = slice(block * size, (block + 1) * size)
+        total = total + dot(left_ref[:, at], right_ref[at], NN)
+    total_ref[...] = total
     lower = lax.axis_index("sub") == 0
     size = keep_ref.shape[0] // CHUNKS
     for chunk in range(CHUNKS):
@@ -324,57 +324,67 @@
         send_ref[at] = jnp.where(lower, second, first)
 
 
-def distance_body(mine_ref, other_ref, select_ref, centers_ref, norm_ref, total_ref, batch_ref):
-    gather_batch(mine_ref, other_ref, select_ref, batch_ref)
-    total_ref[...] = norm_ref[:, 0:1] + nearer(0, centers_ref, batch_ref)
+def distance_body(mine_ref, other_ref, next_ref, select_ref, centers_ref, norm_ref, total_ref, found_ref, batch_ref):
+    half, depth = mine_ref.shape
+    near = select_ref[:, :half]
+    batch_ref[...] = (dot(near, mine_ref[...], NN) + dot(select_ref[:, half:], other_ref[...], NN)).astype(BF16)
+    total_ref[...] = norm_ref[:, 0:1] + row_norms(batch_ref) - 2.0 * dot(centers_ref[:, :depth], batch_ref[...], NT)
+    found_ref[...] = dot(near, next_ref[...], NN).astype(BF16)
 
 
 def predict_body(
-    mine_ref, other_ref, select_ref, centers_ref, before_ref, high_ref, low_ref,
-    keep_ref, send_ref, value_high_ref, value_low_ref, batch_ref, total_ref,
+    found_ref, other_ref, select_ref, centers_ref, before_ref, left_ref,
+    keep_ref, send_ref, right_ref, batch_ref, total_ref,
 ):
-    depth = centers_ref.shape[1]
-    gather_batch(mine_ref, other_ref, select_ref, batch_ref)
-    square = jnp.maximum(before_ref[...] + nearer(depth - batch_ref.shape[1], centers_ref, batch_ref), 0.0)
-    value_high, value_low = two(jnp.exp(jnp.sqrt(square) * (-1.0 / math.sqrt(depth))))
-    value_high_ref[...] = value_high
-    value_low_ref[...] = value_low
-    product(high_ref, low_ref, value_high, value_low, total_ref, keep_ref, send_ref)
-
-
-def distances(mine, other, select, centers, norms):
+    count, depth = centers_ref.shape
+    half, part = other_ref.shape
+    found = found_ref[...].astype(F32) + dot(select_ref[:, half:], other_ref[...], NN)
+    batch_ref[...] = found.astype(BF16)
+    norm = row_norms(batch_ref)
+    size = count // BLOCKS
+    for block in range(BLOCKS):
+        at = slice(block * size, (block + 1) * size)
+        cross = dot(centers_ref[at, depth - part :], batch_ref[...], NT)
+        square = jnp.maximum(before_ref[at] + norm - 2.0 * cross, 0.0)
+        high, low = two(jnp.exp(jnp.sqrt(square) * (-1.0 / math.sqrt(depth))))
+        for k, term in enumerate((high, low, high)):
+            to = (3 * block + k) * size
+            right_ref[to : to + size] = term
+    product(left_ref, right_ref, total_ref, keep_ref, send_ref)
+
+
+def distances(mine, other, following, select, centers, norms):
     depth = mine.shape[1]
     rows = select.shape[0]
     count = centers.shape[0]
     vmem = pl.BlockSpec(memory_space=pltpu.VMEM)
     return pl.pallas_call(
         distance_body,
-        in_specs=[vmem] * 5,
-        out_specs=vmem,
-        out_shape=jax.ShapeDtypeStruct((count, rows), F32),
+        in_specs=[vmem] * 6,
+        out_specs=[vmem, vmem],
+        out_shape=[jax.ShapeDtypeStruct((count, rows), F32), jax.ShapeDtypeStruct((rows, depth), BF16)],
         scratch_shapes=[pltpu.VMEM((rows, depth), BF16)],
         compiler_params=params(),
         cost_estimate=pl.CostEstimate(
             flops=2 * rows * count * depth, bytes_accessed=2 * depth * (count + rows), transcendentals=0
         ),
         name="distances",
-    )(mine, other, select, centers, norms)
-
-
-def predict(mine, other, select, centers, before, high, low):
-    depth = mine.shape[1]
+    )(mine, other, following, select, centers, norms)
+
+
+def predict(found, other, select, centers, before, left):
+    depth = found.shape[1]
     rows = select.shape[0]
     half = rows // 2
     count = centers.shape[0]
-    padded = high.shape[0]
+    padded = left.shape[0]
     out = jax.ShapeDtypeStruct((padded, half), F32)
-    value = jax.ShapeDtypeStruct((count, rows), BF16)
     vmem = pl.BlockSpec(memory_space=pltpu.VMEM)
     return pl.pallas_call(
         predict_body,
-        in_specs=[vmem] * 7,
-        out_specs=[vmem] * 4,
-        out_shape=[out, out, value, value],
+        in_specs=[vmem] * 6,
+        out_specs=[vmem] * 3,
+        out_shape=[out, out, jax.ShapeDtypeStruct((3 * count, rows), BF16)],
         scratch_shapes=[pltpu.VMEM((rows, depth), BF16), pltpu.VMEM((padded, rows), F32)],
         compiler_params=params(),
         cost_estimate=pl.CostEstimate(
@@ -383,27 +393,23 @@
             transcendentals=2 * rows * count,
         ),
         name="predict",
-    )(mine, other, select, centers, before, high, low)
-
-
-def more_body(high_ref, low_ref, value_high_ref, value_low_ref, keep_ref, send_ref, total_ref):
-    product(high_ref, low_ref, value_high_ref[...], value_low_ref[...], total_ref, keep_ref, send_ref)
-
-
-def predict_more(high, low, value_high, value_low):
-    padded = high.shape[0]
-    count, rows = value_high.shape
+    )(found, other, select, centers, before, left)
+
+
+def predict_more(left, right):
+    padded, count = left.shape
+    rows = right.shape[1]
     out = jax.ShapeDtypeStruct((padded, rows // 2), F32)
     return pl.pallas_call(
-        more_body,
+        lambda left, right, keep, send, total: product(left, right, total, keep, send),
         out_shape=[out, out],
         scratch_shapes=[pltpu.VMEM((padded, rows), F32)],
         compiler_params=params(),
         cost_estimate=pl.CostEstimate(
-            flops=int(1.0 * 6) * rows * count * padded, bytes_accessed=4 * padded * (count + rows), transcendentals=0
+            flops=2 * rows * count * padded, bytes_accessed=2 * padded * (count + rows), transcendentals=0
         ),
         name="predict_more",
-    )(high, low, value_high, value_low)
+    )(left, right)
 
 
 def gather_total(mine_ref, other_ref, total_ref):
@@ -420,12 +426,11 @@
             )
 
 
-def write_rows(begin, skip, total_ref, targets_ref, weights_ref, high_ref, low_ref, new_hbm, out_hbm, new_ref, sems):
+def write_rows(begin, skip, total_ref, targets_ref, weights_ref, right_ref, new_hbm, out_hbm, new_ref, sems):
     rows = new_ref.shape[0]
     blocks = sems.shape[0] - 1
     bounds = [8 * (rows // 8 * k // blocks) for k in range(blocks)] + [rows]
-    high_right = high_ref[...]
-    low_right = low_ref[...]
+    right = right_ref[...]
     copies = [
         pltpu.make_async_copy(
             total_ref.at[pl.ds(skip, rows)], out_hbm.at[pl.ds(begin, rows)], sems.at[blocks]
@@ -436,9 +441,7 @@
         low_end, high_end = bounds[k : k + 2]
         here = slice(begin + low_end, begin + high_end)
         high, low = two(total_ref[skip + low_end : skip + high_end] - targets_ref[here])
-        new_ref[low_end:high_end] = weights_ref[here] + (
-            dot(high, high_right, NN) + (dot(high, low_right, NN) + dot(low, high_right, NN))
-        )
+        new_ref[low_end:high_end] = weights_ref[here] + dot(jnp.concatenate([high, high, low], axis=1), right, NN)
         copy = pltpu.make_async_copy(
             new_ref.at[pl.ds(low_end, high_end - low_end)],
             new_hbm.at[pl.ds(begin + low_end, high_end - low_end)],
@@ -452,7 +455,7 @@
 
 def update_body(
     mine_ref, other_ref, targets_ref, index_ref, eigval_ref, spread_ref, weights_ref,
-    new_hbm, out_hbm, high_ref, low_ref, total_ref, new_ref, sems,
+    new_hbm, out_hbm, right_ref, total_ref, new_ref, sems,
 ):
     start = (lax.axis_index("center") * 2 + lax.axis_index("sub")) * spread_ref.shape[1]
     rank, count = spread_ref.shape
@@ -465,8 +468,10 @@
     turned = dot(mixed_high, spread_high, NN) + (
         dot(mixed_high, spread_low, NN) + dot(mixed_low, spread_high, NN)
     )
-    high_ref[...], low_ref[...] = two(turned - pick_rows(index_ref, count, start, F32, 0.25))
-    write_rows(0, rank, total_ref, targets_ref, weights_ref, high_ref, low_ref, new_hbm, out_hbm, new_ref, sems)
+    high, low = two(turned - pick_rows(index_ref, count, start, F32, 0.25))
+    for k, term in enumerate((high, low, high)):
+        right_ref[k * term.shape[0] : (k + 1) * term.shape[0]] = term
+    write_rows(0, rank, total_ref, targets_ref, weights_ref, right_ref, new_hbm, out_hbm, new_ref, sems)
 
 
 def update(mine, other, targets, batch_index, eigval, spread, weights):
@@ -477,16 +482,14 @@
     here = padded - rank
     vmem = pl.BlockSpec(memory_space=pltpu.VMEM)
     hbm = pl.BlockSpec(memory_space=pl.ANY)
-    right = jax.ShapeDtypeStruct((rows, count), BF16)
     return pl.pallas_call(
         update_body,
         in_specs=[vmem] * 7,
-        out_specs=[hbm, hbm, vmem, vmem],
+        out_specs=[hbm, hbm, vmem],
         out_shape=[
             jax.ShapeDtypeStruct((classes, count), F32),
             jax.ShapeDtypeStruct((classes, rows), F32),
-            right,
-            right,
+            jax.ShapeDtypeStruct((3 * rows, count), BF16),
         ],
         scratch_shapes=[
             pltpu.VMEM((padded, rows), F32),
@@ -502,14 +505,14 @@
 
 
 def update_more_body(
-    begin, mine_ref, other_ref, targets_ref, weights_ref, high_ref, low_ref, new_in, out_in,
+    begin, mine_ref, other_ref, targets_ref, weights_ref, right_ref, new_in, out_in,
     new_hbm, out_hbm, total_ref, new_ref, sems,
 ):
     gather_total(mine_ref, other_ref, total_ref)
-    write_rows(begin, 0, total_ref, targets_ref, weights_ref, high_ref, low_ref, new_hbm, out_hbm, new_ref, sems)
-
-
-def update_more(mine, other, targets, weights, high, low, new, out, begin):
+    write_rows(begin, 0, total_ref, targets_ref, weights_ref, right_ref, new_hbm, out_hbm, new_ref, sems)
+
+
+def update_more(mine, other, targets, weights, right, new, out, begin):
     classes, count = weights.shape
     padded, half = mine.shape
     rows = 2 * half
@@ -518,13 +521,13 @@
     hbm = pl.BlockSpec(memory_space=pl.ANY)
     return pl.pallas_call(
         functools.partial(update_more_body, begin),
-        in_specs=[vmem] * 6 + [hbm] * 2,
+        in_specs=[vmem] * 5 + [hbm] * 2,
         out_specs=[hbm, hbm],
         out_shape=[
             jax.ShapeDtypeStruct((classes, count), F32),
             jax.ShapeDtypeStruct((classes, rows), F32),
         ],
-        input_output_aliases={6: 0, 7: 1},
+        input_output_aliases={5: 0, 6: 1},
         scratch_shapes=[
             pltpu.VMEM((padded, rows), F32),
             pltpu.VMEM((here, count), F32),
@@ -535,7 +538,7 @@
             flops=int(1.0 * 6) * rows * count * here, bytes_accessed=8 * here * (count + rows), transcendentals=0
         ),
         name="update_more",
-    )(mine, other, targets, weights, high, low, new, out)
+    )(mine, other, targets, weights, right, new, out)
 
 
 def swap(x, chips, order=None, level=0):
@@ -600,18 +603,18 @@
         ready.append(select_packed(batch_index, count, chips))
         slots = [pack_rows(*far, part) for part in range(PARTS)]
         mine, other = all_of(slots[0], chips)
-        *late, norms, high1, low1, high2, low2, spread, select = all_of(slots[1], chips, ready)
+        next_mine, next_other, norms, left1, left2, spread, select = all_of(slots[1], chips, ready)
     else:
         ready.append(select_summed(rows))
         picked = [pick_batch(*far, part) for part in range(PARTS)]
-        mine, other, norms, high1, low1, high2, low2, spread, select = total_of(*picked[0], chips, ready)
-        late = total_of(*picked[1], chips)
-    before = distances(mine, other, select, centers, norms)
-    keep, send, value_high, value_low = predict(*late, select, centers, before, high1, low1)
+        mine, other = total_of(*picked[0], chips)
+        next_mine, next_other, norms, left1, left2, spread, select = total_of(*picked[1], chips, ready)
+    before, found = distances(mine, other, next_mine, select, centers, norms)
+    keep, send, right = predict(found, next_other, select, centers, before, left1)
     one = total_of(keep, send, chips)
-    another = total_of(*predict_more(high2, low2, value_high, value_low), chips)
-    new, out, high, low = update(*one, targets, batch_index, eigval, spread, weights)
-    return update_more(*another, targets, weights, high, low, new, out, first - depth)
+    another = total_of(*predict_more(left2, right), chips)
+    new, out, right = update(*one, targets, batch_index, eigval, spread, weights)
+    return update_more(*another, targets, weights, right, new, out, first - depth)
 
 
 def on_device(chips, centers, weights, targets, batch_index, nys_index, eigvec, eigval):

time: 75.6 us -> 74.4 us (0.984)
  Pallas kernels: 18.3 us -> 17.4 us
  transfers between devices with their start and end apart: 22 -> 22, of which waited for: 13 -> 12; matrix products, arithmetic and copies ran while one was open for 1% -> 1% of each run, Pallas kernels for 13% -> 13%
where the time goes in v13:
time: 74.4 us; the launch traced here: 74.2 us
  starting transfers between devices  30.7 us (41%)
  waiting for transfers between devices  23.5 us (32%)
  Pallas kernels  17.4 us (23%)
  between operations  1.45 us (2%)
    ppermute x22, starting transfers between devices, swap(): lax.ppermute(x, AXES, [(i, i ^ flip[i & 1]) for i in range(2 * chips)])  30.7 us
    ppermute x22, waiting for transfers between devices, swap(): lax.ppermute(x, AXES, [(i, i ^ flip[i & 1]) for i in range(2 * chips)])  23.5 us
    pallas_call x2, Pallas kernels, pack_rows(): pl.pallas_call(functools.partial(pack_body, part * depth), in_specs=[hbm,...  3.83 us
    pallas_call x1, Pallas kernels, predict(): pl.pallas_call(predict_body, in_specs=[vmem] * 6, out_specs=[vmem] * 3, o...  2.39 us
    pallas_call x1, Pallas kernels, update(): pl.pallas_call(update_body, in_specs=[vmem] * 7, out_specs=[hbm, hbm, vme...  2.23 us
    pallas_call x1, Pallas kernels, update_more(): pl.pallas_call(functools.partial(update_more_body, begin), in_specs=[vmem...  1.96 us
    pallas_call x1, Pallas kernels, spread_weights(): pl.pallas_call(functools.partial(spread_body, first, classes), out_shape=...  1.69 us
  transfers between devices with their start and end apart: 22, of which 12 were waited for; matrix products, arithmetic and copies ran while one was open for 1% of the time, Pallas kernels for 13%

profile of v13, /device:TPU:1, one launch (start us, length us, event | category | flops | bytes accessed | tf_op | source)
XLA Modules:
  0.0 74.2 jit_solution(10208816885787070510)
XLA Ops:
  0.6 1.3 %rows_fit.1 = s32[1]{0:T(128)} custom-call(s32[1,256]{1,0:T(1,128)} %bitcast.17), custom_call_target="tpu_custom_call" | custom-call | tf_op jit(solution)/shard_map/rows_fit/pallas_call | solution.py:139
  2.6 71.4 %conditional.1 = ((f32[1000,768]{1,0:T(8,128)}, f32[1000,256]{1,0:T(8,128)})) conditional(s32[]{:T(128)} %bitcast.2, (s32[1,256]{1,0:T(1,128)}, bf16[768,3072]{1,0:T(8,128)(2,1)}, s32[320]{0:T(512)}, f32[160,320]{1,0:T(8,128)}, f32[1000,768]{1,0:T(8,128)}, /*index=5*/f32[1000,256]{1,0:T(8,128)}, f32[1,160]{1,0:T(1,128)}) %tuple.30, ...), branch_computations={%region_0.1_spmd, %region_1.2_spmd} | conditional | flops 5464187904 | bytes 106462272 | solution.py:622
  2.8 1.9 %pack_rows.3 = bf16[32,1536]{1,0:T(8,128)(2,1)S(1)} custom-call(s32[1,256]{1,0:T(1,128)} %get-tuple-element.58.index_hbm.index_ref, bf16[768,3072]{1,0:T(8,128)(2,1)} %get-tuple-element.59.centers_hbm.centers_ref), custom_call_target="tpu_custom_call" | custom-call | flops 75497472 | bytes 2457600 | tf_op jit(solution)/shard_map/cond/branch_1_fun/pack_rows/pallas_call | solution.py:181
  4.7 0.0 copy-start.8
  4.8 0.0 copy-start.10
  4.8 0.0 copy-start
  4.8 3.2 %collective-permute-start.29 = (bf16[32,1536]{1,0:T(8,128)(2,1)S(1)}, bf16[32,1536]{1,0:T(8,128)(2,1)S(1)}, u32[]{:S(2)}, u32[]{:S(2)}) collective-permute-start(bf16[32,1536]{1,0:T(8,128)(2,1)S(1)} %pack_rows.3), channel_id=1, source_target_pairs={{0,8},{1,9},{2,10},{3,11},{4,12},{5,13},{6,14},{7,15},{8,0},{9,1},... | collective-permute-start | bytes 294920 | tf_op jit(solution)/shard_map/cond/branch_1_fun/ppermute | solution.py:546
  8.0 1.9 %pack_rows.2 = bf16[32,1536]{1,0:T(8,128)(2,1)S(1)} custom-call(s32[1,256]{1,0:T(1,128)} %get-tuple-element.58.index_hbm.index_ref, bf16[768,3072]{1,0:T(8,128)(2,1)} %get-tuple-element.59.centers_hbm.centers_ref), custom_call_target="tpu_custom_call" | custom-call | flops 75497472 | bytes 2457600 | tf_op jit(solution)/shard_map/cond/branch_1_fun/pack_rows/pallas_call | solution.py:181
  9.9 0.0 copy-start.2
  9.9 0.0 copy-start.6
  9.9 0.2 collective-permute-start.28
  10.2 0.3 select_packed.1.select_ref
  10.5 1.2 %center_norms.3.norm_ref = f32[768,128]{1,0:T(8,128)S(1)} custom-call(bf16[768,3072]{1,0:T(8,128)(2,1)S(1)} %copy-done), custom_call_target="tpu_custom_call" | custom-call | flops 4718592 | bytes 4718592 | tf_op jit(solution)/shard_map/cond/branch_1_fun/center_norms/pallas_call | solution.py:289
  11.6 0.1 copy-done.2
  11.8 1.7 %spread_weights.3 = (bf16[608,2304]{1,0:T(8,128)(2,1)S(1)}, bf16[608,2304]{1,0:T(8,128)(2,1)S(1)}, f32[160,768]{1,0:T(8,128)S(1)}) custom-call(s32[1,320]{1,0:T(1,128)S(1)} %reshape.99.index_ref, f32[160,320]{1,0:T(8,128)S(1)} %copy-done.6, f32[1000,768]{1,0:T(8,128)S(1)} %copy-done.2), custom_call_target="tpu_custom_call" | custom-call | flops 235929600 | bytes 7471104 | tf_op jit(solution)/shard_map/cond/branch_1_fun/spread_weights/pallas_call | solution.py:264
  13.5 0.0 collective-permute-done.29
  13.5 1.3 %collective-permute-start.30 = (bf16[64,1536]{1,0:T(8,128)(2,1)S(1)}, bf16[64,1536]{1,0:T(8,128)(2,1)S(1)}, u32[]{:S(2)}, u32[]{:S(2)}) collective-permute-start(bf16[64,1536]{1,0:T(8,128)(2,1)S(1)} %pad_maximum_fusion.14), channel_id=1, source_target_pairs={{0,4},{1,3},{2,6},{3,1},{4,0},{5,7},{6,2},{7,5},{8,12},{9,11},{10,... | collective-permute-start | bytes 589832 | tf_op jit(solution)/shard_map/cond/branch_1_fun/ppermute | solution.py:546
  14.8 0.0 collective-permute-done.28
  14.8 0.9 %collective-permute-start.33 = (bf16[64,1536]{1,0:T(8,128)(2,1)S(1)}, bf16[64,1536]{1,0:T(8,128)(2,1)S(1)}, u32[]{:S(2)}, u32[]{:S(2)}) collective-permute-start(bf16[64,1536]{1,0:T(8,128)(2,1)S(1)} %pad_maximum_fusion.13), channel_id=1, source_target_pairs={{0,4},{1,3},{2,6},{3,1},{4,0},{5,7},{6,2},{7,5},{8,12},{9,11},{10,... | collective-permute-start | bytes 589832 | tf_op jit(solution)/shard_map/cond/branch_1_fun/ppermute | solution.py:546
  15.7 2.7 %collective-permute-done.30 = bf16[64,1536]{1,0:T(8,128)(2,1)S(1)} collective-permute-done((bf16[64,1536]{1,0:T(8,128)(2,1)S(1)}, bf16[64,1536]{1,0:T(8,128)(2,1)S(1)}, u32[]{:S(2)}, u32[]{:S(2)}) %collective-permute-start.30) | collective-permute-done | bytes 196640 | tf_op jit(solution)/shard_map/cond/branch_1_fun/ppermute | solution.py:546
  18.4 2.5 %collective-permute-start.31 = (bf16[128,1536]{1,0:T(8,128)(2,1)S(1)}, bf16[128,1536]{1,0:T(8,128)(2,1)S(1)}, u32[]{:S(2)}, u32[]{:S(2)}) collective-permute-start(bf16[128,1536]{1,0:T(8,128)(2,1)S(1)} %pad_maximum_fusion.9), channel_id=1, source_target_pairs={{0,2},{1,5},{2,0},{3,7},{4,6},{5,1},{6,4},{7,3},{8,10},{9,13},{10,... | collective-permute-start | bytes 1179656 | tf_op jit(solution)/shard_map/cond/branch_1_fun/ppermute | solution.py:546
  20.9 0.0 collective-permute-done.33
  20.9 2.1 %collective-permute-start.34 = (bf16[128,1536]{1,0:T(8,128)(2,1)S(1)}, bf16[128,1536]{1,0:T(8,128)(2,1)S(1)}, u32[]{:S(2)}, u32[]{:S(2)}) collective-permute-start(bf16[128,1536]{1,0:T(8,128)(2,1)S(1)} %pad_maximum_fusion.10), channel_id=1, source_target_pairs={{0,2},{1,5},{2,0},{3,7},{4,6},{5,1},{6,4},{7,3},{8,10},{9,13},{10,... | collective-permute-start | bytes 1179656 | tf_op jit(solution)/shard_map/cond/branch_1_fun/ppermute | solution.py:546
  23.0 4.8 %collective-permute-done.31 = bf16[128,1536]{1,0:T(8,128)(2,1)S(1)} collective-permute-done((bf16[128,1536]{1,0:T(8,128)(2,1)S(1)}, bf16[128,1536]{1,0:T(8,128)(2,1)S(1)}, u32[]{:S(2)}, u32[]{:S(2)}) %collective-permute-start.31) | collective-permute-done | bytes 393248 | tf_op jit(solution)/shard_map/cond/branch_1_fun/ppermute | solution.py:546
  27.8 0.1 pad_maximum_fusion.8.mine_ref
  27.8 0.6 collective-permute-start.32
  28.5 3.5 %collective-permute-done.34 = bf16[128,1536]{1,0:T(8,128)(2,1)S(1)} collective-permute-done((bf16[128,1536]{1,0:T(8,128)(2,1)S(1)}, bf16[128,1536]{1,0:T(8,128)(2,1)S(1)}, u32[]{:S(2)}, u32[]{:S(2)}) %collective-permute-start.34) | collective-permute-done | bytes 393248 | tf_op jit(solution)/shard_map/cond/branch_1_fun/ppermute | solution.py:546
  32.0 1.4 %collective-permute-start.35 = (bf16[256,1536]{1,0:T(8,128)(2,1)S(1)}, bf16[256,1536]{1,0:T(8,128)(2,1)S(1)}, u32[]{:S(2)}, u32[]{:S(2)}) collective-permute-start(bf16[256,1536]{1,0:T(8,128)(2,1)S(1)} %constant_dynamic-update-slice_fusion.next_ref), channel_id=1, source_target_pairs={{0,1},{1,0},{2,3},{3,2},{4,5},{5,4},{6,7},{7,6},{8,9},{9,8},{10,11... | collective-permute-start | bytes 2359304 | tf_op jit(solution)/shard_map/cond/branch_1_fun/ppermute | solution.py:546
  33.4 0.0 collective-permute-done.32.other_ref
  33.4 1.5 %distances.3 = (f32[768,256]{1,0:T(8,128)S(1)}, bf16[256,1536]{1,0:T(8,128)(2,1)S(1)}) custom-call(bf16[256,1536]{1,0:T(8,128)(2,1)S(1)} %pad_maximum_fusion.8.mine_ref, bf16[256,1536]{1,0:T(8,128)(2,1)S(1)} %collective-permute-done.32.other_ref, bf16[256,1536]{1,0:T(8,128)(2,1)S(1)} %constant_dynamic-update-slice_fusion.next_ref, ...), custom_call_target="tpu_custom_call" | custom-call | flops 603979776 | bytes 3145728 | tf_op jit(solution)/shard_map/cond/branch_1_fun/distances/pallas_call | solution.py:361
  34.9 0.4 collective-permute-done.35.other_ref
  35.3 2.4 %predict.3 = (f32[608,128]{1,0:T(8,128)S(1)}, f32[608,128]{1,0:T(8,128)S(1)}, bf16[2304,256]{1,0:T(8,128)(2,1)S(1)}) custom-call(bf16[256,1536]{1,0:T(8,128)(2,1)S(1)} %get-tuple-element.70.found_ref, bf16[256,1536]{1,0:T(8,128)(2,1)S(1)} %collective-permute-done.35.other_ref, bf16[256,512]{1,0:T(8,128)(2,1)S(1)} %select_packed.1.select_ref, ...), custom_call_target="tpu_custom_call" | custom-call | flops 1321205760 | bytes 5636096 | tf_op jit(solution)/shard_map/cond/branch_1_fun/predict/pallas_call | solution.py:383
  37.7 0.4 collective-permute-start.43
  38.2 1.0 %predict_more.3 = (f32[608,128]{1,0:T(8,128)S(1)}, f32[608,128]{1,0:T(8,128)S(1)}) custom-call(bf16[608,2304]{1,0:T(8,128)(2,1)S(1)} %get-tuple-element.66.left, bf16[2304,256]{1,0:T(8,128)(2,1)S(1)} %get-tuple-element.73.right), custom_call_target="tpu_custom_call" | custom-call | flops 717225984 | bytes 3112960 | tf_op jit(solution)/shard_map/cond/branch_1_fun/predict_more/pallas_call | solution.py:403
  39.2 0.2 collective-permute-start.36
  39.4 0.0 collective-permute-done.43
  39.4 0.0 copy-start.4
  39.5 0.0 copy-start.12
  39.5 1.1 %collective-permute-start.44 = (f32[304,128]{1,0:T(8,128)S(1)}, f32[304,128]{1,0:T(8,128)S(1)}, u32[]{:S(2)}, u32[]{:S(2)}) collective-permute-start(f32[304,128]{1,0:T(8,128)S(1)} %slice.96), channel_id=1, source_target_pairs={{0,2},{1,5},{2,0},{3,7},{4,6},{5,1},{6,4},{7,3},{8,10},{9,13},{10,... | collective-permute-start | bytes 466952 | tf_op jit(solution)/shard_map/cond/branch_1_fun/ppermute | solution.py:546
  40.6 0.3 collective-permute-done.36
  40.9 1.1 %collective-permute-start.37 = (f32[304,128]{1,0:T(8,128)S(1)}, f32[304,128]{1,0:T(8,128)S(1)}, u32[]{:S(2)}, u32[]{:S(2)}) collective-permute-start(f32[304,128]{1,0:T(8,128)S(1)} %slice.92), channel_id=1, source_target_pairs={{0,2},{1,5},{2,0},{3,7},{4,6},{5,1},{6,4},{7,3},{8,10},{9,13},{10,... | collective-permute-start | bytes 466952 | tf_op jit(solution)/shard_map/cond/branch_1_fun/ppermute | solution.py:546
  42.0 1.9 %collective-permute-done.44 = f32[304,128]{1,0:T(8,128)S(1)} collective-permute-done((f32[304,128]{1,0:T(8,128)S(1)}, f32[304,128]{1,0:T(8,128)S(1)}, u32[]{:S(2)}, u32[]{:S(2)}) %collective-permute-start.44) | collective-permute-done | bytes 155680 | tf_op jit(solution)/shard_map/cond/branch_1_fun/ppermute | solution.py:546
  44.0 1.3 %collective-permute-start.45 = (f32[152,128]{1,0:T(8,128)S(1)}, f32[152,128]{1,0:T(8,128)S(1)}, u32[]{:S(2)}, u32[]{:S(2)}) collective-permute-start(f32[152,128]{1,0:T(8,128)S(1)} %slice.98), channel_id=1, source_target_pairs={{0,4},{1,3},{2,6},{3,1},{4,0},{5,7},{6,2},{7,5},{8,12},{9,11},{10,... | collective-permute-start | bytes 233480 | tf_op jit(solution)/shard_map/cond/branch_1_fun/ppermute | solution.py:546
  45.3 0.3 collective-permute-done.37
  45.6 1.3 %collective-permute-start.38 = (f32[152,128]{1,0:T(8,128)S(1)}, f32[152,128]{1,0:T(8,128)S(1)}, u32[]{:S(2)}, u32[]{:S(2)}) collective-permute-start(f32[152,128]{1,0:T(8,128)S(1)} %slice.94), channel_id=1, source_target_pairs={{0,4},{1,3},{2,6},{3,1},{4,0},{5,7},{6,2},{7,5},{8,12},{9,11},{10,... | collective-permute-start | bytes 233480 | tf_op jit(solution)/shard_map/cond/branch_1_fun/ppermute | solution.py:546
  46.9 0.3 collective-permute-done.45
  47.3 2.7 %collective-permute-start.46 = (f32[152,128]{1,0:T(8,128)S(1)}, f32[152,128]{1,0:T(8,128)S(1)}, u32[]{:S(2)}, u32[]{:S(2)}) collective-permute-start(f32[152,128]{1,0:T(8,128)S(1)} %slice_add_fusion.10), channel_id=1, source_target_pairs={{0,8},{1,9},{2,10},{3,11},{4,12},{5,13},{6,14},{7,15},{8,0},{9,1},... | collective-permute-start | bytes 233480 | tf_op jit(solution)/shard_map/cond/branch_1_fun/ppermute | solution.py:546
  50.0 0.0 collective-permute-done.38
  50.0 1.7 %collective-permute-start.39 = (f32[152,128]{1,0:T(8,128)S(1)}, f32[152,128]{1,0:T(8,128)S(1)}, u32[]{:S(2)}, u32[]{:S(2)}) collective-permute-start(f32[152,128]{1,0:T(8,128)S(1)} %slice_add_fusion.11), channel_id=1, source_target_pairs={{0,8},{1,9},{2,10},{3,11},{4,12},{5,13},{6,14},{7,15},{8,0},{9,1},... | collective-permute-start | bytes 233480 | tf_op jit(solution)/shard_map/cond/branch_1_fun/ppermute | solution.py:546
  51.7 0.1 collective-permute-done.46
  51.8 1.3 %collective-permute-start.47 = (f32[152,128]{1,0:T(8,128)S(1)}, f32[152,128]{1,0:T(8,128)S(1)}, u32[]{:S(2)}, u32[]{:S(2)}) collective-permute-start(f32[152,128]{1,0:T(8,128)S(1)} %add.135), channel_id=1, source_target_pairs={{0,4},{1,3},{2,6},{3,1},{4,0},{5,7},{6,2},{7,5},{8,12},{9,11},{10,... | collective-permute-start | bytes 233480 | tf_op jit(solution)/shard_map/cond/branch_1_fun/ppermute | solution.py:546
  53.1 3.9 %collective-permute-done.39 = f32[152,128]{1,0:T(8,128)S(1)} collective-permute-done((f32[152,128]{1,0:T(8,128)S(1)}, f32[152,128]{1,0:T(8,128)S(1)}, u32[]{:S(2)}, u32[]{:S(2)}) %collective-permute-start.39) | collective-permute-done | bytes 77856 | tf_op jit(solution)/shard_map/cond/branch_1_fun/ppermute | solution.py:546
  57.1 1.3 %collective-permute-start.40 = (f32[152,128]{1,0:T(8,128)S(1)}, f32[152,128]{1,0:T(8,128)S(1)}, u32[]{:S(2)}, u32[]{:S(2)}) collective-permute-start(f32[152,128]{1,0:T(8,128)S(1)} %add.131), channel_id=1, source_target_pairs={{0,4},{1,3},{2,6},{3,1},{4,0},{5,7},{6,2},{7,5},{8,12},{9,11},{10,... | collective-permute-start | bytes 233480 | tf_op jit(solution)/shard_map/cond/branch_1_fun/ppermute | solution.py:546
  58.4 0.0 collective-permute-done.47
  58.4 0.1 collective-permute-start.48
  58.5 1.9 %collective-permute-done.40 = f32[152,128]{1,0:T(8,128)S(1)} collective-permute-done((f32[152,128]{1,0:T(8,128)S(1)}, f32[152,128]{1,0:T(8,128)S(1)}, u32[]{:S(2)}, u32[]{:S(2)}) %collective-permute-start.40) | collective-permute-done | bytes 77856 | tf_op jit(solution)/shard_map/cond/branch_1_fun/ppermute | solution.py:546
  60.4 0.1 collective-permute-start.41
  60.5 3.3 %collective-permute-done.48 = f32[304,128]{1,0:T(8,128)S(1)} collective-permute-done((f32[304,128]{1,0:T(8,128)S(1)}, f32[304,128]{1,0:T(8,128)S(1)}, u32[]{:S(2)}, u32[]{:S(2)}) %collective-permute-start.48) | collective-permute-done | bytes 155680 | tf_op jit(solution)/shard_map/cond/branch_1_fun/ppermute | solution.py:546
  63.8 4.0 %collective-permute-start.49 = (f32[608,128]{1,0:T(8,128)S(1)}, f32[608,128]{1,0:T(8,128)S(1)}, u32[]{:S(2)}, u32[]{:S(2)}) collective-permute-start(f32[608,128]{1,0:T(8,128)S(1)} %pad_maximum_fusion.12.mine_ref), channel_id=1, source_target_pairs={{0,1},{1,0},{2,3},{3,2},{4,5},{5,4},{6,7},{7,6},{8,9},{9,8},{10,11... | collective-permute-start | bytes 933896 | tf_op jit(solution)/shard_map/cond/branch_1_fun/ppermute | solution.py:546
  67.9 0.0 collective-permute-done.41
  67.9 1.9 %collective-permute-start.42 = (f32[608,128]{1,0:T(8,128)S(1)}, f32[608,128]{1,0:T(8,128)S(1)}, u32[]{:S(2)}, u32[]{:S(2)}) collective-permute-start(f32[608,128]{1,0:T(8,128)S(1)} %pad_maximum_fusion.11.mine_ref), channel_id=1, source_target_pairs={{0,1},{1,0},{2,3},{3,2},{4,5},{5,4},{6,7},{7,6},{8,9},{9,8},{10,11... | collective-permute-start | bytes 933896 | tf_op jit(solution)/shard_map/cond/branch_1_fun/ppermute | solution.py:546
  69.8 2.2 %update.3 = (f32[1000,768]{1,0:T(8,128)}, f32[1000,256]{1,0:T(8,128)}, bf16[768,768]{1,0:T(8,128)(2,1)S(1)}) custom-call(f32[608,128]{1,0:T(8,128)S(1)} %pad_maximum_fusion.12.mine_ref, f32[608,128]{1,0:T(8,128)S(1)} %collective-permute-done.49.other_ref, f32[1000,256]{1,0:T(8,128)S(1)} %copy-done.4, s32[1,256]{1,0:T(1,128)S(1)} %copy-done.8, ...), custom_call_target="tpu_custom_call" | custom-call | flops 717225984 | bytes 3670016 | tf_op jit(solution)/shard_map/cond/branch_1_fun/update/pallas_call | solution.py:485
  72.1 0.0 collective-permute-done.42.other_ref
  72.1 2.0 %update_more.3 = (f32[1000,768]{1,0:T(8,128)}, f32[1000,256]{1,0:T(8,128)}) custom-call(f32[608,128]{1,0:T(8,128)S(1)} %pad_maximum_fusion.11.mine_ref, f32[608,128]{1,0:T(8,128)S(1)} %collective-permute-done.42.other_ref, f32[1000,256]{1,0:T(8,128)S(1)} %copy-done.4, f32[1000,768]{1,0:T(8,128)S(1)} %copy-done.2, ...), custom_call_target="tpu_custom_call", output_to_operand_aliasing={{0}: (5, {}), {1}: (6, {})} | custom-call | flops 651165696 | bytes 4521984 | tf_op jit(solution)/shard_map/cond/branch_1_fun/update_more/pallas_call | solution.py:522
  (31 shorter events, 0.4 us)
Async XLA Ops:
  4.7 5.4 %copy-start.8 = (s32[1,256]{1,0:T(1,128)S(1)}, s32[1,256]{1,0:T(1,128)}, u32[]{:S(2)}) copy-start(s32[1,256]{1,0:T(1,128)} %get-tuple-element.58.index_hbm.index_ref) | copy-start | bytes 3076 | tf_op jit(solution)/shard_map/cond
  4.8 5.7 %copy-start.10 = (s32[320]{0:T(512)S(1)}, s32[320]{0:T(512)}, u32[]{:S(2)}) copy-start(s32[320]{0:T(512)} %get-tuple-element.60) | copy-start | bytes 3844 | tf_op jit(solution)/shard_map/cond
  4.8 5.7 %copy-start = (bf16[768,3072]{1,0:T(8,128)(2,1)S(1)}, bf16[768,3072]{1,0:T(8,128)(2,1)}, u32[]{:S(2)}) copy-start(bf16[768,3072]{1,0:T(8,128)(2,1)} %get-tuple-element.59.centers_hbm.centers_ref) | copy-start | bytes 14155780 | tf_op jit(solution)/shard_map/cond
  4.8 8.7 %collective-permute-start.29 = (bf16[32,1536]{1,0:T(8,128)(2,1)S(1)}, bf16[32,1536]{1,0:T(8,128)(2,1)S(1)}, u32[]{:S(2)}, u32[]{:S(2)}) collective-permute-start(bf16[32,1536]{1,0:T(8,128)(2,1)S(1)} %pack_rows.3), channel_id=1, source_target_pairs={{0,8},{1,9},{2,10},{3,11},{4,12},{5,13},{6,14},{7,15},{8,0},{9,1},... | collective-permute-start | bytes 294920 | tf_op jit(solution)/shard_map/cond/branch_1_fun/ppermute | solution.py:546
  9.9 1.9 %copy-start.2 = (f32[1000,768]{1,0:T(8,128)S(1)}, f32[1000,768]{1,0:T(8,128)}, u32[]{:S(2)}) copy-start(f32[1000,768]{1,0:T(8,128)} %get-tuple-element.62.weights_ref) | copy-start | bytes 9216004 | tf_op jit(solution)/shard_map/cond
  9.9 1.9 %copy-start.6 = (f32[160,320]{1,0:T(8,128)S(1)}, f32[160,320]{1,0:T(8,128)}, u32[]{:S(2)}) copy-start(f32[160,320]{1,0:T(8,128)} %get-tuple-element.61.eigvec_ref) | copy-start | bytes 614404 | tf_op jit(solution)/shard_map/cond
  9.9 4.9 %collective-permute-start.28 = (bf16[32,1536]{1,0:T(8,128)(2,1)S(1)}, bf16[32,1536]{1,0:T(8,128)(2,1)S(1)}, u32[]{:S(2)}, u32[]{:S(2)}) collective-permute-start(bf16[32,1536]{1,0:T(8,128)(2,1)S(1)} %pack_rows.2), channel_id=1, source_target_pairs={{0,8},{1,9},{2,10},{3,11},{4,12},{5,13},{6,14},{7,15},{8,0},{9,1},... | collective-permute-start | bytes 294920 | tf_op jit(solution)/shard_map/cond/branch_1_fun/ppermute | solution.py:546
  13.5 4.9 %collective-permute-start.30 = (bf16[64,1536]{1,0:T(8,128)(2,1)S(1)}, bf16[64,1536]{1,0:T(8,128)(2,1)S(1)}, u32[]{:S(2)}, u32[]{:S(2)}) collective-permute-start(bf16[64,1536]{1,0:T(8,128)(2,1)S(1)} %pad_maximum_fusion.14), channel_id=1, source_target_pairs={{0,4},{1,3},{2,6},{3,1},{4,0},{5,7},{6,2},{7,5},{8,12},{9,11},{10,... | collective-permute-start | bytes 589832 | tf_op jit(solution)/shard_map/cond/branch_1_fun/ppermute | solution.py:546
  14.8 6.1 %collective-permute-start.33 = (bf16[64,1536]{1,0:T(8,128)(2,1)S(1)}, bf16[64,1536]{1,0:T(8,128)(2,1)S(1)}, u32[]{:S(2)}, u32[]{:S(2)}) collective-permute-start(bf16[64,1536]{1,0:T(8,128)(2,1)S(1)} %pad_maximum_fusion.13), channel_id=1, source_target_pairs={{0,4},{1,3},{2,6},{3,1},{4,0},{5,7},{6,2},{7,5},{8,12},{9,11},{10,... | collective-permute-start | bytes 589832 | tf_op jit(solution)/shard_map/cond/branch_1_fun/ppermute | solution.py:546
  18.4 9.4 %collective-permute-start.31 = (bf16[128,1536]{1,0:T(8,128)(2,1)S(1)}, bf16[128,1536]{1,0:T(8,128)(2,1)S(1)}, u32[]{:S(2)}, u32[]{:S(2)}) collective-permute-start(bf16[128,1536]{1,0:T(8,128)(2,1)S(1)} %pad_maximum_fusion.9), channel_id=1, source_target_pairs={{0,2},{1,5},{2,0},{3,7},{4,6},{5,1},{6,4},{7,3},{8,10},{9,13},{10,... | collective-permute-start | bytes 1179656 | tf_op jit(solution)/shard_map/cond/branch_1_fun/ppermute | solution.py:546
  20.9 11.1 %collective-permute-start.34 = (bf16[128,1536]{1,0:T(8,128)(2,1)S(1)}, bf16[128,1536]{1,0:T(8,128)(2,1)S(1)}, u32[]{:S(2)}, u32[]{:S(2)}) collective-permute-start(bf16[128,1536]{1,0:T(8,128)(2,1)S(1)} %pad_maximum_fusion.10), channel_id=1, source_target_pairs={{0,2},{1,5},{2,0},{3,7},{4,6},{5,1},{6,4},{7,3},{8,10},{9,13},{10,... | collective-permute-start | bytes 1179656 | tf_op jit(solution)/shard_map/cond/branch_1_fun/ppermute | solution.py:546
  27.8 5.6 %collective-permute-start.32 = (bf16[256,1536]{1,0:T(8,128)(2,1)S(1)}, bf16[256,1536]{1,0:T(8,128)(2,1)S(1)}, u32[]{:S(2)}, u32[]{:S(2)}) collective-permute-start(bf16[256,1536]{1,0:T(8,128)(2,1)S(1)} %pad_maximum_fusion.8.mine_ref), channel_id=1, source_target_pairs={{0,1},{1,0},{2,3},{3,2},{4,5},{5,4},{6,7},{7,6},{8,9},{9,8},{10,11... | collective-permute-start | bytes 2359304 | tf_op jit(solution)/shard_map/cond/branch_1_fun/ppermute | solution.py:546
  32.0 3.3 %collective-permute-start.35 = (bf16[256,1536]{1,0:T(8,128)(2,1)S(1)}, bf16[256,1536]{1,0:T(8,128)(2,1)S(1)}, u32[]{:S(2)}, u32[]{:S(2)}) collective-permute-start(bf16[256,1536]{1,0:T(8,128)(2,1)S(1)} %constant_dynamic-update-slice_fusion.next_ref), channel_id=1, source_target_pairs={{0,1},{1,0},{2,3},{3,2},{4,5},{5,4},{6,7},{7,6},{8,9},{9,8},{10,11... | collective-permute-start | bytes 2359304 | tf_op jit(solution)/shard_map/cond/branch_1_fun/ppermute | solution.py:546
  37.7 1.7 %collective-permute-start.43 = (f32[608,128]{1,0:T(8,128)S(1)}, f32[608,128]{1,0:T(8,128)S(1)}, u32[]{:S(2)}, u32[]{:S(2)}) collective-permute-start(f32[608,128]{1,0:T(8,128)S(1)} %get-tuple-element.78), channel_id=1, source_target_pairs={{0,1},{1,0},{2,3},{3,2},{4,5},{5,4},{6,7},{7,6},{8,9},{9,8},{10,11... | collective-permute-start | bytes 933896 | tf_op jit(solution)/shard_map/cond/branch_1_fun/ppermute | solution.py:546
  39.2 1.7 %collective-permute-start.36 = (f32[608,128]{1,0:T(8,128)S(1)}, f32[608,128]{1,0:T(8,128)S(1)}, u32[]{:S(2)}, u32[]{:S(2)}) collective-permute-start(f32[608,128]{1,0:T(8,128)S(1)} %get-tuple-element.75), channel_id=1, source_target_pairs={{0,1},{1,0},{2,3},{3,2},{4,5},{5,4},{6,7},{7,6},{8,9},{9,8},{10,11... | collective-permute-start | bytes 933896 | tf_op jit(solution)/shard_map/cond/branch_1_fun/ppermute | solution.py:546
  39.4 30.4 %copy-start.4 = (f32[1000,256]{1,0:T(8,128)S(1)}, f32[1000,256]{1,0:T(8,128)}, u32[]{:S(2)}) copy-start(f32[1000,256]{1,0:T(8,128)} %get-tuple-element.76.targets_ref) | copy-start | bytes 3072004 | tf_op jit(solution)/shard_map/cond
  39.5 30.4 %copy-start.12 = (f32[1,160]{1,0:T(1,128)S(1)}, f32[1,160]{1,0:T(1,128)}, u32[]{:S(2)}) copy-start(f32[1,160]{1,0:T(1,128)} %get-tuple-element.79.eigval_ref) | copy-start | bytes 1924 | tf_op jit(solution)/shard_map/cond
  39.5 4.4 %collective-permute-start.44 = (f32[304,128]{1,0:T(8,128)S(1)}, f32[304,128]{1,0:T(8,128)S(1)}, u32[]{:S(2)}, u32[]{:S(2)}) collective-permute-start(f32[304,128]{1,0:T(8,128)S(1)} %slice.96), channel_id=1, source_target_pairs={{0,2},{1,5},{2,0},{3,7},{4,6},{5,1},{6,4},{7,3},{8,10},{9,13},{10,... | collective-permute-start | bytes 466952 | tf_op jit(solution)/shard_map/cond/branch_1_fun/ppermute | solution.py:546
  40.9 4.7 %collective-permute-start.37 = (f32[304,128]{1,0:T(8,128)S(1)}, f32[304,128]{1,0:T(8,128)S(1)}, u32[]{:S(2)}, u32[]{:S(2)}) collective-permute-start(f32[304,128]{1,0:T(8,128)S(1)} %slice.92), channel_id=1, source_target_pairs={{0,2},{1,5},{2,0},{3,7},{4,6},{5,1},{6,4},{7,3},{8,10},{9,13},{10,... | collective-permute-start | bytes 466952 | tf_op jit(solution)/shard_map/cond/branch_1_fun/ppermute | solution.py:546
  44.0 3.3 %collective-permute-start.45 = (f32[152,128]{1,0:T(8,128)S(1)}, f32[152,128]{1,0:T(8,128)S(1)}, u32[]{:S(2)}, u32[]{:S(2)}) collective-permute-start(f32[152,128]{1,0:T(8,128)S(1)} %slice.98), channel_id=1, source_target_pairs={{0,4},{1,3},{2,6},{3,1},{4,0},{5,7},{6,2},{7,5},{8,12},{9,11},{10,... | collective-permute-start | bytes 233480 | tf_op jit(solution)/shard_map/cond/branch_1_fun/ppermute | solution.py:546
  45.6 4.4 %collective-permute-start.38 = (f32[152,128]{1,0:T(8,128)S(1)}, f32[152,128]{1,0:T(8,128)S(1)}, u32[]{:S(2)}, u32[]{:S(2)}) collective-permute-start(f32[152,128]{1,0:T(8,128)S(1)} %slice.94), channel_id=1, source_target_pairs={{0,4},{1,3},{2,6},{3,1},{4,0},{5,7},{6,2},{7,5},{8,12},{9,11},{10,... | collective-permute-start | bytes 233480 | tf_op jit(solution)/shard_map/cond/branch_1_fun/ppermute | solution.py:546
  47.3 4.5 %collective-permute-start.46 = (f32[152,128]{1,0:T(8,128)S(1)}, f32[152,128]{1,0:T(8,128)S(1)}, u32[]{:S(2)}, u32[]{:S(2)}) collective-permute-start(f32[152,128]{1,0:T(8,128)S(1)} %slice_add_fusion.10), channel_id=1, source_target_pairs={{0,8},{1,9},{2,10},{3,11},{4,12},{5,13},{6,14},{7,15},{8,0},{9,1},... | collective-permute-start | bytes 233480 | tf_op jit(solution)/shard_map/cond/branch_1_fun/ppermute | solution.py:546
  50.0 7.0 %collective-permute-start.39 = (f32[152,128]{1,0:T(8,128)S(1)}, f32[152,128]{1,0:T(8,128)S(1)}, u32[]{:S(2)}, u32[]{:S(2)}) collective-permute-start(f32[152,128]{1,0:T(8,128)S(1)} %slice_add_fusion.11), channel_id=1, source_target_pairs={{0,8},{1,9},{2,10},{3,11},{4,12},{5,13},{6,14},{7,15},{8,0},{9,1},... | collective-permute-start | bytes 233480 | tf_op jit(solution)/shard_map/cond/branch_1_fun/ppermute | solution.py:546
  51.8 6.6 %collective-permute-start.47 = (f32[152,128]{1,0:T(8,128)S(1)}, f32[152,128]{1,0:T(8,128)S(1)}, u32[]{:S(2)}, u32[]{:S(2)}) collective-permute-start(f32[152,128]{1,0:T(8,128)S(1)} %add.135), channel_id=1, source_target_pairs={{0,4},{1,3},{2,6},{3,1},{4,0},{5,7},{6,2},{7,5},{8,12},{9,11},{10,... | collective-permute-start | bytes 233480 | tf_op jit(solution)/shard_map/cond/branch_1_fun/ppermute | solution.py:546
  57.1 3.3 %collective-permute-start.40 = (f32[152,128]{1,0:T(8,128)S(1)}, f32[152,128]{1,0:T(8,128)S(1)}, u32[]{:S(2)}, u32[]{:S(2)}) collective-permute-start(f32[152,128]{1,0:T(8,128)S(1)} %add.131), channel_id=1, source_target_pairs={{0,4},{1,3},{2,6},{3,1},{4,0},{5,7},{6,2},{7,5},{8,12},{9,11},{10,... | collective-permute-start | bytes 233480 | tf_op jit(solution)/shard_map/cond/branch_1_fun/ppermute | solution.py:546
  58.4 5.4 %collective-permute-start.48 = (f32[304,128]{1,0:T(8,128)S(1)}, f32[304,128]{1,0:T(8,128)S(1)}, u32[]{:S(2)}, u32[]{:S(2)}) collective-permute-start(f32[304,128]{1,0:T(8,128)S(1)} %pad_maximum_fusion.16), channel_id=1, source_target_pairs={{0,2},{1,5},{2,0},{3,7},{4,6},{5,1},{6,4},{7,3},{8,10},{9,13},{10,... | collective-permute-start | bytes 466952 | tf_op jit(solution)/shard_map/cond/branch_1_fun/ppermute | solution.py:546
  60.4 7.5 %collective-permute-start.41 = (f32[304,128]{1,0:T(8,128)S(1)}, f32[304,128]{1,0:T(8,128)S(1)}, u32[]{:S(2)}, u32[]{:S(2)}) collective-permute-start(f32[304,128]{1,0:T(8,128)S(1)} %pad_maximum_fusion.15), channel_id=1, source_target_pairs={{0,2},{1,5},{2,0},{3,7},{4,6},{5,1},{6,4},{7,3},{8,10},{9,13},{10,... | collective-permute-start | bytes 466952 | tf_op jit(solution)/shard_map/cond/branch_1_fun/ppermute | solution.py:546
  63.8 6.0 %collective-permute-start.49 = (f32[608,128]{1,0:T(8,128)S(1)}, f32[608,128]{1,0:T(8,128)S(1)}, u32[]{:S(2)}, u32[]{:S(2)}) collective-permute-start(f32[608,128]{1,0:T(8,128)S(1)} %pad_maximum_fusion.12.mine_ref), channel_id=1, source_target_pairs={{0,1},{1,0},{2,3},{3,2},{4,5},{5,4},{6,7},{7,6},{8,9},{9,8},{10,11... | collective-permute-start | bytes 933896 | tf_op jit(solution)/shard_map/cond/branch_1_fun/ppermute | solution.py:546
  67.9 4.2 %collective-permute-start.42 = (f32[608,128]{1,0:T(8,128)S(1)}, f32[608,128]{1,0:T(8,128)S(1)}, u32[]{:S(2)}, u32[]{:S(2)}) collective-permute-start(f32[608,128]{1,0:T(8,128)S(1)} %pad_maximum_fusion.11.mine_ref), channel_id=1, source_target_pairs={{0,1},{1,0},{2,3},{3,2},{4,5},{5,4},{6,7},{7,6},{8,9},{9,8},{10,11... | collective-permute-start | bytes 933896 | tf_op jit(solution)/shard_map/cond/branch_1_fun/ppermute | solution.py:546

commit v14 on v13

--- a/solution.py
+++ b/solution.py
@@ -14,7 +14,7 @@
 HALVINGS = 2
 CHUNKS = 1 << HALVINGS
 LANE = 128
-PARTS = 2
+COLUMNS = 256
 SLOTS = 32
 BLOCKS = 2
 NT = (((1,), (1,)), ((), ()))
@@ -24,6 +24,11 @@
 
 def dot(a, b, dims):
     return lax.dot_general(a, b, dims, preferred_element_type=F32)
+
+
+def depth_parts(depth):
+    first = depth // COLUMNS * 7 // 12 * COLUMNS
+    return [(0, first), (first, depth - first)]
 
 
 def walk(sub, bits):
@@ -100,13 +105,13 @@
 def pick_batch(batch_index, centers, part):
     rows = batch_index.shape[1]
     count, depth = centers.shape
-    depth = depth // PARTS
-    block = 512
+    first, depth = depth_parts(depth)[part]
+    block = COLUMNS
     half = jax.ShapeDtypeStruct((rows // 2, depth), BF16)
     hbm = pl.BlockSpec(memory_space=pltpu.HBM)
     vmem = pl.BlockSpec(memory_space=pltpu.VMEM)
     return pl.pallas_call(
-        functools.partial(pick_body, part * depth),
+        functools.partial(pick_body, first),
         in_specs=[hbm, hbm],
         out_specs=[vmem, vmem],
         out_shape=[half, half],
@@ -175,11 +180,11 @@
 def pack_rows(batch_index, centers, part):
     rows = batch_index.shape[1]
     count, depth = centers.shape
-    depth = depth // PARTS
-    block = 512
+    first, depth = depth_parts(depth)[part]
+    block = COLUMNS
     hbm = pl.BlockSpec(memory_space=pltpu.HBM)
     return pl.pallas_call(
-        functools.partial(pack_body, part * depth),
+        functools.partial(pack_body, first),
         in_specs=[hbm, hbm],
         out_specs=pl.BlockSpec(memory_space=pltpu.VMEM),
         out_shape=jax.ShapeDtypeStruct((SLOTS, depth), BF16),
@@ -362,7 +367,7 @@
         distance_body,
         in_specs=[vmem] * 6,
         out_specs=[vmem, vmem],
-        out_shape=[jax.ShapeDtypeStruct((count, rows), F32), jax.ShapeDtypeStruct((rows, depth), BF16)],
+        out_shape=[jax.ShapeDtypeStruct((count, rows), F32), jax.ShapeDtypeStruct((rows, following.shape[1]), BF16)],
         scratch_shapes=[pltpu.VMEM((rows, depth), BF16)],
         compiler_params=params(),
         cost_estimate=pl.CostEstimate(
@@ -601,12 +606,12 @@
     ready = [center_norms(centers), *spread_weights(nys_index.reshape(1, -1), eigvec, weights, first, second)]
     if packed:
         ready.append(select_packed(batch_index, count, chips))
-        slots = [pack_rows(*far, part) for part in range(PARTS)]
+        slots = [pack_rows(*far, part) for part in range(2)]
         mine, other = all_of(slots[0], chips)
         next_mine, next_other, norms, left1, left2, spread, select = all_of(slots[1], chips, ready)
     else:
         ready.append(select_summed(rows))
-        picked = [pick_batch(*far, part) for part in range(PARTS)]
+        picked = [pick_batch(*far, part) for part in range(2)]
         mine, other = total_of(*picked[0], chips)
         next_mine, next_other, norms, left1, left2, spread, select = total_of(*picked[1], chips, ready)
     before, found = distances(mine, other, next_mine, select, centers, norms)

time: 74.4 us -> 75.3 us (1.012)
  waiting for transfers between devices: 23.5 us -> 19.7 us
  starting transfers between devices: 30.7 us -> 34.4 us
  Pallas kernels: 17.4 us -> 18.4 us
    ppermute x22, waiting for transfers between devices: 23.5 us -> 19.7 us  [swap(): lax.ppermute(x, AXES, [(i, i ^ flip[i & 1]) for i in range(2 * chips)])]
    ppermute x22, starting transfers between devices: 30.7 us -> 34.4 us  [swap(): lax.ppermute(x, AXES, [(i, i ^ flip[i & 1]) for i in range(2 * chips)])]
    pallas_call x2, Pallas kernels: 3.83 us -> 4.82 us  [pack_rows(): pl.pallas_call(functools.partial(pack_body, first), in_specs=[hbm, hbm],...]
  transfers between devices with their start and end apart: 22 -> 22, of which waited for: 12 -> 11; matrix products, arithmetic and copies ran while one was open for 1% -> 1% of each run, Pallas kernels for 13% -> 14%
where the time goes in v14:
time: 75.3 us; the launch traced here: 75.1 us
  starting transfers between devices  34.4 us (46%)
  waiting for transfers between devices  19.7 us (26%)
  Pallas kernels  18.4 us (24%)
  between operations  1.47 us (2%)
    ppermute x22, starting transfers between devices, swap(): lax.ppermute(x, AXES, [(i, i ^ flip[i & 1]) for i in range(2 * chips)])  34.4 us
    ppermute x22, waiting for transfers between devices, swap(): lax.ppermute(x, AXES, [(i, i ^ flip[i & 1]) for i in range(2 * chips)])  19.7 us
    pallas_call x2, Pallas kernels, pack_rows(): pl.pallas_call(functools.partial(pack_body, first), in_specs=[hbm, hbm],...  4.82 us
    pallas_call x1, Pallas kernels, predict(): pl.pallas_call(predict_body, in_specs=[vmem] * 6, out_specs=[vmem] * 3, o...  2.26 us
    pallas_call x1, Pallas kernels, update(): pl.pallas_call(update_body, in_specs=[vmem] * 7, out_specs=[hbm, hbm, vme...  2.18 us
    pallas_call x1, Pallas kernels, update_more(): pl.pallas_call(functools.partial(update_more_body, begin), in_specs=[vmem...  1.87 us
    pallas_call x1, Pallas kernels, distances(): pl.pallas_call(distance_body, in_specs=[vmem] * 6, out_specs=[vmem, vmem]...  1.79 us
    pallas_call x1, Pallas kernels, spread_weights(): pl.pallas_call(functools.partial(spread_body, first, classes), out_shape=...  1.69 us
  transfers between devices with their start and end apart: 22, of which 11 were waited for; matrix products, arithmetic and copies ran while one was open for 1% of the time, Pallas kernels for 14%

profile of v14, /device:TPU:1, one launch (start us, length us, event | category | flops | bytes accessed | tf_op | source)
XLA Modules:
  0.0 75.1 jit_solution(12378276346669303864)
XLA Ops:
  0.6 1.3 %rows_fit.1 = s32[1]{0:T(128)} custom-call(s32[1,256]{1,0:T(1,128)} %bitcast.17), custom_call_target="tpu_custom_call" | custom-call | tf_op jit(solution)/shard_map/rows_fit/pallas_call | solution.py:144
  2.6 72.3 %conditional.1 = ((f32[1000,768]{1,0:T(8,128)}, f32[1000,256]{1,0:T(8,128)})) conditional(s32[]{:T(128)} %bitcast.2, (s32[1,256]{1,0:T(1,128)}, bf16[768,3072]{1,0:T(8,128)(2,1)}, s32[320]{0:T(512)}, f32[160,320]{1,0:T(8,128)}, f32[1000,768]{1,0:T(8,128)}, /*index=5*/f32[1000,256]{1,0:T(8,128)}, f32[1,160]{1,0:T(1,128)}) %tuple.30, ...), branch_computations={%region_0.1_spmd, %region_1.2_spmd} | conditional | flops 5464187904 | bytes 106462256 | solution.py:627
  2.9 2.6 %pack_rows.3 = bf16[32,1792]{1,0:T(8,128)(2,1)S(1)} custom-call(s32[1,256]{1,0:T(1,128)} %get-tuple-element.58.index_hbm.index_ref, bf16[768,3072]{1,0:T(8,128)(2,1)} %get-tuple-element.59.centers_hbm.centers_ref), custom_call_target="tpu_custom_call" | custom-call | flops 88080384 | bytes 2867200 | tf_op jit(solution)/shard_map/cond/branch_1_fun/pack_rows/pallas_call | solution.py:186
  5.5 0.0 copy-start.8
  5.5 0.0 copy-start.10
  5.5 0.0 copy-start
  5.5 3.2 %collective-permute-start.29 = (bf16[32,1792]{1,0:T(8,128)(2,1)S(1)}, bf16[32,1792]{1,0:T(8,128)(2,1)S(1)}, u32[]{:S(2)}, u32[]{:S(2)}) collective-permute-start(bf16[32,1792]{1,0:T(8,128)(2,1)S(1)} %pack_rows.3), channel_id=1, source_target_pairs={{0,8},{1,9},{2,10},{3,11},{4,12},{5,13},{6,14},{7,15},{8,0},{9,1},... | collective-permute-start | bytes 344072 | tf_op jit(solution)/shard_map/cond/branch_1_fun/ppermute | solution.py:551
  8.8 2.2 %pack_rows.2 = bf16[32,1280]{1,0:T(8,128)(2,1)S(1)} custom-call(s32[1,256]{1,0:T(1,128)} %get-tuple-element.58.index_hbm.index_ref, bf16[768,3072]{1,0:T(8,128)(2,1)} %get-tuple-element.59.centers_hbm.centers_ref), custom_call_target="tpu_custom_call" | custom-call | flops 62914560 | bytes 2048000 | tf_op jit(solution)/shard_map/cond/branch_1_fun/pack_rows/pallas_call | solution.py:186
  10.9 0.0 copy-start.2
  10.9 0.0 copy-start.6
  11.0 0.2 collective-permute-start.28
  11.2 0.3 select_packed.1.select_ref
  11.5 1.2 %center_norms.3.norm_ref = f32[768,128]{1,0:T(8,128)S(1)} custom-call(bf16[768,3072]{1,0:T(8,128)(2,1)S(1)} %copy-done), custom_call_target="tpu_custom_call" | custom-call | flops 4718592 | bytes 4718592 | tf_op jit(solution)/shard_map/cond/branch_1_fun/center_norms/pallas_call | solution.py:294
  12.7 0.1 copy-done.2
  12.8 1.7 %spread_weights.3 = (bf16[608,2304]{1,0:T(8,128)(2,1)S(1)}, bf16[608,2304]{1,0:T(8,128)(2,1)S(1)}, f32[160,768]{1,0:T(8,128)S(1)}) custom-call(s32[1,320]{1,0:T(1,128)S(1)} %reshape.99.index_ref, f32[160,320]{1,0:T(8,128)S(1)} %copy-done.6, f32[1000,768]{1,0:T(8,128)S(1)} %copy-done.2), custom_call_target="tpu_custom_call" | custom-call | flops 235929600 | bytes 7471104 | tf_op jit(solution)/shard_map/cond/branch_1_fun/spread_weights/pallas_call | solution.py:269
  14.5 0.0 collective-permute-done.29
  14.5 1.3 %collective-permute-start.30 = (bf16[64,1792]{1,0:T(8,128)(2,1)S(1)}, bf16[64,1792]{1,0:T(8,128)(2,1)S(1)}, u32[]{:S(2)}, u32[]{:S(2)}) collective-permute-start(bf16[64,1792]{1,0:T(8,128)(2,1)S(1)} %pad_maximum_fusion.13), channel_id=1, source_target_pairs={{0,4},{1,3},{2,6},{3,1},{4,0},{5,7},{6,2},{7,5},{8,12},{9,11},{10,... | collective-permute-start | bytes 688136 | tf_op jit(solution)/shard_map/cond/branch_1_fun/ppermute | solution.py:551
  15.9 0.5 collective-permute-done.28
  16.4 1.7 %collective-permute-start.33 = (bf16[64,1280]{1,0:T(8,128)(2,1)S(1)}, bf16[64,1280]{1,0:T(8,128)(2,1)S(1)}, u32[]{:S(2)}, u32[]{:S(2)}) collective-permute-start(bf16[64,1280]{1,0:T(8,128)(2,1)S(1)} %pad_maximum_fusion.14), channel_id=1, source_target_pairs={{0,4},{1,3},{2,6},{3,1},{4,0},{5,7},{6,2},{7,5},{8,12},{9,11},{10,... | collective-permute-start | bytes 491528 | tf_op jit(solution)/shard_map/cond/branch_1_fun/ppermute | solution.py:551
  18.1 1.7 %collective-permute-done.30 = bf16[64,1792]{1,0:T(8,128)(2,1)S(1)} collective-permute-done((bf16[64,1792]{1,0:T(8,128)(2,1)S(1)}, bf16[64,1792]{1,0:T(8,128)(2,1)S(1)}, u32[]{:S(2)}, u32[]{:S(2)}) %collective-permute-start.30) | collective-permute-done | bytes 229408 | tf_op jit(solution)/shard_map/cond/branch_1_fun/ppermute | solution.py:551
  19.8 2.6 %collective-permute-start.31 = (bf16[128,1792]{1,0:T(8,128)(2,1)S(1)}, bf16[128,1792]{1,0:T(8,128)(2,1)S(1)}, u32[]{:S(2)}, u32[]{:S(2)}) collective-permute-start(bf16[128,1792]{1,0:T(8,128)(2,1)S(1)} %pad_maximum_fusion.9), channel_id=1, source_target_pairs={{0,2},{1,5},{2,0},{3,7},{4,6},{5,1},{6,4},{7,3},{8,10},{9,13},{10,... | collective-permute-start | bytes 1376264 | tf_op jit(solution)/shard_map/cond/branch_1_fun/ppermute | solution.py:551
  22.4 0.0 collective-permute-done.33
  22.4 1.7 %collective-permute-start.34 = (bf16[128,1280]{1,0:T(8,128)(2,1)S(1)}, bf16[128,1280]{1,0:T(8,128)(2,1)S(1)}, u32[]{:S(2)}, u32[]{:S(2)}) collective-permute-start(bf16[128,1280]{1,0:T(8,128)(2,1)S(1)} %pad_maximum_fusion.10), channel_id=1, source_target_pairs={{0,2},{1,5},{2,0},{3,7},{4,6},{5,1},{6,4},{7,3},{8,10},{9,13},{10,... | collective-permute-start | bytes 983048 | tf_op jit(solution)/shard_map/cond/branch_1_fun/ppermute | solution.py:551
  24.1 4.6 %collective-permute-done.31 = bf16[128,1792]{1,0:T(8,128)(2,1)S(1)} collective-permute-done((bf16[128,1792]{1,0:T(8,128)(2,1)S(1)}, bf16[128,1792]{1,0:T(8,128)(2,1)S(1)}, u32[]{:S(2)}, u32[]{:S(2)}) %collective-permute-start.31) | collective-permute-done | bytes 458784 | tf_op jit(solution)/shard_map/cond/branch_1_fun/ppermute | solution.py:551
  28.7 0.1 pad_maximum_fusion.8.mine_ref
  28.8 1.9 %collective-permute-start.32 = (bf16[256,1792]{1,0:T(8,128)(2,1)S(1)}, bf16[256,1792]{1,0:T(8,128)(2,1)S(1)}, u32[]{:S(2)}, u32[]{:S(2)}) collective-permute-start(bf16[256,1792]{1,0:T(8,128)(2,1)S(1)} %pad_maximum_fusion.8.mine_ref), channel_id=1, source_target_pairs={{0,1},{1,0},{2,3},{3,2},{4,5},{5,4},{6,7},{7,6},{8,9},{9,8},{10,11... | collective-permute-start | bytes 2752520 | tf_op jit(solution)/shard_map/cond/branch_1_fun/ppermute | solution.py:551
  30.7 1.6 %collective-permute-done.34 = bf16[128,1280]{1,0:T(8,128)(2,1)S(1)} collective-permute-done((bf16[128,1280]{1,0:T(8,128)(2,1)S(1)}, bf16[128,1280]{1,0:T(8,128)(2,1)S(1)}, u32[]{:S(2)}, u32[]{:S(2)}) %collective-permute-start.34) | collective-permute-done | bytes 327712 | tf_op jit(solution)/shard_map/cond/branch_1_fun/ppermute | solution.py:551
  32.3 1.9 %collective-permute-start.35 = (bf16[256,1280]{1,0:T(8,128)(2,1)S(1)}, bf16[256,1280]{1,0:T(8,128)(2,1)S(1)}, u32[]{:S(2)}, u32[]{:S(2)}) collective-permute-start(bf16[256,1280]{1,0:T(8,128)(2,1)S(1)} %constant_dynamic-update-slice_fusion.next_ref), channel_id=1, source_target_pairs={{0,1},{1,0},{2,3},{3,2},{4,5},{5,4},{6,7},{7,6},{8,9},{9,8},{10,11... | collective-permute-start | bytes 1966088 | tf_op jit(solution)/shard_map/cond/branch_1_fun/ppermute | solution.py:551
  34.1 0.0 collective-permute-done.32.other_ref
  34.2 1.8 %distances.3 = (f32[768,256]{1,0:T(8,128)S(1)}, bf16[256,1280]{1,0:T(8,128)(2,1)S(1)}) custom-call(bf16[256,1792]{1,0:T(8,128)(2,1)S(1)} %pad_maximum_fusion.8.mine_ref, bf16[256,1792]{1,0:T(8,128)(2,1)S(1)} %collective-permute-done.32.other_ref, bf16[256,1280]{1,0:T(8,128)(2,1)S(1)} %constant_dynamic-update-slice_fusion.next_ref, ...), custom_call_target="tpu_custom_call" | custom-call | flops 704643072 | bytes 3670016 | tf_op jit(solution)/shard_map/cond/branch_1_fun/distances/pallas_call | solution.py:366
  36.0 0.0 collective-permute-done.35.other_ref
  36.0 2.3 %predict.3 = (f32[608,128]{1,0:T(8,128)S(1)}, f32[608,128]{1,0:T(8,128)S(1)}, bf16[2304,256]{1,0:T(8,128)(2,1)S(1)}) custom-call(bf16[256,1280]{1,0:T(8,128)(2,1)S(1)} %get-tuple-element.70.found_ref, bf16[256,1280]{1,0:T(8,128)(2,1)S(1)} %collective-permute-done.35.other_ref, bf16[256,512]{1,0:T(8,128)(2,1)S(1)} %select_packed.1.select_ref, ...), custom_call_target="tpu_custom_call" | custom-call | flops 1220542464 | bytes 5111808 | tf_op jit(solution)/shard_map/cond/branch_1_fun/predict/pallas_call | solution.py:388
  38.2 0.3 collective-permute-start.43
  38.6 1.0 %predict_more.3 = (f32[608,128]{1,0:T(8,128)S(1)}, f32[608,128]{1,0:T(8,128)S(1)}) custom-call(bf16[608,2304]{1,0:T(8,128)(2,1)S(1)} %get-tuple-element.66.left, bf16[2304,256]{1,0:T(8,128)(2,1)S(1)} %get-tuple-element.73.right), custom_call_target="tpu_custom_call" | custom-call | flops 717225984 | bytes 3112960 | tf_op jit(solution)/shard_map/cond/branch_1_fun/predict_more/pallas_call | solution.py:408
  39.6 0.3 collective-permute-start.36
  39.9 0.0 collective-permute-done.43
  39.9 0.0 copy-start.4
  40.0 0.0 copy-start.12
  40.0 1.8 %collective-permute-start.44 = (f32[304,128]{1,0:T(8,128)S(1)}, f32[304,128]{1,0:T(8,128)S(1)}, u32[]{:S(2)}, u32[]{:S(2)}) collective-permute-start(f32[304,128]{1,0:T(8,128)S(1)} %slice.96), channel_id=1, source_target_pairs={{0,2},{1,5},{2,0},{3,7},{4,6},{5,1},{6,4},{7,3},{8,10},{9,13},{10,... | collective-permute-start | bytes 466952 | tf_op jit(solution)/shard_map/cond/branch_1_fun/ppermute | solution.py:551
  41.9 1.3 %collective-permute-start.37 = (f32[304,128]{1,0:T(8,128)S(1)}, f32[304,128]{1,0:T(8,128)S(1)}, u32[]{:S(2)}, u32[]{:S(2)}) collective-permute-start(f32[304,128]{1,0:T(8,128)S(1)} %slice.92), channel_id=1, source_target_pairs={{0,2},{1,5},{2,0},{3,7},{4,6},{5,1},{6,4},{7,3},{8,10},{9,13},{10,... | collective-permute-start | bytes 466952 | tf_op jit(solution)/shard_map/cond/branch_1_fun/ppermute | solution.py:551
  43.1 1.6 %collective-permute-done.44 = f32[304,128]{1,0:T(8,128)S(1)} collective-permute-done((f32[304,128]{1,0:T(8,128)S(1)}, f32[304,128]{1,0:T(8,128)S(1)}, u32[]{:S(2)}, u32[]{:S(2)}) %collective-permute-start.44) | collective-permute-done | bytes 155680 | tf_op jit(solution)/shard_map/cond/branch_1_fun/ppermute | solution.py:551
  44.7 1.3 %collective-permute-start.45 = (f32[152,128]{1,0:T(8,128)S(1)}, f32[152,128]{1,0:T(8,128)S(1)}, u32[]{:S(2)}, u32[]{:S(2)}) collective-permute-start(f32[152,128]{1,0:T(8,128)S(1)} %slice.98), channel_id=1, source_target_pairs={{0,4},{1,3},{2,6},{3,1},{4,0},{5,7},{6,2},{7,5},{8,12},{9,11},{10,... | collective-permute-start | bytes 233480 | tf_op jit(solution)/shard_map/cond/branch_1_fun/ppermute | solution.py:551
  46.1 0.3 collective-permute-done.37
  46.4 1.3 %collective-permute-start.38 = (f32[152,128]{1,0:T(8,128)S(1)}, f32[152,128]{1,0:T(8,128)S(1)}, u32[]{:S(2)}, u32[]{:S(2)}) collective-permute-start(f32[152,128]{1,0:T(8,128)S(1)} %slice.94), channel_id=1, source_target_pairs={{0,4},{1,3},{2,6},{3,1},{4,0},{5,7},{6,2},{7,5},{8,12},{9,11},{10,... | collective-permute-start | bytes 233480 | tf_op jit(solution)/shard_map/cond/branch_1_fun/ppermute | solution.py:551
  47.7 0.3 collective-permute-done.45
  48.1 3.2 %collective-permute-start.46 = (f32[152,128]{1,0:T(8,128)S(1)}, f32[152,128]{1,0:T(8,128)S(1)}, u32[]{:S(2)}, u32[]{:S(2)}) collective-permute-start(f32[152,128]{1,0:T(8,128)S(1)} %slice_add_fusion.10), channel_id=1, source_target_pairs={{0,8},{1,9},{2,10},{3,11},{4,12},{5,13},{6,14},{7,15},{8,0},{9,1},... | collective-permute-start | bytes 233480 | tf_op jit(solution)/shard_map/cond/branch_1_fun/ppermute | solution.py:551
  51.2 0.0 collective-permute-done.38
  51.2 1.6 %collective-permute-start.39 = (f32[152,128]{1,0:T(8,128)S(1)}, f32[152,128]{1,0:T(8,128)S(1)}, u32[]{:S(2)}, u32[]{:S(2)}) collective-permute-start(f32[152,128]{1,0:T(8,128)S(1)} %slice_add_fusion.11), channel_id=1, source_target_pairs={{0,8},{1,9},{2,10},{3,11},{4,12},{5,13},{6,14},{7,15},{8,0},{9,1},... | collective-permute-start | bytes 233480 | tf_op jit(solution)/shard_map/cond/branch_1_fun/ppermute | solution.py:551
  52.9 0.1 collective-permute-done.46
  53.0 1.3 %collective-permute-start.47 = (f32[152,128]{1,0:T(8,128)S(1)}, f32[152,128]{1,0:T(8,128)S(1)}, u32[]{:S(2)}, u32[]{:S(2)}) collective-permute-start(f32[152,128]{1,0:T(8,128)S(1)} %add.135), channel_id=1, source_target_pairs={{0,4},{1,3},{2,6},{3,1},{4,0},{5,7},{6,2},{7,5},{8,12},{9,11},{10,... | collective-permute-start | bytes 233480 | tf_op jit(solution)/shard_map/cond/branch_1_fun/ppermute | solution.py:551
  54.4 4.0 %collective-permute-done.39 = f32[152,128]{1,0:T(8,128)S(1)} collective-permute-done((f32[152,128]{1,0:T(8,128)S(1)}, f32[152,128]{1,0:T(8,128)S(1)}, u32[]{:S(2)}, u32[]{:S(2)}) %collective-permute-start.39) | collective-permute-done | bytes 77856 | tf_op jit(solution)/shard_map/cond/branch_1_fun/ppermute | solution.py:551
  58.4 1.3 %collective-permute-start.40 = (f32[152,128]{1,0:T(8,128)S(1)}, f32[152,128]{1,0:T(8,128)S(1)}, u32[]{:S(2)}, u32[]{:S(2)}) collective-permute-start(f32[152,128]{1,0:T(8,128)S(1)} %add.131), channel_id=1, source_target_pairs={{0,4},{1,3},{2,6},{3,1},{4,0},{5,7},{6,2},{7,5},{8,12},{9,11},{10,... | collective-permute-start | bytes 233480 | tf_op jit(solution)/shard_map/cond/branch_1_fun/ppermute | solution.py:551
  59.7 0.0 collective-permute-done.47
  59.8 0.1 collective-permute-start.48
  59.8 2.2 %collective-permute-done.40 = f32[152,128]{1,0:T(8,128)S(1)} collective-permute-done((f32[152,128]{1,0:T(8,128)S(1)}, f32[152,128]{1,0:T(8,128)S(1)}, u32[]{:S(2)}, u32[]{:S(2)}) %collective-permute-start.40) | collective-permute-done | bytes 77856 | tf_op jit(solution)/shard_map/cond/branch_1_fun/ppermute | solution.py:551
  62.0 0.1 collective-permute-start.41
  62.1 2.7 %collective-permute-done.48 = f32[304,128]{1,0:T(8,128)S(1)} collective-permute-done((f32[304,128]{1,0:T(8,128)S(1)}, f32[304,128]{1,0:T(8,128)S(1)}, u32[]{:S(2)}, u32[]{:S(2)}) %collective-permute-start.48) | collective-permute-done | bytes 155680 | tf_op jit(solution)/shard_map/cond/branch_1_fun/ppermute | solution.py:551
  64.9 3.9 %collective-permute-start.49 = (f32[608,128]{1,0:T(8,128)S(1)}, f32[608,128]{1,0:T(8,128)S(1)}, u32[]{:S(2)}, u32[]{:S(2)}) collective-permute-start(f32[608,128]{1,0:T(8,128)S(1)} %pad_maximum_fusion.12.mine_ref), channel_id=1, source_target_pairs={{0,1},{1,0},{2,3},{3,2},{4,5},{5,4},{6,7},{7,6},{8,9},{9,8},{10,11... | collective-permute-start | bytes 933896 | tf_op jit(solution)/shard_map/cond/branch_1_fun/ppermute | solution.py:551
  68.8 0.0 collective-permute-done.41
  68.8 2.1 %collective-permute-start.42 = (f32[608,128]{1,0:T(8,128)S(1)}, f32[608,128]{1,0:T(8,128)S(1)}, u32[]{:S(2)}, u32[]{:S(2)}) collective-permute-start(f32[608,128]{1,0:T(8,128)S(1)} %pad_maximum_fusion.11.mine_ref), channel_id=1, source_target_pairs={{0,1},{1,0},{2,3},{3,2},{4,5},{5,4},{6,7},{7,6},{8,9},{9,8},{10,11... | collective-permute-start | bytes 933896 | tf_op jit(solution)/shard_map/cond/branch_1_fun/ppermute | solution.py:551
  70.9 0.0 collective-permute-done.49.other_ref
  70.9 2.2 %update.3 = (f32[1000,768]{1,0:T(8,128)}, f32[1000,256]{1,0:T(8,128)}, bf16[768,768]{1,0:T(8,128)(2,1)S(1)}) custom-call(f32[608,128]{1,0:T(8,128)S(1)} %pad_maximum_fusion.12.mine_ref, f32[608,128]{1,0:T(8,128)S(1)} %collective-permute-done.49.other_ref, f32[1000,256]{1,0:T(8,128)S(1)} %copy-done.4, s32[1,256]{1,0:T(1,128)S(1)} %copy-done.8, ...), custom_call_target="tpu_custom_call" | custom-call | flops 717225984 | bytes 3670016 | tf_op jit(solution)/shard_map/cond/branch_1_fun/update/pallas_call | solution.py:490
  73.1 0.0 collective-permute-done.42.other_ref
  73.1 1.9 %update_more.3 = (f32[1000,768]{1,0:T(8,128)}, f32[1000,256]{1,0:T(8,128)}) custom-call(f32[608,128]{1,0:T(8,128)S(1)} %pad_maximum_fusion.11.mine_ref, f32[608,128]{1,0:T(8,128)S(1)} %collective-permute-done.42.other_ref, f32[1000,256]{1,0:T(8,128)S(1)} %copy-done.4, f32[1000,768]{1,0:T(8,128)S(1)} %copy-done.2, ...), custom_call_target="tpu_custom_call", output_to_operand_aliasing={{0}: (5, {}), {1}: (6, {})} | custom-call | flops 651165696 | bytes 4521984 | tf_op jit(solution)/shard_map/cond/branch_1_fun/update_more/pallas_call | solution.py:527
  (31 shorter events, 0.4 us)
Async XLA Ops:
  5.5 5.7 %copy-start.8 = (s32[1,256]{1,0:T(1,128)S(1)}, s32[1,256]{1,0:T(1,128)}, u32[]{:S(2)}) copy-start(s32[1,256]{1,0:T(1,128)} %get-tuple-element.58.index_hbm.index_ref) | copy-start | bytes 3076 | tf_op jit(solution)/shard_map/cond
  5.5 5.9 %copy-start.10 = (s32[320]{0:T(512)S(1)}, s32[320]{0:T(512)}, u32[]{:S(2)}) copy-start(s32[320]{0:T(512)} %get-tuple-element.60) | copy-start | bytes 3844 | tf_op jit(solution)/shard_map/cond
  5.5 6.0 %copy-start = (bf16[768,3072]{1,0:T(8,128)(2,1)S(1)}, bf16[768,3072]{1,0:T(8,128)(2,1)}, u32[]{:S(2)}) copy-start(bf16[768,3072]{1,0:T(8,128)(2,1)} %get-tuple-element.59.centers_hbm.centers_ref) | copy-start | bytes 14155780 | tf_op jit(solution)/shard_map/cond
  5.5 9.0 %collective-permute-start.29 = (bf16[32,1792]{1,0:T(8,128)(2,1)S(1)}, bf16[32,1792]{1,0:T(8,128)(2,1)S(1)}, u32[]{:S(2)}, u32[]{:S(2)}) collective-permute-start(bf16[32,1792]{1,0:T(8,128)(2,1)S(1)} %pack_rows.3), channel_id=1, source_target_pairs={{0,8},{1,9},{2,10},{3,11},{4,12},{5,13},{6,14},{7,15},{8,0},{9,1},... | collective-permute-start | bytes 344072 | tf_op jit(solution)/shard_map/cond/branch_1_fun/ppermute | solution.py:551
  10.9 1.9 %copy-start.2 = (f32[1000,768]{1,0:T(8,128)S(1)}, f32[1000,768]{1,0:T(8,128)}, u32[]{:S(2)}) copy-start(f32[1000,768]{1,0:T(8,128)} %get-tuple-element.62.weights_ref) | copy-start | bytes 9216004 | tf_op jit(solution)/shard_map/cond
  10.9 1.9 %copy-start.6 = (f32[160,320]{1,0:T(8,128)S(1)}, f32[160,320]{1,0:T(8,128)}, u32[]{:S(2)}) copy-start(f32[160,320]{1,0:T(8,128)} %get-tuple-element.61.eigvec_ref) | copy-start | bytes 614404 | tf_op jit(solution)/shard_map/cond
  11.0 5.4 %collective-permute-start.28 = (bf16[32,1280]{1,0:T(8,128)(2,1)S(1)}, bf16[32,1280]{1,0:T(8,128)(2,1)S(1)}, u32[]{:S(2)}, u32[]{:S(2)}) collective-permute-start(bf16[32,1280]{1,0:T(8,128)(2,1)S(1)} %pack_rows.2), channel_id=1, source_target_pairs={{0,8},{1,9},{2,10},{3,11},{4,12},{5,13},{6,14},{7,15},{8,0},{9,1},... | collective-permute-start | bytes 245768 | tf_op jit(solution)/shard_map/cond/branch_1_fun/ppermute | solution.py:551
  14.5 5.2 %collective-permute-start.30 = (bf16[64,1792]{1,0:T(8,128)(2,1)S(1)}, bf16[64,1792]{1,0:T(8,128)(2,1)S(1)}, u32[]{:S(2)}, u32[]{:S(2)}) collective-permute-start(bf16[64,1792]{1,0:T(8,128)(2,1)S(1)} %pad_maximum_fusion.13), channel_id=1, source_target_pairs={{0,4},{1,3},{2,6},{3,1},{4,0},{5,7},{6,2},{7,5},{8,12},{9,11},{10,... | collective-permute-start | bytes 688136 | tf_op jit(solution)/shard_map/cond/branch_1_fun/ppermute | solution.py:551
  16.4 6.0 %collective-permute-start.33 = (bf16[64,1280]{1,0:T(8,128)(2,1)S(1)}, bf16[64,1280]{1,0:T(8,128)(2,1)S(1)}, u32[]{:S(2)}, u32[]{:S(2)}) collective-permute-start(bf16[64,1280]{1,0:T(8,128)(2,1)S(1)} %pad_maximum_fusion.14), channel_id=1, source_target_pairs={{0,4},{1,3},{2,6},{3,1},{4,0},{5,7},{6,2},{7,5},{8,12},{9,11},{10,... | collective-permute-start | bytes 491528 | tf_op jit(solution)/shard_map/cond/branch_1_fun/ppermute | solution.py:551
  19.8 8.9 %collective-permute-start.31 = (bf16[128,1792]{1,0:T(8,128)(2,1)S(1)}, bf16[128,1792]{1,0:T(8,128)(2,1)S(1)}, u32[]{:S(2)}, u32[]{:S(2)}) collective-permute-start(bf16[128,1792]{1,0:T(8,128)(2,1)S(1)} %pad_maximum_fusion.9), channel_id=1, source_target_pairs={{0,2},{1,5},{2,0},{3,7},{4,6},{5,1},{6,4},{7,3},{8,10},{9,13},{10,... | collective-permute-start | bytes 1376264 | tf_op jit(solution)/shard_map/cond/branch_1_fun/ppermute | solution.py:551
  22.4 9.8 %collective-permute-start.34 = (bf16[128,1280]{1,0:T(8,128)(2,1)S(1)}, bf16[128,1280]{1,0:T(8,128)(2,1)S(1)}, u32[]{:S(2)}, u32[]{:S(2)}) collective-permute-start(bf16[128,1280]{1,0:T(8,128)(2,1)S(1)} %pad_maximum_fusion.10), channel_id=1, source_target_pairs={{0,2},{1,5},{2,0},{3,7},{4,6},{5,1},{6,4},{7,3},{8,10},{9,13},{10,... | collective-permute-start | bytes 983048 | tf_op jit(solution)/shard_map/cond/branch_1_fun/ppermute | solution.py:551
  28.8 5.3 %collective-permute-start.32 = (bf16[256,1792]{1,0:T(8,128)(2,1)S(1)}, bf16[256,1792]{1,0:T(8,128)(2,1)S(1)}, u32[]{:S(2)}, u32[]{:S(2)}) collective-permute-start(bf16[256,1792]{1,0:T(8,128)(2,1)S(1)} %pad_maximum_fusion.8.mine_ref), channel_id=1, source_target_pairs={{0,1},{1,0},{2,3},{3,2},{4,5},{5,4},{6,7},{7,6},{8,9},{9,8},{10,11... | collective-permute-start | bytes 2752520 | tf_op jit(solution)/shard_map/cond/branch_1_fun/ppermute | solution.py:551
  32.3 3.7 %collective-permute-start.35 = (bf16[256,1280]{1,0:T(8,128)(2,1)S(1)}, bf16[256,1280]{1,0:T(8,128)(2,1)S(1)}, u32[]{:S(2)}, u32[]{:S(2)}) collective-permute-start(bf16[256,1280]{1,0:T(8,128)(2,1)S(1)} %constant_dynamic-update-slice_fusion.next_ref), channel_id=1, source_target_pairs={{0,1},{1,0},{2,3},{3,2},{4,5},{5,4},{6,7},{7,6},{8,9},{9,8},{10,11... | collective-permute-start | bytes 1966088 | tf_op jit(solution)/shard_map/cond/branch_1_fun/ppermute | solution.py:551
  38.2 1.7 %collective-permute-start.43 = (f32[608,128]{1,0:T(8,128)S(1)}, f32[608,128]{1,0:T(8,128)S(1)}, u32[]{:S(2)}, u32[]{:S(2)}) collective-permute-start(f32[608,128]{1,0:T(8,128)S(1)} %get-tuple-element.78), channel_id=1, source_target_pairs={{0,1},{1,0},{2,3},{3,2},{4,5},{5,4},{6,7},{7,6},{8,9},{9,8},{10,11... | collective-permute-start | bytes 933896 | tf_op jit(solution)/shard_map/cond/branch_1_fun/ppermute | solution.py:551
  39.6 2.2 %collective-permute-start.36 = (f32[608,128]{1,0:T(8,128)S(1)}, f32[608,128]{1,0:T(8,128)S(1)}, u32[]{:S(2)}, u32[]{:S(2)}) collective-permute-start(f32[608,128]{1,0:T(8,128)S(1)} %get-tuple-element.75), channel_id=1, source_target_pairs={{0,1},{1,0},{2,3},{3,2},{4,5},{5,4},{6,7},{7,6},{8,9},{9,8},{10,11... | collective-permute-start | bytes 933896 | tf_op jit(solution)/shard_map/cond/branch_1_fun/ppermute | solution.py:551
  39.9 30.9 %copy-start.4 = (f32[1000,256]{1,0:T(8,128)S(1)}, f32[1000,256]{1,0:T(8,128)}, u32[]{:S(2)}) copy-start(f32[1000,256]{1,0:T(8,128)} %get-tuple-element.76.targets_ref) | copy-start | bytes 3072004 | tf_op jit(solution)/shard_map/cond
  40.0 30.9 %copy-start.12 = (f32[1,160]{1,0:T(1,128)S(1)}, f32[1,160]{1,0:T(1,128)}, u32[]{:S(2)}) copy-start(f32[1,160]{1,0:T(1,128)} %get-tuple-element.79.eigval_ref) | copy-start | bytes 1924 | tf_op jit(solution)/shard_map/cond
  40.0 4.7 %collective-permute-start.44 = (f32[304,128]{1,0:T(8,128)S(1)}, f32[304,128]{1,0:T(8,128)S(1)}, u32[]{:S(2)}, u32[]{:S(2)}) collective-permute-start(f32[304,128]{1,0:T(8,128)S(1)} %slice.96), channel_id=1, source_target_pairs={{0,2},{1,5},{2,0},{3,7},{4,6},{5,1},{6,4},{7,3},{8,10},{9,13},{10,... | collective-permute-start | bytes 466952 | tf_op jit(solution)/shard_map/cond/branch_1_fun/ppermute | solution.py:551
  41.9 4.5 %collective-permute-start.37 = (f32[304,128]{1,0:T(8,128)S(1)}, f32[304,128]{1,0:T(8,128)S(1)}, u32[]{:S(2)}, u32[]{:S(2)}) collective-permute-start(f32[304,128]{1,0:T(8,128)S(1)} %slice.92), channel_id=1, source_target_pairs={{0,2},{1,5},{2,0},{3,7},{4,6},{5,1},{6,4},{7,3},{8,10},{9,13},{10,... | collective-permute-start | bytes 466952 | tf_op jit(solution)/shard_map/cond/branch_1_fun/ppermute | solution.py:551
  44.7 3.3 %collective-permute-start.45 = (f32[152,128]{1,0:T(8,128)S(1)}, f32[152,128]{1,0:T(8,128)S(1)}, u32[]{:S(2)}, u32[]{:S(2)}) collective-permute-start(f32[152,128]{1,0:T(8,128)S(1)} %slice.98), channel_id=1, source_target_pairs={{0,4},{1,3},{2,6},{3,1},{4,0},{5,7},{6,2},{7,5},{8,12},{9,11},{10,... | collective-permute-start | bytes 233480 | tf_op jit(solution)/shard_map/cond/branch_1_fun/ppermute | solution.py:551
  46.4 4.8 %collective-permute-start.38 = (f32[152,128]{1,0:T(8,128)S(1)}, f32[152,128]{1,0:T(8,128)S(1)}, u32[]{:S(2)}, u32[]{:S(2)}) collective-permute-start(f32[152,128]{1,0:T(8,128)S(1)} %slice.94), channel_id=1, source_target_pairs={{0,4},{1,3},{2,6},{3,1},{4,0},{5,7},{6,2},{7,5},{8,12},{9,11},{10,... | collective-permute-start | bytes 233480 | tf_op jit(solution)/shard_map/cond/branch_1_fun/ppermute | solution.py:551
  48.1 4.9 %collective-permute-start.46 = (f32[152,128]{1,0:T(8,128)S(1)}, f32[152,128]{1,0:T(8,128)S(1)}, u32[]{:S(2)}, u32[]{:S(2)}) collective-permute-start(f32[152,128]{1,0:T(8,128)S(1)} %slice_add_fusion.10), channel_id=1, source_target_pairs={{0,8},{1,9},{2,10},{3,11},{4,12},{5,13},{6,14},{7,15},{8,0},{9,1},... | collective-permute-start | bytes 233480 | tf_op jit(solution)/shard_map/cond/branch_1_fun/ppermute | solution.py:551
  51.2 7.1 %collective-permute-start.39 = (f32[152,128]{1,0:T(8,128)S(1)}, f32[152,128]{1,0:T(8,128)S(1)}, u32[]{:S(2)}, u32[]{:S(2)}) collective-permute-start(f32[152,128]{1,0:T(8,128)S(1)} %slice_add_fusion.11), channel_id=1, source_target_pairs={{0,8},{1,9},{2,10},{3,11},{4,12},{5,13},{6,14},{7,15},{8,0},{9,1},... | collective-permute-start | bytes 233480 | tf_op jit(solution)/shard_map/cond/branch_1_fun/ppermute | solution.py:551
  53.0 6.7 %collective-permute-start.47 = (f32[152,128]{1,0:T(8,128)S(1)}, f32[152,128]{1,0:T(8,128)S(1)}, u32[]{:S(2)}, u32[]{:S(2)}) collective-permute-start(f32[152,128]{1,0:T(8,128)S(1)} %add.135), channel_id=1, source_target_pairs={{0,4},{1,3},{2,6},{3,1},{4,0},{5,7},{6,2},{7,5},{8,12},{9,11},{10,... | collective-permute-start | bytes 233480 | tf_op jit(solution)/shard_map/cond/branch_1_fun/ppermute | solution.py:551
  58.4 3.6 %collective-permute-start.40 = (f32[152,128]{1,0:T(8,128)S(1)}, f32[152,128]{1,0:T(8,128)S(1)}, u32[]{:S(2)}, u32[]{:S(2)}) collective-permute-start(f32[152,128]{1,0:T(8,128)S(1)} %add.131), channel_id=1, source_target_pairs={{0,4},{1,3},{2,6},{3,1},{4,0},{5,7},{6,2},{7,5},{8,12},{9,11},{10,... | collective-permute-start | bytes 233480 | tf_op jit(solution)/shard_map/cond/branch_1_fun/ppermute | solution.py:551
  59.8 5.1 %collective-permute-start.48 = (f32[304,128]{1,0:T(8,128)S(1)}, f32[304,128]{1,0:T(8,128)S(1)}, u32[]{:S(2)}, u32[]{:S(2)}) collective-permute-start(f32[304,128]{1,0:T(8,128)S(1)} %pad_maximum_fusion.16), channel_id=1, source_target_pairs={{0,2},{1,5},{2,0},{3,7},{4,6},{5,1},{6,4},{7,3},{8,10},{9,13},{10,... | collective-permute-start | bytes 466952 | tf_op jit(solution)/shard_map/cond/branch_1_fun/ppermute | solution.py:551
  62.0 6.7 %collective-permute-start.41 = (f32[304,128]{1,0:T(8,128)S(1)}, f32[304,128]{1,0:T(8,128)S(1)}, u32[]{:S(2)}, u32[]{:S(2)}) collective-permute-start(f32[304,128]{1,0:T(8,128)S(1)} %pad_maximum_fusion.15), channel_id=1, source_target_pairs={{0,2},{1,5},{2,0},{3,7},{4,6},{5,1},{6,4},{7,3},{8,10},{9,13},{10,... | collective-permute-start | bytes 466952 | tf_op jit(solution)/shard_map/cond/branch_1_fun/ppermute | solution.py:551
  64.9 6.0 %collective-permute-start.49 = (f32[608,128]{1,0:T(8,128)S(1)}, f32[608,128]{1,0:T(8,128)S(1)}, u32[]{:S(2)}, u32[]{:S(2)}) collective-permute-start(f32[608,128]{1,0:T(8,128)S(1)} %pad_maximum_fusion.12.mine_ref), channel_id=1, source_target_pairs={{0,1},{1,0},{2,3},{3,2},{4,5},{5,4},{6,7},{7,6},{8,9},{9,8},{10,11... | collective-permute-start | bytes 933896 | tf_op jit(solution)/shard_map/cond/branch_1_fun/ppermute | solution.py:551
  68.8 4.3 %collective-permute-start.42 = (f32[608,128]{1,0:T(8,128)S(1)}, f32[608,128]{1,0:T(8,128)S(1)}, u32[]{:S(2)}, u32[]{:S(2)}) collective-permute-start(f32[608,128]{1,0:T(8,128)S(1)} %pad_maximum_fusion.11.mine_ref), channel_id=1, source_target_pairs={{0,1},{1,0},{2,3},{3,2},{4,5},{5,4},{6,7},{7,6},{8,9},{9,8},{10,11... | collective-permute-start | bytes 933896 | tf_op jit(solution)/shard_map/cond/branch_1_fun/ppermute | solution.py:551

commit v15 on v13

--- a/solution.py
+++ b/solution.py
@@ -16,6 +16,7 @@
 LANE = 128
 PARTS = 2
 SLOTS = 32
+GROUP_SLOTS = 96
 BLOCKS = 2
 NT = (((1,), (1,)), ((), ()))
 NN = (((1,), (0,)), ((), ()))
@@ -124,15 +125,32 @@
     )(batch_index, centers)
 
 
+def group_of(device, chips):
+    bits = chips.bit_length() - 1
+    masks = [sum(1 << bit for bit in far_first(sub, bits)[:2]) for sub in range(2)]
+    center = device >> 1
+    return (jnp.where((device & 1) == 0, center & ~masks[0], center & ~masks[1]) << 1) + (device & 1)
+
+
+def owners(index, count, chips):
+    owner = jnp.zeros_like(index)
+    for device in range(1, 2 * chips):
+        owner = owner + jnp.where(index >= device * count, 1, 0)
+    return owner
+
+
 def fits_body(count, index_hbm, fits_ref, index_ref, sem):
     copy = pltpu.make_async_copy(index_hbm, index_ref, sem)
     copy.start()
     copy.wait()
-    devices = 2 * lax.axis_size("center")
-    starts = lax.broadcasted_iota(jnp.int32, (devices, 1), 0) * count
-    local = index_ref[...] - starts
-    held = jnp.sum(jnp.where((local >= 0) & (local < count), 1.0, 0.0), axis=1, keepdims=True)
-    fits_ref[0] = (jnp.max(held) <= SLOTS).astype(jnp.int32)
+    chips = lax.axis_size("center")
+    owner = owners(index_ref[...], count, chips)
+    device = lax.broadcasted_iota(jnp.int32, (2 * chips, 1), 0)
+    held = jnp.sum(jnp.where(owner == device, 1.0, 0.0), axis=1, keepdims=True)
+    same = group_of(owner, chips) == group_of(device, chips)
+    shared = jnp.sum(jnp.where(same, 1.0, 0.0), axis=1, keepdims=True)
+    over = jnp.max(jnp.maximum(held - SLOTS, shared - GROUP_SLOTS))
+    fits_ref[0] = (over <= 0.0).astype(jnp.int32)
 
 
 def rows_fit(batch_index, count):
@@ -196,38 +214,72 @@
     )(batch_index, centers)
 
 
-def select_body(count, index_ref, select_ref):
+def select_body(count, index_ref, select_ref, squeeze_ref):
     rows, slots = select_ref.shape
-    chips = slots // (2 * SLOTS)
-    index = index_ref[...]
-    owner = jnp.zeros_like(index)
-    for device in range(1, 2 * chips):
-        owner = owner + jnp.where(index >= device * count, 1, 0)
-    column = column_of(owner, LANE)
-    same = jnp.concatenate([column] * (rows // LANE), axis=1) == owner.astype(F32)
+    chips = lax.axis_size("center")
+    center, sub = lax.axis_index("center"), lax.axis_index("sub")
+    owner = owners(index_ref[...], count, chips)
+    group = group_of(owner, chips)
     earlier = lax.broadcasted_iota(jnp.int32, (rows, rows), 0) < lax.broadcasted_iota(jnp.int32, (rows, rows), 1)
-    rank = jnp.sum(jnp.where(same & earlier, 1.0, 0.0), axis=0, keepdims=True)
-    away = (owner >> 1) ^ lax.axis_index("center")
-    places = [
-        sum(((away >> bit) & 1) << k for k, bit in enumerate(far_first(sub, chips.bit_length() - 1)))
-        for sub in range(2)
-    ]
-    place = jnp.where((owner & 1) == 0, *places)
-    far = jnp.where((owner & 1) == lax.axis_index("sub"), 0, chips * SLOTS)
-    slot = column_of((far + place * SLOTS).astype(F32) + rank, LANE)
+
+    def rank_among(key):
+        column = jnp.concatenate([column_of(key, LANE)] * (rows // LANE), axis=1)
+        return jnp.sum(jnp.where((column == key.astype(F32)) & earlier, 1.0, 0.0), axis=0, keepdims=True)
+
+    away = (owner >> 1) ^ center
+    orders = [far_first(side, chips.bit_length() - 1) for side in range(2)]
+
+    def place(low, high):
+        places = [
+            sum(((away >> bit) & 1) << k for k, bit in enumerate(order[low:high])) + jnp.zeros_like(away)
+            for order in orders
+        ]
+        return jnp.where((owner & 1) == 0, *places).astype(F32)
+
     lanes = lax.broadcasted_iota(jnp.int32, (1, LANE), 1).astype(F32)
+    rank = rank_among(group)
+    far = jnp.where((owner & 1) == sub, 0, slots // 2).astype(F32)
+    slot = column_of(far + place(2, None) * float(GROUP_SLOTS) + rank, LANE)
     for k in range(slots // LANE):
         select_ref[:, k * LANE : (k + 1) * LANE] = jnp.where(slot == lanes + float(LANE * k), 1.0, 0.0).astype(BF16)
+    before = column_of(place(0, 2) * float(SLOTS) + rank_among(owner), LANE)
+    spots = lax.broadcasted_iota(jnp.int32, (GROUP_SLOTS, 1), 0).astype(F32)
+    mine = group == group_of(center * 2 + sub, chips)
+    to_spot = jnp.where((spots == rank) & mine, 1.0, 0.0).astype(BF16)
+    squeeze_ref[...] = dot(to_spot, jnp.where(before == lanes, 1.0, 0.0).astype(BF16), NN).astype(BF16)
 
 
 def select_packed(batch_index, count, chips):
     rows = batch_index.shape[1]
+    half = -(-chips // 4 * GROUP_SLOTS // LANE) * LANE
     return pl.pallas_call(
         functools.partial(select_body, count),
-        out_shape=jax.ShapeDtypeStruct((rows, 2 * chips * SLOTS), BF16),
+        out_shape=[
+            jax.ShapeDtypeStruct((rows, 2 * half), BF16),
+            jax.ShapeDtypeStruct((GROUP_SLOTS, 4 * SLOTS), BF16),
+        ],
         compiler_params=params(),
         name="select_packed",
     )(batch_index)
+
+
+def squeeze_body(squeeze_ref, keep_ref, got_ref, out_ref):
+    rows = keep_ref.shape[0]
+    found = dot(squeeze_ref[:, :rows], keep_ref[...], NN) + dot(squeeze_ref[:, rows:], got_ref[...], NN)
+    out_ref[...] = found.astype(BF16)
+
+
+def squeeze_slots(squeeze, keep, got):
+    depth = keep.shape[1]
+    return pl.pallas_call(
+        squeeze_body,
+        out_shape=jax.ShapeDtypeStruct((squeeze.shape[0], depth), BF16),
+        compiler_params=params(),
+        cost_estimate=pl.CostEstimate(
+            flops=40 * squeeze.size * depth, bytes_accessed=4 * squeeze.shape[1] * depth, transcendentals=0
+        ),
+        name="squeeze_slots",
+    )(squeeze, keep, got)
 
 
 def spread_body(
@@ -326,8 +378,10 @@
 
 def distance_body(mine_ref, other_ref, next_ref, select_ref, centers_ref, norm_ref, total_ref, found_ref, batch_ref):
     half, depth = mine_ref.shape
+    wide = select_ref.shape[1] // 2
     near = select_ref[:, :half]
-    batch_ref[...] = (dot(near, mine_ref[...], NN) + dot(select_ref[:, half:], other_ref[...], NN)).astype(BF16)
+    far = select_ref[:, wide : wide + half]
+    batch_ref[...] = (dot(near, mine_ref[...], NN) + dot(far, other_ref[...], NN)).astype(BF16)
     total_ref[...] = norm_ref[:, 0:1] + row_norms(batch_ref) - 2.0 * dot(centers_ref[:, :depth], batch_ref[...], NT)
     found_ref[...] = dot(near, next_ref[...], NN).astype(BF16)
 
@@ -338,7 +392,8 @@
 ):
     count, depth = centers_ref.shape
     half, part = other_ref.shape
-    found = found_ref[...].astype(F32) + dot(select_ref[:, half:], other_ref[...], NN)
+    wide = select_ref.shape[1] // 2
+    found = found_ref[...].astype(F32) + dot(select_ref[:, wide : wide + half], other_ref[...], NN)
     batch_ref[...] = found.astype(BF16)
     norm = row_norms(batch_ref)
     size = count // BLOCKS
@@ -567,12 +622,20 @@
     return [keep, swap(keep, chips), *tied]
 
 
-def all_of(keep, chips, tied=()):
+def gathered(first, second, squeeze, chips, ready):
     for level in range(chips.bit_length() - 1):
-        if level == 1 and tied:
-            keep, tied = tie(keep, tied)
-        keep = jnp.concatenate([keep, swap(keep, chips, far_first, level)])
-    return [keep, swap(keep, chips), *tied]
+        if level == 1:
+            second, ready = tie(second, ready)
+        got = swap(first, chips, far_first, level)
+        late = swap(second, chips, far_first, level)
+        if level == 1:
+            got, _ = tie(got, [second])
+            first = squeeze_slots(squeeze, first, got)
+            second = squeeze_slots(squeeze, second, late)
+        else:
+            first = jnp.concatenate([first, got])
+            second = jnp.concatenate([second, late])
+    return [first, swap(first, chips), second, swap(second, chips), *ready]
 
 
 def one_hot(slot, slots):
@@ -600,10 +663,11 @@
     far = [pltpu.with_memory_space_constraint(x, pltpu.HBM) for x in (batch_index, centers)]
     ready = [center_norms(centers), *spread_weights(nys_index.reshape(1, -1), eigvec, weights, first, second)]
     if packed:
-        ready.append(select_packed(batch_index, count, chips))
+        select, squeeze = select_packed(batch_index, count, chips)
+        ready.append(select)
         slots = [pack_rows(*far, part) for part in range(PARTS)]
-        mine, other = all_of(slots[0], chips)
-        next_mine, next_other, norms, left1, left2, spread, select = all_of(slots[1], chips, ready)
+        mine, other, next_mine, next_other, *ready = gathered(*slots, squeeze, chips, ready)
+        norms, left1, left2, spread, select = ready
     else:
         ready.append(select_summed(rows))
         picked = [pick_batch(*far, part) for part in range(PARTS)]

time: 74.4 us -> 72.5 us (0.974)
  waiting for transfers between devices: 23.5 us -> 15.7 us
  starting transfers between devices: 30.7 us -> 36 us
  Pallas kernels: 17.4 us -> 18.2 us
    ppermute x22, waiting for transfers between devices: 23.5 us -> 15.7 us  [swap(): lax.ppermute(x, AXES, [(i, i ^ flip[i & 1]) for i in range(2 * chips)])]
    ppermute x22, starting transfers between devices: 30.7 us -> 36 us  [swap(): lax.ppermute(x, AXES, [(i, i ^ flip[i & 1]) for i in range(2 * chips)])]
    pallas_call x1 -> x3, Pallas kernels: 0.26 us -> 1.05 us  [the longest x2 0.68 us: squeeze_slots(): pl.pallas_call(squeeze_body, out_shape=jax.ShapeDtypeStruct((squeeze.shap...]
  transfers between devices with their start and end apart: 22 -> 22, of which waited for: 12 -> 11; matrix products, arithmetic and copies ran while one was open for 1% -> 1% of each run, Pallas kernels for 13% -> 15%
where the time goes in v15:
time: 72.5 us; the launch traced here: 72.3 us
  starting transfers between devices  36 us (50%)
  Pallas kernels  18.2 us (25%)
  waiting for transfers between devices  15.7 us (22%)
  between operations  1.45 us (2%)
    ppermute x22, starting transfers between devices, swap(): lax.ppermute(x, AXES, [(i, i ^ flip[i & 1]) for i in range(2 * chips)])  36 us
    ppermute x22, waiting for transfers between devices, swap(): lax.ppermute(x, AXES, [(i, i ^ flip[i & 1]) for i in range(2 * chips)])  15.7 us
    pallas_call x2, Pallas kernels, pack_rows(): pl.pallas_call(functools.partial(pack_body, part * depth), in_specs=[hbm,...  3.84 us
    pallas_call x1, Pallas kernels, predict(): pl.pallas_call(predict_body, in_specs=[vmem] * 6, out_specs=[vmem] * 3, o...  2.4 us
    pallas_call x1, Pallas kernels, update(): pl.pallas_call(update_body, in_specs=[vmem] * 7, out_specs=[hbm, hbm, vme...  2.23 us
    pallas_call x1, Pallas kernels, update_more(): pl.pallas_call(functools.partial(update_more_body, begin), in_specs=[vmem...  1.97 us
    pallas_call x1, Pallas kernels, spread_weights(): pl.pallas_call(functools.partial(spread_body, first, classes), out_shape=...  1.69 us
    pallas_call x1, Pallas kernels, distances(): pl.pallas_call(distance_body, in_specs=[vmem] * 6, out_specs=[vmem, vmem]...  1.46 us
  transfers between devices with their start and end apart: 22, of which 11 were waited for; matrix products, arithmetic and copies ran while one was open for 1% of the time, Pallas kernels for 15%

profile of v15, /device:TPU:1, one launch (start us, length us, event | category | flops | bytes accessed | tf_op | source)
XLA Modules:
  0.0 72.3 jit_solution(10502975645530380294)
XLA Ops:
  0.6 1.4 %rows_fit.1 = s32[1]{0:T(128)} custom-call(s32[1,256]{1,0:T(1,128)} %bitcast.17), custom_call_target="tpu_custom_call" | custom-call | tf_op jit(solution)/shard_map/rows_fit/pallas_call | solution.py:157
  2.6 69.5 %conditional.1 = ((f32[1000,768]{1,0:T(8,128)}, f32[1000,256]{1,0:T(8,128)})) conditional(s32[]{:T(128)} %bitcast.2, (s32[1,256]{1,0:T(1,128)}, bf16[768,3072]{1,0:T(8,128)(2,1)}, s32[320]{0:T(512)}, f32[160,320]{1,0:T(8,128)}, f32[1000,768]{1,0:T(8,128)}, /*index=5*/f32[1000,256]{1,0:T(8,128)}, f32[1,160]{1,0:T(1,128)}) %tuple.31, ...), branch_computations={%region_0.1_spmd, %region_1.2_spmd} | conditional | flops 5916241920 | bytes 106008064 | solution.py:686
  2.8 1.9 %pack_rows.3 = bf16[32,1536]{1,0:T(8,128)(2,1)S(1)} custom-call(s32[1,256]{1,0:T(1,128)} %get-tuple-element.58.index_hbm.index_ref, bf16[768,3072]{1,0:T(8,128)(2,1)} %get-tuple-element.59.centers_hbm.centers_ref), custom_call_target="tpu_custom_call" | custom-call | flops 75497472 | bytes 2457600 | tf_op jit(solution)/shard_map/cond/branch_1_fun/pack_rows/pallas_call | solution.py:199
  4.8 0.0 copy-start.8
  4.8 0.0 copy-start.10
  4.8 0.0 copy-start
  4.8 3.2 %collective-permute-start.29 = (bf16[32,1536]{1,0:T(8,128)(2,1)S(1)}, bf16[32,1536]{1,0:T(8,128)(2,1)S(1)}, u32[]{:S(2)}, u32[]{:S(2)}) collective-permute-start(bf16[32,1536]{1,0:T(8,128)(2,1)S(1)} %pack_rows.3), channel_id=1, source_target_pairs={{0,8},{1,9},{2,10},{3,11},{4,12},{5,13},{6,14},{7,15},{8,0},{9,1},... | collective-permute-start | bytes 294920 | tf_op jit(solution)/shard_map/cond/branch_1_fun/ppermute | solution.py:601
  8.0 1.9 %pack_rows.2 = bf16[32,1536]{1,0:T(8,128)(2,1)S(1)} custom-call(s32[1,256]{1,0:T(1,128)} %get-tuple-element.58.index_hbm.index_ref, bf16[768,3072]{1,0:T(8,128)(2,1)} %get-tuple-element.59.centers_hbm.centers_ref), custom_call_target="tpu_custom_call" | custom-call | flops 75497472 | bytes 2457600 | tf_op jit(solution)/shard_map/cond/branch_1_fun/pack_rows/pallas_call | solution.py:199
  9.9 0.0 copy-start.2
  9.9 0.0 copy-start.6
  10.0 0.2 collective-permute-start.28
  10.2 0.4 select_packed.1
  10.6 1.2 %center_norms.3.norm_ref = f32[768,128]{1,0:T(8,128)S(1)} custom-call(bf16[768,3072]{1,0:T(8,128)(2,1)S(1)} %copy-done), custom_call_target="tpu_custom_call" | custom-call | flops 4718592 | bytes 4718592 | tf_op jit(solution)/shard_map/cond/branch_1_fun/center_norms/pallas_call | solution.py:341
  11.8 0.0 copy-done.2
  11.8 1.7 %spread_weights.3 = (bf16[608,2304]{1,0:T(8,128)(2,1)S(1)}, bf16[608,2304]{1,0:T(8,128)(2,1)S(1)}, f32[160,768]{1,0:T(8,128)S(1)}) custom-call(s32[1,320]{1,0:T(1,128)S(1)} %reshape.99.index_ref, f32[160,320]{1,0:T(8,128)S(1)} %copy-done.6, f32[1000,768]{1,0:T(8,128)S(1)} %copy-done.2), custom_call_target="tpu_custom_call" | custom-call | flops 235929600 | bytes 7471104 | tf_op jit(solution)/shard_map/cond/branch_1_fun/spread_weights/pallas_call | solution.py:316
  13.5 0.0 collective-permute-done.29
  13.5 1.3 %collective-permute-start.30 = (bf16[64,1536]{1,0:T(8,128)(2,1)S(1)}, bf16[64,1536]{1,0:T(8,128)(2,1)S(1)}, u32[]{:S(2)}, u32[]{:S(2)}) collective-permute-start(bf16[64,1536]{1,0:T(8,128)(2,1)S(1)} %pad_maximum_fusion.13.keep_ref), channel_id=1, source_target_pairs={{0,4},{1,3},{2,6},{3,1},{4,0},{5,7},{6,2},{7,5},{8,12},{9,11},{10,... | collective-permute-start | bytes 589832 | tf_op jit(solution)/shard_map/cond/branch_1_fun/ppermute | solution.py:601
  14.9 0.0 collective-permute-done.28
  14.9 0.8 %collective-permute-start.33 = (bf16[64,1536]{1,0:T(8,128)(2,1)S(1)}, bf16[64,1536]{1,0:T(8,128)(2,1)S(1)}, u32[]{:S(2)}, u32[]{:S(2)}) collective-permute-start(bf16[64,1536]{1,0:T(8,128)(2,1)S(1)} %pad_maximum_fusion.12.keep_ref), channel_id=1, source_target_pairs={{0,4},{1,3},{2,6},{3,1},{4,0},{5,7},{6,2},{7,5},{8,12},{9,11},{10,... | collective-permute-start | bytes 589832 | tf_op jit(solution)/shard_map/cond/branch_1_fun/ppermute | solution.py:601
  15.7 2.7 %collective-permute-done.30.got_ref = bf16[64,1536]{1,0:T(8,128)(2,1)S(1)} collective-permute-done((bf16[64,1536]{1,0:T(8,128)(2,1)S(1)}, bf16[64,1536]{1,0:T(8,128)(2,1)S(1)}, u32[]{:S(2)}, u32[]{:S(2)}) %collective-permute-start.30) | collective-permute-done | bytes 196640 | tf_op jit(solution)/shard_map/cond/branch_1_fun/ppermute | solution.py:601
  18.4 0.3 squeeze_slots.2
  18.8 2.5 %collective-permute-start.31 = (bf16[96,1536]{1,0:T(8,128)(2,1)S(1)}, bf16[96,1536]{1,0:T(8,128)(2,1)S(1)}, u32[]{:S(2)}, u32[]{:S(2)}) collective-permute-start(bf16[96,1536]{1,0:T(8,128)(2,1)S(1)} %squeeze_slots.2), channel_id=1, source_target_pairs={{0,2},{1,5},{2,0},{3,7},{4,6},{5,1},{6,4},{7,3},{8,10},{9,13},{10,... | collective-permute-start | bytes 884744 | tf_op jit(solution)/shard_map/cond/branch_1_fun/ppermute | solution.py:601
  21.2 0.0 collective-permute-done.33.got_ref
  21.2 0.3 squeeze_slots.3
  21.6 1.8 %collective-permute-start.34 = (bf16[96,1536]{1,0:T(8,128)(2,1)S(1)}, bf16[96,1536]{1,0:T(8,128)(2,1)S(1)}, u32[]{:S(2)}, u32[]{:S(2)}) collective-permute-start(bf16[96,1536]{1,0:T(8,128)(2,1)S(1)} %squeeze_slots.3), channel_id=1, source_target_pairs={{0,2},{1,5},{2,0},{3,7},{4,6},{5,1},{6,4},{7,3},{8,10},{9,13},{10,... | collective-permute-start | bytes 884744 | tf_op jit(solution)/shard_map/cond/branch_1_fun/ppermute | solution.py:601
  23.3 3.4 %collective-permute-done.31 = bf16[96,1536]{1,0:T(8,128)(2,1)S(1)} collective-permute-done((bf16[96,1536]{1,0:T(8,128)(2,1)S(1)}, bf16[96,1536]{1,0:T(8,128)(2,1)S(1)}, u32[]{:S(2)}, u32[]{:S(2)}) %collective-permute-start.31) | collective-permute-done | bytes 294944 | tf_op jit(solution)/shard_map/cond/branch_1_fun/ppermute | solution.py:601
  26.8 1.0 %collective-permute-start.32 = (bf16[192,1536]{1,0:T(8,128)(2,1)S(1)}, bf16[192,1536]{1,0:T(8,128)(2,1)S(1)}, u32[]{:S(2)}, u32[]{:S(2)}) collective-permute-start(bf16[192,1536]{1,0:T(8,128)(2,1)S(1)} %pad_maximum_fusion.8.mine_ref), channel_id=1, source_target_pairs={{0,1},{1,0},{2,3},{3,2},{4,5},{5,4},{6,7},{7,6},{8,9},{9,8},{10,11... | collective-permute-start | bytes 1769480 | tf_op jit(solution)/shard_map/cond/branch_1_fun/ppermute | solution.py:601
  27.8 2.1 %collective-permute-done.34 = bf16[96,1536]{1,0:T(8,128)(2,1)S(1)} collective-permute-done((bf16[96,1536]{1,0:T(8,128)(2,1)S(1)}, bf16[96,1536]{1,0:T(8,128)(2,1)S(1)}, u32[]{:S(2)}, u32[]{:S(2)}) %collective-permute-start.34) | collective-permute-done | bytes 294944 | tf_op jit(solution)/shard_map/cond/branch_1_fun/ppermute | solution.py:601
  30.0 2.4 %collective-permute-start.35 = (bf16[192,1536]{1,0:T(8,128)(2,1)S(1)}, bf16[192,1536]{1,0:T(8,128)(2,1)S(1)}, u32[]{:S(2)}, u32[]{:S(2)}) collective-permute-start(bf16[192,1536]{1,0:T(8,128)(2,1)S(1)} %pad_maximum_fusion.9.next_ref), channel_id=1, source_target_pairs={{0,1},{1,0},{2,3},{3,2},{4,5},{5,4},{6,7},{7,6},{8,9},{9,8},{10,11... | collective-permute-start | bytes 1769480 | tf_op jit(solution)/shard_map/cond/branch_1_fun/ppermute | solution.py:601
  32.3 0.0 collective-permute-done.32.other_ref
  32.3 1.5 %distances.3 = (f32[768,256]{1,0:T(8,128)S(1)}, bf16[256,1536]{1,0:T(8,128)(2,1)S(1)}) custom-call(bf16[192,1536]{1,0:T(8,128)(2,1)S(1)} %pad_maximum_fusion.8.mine_ref, bf16[192,1536]{1,0:T(8,128)(2,1)S(1)} %collective-permute-done.32.other_ref, bf16[192,1536]{1,0:T(8,128)(2,1)S(1)} %pad_maximum_fusion.9.next_ref, ...), custom_call_target="tpu_custom_call" | custom-call | flops 603979776 | bytes 3145728 | tf_op jit(solution)/shard_map/cond/branch_1_fun/distances/pallas_call | solution.py:416
  33.8 0.2 collective-permute-done.35.other_ref
  34.0 2.4 %predict.3 = (f32[608,128]{1,0:T(8,128)S(1)}, f32[608,128]{1,0:T(8,128)S(1)}, bf16[2304,256]{1,0:T(8,128)(2,1)S(1)}) custom-call(bf16[256,1536]{1,0:T(8,128)(2,1)S(1)} %get-tuple-element.73.found_ref, bf16[192,1536]{1,0:T(8,128)(2,1)S(1)} %collective-permute-done.35.other_ref, bf16[256,512]{1,0:T(8,128)(2,1)S(1)} %get-tuple-element.71.select_ref, ...), custom_call_target="tpu_custom_call" | custom-call | flops 1321205760 | bytes 5636096 | tf_op jit(solution)/shard_map/cond/branch_1_fun/predict/pallas_call | solution.py:438
  36.4 0.4 collective-permute-start.43
  36.8 1.0 %predict_more.3 = (f32[608,128]{1,0:T(8,128)S(1)}, f32[608,128]{1,0:T(8,128)S(1)}) custom-call(bf16[608,2304]{1,0:T(8,128)(2,1)S(1)} %get-tuple-element.67.left, bf16[2304,256]{1,0:T(8,128)(2,1)S(1)} %get-tuple-element.76.right), custom_call_target="tpu_custom_call" | custom-call | flops 717225984 | bytes 3112960 | tf_op jit(solution)/shard_map/cond/branch_1_fun/predict_more/pallas_call | solution.py:458
  37.8 0.2 collective-permute-start.36
  38.0 0.0 collective-permute-done.43
  38.1 0.0 copy-start.4
  38.1 0.0 copy-start.12
  38.1 0.4 collective-permute-start.44
  38.5 1.0 %collective-permute-done.36 = f32[608,128]{1,0:T(8,128)S(1)} collective-permute-done((f32[608,128]{1,0:T(8,128)S(1)}, f32[608,128]{1,0:T(8,128)S(1)}, u32[]{:S(2)}, u32[]{:S(2)}) %collective-permute-start.36) | collective-permute-done | bytes 311328 | tf_op jit(solution)/shard_map/cond/branch_1_fun/ppermute | solution.py:601
  39.6 0.4 collective-permute-start.37
  39.9 2.6 %collective-permute-done.44 = f32[304,128]{1,0:T(8,128)S(1)} collective-permute-done((f32[304,128]{1,0:T(8,128)S(1)}, f32[304,128]{1,0:T(8,128)S(1)}, u32[]{:S(2)}, u32[]{:S(2)}) %collective-permute-start.44) | collective-permute-done | bytes 155680 | tf_op jit(solution)/shard_map/cond/branch_1_fun/ppermute | solution.py:601
  42.6 1.3 %collective-permute-start.45 = (f32[152,128]{1,0:T(8,128)S(1)}, f32[152,128]{1,0:T(8,128)S(1)}, u32[]{:S(2)}, u32[]{:S(2)}) collective-permute-start(f32[152,128]{1,0:T(8,128)S(1)} %slice.98), channel_id=1, source_target_pairs={{0,4},{1,3},{2,6},{3,1},{4,0},{5,7},{6,2},{7,5},{8,12},{9,11},{10,... | collective-permute-start | bytes 233480 | tf_op jit(solution)/shard_map/cond/branch_1_fun/ppermute | solution.py:601
  43.9 0.3 collective-permute-done.37
  44.3 1.3 %collective-permute-start.38 = (f32[152,128]{1,0:T(8,128)S(1)}, f32[152,128]{1,0:T(8,128)S(1)}, u32[]{:S(2)}, u32[]{:S(2)}) collective-permute-start(f32[152,128]{1,0:T(8,128)S(1)} %slice.94), channel_id=1, source_target_pairs={{0,4},{1,3},{2,6},{3,1},{4,0},{5,7},{6,2},{7,5},{8,12},{9,11},{10,... | collective-permute-start | bytes 233480 | tf_op jit(solution)/shard_map/cond/branch_1_fun/ppermute | solution.py:601
  45.6 0.3 collective-permute-done.45
  45.9 2.0 %collective-permute-start.46 = (f32[152,128]{1,0:T(8,128)S(1)}, f32[152,128]{1,0:T(8,128)S(1)}, u32[]{:S(2)}, u32[]{:S(2)}) collective-permute-start(f32[152,128]{1,0:T(8,128)S(1)} %slice_add_fusion.10), channel_id=1, source_target_pairs={{0,8},{1,9},{2,10},{3,11},{4,12},{5,13},{6,14},{7,15},{8,0},{9,1},... | collective-permute-start | bytes 233480 | tf_op jit(solution)/shard_map/cond/branch_1_fun/ppermute | solution.py:601
  48.0 0.0 collective-permute-done.38
  48.0 1.7 %collective-permute-start.39 = (f32[152,128]{1,0:T(8,128)S(1)}, f32[152,128]{1,0:T(8,128)S(1)}, u32[]{:S(2)}, u32[]{:S(2)}) collective-permute-start(f32[152,128]{1,0:T(8,128)S(1)} %slice_add_fusion.11), channel_id=1, source_target_pairs={{0,8},{1,9},{2,10},{3,11},{4,12},{5,13},{6,14},{7,15},{8,0},{9,1},... | collective-permute-start | bytes 233480 | tf_op jit(solution)/shard_map/cond/branch_1_fun/ppermute | solution.py:601
  49.7 0.5 collective-permute-done.46
  50.2 1.3 %collective-permute-start.47 = (f32[152,128]{1,0:T(8,128)S(1)}, f32[152,128]{1,0:T(8,128)S(1)}, u32[]{:S(2)}, u32[]{:S(2)}) collective-permute-start(f32[152,128]{1,0:T(8,128)S(1)} %add.135), channel_id=1, source_target_pairs={{0,4},{1,3},{2,6},{3,1},{4,0},{5,7},{6,2},{7,5},{8,12},{9,11},{10,... | collective-permute-start | bytes 233480 | tf_op jit(solution)/shard_map/cond/branch_1_fun/ppermute | solution.py:601
  51.5 1.2 %collective-permute-done.39 = f32[152,128]{1,0:T(8,128)S(1)} collective-permute-done((f32[152,128]{1,0:T(8,128)S(1)}, f32[152,128]{1,0:T(8,128)S(1)}, u32[]{:S(2)}, u32[]{:S(2)}) %collective-permute-start.39) | collective-permute-done | bytes 77856 | tf_op jit(solution)/shard_map/cond/branch_1_fun/ppermute | solution.py:601
  52.7 1.4 %collective-permute-start.40 = (f32[152,128]{1,0:T(8,128)S(1)}, f32[152,128]{1,0:T(8,128)S(1)}, u32[]{:S(2)}, u32[]{:S(2)}) collective-permute-start(f32[152,128]{1,0:T(8,128)S(1)} %add.131), channel_id=1, source_target_pairs={{0,4},{1,3},{2,6},{3,1},{4,0},{5,7},{6,2},{7,5},{8,12},{9,11},{10,... | collective-permute-start | bytes 233480 | tf_op jit(solution)/shard_map/cond/branch_1_fun/ppermute | solution.py:601
  54.1 0.0 collective-permute-done.47
  54.1 2.0 %collective-permute-start.48 = (f32[304,128]{1,0:T(8,128)S(1)}, f32[304,128]{1,0:T(8,128)S(1)}, u32[]{:S(2)}, u32[]{:S(2)}) collective-permute-start(f32[304,128]{1,0:T(8,128)S(1)} %pad_maximum_fusion.15), channel_id=1, source_target_pairs={{0,2},{1,5},{2,0},{3,7},{4,6},{5,1},{6,4},{7,3},{8,10},{9,13},{10,... | collective-permute-start | bytes 466952 | tf_op jit(solution)/shard_map/cond/branch_1_fun/ppermute | solution.py:601
  56.1 2.0 %collective-permute-start.41 = (f32[304,128]{1,0:T(8,128)S(1)}, f32[304,128]{1,0:T(8,128)S(1)}, u32[]{:S(2)}, u32[]{:S(2)}) collective-permute-start(f32[304,128]{1,0:T(8,128)S(1)} %pad_maximum_fusion.14), channel_id=1, source_target_pairs={{0,2},{1,5},{2,0},{3,7},{4,6},{5,1},{6,4},{7,3},{8,10},{9,13},{10,... | collective-permute-start | bytes 466952 | tf_op jit(solution)/shard_map/cond/branch_1_fun/ppermute | solution.py:601
  58.1 1.2 %collective-permute-done.48 = f32[304,128]{1,0:T(8,128)S(1)} collective-permute-done((f32[304,128]{1,0:T(8,128)S(1)}, f32[304,128]{1,0:T(8,128)S(1)}, u32[]{:S(2)}, u32[]{:S(2)}) %collective-permute-start.48) | collective-permute-done | bytes 155680 | tf_op jit(solution)/shard_map/cond/branch_1_fun/ppermute | solution.py:601
  59.4 6.8 %collective-permute-start.49 = (f32[608,128]{1,0:T(8,128)S(1)}, f32[608,128]{1,0:T(8,128)S(1)}, u32[]{:S(2)}, u32[]{:S(2)}) collective-permute-start(f32[608,128]{1,0:T(8,128)S(1)} %pad_maximum_fusion.11.mine_ref), channel_id=1, source_target_pairs={{0,1},{1,0},{2,3},{3,2},{4,5},{5,4},{6,7},{7,6},{8,9},{9,8},{10,11... | collective-permute-start | bytes 933896 | tf_op jit(solution)/shard_map/cond/branch_1_fun/ppermute | solution.py:601
  66.2 1.6 %collective-permute-start.42 = (f32[608,128]{1,0:T(8,128)S(1)}, f32[608,128]{1,0:T(8,128)S(1)}, u32[]{:S(2)}, u32[]{:S(2)}) collective-permute-start(f32[608,128]{1,0:T(8,128)S(1)} %pad_maximum_fusion.10.mine_ref), channel_id=1, source_target_pairs={{0,1},{1,0},{2,3},{3,2},{4,5},{5,4},{6,7},{7,6},{8,9},{9,8},{10,11... | collective-permute-start | bytes 933896 | tf_op jit(solution)/shard_map/cond/branch_1_fun/ppermute | solution.py:601
  67.9 0.0 collective-permute-done.49.other_ref
  67.9 2.2 %update.3 = (f32[1000,768]{1,0:T(8,128)}, f32[1000,256]{1,0:T(8,128)}, bf16[768,768]{1,0:T(8,128)(2,1)S(1)}) custom-call(f32[608,128]{1,0:T(8,128)S(1)} %pad_maximum_fusion.11.mine_ref, f32[608,128]{1,0:T(8,128)S(1)} %collective-permute-done.49.other_ref, f32[1000,256]{1,0:T(8,128)S(1)} %copy-done.4, s32[1,256]{1,0:T(1,128)S(1)} %copy-done.8, ...), custom_call_target="tpu_custom_call" | custom-call | flops 717225984 | bytes 3670016 | tf_op jit(solution)/shard_map/cond/branch_1_fun/update/pallas_call | solution.py:540
  70.1 0.0 collective-permute-done.42.other_ref
  70.1 2.0 %update_more.3 = (f32[1000,768]{1,0:T(8,128)}, f32[1000,256]{1,0:T(8,128)}) custom-call(f32[608,128]{1,0:T(8,128)S(1)} %pad_maximum_fusion.10.mine_ref, f32[608,128]{1,0:T(8,128)S(1)} %collective-permute-done.42.other_ref, f32[1000,256]{1,0:T(8,128)S(1)} %copy-done.4, f32[1000,768]{1,0:T(8,128)S(1)} %copy-done.2, ...), custom_call_target="tpu_custom_call", output_to_operand_aliasing={{0}: (5, {}), {1}: (6, {})} | custom-call | flops 651165696 | bytes 4521984 | tf_op jit(solution)/shard_map/cond/branch_1_fun/update_more/pallas_call | solution.py:577
  (29 shorter events, 0.4 us)
Async XLA Ops:
  4.8 5.4 %copy-start.8 = (s32[1,256]{1,0:T(1,128)S(1)}, s32[1,256]{1,0:T(1,128)}, u32[]{:S(2)}) copy-start(s32[1,256]{1,0:T(1,128)} %get-tuple-element.58.index_hbm.index_ref) | copy-start | bytes 3076 | tf_op jit(solution)/shard_map/cond
  4.8 5.8 %copy-start.10 = (s32[320]{0:T(512)S(1)}, s32[320]{0:T(512)}, u32[]{:S(2)}) copy-start(s32[320]{0:T(512)} %get-tuple-element.60) | copy-start | bytes 3844 | tf_op jit(solution)/shard_map/cond
  4.8 5.8 %copy-start = (bf16[768,3072]{1,0:T(8,128)(2,1)S(1)}, bf16[768,3072]{1,0:T(8,128)(2,1)}, u32[]{:S(2)}) copy-start(bf16[768,3072]{1,0:T(8,128)(2,1)} %get-tuple-element.59.centers_hbm.centers_ref) | copy-start | bytes 14155780 | tf_op jit(solution)/shard_map/cond
  4.8 8.7 %collective-permute-start.29 = (bf16[32,1536]{1,0:T(8,128)(2,1)S(1)}, bf16[32,1536]{1,0:T(8,128)(2,1)S(1)}, u32[]{:S(2)}, u32[]{:S(2)}) collective-permute-start(bf16[32,1536]{1,0:T(8,128)(2,1)S(1)} %pack_rows.3), channel_id=1, source_target_pairs={{0,8},{1,9},{2,10},{3,11},{4,12},{5,13},{6,14},{7,15},{8,0},{9,1},... | collective-permute-start | bytes 294920 | tf_op jit(solution)/shard_map/cond/branch_1_fun/ppermute | solution.py:601
  9.9 1.9 %copy-start.2 = (f32[1000,768]{1,0:T(8,128)S(1)}, f32[1000,768]{1,0:T(8,128)}, u32[]{:S(2)}) copy-start(f32[1000,768]{1,0:T(8,128)} %get-tuple-element.62.weights_ref) | copy-start | bytes 9216004 | tf_op jit(solution)/shard_map/cond
  9.9 1.9 %copy-start.6 = (f32[160,320]{1,0:T(8,128)S(1)}, f32[160,320]{1,0:T(8,128)}, u32[]{:S(2)}) copy-start(f32[160,320]{1,0:T(8,128)} %get-tuple-element.61.eigvec_ref) | copy-start | bytes 614404 | tf_op jit(solution)/shard_map/cond
  10.0 4.9 %collective-permute-start.28 = (bf16[32,1536]{1,0:T(8,128)(2,1)S(1)}, bf16[32,1536]{1,0:T(8,128)(2,1)S(1)}, u32[]{:S(2)}, u32[]{:S(2)}) collective-permute-start(bf16[32,1536]{1,0:T(8,128)(2,1)S(1)} %pack_rows.2), channel_id=1, source_target_pairs={{0,8},{1,9},{2,10},{3,11},{4,12},{5,13},{6,14},{7,15},{8,0},{9,1},... | collective-permute-start | bytes 294920 | tf_op jit(solution)/shard_map/cond/branch_1_fun/ppermute | solution.py:601
  13.5 4.9 %collective-permute-start.30 = (bf16[64,1536]{1,0:T(8,128)(2,1)S(1)}, bf16[64,1536]{1,0:T(8,128)(2,1)S(1)}, u32[]{:S(2)}, u32[]{:S(2)}) collective-permute-start(bf16[64,1536]{1,0:T(8,128)(2,1)S(1)} %pad_maximum_fusion.13.keep_ref), channel_id=1, source_target_pairs={{0,4},{1,3},{2,6},{3,1},{4,0},{5,7},{6,2},{7,5},{8,12},{9,11},{10,... | collective-permute-start | bytes 589832 | tf_op jit(solution)/shard_map/cond/branch_1_fun/ppermute | solution.py:601
  14.9 6.4 %collective-permute-start.33 = (bf16[64,1536]{1,0:T(8,128)(2,1)S(1)}, bf16[64,1536]{1,0:T(8,128)(2,1)S(1)}, u32[]{:S(2)}, u32[]{:S(2)}) collective-permute-start(bf16[64,1536]{1,0:T(8,128)(2,1)S(1)} %pad_maximum_fusion.12.keep_ref), channel_id=1, source_target_pairs={{0,4},{1,3},{2,6},{3,1},{4,0},{5,7},{6,2},{7,5},{8,12},{9,11},{10,... | collective-permute-start | bytes 589832 | tf_op jit(solution)/shard_map/cond/branch_1_fun/ppermute | solution.py:601
  18.8 8.0 %collective-permute-start.31 = (bf16[96,1536]{1,0:T(8,128)(2,1)S(1)}, bf16[96,1536]{1,0:T(8,128)(2,1)S(1)}, u32[]{:S(2)}, u32[]{:S(2)}) collective-permute-start(bf16[96,1536]{1,0:T(8,128)(2,1)S(1)} %squeeze_slots.2), channel_id=1, source_target_pairs={{0,2},{1,5},{2,0},{3,7},{4,6},{5,1},{6,4},{7,3},{8,10},{9,13},{10,... | collective-permute-start | bytes 884744 | tf_op jit(solution)/shard_map/cond/branch_1_fun/ppermute | solution.py:601
  21.6 8.3 %collective-permute-start.34 = (bf16[96,1536]{1,0:T(8,128)(2,1)S(1)}, bf16[96,1536]{1,0:T(8,128)(2,1)S(1)}, u32[]{:S(2)}, u32[]{:S(2)}) collective-permute-start(bf16[96,1536]{1,0:T(8,128)(2,1)S(1)} %squeeze_slots.3), channel_id=1, source_target_pairs={{0,2},{1,5},{2,0},{3,7},{4,6},{5,1},{6,4},{7,3},{8,10},{9,13},{10,... | collective-permute-start | bytes 884744 | tf_op jit(solution)/shard_map/cond/branch_1_fun/ppermute | solution.py:601
  26.8 5.6 %collective-permute-start.32 = (bf16[192,1536]{1,0:T(8,128)(2,1)S(1)}, bf16[192,1536]{1,0:T(8,128)(2,1)S(1)}, u32[]{:S(2)}, u32[]{:S(2)}) collective-permute-start(bf16[192,1536]{1,0:T(8,128)(2,1)S(1)} %pad_maximum_fusion.8.mine_ref), channel_id=1, source_target_pairs={{0,1},{1,0},{2,3},{3,2},{4,5},{5,4},{6,7},{7,6},{8,9},{9,8},{10,11... | collective-permute-start | bytes 1769480 | tf_op jit(solution)/shard_map/cond/branch_1_fun/ppermute | solution.py:601
  30.0 4.0 %collective-permute-start.35 = (bf16[192,1536]{1,0:T(8,128)(2,1)S(1)}, bf16[192,1536]{1,0:T(8,128)(2,1)S(1)}, u32[]{:S(2)}, u32[]{:S(2)}) collective-permute-start(bf16[192,1536]{1,0:T(8,128)(2,1)S(1)} %pad_maximum_fusion.9.next_ref), channel_id=1, source_target_pairs={{0,1},{1,0},{2,3},{3,2},{4,5},{5,4},{6,7},{7,6},{8,9},{9,8},{10,11... | collective-permute-start | bytes 1769480 | tf_op jit(solution)/shard_map/cond/branch_1_fun/ppermute | solution.py:601
  36.4 1.7 %collective-permute-start.43 = (f32[608,128]{1,0:T(8,128)S(1)}, f32[608,128]{1,0:T(8,128)S(1)}, u32[]{:S(2)}, u32[]{:S(2)}) collective-permute-start(f32[608,128]{1,0:T(8,128)S(1)} %get-tuple-element.81), channel_id=1, source_target_pairs={{0,1},{1,0},{2,3},{3,2},{4,5},{5,4},{6,7},{7,6},{8,9},{9,8},{10,11... | collective-permute-start | bytes 933896 | tf_op jit(solution)/shard_map/cond/branch_1_fun/ppermute | solution.py:601
  37.8 1.7 %collective-permute-start.36 = (f32[608,128]{1,0:T(8,128)S(1)}, f32[608,128]{1,0:T(8,128)S(1)}, u32[]{:S(2)}, u32[]{:S(2)}) collective-permute-start(f32[608,128]{1,0:T(8,128)S(1)} %get-tuple-element.78), channel_id=1, source_target_pairs={{0,1},{1,0},{2,3},{3,2},{4,5},{5,4},{6,7},{7,6},{8,9},{9,8},{10,11... | collective-permute-start | bytes 933896 | tf_op jit(solution)/shard_map/cond/branch_1_fun/ppermute | solution.py:601
  38.1 29.8 %copy-start.4 = (f32[1000,256]{1,0:T(8,128)S(1)}, f32[1000,256]{1,0:T(8,128)}, u32[]{:S(2)}) copy-start(f32[1000,256]{1,0:T(8,128)} %get-tuple-element.79.targets_ref) | copy-start | bytes 3072004 | tf_op jit(solution)/shard_map/cond
  38.1 29.8 %copy-start.12 = (f32[1,160]{1,0:T(1,128)S(1)}, f32[1,160]{1,0:T(1,128)}, u32[]{:S(2)}) copy-start(f32[1,160]{1,0:T(1,128)} %get-tuple-element.82.eigval_ref) | copy-start | bytes 1924 | tf_op jit(solution)/shard_map/cond
  38.1 4.4 %collective-permute-start.44 = (f32[304,128]{1,0:T(8,128)S(1)}, f32[304,128]{1,0:T(8,128)S(1)}, u32[]{:S(2)}, u32[]{:S(2)}) collective-permute-start(f32[304,128]{1,0:T(8,128)S(1)} %slice.96), channel_id=1, source_target_pairs={{0,2},{1,5},{2,0},{3,7},{4,6},{5,1},{6,4},{7,3},{8,10},{9,13},{10,... | collective-permute-start | bytes 466952 | tf_op jit(solution)/shard_map/cond/branch_1_fun/ppermute | solution.py:601
  39.6 4.7 %collective-permute-start.37 = (f32[304,128]{1,0:T(8,128)S(1)}, f32[304,128]{1,0:T(8,128)S(1)}, u32[]{:S(2)}, u32[]{:S(2)}) collective-permute-start(f32[304,128]{1,0:T(8,128)S(1)} %slice.92), channel_id=1, source_target_pairs={{0,2},{1,5},{2,0},{3,7},{4,6},{5,1},{6,4},{7,3},{8,10},{9,13},{10,... | collective-permute-start | bytes 466952 | tf_op jit(solution)/shard_map/cond/branch_1_fun/ppermute | solution.py:601
  42.6 3.3 %collective-permute-start.45 = (f32[152,128]{1,0:T(8,128)S(1)}, f32[152,128]{1,0:T(8,128)S(1)}, u32[]{:S(2)}, u32[]{:S(2)}) collective-permute-start(f32[152,128]{1,0:T(8,128)S(1)} %slice.98), channel_id=1, source_target_pairs={{0,4},{1,3},{2,6},{3,1},{4,0},{5,7},{6,2},{7,5},{8,12},{9,11},{10,... | collective-permute-start | bytes 233480 | tf_op jit(solution)/shard_map/cond/branch_1_fun/ppermute | solution.py:601
  44.3 3.7 %collective-permute-start.38 = (f32[152,128]{1,0:T(8,128)S(1)}, f32[152,128]{1,0:T(8,128)S(1)}, u32[]{:S(2)}, u32[]{:S(2)}) collective-permute-start(f32[152,128]{1,0:T(8,128)S(1)} %slice.94), channel_id=1, source_target_pairs={{0,4},{1,3},{2,6},{3,1},{4,0},{5,7},{6,2},{7,5},{8,12},{9,11},{10,... | collective-permute-start | bytes 233480 | tf_op jit(solution)/shard_map/cond/branch_1_fun/ppermute | solution.py:601
  45.9 4.2 %collective-permute-start.46 = (f32[152,128]{1,0:T(8,128)S(1)}, f32[152,128]{1,0:T(8,128)S(1)}, u32[]{:S(2)}, u32[]{:S(2)}) collective-permute-start(f32[152,128]{1,0:T(8,128)S(1)} %slice_add_fusion.10), channel_id=1, source_target_pairs={{0,8},{1,9},{2,10},{3,11},{4,12},{5,13},{6,14},{7,15},{8,0},{9,1},... | collective-permute-start | bytes 233480 | tf_op jit(solution)/shard_map/cond/branch_1_fun/ppermute | solution.py:601
  48.0 4.7 %collective-permute-start.39 = (f32[152,128]{1,0:T(8,128)S(1)}, f32[152,128]{1,0:T(8,128)S(1)}, u32[]{:S(2)}, u32[]{:S(2)}) collective-permute-start(f32[152,128]{1,0:T(8,128)S(1)} %slice_add_fusion.11), channel_id=1, source_target_pairs={{0,8},{1,9},{2,10},{3,11},{4,12},{5,13},{6,14},{7,15},{8,0},{9,1},... | collective-permute-start | bytes 233480 | tf_op jit(solution)/shard_map/cond/branch_1_fun/ppermute | solution.py:601
  50.2 3.9 %collective-permute-start.47 = (f32[152,128]{1,0:T(8,128)S(1)}, f32[152,128]{1,0:T(8,128)S(1)}, u32[]{:S(2)}, u32[]{:S(2)}) collective-permute-start(f32[152,128]{1,0:T(8,128)S(1)} %add.135), channel_id=1, source_target_pairs={{0,4},{1,3},{2,6},{3,1},{4,0},{5,7},{6,2},{7,5},{8,12},{9,11},{10,... | collective-permute-start | bytes 233480 | tf_op jit(solution)/shard_map/cond/branch_1_fun/ppermute | solution.py:601
  52.7 3.4 %collective-permute-start.40 = (f32[152,128]{1,0:T(8,128)S(1)}, f32[152,128]{1,0:T(8,128)S(1)}, u32[]{:S(2)}, u32[]{:S(2)}) collective-permute-start(f32[152,128]{1,0:T(8,128)S(1)} %add.131), channel_id=1, source_target_pairs={{0,4},{1,3},{2,6},{3,1},{4,0},{5,7},{6,2},{7,5},{8,12},{9,11},{10,... | collective-permute-start | bytes 233480 | tf_op jit(solution)/shard_map/cond/branch_1_fun/ppermute | solution.py:601
  54.1 5.2 %collective-permute-start.48 = (f32[304,128]{1,0:T(8,128)S(1)}, f32[304,128]{1,0:T(8,128)S(1)}, u32[]{:S(2)}, u32[]{:S(2)}) collective-permute-start(f32[304,128]{1,0:T(8,128)S(1)} %pad_maximum_fusion.15), channel_id=1, source_target_pairs={{0,2},{1,5},{2,0},{3,7},{4,6},{5,1},{6,4},{7,3},{8,10},{9,13},{10,... | collective-permute-start | bytes 466952 | tf_op jit(solution)/shard_map/cond/branch_1_fun/ppermute | solution.py:601
  56.1 10.1 %collective-permute-start.41 = (f32[304,128]{1,0:T(8,128)S(1)}, f32[304,128]{1,0:T(8,128)S(1)}, u32[]{:S(2)}, u32[]{:S(2)}) collective-permute-start(f32[304,128]{1,0:T(8,128)S(1)} %pad_maximum_fusion.14), channel_id=1, source_target_pairs={{0,2},{1,5},{2,0},{3,7},{4,6},{5,1},{6,4},{7,3},{8,10},{9,13},{10,... | collective-permute-start | bytes 466952 | tf_op jit(solution)/shard_map/cond/branch_1_fun/ppermute | solution.py:601
  59.4 8.5 %collective-permute-start.49 = (f32[608,128]{1,0:T(8,128)S(1)}, f32[608,128]{1,0:T(8,128)S(1)}, u32[]{:S(2)}, u32[]{:S(2)}) collective-permute-start(f32[608,128]{1,0:T(8,128)S(1)} %pad_maximum_fusion.11.mine_ref), channel_id=1, source_target_pairs={{0,1},{1,0},{2,3},{3,2},{4,5},{5,4},{6,7},{7,6},{8,9},{9,8},{10,11... | collective-permute-start | bytes 933896 | tf_op jit(solution)/shard_map/cond/branch_1_fun/ppermute | solution.py:601
  66.2 3.9 %collective-permute-start.42 = (f32[608,128]{1,0:T(8,128)S(1)}, f32[608,128]{1,0:T(8,128)S(1)}, u32[]{:S(2)}, u32[]{:S(2)}) collective-permute-start(f32[608,128]{1,0:T(8,128)S(1)} %pad_maximum_fusion.10.mine_ref), channel_id=1, source_target_pairs={{0,1},{1,0},{2,3},{3,2},{4,5},{5,4},{6,7},{7,6},{8,9},{9,8},{10,11... | collective-permute-start | bytes 933896 | tf_op jit(solution)/shard_map/cond/branch_1_fun/ppermute | solution.py:601

commit v16 on v15

--- a/solution.py
+++ b/solution.py
@@ -29,12 +29,12 @@
 
 def walk(sub, bits):
     order = list(range(bits))
-    return order if sub == 0 else order[1::-1] + order[2:]
+    return order if sub == 1 else order[1::-1] + order[2:]
 
 
 def far_first(sub, bits):
     order = list(range(bits))[::-1]
-    return order if sub == 0 else order[:-2] + order[:-3:-1]
+    return order if sub == 1 else order[:-2] + order[:-3:-1]
 
 
 def turns():

time: 72.5 us -> 72.1 us (level)
  starting transfers between devices: 36 us -> 34.4 us
  waiting for transfers between devices: 15.7 us -> 16.9 us
    ppermute x22, starting transfers between devices: 36 us -> 34.4 us  [swap(): lax.ppermute(x, AXES, [(i, i ^ flip[i & 1]) for i in range(2 * chips)])]
    ppermute x22, waiting for transfers between devices: 15.7 us -> 16.9 us  [swap(): lax.ppermute(x, AXES, [(i, i ^ flip[i & 1]) for i in range(2 * chips)])]
  transfers between devices with their start and end apart: 22 -> 22, of which waited for: 11 -> 13; matrix products, arithmetic and copies ran while one was open for 1% -> 1% of each run, Pallas kernels for 15% -> 15%
where the time goes in v16:
time: 72.1 us; the launch traced here: 71.9 us
  starting transfers between devices  34.4 us (48%)
  Pallas kernels  18.2 us (25%)
  waiting for transfers between devices  16.9 us (23%)
  between operations  1.45 us (2%)
    ppermute x22, starting transfers between devices, swap(): lax.ppermute(x, AXES, [(i, i ^ flip[i & 1]) for i in range(2 * chips)])  34.4 us
    ppermute x22, waiting for transfers between devices, swap(): lax.ppermute(x, AXES, [(i, i ^ flip[i & 1]) for i in range(2 * chips)])  16.9 us
    pallas_call x2, Pallas kernels, pack_rows(): pl.pallas_call(functools.partial(pack_body, part * depth), in_specs=[hbm,...  3.84 us
    pallas_call x1, Pallas kernels, predict(): pl.pallas_call(predict_body, in_specs=[vmem] * 6, out_specs=[vmem] * 3, o...  2.4 us
    pallas_call x1, Pallas kernels, update(): pl.pallas_call(update_body, in_specs=[vmem] * 7, out_specs=[hbm, hbm, vme...  2.24 us
    pallas_call x1, Pallas kernels, update_more(): pl.pallas_call(functools.partial(update_more_body, begin), in_specs=[vmem...  1.97 us
    pallas_call x1, Pallas kernels, spread_weights(): pl.pallas_call(functools.partial(spread_body, first, classes), out_shape=...  1.69 us
    pallas_call x1, Pallas kernels, distances(): pl.pallas_call(distance_body, in_specs=[vmem] * 6, out_specs=[vmem, vmem]...  1.47 us
  transfers between devices with their start and end apart: 22, of which 13 were waited for; matrix products, arithmetic and copies ran while one was open for 1% of the time, Pallas kernels for 15%

profile of v16, /device:TPU:1, one launch (start us, length us, event | category | flops | bytes accessed | tf_op | source)
XLA Modules:
  0.0 71.9 jit_solution(14519877937099758187)
XLA Ops:
  0.6 1.4 %rows_fit.1 = s32[1]{0:T(128)} custom-call(s32[1,256]{1,0:T(1,128)} %bitcast.17), custom_call_target="tpu_custom_call" | custom-call | tf_op jit(solution)/shard_map/rows_fit/pallas_call | solution.py:157
  2.6 69.1 %conditional.1 = ((f32[1000,768]{1,0:T(8,128)}, f32[1000,256]{1,0:T(8,128)})) conditional(s32[]{:T(128)} %bitcast.2, (s32[1,256]{1,0:T(1,128)}, bf16[768,3072]{1,0:T(8,128)(2,1)}, s32[320]{0:T(512)}, f32[160,320]{1,0:T(8,128)}, f32[1000,768]{1,0:T(8,128)}, /*index=5*/f32[1000,256]{1,0:T(8,128)}, f32[1,160]{1,0:T(1,128)}) %tuple.31, ...), branch_computations={%region_0.1_spmd, %region_1.2_spmd} | conditional | flops 5916241920 | bytes 106008064 | solution.py:686
  2.8 1.9 %pack_rows.3 = bf16[32,1536]{1,0:T(8,128)(2,1)S(1)} custom-call(s32[1,256]{1,0:T(1,128)} %get-tuple-element.58.index_hbm.index_ref, bf16[768,3072]{1,0:T(8,128)(2,1)} %get-tuple-element.59.centers_hbm.centers_ref), custom_call_target="tpu_custom_call" | custom-call | flops 75497472 | bytes 2457600 | tf_op jit(solution)/shard_map/cond/branch_1_fun/pack_rows/pallas_call | solution.py:199
  4.8 0.0 copy-start.8
  4.8 0.0 copy-start.10
  4.8 0.0 copy-start
  4.8 3.2 %collective-permute-start.29 = (bf16[32,1536]{1,0:T(8,128)(2,1)S(1)}, bf16[32,1536]{1,0:T(8,128)(2,1)S(1)}, u32[]{:S(2)}, u32[]{:S(2)}) collective-permute-start(bf16[32,1536]{1,0:T(8,128)(2,1)S(1)} %pack_rows.3), channel_id=1, source_target_pairs={{0,8},{1,9},{2,10},{3,11},{4,12},{5,13},{6,14},{7,15},{8,0},{9,1},... | collective-permute-start | bytes 294920 | tf_op jit(solution)/shard_map/cond/branch_1_fun/ppermute | solution.py:601
  8.0 1.9 %pack_rows.2 = bf16[32,1536]{1,0:T(8,128)(2,1)S(1)} custom-call(s32[1,256]{1,0:T(1,128)} %get-tuple-element.58.index_hbm.index_ref, bf16[768,3072]{1,0:T(8,128)(2,1)} %get-tuple-element.59.centers_hbm.centers_ref), custom_call_target="tpu_custom_call" | custom-call | flops 75497472 | bytes 2457600 | tf_op jit(solution)/shard_map/cond/branch_1_fun/pack_rows/pallas_call | solution.py:199
  9.9 0.0 copy-start.2
  9.9 0.0 copy-start.6
  10.0 0.2 collective-permute-start.28
  10.2 0.4 select_packed.1
  10.6 1.2 %center_norms.3.norm_ref = f32[768,128]{1,0:T(8,128)S(1)} custom-call(bf16[768,3072]{1,0:T(8,128)(2,1)S(1)} %copy-done), custom_call_target="tpu_custom_call" | custom-call | flops 4718592 | bytes 4718592 | tf_op jit(solution)/shard_map/cond/branch_1_fun/center_norms/pallas_call | solution.py:341
  11.8 0.0 copy-done.2
  11.8 1.7 %spread_weights.3 = (bf16[608,2304]{1,0:T(8,128)(2,1)S(1)}, bf16[608,2304]{1,0:T(8,128)(2,1)S(1)}, f32[160,768]{1,0:T(8,128)S(1)}) custom-call(s32[1,320]{1,0:T(1,128)S(1)} %reshape.99.index_ref, f32[160,320]{1,0:T(8,128)S(1)} %copy-done.6, f32[1000,768]{1,0:T(8,128)S(1)} %copy-done.2), custom_call_target="tpu_custom_call" | custom-call | flops 235929600 | bytes 7471104 | tf_op jit(solution)/shard_map/cond/branch_1_fun/spread_weights/pallas_call | solution.py:316
  13.5 0.0 collective-permute-done.29
  13.5 2.5 %collective-permute-start.30 = (bf16[64,1536]{1,0:T(8,128)(2,1)S(1)}, bf16[64,1536]{1,0:T(8,128)(2,1)S(1)}, u32[]{:S(2)}, u32[]{:S(2)}) collective-permute-start(bf16[64,1536]{1,0:T(8,128)(2,1)S(1)} %pad_maximum_fusion.13.keep_ref), channel_id=1, source_target_pairs={{0,2},{1,5},{2,0},{3,7},{4,6},{5,1},{6,4},{7,3},{8,10},{9,13},{10,... | collective-permute-start | bytes 589832 | tf_op jit(solution)/shard_map/cond/branch_1_fun/ppermute | solution.py:601
  16.0 0.0 collective-permute-done.28
  16.0 2.1 %collective-permute-start.33 = (bf16[64,1536]{1,0:T(8,128)(2,1)S(1)}, bf16[64,1536]{1,0:T(8,128)(2,1)S(1)}, u32[]{:S(2)}, u32[]{:S(2)}) collective-permute-start(bf16[64,1536]{1,0:T(8,128)(2,1)S(1)} %pad_maximum_fusion.12.keep_ref), channel_id=1, source_target_pairs={{0,2},{1,5},{2,0},{3,7},{4,6},{5,1},{6,4},{7,3},{8,10},{9,13},{10,... | collective-permute-start | bytes 589832 | tf_op jit(solution)/shard_map/cond/branch_1_fun/ppermute | solution.py:601
  18.1 1.7 %collective-permute-done.30.got_ref = bf16[64,1536]{1,0:T(8,128)(2,1)S(1)} collective-permute-done((bf16[64,1536]{1,0:T(8,128)(2,1)S(1)}, bf16[64,1536]{1,0:T(8,128)(2,1)S(1)}, u32[]{:S(2)}, u32[]{:S(2)}) %collective-permute-start.30) | collective-permute-done | bytes 196640 | tf_op jit(solution)/shard_map/cond/branch_1_fun/ppermute | solution.py:601
  19.8 0.3 squeeze_slots.2
  20.2 1.4 %collective-permute-start.31 = (bf16[96,1536]{1,0:T(8,128)(2,1)S(1)}, bf16[96,1536]{1,0:T(8,128)(2,1)S(1)}, u32[]{:S(2)}, u32[]{:S(2)}) collective-permute-start(bf16[96,1536]{1,0:T(8,128)(2,1)S(1)} %squeeze_slots.2), channel_id=1, source_target_pairs={{0,4},{1,3},{2,6},{3,1},{4,0},{5,7},{6,2},{7,5},{8,12},{9,11},{10,... | collective-permute-start | bytes 884744 | tf_op jit(solution)/shard_map/cond/branch_1_fun/ppermute | solution.py:601
  21.6 0.5 collective-permute-done.33.got_ref
  22.1 0.3 squeeze_slots.3
  22.4 1.3 %collective-permute-start.34 = (bf16[96,1536]{1,0:T(8,128)(2,1)S(1)}, bf16[96,1536]{1,0:T(8,128)(2,1)S(1)}, u32[]{:S(2)}, u32[]{:S(2)}) collective-permute-start(bf16[96,1536]{1,0:T(8,128)(2,1)S(1)} %squeeze_slots.3), channel_id=1, source_target_pairs={{0,4},{1,3},{2,6},{3,1},{4,0},{5,7},{6,2},{7,5},{8,12},{9,11},{10,... | collective-permute-start | bytes 884744 | tf_op jit(solution)/shard_map/cond/branch_1_fun/ppermute | solution.py:601
  23.7 3.1 %collective-permute-done.31 = bf16[96,1536]{1,0:T(8,128)(2,1)S(1)} collective-permute-done((bf16[96,1536]{1,0:T(8,128)(2,1)S(1)}, bf16[96,1536]{1,0:T(8,128)(2,1)S(1)}, u32[]{:S(2)}, u32[]{:S(2)}) %collective-permute-start.31) | collective-permute-done | bytes 294944 | tf_op jit(solution)/shard_map/cond/branch_1_fun/ppermute | solution.py:601
  26.9 0.9 %collective-permute-start.32 = (bf16[192,1536]{1,0:T(8,128)(2,1)S(1)}, bf16[192,1536]{1,0:T(8,128)(2,1)S(1)}, u32[]{:S(2)}, u32[]{:S(2)}) collective-permute-start(bf16[192,1536]{1,0:T(8,128)(2,1)S(1)} %pad_maximum_fusion.8.mine_ref), channel_id=1, source_target_pairs={{0,1},{1,0},{2,3},{3,2},{4,5},{5,4},{6,7},{7,6},{8,9},{9,8},{10,11... | collective-permute-start | bytes 1769480 | tf_op jit(solution)/shard_map/cond/branch_1_fun/ppermute | solution.py:601
  27.8 2.2 %collective-permute-done.34 = bf16[96,1536]{1,0:T(8,128)(2,1)S(1)} collective-permute-done((bf16[96,1536]{1,0:T(8,128)(2,1)S(1)}, bf16[96,1536]{1,0:T(8,128)(2,1)S(1)}, u32[]{:S(2)}, u32[]{:S(2)}) %collective-permute-start.34) | collective-permute-done | bytes 294944 | tf_op jit(solution)/shard_map/cond/branch_1_fun/ppermute | solution.py:601
  30.0 1.9 %collective-permute-start.35 = (bf16[192,1536]{1,0:T(8,128)(2,1)S(1)}, bf16[192,1536]{1,0:T(8,128)(2,1)S(1)}, u32[]{:S(2)}, u32[]{:S(2)}) collective-permute-start(bf16[192,1536]{1,0:T(8,128)(2,1)S(1)} %pad_maximum_fusion.9.next_ref), channel_id=1, source_target_pairs={{0,1},{1,0},{2,3},{3,2},{4,5},{5,4},{6,7},{7,6},{8,9},{9,8},{10,11... | collective-permute-start | bytes 1769480 | tf_op jit(solution)/shard_map/cond/branch_1_fun/ppermute | solution.py:601
  31.9 0.0 collective-permute-done.32.other_ref
  31.9 1.5 %distances.3 = (f32[768,256]{1,0:T(8,128)S(1)}, bf16[256,1536]{1,0:T(8,128)(2,1)S(1)}) custom-call(bf16[192,1536]{1,0:T(8,128)(2,1)S(1)} %pad_maximum_fusion.8.mine_ref, bf16[192,1536]{1,0:T(8,128)(2,1)S(1)} %collective-permute-done.32.other_ref, bf16[192,1536]{1,0:T(8,128)(2,1)S(1)} %pad_maximum_fusion.9.next_ref, ...), custom_call_target="tpu_custom_call" | custom-call | flops 603979776 | bytes 3145728 | tf_op jit(solution)/shard_map/cond/branch_1_fun/distances/pallas_call | solution.py:416
  33.4 0.2 collective-permute-done.35.other_ref
  33.6 2.4 %predict.3 = (f32[608,128]{1,0:T(8,128)S(1)}, f32[608,128]{1,0:T(8,128)S(1)}, bf16[2304,256]{1,0:T(8,128)(2,1)S(1)}) custom-call(bf16[256,1536]{1,0:T(8,128)(2,1)S(1)} %get-tuple-element.73.found_ref, bf16[192,1536]{1,0:T(8,128)(2,1)S(1)} %collective-permute-done.35.other_ref, bf16[256,512]{1,0:T(8,128)(2,1)S(1)} %get-tuple-element.71.select_ref, ...), custom_call_target="tpu_custom_call" | custom-call | flops 1321205760 | bytes 5636096 | tf_op jit(solution)/shard_map/cond/branch_1_fun/predict/pallas_call | solution.py:438
  36.0 0.4 collective-permute-start.43
  36.4 1.0 %predict_more.3 = (f32[608,128]{1,0:T(8,128)S(1)}, f32[608,128]{1,0:T(8,128)S(1)}) custom-call(bf16[608,2304]{1,0:T(8,128)(2,1)S(1)} %get-tuple-element.67.left, bf16[2304,256]{1,0:T(8,128)(2,1)S(1)} %get-tuple-element.76.right), custom_call_target="tpu_custom_call" | custom-call | flops 717225984 | bytes 3112960 | tf_op jit(solution)/shard_map/cond/branch_1_fun/predict_more/pallas_call | solution.py:458
  37.4 0.2 collective-permute-start.36
  37.6 0.0 collective-permute-done.43
  37.7 0.0 copy-start.4
  37.7 0.0 copy-start.12
  37.7 1.2 %collective-permute-start.44 = (f32[304,128]{1,0:T(8,128)S(1)}, f32[304,128]{1,0:T(8,128)S(1)}, u32[]{:S(2)}, u32[]{:S(2)}) collective-permute-start(f32[304,128]{1,0:T(8,128)S(1)} %slice.96), channel_id=1, source_target_pairs={{0,4},{1,3},{2,6},{3,1},{4,0},{5,7},{6,2},{7,5},{8,12},{9,11},{10,... | collective-permute-start | bytes 466952 | tf_op jit(solution)/shard_map/cond/branch_1_fun/ppermute | solution.py:601
  38.9 0.2 collective-permute-done.36
  39.2 1.2 %collective-permute-start.37 = (f32[304,128]{1,0:T(8,128)S(1)}, f32[304,128]{1,0:T(8,128)S(1)}, u32[]{:S(2)}, u32[]{:S(2)}) collective-permute-start(f32[304,128]{1,0:T(8,128)S(1)} %slice.92), channel_id=1, source_target_pairs={{0,4},{1,3},{2,6},{3,1},{4,0},{5,7},{6,2},{7,5},{8,12},{9,11},{10,... | collective-permute-start | bytes 466952 | tf_op jit(solution)/shard_map/cond/branch_1_fun/ppermute | solution.py:601
  40.3 1.8 %collective-permute-done.44 = f32[304,128]{1,0:T(8,128)S(1)} collective-permute-done((f32[304,128]{1,0:T(8,128)S(1)}, f32[304,128]{1,0:T(8,128)S(1)}, u32[]{:S(2)}, u32[]{:S(2)}) %collective-permute-start.44) | collective-permute-done | bytes 155680 | tf_op jit(solution)/shard_map/cond/branch_1_fun/ppermute | solution.py:601
  42.2 0.8 %collective-permute-start.45 = (f32[152,128]{1,0:T(8,128)S(1)}, f32[152,128]{1,0:T(8,128)S(1)}, u32[]{:S(2)}, u32[]{:S(2)}) collective-permute-start(f32[152,128]{1,0:T(8,128)S(1)} %slice.98), channel_id=1, source_target_pairs={{0,2},{1,5},{2,0},{3,7},{4,6},{5,1},{6,4},{7,3},{8,10},{9,13},{10,... | collective-permute-start | bytes 233480 | tf_op jit(solution)/shard_map/cond/branch_1_fun/ppermute | solution.py:601
  43.0 0.8 %collective-permute-done.37 = f32[304,128]{1,0:T(8,128)S(1)} collective-permute-done((f32[304,128]{1,0:T(8,128)S(1)}, f32[304,128]{1,0:T(8,128)S(1)}, u32[]{:S(2)}, u32[]{:S(2)}) %collective-permute-start.37) | collective-permute-done | bytes 155680 | tf_op jit(solution)/shard_map/cond/branch_1_fun/ppermute | solution.py:601
  43.9 0.8 %collective-permute-start.38 = (f32[152,128]{1,0:T(8,128)S(1)}, f32[152,128]{1,0:T(8,128)S(1)}, u32[]{:S(2)}, u32[]{:S(2)}) collective-permute-start(f32[152,128]{1,0:T(8,128)S(1)} %slice.94), channel_id=1, source_target_pairs={{0,2},{1,5},{2,0},{3,7},{4,6},{5,1},{6,4},{7,3},{8,10},{9,13},{10,... | collective-permute-start | bytes 233480 | tf_op jit(solution)/shard_map/cond/branch_1_fun/ppermute | solution.py:601
  44.7 0.9 %collective-permute-done.45 = f32[152,128]{1,0:T(8,128)S(1)} collective-permute-done((f32[152,128]{1,0:T(8,128)S(1)}, f32[152,128]{1,0:T(8,128)S(1)}, u32[]{:S(2)}, u32[]{:S(2)}) %collective-permute-start.45) | collective-permute-done | bytes 77856 | tf_op jit(solution)/shard_map/cond/branch_1_fun/ppermute | solution.py:601
  45.5 2.4 %collective-permute-start.46 = (f32[152,128]{1,0:T(8,128)S(1)}, f32[152,128]{1,0:T(8,128)S(1)}, u32[]{:S(2)}, u32[]{:S(2)}) collective-permute-start(f32[152,128]{1,0:T(8,128)S(1)} %slice_add_fusion.10), channel_id=1, source_target_pairs={{0,8},{1,9},{2,10},{3,11},{4,12},{5,13},{6,14},{7,15},{8,0},{9,1},... | collective-permute-start | bytes 233480 | tf_op jit(solution)/shard_map/cond/branch_1_fun/ppermute | solution.py:601
  48.0 0.0 collective-permute-done.38
  48.0 1.7 %collective-permute-start.39 = (f32[152,128]{1,0:T(8,128)S(1)}, f32[152,128]{1,0:T(8,128)S(1)}, u32[]{:S(2)}, u32[]{:S(2)}) collective-permute-start(f32[152,128]{1,0:T(8,128)S(1)} %slice_add_fusion.11), channel_id=1, source_target_pairs={{0,8},{1,9},{2,10},{3,11},{4,12},{5,13},{6,14},{7,15},{8,0},{9,1},... | collective-permute-start | bytes 233480 | tf_op jit(solution)/shard_map/cond/branch_1_fun/ppermute | solution.py:601
  49.7 0.1 collective-permute-done.46
  49.8 1.7 %collective-permute-start.47 = (f32[152,128]{1,0:T(8,128)S(1)}, f32[152,128]{1,0:T(8,128)S(1)}, u32[]{:S(2)}, u32[]{:S(2)}) collective-permute-start(f32[152,128]{1,0:T(8,128)S(1)} %add.135), channel_id=1, source_target_pairs={{0,2},{1,5},{2,0},{3,7},{4,6},{5,1},{6,4},{7,3},{8,10},{9,13},{10,... | collective-permute-start | bytes 233480 | tf_op jit(solution)/shard_map/cond/branch_1_fun/ppermute | solution.py:601
  51.5 3.2 %collective-permute-done.39 = f32[152,128]{1,0:T(8,128)S(1)} collective-permute-done((f32[152,128]{1,0:T(8,128)S(1)}, f32[152,128]{1,0:T(8,128)S(1)}, u32[]{:S(2)}, u32[]{:S(2)}) %collective-permute-start.39) | collective-permute-done | bytes 77856 | tf_op jit(solution)/shard_map/cond/branch_1_fun/ppermute | solution.py:601
  54.7 0.1 collective-permute-start.40
  54.8 1.4 %collective-permute-start.48 = (f32[304,128]{1,0:T(8,128)S(1)}, f32[304,128]{1,0:T(8,128)S(1)}, u32[]{:S(2)}, u32[]{:S(2)}) collective-permute-start(f32[304,128]{1,0:T(8,128)S(1)} %pad_maximum_fusion.15), channel_id=1, source_target_pairs={{0,4},{1,3},{2,6},{3,1},{4,0},{5,7},{6,2},{7,5},{8,12},{9,11},{10,... | collective-permute-start | bytes 466952 | tf_op jit(solution)/shard_map/cond/branch_1_fun/ppermute | solution.py:601
  56.2 1.8 %collective-permute-done.40 = f32[152,128]{1,0:T(8,128)S(1)} collective-permute-done((f32[152,128]{1,0:T(8,128)S(1)}, f32[152,128]{1,0:T(8,128)S(1)}, u32[]{:S(2)}, u32[]{:S(2)}) %collective-permute-start.40) | collective-permute-done | bytes 77856 | tf_op jit(solution)/shard_map/cond/branch_1_fun/ppermute | solution.py:601
  58.0 1.4 %collective-permute-start.41 = (f32[304,128]{1,0:T(8,128)S(1)}, f32[304,128]{1,0:T(8,128)S(1)}, u32[]{:S(2)}, u32[]{:S(2)}) collective-permute-start(f32[304,128]{1,0:T(8,128)S(1)} %pad_maximum_fusion.14), channel_id=1, source_target_pairs={{0,4},{1,3},{2,6},{3,1},{4,0},{5,7},{6,2},{7,5},{8,12},{9,11},{10,... | collective-permute-start | bytes 466952 | tf_op jit(solution)/shard_map/cond/branch_1_fun/ppermute | solution.py:601
  59.4 0.4 collective-permute-done.48
  59.9 6.0 %collective-permute-start.49 = (f32[608,128]{1,0:T(8,128)S(1)}, f32[608,128]{1,0:T(8,128)S(1)}, u32[]{:S(2)}, u32[]{:S(2)}) collective-permute-start(f32[608,128]{1,0:T(8,128)S(1)} %pad_maximum_fusion.11.mine_ref), channel_id=1, source_target_pairs={{0,1},{1,0},{2,3},{3,2},{4,5},{5,4},{6,7},{7,6},{8,9},{9,8},{10,11... | collective-permute-start | bytes 933896 | tf_op jit(solution)/shard_map/cond/branch_1_fun/ppermute | solution.py:601
  65.9 1.6 %collective-permute-start.42 = (f32[608,128]{1,0:T(8,128)S(1)}, f32[608,128]{1,0:T(8,128)S(1)}, u32[]{:S(2)}, u32[]{:S(2)}) collective-permute-start(f32[608,128]{1,0:T(8,128)S(1)} %pad_maximum_fusion.10.mine_ref), channel_id=1, source_target_pairs={{0,1},{1,0},{2,3},{3,2},{4,5},{5,4},{6,7},{7,6},{8,9},{9,8},{10,11... | collective-permute-start | bytes 933896 | tf_op jit(solution)/shard_map/cond/branch_1_fun/ppermute | solution.py:601
  67.5 0.0 collective-permute-done.49.other_ref
  67.6 2.2 %update.3 = (f32[1000,768]{1,0:T(8,128)}, f32[1000,256]{1,0:T(8,128)}, bf16[768,768]{1,0:T(8,128)(2,1)S(1)}) custom-call(f32[608,128]{1,0:T(8,128)S(1)} %pad_maximum_fusion.11.mine_ref, f32[608,128]{1,0:T(8,128)S(1)} %collective-permute-done.49.other_ref, f32[1000,256]{1,0:T(8,128)S(1)} %copy-done.4, s32[1,256]{1,0:T(1,128)S(1)} %copy-done.8, ...), custom_call_target="tpu_custom_call" | custom-call | flops 717225984 | bytes 3670016 | tf_op jit(solution)/shard_map/cond/branch_1_fun/update/pallas_call | solution.py:540
  69.8 0.0 collective-permute-done.42.other_ref
  69.8 2.0 %update_more.3 = (f32[1000,768]{1,0:T(8,128)}, f32[1000,256]{1,0:T(8,128)}) custom-call(f32[608,128]{1,0:T(8,128)S(1)} %pad_maximum_fusion.10.mine_ref, f32[608,128]{1,0:T(8,128)S(1)} %collective-permute-done.42.other_ref, f32[1000,256]{1,0:T(8,128)S(1)} %copy-done.4, f32[1000,768]{1,0:T(8,128)S(1)} %copy-done.2, ...), custom_call_target="tpu_custom_call", output_to_operand_aliasing={{0}: (5, {}), {1}: (6, {})} | custom-call | flops 651165696 | bytes 4521984 | tf_op jit(solution)/shard_map/cond/branch_1_fun/update_more/pallas_call | solution.py:577
  (29 shorter events, 0.4 us)
Async XLA Ops:
  4.8 5.4 %copy-start.8 = (s32[1,256]{1,0:T(1,128)S(1)}, s32[1,256]{1,0:T(1,128)}, u32[]{:S(2)}) copy-start(s32[1,256]{1,0:T(1,128)} %get-tuple-element.58.index_hbm.index_ref) | copy-start | bytes 3076 | tf_op jit(solution)/shard_map/cond
  4.8 5.8 %copy-start.10 = (s32[320]{0:T(512)S(1)}, s32[320]{0:T(512)}, u32[]{:S(2)}) copy-start(s32[320]{0:T(512)} %get-tuple-element.60) | copy-start | bytes 3844 | tf_op jit(solution)/shard_map/cond
  4.8 5.8 %copy-start = (bf16[768,3072]{1,0:T(8,128)(2,1)S(1)}, bf16[768,3072]{1,0:T(8,128)(2,1)}, u32[]{:S(2)}) copy-start(bf16[768,3072]{1,0:T(8,128)(2,1)} %get-tuple-element.59.centers_hbm.centers_ref) | copy-start | bytes 14155780 | tf_op jit(solution)/shard_map/cond
  4.8 8.7 %collective-permute-start.29 = (bf16[32,1536]{1,0:T(8,128)(2,1)S(1)}, bf16[32,1536]{1,0:T(8,128)(2,1)S(1)}, u32[]{:S(2)}, u32[]{:S(2)}) collective-permute-start(bf16[32,1536]{1,0:T(8,128)(2,1)S(1)} %pack_rows.3), channel_id=1, source_target_pairs={{0,8},{1,9},{2,10},{3,11},{4,12},{5,13},{6,14},{7,15},{8,0},{9,1},... | collective-permute-start | bytes 294920 | tf_op jit(solution)/shard_map/cond/branch_1_fun/ppermute | solution.py:601
  9.9 1.9 %copy-start.2 = (f32[1000,768]{1,0:T(8,128)S(1)}, f32[1000,768]{1,0:T(8,128)}, u32[]{:S(2)}) copy-start(f32[1000,768]{1,0:T(8,128)} %get-tuple-element.62.weights_ref) | copy-start | bytes 9216004 | tf_op jit(solution)/shard_map/cond
  9.9 1.9 %copy-start.6 = (f32[160,320]{1,0:T(8,128)S(1)}, f32[160,320]{1,0:T(8,128)}, u32[]{:S(2)}) copy-start(f32[160,320]{1,0:T(8,128)} %get-tuple-element.61.eigvec_ref) | copy-start | bytes 614404 | tf_op jit(solution)/shard_map/cond
  10.0 6.0 %collective-permute-start.28 = (bf16[32,1536]{1,0:T(8,128)(2,1)S(1)}, bf16[32,1536]{1,0:T(8,128)(2,1)S(1)}, u32[]{:S(2)}, u32[]{:S(2)}) collective-permute-start(bf16[32,1536]{1,0:T(8,128)(2,1)S(1)} %pack_rows.2), channel_id=1, source_target_pairs={{0,8},{1,9},{2,10},{3,11},{4,12},{5,13},{6,14},{7,15},{8,0},{9,1},... | collective-permute-start | bytes 294920 | tf_op jit(solution)/shard_map/cond/branch_1_fun/ppermute | solution.py:601
  13.5 6.3 %collective-permute-start.30 = (bf16[64,1536]{1,0:T(8,128)(2,1)S(1)}, bf16[64,1536]{1,0:T(8,128)(2,1)S(1)}, u32[]{:S(2)}, u32[]{:S(2)}) collective-permute-start(bf16[64,1536]{1,0:T(8,128)(2,1)S(1)} %pad_maximum_fusion.13.keep_ref), channel_id=1, source_target_pairs={{0,2},{1,5},{2,0},{3,7},{4,6},{5,1},{6,4},{7,3},{8,10},{9,13},{10,... | collective-permute-start | bytes 589832 | tf_op jit(solution)/shard_map/cond/branch_1_fun/ppermute | solution.py:601
  16.0 6.0 %collective-permute-start.33 = (bf16[64,1536]{1,0:T(8,128)(2,1)S(1)}, bf16[64,1536]{1,0:T(8,128)(2,1)S(1)}, u32[]{:S(2)}, u32[]{:S(2)}) collective-permute-start(bf16[64,1536]{1,0:T(8,128)(2,1)S(1)} %pad_maximum_fusion.12.keep_ref), channel_id=1, source_target_pairs={{0,2},{1,5},{2,0},{3,7},{4,6},{5,1},{6,4},{7,3},{8,10},{9,13},{10,... | collective-permute-start | bytes 589832 | tf_op jit(solution)/shard_map/cond/branch_1_fun/ppermute | solution.py:601
  20.2 6.6 %collective-permute-start.31 = (bf16[96,1536]{1,0:T(8,128)(2,1)S(1)}, bf16[96,1536]{1,0:T(8,128)(2,1)S(1)}, u32[]{:S(2)}, u32[]{:S(2)}) collective-permute-start(bf16[96,1536]{1,0:T(8,128)(2,1)S(1)} %squeeze_slots.2), channel_id=1, source_target_pairs={{0,4},{1,3},{2,6},{3,1},{4,0},{5,7},{6,2},{7,5},{8,12},{9,11},{10,... | collective-permute-start | bytes 884744 | tf_op jit(solution)/shard_map/cond/branch_1_fun/ppermute | solution.py:601
  22.4 7.6 %collective-permute-start.34 = (bf16[96,1536]{1,0:T(8,128)(2,1)S(1)}, bf16[96,1536]{1,0:T(8,128)(2,1)S(1)}, u32[]{:S(2)}, u32[]{:S(2)}) collective-permute-start(bf16[96,1536]{1,0:T(8,128)(2,1)S(1)} %squeeze_slots.3), channel_id=1, source_target_pairs={{0,4},{1,3},{2,6},{3,1},{4,0},{5,7},{6,2},{7,5},{8,12},{9,11},{10,... | collective-permute-start | bytes 884744 | tf_op jit(solution)/shard_map/cond/branch_1_fun/ppermute | solution.py:601
  26.9 5.1 %collective-permute-start.32 = (bf16[192,1536]{1,0:T(8,128)(2,1)S(1)}, bf16[192,1536]{1,0:T(8,128)(2,1)S(1)}, u32[]{:S(2)}, u32[]{:S(2)}) collective-permute-start(bf16[192,1536]{1,0:T(8,128)(2,1)S(1)} %pad_maximum_fusion.8.mine_ref), channel_id=1, source_target_pairs={{0,1},{1,0},{2,3},{3,2},{4,5},{5,4},{6,7},{7,6},{8,9},{9,8},{10,11... | collective-permute-start | bytes 1769480 | tf_op jit(solution)/shard_map/cond/branch_1_fun/ppermute | solution.py:601
  30.0 3.6 %collective-permute-start.35 = (bf16[192,1536]{1,0:T(8,128)(2,1)S(1)}, bf16[192,1536]{1,0:T(8,128)(2,1)S(1)}, u32[]{:S(2)}, u32[]{:S(2)}) collective-permute-start(bf16[192,1536]{1,0:T(8,128)(2,1)S(1)} %pad_maximum_fusion.9.next_ref), channel_id=1, source_target_pairs={{0,1},{1,0},{2,3},{3,2},{4,5},{5,4},{6,7},{7,6},{8,9},{9,8},{10,11... | collective-permute-start | bytes 1769480 | tf_op jit(solution)/shard_map/cond/branch_1_fun/ppermute | solution.py:601
  36.0 1.7 %collective-permute-start.43 = (f32[608,128]{1,0:T(8,128)S(1)}, f32[608,128]{1,0:T(8,128)S(1)}, u32[]{:S(2)}, u32[]{:S(2)}) collective-permute-start(f32[608,128]{1,0:T(8,128)S(1)} %get-tuple-element.81), channel_id=1, source_target_pairs={{0,1},{1,0},{2,3},{3,2},{4,5},{5,4},{6,7},{7,6},{8,9},{9,8},{10,11... | collective-permute-start | bytes 933896 | tf_op jit(solution)/shard_map/cond/branch_1_fun/ppermute | solution.py:601
  37.4 1.7 %collective-permute-start.36 = (f32[608,128]{1,0:T(8,128)S(1)}, f32[608,128]{1,0:T(8,128)S(1)}, u32[]{:S(2)}, u32[]{:S(2)}) collective-permute-start(f32[608,128]{1,0:T(8,128)S(1)} %get-tuple-element.78), channel_id=1, source_target_pairs={{0,1},{1,0},{2,3},{3,2},{4,5},{5,4},{6,7},{7,6},{8,9},{9,8},{10,11... | collective-permute-start | bytes 933896 | tf_op jit(solution)/shard_map/cond/branch_1_fun/ppermute | solution.py:601
  37.7 29.9 %copy-start.4 = (f32[1000,256]{1,0:T(8,128)S(1)}, f32[1000,256]{1,0:T(8,128)}, u32[]{:S(2)}) copy-start(f32[1000,256]{1,0:T(8,128)} %get-tuple-element.79.targets_ref) | copy-start | bytes 3072004 | tf_op jit(solution)/shard_map/cond
  37.7 29.9 %copy-start.12 = (f32[1,160]{1,0:T(1,128)S(1)}, f32[1,160]{1,0:T(1,128)}, u32[]{:S(2)}) copy-start(f32[1,160]{1,0:T(1,128)} %get-tuple-element.82.eigval_ref) | copy-start | bytes 1924 | tf_op jit(solution)/shard_map/cond
  37.7 4.4 %collective-permute-start.44 = (f32[304,128]{1,0:T(8,128)S(1)}, f32[304,128]{1,0:T(8,128)S(1)}, u32[]{:S(2)}, u32[]{:S(2)}) collective-permute-start(f32[304,128]{1,0:T(8,128)S(1)} %slice.96), channel_id=1, source_target_pairs={{0,4},{1,3},{2,6},{3,1},{4,0},{5,7},{6,2},{7,5},{8,12},{9,11},{10,... | collective-permute-start | bytes 466952 | tf_op jit(solution)/shard_map/cond/branch_1_fun/ppermute | solution.py:601
  39.2 4.7 %collective-permute-start.37 = (f32[304,128]{1,0:T(8,128)S(1)}, f32[304,128]{1,0:T(8,128)S(1)}, u32[]{:S(2)}, u32[]{:S(2)}) collective-permute-start(f32[304,128]{1,0:T(8,128)S(1)} %slice.92), channel_id=1, source_target_pairs={{0,4},{1,3},{2,6},{3,1},{4,0},{5,7},{6,2},{7,5},{8,12},{9,11},{10,... | collective-permute-start | bytes 466952 | tf_op jit(solution)/shard_map/cond/branch_1_fun/ppermute | solution.py:601
  42.2 3.3 %collective-permute-start.45 = (f32[152,128]{1,0:T(8,128)S(1)}, f32[152,128]{1,0:T(8,128)S(1)}, u32[]{:S(2)}, u32[]{:S(2)}) collective-permute-start(f32[152,128]{1,0:T(8,128)S(1)} %slice.98), channel_id=1, source_target_pairs={{0,2},{1,5},{2,0},{3,7},{4,6},{5,1},{6,4},{7,3},{8,10},{9,13},{10,... | collective-permute-start | bytes 233480 | tf_op jit(solution)/shard_map/cond/branch_1_fun/ppermute | solution.py:601
  43.9 4.1 %collective-permute-start.38 = (f32[152,128]{1,0:T(8,128)S(1)}, f32[152,128]{1,0:T(8,128)S(1)}, u32[]{:S(2)}, u32[]{:S(2)}) collective-permute-start(f32[152,128]{1,0:T(8,128)S(1)} %slice.94), channel_id=1, source_target_pairs={{0,2},{1,5},{2,0},{3,7},{4,6},{5,1},{6,4},{7,3},{8,10},{9,13},{10,... | collective-permute-start | bytes 233480 | tf_op jit(solution)/shard_map/cond/branch_1_fun/ppermute | solution.py:601
  45.5 4.2 %collective-permute-start.46 = (f32[152,128]{1,0:T(8,128)S(1)}, f32[152,128]{1,0:T(8,128)S(1)}, u32[]{:S(2)}, u32[]{:S(2)}) collective-permute-start(f32[152,128]{1,0:T(8,128)S(1)} %slice_add_fusion.10), channel_id=1, source_target_pairs={{0,8},{1,9},{2,10},{3,11},{4,12},{5,13},{6,14},{7,15},{8,0},{9,1},... | collective-permute-start | bytes 233480 | tf_op jit(solution)/shard_map/cond/branch_1_fun/ppermute | solution.py:601
  48.0 6.7 %collective-permute-start.39 = (f32[152,128]{1,0:T(8,128)S(1)}, f32[152,128]{1,0:T(8,128)S(1)}, u32[]{:S(2)}, u32[]{:S(2)}) collective-permute-start(f32[152,128]{1,0:T(8,128)S(1)} %slice_add_fusion.11), channel_id=1, source_target_pairs={{0,8},{1,9},{2,10},{3,11},{4,12},{5,13},{6,14},{7,15},{8,0},{9,1},... | collective-permute-start | bytes 233480 | tf_op jit(solution)/shard_map/cond/branch_1_fun/ppermute | solution.py:601
  49.8 5.0 %collective-permute-start.47 = (f32[152,128]{1,0:T(8,128)S(1)}, f32[152,128]{1,0:T(8,128)S(1)}, u32[]{:S(2)}, u32[]{:S(2)}) collective-permute-start(f32[152,128]{1,0:T(8,128)S(1)} %add.135), channel_id=1, source_target_pairs={{0,2},{1,5},{2,0},{3,7},{4,6},{5,1},{6,4},{7,3},{8,10},{9,13},{10,... | collective-permute-start | bytes 233480 | tf_op jit(solution)/shard_map/cond/branch_1_fun/ppermute | solution.py:601
  54.7 3.3 %collective-permute-start.40 = (f32[152,128]{1,0:T(8,128)S(1)}, f32[152,128]{1,0:T(8,128)S(1)}, u32[]{:S(2)}, u32[]{:S(2)}) collective-permute-start(f32[152,128]{1,0:T(8,128)S(1)} %add.131), channel_id=1, source_target_pairs={{0,2},{1,5},{2,0},{3,7},{4,6},{5,1},{6,4},{7,3},{8,10},{9,13},{10,... | collective-permute-start | bytes 233480 | tf_op jit(solution)/shard_map/cond/branch_1_fun/ppermute | solution.py:601
  54.8 5.1 %collective-permute-start.48 = (f32[304,128]{1,0:T(8,128)S(1)}, f32[304,128]{1,0:T(8,128)S(1)}, u32[]{:S(2)}, u32[]{:S(2)}) collective-permute-start(f32[304,128]{1,0:T(8,128)S(1)} %pad_maximum_fusion.15), channel_id=1, source_target_pairs={{0,4},{1,3},{2,6},{3,1},{4,0},{5,7},{6,2},{7,5},{8,12},{9,11},{10,... | collective-permute-start | bytes 466952 | tf_op jit(solution)/shard_map/cond/branch_1_fun/ppermute | solution.py:601
  58.0 7.9 %collective-permute-start.41 = (f32[304,128]{1,0:T(8,128)S(1)}, f32[304,128]{1,0:T(8,128)S(1)}, u32[]{:S(2)}, u32[]{:S(2)}) collective-permute-start(f32[304,128]{1,0:T(8,128)S(1)} %pad_maximum_fusion.14), channel_id=1, source_target_pairs={{0,4},{1,3},{2,6},{3,1},{4,0},{5,7},{6,2},{7,5},{8,12},{9,11},{10,... | collective-permute-start | bytes 466952 | tf_op jit(solution)/shard_map/cond/branch_1_fun/ppermute | solution.py:601
  59.9 7.7 %collective-permute-start.49 = (f32[608,128]{1,0:T(8,128)S(1)}, f32[608,128]{1,0:T(8,128)S(1)}, u32[]{:S(2)}, u32[]{:S(2)}) collective-permute-start(f32[608,128]{1,0:T(8,128)S(1)} %pad_maximum_fusion.11.mine_ref), channel_id=1, source_target_pairs={{0,1},{1,0},{2,3},{3,2},{4,5},{5,4},{6,7},{7,6},{8,9},{9,8},{10,11... | collective-permute-start | bytes 933896 | tf_op jit(solution)/shard_map/cond/branch_1_fun/ppermute | solution.py:601
  65.9 3.9 %collective-permute-start.42 = (f32[608,128]{1,0:T(8,128)S(1)}, f32[608,128]{1,0:T(8,128)S(1)}, u32[]{:S(2)}, u32[]{:S(2)}) collective-permute-start(f32[608,128]{1,0:T(8,128)S(1)} %pad_maximum_fusion.10.mine_ref), channel_id=1, source_target_pairs={{0,1},{1,0},{2,3},{3,2},{4,5},{5,4},{6,7},{7,6},{8,9},{9,8},{10,11... | collective-permute-start | bytes 933896 | tf_op jit(solution)/shard_map/cond/branch_1_fun/ppermute | solution.py:601

commit v17 on v16

--- a/solution.py
+++ b/solution.py
@@ -17,7 +17,7 @@
 PARTS = 2
 SLOTS = 32
 GROUP_SLOTS = 96
-BLOCKS = 2
+BLOCKS = 3
 NT = (((1,), (1,)), ((), ()))
 NN = (((1,), (0,)), ((), ()))
 VMEM_LIMIT = 24 * 1024 * 1024
@@ -549,7 +549,7 @@
         scratch_shapes=[
             pltpu.VMEM((padded, rows), F32),
             pltpu.VMEM((here, count), F32),
-            pltpu.SemaphoreType.DMA((4,)),
+            pltpu.SemaphoreType.DMA((8,)),
         ],
         compiler_params=params(),
         cost_estimate=pl.CostEstimate(
@@ -586,7 +586,7 @@
         scratch_shapes=[
             pltpu.VMEM((padded, rows), F32),
             pltpu.VMEM((here, count), F32),
-            pltpu.SemaphoreType.DMA((6,)),
+            pltpu.SemaphoreType.DMA((9,)),
         ],
         compiler_params=params(),
         cost_estimate=pl.CostEstimate(

time: 72.1 us -> 73.2 us (1.015)
  starting transfers between devices: 34.4 us -> 37.3 us
  waiting for transfers between devices: 16.9 us -> 14.2 us
  Pallas kernels: 18.2 us -> 19 us
    ppermute x22, starting transfers between devices: 34.4 us -> 37.3 us  [swap(): lax.ppermute(x, AXES, [(i, i ^ flip[i & 1]) for i in range(2 * chips)])]
    ppermute x22, waiting for transfers between devices: 16.9 us -> 14.2 us  [swap(): lax.ppermute(x, AXES, [(i, i ^ flip[i & 1]) for i in range(2 * chips)])]
    pallas_call x1, Pallas kernels: 1.97 us -> 2.71 us  [update_more(): pl.pallas_call(functools.partial(update_more_body, begin), in_specs=[vmem...]
  transfers between devices with their start and end apart: 22 -> 22, of which waited for: 13 -> 14; matrix products, arithmetic and copies ran while one was open for 1% -> 1% of each run, Pallas kernels for 15% -> 15%
where the time goes in v17:
time: 73.2 us; the launch traced here: 72.9 us
  starting transfers between devices  37.3 us (51%)
  Pallas kernels  19 us (26%)
  waiting for transfers between devices  14.2 us (19%)
  between operations  1.45 us (2%)
    ppermute x22, starting transfers between devices, swap(): lax.ppermute(x, AXES, [(i, i ^ flip[i & 1]) for i in range(2 * chips)])  37.3 us
    ppermute x22, waiting for transfers between devices, swap(): lax.ppermute(x, AXES, [(i, i ^ flip[i & 1]) for i in range(2 * chips)])  14.2 us
    pallas_call x2, Pallas kernels, pack_rows(): pl.pallas_call(functools.partial(pack_body, part * depth), in_specs=[hbm,...  3.84 us
    pallas_call x1, Pallas kernels, update_more(): pl.pallas_call(functools.partial(update_more_body, begin), in_specs=[vmem...  2.71 us
    pallas_call x1, Pallas kernels, update(): pl.pallas_call(update_body, in_specs=[vmem] * 7, out_specs=[hbm, hbm, vme...  2.65 us
    pallas_call x1, Pallas kernels, predict(): pl.pallas_call(predict_body, in_specs=[vmem] * 6, out_specs=[vmem] * 3, o...  2.25 us
    pallas_call x1, Pallas kernels, spread_weights(): pl.pallas_call(functools.partial(spread_body, first, classes), out_shape=...  1.6 us
  transfers between devices with their start and end apart: 22, of which 14 were waited for; matrix products, arithmetic and copies ran while one was open for 1% of the time, Pallas kernels for 15%

profile of v17, /device:TPU:1, one launch (start us, length us, event | category | flops | bytes accessed | tf_op | source)
XLA Modules:
  0.0 72.9 jit_solution(14064938776008590025)
XLA Ops:
  0.6 1.4 %rows_fit.1 = s32[1]{0:T(128)} custom-call(s32[1,256]{1,0:T(1,128)} %bitcast.17), custom_call_target="tpu_custom_call" | custom-call | tf_op jit(solution)/shard_map/rows_fit/pallas_call | solution.py:157
  2.6 70.1 %conditional.1 = ((f32[1000,768]{1,0:T(8,128)}, f32[1000,256]{1,0:T(8,128)})) conditional(s32[]{:T(128)} %bitcast.2, (s32[1,256]{1,0:T(1,128)}, bf16[768,3072]{1,0:T(8,128)(2,1)}, s32[320]{0:T(512)}, f32[160,320]{1,0:T(8,128)}, f32[1000,768]{1,0:T(8,128)}, /*index=5*/f32[1000,256]{1,0:T(8,128)}, f32[1,160]{1,0:T(1,128)}) %tuple.31, ...), branch_computations={%region_0.1_spmd, %region_1.2_spmd} | conditional | flops 5916241920 | bytes 106008064 | solution.py:686
  2.8 1.9 %pack_rows.3 = bf16[32,1536]{1,0:T(8,128)(2,1)S(1)} custom-call(s32[1,256]{1,0:T(1,128)} %get-tuple-element.58.index_hbm.index_ref, bf16[768,3072]{1,0:T(8,128)(2,1)} %get-tuple-element.59.centers_hbm.centers_ref), custom_call_target="tpu_custom_call" | custom-call | flops 75497472 | bytes 2457600 | tf_op jit(solution)/shard_map/cond/branch_1_fun/pack_rows/pallas_call | solution.py:199
  4.8 0.0 copy-start.8
  4.8 0.0 copy-start.10
  4.8 0.0 copy-start
  4.8 3.2 %collective-permute-start.29 = (bf16[32,1536]{1,0:T(8,128)(2,1)S(1)}, bf16[32,1536]{1,0:T(8,128)(2,1)S(1)}, u32[]{:S(2)}, u32[]{:S(2)}) collective-permute-start(bf16[32,1536]{1,0:T(8,128)(2,1)S(1)} %pack_rows.3), channel_id=1, source_target_pairs={{0,8},{1,9},{2,10},{3,11},{4,12},{5,13},{6,14},{7,15},{8,0},{9,1},... | collective-permute-start | bytes 294920 | tf_op jit(solution)/shard_map/cond/branch_1_fun/ppermute | solution.py:601
  8.0 1.9 %pack_rows.2 = bf16[32,1536]{1,0:T(8,128)(2,1)S(1)} custom-call(s32[1,256]{1,0:T(1,128)} %get-tuple-element.58.index_hbm.index_ref, bf16[768,3072]{1,0:T(8,128)(2,1)} %get-tuple-element.59.centers_hbm.centers_ref), custom_call_target="tpu_custom_call" | custom-call | flops 75497472 | bytes 2457600 | tf_op jit(solution)/shard_map/cond/branch_1_fun/pack_rows/pallas_call | solution.py:199
  9.9 0.0 copy-start.2
  9.9 0.0 copy-start.6
  10.0 0.2 collective-permute-start.28
  10.2 0.4 select_packed.1
  10.6 1.2 %center_norms.3.norm_ref = f32[768,128]{1,0:T(8,128)S(1)} custom-call(bf16[768,3072]{1,0:T(8,128)(2,1)S(1)} %copy-done), custom_call_target="tpu_custom_call" | custom-call | flops 4718592 | bytes 4718592 | tf_op jit(solution)/shard_map/cond/branch_1_fun/center_norms/pallas_call | solution.py:341
  11.8 0.0 copy-done.2
  11.8 1.6 %spread_weights.3 = (bf16[608,2304]{1,0:T(8,128)(2,1)S(1)}, bf16[608,2304]{1,0:T(8,128)(2,1)S(1)}, f32[160,768]{1,0:T(8,128)S(1)}) custom-call(s32[1,320]{1,0:T(1,128)S(1)} %reshape.99.index_ref, f32[160,320]{1,0:T(8,128)S(1)} %copy-done.6, f32[1000,768]{1,0:T(8,128)S(1)} %copy-done.2), custom_call_target="tpu_custom_call" | custom-call | flops 235929600 | bytes 7471104 | tf_op jit(solution)/shard_map/cond/branch_1_fun/spread_weights/pallas_call | solution.py:316
  13.4 0.0 collective-permute-done.29
  13.4 2.6 %collective-permute-start.30 = (bf16[64,1536]{1,0:T(8,128)(2,1)S(1)}, bf16[64,1536]{1,0:T(8,128)(2,1)S(1)}, u32[]{:S(2)}, u32[]{:S(2)}) collective-permute-start(bf16[64,1536]{1,0:T(8,128)(2,1)S(1)} %pad_maximum_fusion.13.keep_ref), channel_id=1, source_target_pairs={{0,2},{1,5},{2,0},{3,7},{4,6},{5,1},{6,4},{7,3},{8,10},{9,13},{10,... | collective-permute-start | bytes 589832 | tf_op jit(solution)/shard_map/cond/branch_1_fun/ppermute | solution.py:601
  16.0 0.0 collective-permute-done.28
  16.0 2.1 %collective-permute-start.33 = (bf16[64,1536]{1,0:T(8,128)(2,1)S(1)}, bf16[64,1536]{1,0:T(8,128)(2,1)S(1)}, u32[]{:S(2)}, u32[]{:S(2)}) collective-permute-start(bf16[64,1536]{1,0:T(8,128)(2,1)S(1)} %pad_maximum_fusion.12.keep_ref), channel_id=1, source_target_pairs={{0,2},{1,5},{2,0},{3,7},{4,6},{5,1},{6,4},{7,3},{8,10},{9,13},{10,... | collective-permute-start | bytes 589832 | tf_op jit(solution)/shard_map/cond/branch_1_fun/ppermute | solution.py:601
  18.1 1.6 %collective-permute-done.30.got_ref = bf16[64,1536]{1,0:T(8,128)(2,1)S(1)} collective-permute-done((bf16[64,1536]{1,0:T(8,128)(2,1)S(1)}, bf16[64,1536]{1,0:T(8,128)(2,1)S(1)}, u32[]{:S(2)}, u32[]{:S(2)}) %collective-permute-start.30) | collective-permute-done | bytes 196640 | tf_op jit(solution)/shard_map/cond/branch_1_fun/ppermute | solution.py:601
  19.7 0.3 squeeze_slots.2
  20.1 1.5 %collective-permute-start.31 = (bf16[96,1536]{1,0:T(8,128)(2,1)S(1)}, bf16[96,1536]{1,0:T(8,128)(2,1)S(1)}, u32[]{:S(2)}, u32[]{:S(2)}) collective-permute-start(bf16[96,1536]{1,0:T(8,128)(2,1)S(1)} %squeeze_slots.2), channel_id=1, source_target_pairs={{0,4},{1,3},{2,6},{3,1},{4,0},{5,7},{6,2},{7,5},{8,12},{9,11},{10,... | collective-permute-start | bytes 884744 | tf_op jit(solution)/shard_map/cond/branch_1_fun/ppermute | solution.py:601
  21.6 0.5 collective-permute-done.33.got_ref
  22.1 0.3 squeeze_slots.3
  22.4 1.3 %collective-permute-start.34 = (bf16[96,1536]{1,0:T(8,128)(2,1)S(1)}, bf16[96,1536]{1,0:T(8,128)(2,1)S(1)}, u32[]{:S(2)}, u32[]{:S(2)}) collective-permute-start(bf16[96,1536]{1,0:T(8,128)(2,1)S(1)} %squeeze_slots.3), channel_id=1, source_target_pairs={{0,4},{1,3},{2,6},{3,1},{4,0},{5,7},{6,2},{7,5},{8,12},{9,11},{10,... | collective-permute-start | bytes 884744 | tf_op jit(solution)/shard_map/cond/branch_1_fun/ppermute | solution.py:601
  23.7 3.1 %collective-permute-done.31 = bf16[96,1536]{1,0:T(8,128)(2,1)S(1)} collective-permute-done((bf16[96,1536]{1,0:T(8,128)(2,1)S(1)}, bf16[96,1536]{1,0:T(8,128)(2,1)S(1)}, u32[]{:S(2)}, u32[]{:S(2)}) %collective-permute-start.31) | collective-permute-done | bytes 294944 | tf_op jit(solution)/shard_map/cond/branch_1_fun/ppermute | solution.py:601
  26.9 0.9 %collective-permute-start.32 = (bf16[192,1536]{1,0:T(8,128)(2,1)S(1)}, bf16[192,1536]{1,0:T(8,128)(2,1)S(1)}, u32[]{:S(2)}, u32[]{:S(2)}) collective-permute-start(bf16[192,1536]{1,0:T(8,128)(2,1)S(1)} %pad_maximum_fusion.8.mine_ref), channel_id=1, source_target_pairs={{0,1},{1,0},{2,3},{3,2},{4,5},{5,4},{6,7},{7,6},{8,9},{9,8},{10,11... | collective-permute-start | bytes 1769480 | tf_op jit(solution)/shard_map/cond/branch_1_fun/ppermute | solution.py:601
  27.8 2.2 %collective-permute-done.34 = bf16[96,1536]{1,0:T(8,128)(2,1)S(1)} collective-permute-done((bf16[96,1536]{1,0:T(8,128)(2,1)S(1)}, bf16[96,1536]{1,0:T(8,128)(2,1)S(1)}, u32[]{:S(2)}, u32[]{:S(2)}) %collective-permute-start.34) | collective-permute-done | bytes 294944 | tf_op jit(solution)/shard_map/cond/branch_1_fun/ppermute | solution.py:601
  30.0 2.0 %collective-permute-start.35 = (bf16[192,1536]{1,0:T(8,128)(2,1)S(1)}, bf16[192,1536]{1,0:T(8,128)(2,1)S(1)}, u32[]{:S(2)}, u32[]{:S(2)}) collective-permute-start(bf16[192,1536]{1,0:T(8,128)(2,1)S(1)} %pad_maximum_fusion.9.next_ref), channel_id=1, source_target_pairs={{0,1},{1,0},{2,3},{3,2},{4,5},{5,4},{6,7},{7,6},{8,9},{9,8},{10,11... | collective-permute-start | bytes 1769480 | tf_op jit(solution)/shard_map/cond/branch_1_fun/ppermute | solution.py:601
  32.0 0.0 collective-permute-done.32.other_ref
  32.0 1.5 %distances.3 = (f32[768,256]{1,0:T(8,128)S(1)}, bf16[256,1536]{1,0:T(8,128)(2,1)S(1)}) custom-call(bf16[192,1536]{1,0:T(8,128)(2,1)S(1)} %pad_maximum_fusion.8.mine_ref, bf16[192,1536]{1,0:T(8,128)(2,1)S(1)} %collective-permute-done.32.other_ref, bf16[192,1536]{1,0:T(8,128)(2,1)S(1)} %pad_maximum_fusion.9.next_ref, ...), custom_call_target="tpu_custom_call" | custom-call | flops 603979776 | bytes 3145728 | tf_op jit(solution)/shard_map/cond/branch_1_fun/distances/pallas_call | solution.py:416
  33.5 0.2 collective-permute-done.35.other_ref
  33.7 2.2 %predict.3 = (f32[608,128]{1,0:T(8,128)S(1)}, f32[608,128]{1,0:T(8,128)S(1)}, bf16[2304,256]{1,0:T(8,128)(2,1)S(1)}) custom-call(bf16[256,1536]{1,0:T(8,128)(2,1)S(1)} %get-tuple-element.73.found_ref, bf16[192,1536]{1,0:T(8,128)(2,1)S(1)} %collective-permute-done.35.other_ref, bf16[256,512]{1,0:T(8,128)(2,1)S(1)} %get-tuple-element.71.select_ref, ...), custom_call_target="tpu_custom_call" | custom-call | flops 1321205760 | bytes 5636096 | tf_op jit(solution)/shard_map/cond/branch_1_fun/predict/pallas_call | solution.py:438
  35.9 0.4 collective-permute-start.43
  36.4 0.9 %predict_more.3 = (f32[608,128]{1,0:T(8,128)S(1)}, f32[608,128]{1,0:T(8,128)S(1)}) custom-call(bf16[608,2304]{1,0:T(8,128)(2,1)S(1)} %get-tuple-element.67.left, bf16[2304,256]{1,0:T(8,128)(2,1)S(1)} %get-tuple-element.76.right), custom_call_target="tpu_custom_call" | custom-call | flops 717225984 | bytes 3112960 | tf_op jit(solution)/shard_map/cond/branch_1_fun/predict_more/pallas_call | solution.py:458
  37.3 0.2 collective-permute-start.36
  37.5 0.1 collective-permute-done.43
  37.6 0.0 copy-start.4
  37.7 0.0 copy-start.12
  37.7 1.1 %collective-permute-start.44 = (f32[304,128]{1,0:T(8,128)S(1)}, f32[304,128]{1,0:T(8,128)S(1)}, u32[]{:S(2)}, u32[]{:S(2)}) collective-permute-start(f32[304,128]{1,0:T(8,128)S(1)} %slice.96), channel_id=1, source_target_pairs={{0,4},{1,3},{2,6},{3,1},{4,0},{5,7},{6,2},{7,5},{8,12},{9,11},{10,... | collective-permute-start | bytes 466952 | tf_op jit(solution)/shard_map/cond/branch_1_fun/ppermute | solution.py:601
  38.8 0.2 collective-permute-done.36
  39.0 1.1 %collective-permute-start.37 = (f32[304,128]{1,0:T(8,128)S(1)}, f32[304,128]{1,0:T(8,128)S(1)}, u32[]{:S(2)}, u32[]{:S(2)}) collective-permute-start(f32[304,128]{1,0:T(8,128)S(1)} %slice.92), channel_id=1, source_target_pairs={{0,4},{1,3},{2,6},{3,1},{4,0},{5,7},{6,2},{7,5},{8,12},{9,11},{10,... | collective-permute-start | bytes 466952 | tf_op jit(solution)/shard_map/cond/branch_1_fun/ppermute | solution.py:601
  40.1 2.0 %collective-permute-done.44 = f32[304,128]{1,0:T(8,128)S(1)} collective-permute-done((f32[304,128]{1,0:T(8,128)S(1)}, f32[304,128]{1,0:T(8,128)S(1)}, u32[]{:S(2)}, u32[]{:S(2)}) %collective-permute-start.44) | collective-permute-done | bytes 155680 | tf_op jit(solution)/shard_map/cond/branch_1_fun/ppermute | solution.py:601
  42.2 0.7 collective-permute-start.45
  42.8 0.9 %collective-permute-done.37 = f32[304,128]{1,0:T(8,128)S(1)} collective-permute-done((f32[304,128]{1,0:T(8,128)S(1)}, f32[304,128]{1,0:T(8,128)S(1)}, u32[]{:S(2)}, u32[]{:S(2)}) %collective-permute-start.37) | collective-permute-done | bytes 155680 | tf_op jit(solution)/shard_map/cond/branch_1_fun/ppermute | solution.py:601
  43.8 0.7 collective-permute-start.38
  44.5 1.0 %collective-permute-done.45 = f32[152,128]{1,0:T(8,128)S(1)} collective-permute-done((f32[152,128]{1,0:T(8,128)S(1)}, f32[152,128]{1,0:T(8,128)S(1)}, u32[]{:S(2)}, u32[]{:S(2)}) %collective-permute-start.45) | collective-permute-done | bytes 77856 | tf_op jit(solution)/shard_map/cond/branch_1_fun/ppermute | solution.py:601
  45.5 2.3 %collective-permute-start.46 = (f32[152,128]{1,0:T(8,128)S(1)}, f32[152,128]{1,0:T(8,128)S(1)}, u32[]{:S(2)}, u32[]{:S(2)}) collective-permute-start(f32[152,128]{1,0:T(8,128)S(1)} %slice_add_fusion.10), channel_id=1, source_target_pairs={{0,8},{1,9},{2,10},{3,11},{4,12},{5,13},{6,14},{7,15},{8,0},{9,1},... | collective-permute-start | bytes 233480 | tf_op jit(solution)/shard_map/cond/branch_1_fun/ppermute | solution.py:601
  47.8 0.0 collective-permute-done.38
  47.8 1.7 %collective-permute-start.39 = (f32[152,128]{1,0:T(8,128)S(1)}, f32[152,128]{1,0:T(8,128)S(1)}, u32[]{:S(2)}, u32[]{:S(2)}) collective-permute-start(f32[152,128]{1,0:T(8,128)S(1)} %slice_add_fusion.11), channel_id=1, source_target_pairs={{0,8},{1,9},{2,10},{3,11},{4,12},{5,13},{6,14},{7,15},{8,0},{9,1},... | collective-permute-start | bytes 233480 | tf_op jit(solution)/shard_map/cond/branch_1_fun/ppermute | solution.py:601
  49.5 0.2 collective-permute-done.46
  49.7 1.6 %collective-permute-start.47 = (f32[152,128]{1,0:T(8,128)S(1)}, f32[152,128]{1,0:T(8,128)S(1)}, u32[]{:S(2)}, u32[]{:S(2)}) collective-permute-start(f32[152,128]{1,0:T(8,128)S(1)} %add.135), channel_id=1, source_target_pairs={{0,2},{1,5},{2,0},{3,7},{4,6},{5,1},{6,4},{7,3},{8,10},{9,13},{10,... | collective-permute-start | bytes 233480 | tf_op jit(solution)/shard_map/cond/branch_1_fun/ppermute | solution.py:601
  51.3 1.4 %collective-permute-done.39 = f32[152,128]{1,0:T(8,128)S(1)} collective-permute-done((f32[152,128]{1,0:T(8,128)S(1)}, f32[152,128]{1,0:T(8,128)S(1)}, u32[]{:S(2)}, u32[]{:S(2)}) %collective-permute-start.39) | collective-permute-done | bytes 77856 | tf_op jit(solution)/shard_map/cond/branch_1_fun/ppermute | solution.py:601
  52.8 1.9 %collective-permute-start.40 = (f32[152,128]{1,0:T(8,128)S(1)}, f32[152,128]{1,0:T(8,128)S(1)}, u32[]{:S(2)}, u32[]{:S(2)}) collective-permute-start(f32[152,128]{1,0:T(8,128)S(1)} %add.131), channel_id=1, source_target_pairs={{0,2},{1,5},{2,0},{3,7},{4,6},{5,1},{6,4},{7,3},{8,10},{9,13},{10,... | collective-permute-start | bytes 233480 | tf_op jit(solution)/shard_map/cond/branch_1_fun/ppermute | solution.py:601
  54.6 0.0 collective-permute-done.47
  54.7 1.4 %collective-permute-start.48 = (f32[304,128]{1,0:T(8,128)S(1)}, f32[304,128]{1,0:T(8,128)S(1)}, u32[]{:S(2)}, u32[]{:S(2)}) collective-permute-start(f32[304,128]{1,0:T(8,128)S(1)} %pad_maximum_fusion.15), channel_id=1, source_target_pairs={{0,4},{1,3},{2,6},{3,1},{4,0},{5,7},{6,2},{7,5},{8,12},{9,11},{10,... | collective-permute-start | bytes 466952 | tf_op jit(solution)/shard_map/cond/branch_1_fun/ppermute | solution.py:601
  56.0 0.4 collective-permute-done.40
  56.4 2.8 %collective-permute-start.41 = (f32[304,128]{1,0:T(8,128)S(1)}, f32[304,128]{1,0:T(8,128)S(1)}, u32[]{:S(2)}, u32[]{:S(2)}) collective-permute-start(f32[304,128]{1,0:T(8,128)S(1)} %pad_maximum_fusion.14), channel_id=1, source_target_pairs={{0,4},{1,3},{2,6},{3,1},{4,0},{5,7},{6,2},{7,5},{8,12},{9,11},{10,... | collective-permute-start | bytes 466952 | tf_op jit(solution)/shard_map/cond/branch_1_fun/ppermute | solution.py:601
  59.3 0.4 collective-permute-done.48
  59.7 6.0 %collective-permute-start.49 = (f32[608,128]{1,0:T(8,128)S(1)}, f32[608,128]{1,0:T(8,128)S(1)}, u32[]{:S(2)}, u32[]{:S(2)}) collective-permute-start(f32[608,128]{1,0:T(8,128)S(1)} %pad_maximum_fusion.11.mine_ref), channel_id=1, source_target_pairs={{0,1},{1,0},{2,3},{3,2},{4,5},{5,4},{6,7},{7,6},{8,9},{9,8},{10,11... | collective-permute-start | bytes 933896 | tf_op jit(solution)/shard_map/cond/branch_1_fun/ppermute | solution.py:601
  65.7 0.0 collective-permute-done.41
  65.8 1.6 %collective-permute-start.42 = (f32[608,128]{1,0:T(8,128)S(1)}, f32[608,128]{1,0:T(8,128)S(1)}, u32[]{:S(2)}, u32[]{:S(2)}) collective-permute-start(f32[608,128]{1,0:T(8,128)S(1)} %pad_maximum_fusion.10.mine_ref), channel_id=1, source_target_pairs={{0,1},{1,0},{2,3},{3,2},{4,5},{5,4},{6,7},{7,6},{8,9},{9,8},{10,11... | collective-permute-start | bytes 933896 | tf_op jit(solution)/shard_map/cond/branch_1_fun/ppermute | solution.py:601
  67.4 2.7 %update.3 = (f32[1000,768]{1,0:T(8,128)}, f32[1000,256]{1,0:T(8,128)}, bf16[768,768]{1,0:T(8,128)(2,1)S(1)}) custom-call(f32[608,128]{1,0:T(8,128)S(1)} %pad_maximum_fusion.11.mine_ref, f32[608,128]{1,0:T(8,128)S(1)} %collective-permute-done.49.other_ref, f32[1000,256]{1,0:T(8,128)S(1)} %copy-done.4, s32[1,256]{1,0:T(1,128)S(1)} %copy-done.8, ...), custom_call_target="tpu_custom_call" | custom-call | flops 717225984 | bytes 3670016 | tf_op jit(solution)/shard_map/cond/branch_1_fun/update/pallas_call | solution.py:540
  70.1 2.7 %update_more.3 = (f32[1000,768]{1,0:T(8,128)}, f32[1000,256]{1,0:T(8,128)}) custom-call(f32[608,128]{1,0:T(8,128)S(1)} %pad_maximum_fusion.10.mine_ref, f32[608,128]{1,0:T(8,128)S(1)} %collective-permute-done.42.other_ref, f32[1000,256]{1,0:T(8,128)S(1)} %copy-done.4, f32[1000,768]{1,0:T(8,128)S(1)} %copy-done.2, ...), custom_call_target="tpu_custom_call", output_to_operand_aliasing={{0}: (5, {}), {1}: (6, {})} | custom-call | flops 651165696 | bytes 4521984 | tf_op jit(solution)/shard_map/cond/branch_1_fun/update_more/pallas_call | solution.py:577
  (29 shorter events, 0.4 us)
Async XLA Ops:
  4.8 5.4 %copy-start.8 = (s32[1,256]{1,0:T(1,128)S(1)}, s32[1,256]{1,0:T(1,128)}, u32[]{:S(2)}) copy-start(s32[1,256]{1,0:T(1,128)} %get-tuple-element.58.index_hbm.index_ref) | copy-start | bytes 3076 | tf_op jit(solution)/shard_map/cond
  4.8 5.8 %copy-start.10 = (s32[320]{0:T(512)S(1)}, s32[320]{0:T(512)}, u32[]{:S(2)}) copy-start(s32[320]{0:T(512)} %get-tuple-element.60) | copy-start | bytes 3844 | tf_op jit(solution)/shard_map/cond
  4.8 5.8 %copy-start = (bf16[768,3072]{1,0:T(8,128)(2,1)S(1)}, bf16[768,3072]{1,0:T(8,128)(2,1)}, u32[]{:S(2)}) copy-start(bf16[768,3072]{1,0:T(8,128)(2,1)} %get-tuple-element.59.centers_hbm.centers_ref) | copy-start | bytes 14155780 | tf_op jit(solution)/shard_map/cond
  4.8 8.6 %collective-permute-start.29 = (bf16[32,1536]{1,0:T(8,128)(2,1)S(1)}, bf16[32,1536]{1,0:T(8,128)(2,1)S(1)}, u32[]{:S(2)}, u32[]{:S(2)}) collective-permute-start(bf16[32,1536]{1,0:T(8,128)(2,1)S(1)} %pack_rows.3), channel_id=1, source_target_pairs={{0,8},{1,9},{2,10},{3,11},{4,12},{5,13},{6,14},{7,15},{8,0},{9,1},... | collective-permute-start | bytes 294920 | tf_op jit(solution)/shard_map/cond/branch_1_fun/ppermute | solution.py:601
  9.9 1.9 %copy-start.2 = (f32[1000,768]{1,0:T(8,128)S(1)}, f32[1000,768]{1,0:T(8,128)}, u32[]{:S(2)}) copy-start(f32[1000,768]{1,0:T(8,128)} %get-tuple-element.62.weights_ref) | copy-start | bytes 9216004 | tf_op jit(solution)/shard_map/cond
  9.9 1.9 %copy-start.6 = (f32[160,320]{1,0:T(8,128)S(1)}, f32[160,320]{1,0:T(8,128)}, u32[]{:S(2)}) copy-start(f32[160,320]{1,0:T(8,128)} %get-tuple-element.61.eigvec_ref) | copy-start | bytes 614404 | tf_op jit(solution)/shard_map/cond
  10.0 6.0 %collective-permute-start.28 = (bf16[32,1536]{1,0:T(8,128)(2,1)S(1)}, bf16[32,1536]{1,0:T(8,128)(2,1)S(1)}, u32[]{:S(2)}, u32[]{:S(2)}) collective-permute-start(bf16[32,1536]{1,0:T(8,128)(2,1)S(1)} %pack_rows.2), channel_id=1, source_target_pairs={{0,8},{1,9},{2,10},{3,11},{4,12},{5,13},{6,14},{7,15},{8,0},{9,1},... | collective-permute-start | bytes 294920 | tf_op jit(solution)/shard_map/cond/branch_1_fun/ppermute | solution.py:601
  13.4 6.3 %collective-permute-start.30 = (bf16[64,1536]{1,0:T(8,128)(2,1)S(1)}, bf16[64,1536]{1,0:T(8,128)(2,1)S(1)}, u32[]{:S(2)}, u32[]{:S(2)}) collective-permute-start(bf16[64,1536]{1,0:T(8,128)(2,1)S(1)} %pad_maximum_fusion.13.keep_ref), channel_id=1, source_target_pairs={{0,2},{1,5},{2,0},{3,7},{4,6},{5,1},{6,4},{7,3},{8,10},{9,13},{10,... | collective-permute-start | bytes 589832 | tf_op jit(solution)/shard_map/cond/branch_1_fun/ppermute | solution.py:601
  16.0 6.0 %collective-permute-start.33 = (bf16[64,1536]{1,0:T(8,128)(2,1)S(1)}, bf16[64,1536]{1,0:T(8,128)(2,1)S(1)}, u32[]{:S(2)}, u32[]{:S(2)}) collective-permute-start(bf16[64,1536]{1,0:T(8,128)(2,1)S(1)} %pad_maximum_fusion.12.keep_ref), channel_id=1, source_target_pairs={{0,2},{1,5},{2,0},{3,7},{4,6},{5,1},{6,4},{7,3},{8,10},{9,13},{10,... | collective-permute-start | bytes 589832 | tf_op jit(solution)/shard_map/cond/branch_1_fun/ppermute | solution.py:601
  20.1 6.7 %collective-permute-start.31 = (bf16[96,1536]{1,0:T(8,128)(2,1)S(1)}, bf16[96,1536]{1,0:T(8,128)(2,1)S(1)}, u32[]{:S(2)}, u32[]{:S(2)}) collective-permute-start(bf16[96,1536]{1,0:T(8,128)(2,1)S(1)} %squeeze_slots.2), channel_id=1, source_target_pairs={{0,4},{1,3},{2,6},{3,1},{4,0},{5,7},{6,2},{7,5},{8,12},{9,11},{10,... | collective-permute-start | bytes 884744 | tf_op jit(solution)/shard_map/cond/branch_1_fun/ppermute | solution.py:601
  22.4 7.6 %collective-permute-start.34 = (bf16[96,1536]{1,0:T(8,128)(2,1)S(1)}, bf16[96,1536]{1,0:T(8,128)(2,1)S(1)}, u32[]{:S(2)}, u32[]{:S(2)}) collective-permute-start(bf16[96,1536]{1,0:T(8,128)(2,1)S(1)} %squeeze_slots.3), channel_id=1, source_target_pairs={{0,4},{1,3},{2,6},{3,1},{4,0},{5,7},{6,2},{7,5},{8,12},{9,11},{10,... | collective-permute-start | bytes 884744 | tf_op jit(solution)/shard_map/cond/branch_1_fun/ppermute | solution.py:601
  26.9 5.2 %collective-permute-start.32 = (bf16[192,1536]{1,0:T(8,128)(2,1)S(1)}, bf16[192,1536]{1,0:T(8,128)(2,1)S(1)}, u32[]{:S(2)}, u32[]{:S(2)}) collective-permute-start(bf16[192,1536]{1,0:T(8,128)(2,1)S(1)} %pad_maximum_fusion.8.mine_ref), channel_id=1, source_target_pairs={{0,1},{1,0},{2,3},{3,2},{4,5},{5,4},{6,7},{7,6},{8,9},{9,8},{10,11... | collective-permute-start | bytes 1769480 | tf_op jit(solution)/shard_map/cond/branch_1_fun/ppermute | solution.py:601
  30.0 3.7 %collective-permute-start.35 = (bf16[192,1536]{1,0:T(8,128)(2,1)S(1)}, bf16[192,1536]{1,0:T(8,128)(2,1)S(1)}, u32[]{:S(2)}, u32[]{:S(2)}) collective-permute-start(bf16[192,1536]{1,0:T(8,128)(2,1)S(1)} %pad_maximum_fusion.9.next_ref), channel_id=1, source_target_pairs={{0,1},{1,0},{2,3},{3,2},{4,5},{5,4},{6,7},{7,6},{8,9},{9,8},{10,11... | collective-permute-start | bytes 1769480 | tf_op jit(solution)/shard_map/cond/branch_1_fun/ppermute | solution.py:601
  35.9 1.7 %collective-permute-start.43 = (f32[608,128]{1,0:T(8,128)S(1)}, f32[608,128]{1,0:T(8,128)S(1)}, u32[]{:S(2)}, u32[]{:S(2)}) collective-permute-start(f32[608,128]{1,0:T(8,128)S(1)} %get-tuple-element.81), channel_id=1, source_target_pairs={{0,1},{1,0},{2,3},{3,2},{4,5},{5,4},{6,7},{7,6},{8,9},{9,8},{10,11... | collective-permute-start | bytes 933896 | tf_op jit(solution)/shard_map/cond/branch_1_fun/ppermute | solution.py:601
  37.3 1.7 %collective-permute-start.36 = (f32[608,128]{1,0:T(8,128)S(1)}, f32[608,128]{1,0:T(8,128)S(1)}, u32[]{:S(2)}, u32[]{:S(2)}) collective-permute-start(f32[608,128]{1,0:T(8,128)S(1)} %get-tuple-element.78), channel_id=1, source_target_pairs={{0,1},{1,0},{2,3},{3,2},{4,5},{5,4},{6,7},{7,6},{8,9},{9,8},{10,11... | collective-permute-start | bytes 933896 | tf_op jit(solution)/shard_map/cond/branch_1_fun/ppermute | solution.py:601
  37.6 29.8 %copy-start.4 = (f32[1000,256]{1,0:T(8,128)S(1)}, f32[1000,256]{1,0:T(8,128)}, u32[]{:S(2)}) copy-start(f32[1000,256]{1,0:T(8,128)} %get-tuple-element.79.targets_ref) | copy-start | bytes 3072004 | tf_op jit(solution)/shard_map/cond
  37.7 29.7 %copy-start.12 = (f32[1,160]{1,0:T(1,128)S(1)}, f32[1,160]{1,0:T(1,128)}, u32[]{:S(2)}) copy-start(f32[1,160]{1,0:T(1,128)} %get-tuple-element.82.eigval_ref) | copy-start | bytes 1924 | tf_op jit(solution)/shard_map/cond
  37.7 4.4 %collective-permute-start.44 = (f32[304,128]{1,0:T(8,128)S(1)}, f32[304,128]{1,0:T(8,128)S(1)}, u32[]{:S(2)}, u32[]{:S(2)}) collective-permute-start(f32[304,128]{1,0:T(8,128)S(1)} %slice.96), channel_id=1, source_target_pairs={{0,4},{1,3},{2,6},{3,1},{4,0},{5,7},{6,2},{7,5},{8,12},{9,11},{10,... | collective-permute-start | bytes 466952 | tf_op jit(solution)/shard_map/cond/branch_1_fun/ppermute | solution.py:601
  39.0 4.7 %collective-permute-start.37 = (f32[304,128]{1,0:T(8,128)S(1)}, f32[304,128]{1,0:T(8,128)S(1)}, u32[]{:S(2)}, u32[]{:S(2)}) collective-permute-start(f32[304,128]{1,0:T(8,128)S(1)} %slice.92), channel_id=1, source_target_pairs={{0,4},{1,3},{2,6},{3,1},{4,0},{5,7},{6,2},{7,5},{8,12},{9,11},{10,... | collective-permute-start | bytes 466952 | tf_op jit(solution)/shard_map/cond/branch_1_fun/ppermute | solution.py:601
  42.2 3.3 %collective-permute-start.45 = (f32[152,128]{1,0:T(8,128)S(1)}, f32[152,128]{1,0:T(8,128)S(1)}, u32[]{:S(2)}, u32[]{:S(2)}) collective-permute-start(f32[152,128]{1,0:T(8,128)S(1)} %slice.98), channel_id=1, source_target_pairs={{0,2},{1,5},{2,0},{3,7},{4,6},{5,1},{6,4},{7,3},{8,10},{9,13},{10,... | collective-permute-start | bytes 233480 | tf_op jit(solution)/shard_map/cond/branch_1_fun/ppermute | solution.py:601
  43.8 4.0 %collective-permute-start.38 = (f32[152,128]{1,0:T(8,128)S(1)}, f32[152,128]{1,0:T(8,128)S(1)}, u32[]{:S(2)}, u32[]{:S(2)}) collective-permute-start(f32[152,128]{1,0:T(8,128)S(1)} %slice.94), channel_id=1, source_target_pairs={{0,2},{1,5},{2,0},{3,7},{4,6},{5,1},{6,4},{7,3},{8,10},{9,13},{10,... | collective-permute-start | bytes 233480 | tf_op jit(solution)/shard_map/cond/branch_1_fun/ppermute | solution.py:601
  45.5 4.2 %collective-permute-start.46 = (f32[152,128]{1,0:T(8,128)S(1)}, f32[152,128]{1,0:T(8,128)S(1)}, u32[]{:S(2)}, u32[]{:S(2)}) collective-permute-start(f32[152,128]{1,0:T(8,128)S(1)} %slice_add_fusion.10), channel_id=1, source_target_pairs={{0,8},{1,9},{2,10},{3,11},{4,12},{5,13},{6,14},{7,15},{8,0},{9,1},... | collective-permute-start | bytes 233480 | tf_op jit(solution)/shard_map/cond/branch_1_fun/ppermute | solution.py:601
  47.8 4.9 %collective-permute-start.39 = (f32[152,128]{1,0:T(8,128)S(1)}, f32[152,128]{1,0:T(8,128)S(1)}, u32[]{:S(2)}, u32[]{:S(2)}) collective-permute-start(f32[152,128]{1,0:T(8,128)S(1)} %slice_add_fusion.11), channel_id=1, source_target_pairs={{0,8},{1,9},{2,10},{3,11},{4,12},{5,13},{6,14},{7,15},{8,0},{9,1},... | collective-permute-start | bytes 233480 | tf_op jit(solution)/shard_map/cond/branch_1_fun/ppermute | solution.py:601
  49.7 4.9 %collective-permute-start.47 = (f32[152,128]{1,0:T(8,128)S(1)}, f32[152,128]{1,0:T(8,128)S(1)}, u32[]{:S(2)}, u32[]{:S(2)}) collective-permute-start(f32[152,128]{1,0:T(8,128)S(1)} %add.135), channel_id=1, source_target_pairs={{0,2},{1,5},{2,0},{3,7},{4,6},{5,1},{6,4},{7,3},{8,10},{9,13},{10,... | collective-permute-start | bytes 233480 | tf_op jit(solution)/shard_map/cond/branch_1_fun/ppermute | solution.py:601
  52.8 3.7 %collective-permute-start.40 = (f32[152,128]{1,0:T(8,128)S(1)}, f32[152,128]{1,0:T(8,128)S(1)}, u32[]{:S(2)}, u32[]{:S(2)}) collective-permute-start(f32[152,128]{1,0:T(8,128)S(1)} %add.131), channel_id=1, source_target_pairs={{0,2},{1,5},{2,0},{3,7},{4,6},{5,1},{6,4},{7,3},{8,10},{9,13},{10,... | collective-permute-start | bytes 233480 | tf_op jit(solution)/shard_map/cond/branch_1_fun/ppermute | solution.py:601
  54.7 5.1 %collective-permute-start.48 = (f32[304,128]{1,0:T(8,128)S(1)}, f32[304,128]{1,0:T(8,128)S(1)}, u32[]{:S(2)}, u32[]{:S(2)}) collective-permute-start(f32[304,128]{1,0:T(8,128)S(1)} %pad_maximum_fusion.15), channel_id=1, source_target_pairs={{0,4},{1,3},{2,6},{3,1},{4,0},{5,7},{6,2},{7,5},{8,12},{9,11},{10,... | collective-permute-start | bytes 466952 | tf_op jit(solution)/shard_map/cond/branch_1_fun/ppermute | solution.py:601
  56.4 9.3 %collective-permute-start.41 = (f32[304,128]{1,0:T(8,128)S(1)}, f32[304,128]{1,0:T(8,128)S(1)}, u32[]{:S(2)}, u32[]{:S(2)}) collective-permute-start(f32[304,128]{1,0:T(8,128)S(1)} %pad_maximum_fusion.14), channel_id=1, source_target_pairs={{0,4},{1,3},{2,6},{3,1},{4,0},{5,7},{6,2},{7,5},{8,12},{9,11},{10,... | collective-permute-start | bytes 466952 | tf_op jit(solution)/shard_map/cond/branch_1_fun/ppermute | solution.py:601
  59.7 7.7 %collective-permute-start.49 = (f32[608,128]{1,0:T(8,128)S(1)}, f32[608,128]{1,0:T(8,128)S(1)}, u32[]{:S(2)}, u32[]{:S(2)}) collective-permute-start(f32[608,128]{1,0:T(8,128)S(1)} %pad_maximum_fusion.11.mine_ref), channel_id=1, source_target_pairs={{0,1},{1,0},{2,3},{3,2},{4,5},{5,4},{6,7},{7,6},{8,9},{9,8},{10,11... | collective-permute-start | bytes 933896 | tf_op jit(solution)/shard_map/cond/branch_1_fun/ppermute | solution.py:601
  65.8 4.3 %collective-permute-start.42 = (f32[608,128]{1,0:T(8,128)S(1)}, f32[608,128]{1,0:T(8,128)S(1)}, u32[]{:S(2)}, u32[]{:S(2)}) collective-permute-start(f32[608,128]{1,0:T(8,128)S(1)} %pad_maximum_fusion.10.mine_ref), channel_id=1, source_target_pairs={{0,1},{1,0},{2,3},{3,2},{4,5},{5,4},{6,7},{7,6},{8,9},{9,8},{10,11... | collective-permute-start | bytes 933896 | tf_op jit(solution)/shard_map/cond/branch_1_fun/ppermute | solution.py:601

commit v18 on v17

--- a/solution.py
+++ b/solution.py
@@ -549,7 +549,7 @@
         scratch_shapes=[
             pltpu.VMEM((padded, rows), F32),
             pltpu.VMEM((here, count), F32),
-            pltpu.SemaphoreType.DMA((8,)),
+            pltpu.SemaphoreType.DMA((3,)),
         ],
         compiler_params=params(),
         cost_estimate=pl.CostEstimate(
@@ -586,7 +586,7 @@
         scratch_shapes=[
             pltpu.VMEM((padded, rows), F32),
             pltpu.VMEM((here, count), F32),
-            pltpu.SemaphoreType.DMA((9,)),
+            pltpu.SemaphoreType.DMA((3,)),
         ],
         compiler_params=params(),
         cost_estimate=pl.CostEstimate(

time: 73.2 us -> 72.2 us (0.986)
  Pallas kernels: 19 us -> 18.1 us
    pallas_call x1, Pallas kernels: 2.71 us -> 1.93 us  [update_more(): pl.pallas_call(functools.partial(update_more_body, begin), in_specs=[vmem...]
where the time goes in v18:
time: 72.2 us; the launch traced here: 72 us
  starting transfers between devices  37.3 us (52%)
  Pallas kernels  18.1 us (25%)
  waiting for transfers between devices  14.2 us (20%)
  between operations  1.45 us (2%)
    ppermute x22, starting transfers between devices, swap(): lax.ppermute(x, AXES, [(i, i ^ flip[i & 1]) for i in range(2 * chips)])  37.3 us
    ppermute x22, waiting for transfers between devices, swap(): lax.ppermute(x, AXES, [(i, i ^ flip[i & 1]) for i in range(2 * chips)])  14.2 us
    pallas_call x2, Pallas kernels, pack_rows(): pl.pallas_call(functools.partial(pack_body, part * depth), in_specs=[hbm,...  3.84 us
    pallas_call x1, Pallas kernels, update(): pl.pallas_call(update_body, in_specs=[vmem] * 7, out_specs=[hbm, hbm, vme...  2.48 us
    pallas_call x1, Pallas kernels, predict(): pl.pallas_call(predict_body, in_specs=[vmem] * 6, out_specs=[vmem] * 3, o...  2.25 us
    pallas_call x1, Pallas kernels, update_more(): pl.pallas_call(functools.partial(update_more_body, begin), in_specs=[vmem...  1.93 us
    pallas_call x1, Pallas kernels, spread_weights(): pl.pallas_call(functools.partial(spread_body, first, classes), out_shape=...  1.6 us
    pallas_call x1, Pallas kernels, distances(): pl.pallas_call(distance_body, in_specs=[vmem] * 6, out_specs=[vmem, vmem]...  1.46 us
  transfers between devices with their start and end apart: 22, of which 14 were waited for; matrix products, arithmetic and copies ran while one was open for 1% of the time, Pallas kernels for 15%

profile of v18, /device:TPU:1, one launch (start us, length us, event | category | flops | bytes accessed | tf_op | source)
XLA Modules:
  0.0 72.0 jit_solution(16938936882693913733)
XLA Ops:
  0.6 1.4 %rows_fit.1 = s32[1]{0:T(128)} custom-call(s32[1,256]{1,0:T(1,128)} %bitcast.17), custom_call_target="tpu_custom_call" | custom-call | tf_op jit(solution)/shard_map/rows_fit/pallas_call | solution.py:157
  2.6 69.2 %conditional.1 = ((f32[1000,768]{1,0:T(8,128)}, f32[1000,256]{1,0:T(8,128)})) conditional(s32[]{:T(128)} %bitcast.2, (s32[1,256]{1,0:T(1,128)}, bf16[768,3072]{1,0:T(8,128)(2,1)}, s32[320]{0:T(512)}, f32[160,320]{1,0:T(8,128)}, f32[1000,768]{1,0:T(8,128)}, /*index=5*/f32[1000,256]{1,0:T(8,128)}, f32[1,160]{1,0:T(1,128)}) %tuple.31, ...), branch_computations={%region_0.1_spmd, %region_1.2_spmd} | conditional | flops 5916241920 | bytes 106008064 | solution.py:686
  2.8 1.9 %pack_rows.3 = bf16[32,1536]{1,0:T(8,128)(2,1)S(1)} custom-call(s32[1,256]{1,0:T(1,128)} %get-tuple-element.58.index_hbm.index_ref, bf16[768,3072]{1,0:T(8,128)(2,1)} %get-tuple-element.59.centers_hbm.centers_ref), custom_call_target="tpu_custom_call" | custom-call | flops 75497472 | bytes 2457600 | tf_op jit(solution)/shard_map/cond/branch_1_fun/pack_rows/pallas_call | solution.py:199
  4.8 0.0 copy-start.8
  4.8 0.0 copy-start.10
  4.8 0.0 copy-start
  4.8 3.2 %collective-permute-start.29 = (bf16[32,1536]{1,0:T(8,128)(2,1)S(1)}, bf16[32,1536]{1,0:T(8,128)(2,1)S(1)}, u32[]{:S(2)}, u32[]{:S(2)}) collective-permute-start(bf16[32,1536]{1,0:T(8,128)(2,1)S(1)} %pack_rows.3), channel_id=1, source_target_pairs={{0,8},{1,9},{2,10},{3,11},{4,12},{5,13},{6,14},{7,15},{8,0},{9,1},... | collective-permute-start | bytes 294920 | tf_op jit(solution)/shard_map/cond/branch_1_fun/ppermute | solution.py:601
  8.0 1.9 %pack_rows.2 = bf16[32,1536]{1,0:T(8,128)(2,1)S(1)} custom-call(s32[1,256]{1,0:T(1,128)} %get-tuple-element.58.index_hbm.index_ref, bf16[768,3072]{1,0:T(8,128)(2,1)} %get-tuple-element.59.centers_hbm.centers_ref), custom_call_target="tpu_custom_call" | custom-call | flops 75497472 | bytes 2457600 | tf_op jit(solution)/shard_map/cond/branch_1_fun/pack_rows/pallas_call | solution.py:199
  9.9 0.0 copy-start.2
  9.9 0.0 copy-start.6
  10.0 0.2 collective-permute-start.28
  10.2 0.4 select_packed.1
  10.6 1.2 %center_norms.3.norm_ref = f32[768,128]{1,0:T(8,128)S(1)} custom-call(bf16[768,3072]{1,0:T(8,128)(2,1)S(1)} %copy-done), custom_call_target="tpu_custom_call" | custom-call | flops 4718592 | bytes 4718592 | tf_op jit(solution)/shard_map/cond/branch_1_fun/center_norms/pallas_call | solution.py:341
  11.8 0.0 copy-done.2
  11.8 1.6 %spread_weights.3 = (bf16[608,2304]{1,0:T(8,128)(2,1)S(1)}, bf16[608,2304]{1,0:T(8,128)(2,1)S(1)}, f32[160,768]{1,0:T(8,128)S(1)}) custom-call(s32[1,320]{1,0:T(1,128)S(1)} %reshape.99.index_ref, f32[160,320]{1,0:T(8,128)S(1)} %copy-done.6, f32[1000,768]{1,0:T(8,128)S(1)} %copy-done.2), custom_call_target="tpu_custom_call" | custom-call | flops 235929600 | bytes 7471104 | tf_op jit(solution)/shard_map/cond/branch_1_fun/spread_weights/pallas_call | solution.py:316
  13.4 0.0 collective-permute-done.29
  13.4 2.6 %collective-permute-start.30 = (bf16[64,1536]{1,0:T(8,128)(2,1)S(1)}, bf16[64,1536]{1,0:T(8,128)(2,1)S(1)}, u32[]{:S(2)}, u32[]{:S(2)}) collective-permute-start(bf16[64,1536]{1,0:T(8,128)(2,1)S(1)} %pad_maximum_fusion.13.keep_ref), channel_id=1, source_target_pairs={{0,2},{1,5},{2,0},{3,7},{4,6},{5,1},{6,4},{7,3},{8,10},{9,13},{10,... | collective-permute-start | bytes 589832 | tf_op jit(solution)/shard_map/cond/branch_1_fun/ppermute | solution.py:601
  16.0 0.0 collective-permute-done.28
  16.0 2.1 %collective-permute-start.33 = (bf16[64,1536]{1,0:T(8,128)(2,1)S(1)}, bf16[64,1536]{1,0:T(8,128)(2,1)S(1)}, u32[]{:S(2)}, u32[]{:S(2)}) collective-permute-start(bf16[64,1536]{1,0:T(8,128)(2,1)S(1)} %pad_maximum_fusion.12.keep_ref), channel_id=1, source_target_pairs={{0,2},{1,5},{2,0},{3,7},{4,6},{5,1},{6,4},{7,3},{8,10},{9,13},{10,... | collective-permute-start | bytes 589832 | tf_op jit(solution)/shard_map/cond/branch_1_fun/ppermute | solution.py:601
  18.1 1.6 %collective-permute-done.30.got_ref = bf16[64,1536]{1,0:T(8,128)(2,1)S(1)} collective-permute-done((bf16[64,1536]{1,0:T(8,128)(2,1)S(1)}, bf16[64,1536]{1,0:T(8,128)(2,1)S(1)}, u32[]{:S(2)}, u32[]{:S(2)}) %collective-permute-start.30) | collective-permute-done | bytes 196640 | tf_op jit(solution)/shard_map/cond/branch_1_fun/ppermute | solution.py:601
  19.7 0.3 squeeze_slots.2
  20.1 1.5 %collective-permute-start.31 = (bf16[96,1536]{1,0:T(8,128)(2,1)S(1)}, bf16[96,1536]{1,0:T(8,128)(2,1)S(1)}, u32[]{:S(2)}, u32[]{:S(2)}) collective-permute-start(bf16[96,1536]{1,0:T(8,128)(2,1)S(1)} %squeeze_slots.2), channel_id=1, source_target_pairs={{0,4},{1,3},{2,6},{3,1},{4,0},{5,7},{6,2},{7,5},{8,12},{9,11},{10,... | collective-permute-start | bytes 884744 | tf_op jit(solution)/shard_map/cond/branch_1_fun/ppermute | solution.py:601
  21.6 0.5 collective-permute-done.33.got_ref
  22.1 0.3 squeeze_slots.3
  22.4 1.3 %collective-permute-start.34 = (bf16[96,1536]{1,0:T(8,128)(2,1)S(1)}, bf16[96,1536]{1,0:T(8,128)(2,1)S(1)}, u32[]{:S(2)}, u32[]{:S(2)}) collective-permute-start(bf16[96,1536]{1,0:T(8,128)(2,1)S(1)} %squeeze_slots.3), channel_id=1, source_target_pairs={{0,4},{1,3},{2,6},{3,1},{4,0},{5,7},{6,2},{7,5},{8,12},{9,11},{10,... | collective-permute-start | bytes 884744 | tf_op jit(solution)/shard_map/cond/branch_1_fun/ppermute | solution.py:601
  23.7 3.1 %collective-permute-done.31 = bf16[96,1536]{1,0:T(8,128)(2,1)S(1)} collective-permute-done((bf16[96,1536]{1,0:T(8,128)(2,1)S(1)}, bf16[96,1536]{1,0:T(8,128)(2,1)S(1)}, u32[]{:S(2)}, u32[]{:S(2)}) %collective-permute-start.31) | collective-permute-done | bytes 294944 | tf_op jit(solution)/shard_map/cond/branch_1_fun/ppermute | solution.py:601
  26.9 0.9 %collective-permute-start.32 = (bf16[192,1536]{1,0:T(8,128)(2,1)S(1)}, bf16[192,1536]{1,0:T(8,128)(2,1)S(1)}, u32[]{:S(2)}, u32[]{:S(2)}) collective-permute-start(bf16[192,1536]{1,0:T(8,128)(2,1)S(1)} %pad_maximum_fusion.8.mine_ref), channel_id=1, source_target_pairs={{0,1},{1,0},{2,3},{3,2},{4,5},{5,4},{6,7},{7,6},{8,9},{9,8},{10,11... | collective-permute-start | bytes 1769480 | tf_op jit(solution)/shard_map/cond/branch_1_fun/ppermute | solution.py:601
  27.8 2.2 %collective-permute-done.34 = bf16[96,1536]{1,0:T(8,128)(2,1)S(1)} collective-permute-done((bf16[96,1536]{1,0:T(8,128)(2,1)S(1)}, bf16[96,1536]{1,0:T(8,128)(2,1)S(1)}, u32[]{:S(2)}, u32[]{:S(2)}) %collective-permute-start.34) | collective-permute-done | bytes 294944 | tf_op jit(solution)/shard_map/cond/branch_1_fun/ppermute | solution.py:601
  30.0 2.0 %collective-permute-start.35 = (bf16[192,1536]{1,0:T(8,128)(2,1)S(1)}, bf16[192,1536]{1,0:T(8,128)(2,1)S(1)}, u32[]{:S(2)}, u32[]{:S(2)}) collective-permute-start(bf16[192,1536]{1,0:T(8,128)(2,1)S(1)} %pad_maximum_fusion.9.next_ref), channel_id=1, source_target_pairs={{0,1},{1,0},{2,3},{3,2},{4,5},{5,4},{6,7},{7,6},{8,9},{9,8},{10,11... | collective-permute-start | bytes 1769480 | tf_op jit(solution)/shard_map/cond/branch_1_fun/ppermute | solution.py:601
  32.0 0.0 collective-permute-done.32.other_ref
  32.0 1.5 %distances.3 = (f32[768,256]{1,0:T(8,128)S(1)}, bf16[256,1536]{1,0:T(8,128)(2,1)S(1)}) custom-call(bf16[192,1536]{1,0:T(8,128)(2,1)S(1)} %pad_maximum_fusion.8.mine_ref, bf16[192,1536]{1,0:T(8,128)(2,1)S(1)} %collective-permute-done.32.other_ref, bf16[192,1536]{1,0:T(8,128)(2,1)S(1)} %pad_maximum_fusion.9.next_ref, ...), custom_call_target="tpu_custom_call" | custom-call | flops 603979776 | bytes 3145728 | tf_op jit(solution)/shard_map/cond/branch_1_fun/distances/pallas_call | solution.py:416
  33.5 0.2 collective-permute-done.35.other_ref
  33.7 2.2 %predict.3 = (f32[608,128]{1,0:T(8,128)S(1)}, f32[608,128]{1,0:T(8,128)S(1)}, bf16[2304,256]{1,0:T(8,128)(2,1)S(1)}) custom-call(bf16[256,1536]{1,0:T(8,128)(2,1)S(1)} %get-tuple-element.73.found_ref, bf16[192,1536]{1,0:T(8,128)(2,1)S(1)} %collective-permute-done.35.other_ref, bf16[256,512]{1,0:T(8,128)(2,1)S(1)} %get-tuple-element.71.select_ref, ...), custom_call_target="tpu_custom_call" | custom-call | flops 1321205760 | bytes 5636096 | tf_op jit(solution)/shard_map/cond/branch_1_fun/predict/pallas_call | solution.py:438
  35.9 0.4 collective-permute-start.43
  36.4 0.9 %predict_more.3 = (f32[608,128]{1,0:T(8,128)S(1)}, f32[608,128]{1,0:T(8,128)S(1)}) custom-call(bf16[608,2304]{1,0:T(8,128)(2,1)S(1)} %get-tuple-element.67.left, bf16[2304,256]{1,0:T(8,128)(2,1)S(1)} %get-tuple-element.76.right), custom_call_target="tpu_custom_call" | custom-call | flops 717225984 | bytes 3112960 | tf_op jit(solution)/shard_map/cond/branch_1_fun/predict_more/pallas_call | solution.py:458
  37.3 0.2 collective-permute-start.36
  37.5 0.1 collective-permute-done.43
  37.6 0.0 copy-start.4
  37.7 0.0 copy-start.12
  37.7 1.1 %collective-permute-start.44 = (f32[304,128]{1,0:T(8,128)S(1)}, f32[304,128]{1,0:T(8,128)S(1)}, u32[]{:S(2)}, u32[]{:S(2)}) collective-permute-start(f32[304,128]{1,0:T(8,128)S(1)} %slice.96), channel_id=1, source_target_pairs={{0,4},{1,3},{2,6},{3,1},{4,0},{5,7},{6,2},{7,5},{8,12},{9,11},{10,... | collective-permute-start | bytes 466952 | tf_op jit(solution)/shard_map/cond/branch_1_fun/ppermute | solution.py:601
  38.8 0.2 collective-permute-done.36
  39.0 1.1 %collective-permute-start.37 = (f32[304,128]{1,0:T(8,128)S(1)}, f32[304,128]{1,0:T(8,128)S(1)}, u32[]{:S(2)}, u32[]{:S(2)}) collective-permute-start(f32[304,128]{1,0:T(8,128)S(1)} %slice.92), channel_id=1, source_target_pairs={{0,4},{1,3},{2,6},{3,1},{4,0},{5,7},{6,2},{7,5},{8,12},{9,11},{10,... | collective-permute-start | bytes 466952 | tf_op jit(solution)/shard_map/cond/branch_1_fun/ppermute | solution.py:601
  40.1 2.0 %collective-permute-done.44 = f32[304,128]{1,0:T(8,128)S(1)} collective-permute-done((f32[304,128]{1,0:T(8,128)S(1)}, f32[304,128]{1,0:T(8,128)S(1)}, u32[]{:S(2)}, u32[]{:S(2)}) %collective-permute-start.44) | collective-permute-done | bytes 155680 | tf_op jit(solution)/shard_map/cond/branch_1_fun/ppermute | solution.py:601
  42.2 0.7 collective-permute-start.45
  42.8 0.9 %collective-permute-done.37 = f32[304,128]{1,0:T(8,128)S(1)} collective-permute-done((f32[304,128]{1,0:T(8,128)S(1)}, f32[304,128]{1,0:T(8,128)S(1)}, u32[]{:S(2)}, u32[]{:S(2)}) %collective-permute-start.37) | collective-permute-done | bytes 155680 | tf_op jit(solution)/shard_map/cond/branch_1_fun/ppermute | solution.py:601
  43.8 0.7 collective-permute-start.38
  44.5 1.0 %collective-permute-done.45 = f32[152,128]{1,0:T(8,128)S(1)} collective-permute-done((f32[152,128]{1,0:T(8,128)S(1)}, f32[152,128]{1,0:T(8,128)S(1)}, u32[]{:S(2)}, u32[]{:S(2)}) %collective-permute-start.45) | collective-permute-done | bytes 77856 | tf_op jit(solution)/shard_map/cond/branch_1_fun/ppermute | solution.py:601
  45.5 2.3 %collective-permute-start.46 = (f32[152,128]{1,0:T(8,128)S(1)}, f32[152,128]{1,0:T(8,128)S(1)}, u32[]{:S(2)}, u32[]{:S(2)}) collective-permute-start(f32[152,128]{1,0:T(8,128)S(1)} %slice_add_fusion.10), channel_id=1, source_target_pairs={{0,8},{1,9},{2,10},{3,11},{4,12},{5,13},{6,14},{7,15},{8,0},{9,1},... | collective-permute-start | bytes 233480 | tf_op jit(solution)/shard_map/cond/branch_1_fun/ppermute | solution.py:601
  47.8 0.0 collective-permute-done.38
  47.8 1.7 %collective-permute-start.39 = (f32[152,128]{1,0:T(8,128)S(1)}, f32[152,128]{1,0:T(8,128)S(1)}, u32[]{:S(2)}, u32[]{:S(2)}) collective-permute-start(f32[152,128]{1,0:T(8,128)S(1)} %slice_add_fusion.11), channel_id=1, source_target_pairs={{0,8},{1,9},{2,10},{3,11},{4,12},{5,13},{6,14},{7,15},{8,0},{9,1},... | collective-permute-start | bytes 233480 | tf_op jit(solution)/shard_map/cond/branch_1_fun/ppermute | solution.py:601
  49.5 0.2 collective-permute-done.46
  49.7 1.6 %collective-permute-start.47 = (f32[152,128]{1,0:T(8,128)S(1)}, f32[152,128]{1,0:T(8,128)S(1)}, u32[]{:S(2)}, u32[]{:S(2)}) collective-permute-start(f32[152,128]{1,0:T(8,128)S(1)} %add.135), channel_id=1, source_target_pairs={{0,2},{1,5},{2,0},{3,7},{4,6},{5,1},{6,4},{7,3},{8,10},{9,13},{10,... | collective-permute-start | bytes 233480 | tf_op jit(solution)/shard_map/cond/branch_1_fun/ppermute | solution.py:601
  51.3 1.4 %collective-permute-done.39 = f32[152,128]{1,0:T(8,128)S(1)} collective-permute-done((f32[152,128]{1,0:T(8,128)S(1)}, f32[152,128]{1,0:T(8,128)S(1)}, u32[]{:S(2)}, u32[]{:S(2)}) %collective-permute-start.39) | collective-permute-done | bytes 77856 | tf_op jit(solution)/shard_map/cond/branch_1_fun/ppermute | solution.py:601
  52.8 1.9 %collective-permute-start.40 = (f32[152,128]{1,0:T(8,128)S(1)}, f32[152,128]{1,0:T(8,128)S(1)}, u32[]{:S(2)}, u32[]{:S(2)}) collective-permute-start(f32[152,128]{1,0:T(8,128)S(1)} %add.131), channel_id=1, source_target_pairs={{0,2},{1,5},{2,0},{3,7},{4,6},{5,1},{6,4},{7,3},{8,10},{9,13},{10,... | collective-permute-start | bytes 233480 | tf_op jit(solution)/shard_map/cond/branch_1_fun/ppermute | solution.py:601
  54.6 0.0 collective-permute-done.47
  54.7 1.4 %collective-permute-start.48 = (f32[304,128]{1,0:T(8,128)S(1)}, f32[304,128]{1,0:T(8,128)S(1)}, u32[]{:S(2)}, u32[]{:S(2)}) collective-permute-start(f32[304,128]{1,0:T(8,128)S(1)} %pad_maximum_fusion.15), channel_id=1, source_target_pairs={{0,4},{1,3},{2,6},{3,1},{4,0},{5,7},{6,2},{7,5},{8,12},{9,11},{10,... | collective-permute-start | bytes 466952 | tf_op jit(solution)/shard_map/cond/branch_1_fun/ppermute | solution.py:601
  56.0 0.4 collective-permute-done.40
  56.4 2.8 %collective-permute-start.41 = (f32[304,128]{1,0:T(8,128)S(1)}, f32[304,128]{1,0:T(8,128)S(1)}, u32[]{:S(2)}, u32[]{:S(2)}) collective-permute-start(f32[304,128]{1,0:T(8,128)S(1)} %pad_maximum_fusion.14), channel_id=1, source_target_pairs={{0,4},{1,3},{2,6},{3,1},{4,0},{5,7},{6,2},{7,5},{8,12},{9,11},{10,... | collective-permute-start | bytes 466952 | tf_op jit(solution)/shard_map/cond/branch_1_fun/ppermute | solution.py:601
  59.3 0.4 collective-permute-done.48
  59.7 6.0 %collective-permute-start.49 = (f32[608,128]{1,0:T(8,128)S(1)}, f32[608,128]{1,0:T(8,128)S(1)}, u32[]{:S(2)}, u32[]{:S(2)}) collective-permute-start(f32[608,128]{1,0:T(8,128)S(1)} %pad_maximum_fusion.11.mine_ref), channel_id=1, source_target_pairs={{0,1},{1,0},{2,3},{3,2},{4,5},{5,4},{6,7},{7,6},{8,9},{9,8},{10,11... | collective-permute-start | bytes 933896 | tf_op jit(solution)/shard_map/cond/branch_1_fun/ppermute | solution.py:601
  65.8 1.6 %collective-permute-start.42 = (f32[608,128]{1,0:T(8,128)S(1)}, f32[608,128]{1,0:T(8,128)S(1)}, u32[]{:S(2)}, u32[]{:S(2)}) collective-permute-start(f32[608,128]{1,0:T(8,128)S(1)} %pad_maximum_fusion.10.mine_ref), channel_id=1, source_target_pairs={{0,1},{1,0},{2,3},{3,2},{4,5},{5,4},{6,7},{7,6},{8,9},{9,8},{10,11... | collective-permute-start | bytes 933896 | tf_op jit(solution)/shard_map/cond/branch_1_fun/ppermute | solution.py:601
  67.4 0.0 collective-permute-done.49.other_ref
  67.4 2.5 %update.3 = (f32[1000,768]{1,0:T(8,128)}, f32[1000,256]{1,0:T(8,128)}, bf16[768,768]{1,0:T(8,128)(2,1)S(1)}) custom-call(f32[608,128]{1,0:T(8,128)S(1)} %pad_maximum_fusion.11.mine_ref, f32[608,128]{1,0:T(8,128)S(1)} %collective-permute-done.49.other_ref, f32[1000,256]{1,0:T(8,128)S(1)} %copy-done.4, s32[1,256]{1,0:T(1,128)S(1)} %copy-done.8, ...), custom_call_target="tpu_custom_call" | custom-call | flops 717225984 | bytes 3670016 | tf_op jit(solution)/shard_map/cond/branch_1_fun/update/pallas_call | solution.py:540
  69.9 1.9 %update_more.3 = (f32[1000,768]{1,0:T(8,128)}, f32[1000,256]{1,0:T(8,128)}) custom-call(f32[608,128]{1,0:T(8,128)S(1)} %pad_maximum_fusion.10.mine_ref, f32[608,128]{1,0:T(8,128)S(1)} %collective-permute-done.42.other_ref, f32[1000,256]{1,0:T(8,128)S(1)} %copy-done.4, f32[1000,768]{1,0:T(8,128)S(1)} %copy-done.2, ...), custom_call_target="tpu_custom_call", output_to_operand_aliasing={{0}: (5, {}), {1}: (6, {})} | custom-call | flops 651165696 | bytes 4521984 | tf_op jit(solution)/shard_map/cond/branch_1_fun/update_more/pallas_call | solution.py:577
  (29 shorter events, 0.4 us)
Async XLA Ops:
  4.8 5.4 %copy-start.8 = (s32[1,256]{1,0:T(1,128)S(1)}, s32[1,256]{1,0:T(1,128)}, u32[]{:S(2)}) copy-start(s32[1,256]{1,0:T(1,128)} %get-tuple-element.58.index_hbm.index_ref) | copy-start | bytes 3076 | tf_op jit(solution)/shard_map/cond
  4.8 5.8 %copy-start.10 = (s32[320]{0:T(512)S(1)}, s32[320]{0:T(512)}, u32[]{:S(2)}) copy-start(s32[320]{0:T(512)} %get-tuple-element.60) | copy-start | bytes 3844 | tf_op jit(solution)/shard_map/cond
  4.8 5.8 %copy-start = (bf16[768,3072]{1,0:T(8,128)(2,1)S(1)}, bf16[768,3072]{1,0:T(8,128)(2,1)}, u32[]{:S(2)}) copy-start(bf16[768,3072]{1,0:T(8,128)(2,1)} %get-tuple-element.59.centers_hbm.centers_ref) | copy-start | bytes 14155780 | tf_op jit(solution)/shard_map/cond
  4.8 8.6 %collective-permute-start.29 = (bf16[32,1536]{1,0:T(8,128)(2,1)S(1)}, bf16[32,1536]{1,0:T(8,128)(2,1)S(1)}, u32[]{:S(2)}, u32[]{:S(2)}) collective-permute-start(bf16[32,1536]{1,0:T(8,128)(2,1)S(1)} %pack_rows.3), channel_id=1, source_target_pairs={{0,8},{1,9},{2,10},{3,11},{4,12},{5,13},{6,14},{7,15},{8,0},{9,1},... | collective-permute-start | bytes 294920 | tf_op jit(solution)/shard_map/cond/branch_1_fun/ppermute | solution.py:601
  9.9 1.9 %copy-start.2 = (f32[1000,768]{1,0:T(8,128)S(1)}, f32[1000,768]{1,0:T(8,128)}, u32[]{:S(2)}) copy-start(f32[1000,768]{1,0:T(8,128)} %get-tuple-element.62.weights_ref) | copy-start | bytes 9216004 | tf_op jit(solution)/shard_map/cond
  9.9 1.9 %copy-start.6 = (f32[160,320]{1,0:T(8,128)S(1)}, f32[160,320]{1,0:T(8,128)}, u32[]{:S(2)}) copy-start(f32[160,320]{1,0:T(8,128)} %get-tuple-element.61.eigvec_ref) | copy-start | bytes 614404 | tf_op jit(solution)/shard_map/cond
  10.0 6.0 %collective-permute-start.28 = (bf16[32,1536]{1,0:T(8,128)(2,1)S(1)}, bf16[32,1536]{1,0:T(8,128)(2,1)S(1)}, u32[]{:S(2)}, u32[]{:S(2)}) collective-permute-start(bf16[32,1536]{1,0:T(8,128)(2,1)S(1)} %pack_rows.2), channel_id=1, source_target_pairs={{0,8},{1,9},{2,10},{3,11},{4,12},{5,13},{6,14},{7,15},{8,0},{9,1},... | collective-permute-start | bytes 294920 | tf_op jit(solution)/shard_map/cond/branch_1_fun/ppermute | solution.py:601
  13.4 6.3 %collective-permute-start.30 = (bf16[64,1536]{1,0:T(8,128)(2,1)S(1)}, bf16[64,1536]{1,0:T(8,128)(2,1)S(1)}, u32[]{:S(2)}, u32[]{:S(2)}) collective-permute-start(bf16[64,1536]{1,0:T(8,128)(2,1)S(1)} %pad_maximum_fusion.13.keep_ref), channel_id=1, source_target_pairs={{0,2},{1,5},{2,0},{3,7},{4,6},{5,1},{6,4},{7,3},{8,10},{9,13},{10,... | collective-permute-start | bytes 589832 | tf_op jit(solution)/shard_map/cond/branch_1_fun/ppermute | solution.py:601
  16.0 6.0 %collective-permute-start.33 = (bf16[64,1536]{1,0:T(8,128)(2,1)S(1)}, bf16[64,1536]{1,0:T(8,128)(2,1)S(1)}, u32[]{:S(2)}, u32[]{:S(2)}) collective-permute-start(bf16[64,1536]{1,0:T(8,128)(2,1)S(1)} %pad_maximum_fusion.12.keep_ref), channel_id=1, source_target_pairs={{0,2},{1,5},{2,0},{3,7},{4,6},{5,1},{6,4},{7,3},{8,10},{9,13},{10,... | collective-permute-start | bytes 589832 | tf_op jit(solution)/shard_map/cond/branch_1_fun/ppermute | solution.py:601
  20.1 6.7 %collective-permute-start.31 = (bf16[96,1536]{1,0:T(8,128)(2,1)S(1)}, bf16[96,1536]{1,0:T(8,128)(2,1)S(1)}, u32[]{:S(2)}, u32[]{:S(2)}) collective-permute-start(bf16[96,1536]{1,0:T(8,128)(2,1)S(1)} %squeeze_slots.2), channel_id=1, source_target_pairs={{0,4},{1,3},{2,6},{3,1},{4,0},{5,7},{6,2},{7,5},{8,12},{9,11},{10,... | collective-permute-start | bytes 884744 | tf_op jit(solution)/shard_map/cond/branch_1_fun/ppermute | solution.py:601
  22.4 7.6 %collective-permute-start.34 = (bf16[96,1536]{1,0:T(8,128)(2,1)S(1)}, bf16[96,1536]{1,0:T(8,128)(2,1)S(1)}, u32[]{:S(2)}, u32[]{:S(2)}) collective-permute-start(bf16[96,1536]{1,0:T(8,128)(2,1)S(1)} %squeeze_slots.3), channel_id=1, source_target_pairs={{0,4},{1,3},{2,6},{3,1},{4,0},{5,7},{6,2},{7,5},{8,12},{9,11},{10,... | collective-permute-start | bytes 884744 | tf_op jit(solution)/shard_map/cond/branch_1_fun/ppermute | solution.py:601
  26.9 5.2 %collective-permute-start.32 = (bf16[192,1536]{1,0:T(8,128)(2,1)S(1)}, bf16[192,1536]{1,0:T(8,128)(2,1)S(1)}, u32[]{:S(2)}, u32[]{:S(2)}) collective-permute-start(bf16[192,1536]{1,0:T(8,128)(2,1)S(1)} %pad_maximum_fusion.8.mine_ref), channel_id=1, source_target_pairs={{0,1},{1,0},{2,3},{3,2},{4,5},{5,4},{6,7},{7,6},{8,9},{9,8},{10,11... | collective-permute-start | bytes 1769480 | tf_op jit(solution)/shard_map/cond/branch_1_fun/ppermute | solution.py:601
  30.0 3.7 %collective-permute-start.35 = (bf16[192,1536]{1,0:T(8,128)(2,1)S(1)}, bf16[192,1536]{1,0:T(8,128)(2,1)S(1)}, u32[]{:S(2)}, u32[]{:S(2)}) collective-permute-start(bf16[192,1536]{1,0:T(8,128)(2,1)S(1)} %pad_maximum_fusion.9.next_ref), channel_id=1, source_target_pairs={{0,1},{1,0},{2,3},{3,2},{4,5},{5,4},{6,7},{7,6},{8,9},{9,8},{10,11... | collective-permute-start | bytes 1769480 | tf_op jit(solution)/shard_map/cond/branch_1_fun/ppermute | solution.py:601
  35.9 1.7 %collective-permute-start.43 = (f32[608,128]{1,0:T(8,128)S(1)}, f32[608,128]{1,0:T(8,128)S(1)}, u32[]{:S(2)}, u32[]{:S(2)}) collective-permute-start(f32[608,128]{1,0:T(8,128)S(1)} %get-tuple-element.81), channel_id=1, source_target_pairs={{0,1},{1,0},{2,3},{3,2},{4,5},{5,4},{6,7},{7,6},{8,9},{9,8},{10,11... | collective-permute-start | bytes 933896 | tf_op jit(solution)/shard_map/cond/branch_1_fun/ppermute | solution.py:601
  37.3 1.7 %collective-permute-start.36 = (f32[608,128]{1,0:T(8,128)S(1)}, f32[608,128]{1,0:T(8,128)S(1)}, u32[]{:S(2)}, u32[]{:S(2)}) collective-permute-start(f32[608,128]{1,0:T(8,128)S(1)} %get-tuple-element.78), channel_id=1, source_target_pairs={{0,1},{1,0},{2,3},{3,2},{4,5},{5,4},{6,7},{7,6},{8,9},{9,8},{10,11... | collective-permute-start | bytes 933896 | tf_op jit(solution)/shard_map/cond/branch_1_fun/ppermute | solution.py:601
  37.6 29.8 %copy-start.4 = (f32[1000,256]{1,0:T(8,128)S(1)}, f32[1000,256]{1,0:T(8,128)}, u32[]{:S(2)}) copy-start(f32[1000,256]{1,0:T(8,128)} %get-tuple-element.79.targets_ref) | copy-start | bytes 3072004 | tf_op jit(solution)/shard_map/cond
  37.7 29.7 %copy-start.12 = (f32[1,160]{1,0:T(1,128)S(1)}, f32[1,160]{1,0:T(1,128)}, u32[]{:S(2)}) copy-start(f32[1,160]{1,0:T(1,128)} %get-tuple-element.82.eigval_ref) | copy-start | bytes 1924 | tf_op jit(solution)/shard_map/cond
  37.7 4.4 %collective-permute-start.44 = (f32[304,128]{1,0:T(8,128)S(1)}, f32[304,128]{1,0:T(8,128)S(1)}, u32[]{:S(2)}, u32[]{:S(2)}) collective-permute-start(f32[304,128]{1,0:T(8,128)S(1)} %slice.96), channel_id=1, source_target_pairs={{0,4},{1,3},{2,6},{3,1},{4,0},{5,7},{6,2},{7,5},{8,12},{9,11},{10,... | collective-permute-start | bytes 466952 | tf_op jit(solution)/shard_map/cond/branch_1_fun/ppermute | solution.py:601
  39.0 4.7 %collective-permute-start.37 = (f32[304,128]{1,0:T(8,128)S(1)}, f32[304,128]{1,0:T(8,128)S(1)}, u32[]{:S(2)}, u32[]{:S(2)}) collective-permute-start(f32[304,128]{1,0:T(8,128)S(1)} %slice.92), channel_id=1, source_target_pairs={{0,4},{1,3},{2,6},{3,1},{4,0},{5,7},{6,2},{7,5},{8,12},{9,11},{10,... | collective-permute-start | bytes 466952 | tf_op jit(solution)/shard_map/cond/branch_1_fun/ppermute | solution.py:601
  42.2 3.3 %collective-permute-start.45 = (f32[152,128]{1,0:T(8,128)S(1)}, f32[152,128]{1,0:T(8,128)S(1)}, u32[]{:S(2)}, u32[]{:S(2)}) collective-permute-start(f32[152,128]{1,0:T(8,128)S(1)} %slice.98), channel_id=1, source_target_pairs={{0,2},{1,5},{2,0},{3,7},{4,6},{5,1},{6,4},{7,3},{8,10},{9,13},{10,... | collective-permute-start | bytes 233480 | tf_op jit(solution)/shard_map/cond/branch_1_fun/ppermute | solution.py:601
  43.8 4.0 %collective-permute-start.38 = (f32[152,128]{1,0:T(8,128)S(1)}, f32[152,128]{1,0:T(8,128)S(1)}, u32[]{:S(2)}, u32[]{:S(2)}) collective-permute-start(f32[152,128]{1,0:T(8,128)S(1)} %slice.94), channel_id=1, source_target_pairs={{0,2},{1,5},{2,0},{3,7},{4,6},{5,1},{6,4},{7,3},{8,10},{9,13},{10,... | collective-permute-start | bytes 233480 | tf_op jit(solution)/shard_map/cond/branch_1_fun/ppermute | solution.py:601
  45.5 4.2 %collective-permute-start.46 = (f32[152,128]{1,0:T(8,128)S(1)}, f32[152,128]{1,0:T(8,128)S(1)}, u32[]{:S(2)}, u32[]{:S(2)}) collective-permute-start(f32[152,128]{1,0:T(8,128)S(1)} %slice_add_fusion.10), channel_id=1, source_target_pairs={{0,8},{1,9},{2,10},{3,11},{4,12},{5,13},{6,14},{7,15},{8,0},{9,1},... | collective-permute-start | bytes 233480 | tf_op jit(solution)/shard_map/cond/branch_1_fun/ppermute | solution.py:601
  47.8 4.9 %collective-permute-start.39 = (f32[152,128]{1,0:T(8,128)S(1)}, f32[152,128]{1,0:T(8,128)S(1)}, u32[]{:S(2)}, u32[]{:S(2)}) collective-permute-start(f32[152,128]{1,0:T(8,128)S(1)} %slice_add_fusion.11), channel_id=1, source_target_pairs={{0,8},{1,9},{2,10},{3,11},{4,12},{5,13},{6,14},{7,15},{8,0},{9,1},... | collective-permute-start | bytes 233480 | tf_op jit(solution)/shard_map/cond/branch_1_fun/ppermute | solution.py:601
  49.7 4.9 %collective-permute-start.47 = (f32[152,128]{1,0:T(8,128)S(1)}, f32[152,128]{1,0:T(8,128)S(1)}, u32[]{:S(2)}, u32[]{:S(2)}) collective-permute-start(f32[152,128]{1,0:T(8,128)S(1)} %add.135), channel_id=1, source_target_pairs={{0,2},{1,5},{2,0},{3,7},{4,6},{5,1},{6,4},{7,3},{8,10},{9,13},{10,... | collective-permute-start | bytes 233480 | tf_op jit(solution)/shard_map/cond/branch_1_fun/ppermute | solution.py:601
  52.8 3.7 %collective-permute-start.40 = (f32[152,128]{1,0:T(8,128)S(1)}, f32[152,128]{1,0:T(8,128)S(1)}, u32[]{:S(2)}, u32[]{:S(2)}) collective-permute-start(f32[152,128]{1,0:T(8,128)S(1)} %add.131), channel_id=1, source_target_pairs={{0,2},{1,5},{2,0},{3,7},{4,6},{5,1},{6,4},{7,3},{8,10},{9,13},{10,... | collective-permute-start | bytes 233480 | tf_op jit(solution)/shard_map/cond/branch_1_fun/ppermute | solution.py:601
  54.7 5.1 %collective-permute-start.48 = (f32[304,128]{1,0:T(8,128)S(1)}, f32[304,128]{1,0:T(8,128)S(1)}, u32[]{:S(2)}, u32[]{:S(2)}) collective-permute-start(f32[304,128]{1,0:T(8,128)S(1)} %pad_maximum_fusion.15), channel_id=1, source_target_pairs={{0,4},{1,3},{2,6},{3,1},{4,0},{5,7},{6,2},{7,5},{8,12},{9,11},{10,... | collective-permute-start | bytes 466952 | tf_op jit(solution)/shard_map/cond/branch_1_fun/ppermute | solution.py:601
  56.4 9.3 %collective-permute-start.41 = (f32[304,128]{1,0:T(8,128)S(1)}, f32[304,128]{1,0:T(8,128)S(1)}, u32[]{:S(2)}, u32[]{:S(2)}) collective-permute-start(f32[304,128]{1,0:T(8,128)S(1)} %pad_maximum_fusion.14), channel_id=1, source_target_pairs={{0,4},{1,3},{2,6},{3,1},{4,0},{5,7},{6,2},{7,5},{8,12},{9,11},{10,... | collective-permute-start | bytes 466952 | tf_op jit(solution)/shard_map/cond/branch_1_fun/ppermute | solution.py:601
  59.7 7.7 %collective-permute-start.49 = (f32[608,128]{1,0:T(8,128)S(1)}, f32[608,128]{1,0:T(8,128)S(1)}, u32[]{:S(2)}, u32[]{:S(2)}) collective-permute-start(f32[608,128]{1,0:T(8,128)S(1)} %pad_maximum_fusion.11.mine_ref), channel_id=1, source_target_pairs={{0,1},{1,0},{2,3},{3,2},{4,5},{5,4},{6,7},{7,6},{8,9},{9,8},{10,11... | collective-permute-start | bytes 933896 | tf_op jit(solution)/shard_map/cond/branch_1_fun/ppermute | solution.py:601
  65.8 4.1 %collective-permute-start.42 = (f32[608,128]{1,0:T(8,128)S(1)}, f32[608,128]{1,0:T(8,128)S(1)}, u32[]{:S(2)}, u32[]{:S(2)}) collective-permute-start(f32[608,128]{1,0:T(8,128)S(1)} %pad_maximum_fusion.10.mine_ref), channel_id=1, source_target_pairs={{0,1},{1,0},{2,3},{3,2},{4,5},{5,4},{6,7},{7,6},{8,9},{9,8},{10,11... | collective-permute-start | bytes 933896 | tf_op jit(solution)/shard_map/cond/branch_1_fun/ppermute | solution.py:601

commit v19 on v18

--- a/solution.py
+++ b/solution.py
@@ -549,7 +549,7 @@
         scratch_shapes=[
             pltpu.VMEM((padded, rows), F32),
             pltpu.VMEM((here, count), F32),
-            pltpu.SemaphoreType.DMA((3,)),
+            pltpu.SemaphoreType.DMA((4,)),
         ],
         compiler_params=params(),
         cost_estimate=pl.CostEstimate(

time: 72.2 us -> 72 us (level)
  transfers between devices with their start and end apart: 22 -> 22, of which waited for: 14 -> 14; matrix products, arithmetic and copies ran while one was open for 1% -> 1% of each run, Pallas kernels for 15% -> 14%
where the time goes in v19:
time: 72 us; the launch traced here: 71.8 us
  starting transfers between devices  37.3 us (52%)
  Pallas kernels  17.8 us (25%)
  waiting for transfers between devices  14.2 us (20%)
  between operations  1.45 us (2%)
    ppermute x22, starting transfers between devices, swap(): lax.ppermute(x, AXES, [(i, i ^ flip[i & 1]) for i in range(2 * chips)])  37.3 us
    ppermute x22, waiting for transfers between devices, swap(): lax.ppermute(x, AXES, [(i, i ^ flip[i & 1]) for i in range(2 * chips)])  14.2 us
    pallas_call x2, Pallas kernels, pack_rows(): pl.pallas_call(functools.partial(pack_body, part * depth), in_specs=[hbm,...  3.84 us
    pallas_call x1, Pallas kernels, predict(): pl.pallas_call(predict_body, in_specs=[vmem] * 6, out_specs=[vmem] * 3, o...  2.25 us
    pallas_call x1, Pallas kernels, update(): pl.pallas_call(update_body, in_specs=[vmem] * 7, out_specs=[hbm, hbm, vme...  2.24 us
    pallas_call x1, Pallas kernels, update_more(): pl.pallas_call(functools.partial(update_more_body, begin), in_specs=[vmem...  1.93 us
    pallas_call x1, Pallas kernels, spread_weights(): pl.pallas_call(functools.partial(spread_body, first, classes), out_shape=...  1.6 us
    pallas_call x1, Pallas kernels, distances(): pl.pallas_call(distance_body, in_specs=[vmem] * 6, out_specs=[vmem, vmem]...  1.46 us
  transfers between devices with their start and end apart: 22, of which 14 were waited for; matrix products, arithmetic and copies ran while one was open for 1% of the time, Pallas kernels for 14%

profile of v19, /device:TPU:1, one launch (start us, length us, event | category | flops | bytes accessed | tf_op | source)
XLA Modules:
  0.0 71.8 jit_solution(18030011756246976952)
XLA Ops:
  0.6 1.4 %rows_fit.1 = s32[1]{0:T(128)} custom-call(s32[1,256]{1,0:T(1,128)} %bitcast.17), custom_call_target="tpu_custom_call" | custom-call | tf_op jit(solution)/shard_map/rows_fit/pallas_call | solution.py:157
  2.6 69.0 %conditional.1 = ((f32[1000,768]{1,0:T(8,128)}, f32[1000,256]{1,0:T(8,128)})) conditional(s32[]{:T(128)} %bitcast.2, (s32[1,256]{1,0:T(1,128)}, bf16[768,3072]{1,0:T(8,128)(2,1)}, s32[320]{0:T(512)}, f32[160,320]{1,0:T(8,128)}, f32[1000,768]{1,0:T(8,128)}, /*index=5*/f32[1000,256]{1,0:T(8,128)}, f32[1,160]{1,0:T(1,128)}) %tuple.31, ...), branch_computations={%region_0.1_spmd, %region_1.2_spmd} | conditional | flops 5916241920 | bytes 106008064 | solution.py:686
  2.8 1.9 %pack_rows.3 = bf16[32,1536]{1,0:T(8,128)(2,1)S(1)} custom-call(s32[1,256]{1,0:T(1,128)} %get-tuple-element.58.index_hbm.index_ref, bf16[768,3072]{1,0:T(8,128)(2,1)} %get-tuple-element.59.centers_hbm.centers_ref), custom_call_target="tpu_custom_call" | custom-call | flops 75497472 | bytes 2457600 | tf_op jit(solution)/shard_map/cond/branch_1_fun/pack_rows/pallas_call | solution.py:199
  4.8 0.0 copy-start.8
  4.8 0.0 copy-start.10
  4.8 0.0 copy-start
  4.8 3.2 %collective-permute-start.29 = (bf16[32,1536]{1,0:T(8,128)(2,1)S(1)}, bf16[32,1536]{1,0:T(8,128)(2,1)S(1)}, u32[]{:S(2)}, u32[]{:S(2)}) collective-permute-start(bf16[32,1536]{1,0:T(8,128)(2,1)S(1)} %pack_rows.3), channel_id=1, source_target_pairs={{0,8},{1,9},{2,10},{3,11},{4,12},{5,13},{6,14},{7,15},{8,0},{9,1},... | collective-permute-start | bytes 294920 | tf_op jit(solution)/shard_map/cond/branch_1_fun/ppermute | solution.py:601
  8.0 1.9 %pack_rows.2 = bf16[32,1536]{1,0:T(8,128)(2,1)S(1)} custom-call(s32[1,256]{1,0:T(1,128)} %get-tuple-element.58.index_hbm.index_ref, bf16[768,3072]{1,0:T(8,128)(2,1)} %get-tuple-element.59.centers_hbm.centers_ref), custom_call_target="tpu_custom_call" | custom-call | flops 75497472 | bytes 2457600 | tf_op jit(solution)/shard_map/cond/branch_1_fun/pack_rows/pallas_call | solution.py:199
  9.9 0.0 copy-start.2
  9.9 0.0 copy-start.6
  10.0 0.2 collective-permute-start.28
  10.2 0.4 select_packed.1
  10.6 1.2 %center_norms.3.norm_ref = f32[768,128]{1,0:T(8,128)S(1)} custom-call(bf16[768,3072]{1,0:T(8,128)(2,1)S(1)} %copy-done), custom_call_target="tpu_custom_call" | custom-call | flops 4718592 | bytes 4718592 | tf_op jit(solution)/shard_map/cond/branch_1_fun/center_norms/pallas_call | solution.py:341
  11.8 0.0 copy-done.2
  11.8 1.6 %spread_weights.3 = (bf16[608,2304]{1,0:T(8,128)(2,1)S(1)}, bf16[608,2304]{1,0:T(8,128)(2,1)S(1)}, f32[160,768]{1,0:T(8,128)S(1)}) custom-call(s32[1,320]{1,0:T(1,128)S(1)} %reshape.99.index_ref, f32[160,320]{1,0:T(8,128)S(1)} %copy-done.6, f32[1000,768]{1,0:T(8,128)S(1)} %copy-done.2), custom_call_target="tpu_custom_call" | custom-call | flops 235929600 | bytes 7471104 | tf_op jit(solution)/shard_map/cond/branch_1_fun/spread_weights/pallas_call | solution.py:316
  13.4 0.0 collective-permute-done.29
  13.4 2.6 %collective-permute-start.30 = (bf16[64,1536]{1,0:T(8,128)(2,1)S(1)}, bf16[64,1536]{1,0:T(8,128)(2,1)S(1)}, u32[]{:S(2)}, u32[]{:S(2)}) collective-permute-start(bf16[64,1536]{1,0:T(8,128)(2,1)S(1)} %pad_maximum_fusion.13.keep_ref), channel_id=1, source_target_pairs={{0,2},{1,5},{2,0},{3,7},{4,6},{5,1},{6,4},{7,3},{8,10},{9,13},{10,... | collective-permute-start | bytes 589832 | tf_op jit(solution)/shard_map/cond/branch_1_fun/ppermute | solution.py:601
  16.0 2.1 %collective-permute-start.33 = (bf16[64,1536]{1,0:T(8,128)(2,1)S(1)}, bf16[64,1536]{1,0:T(8,128)(2,1)S(1)}, u32[]{:S(2)}, u32[]{:S(2)}) collective-permute-start(bf16[64,1536]{1,0:T(8,128)(2,1)S(1)} %pad_maximum_fusion.12.keep_ref), channel_id=1, source_target_pairs={{0,2},{1,5},{2,0},{3,7},{4,6},{5,1},{6,4},{7,3},{8,10},{9,13},{10,... | collective-permute-start | bytes 589832 | tf_op jit(solution)/shard_map/cond/branch_1_fun/ppermute | solution.py:601
  18.1 1.6 %collective-permute-done.30.got_ref = bf16[64,1536]{1,0:T(8,128)(2,1)S(1)} collective-permute-done((bf16[64,1536]{1,0:T(8,128)(2,1)S(1)}, bf16[64,1536]{1,0:T(8,128)(2,1)S(1)}, u32[]{:S(2)}, u32[]{:S(2)}) %collective-permute-start.30) | collective-permute-done | bytes 196640 | tf_op jit(solution)/shard_map/cond/branch_1_fun/ppermute | solution.py:601
  19.7 0.3 squeeze_slots.2
  20.1 1.5 %collective-permute-start.31 = (bf16[96,1536]{1,0:T(8,128)(2,1)S(1)}, bf16[96,1536]{1,0:T(8,128)(2,1)S(1)}, u32[]{:S(2)}, u32[]{:S(2)}) collective-permute-start(bf16[96,1536]{1,0:T(8,128)(2,1)S(1)} %squeeze_slots.2), channel_id=1, source_target_pairs={{0,4},{1,3},{2,6},{3,1},{4,0},{5,7},{6,2},{7,5},{8,12},{9,11},{10,... | collective-permute-start | bytes 884744 | tf_op jit(solution)/shard_map/cond/branch_1_fun/ppermute | solution.py:601
  21.6 0.5 collective-permute-done.33.got_ref
  22.1 0.3 squeeze_slots.3
  22.4 1.3 %collective-permute-start.34 = (bf16[96,1536]{1,0:T(8,128)(2,1)S(1)}, bf16[96,1536]{1,0:T(8,128)(2,1)S(1)}, u32[]{:S(2)}, u32[]{:S(2)}) collective-permute-start(bf16[96,1536]{1,0:T(8,128)(2,1)S(1)} %squeeze_slots.3), channel_id=1, source_target_pairs={{0,4},{1,3},{2,6},{3,1},{4,0},{5,7},{6,2},{7,5},{8,12},{9,11},{10,... | collective-permute-start | bytes 884744 | tf_op jit(solution)/shard_map/cond/branch_1_fun/ppermute | solution.py:601
  23.7 3.1 %collective-permute-done.31 = bf16[96,1536]{1,0:T(8,128)(2,1)S(1)} collective-permute-done((bf16[96,1536]{1,0:T(8,128)(2,1)S(1)}, bf16[96,1536]{1,0:T(8,128)(2,1)S(1)}, u32[]{:S(2)}, u32[]{:S(2)}) %collective-permute-start.31) | collective-permute-done | bytes 294944 | tf_op jit(solution)/shard_map/cond/branch_1_fun/ppermute | solution.py:601
  26.9 0.9 %collective-permute-start.32 = (bf16[192,1536]{1,0:T(8,128)(2,1)S(1)}, bf16[192,1536]{1,0:T(8,128)(2,1)S(1)}, u32[]{:S(2)}, u32[]{:S(2)}) collective-permute-start(bf16[192,1536]{1,0:T(8,128)(2,1)S(1)} %pad_maximum_fusion.8.mine_ref), channel_id=1, source_target_pairs={{0,1},{1,0},{2,3},{3,2},{4,5},{5,4},{6,7},{7,6},{8,9},{9,8},{10,11... | collective-permute-start | bytes 1769480 | tf_op jit(solution)/shard_map/cond/branch_1_fun/ppermute | solution.py:601
  27.8 2.2 %collective-permute-done.34 = bf16[96,1536]{1,0:T(8,128)(2,1)S(1)} collective-permute-done((bf16[96,1536]{1,0:T(8,128)(2,1)S(1)}, bf16[96,1536]{1,0:T(8,128)(2,1)S(1)}, u32[]{:S(2)}, u32[]{:S(2)}) %collective-permute-start.34) | collective-permute-done | bytes 294944 | tf_op jit(solution)/shard_map/cond/branch_1_fun/ppermute | solution.py:601
  30.0 2.0 %collective-permute-start.35 = (bf16[192,1536]{1,0:T(8,128)(2,1)S(1)}, bf16[192,1536]{1,0:T(8,128)(2,1)S(1)}, u32[]{:S(2)}, u32[]{:S(2)}) collective-permute-start(bf16[192,1536]{1,0:T(8,128)(2,1)S(1)} %pad_maximum_fusion.9.next_ref), channel_id=1, source_target_pairs={{0,1},{1,0},{2,3},{3,2},{4,5},{5,4},{6,7},{7,6},{8,9},{9,8},{10,11... | collective-permute-start | bytes 1769480 | tf_op jit(solution)/shard_map/cond/branch_1_fun/ppermute | solution.py:601
  32.0 1.5 %distances.3 = (f32[768,256]{1,0:T(8,128)S(1)}, bf16[256,1536]{1,0:T(8,128)(2,1)S(1)}) custom-call(bf16[192,1536]{1,0:T(8,128)(2,1)S(1)} %pad_maximum_fusion.8.mine_ref, bf16[192,1536]{1,0:T(8,128)(2,1)S(1)} %collective-permute-done.32.other_ref, bf16[192,1536]{1,0:T(8,128)(2,1)S(1)} %pad_maximum_fusion.9.next_ref, ...), custom_call_target="tpu_custom_call" | custom-call | flops 603979776 | bytes 3145728 | tf_op jit(solution)/shard_map/cond/branch_1_fun/distances/pallas_call | solution.py:416
  33.5 0.2 collective-permute-done.35.other_ref
  33.7 2.2 %predict.3 = (f32[608,128]{1,0:T(8,128)S(1)}, f32[608,128]{1,0:T(8,128)S(1)}, bf16[2304,256]{1,0:T(8,128)(2,1)S(1)}) custom-call(bf16[256,1536]{1,0:T(8,128)(2,1)S(1)} %get-tuple-element.73.found_ref, bf16[192,1536]{1,0:T(8,128)(2,1)S(1)} %collective-permute-done.35.other_ref, bf16[256,512]{1,0:T(8,128)(2,1)S(1)} %get-tuple-element.71.select_ref, ...), custom_call_target="tpu_custom_call" | custom-call | flops 1321205760 | bytes 5636096 | tf_op jit(solution)/shard_map/cond/branch_1_fun/predict/pallas_call | solution.py:438
  35.9 0.4 collective-permute-start.43
  36.4 0.9 %predict_more.3 = (f32[608,128]{1,0:T(8,128)S(1)}, f32[608,128]{1,0:T(8,128)S(1)}) custom-call(bf16[608,2304]{1,0:T(8,128)(2,1)S(1)} %get-tuple-element.67.left, bf16[2304,256]{1,0:T(8,128)(2,1)S(1)} %get-tuple-element.76.right), custom_call_target="tpu_custom_call" | custom-call | flops 717225984 | bytes 3112960 | tf_op jit(solution)/shard_map/cond/branch_1_fun/predict_more/pallas_call | solution.py:458
  37.3 0.2 collective-permute-start.36
  37.5 0.1 collective-permute-done.43
  37.6 0.0 copy-start.4
  37.7 0.0 copy-start.12
  37.7 1.1 %collective-permute-start.44 = (f32[304,128]{1,0:T(8,128)S(1)}, f32[304,128]{1,0:T(8,128)S(1)}, u32[]{:S(2)}, u32[]{:S(2)}) collective-permute-start(f32[304,128]{1,0:T(8,128)S(1)} %slice.96), channel_id=1, source_target_pairs={{0,4},{1,3},{2,6},{3,1},{4,0},{5,7},{6,2},{7,5},{8,12},{9,11},{10,... | collective-permute-start | bytes 466952 | tf_op jit(solution)/shard_map/cond/branch_1_fun/ppermute | solution.py:601
  38.8 0.2 collective-permute-done.36
  39.0 1.1 %collective-permute-start.37 = (f32[304,128]{1,0:T(8,128)S(1)}, f32[304,128]{1,0:T(8,128)S(1)}, u32[]{:S(2)}, u32[]{:S(2)}) collective-permute-start(f32[304,128]{1,0:T(8,128)S(1)} %slice.92), channel_id=1, source_target_pairs={{0,4},{1,3},{2,6},{3,1},{4,0},{5,7},{6,2},{7,5},{8,12},{9,11},{10,... | collective-permute-start | bytes 466952 | tf_op jit(solution)/shard_map/cond/branch_1_fun/ppermute | solution.py:601
  40.1 2.0 %collective-permute-done.44 = f32[304,128]{1,0:T(8,128)S(1)} collective-permute-done((f32[304,128]{1,0:T(8,128)S(1)}, f32[304,128]{1,0:T(8,128)S(1)}, u32[]{:S(2)}, u32[]{:S(2)}) %collective-permute-start.44) | collective-permute-done | bytes 155680 | tf_op jit(solution)/shard_map/cond/branch_1_fun/ppermute | solution.py:601
  42.2 0.7 collective-permute-start.45
  42.8 0.9 %collective-permute-done.37 = f32[304,128]{1,0:T(8,128)S(1)} collective-permute-done((f32[304,128]{1,0:T(8,128)S(1)}, f32[304,128]{1,0:T(8,128)S(1)}, u32[]{:S(2)}, u32[]{:S(2)}) %collective-permute-start.37) | collective-permute-done | bytes 155680 | tf_op jit(solution)/shard_map/cond/branch_1_fun/ppermute | solution.py:601
  43.8 0.7 collective-permute-start.38
  44.5 1.0 %collective-permute-done.45 = f32[152,128]{1,0:T(8,128)S(1)} collective-permute-done((f32[152,128]{1,0:T(8,128)S(1)}, f32[152,128]{1,0:T(8,128)S(1)}, u32[]{:S(2)}, u32[]{:S(2)}) %collective-permute-start.45) | collective-permute-done | bytes 77856 | tf_op jit(solution)/shard_map/cond/branch_1_fun/ppermute | solution.py:601
  45.5 2.3 %collective-permute-start.46 = (f32[152,128]{1,0:T(8,128)S(1)}, f32[152,128]{1,0:T(8,128)S(1)}, u32[]{:S(2)}, u32[]{:S(2)}) collective-permute-start(f32[152,128]{1,0:T(8,128)S(1)} %slice_add_fusion.10), channel_id=1, source_target_pairs={{0,8},{1,9},{2,10},{3,11},{4,12},{5,13},{6,14},{7,15},{8,0},{9,1},... | collective-permute-start | bytes 233480 | tf_op jit(solution)/shard_map/cond/branch_1_fun/ppermute | solution.py:601
  47.8 0.0 collective-permute-done.38
  47.8 1.7 %collective-permute-start.39 = (f32[152,128]{1,0:T(8,128)S(1)}, f32[152,128]{1,0:T(8,128)S(1)}, u32[]{:S(2)}, u32[]{:S(2)}) collective-permute-start(f32[152,128]{1,0:T(8,128)S(1)} %slice_add_fusion.11), channel_id=1, source_target_pairs={{0,8},{1,9},{2,10},{3,11},{4,12},{5,13},{6,14},{7,15},{8,0},{9,1},... | collective-permute-start | bytes 233480 | tf_op jit(solution)/shard_map/cond/branch_1_fun/ppermute | solution.py:601
  49.5 0.2 collective-permute-done.46
  49.7 1.6 %collective-permute-start.47 = (f32[152,128]{1,0:T(8,128)S(1)}, f32[152,128]{1,0:T(8,128)S(1)}, u32[]{:S(2)}, u32[]{:S(2)}) collective-permute-start(f32[152,128]{1,0:T(8,128)S(1)} %add.135), channel_id=1, source_target_pairs={{0,2},{1,5},{2,0},{3,7},{4,6},{5,1},{6,4},{7,3},{8,10},{9,13},{10,... | collective-permute-start | bytes 233480 | tf_op jit(solution)/shard_map/cond/branch_1_fun/ppermute | solution.py:601
  51.3 1.4 %collective-permute-done.39 = f32[152,128]{1,0:T(8,128)S(1)} collective-permute-done((f32[152,128]{1,0:T(8,128)S(1)}, f32[152,128]{1,0:T(8,128)S(1)}, u32[]{:S(2)}, u32[]{:S(2)}) %collective-permute-start.39) | collective-permute-done | bytes 77856 | tf_op jit(solution)/shard_map/cond/branch_1_fun/ppermute | solution.py:601
  52.8 1.9 %collective-permute-start.40 = (f32[152,128]{1,0:T(8,128)S(1)}, f32[152,128]{1,0:T(8,128)S(1)}, u32[]{:S(2)}, u32[]{:S(2)}) collective-permute-start(f32[152,128]{1,0:T(8,128)S(1)} %add.131), channel_id=1, source_target_pairs={{0,2},{1,5},{2,0},{3,7},{4,6},{5,1},{6,4},{7,3},{8,10},{9,13},{10,... | collective-permute-start | bytes 233480 | tf_op jit(solution)/shard_map/cond/branch_1_fun/ppermute | solution.py:601
  54.6 0.0 collective-permute-done.47
  54.7 1.4 %collective-permute-start.48 = (f32[304,128]{1,0:T(8,128)S(1)}, f32[304,128]{1,0:T(8,128)S(1)}, u32[]{:S(2)}, u32[]{:S(2)}) collective-permute-start(f32[304,128]{1,0:T(8,128)S(1)} %pad_maximum_fusion.15), channel_id=1, source_target_pairs={{0,4},{1,3},{2,6},{3,1},{4,0},{5,7},{6,2},{7,5},{8,12},{9,11},{10,... | collective-permute-start | bytes 466952 | tf_op jit(solution)/shard_map/cond/branch_1_fun/ppermute | solution.py:601
  56.0 0.4 collective-permute-done.40
  56.4 2.8 %collective-permute-start.41 = (f32[304,128]{1,0:T(8,128)S(1)}, f32[304,128]{1,0:T(8,128)S(1)}, u32[]{:S(2)}, u32[]{:S(2)}) collective-permute-start(f32[304,128]{1,0:T(8,128)S(1)} %pad_maximum_fusion.14), channel_id=1, source_target_pairs={{0,4},{1,3},{2,6},{3,1},{4,0},{5,7},{6,2},{7,5},{8,12},{9,11},{10,... | collective-permute-start | bytes 466952 | tf_op jit(solution)/shard_map/cond/branch_1_fun/ppermute | solution.py:601
  59.3 0.4 collective-permute-done.48
  59.7 6.0 %collective-permute-start.49 = (f32[608,128]{1,0:T(8,128)S(1)}, f32[608,128]{1,0:T(8,128)S(1)}, u32[]{:S(2)}, u32[]{:S(2)}) collective-permute-start(f32[608,128]{1,0:T(8,128)S(1)} %pad_maximum_fusion.11.mine_ref), channel_id=1, source_target_pairs={{0,1},{1,0},{2,3},{3,2},{4,5},{5,4},{6,7},{7,6},{8,9},{9,8},{10,11... | collective-permute-start | bytes 933896 | tf_op jit(solution)/shard_map/cond/branch_1_fun/ppermute | solution.py:601
  65.7 0.0 collective-permute-done.41
  65.8 1.6 %collective-permute-start.42 = (f32[608,128]{1,0:T(8,128)S(1)}, f32[608,128]{1,0:T(8,128)S(1)}, u32[]{:S(2)}, u32[]{:S(2)}) collective-permute-start(f32[608,128]{1,0:T(8,128)S(1)} %pad_maximum_fusion.10.mine_ref), channel_id=1, source_target_pairs={{0,1},{1,0},{2,3},{3,2},{4,5},{5,4},{6,7},{7,6},{8,9},{9,8},{10,11... | collective-permute-start | bytes 933896 | tf_op jit(solution)/shard_map/cond/branch_1_fun/ppermute | solution.py:601
  67.4 0.0 collective-permute-done.49.other_ref
  67.4 2.2 %update.3 = (f32[1000,768]{1,0:T(8,128)}, f32[1000,256]{1,0:T(8,128)}, bf16[768,768]{1,0:T(8,128)(2,1)S(1)}) custom-call(f32[608,128]{1,0:T(8,128)S(1)} %pad_maximum_fusion.11.mine_ref, f32[608,128]{1,0:T(8,128)S(1)} %collective-permute-done.49.other_ref, f32[1000,256]{1,0:T(8,128)S(1)} %copy-done.4, s32[1,256]{1,0:T(1,128)S(1)} %copy-done.8, ...), custom_call_target="tpu_custom_call" | custom-call | flops 717225984 | bytes 3670016 | tf_op jit(solution)/shard_map/cond/branch_1_fun/update/pallas_call | solution.py:540
  69.7 0.0 collective-permute-done.42.other_ref
  69.7 1.9 %update_more.3 = (f32[1000,768]{1,0:T(8,128)}, f32[1000,256]{1,0:T(8,128)}) custom-call(f32[608,128]{1,0:T(8,128)S(1)} %pad_maximum_fusion.10.mine_ref, f32[608,128]{1,0:T(8,128)S(1)} %collective-permute-done.42.other_ref, f32[1000,256]{1,0:T(8,128)S(1)} %copy-done.4, f32[1000,768]{1,0:T(8,128)S(1)} %copy-done.2, ...), custom_call_target="tpu_custom_call", output_to_operand_aliasing={{0}: (5, {}), {1}: (6, {})} | custom-call | flops 651165696 | bytes 4521984 | tf_op jit(solution)/shard_map/cond/branch_1_fun/update_more/pallas_call | solution.py:577
  (29 shorter events, 0.4 us)
Async XLA Ops:
  4.8 5.4 %copy-start.8 = (s32[1,256]{1,0:T(1,128)S(1)}, s32[1,256]{1,0:T(1,128)}, u32[]{:S(2)}) copy-start(s32[1,256]{1,0:T(1,128)} %get-tuple-element.58.index_hbm.index_ref) | copy-start | bytes 3076 | tf_op jit(solution)/shard_map/cond
  4.8 5.8 %copy-start.10 = (s32[320]{0:T(512)S(1)}, s32[320]{0:T(512)}, u32[]{:S(2)}) copy-start(s32[320]{0:T(512)} %get-tuple-element.60) | copy-start | bytes 3844 | tf_op jit(solution)/shard_map/cond
  4.8 5.8 %copy-start = (bf16[768,3072]{1,0:T(8,128)(2,1)S(1)}, bf16[768,3072]{1,0:T(8,128)(2,1)}, u32[]{:S(2)}) copy-start(bf16[768,3072]{1,0:T(8,128)(2,1)} %get-tuple-element.59.centers_hbm.centers_ref) | copy-start | bytes 14155780 | tf_op jit(solution)/shard_map/cond
  4.8 8.6 %collective-permute-start.29 = (bf16[32,1536]{1,0:T(8,128)(2,1)S(1)}, bf16[32,1536]{1,0:T(8,128)(2,1)S(1)}, u32[]{:S(2)}, u32[]{:S(2)}) collective-permute-start(bf16[32,1536]{1,0:T(8,128)(2,1)S(1)} %pack_rows.3), channel_id=1, source_target_pairs={{0,8},{1,9},{2,10},{3,11},{4,12},{5,13},{6,14},{7,15},{8,0},{9,1},... | collective-permute-start | bytes 294920 | tf_op jit(solution)/shard_map/cond/branch_1_fun/ppermute | solution.py:601
  9.9 1.9 %copy-start.2 = (f32[1000,768]{1,0:T(8,128)S(1)}, f32[1000,768]{1,0:T(8,128)}, u32[]{:S(2)}) copy-start(f32[1000,768]{1,0:T(8,128)} %get-tuple-element.62.weights_ref) | copy-start | bytes 9216004 | tf_op jit(solution)/shard_map/cond
  9.9 1.9 %copy-start.6 = (f32[160,320]{1,0:T(8,128)S(1)}, f32[160,320]{1,0:T(8,128)}, u32[]{:S(2)}) copy-start(f32[160,320]{1,0:T(8,128)} %get-tuple-element.61.eigvec_ref) | copy-start | bytes 614404 | tf_op jit(solution)/shard_map/cond
  10.0 6.0 %collective-permute-start.28 = (bf16[32,1536]{1,0:T(8,128)(2,1)S(1)}, bf16[32,1536]{1,0:T(8,128)(2,1)S(1)}, u32[]{:S(2)}, u32[]{:S(2)}) collective-permute-start(bf16[32,1536]{1,0:T(8,128)(2,1)S(1)} %pack_rows.2), channel_id=1, source_target_pairs={{0,8},{1,9},{2,10},{3,11},{4,12},{5,13},{6,14},{7,15},{8,0},{9,1},... | collective-permute-start | bytes 294920 | tf_op jit(solution)/shard_map/cond/branch_1_fun/ppermute | solution.py:601
  13.4 6.3 %collective-permute-start.30 = (bf16[64,1536]{1,0:T(8,128)(2,1)S(1)}, bf16[64,1536]{1,0:T(8,128)(2,1)S(1)}, u32[]{:S(2)}, u32[]{:S(2)}) collective-permute-start(bf16[64,1536]{1,0:T(8,128)(2,1)S(1)} %pad_maximum_fusion.13.keep_ref), channel_id=1, source_target_pairs={{0,2},{1,5},{2,0},{3,7},{4,6},{5,1},{6,4},{7,3},{8,10},{9,13},{10,... | collective-permute-start | bytes 589832 | tf_op jit(solution)/shard_map/cond/branch_1_fun/ppermute | solution.py:601
  16.0 6.0 %collective-permute-start.33 = (bf16[64,1536]{1,0:T(8,128)(2,1)S(1)}, bf16[64,1536]{1,0:T(8,128)(2,1)S(1)}, u32[]{:S(2)}, u32[]{:S(2)}) collective-permute-start(bf16[64,1536]{1,0:T(8,128)(2,1)S(1)} %pad_maximum_fusion.12.keep_ref), channel_id=1, source_target_pairs={{0,2},{1,5},{2,0},{3,7},{4,6},{5,1},{6,4},{7,3},{8,10},{9,13},{10,... | collective-permute-start | bytes 589832 | tf_op jit(solution)/shard_map/cond/branch_1_fun/ppermute | solution.py:601
  20.1 6.7 %collective-permute-start.31 = (bf16[96,1536]{1,0:T(8,128)(2,1)S(1)}, bf16[96,1536]{1,0:T(8,128)(2,1)S(1)}, u32[]{:S(2)}, u32[]{:S(2)}) collective-permute-start(bf16[96,1536]{1,0:T(8,128)(2,1)S(1)} %squeeze_slots.2), channel_id=1, source_target_pairs={{0,4},{1,3},{2,6},{3,1},{4,0},{5,7},{6,2},{7,5},{8,12},{9,11},{10,... | collective-permute-start | bytes 884744 | tf_op jit(solution)/shard_map/cond/branch_1_fun/ppermute | solution.py:601
  22.4 7.6 %collective-permute-start.34 = (bf16[96,1536]{1,0:T(8,128)(2,1)S(1)}, bf16[96,1536]{1,0:T(8,128)(2,1)S(1)}, u32[]{:S(2)}, u32[]{:S(2)}) collective-permute-start(bf16[96,1536]{1,0:T(8,128)(2,1)S(1)} %squeeze_slots.3), channel_id=1, source_target_pairs={{0,4},{1,3},{2,6},{3,1},{4,0},{5,7},{6,2},{7,5},{8,12},{9,11},{10,... | collective-permute-start | bytes 884744 | tf_op jit(solution)/shard_map/cond/branch_1_fun/ppermute | solution.py:601
  26.9 5.2 %collective-permute-start.32 = (bf16[192,1536]{1,0:T(8,128)(2,1)S(1)}, bf16[192,1536]{1,0:T(8,128)(2,1)S(1)}, u32[]{:S(2)}, u32[]{:S(2)}) collective-permute-start(bf16[192,1536]{1,0:T(8,128)(2,1)S(1)} %pad_maximum_fusion.8.mine_ref), channel_id=1, source_target_pairs={{0,1},{1,0},{2,3},{3,2},{4,5},{5,4},{6,7},{7,6},{8,9},{9,8},{10,11... | collective-permute-start | bytes 1769480 | tf_op jit(solution)/shard_map/cond/branch_1_fun/ppermute | solution.py:601
  30.0 3.7 %collective-permute-start.35 = (bf16[192,1536]{1,0:T(8,128)(2,1)S(1)}, bf16[192,1536]{1,0:T(8,128)(2,1)S(1)}, u32[]{:S(2)}, u32[]{:S(2)}) collective-permute-start(bf16[192,1536]{1,0:T(8,128)(2,1)S(1)} %pad_maximum_fusion.9.next_ref), channel_id=1, source_target_pairs={{0,1},{1,0},{2,3},{3,2},{4,5},{5,4},{6,7},{7,6},{8,9},{9,8},{10,11... | collective-permute-start | bytes 1769480 | tf_op jit(solution)/shard_map/cond/branch_1_fun/ppermute | solution.py:601
  35.9 1.7 %collective-permute-start.43 = (f32[608,128]{1,0:T(8,128)S(1)}, f32[608,128]{1,0:T(8,128)S(1)}, u32[]{:S(2)}, u32[]{:S(2)}) collective-permute-start(f32[608,128]{1,0:T(8,128)S(1)} %get-tuple-element.81), channel_id=1, source_target_pairs={{0,1},{1,0},{2,3},{3,2},{4,5},{5,4},{6,7},{7,6},{8,9},{9,8},{10,11... | collective-permute-start | bytes 933896 | tf_op jit(solution)/shard_map/cond/branch_1_fun/ppermute | solution.py:601
  37.3 1.7 %collective-permute-start.36 = (f32[608,128]{1,0:T(8,128)S(1)}, f32[608,128]{1,0:T(8,128)S(1)}, u32[]{:S(2)}, u32[]{:S(2)}) collective-permute-start(f32[608,128]{1,0:T(8,128)S(1)} %get-tuple-element.78), channel_id=1, source_target_pairs={{0,1},{1,0},{2,3},{3,2},{4,5},{5,4},{6,7},{7,6},{8,9},{9,8},{10,11... | collective-permute-start | bytes 933896 | tf_op jit(solution)/shard_map/cond/branch_1_fun/ppermute | solution.py:601
  37.6 29.8 %copy-start.4 = (f32[1000,256]{1,0:T(8,128)S(1)}, f32[1000,256]{1,0:T(8,128)}, u32[]{:S(2)}) copy-start(f32[1000,256]{1,0:T(8,128)} %get-tuple-element.79.targets_ref) | copy-start | bytes 3072004 | tf_op jit(solution)/shard_map/cond
  37.7 29.7 %copy-start.12 = (f32[1,160]{1,0:T(1,128)S(1)}, f32[1,160]{1,0:T(1,128)}, u32[]{:S(2)}) copy-start(f32[1,160]{1,0:T(1,128)} %get-tuple-element.82.eigval_ref) | copy-start | bytes 1924 | tf_op jit(solution)/shard_map/cond
  37.7 4.4 %collective-permute-start.44 = (f32[304,128]{1,0:T(8,128)S(1)}, f32[304,128]{1,0:T(8,128)S(1)}, u32[]{:S(2)}, u32[]{:S(2)}) collective-permute-start(f32[304,128]{1,0:T(8,128)S(1)} %slice.96), channel_id=1, source_target_pairs={{0,4},{1,3},{2,6},{3,1},{4,0},{5,7},{6,2},{7,5},{8,12},{9,11},{10,... | collective-permute-start | bytes 466952 | tf_op jit(solution)/shard_map/cond/branch_1_fun/ppermute | solution.py:601
  39.0 4.7 %collective-permute-start.37 = (f32[304,128]{1,0:T(8,128)S(1)}, f32[304,128]{1,0:T(8,128)S(1)}, u32[]{:S(2)}, u32[]{:S(2)}) collective-permute-start(f32[304,128]{1,0:T(8,128)S(1)} %slice.92), channel_id=1, source_target_pairs={{0,4},{1,3},{2,6},{3,1},{4,0},{5,7},{6,2},{7,5},{8,12},{9,11},{10,... | collective-permute-start | bytes 466952 | tf_op jit(solution)/shard_map/cond/branch_1_fun/ppermute | solution.py:601
  42.2 3.3 %collective-permute-start.45 = (f32[152,128]{1,0:T(8,128)S(1)}, f32[152,128]{1,0:T(8,128)S(1)}, u32[]{:S(2)}, u32[]{:S(2)}) collective-permute-start(f32[152,128]{1,0:T(8,128)S(1)} %slice.98), channel_id=1, source_target_pairs={{0,2},{1,5},{2,0},{3,7},{4,6},{5,1},{6,4},{7,3},{8,10},{9,13},{10,... | collective-permute-start | bytes 233480 | tf_op jit(solution)/shard_map/cond/branch_1_fun/ppermute | solution.py:601
  43.8 4.0 %collective-permute-start.38 = (f32[152,128]{1,0:T(8,128)S(1)}, f32[152,128]{1,0:T(8,128)S(1)}, u32[]{:S(2)}, u32[]{:S(2)}) collective-permute-start(f32[152,128]{1,0:T(8,128)S(1)} %slice.94), channel_id=1, source_target_pairs={{0,2},{1,5},{2,0},{3,7},{4,6},{5,1},{6,4},{7,3},{8,10},{9,13},{10,... | collective-permute-start | bytes 233480 | tf_op jit(solution)/shard_map/cond/branch_1_fun/ppermute | solution.py:601
  45.5 4.2 %collective-permute-start.46 = (f32[152,128]{1,0:T(8,128)S(1)}, f32[152,128]{1,0:T(8,128)S(1)}, u32[]{:S(2)}, u32[]{:S(2)}) collective-permute-start(f32[152,128]{1,0:T(8,128)S(1)} %slice_add_fusion.10), channel_id=1, source_target_pairs={{0,8},{1,9},{2,10},{3,11},{4,12},{5,13},{6,14},{7,15},{8,0},{9,1},... | collective-permute-start | bytes 233480 | tf_op jit(solution)/shard_map/cond/branch_1_fun/ppermute | solution.py:601
  47.8 4.9 %collective-permute-start.39 = (f32[152,128]{1,0:T(8,128)S(1)}, f32[152,128]{1,0:T(8,128)S(1)}, u32[]{:S(2)}, u32[]{:S(2)}) collective-permute-start(f32[152,128]{1,0:T(8,128)S(1)} %slice_add_fusion.11), channel_id=1, source_target_pairs={{0,8},{1,9},{2,10},{3,11},{4,12},{5,13},{6,14},{7,15},{8,0},{9,1},... | collective-permute-start | bytes 233480 | tf_op jit(solution)/shard_map/cond/branch_1_fun/ppermute | solution.py:601
  49.7 4.9 %collective-permute-start.47 = (f32[152,128]{1,0:T(8,128)S(1)}, f32[152,128]{1,0:T(8,128)S(1)}, u32[]{:S(2)}, u32[]{:S(2)}) collective-permute-start(f32[152,128]{1,0:T(8,128)S(1)} %add.135), channel_id=1, source_target_pairs={{0,2},{1,5},{2,0},{3,7},{4,6},{5,1},{6,4},{7,3},{8,10},{9,13},{10,... | collective-permute-start | bytes 233480 | tf_op jit(solution)/shard_map/cond/branch_1_fun/ppermute | solution.py:601
  52.8 3.7 %collective-permute-start.40 = (f32[152,128]{1,0:T(8,128)S(1)}, f32[152,128]{1,0:T(8,128)S(1)}, u32[]{:S(2)}, u32[]{:S(2)}) collective-permute-start(f32[152,128]{1,0:T(8,128)S(1)} %add.131), channel_id=1, source_target_pairs={{0,2},{1,5},{2,0},{3,7},{4,6},{5,1},{6,4},{7,3},{8,10},{9,13},{10,... | collective-permute-start | bytes 233480 | tf_op jit(solution)/shard_map/cond/branch_1_fun/ppermute | solution.py:601
  54.7 5.1 %collective-permute-start.48 = (f32[304,128]{1,0:T(8,128)S(1)}, f32[304,128]{1,0:T(8,128)S(1)}, u32[]{:S(2)}, u32[]{:S(2)}) collective-permute-start(f32[304,128]{1,0:T(8,128)S(1)} %pad_maximum_fusion.15), channel_id=1, source_target_pairs={{0,4},{1,3},{2,6},{3,1},{4,0},{5,7},{6,2},{7,5},{8,12},{9,11},{10,... | collective-permute-start | bytes 466952 | tf_op jit(solution)/shard_map/cond/branch_1_fun/ppermute | solution.py:601
  56.4 9.3 %collective-permute-start.41 = (f32[304,128]{1,0:T(8,128)S(1)}, f32[304,128]{1,0:T(8,128)S(1)}, u32[]{:S(2)}, u32[]{:S(2)}) collective-permute-start(f32[304,128]{1,0:T(8,128)S(1)} %pad_maximum_fusion.14), channel_id=1, source_target_pairs={{0,4},{1,3},{2,6},{3,1},{4,0},{5,7},{6,2},{7,5},{8,12},{9,11},{10,... | collective-permute-start | bytes 466952 | tf_op jit(solution)/shard_map/cond/branch_1_fun/ppermute | solution.py:601
  59.7 7.7 %collective-permute-start.49 = (f32[608,128]{1,0:T(8,128)S(1)}, f32[608,128]{1,0:T(8,128)S(1)}, u32[]{:S(2)}, u32[]{:S(2)}) collective-permute-start(f32[608,128]{1,0:T(8,128)S(1)} %pad_maximum_fusion.11.mine_ref), channel_id=1, source_target_pairs={{0,1},{1,0},{2,3},{3,2},{4,5},{5,4},{6,7},{7,6},{8,9},{9,8},{10,11... | collective-permute-start | bytes 933896 | tf_op jit(solution)/shard_map/cond/branch_1_fun/ppermute | solution.py:601
  65.8 3.9 %collective-permute-start.42 = (f32[608,128]{1,0:T(8,128)S(1)}, f32[608,128]{1,0:T(8,128)S(1)}, u32[]{:S(2)}, u32[]{:S(2)}) collective-permute-start(f32[608,128]{1,0:T(8,128)S(1)} %pad_maximum_fusion.10.mine_ref), channel_id=1, source_target_pairs={{0,1},{1,0},{2,3},{3,2},{4,5},{5,4},{6,7},{7,6},{8,9},{9,8},{10,11... | collective-permute-start | bytes 933896 | tf_op jit(solution)/shard_map/cond/branch_1_fun/ppermute | solution.py:601
